TPU v7x, 32 devices: a whole 2x2x4 slice. The times are simulated.
32 devices in a mesh: section: 8 (over y, x, core), ep: 4 (over z).
Axes of the slice: x: 2, y: 2, z: 4, core: 2. Of those that a mesh axis runs over, the one named last changes fastest.
Arguments:
- grad_out: bfloat16 [8, 2048, 2048], P('section', 'ep'), may hold values from -0.125 to 0.125
- router_weights: bfloat16 [8, 2048, 8], P('section', 'ep'), may hold values from 0.049804688 to 0.29882812
- expert_ids: int32 [8, 2048, 8], P('section', 'ep'), may hold values from 0 to 127, all different within a row; in each aligned block of 512 rows (0 to 511, 512 to 1023, ..., all dimensions but the last counted through in order) at most 64 rows name the same one
- hidden: bfloat16 [8, 4, 768, 256], P('section', 'ep'), may hold values from -6 to 6
- master: float32 [8, 4, 768, 1024], P('section', 'ep'), may hold values from -0.25 to 0.25
- moment: bfloat16 [8, 4, 768, 1024], P('section', 'ep'), may hold values from -0.049804688 to 0.049804688
- second: bfloat16 [8, 4, 768, 1024], P('section', 'ep'), may hold values from 0.0019989014 to 0.019897461
Outputs:
- update: float32 [8, 4, 768, 1024], P('section', 'ep')
- router_grad: float32 [8, 2048, 8], P('section', 'ep')
Inputs may be any that keep to these rules, and one draw needn't show every extreme that they name: `expert_ids`: in the rows of one device (aligned blocks of 512 rows) no expert is named by more than 64 rows, a bound that some block reaches.
All inputs are finite; a program needn't handle non-finite values.
Results may differ from a plain program's by a relative error of at most 0.0029.
Values may be sent and summed in bfloat16 or wider, within the bound.
No kernel may reach another device: no remote copies, remote signals or barrier semaphores. Data moves between devices by JAX's collectives and lax.ppermute only.
A program may use at most 128 MiB of HBM per device.

v0:
```python
import jax
import jax.numpy as jnp
from jax import lax
from jax.sharding import PartitionSpec as P

beta_first = 0.9
beta_second = 0.95
adam_eps = 1e-08
decay_rate = 0.1
first_fix = 1.0 - 0.9**10
second_fix = 1.0 - 0.95**10


def swapped(array, axis, distance):
    return lax.ppermute(array, axis, [(i, i ^ 1 << distance) for i in range(lax.axis_size(axis))])


def slot_ranks(routes, count):
    onehot = (routes[:, :, None] == jnp.arange(count, dtype=jnp.int32)[None, None, :]).astype(
        jnp.int32
    )
    per_token = jnp.sum(onehot, axis=1)
    before = jnp.cumsum(per_token, axis=0, dtype=jnp.int32) - per_token
    return jnp.sum(before[:, None, :] * onehot, axis=2)


def adam_update(total, param, first, second_moment):
    first_new = beta_first * first + (1.0 - beta_first) * total
    second_new = beta_second * second_moment + (1.0 - beta_second) * total * total
    return (
        first_new / first_fix / (jnp.sqrt(second_new / second_fix) + adam_eps) + decay_rate * param
    )


def scale_hidden(hid_block, slot_weights):
    return (hid_block.astype(jnp.float32) * slot_weights[None, :].astype(jnp.float32)).astype(
        jnp.bfloat16
    )


def project_score(row_block, weight, hid_block):
    proj = jnp.einsum("rd,hd->hr", row_block, weight, preferred_element_type=jnp.float32)
    return jnp.sum(hid_block.astype(jnp.float32) * proj, axis=0)


def local(grad_out, router_weights, expert_ids, hidden, master, moment, second):
    group = lax.axis_size("ep")
    tok_count = grad_out.shape[1]
    top_count = expert_ids.shape[2]
    width = grad_out.shape[2]
    slot_count = hidden.shape[3]
    capacity = slot_count // group
    token_grads = grad_out[0]
    token_weights = router_weights[0]
    routes = expert_ids[0]
    in_flight = routes < group
    slots = slot_ranks(routes, group)
    flat = jnp.where(in_flight, routes * capacity + slots, slot_count).reshape(-1)
    token_index = (
        jnp.arange(tok_count, dtype=jnp.int32)[:, None] + jnp.zeros_like(routes)
    ).reshape(-1)
    inverse = jnp.zeros((slot_count,), jnp.int32).at[flat].set(token_index, mode="drop")
    live = jnp.zeros((slot_count,), jnp.bool_).at[flat].set(True, mode="drop")
    slot_weight = (
        jnp.zeros((slot_count,), jnp.bfloat16).at[flat].set(token_weights.reshape(-1), mode="drop")
    )
    picked = jnp.where(
        live[:, None], jnp.take(token_grads, inverse, axis=0), jnp.zeros((), jnp.bfloat16)
    )
    picked = picked.reshape(group, capacity, width)
    received, received_weight = (
        lax.all_to_all(picked, "ep", split_axis=0, concat_axis=0, tiled=True),
        lax.all_to_all(
            slot_weight.reshape(group, capacity), "ep", split_axis=0, concat_axis=0, tiled=True
        ),
    )
    rows = received.reshape(slot_count, width)
    row_weights = received_weight.reshape(slot_count)
    hid_local = hidden[0, 0]
    param = master[0, 0]
    own_bf = param.astype(jnp.bfloat16)
    half = param.shape[1]
    lower = lax.axis_index("section") < lax.axis_size("section") // 2
    top_bit = lax.axis_size("section").bit_length() - 2
    partner_bf = swapped(own_bf, "section", top_bit)
    full_weights = jnp.where(
        lower, jnp.concatenate([own_bf, partner_bf], 1), jnp.concatenate([partner_bf, own_bf], 1)
    )
    score = project_score(rows, full_weights, hid_local)
    scaled = scale_hidden(hid_local, row_weights)
    grad = jnp.dot(scaled, rows, preferred_element_type=jnp.float32)
    own_grad = jnp.where(lower, grad[:, :half], grad[:, half:])
    outgoing = jnp.where(lower, grad[:, half:], grad[:, :half])
    incoming = swapped(outgoing, "section", top_bit)
    total = own_grad + incoming
    back = lax.all_to_all(
        score.reshape(group, capacity), "ep", split_axis=0, concat_axis=0, tiled=True
    )
    chosen = back.reshape(-1)[jnp.minimum(flat, slot_count - 1)]
    router = jnp.where(in_flight.reshape(-1), chosen, jnp.zeros_like(chosen)).reshape(
        tok_count, top_count
    )
    update = adam_update(
        total, param, moment[0, 0].astype(jnp.float32), second[0, 0].astype(jnp.float32)
    )
    return (update[None, None], router[None])


def solution(mesh):
    placed = (
        P("section", "ep", None),
        P("section", "ep", None),
        P("section", "ep", None),
        P("section", "ep", None, None),
        P("section", "ep", None, None),
        P("section", "ep", None, None),
        P("section", "ep", None, None),
    )
    return jax.shard_map(
        local,
        mesh=mesh,
        in_specs=placed,
        out_specs=(P("section", "ep", None, None), P("section", "ep", None)),
        check_vma=False,
    )
```

profile of v0, /device:TPU:0, one launch (start us, length us, event | category | flops | bytes accessed | tf_op | source)
XLA Modules:
  0.0 265.2 jit_solution(3669212825370743050)
XLA Ops:
  0.6 0.9 broadcast_multiply_fusion
  1.5 0.8 copy.24
  2.4 0.8 convert_reduce_fusion
  3.1 1.2 reduce-window.6
  4.8 0.7 select_reduce_fusion
  5.6 0.9 copy.27
  7.5 28.5 %scatter_custom_fusion = bf16[256]{0:T(256)(128)(2,1)S(1)} fusion(s32[4096]{0:T(1024)S(1)} %bitcast.58, bf16[4096]{0:T(1024)(128)(2,1)S(1)} %reshape.181, bf16[]{:T(256)} %constant.13.clone.1), kind=kCustom, calls=%fused_computation.56 | custom fusion | bytes 514 | tf_op jit(solution)/shard_map/scatter | solution.py:65
  36.7 6.3 %all-to-all-start = ((bf16[4,1,64]{2,1,0:T(2,128)(2,1)}), bf16[4,1,64]{2,1,0:T(2,128)(2,1)S(1)}, u32[]{:S(2)}, u32[]{:S(2)}) async-start(bf16[4,1,64]{2,1,0:T(2,128)(2,1)} %all_to_all.20), calls=%async_computation | async-start | bytes 4096 | tf_op jit(solution)/shard_map/all_to_all | solution.py:73
  43.2 15.5 %scatter_custom_fusion.2 = s32[256]{0:T(256)S(1)} fusion(s32[4096]{0:T(1024)S(1)} %bitcast.59, s32[4096]{0:T(1024)S(1)} %reshape.197, s32[]{:T(128)} %constant.27.clone.1), kind=kCustom, calls=%fused_computation.54 | custom fusion | bytes 1028 | tf_op jit(solution)/shard_map/scatter | solution.py:62
  58.8 17.6 %scatter_custom_fusion.1 = pred[256]{0:T(512)(128)(4,1)S(1)} fusion(s32[4096]{0:T(1024)S(1)} %bitcast.60, pred[4096]{0:T(1024)(128)(4,1)S(1)} %broadcast.120, pred[]{:T(512)} %constant.29.clone.1), kind=kCustom, calls=%fused_computation.52 | custom fusion | bytes 257 | tf_op jit(solution)/shard_map/scatter | solution.py:63
  76.6 1.4 gather_fusion
  77.9 1.2 select_select_fusion
  79.1 5.3 %all-to-all-start.1 = ((bf16[4,64,2048]{2,1,0:T(8,128)(2,1)}), bf16[4,64,2048]{2,1,0:T(8,128)(2,1)S(1)}, u32[]{:S(2)}, u32[]{:S(2)}) async-start(bf16[4,64,2048]{2,1,0:T(8,128)(2,1)} %select_select_fusion), calls=%async_computation.1 | async-start | bytes 2097152 | tf_op jit(solution)/shard_map/all_to_all | solution.py:72
  84.5 25.1 %all-to-all-done.1 = bf16[4,64,2048]{2,1,0:T(8,128)(2,1)S(1)} async-done(((bf16[4,64,2048]{2,1,0:T(8,128)(2,1)}), bf16[4,64,2048]{2,1,0:T(8,128)(2,1)S(1)}, u32[]{:S(2)}, u32[]{:S(2)}) %all-to-all-start.1) | async-done | bytes 1048608 | tf_op jit(solution)/shard_map/all_to_all | solution.py:72
  109.5 2.0 fusion.19
  111.5 2.6 slice_select_fusion
  114.2 1.5 copy-done.1
  115.7 1.5 collective-permute-start
  118.1 100.6 %collective-permute-done.1 = bf16[768,1024]{1,0:T(8,128)(2,1)S(1)} collective-permute-done((bf16[768,1024]{1,0:T(8,128)(2,1)S(1)}, bf16[768,1024]{1,0:T(8,128)(2,1)S(1)}, u32[]{:S(2)}, u32[]{:S(2)}) %collective-permute-start.1) | collective-permute-done | bytes 1572896 | tf_op jit(solution)/shard_map/ppermute | solution.py:15
  218.7 1.3 fusion.16
  220.6 3.2 %all-to-all-start.2 = ((f32[4,1,64]{2,1,0:T(1,128)}), f32[4,1,64]{2,1,0:T(1,128)S(1)}, u32[]{:S(2)}, u32[]{:S(2)}) async-start(f32[4,1,64]{2,1,0:T(1,128)} %all_to_all.18), calls=%async_computation.2 | async-start | bytes 4096 | tf_op jit(solution)/shard_map/all_to_all | solution.py:96
  223.9 5.4 %all-to-all-done.2 = f32[4,1,64]{2,1,0:T(1,128)S(1)} async-done(((f32[4,1,64]{2,1,0:T(1,128)}), f32[4,1,64]{2,1,0:T(1,128)S(1)}, u32[]{:S(2)}, u32[]{:S(2)}) %all-to-all-start.2) | async-done | bytes 1056 | tf_op jit(solution)/shard_map/all_to_all | solution.py:96
  230.5 25.7 %gather_fusion.1 = f32[4096]{0:T(1024)S(1)} fusion(f32[256]{0:T(256)S(1)} %reshape.158, s32[4096]{0:T(1024)S(1)} %broadcast_clamp_fusion), kind=kCustom, calls=%fused_computation.1 | custom fusion | bytes 49152 | tf_op jit(solution)/shard_map/gather | solution.py:99
  257.2 8.0 %fusion.13 = f32[1,1,768,1024]{3,2,1,0:T(8,128)} fusion(f32[1,1,768,1024]{3,2,1,0:T(8,128)} %param.11, bf16[1,1,768,1024]{3,2,1,0:T(8,128)(2,1)} %param.13, f32[768,1024]{1,0:T(8,128)} %collective-permute-done, bf16[1,1,768,1024]{3,2,1,0:T(8,128)(2,1)} %param.12, f32[768,2048]{1,0:T(8,128)} %copy-done.1, pred[]{:T(512)S(6)} %lt.54), kind=kLoop, calls=%fused_computation.21 | loop fusion | flops 13369344 | bytes 18874368 | tf_op jit(solution)/shard_map/broadcast_in_dim | solution.py:106
  (43 shorter events, 6.3 us)
Async XLA Ops:
  0.6 75.9 %copy-start = (bf16[1,512,2048]{2,1,0:T(8,128)(2,1)S(1)}, bf16[1,512,2048]{2,1,0:T(8,128)(2,1)}, u32[]{:S(2)}) copy-start(bf16[1,512,2048]{2,1,0:T(8,128)(2,1)} %param.7) | copy-start | bytes 6291460
  36.7 42.4 %all-to-all-start = ((bf16[4,1,64]{2,1,0:T(2,128)(2,1)}), bf16[4,1,64]{2,1,0:T(2,128)(2,1)S(1)}, u32[]{:S(2)}, u32[]{:S(2)}) async-start(bf16[4,1,64]{2,1,0:T(2,128)(2,1)} %all_to_all.20), calls=%async_computation | async-start | bytes 4096 | tf_op jit(solution)/shard_map/all_to_all | solution.py:73
  79.1 30.4 %all-to-all-start.1 = ((bf16[4,64,2048]{2,1,0:T(8,128)(2,1)}), bf16[4,64,2048]{2,1,0:T(8,128)(2,1)S(1)}, u32[]{:S(2)}, u32[]{:S(2)}) async-start(bf16[4,64,2048]{2,1,0:T(8,128)(2,1)} %select_select_fusion), calls=%async_computation.1 | async-start | bytes 2097152 | tf_op jit(solution)/shard_map/all_to_all | solution.py:72
  111.5 4.2 %copy-start.1 = (f32[768,2048]{1,0:T(8,128)}, f32[768,2048]{1,0:T(8,128)S(1)}, u32[]{:S(2)}) copy-start(f32[768,2048]{1,0:T(8,128)S(1)} %fusion.19) | copy-start | bytes 18874372
  111.5 5.7 %copy-start.2 = (f32[1,1,768,1024]{3,2,1,0:T(8,128)S(1)}, f32[1,1,768,1024]{3,2,1,0:T(8,128)}, u32[]{:S(2)}) copy-start(f32[1,1,768,1024]{3,2,1,0:T(8,128)} %param.11) | copy-start | bytes 9437188
  115.7 103.0 %copy-start.3 = (bf16[1,1,768,256]{3,2,1,0:T(8,128)(2,1)S(1)}, bf16[1,1,768,256]{3,2,1,0:T(8,128)(2,1)}, u32[]{:S(2)}) copy-start(bf16[1,1,768,256]{3,2,1,0:T(8,128)(2,1)} %param.10) | copy-start | bytes 1179652
  115.7 141.5 %collective-permute-start = (f32[768,1024]{1,0:T(8,128)}, f32[768,1024]{1,0:T(8,128)}, u32[]{:S(2)}, u32[]{:S(2)}) collective-permute-start(f32[768,1024]{1,0:T(8,128)} %slice_select_fusion), channel_id=1, source_target_pairs={{0,16},{4,20},{8,24},{12,28},{16,0},{20,4},{24,8},{28,12},{1,17},{... | collective-permute-start | bytes 9437192 | tf_op jit(solution)/shard_map/ppermute | solution.py:15
  117.5 101.2 %collective-permute-start.1 = (bf16[768,1024]{1,0:T(8,128)(2,1)S(1)}, bf16[768,1024]{1,0:T(8,128)(2,1)S(1)}, u32[]{:S(2)}, u32[]{:S(2)}) collective-permute-start(bf16[768,1024]{1,0:T(8,128)(2,1)S(1)} %convert_bitcast_fusion), channel_id=1, source_target_pairs={{0,16},{4,20},{8,24},{12,28},{16,0},{20,4},{24,8},{28,12},{1,17},{... | collective-permute-start | bytes 4718600 | tf_op jit(solution)/shard_map/ppermute | solution.py:15
  220.6 8.7 %all-to-all-start.2 = ((f32[4,1,64]{2,1,0:T(1,128)}), f32[4,1,64]{2,1,0:T(1,128)S(1)}, u32[]{:S(2)}, u32[]{:S(2)}) async-start(f32[4,1,64]{2,1,0:T(1,128)} %all_to_all.18), calls=%async_computation.2 | async-start | bytes 4096 | tf_op jit(solution)/shard_map/all_to_all | solution.py:96
where the time goes:
time: 266 us; the launch traced here: 265 us
  waiting for transfers between devices  131 us (49%)
  local copies, waits for them, and re-layouts  96.4 us (36%)
  starting transfers between devices  16.9 us (6%)
  other arithmetic  16.7 us (6%)
  matrix products  3.24 us (1%)
    ppermute x2, waiting for transfers between devices, swapped(): lax.ppermute(array, axis, [(i, i ^ 1 << distance) for i in range(lax.axis...  101 us
    scatter x1, local copies, waits for them, and re-layouts, local(): jnp.zeros((slot_count,), jnp.bfloat16).at[flat]  28.5 us
    gather x2, local copies, waits for them, and re-layouts, local(): chosen = back.reshape(-1)[jnp.minimum(flat, slot_count - 1)]  25.9 us
    all_to_all x1, waiting for transfers between devices, local(): lax.all_to_all(picked, 'ep', split_axis=0, concat_axis=0, tiled=True)  25.1 us
    scatter x1, local copies, waits for them, and re-layouts, local(): live = jnp.zeros((slot_count,), jnp.bool_).at[flat].set(True, mode='drop')  17.6 us
    scatter x1, local copies, waits for them, and re-layouts, local(): jnp.zeros((slot_count,), jnp.int32).at[flat].set(token_index, mode='drop')  15.5 us
    broadcast_in_dim x1, other arithmetic, local(): return (update[None, None], router[None])  7.97 us
    all_to_all x1, starting transfers between devices, local(): lax.all_to_all(slot_weight.reshape(group, capacity), 'ep', split_axis=0,...  6.32 us
  transfers between devices with their start and end apart: 5, of which 3 were waited for; matrix products, arithmetic and copies ran while one was open for 25% of the time, Pallas kernels for 0%

commit v1 on v0

v1 whole, which is shorter than its diff:
```python
import functools

import jax
import jax.numpy as jnp
from jax import lax
from jax.experimental import pallas as pl
from jax.experimental.pallas import tpu as pltpu
from jax.sharding import PartitionSpec as P

beta_first = 0.9
beta_second = 0.95
adam_eps = 1e-08
decay_rate = 0.1
first_fix = 1.0 - 0.9**10
second_fix = 1.0 - 0.95**10

LANES = 128
TILE = 16
VMEM_BYTES = 48 * 1024 * 1024
F32 = jnp.float32
BF16 = jnp.bfloat16


def params(**kwargs):
    return pltpu.CompilerParams(vmem_limit_bytes=VMEM_BYTES, **kwargs)


def vmem_specs(count):
    return [pl.BlockSpec(memory_space=pltpu.VMEM) for _ in range(count)]


def own_half():
    sections = lax.axis_size("section")
    return jnp.where(lax.axis_index("section") < sections // 2, 0, 1).astype(jnp.int32)


def route_kernel(group, cap, ids_ref, weight_ref, grads_ref, slots_ref, *rest):
    chunks, (held, sems) = rest[: 2 * group], rest[2 * group :]
    tokens, half = held.shape[1], held.shape[2]
    me = lax.axis_index("ep").astype(jnp.int32)
    mine = own_half()
    copies = []
    for turn in range(2):
        side = 1 - mine if turn == 0 else mine
        columns = pl.ds(pl.multiple_of(side * half, half), half)
        copy = pltpu.make_async_copy(grads_ref.at[:, columns], held.at[turn], sems.at[turn])
        copy.start()
        copies.append(copy)
    ids = ids_ref[...]
    weights = weight_ref[...].astype(F32)
    members, scales = [], []
    for k in range(group):
        named = ids == (me ^ k)
        members.append(jnp.sum(jnp.where(named, 1.0, 0.0), axis=0, keepdims=True))
        scales.append(jnp.sum(jnp.where(named, weights, 0.0), axis=0, keepdims=True))
    member = jnp.concatenate(
        members + [jnp.zeros((-group % TILE, tokens), F32)] if group % TILE else members, axis=0
    )
    earlier = lax.broadcasted_iota(jnp.int32, (tokens, tokens), 0)
    later = lax.broadcasted_iota(jnp.int32, (tokens, tokens), 1)
    ahead = jnp.where(earlier < later, 1.0, 0.0).astype(BF16)
    before = jnp.dot(member.astype(BF16), ahead, preferred_element_type=F32)
    slots = jnp.where(member > 0.5, before, -1.0)
    slots_ref[...] = slots
    place = lax.broadcasted_iota(jnp.int32, (cap, tokens), 0).astype(F32)
    picks = [
        jnp.where(place == slots[k : k + 1, :], 1.0, 0.0).astype(BF16) for k in range(group)
    ]
    base = me * cap
    tile_row = lax.broadcasted_iota(jnp.int32, (TILE, LANES), 0)
    tile_lane = lax.broadcasted_iota(jnp.int32, (TILE, LANES), 1)
    kept = (tile_row * LANES + tile_lane >= base) & (tile_row * LANES + tile_lane < base + cap)
    data_rows = half // LANES * cap
    for k in range(group):
        spread = jnp.broadcast_to(scales[k], (TILE, tokens)).astype(BF16)
        doubled = jnp.concatenate([picks[k]] * (LANES // cap), axis=0)
        tile = lax.dot_general(
            spread, doubled, (((1,), (1,)), ((), ())), preferred_element_type=F32
        )
        tile = jnp.where(kept, tile, 0.0).astype(BF16)
        for turn in range(2):
            chunks[turn * group + k][data_rows:, :] = tile
    pick = jnp.concatenate(picks, axis=0)
    step = min(half, 2 * LANES)
    for turn in range(2):
        copies[turn].wait()
        for column in range(0, half, step):
            block = jnp.dot(
                pick, held[turn, :, column : column + step], preferred_element_type=F32
            ).astype(BF16)
            for k in range(group):
                for part in range(step // LANES):
                    at = (column // LANES + part) * cap
                    chunks[turn * group + k][at : at + cap, :] = block[
                        k * cap : (k + 1) * cap, part * LANES : (part + 1) * LANES
                    ]


def inner_kernel(own_ref, other_ref, master_ref, inner_ref):
    weights = master_ref[...].astype(BF16)
    slots = own_ref.shape[1]
    for at, ref in ((0, own_ref), (slots, other_ref)):
        inner_ref[at : at + slots, :] = lax.dot_general(
            ref[...], weights, (((0,), (0,)), ((), ())), preferred_element_type=F32
        )


def score_kernel(group, cap, inner_ref, *rest):
    chunks, outs = rest[: 2 * group], rest[2 * group :]
    slots = group * cap
    blocks = inner_ref.shape[1] // LANES
    me = lax.axis_index("ep").astype(jnp.int32)
    for k in range(group):
        sums = []
        for side in range(2):
            start = pl.multiple_of(side * slots + (me ^ k) * cap, cap)
            total = jnp.zeros((cap, LANES), F32)
            for block in range(blocks):
                rows = chunks[side * group + k][block * cap : (block + 1) * cap, :].astype(F32)
                total += rows * inner_ref[
                    pl.ds(start, cap), block * LANES : (block + 1) * LANES
                ]
            sums.append(total)
        both = jnp.concatenate(sums, axis=0)
        line = jnp.sum(both.T, axis=0, keepdims=True)
        outs[k][...] = jnp.broadcast_to(line, outs[k].shape)


def update_kernel(
    group, cap, own_ref, other_ref, master_ref, moment_ref, second_ref, *rest
):
    chunks, (update_ref, rows, scales) = rest[: 2 * group], rest[2 * group :]
    slots = group * cap
    half = rows.shape[1]
    data_rows = half // LANES * cap
    me = lax.axis_index("ep").astype(jnp.int32)

    @pl.when(pl.program_id(0) == 0)
    def _():
        for side in range(2):
            tile = jnp.zeros((TILE, LANES), F32)
            for k in range(group):
                chunk = chunks[side * group + k]
                tile += chunk[data_rows:, :].astype(F32)
                start = pl.multiple_of(side * slots + (me ^ k) * cap, cap)
                for block in range(half // LANES):
                    rows[pl.ds(start, cap), block * LANES : (block + 1) * LANES] = chunk[
                        block * cap : (block + 1) * cap, :
                    ]
            scales[side] = tile

    parts = []
    for side, ref in enumerate((own_ref, other_ref)):
        for part in range(slots // LANES):
            hidden = ref[:, part * LANES : (part + 1) * LANES].astype(F32)
            parts.append((hidden * scales[side, part : part + 1, :]).astype(BF16))
    scaled = jnp.concatenate(parts, axis=1)
    total = jnp.dot(scaled, rows[...], preferred_element_type=F32)
    first = beta_first * moment_ref[...].astype(F32) + (1.0 - beta_first) * total
    second = beta_second * second_ref[...].astype(F32) + (1.0 - beta_second) * total * total
    update_ref[...] = (first * (1.0 / first_fix)) / (
        jnp.sqrt(second * (1.0 / second_fix)) + adam_eps
    ) + decay_rate * master_ref[...]


def combine_kernel(group, cap, ids_ref, slots_ref, *rest):
    own, other, out_ref = rest[:group], rest[group : 2 * group], rest[2 * group]
    tokens = ids_ref.shape[1]
    me = lax.axis_index("ep").astype(jnp.int32)
    lane = lax.broadcasted_iota(jnp.int32, (1, LANES), 1)
    lines = [
        jnp.where(lane < cap, own[k][0:1, :], other[k][0:1, :]) for k in range(group)
    ]
    lines.append(jnp.zeros((LANES - group, LANES), F32))
    columns = jnp.concatenate(lines, axis=0).T
    columns = columns[:cap] + columns[cap : 2 * cap]
    place = lax.broadcasted_iota(jnp.int32, (cap, tokens), 0).astype(F32)
    ids = ids_ref[...]
    result = jnp.zeros(ids.shape, F32)
    for k in range(group):
        at_slot = jnp.where(place == slots_ref[k : k + 1, :], columns[:, k : k + 1], 0.0)
        chosen = jnp.sum(at_slot, axis=0, keepdims=True)
        result = jnp.where(ids == (me ^ k), chosen, result)
    out_ref[...] = result


def moved(array, flip, step):
    sections, group = lax.axis_size("section"), lax.axis_size("ep")
    pairs = []
    for s in range(sections):
        target = (s + sections // 2) % sections if flip else s
        for e in range(group):
            pairs.append((s * group + e, target * group + (e ^ step)))
    return lax.ppermute(array, ("section", "ep"), pairs)


def cost(flops, touched):
    return pl.CostEstimate(flops=int(flops), bytes_accessed=int(touched), transcendentals=0)


def local(grad_out, router_weights, expert_ids, hidden, master, moment, second):
    group = lax.axis_size("ep")
    tokens, width = grad_out.shape[1:]
    top = expert_ids.shape[2]
    hid, slots = hidden.shape[2:]
    half = master.shape[3]
    cap = slots // group
    ids = expert_ids[0].T
    weights = router_weights[0].T
    own_hidden = hidden[0, 0]
    param = master[0, 0]
    other_hidden = moved(own_hidden, True, 0)

    chunk_shape = jax.ShapeDtypeStruct((half // LANES * cap + TILE, LANES), BF16)
    slot_rows = group + -group % TILE
    routed = pl.pallas_call(
        functools.partial(route_kernel, group, cap),
        out_shape=[jax.ShapeDtypeStruct((slot_rows, tokens), F32)] + [chunk_shape] * (2 * group),
        in_specs=vmem_specs(2) + [pl.BlockSpec(memory_space=pl.ANY)],
        out_specs=vmem_specs(1 + 2 * group),
        scratch_shapes=[
            pltpu.VMEM((2, tokens, half), BF16),
            pltpu.SemaphoreType.DMA((2,)),
        ],
        compiler_params=params(),
        cost_estimate=cost(2 * slots * tokens * width, 2 * (tokens + slots) * width),
        name="route",
    )(ids, weights, grad_out[0])
    slot_of, sent = routed[0], routed[1:]
    order = sorted(range(group), key=lambda k: -k)
    arrived = {}
    for k in order:
        for side in (1, 0):
            source = sent[k] if side else sent[group + k]
            arrived[side, k] = source if not side and k == 0 else moved(source, side == 1, k)
    chunks = [arrived[side, k] for side in range(2) for k in range(group)]

    inner = pl.pallas_call(
        inner_kernel,
        out_shape=jax.ShapeDtypeStruct((2 * slots, half), F32),
        in_specs=vmem_specs(3),
        out_specs=vmem_specs(1)[0],
        compiler_params=params(),
        cost_estimate=cost(4 * slots * hid * half, 4 * hid * half + 8 * slots * half),
        name="inner",
    )(own_hidden, other_hidden, param)
    scores = pl.pallas_call(
        functools.partial(score_kernel, group, cap),
        out_shape=[jax.ShapeDtypeStruct((8, LANES), F32)] * group,
        in_specs=vmem_specs(1 + 2 * group),
        out_specs=vmem_specs(group),
        compiler_params=params(),
        cost_estimate=cost(4 * slots * half, 12 * slots * half),
        name="score",
    )(inner, *chunks)
    own_scores = [scores[k] if k == 0 else moved(scores[k], False, k) for k in range(group)]
    other_scores = [moved(scores[k], True, k) for k in range(group)]

    block = LANES
    tile = pl.BlockSpec((block, half), lambda i: (i, 0))
    hidden_tile = pl.BlockSpec((block, slots), lambda i: (i, 0))
    whole = pl.BlockSpec(chunk_shape.shape, lambda i: (0, 0))
    update = pl.pallas_call(
        functools.partial(update_kernel, group, cap),
        out_shape=jax.ShapeDtypeStruct((hid, half), F32),
        grid=(hid // block,),
        in_specs=[hidden_tile, hidden_tile, tile, tile, tile] + [whole] * (2 * group),
        out_specs=tile,
        scratch_shapes=[
            pltpu.VMEM((2 * slots, half), BF16),
            pltpu.VMEM((2, TILE, LANES), F32),
        ],
        compiler_params=params(),
        cost_estimate=cost(4 * slots * hid * half, 12 * hid * half + 4 * slots * half),
        name="update",
    )(own_hidden, other_hidden, param, moment[0, 0], second[0, 0], *chunks)
    router = pl.pallas_call(
        functools.partial(combine_kernel, group, cap),
        out_shape=jax.ShapeDtypeStruct((top, tokens), F32),
        in_specs=vmem_specs(2 + 2 * group),
        out_specs=vmem_specs(1)[0],
        compiler_params=params(),
        cost_estimate=cost(4 * slots * tokens, 8 * top * tokens),
        name="combine",
    )(ids, slot_of, *own_scores, *other_scores)
    return (update[None, None], router.T[None])


def solution(mesh):
    placed = (
        P("section", "ep", None),
        P("section", "ep", None),
        P("section", "ep", None),
        P("section", "ep", None, None),
        P("section", "ep", None, None),
        P("section", "ep", None, None),
        P("section", "ep", None, None),
    )
    return jax.shard_map(
        local,
        mesh=mesh,
        in_specs=placed,
        out_specs=(P("section", "ep", None, None), P("section", "ep", None)),
        check_vma=False,
    )
```

time: 266 us -> 54.4 us (0.20)
  waiting for transfers between devices: 131 us -> 14.9 us
  local copies, waits for them, and re-layouts: 96.4 us -> 4.91 us
  other arithmetic: 16.7 us -> 0 us
  Pallas kernels: 0 us -> 10.8 us
  starting transfers between devices: 16.9 us -> 22.7 us
  matrix products: 3.24 us -> 0 us
    ppermute x2 -> x15, waiting for transfers between devices: 101 us -> 14.9 us  [moved(): return lax.ppermute(array, ('section', 'ep'), pairs)]
    scatter x3 -> x0, local copies, waits for them, and re-layouts: 61.7 us -> none  [the longest x1 28.5 us: local(): jnp.zeros((slot_count,), jnp.bfloat16).at[flat]]
    all_to_all x3 -> x0, waiting for transfers between devices: 30.5 us -> none  [the longest x1 25.1 us: local(): lax.all_to_all(picked, 'ep', split_axis=0, concat_axis=0, tiled=True)]
    gather x3 -> x0, local copies, waits for them, and re-layouts: 27.3 us -> none  [the longest x2 25.9 us: local(): chosen = back.reshape(-1)[jnp.minimum(flat, slot_count - 1)]]
    ppermute x2 -> x15, starting transfers between devices: 2.09 us -> 22.7 us  [moved(): return lax.ppermute(array, ('section', 'ep'), pairs)]
    all_to_all x3 -> x0, starting transfers between devices: 14.8 us -> none  [the longest x1 6.32 us: local(): lax.all_to_all(slot_weight.reshape(group, capacity), 'ep', split_axis=0,...]
    pallas_call x0 -> x5, Pallas kernels: none -> 10.8 us  [the longest x1 7.02 us: local(): pl.pallas_call(functools.partial(update_kernel, group, cap), out_shape=ja...]
    broadcast_in_dim x1 -> x0, other arithmetic: 7.97 us -> none  [local(): return (update[None, None], router[None])]
  transfers between devices with their start and end apart: 5 -> 15, of which waited for: 3 -> 3; matrix products, arithmetic and copies ran while one was open for 25% -> 0% of each run, Pallas kernels for 0% -> 18%
where the time goes in v1:
time: 54.4 us; the launch traced here: 54 us
  starting transfers between devices  22.7 us (42%)
  waiting for transfers between devices  14.9 us (27%)
  Pallas kernels  10.8 us (20%)
  local copies, waits for them, and re-layouts  4.91 us (9%)
  between operations  0.73 us (1%)
    ppermute x15, starting transfers between devices, moved(): return lax.ppermute(array, ('section', 'ep'), pairs)  22.7 us
    ppermute x15, waiting for transfers between devices, moved(): return lax.ppermute(array, ('section', 'ep'), pairs)  14.9 us
    pallas_call x1, Pallas kernels, local(): pl.pallas_call(functools.partial(update_kernel, group, cap), out_shape=ja...  7.02 us
    unnamed x16, local copies, waits for them, and re-layouts  4.91 us
    pallas_call x1, Pallas kernels, local(): pl.pallas_call(functools.partial(route_kernel, group, cap), out_shape=[ja...  1.6 us
  transfers between devices with their start and end apart: 15, of which 3 were waited for; matrix products, arithmetic and copies ran while one was open for 0% of the time, Pallas kernels for 18%

profile of v1, /device:TPU:0, one launch (start us, length us, event | category | flops | bytes accessed | tf_op | source)
XLA Modules:
  0.0 54.0 jit_solution(15535531019391910713)
XLA Ops:
  0.6 3.0 %collective-permute-start = (bf16[768,256]{1,0:T(8,128)(2,1)}, bf16[768,256]{1,0:T(8,128)(2,1)S(1)}, u32[]{:S(2)}, u32[]{:S(2)}) collective-permute-start(bf16[768,256]{1,0:T(8,128)(2,1)} %bitcast.18), channel_id=1, source_target_pairs={{0,16},{1,17},{2,18},{3,19},{4,20},{5,21},{6,22},{7,23},{8,24},{9,... | collective-permute-start | bytes 1179656 | tf_op jit(solution)/shard_map/ppermute | solution.py:194
  3.7 1.6 %copy-done.1 = bf16[1,512,2048]{2,1,0:T(8,128)(2,1)S(1)} copy-done((bf16[1,512,2048]{2,1,0:T(8,128)(2,1)S(1)}, bf16[1,512,2048]{2,1,0:T(8,128)(2,1)}, u32[]{:S(2)}) %copy-start.1) | copy-done | bytes 2097176
  5.3 0.7 %copy-done.5 = s32[1,512,8]{1,2,0:T(8,128)S(1)} copy-done((s32[1,512,8]{1,2,0:T(8,128)S(1)}, s32[1,512,8]{1,2,0:T(8,128)}, u32[]{:S(2)}) %copy-start.5) | copy-done | bytes 16408
  6.0 0.7 %copy-done.7 = bf16[1,512,8]{1,2,0:T(8,128)(2,1)S(1)} copy-done((bf16[1,512,8]{1,2,0:T(8,128)(2,1)S(1)}, bf16[1,512,8]{1,2,0:T(8,128)(2,1)}, u32[]{:S(2)}) %copy-start.7) | copy-done | bytes 8216
  6.7 1.6 %route.1 = (f32[16,512]{1,0:T(8,128)S(1)}, bf16[528,128]{1,0:T(8,128)(2,1)S(1)}, bf16[528,128]{1,0:T(8,128)(2,1)S(1)}, bf16[528,128]{1,0:T(8,128)(2,1)S(1)}, bf1...) custom-call(s32[8,512]{1,0:T(8,128)S(1)} %bitcast.23, ...), custom_call_target="tpu_custom_call" | custom-call | flops 536870912 | bytes 3145728 | tf_op jit(solution)/shard_map/route/pallas_call | solution.py:216
  8.3 1.6 %collective-permute-start.1 = (bf16[528,128]{1,0:T(8,128)(2,1)S(1)}, bf16[528,128]{1,0:T(8,128)(2,1)S(1)}, u32[]{:S(2)}, u32[]{:S(2)}) collective-permute-start(bf16[528,128]{1,0:T(8,128)(2,1)S(1)} %get-tuple-element.16), channel_id=1, source_target_pairs={{0,1},{1,0},{2,3},{3,2},{4,5},{5,4},{6,7},{7,6},{8,9},{9,8},{10,11... | collective-permute-start | bytes 405512 | tf_op jit(solution)/shard_map/ppermute | solution.py:194
  9.9 2.6 %collective-permute-start.2 = (bf16[528,128]{1,0:T(8,128)(2,1)S(1)}, bf16[528,128]{1,0:T(8,128)(2,1)S(1)}, u32[]{:S(2)}, u32[]{:S(2)}) collective-permute-start(bf16[528,128]{1,0:T(8,128)(2,1)S(1)} %get-tuple-element.17), channel_id=1, source_target_pairs={{0,2},{1,3},{2,0},{3,1},{4,6},{5,7},{6,4},{7,5},{8,10},{9,11},{10,... | collective-permute-start | bytes 405512 | tf_op jit(solution)/shard_map/ppermute | solution.py:194
  12.5 0.2 collective-permute-start.3
  12.7 0.3 collective-permute-start.4
  13.0 1.9 %collective-permute-done.1.rest_1_ = bf16[528,128]{1,0:T(8,128)(2,1)S(1)} collective-permute-done((bf16[528,128]{1,0:T(8,128)(2,1)S(1)}, bf16[528,128]{1,0:T(8,128)(2,1)S(1)}, u32[]{:S(2)}, u32[]{:S(2)}) %collective-permute-start.1) | collective-permute-done | bytes 135200 | tf_op jit(solution)/shard_map/ppermute | solution.py:194
  15.0 0.6 %collective-permute-start.5 = (bf16[528,128]{1,0:T(8,128)(2,1)S(1)}, bf16[528,128]{1,0:T(8,128)(2,1)S(1)}, u32[]{:S(2)}, u32[]{:S(2)}) collective-permute-start(bf16[528,128]{1,0:T(8,128)(2,1)S(1)} %get-tuple-element.20), channel_id=1, source_target_pairs={{0,17},{1,16},{2,19},{3,18},{4,21},{5,20},{6,23},{7,22},{8,25},{9,... | collective-permute-start | bytes 405512 | tf_op jit(solution)/shard_map/ppermute | solution.py:194
  15.5 7.7 %collective-permute-done.2.rest_2_ = bf16[528,128]{1,0:T(8,128)(2,1)S(1)} collective-permute-done((bf16[528,128]{1,0:T(8,128)(2,1)S(1)}, bf16[528,128]{1,0:T(8,128)(2,1)S(1)}, u32[]{:S(2)}, u32[]{:S(2)}) %collective-permute-start.2) | collective-permute-done | bytes 135200 | tf_op jit(solution)/shard_map/ppermute | solution.py:194
  23.2 3.0 %collective-permute-start.7 = (bf16[528,128]{1,0:T(8,128)(2,1)S(1)}, bf16[528,128]{1,0:T(8,128)(2,1)S(1)}, u32[]{:S(2)}, u32[]{:S(2)}) collective-permute-start(bf16[528,128]{1,0:T(8,128)(2,1)S(1)} %get-tuple-element.22), channel_id=1, source_target_pairs={{0,19},{1,18},{2,17},{3,16},{4,23},{5,22},{6,21},{7,20},{8,27},{9,... | collective-permute-start | bytes 405512 | tf_op jit(solution)/shard_map/ppermute | solution.py:194
  26.2 1.9 %copy-done = f32[1,1,768,1024]{3,2,1,0:T(8,128)S(1)} copy-done((f32[1,1,768,1024]{3,2,1,0:T(8,128)S(1)}, f32[1,1,768,1024]{3,2,1,0:T(8,128)}, u32[]{:S(2)}) %copy-start) | copy-done | bytes 3145752
  28.1 1.0 %inner.1.inner_ref = f32[512,1024]{1,0:T(8,128)S(1)} custom-call(bf16[768,256]{1,0:T(8,128)(2,1)S(1)} %bitcast.19, bf16[768,256]{1,0:T(8,128)(2,1)S(1)} %collective-permute-done.other_ref, f32[768,1024]{1,0:T(8,128)S(1)} %bitcast.16), custom_call_target="tpu_custom_call" | custom-call | flops 805306368 | bytes 5242880 | tf_op jit(solution)/shard_map/inner/pallas_call | solution.py:238
  29.2 5.2 %collective-permute-done.6.rest_6_ = bf16[528,128]{1,0:T(8,128)(2,1)S(1)} collective-permute-done((bf16[528,128]{1,0:T(8,128)(2,1)S(1)}, bf16[528,128]{1,0:T(8,128)(2,1)S(1)}, u32[]{:S(2)}, u32[]{:S(2)}) %collective-permute-start.6) | collective-permute-done | bytes 135200 | tf_op jit(solution)/shard_map/ppermute | solution.py:194
  34.4 0.3 score.1
  34.7 1.6 %collective-permute-start.11 = (f32[8,128]{1,0:T(8,128)S(1)}, f32[8,128]{1,0:T(8,128)S(1)}, u32[]{:S(2)}, u32[]{:S(2)}) collective-permute-start(f32[8,128]{1,0:T(8,128)S(1)} %get-tuple-element.24.rest_0_), channel_id=1, source_target_pairs={{0,16},{1,17},{2,18},{3,19},{4,20},{5,21},{6,22},{7,23},{8,24},{9,... | collective-permute-start | bytes 12296 | tf_op jit(solution)/shard_map/ppermute | solution.py:194
  36.3 2.0 %collective-permute-start.12 = (f32[8,128]{1,0:T(8,128)S(1)}, f32[8,128]{1,0:T(8,128)S(1)}, u32[]{:S(2)}, u32[]{:S(2)}) collective-permute-start(f32[8,128]{1,0:T(8,128)S(1)} %get-tuple-element.25), channel_id=1, source_target_pairs={{0,17},{1,16},{2,19},{3,18},{4,21},{5,20},{6,23},{7,22},{8,25},{9,... | collective-permute-start | bytes 12296 | tf_op jit(solution)/shard_map/ppermute | solution.py:194
  38.3 3.9 %collective-permute-start.13 = (f32[8,128]{1,0:T(8,128)S(1)}, f32[8,128]{1,0:T(8,128)S(1)}, u32[]{:S(2)}, u32[]{:S(2)}) collective-permute-start(f32[8,128]{1,0:T(8,128)S(1)} %get-tuple-element.26), channel_id=1, source_target_pairs={{0,18},{1,19},{2,16},{3,17},{4,22},{5,23},{6,20},{7,21},{8,26},{9,... | collective-permute-start | bytes 12296 | tf_op jit(solution)/shard_map/ppermute | solution.py:194
  42.3 2.4 %collective-permute-start.14 = (f32[8,128]{1,0:T(8,128)S(1)}, f32[8,128]{1,0:T(8,128)S(1)}, u32[]{:S(2)}, u32[]{:S(2)}) collective-permute-start(f32[8,128]{1,0:T(8,128)S(1)} %get-tuple-element.27), channel_id=1, source_target_pairs={{0,19},{1,18},{2,17},{3,16},{4,23},{5,22},{6,21},{7,20},{8,27},{9,... | collective-permute-start | bytes 12296 | tf_op jit(solution)/shard_map/ppermute | solution.py:194
  44.6 1.5 %collective-permute-start.10 = (f32[8,128]{1,0:T(8,128)S(1)}, f32[8,128]{1,0:T(8,128)S(1)}, u32[]{:S(2)}, u32[]{:S(2)}) collective-permute-start(f32[8,128]{1,0:T(8,128)S(1)} %get-tuple-element.27), channel_id=1, source_target_pairs={{0,3},{1,2},{2,1},{3,0},{4,7},{5,6},{6,5},{7,4},{8,11},{9,10},{10,... | collective-permute-start | bytes 12296 | tf_op jit(solution)/shard_map/ppermute | solution.py:194
  46.1 7.0 %update.1 = f32[768,1024]{1,0:T(8,128)} custom-call(bf16[768,256]{1,0:T(8,128)(2,1)S(1)} %bitcast.20, bf16[768,256]{1,0:T(8,128)(2,1)S(1)} %collective-permute-done.other_ref, f32[768,1024]{1,0:T(8,128)} %bitcast.15, bf16[768,1024]{1,0:T(8,128)(2,1)S(1)} %bitcast.21, bf16[768,1024]{1,0:T(8,128)(2,1)S(1)} %bitcast.22, ...), custom_call_target="tpu_custom_call" | custom-call | flops 805306368 | bytes 10485760 | tf_op jit(solution)/shard_map/update/pallas_call | solution.py:263
  53.2 0.9 %combine.1 = f32[8,512]{1,0:T(8,128)} custom-call(s32[8,512]{1,0:T(8,128)S(1)} %bitcast.24, f32[16,512]{1,0:T(8,128)S(1)} %get-tuple-element.23.slots_ref, f32[8,128]{1,0:T(8,128)S(1)} %get-tuple-element.24.rest_0_, f32[8,128]{1,0:T(8,128)S(1)} %collective-permute-done.8.rest_1_, f32[8,128]{1,0:T(8,128)S(1)} %collective-permute-done.9.rest_2_, ...), custom_call_target="tpu_custom_call" | custom-call | flops 524288 | bytes 32768 | tf_op jit(solution)/shard_map/combine/pallas_call | solution.py:277
  (27 shorter events, 0.1 us)
Async XLA Ops:
  0.6 22.6 %collective-permute-start = (bf16[768,256]{1,0:T(8,128)(2,1)}, bf16[768,256]{1,0:T(8,128)(2,1)S(1)}, u32[]{:S(2)}, u32[]{:S(2)}) collective-permute-start(bf16[768,256]{1,0:T(8,128)(2,1)} %bitcast.18), channel_id=1, source_target_pairs={{0,16},{1,17},{2,18},{3,19},{4,20},{5,21},{6,22},{7,23},{8,24},{9,... | collective-permute-start | bytes 1179656 | tf_op jit(solution)/shard_map/ppermute | solution.py:194
  3.7 1.6 %copy-start.1 = (bf16[1,512,2048]{2,1,0:T(8,128)(2,1)S(1)}, bf16[1,512,2048]{2,1,0:T(8,128)(2,1)}, u32[]{:S(2)}) copy-start(bf16[1,512,2048]{2,1,0:T(8,128)(2,1)} %param.7) | copy-start | bytes 6291460
  5.3 0.7 %copy-start.5 = (s32[1,512,8]{1,2,0:T(8,128)S(1)}, s32[1,512,8]{1,2,0:T(8,128)}, u32[]{:S(2)}) copy-start(s32[1,512,8]{1,2,0:T(8,128)} %param.9) | copy-start | bytes 49156
  6.0 0.7 %copy-start.7 = (bf16[1,512,8]{1,2,0:T(8,128)(2,1)S(1)}, bf16[1,512,8]{1,2,0:T(8,128)(2,1)}, u32[]{:S(2)}) copy-start(bf16[1,512,8]{1,2,0:T(8,128)(2,1)} %param.8) | copy-start | bytes 24580
  6.7 19.5 %copy-start.2 = (bf16[1,1,768,256]{3,2,1,0:T(8,128)(2,1)S(1)}, bf16[1,1,768,256]{3,2,1,0:T(8,128)(2,1)}, u32[]{:S(2)}) copy-start(bf16[1,1,768,256]{3,2,1,0:T(8,128)(2,1)} %param.10) | copy-start | bytes 1179652
  8.3 6.7 %collective-permute-start.1 = (bf16[528,128]{1,0:T(8,128)(2,1)S(1)}, bf16[528,128]{1,0:T(8,128)(2,1)S(1)}, u32[]{:S(2)}, u32[]{:S(2)}) collective-permute-start(bf16[528,128]{1,0:T(8,128)(2,1)S(1)} %get-tuple-element.16), channel_id=1, source_target_pairs={{0,1},{1,0},{2,3},{3,2},{4,5},{5,4},{6,7},{7,6},{8,9},{9,8},{10,11... | collective-permute-start | bytes 405512 | tf_op jit(solution)/shard_map/ppermute | solution.py:194
  9.9 13.3 %collective-permute-start.2 = (bf16[528,128]{1,0:T(8,128)(2,1)S(1)}, bf16[528,128]{1,0:T(8,128)(2,1)S(1)}, u32[]{:S(2)}, u32[]{:S(2)}) collective-permute-start(bf16[528,128]{1,0:T(8,128)(2,1)S(1)} %get-tuple-element.17), channel_id=1, source_target_pairs={{0,2},{1,3},{2,0},{3,1},{4,6},{5,7},{6,4},{7,5},{8,10},{9,11},{10,... | collective-permute-start | bytes 405512 | tf_op jit(solution)/shard_map/ppermute | solution.py:194
  12.5 16.6 %collective-permute-start.3 = (bf16[528,128]{1,0:T(8,128)(2,1)S(1)}, bf16[528,128]{1,0:T(8,128)(2,1)S(1)}, u32[]{:S(2)}, u32[]{:S(2)}) collective-permute-start(bf16[528,128]{1,0:T(8,128)(2,1)S(1)} %get-tuple-element.18), channel_id=1, source_target_pairs={{0,3},{1,2},{2,1},{3,0},{4,7},{5,6},{6,5},{7,4},{8,11},{9,10},{10,... | collective-permute-start | bytes 405512 | tf_op jit(solution)/shard_map/ppermute | solution.py:194
  12.7 16.4 %collective-permute-start.4 = (bf16[528,128]{1,0:T(8,128)(2,1)S(1)}, bf16[528,128]{1,0:T(8,128)(2,1)S(1)}, u32[]{:S(2)}, u32[]{:S(2)}) collective-permute-start(bf16[528,128]{1,0:T(8,128)(2,1)S(1)} %get-tuple-element.19), channel_id=1, source_target_pairs={{0,16},{1,17},{2,18},{3,19},{4,20},{5,21},{6,22},{7,23},{8,24},{9,... | collective-permute-start | bytes 405512 | tf_op jit(solution)/shard_map/ppermute | solution.py:194
  15.0 14.2 %collective-permute-start.5 = (bf16[528,128]{1,0:T(8,128)(2,1)S(1)}, bf16[528,128]{1,0:T(8,128)(2,1)S(1)}, u32[]{:S(2)}, u32[]{:S(2)}) collective-permute-start(bf16[528,128]{1,0:T(8,128)(2,1)S(1)} %get-tuple-element.20), channel_id=1, source_target_pairs={{0,17},{1,16},{2,19},{3,18},{4,21},{5,20},{6,23},{7,22},{8,25},{9,... | collective-permute-start | bytes 405512 | tf_op jit(solution)/shard_map/ppermute | solution.py:194
  23.2 11.2 %collective-permute-start.6 = (bf16[528,128]{1,0:T(8,128)(2,1)S(1)}, bf16[528,128]{1,0:T(8,128)(2,1)S(1)}, u32[]{:S(2)}, u32[]{:S(2)}) collective-permute-start(bf16[528,128]{1,0:T(8,128)(2,1)S(1)} %get-tuple-element.21), channel_id=1, source_target_pairs={{0,18},{1,19},{2,16},{3,17},{4,22},{5,23},{6,20},{7,21},{8,26},{9,... | collective-permute-start | bytes 405512 | tf_op jit(solution)/shard_map/ppermute | solution.py:194
  23.2 11.2 %collective-permute-start.7 = (bf16[528,128]{1,0:T(8,128)(2,1)S(1)}, bf16[528,128]{1,0:T(8,128)(2,1)S(1)}, u32[]{:S(2)}, u32[]{:S(2)}) collective-permute-start(bf16[528,128]{1,0:T(8,128)(2,1)S(1)} %get-tuple-element.22), channel_id=1, source_target_pairs={{0,19},{1,18},{2,17},{3,16},{4,23},{5,22},{6,21},{7,20},{8,27},{9,... | collective-permute-start | bytes 405512 | tf_op jit(solution)/shard_map/ppermute | solution.py:194
  26.2 1.9 %copy-start = (f32[1,1,768,1024]{3,2,1,0:T(8,128)S(1)}, f32[1,1,768,1024]{3,2,1,0:T(8,128)}, u32[]{:S(2)}) copy-start(f32[1,1,768,1024]{3,2,1,0:T(8,128)} %param.11) | copy-start | bytes 9437188
  29.1 17.0 %copy-start.3 = (bf16[1,1,768,1024]{3,2,1,0:T(8,128)(2,1)S(1)}, bf16[1,1,768,1024]{3,2,1,0:T(8,128)(2,1)}, u32[]{:S(2)}) copy-start(bf16[1,1,768,1024]{3,2,1,0:T(8,128)(2,1)} %param.12) | copy-start | bytes 4718596
  29.1 17.0 %copy-start.4 = (bf16[1,1,768,1024]{3,2,1,0:T(8,128)(2,1)S(1)}, bf16[1,1,768,1024]{3,2,1,0:T(8,128)(2,1)}, u32[]{:S(2)}) copy-start(bf16[1,1,768,1024]{3,2,1,0:T(8,128)(2,1)} %param.13) | copy-start | bytes 4718596
  34.7 7.5 %collective-permute-start.11 = (f32[8,128]{1,0:T(8,128)S(1)}, f32[8,128]{1,0:T(8,128)S(1)}, u32[]{:S(2)}, u32[]{:S(2)}) collective-permute-start(f32[8,128]{1,0:T(8,128)S(1)} %get-tuple-element.24.rest_0_), channel_id=1, source_target_pairs={{0,16},{1,17},{2,18},{3,19},{4,20},{5,21},{6,22},{7,23},{8,24},{9,... | collective-permute-start | bytes 12296 | tf_op jit(solution)/shard_map/ppermute | solution.py:194
  36.3 8.3 %collective-permute-start.12 = (f32[8,128]{1,0:T(8,128)S(1)}, f32[8,128]{1,0:T(8,128)S(1)}, u32[]{:S(2)}, u32[]{:S(2)}) collective-permute-start(f32[8,128]{1,0:T(8,128)S(1)} %get-tuple-element.25), channel_id=1, source_target_pairs={{0,17},{1,16},{2,19},{3,18},{4,21},{5,20},{6,23},{7,22},{8,25},{9,... | collective-permute-start | bytes 12296 | tf_op jit(solution)/shard_map/ppermute | solution.py:194
  38.3 14.9 %collective-permute-start.8 = (f32[8,128]{1,0:T(8,128)S(1)}, f32[8,128]{1,0:T(8,128)S(1)}, u32[]{:S(2)}, u32[]{:S(2)}) collective-permute-start(f32[8,128]{1,0:T(8,128)S(1)} %get-tuple-element.25), channel_id=1, source_target_pairs={{0,1},{1,0},{2,3},{3,2},{4,5},{5,4},{6,7},{7,6},{8,9},{9,8},{10,11... | collective-permute-start | bytes 12296 | tf_op jit(solution)/shard_map/ppermute | solution.py:194
  38.3 14.8 %collective-permute-start.13 = (f32[8,128]{1,0:T(8,128)S(1)}, f32[8,128]{1,0:T(8,128)S(1)}, u32[]{:S(2)}, u32[]{:S(2)}) collective-permute-start(f32[8,128]{1,0:T(8,128)S(1)} %get-tuple-element.26), channel_id=1, source_target_pairs={{0,18},{1,19},{2,16},{3,17},{4,22},{5,23},{6,20},{7,21},{8,26},{9,... | collective-permute-start | bytes 12296 | tf_op jit(solution)/shard_map/ppermute | solution.py:194
  42.3 10.9 %collective-permute-start.9 = (f32[8,128]{1,0:T(8,128)S(1)}, f32[8,128]{1,0:T(8,128)S(1)}, u32[]{:S(2)}, u32[]{:S(2)}) collective-permute-start(f32[8,128]{1,0:T(8,128)S(1)} %get-tuple-element.26), channel_id=1, source_target_pairs={{0,2},{1,3},{2,0},{3,1},{4,6},{5,7},{6,4},{7,5},{8,10},{9,11},{10,... | collective-permute-start | bytes 12296 | tf_op jit(solution)/shard_map/ppermute | solution.py:194
  42.3 10.9 %collective-permute-start.14 = (f32[8,128]{1,0:T(8,128)S(1)}, f32[8,128]{1,0:T(8,128)S(1)}, u32[]{:S(2)}, u32[]{:S(2)}) collective-permute-start(f32[8,128]{1,0:T(8,128)S(1)} %get-tuple-element.27), channel_id=1, source_target_pairs={{0,19},{1,18},{2,17},{3,16},{4,23},{5,22},{6,21},{7,20},{8,27},{9,... | collective-permute-start | bytes 12296 | tf_op jit(solution)/shard_map/ppermute | solution.py:194
  44.6 8.5 %collective-permute-start.10 = (f32[8,128]{1,0:T(8,128)S(1)}, f32[8,128]{1,0:T(8,128)S(1)}, u32[]{:S(2)}, u32[]{:S(2)}) collective-permute-start(f32[8,128]{1,0:T(8,128)S(1)} %get-tuple-element.27), channel_id=1, source_target_pairs={{0,3},{1,2},{2,1},{3,0},{4,7},{5,6},{6,5},{7,4},{8,11},{9,10},{10,... | collective-permute-start | bytes 12296 | tf_op jit(solution)/shard_map/ppermute | solution.py:194
  46.1 7.1 %copy-start.6 = (s32[1,512,8]{1,2,0:T(8,128)S(1)}, s32[1,512,8]{1,2,0:T(8,128)}, u32[]{:S(2)}) copy-start(s32[1,512,8]{1,2,0:T(8,128)} %param.9) | copy-start | bytes 49156

commit v2 on v1

v2 whole, which is shorter than its diff:
```python
import functools

import jax
import jax.numpy as jnp
from jax import lax
from jax.experimental import pallas as pl
from jax.experimental.pallas import tpu as pltpu
from jax.sharding import PartitionSpec as P

beta_first = 0.9
beta_second = 0.95
adam_eps = 1e-08
decay_rate = 0.1
first_fix = 1.0 - 0.9**10
second_fix = 1.0 - 0.95**10

LANES = 128
TILE = 16
VMEM_BYTES = 48 * 1024 * 1024
F32 = jnp.float32
BF16 = jnp.bfloat16


def params():
    return pltpu.CompilerParams(vmem_limit_bytes=VMEM_BYTES)


def cost(flops, touched):
    return pl.CostEstimate(flops=int(flops), bytes_accessed=int(touched), transcendentals=0)


def specs(space, count):
    return [pl.BlockSpec(memory_space=space) for _ in range(count)]


def ep_index():
    return lax.axis_index("ep").astype(jnp.int32)


def own_half():
    sections = lax.axis_size("section")
    return jnp.where(lax.axis_index("section") < sections // 2, 0, 1).astype(jnp.int32)


def start_grads(grads_hbm, held, sems):
    half = held.shape[2]
    mine = own_half()
    copies = []
    for side in range(2):
        column = pl.multiple_of((1 - mine if side else mine) * half, half)
        copies.append(
            pltpu.make_async_copy(
                grads_hbm.at[:, pl.ds(column, half)], held.at[side], sems.at[side]
            )
        )
        copies[-1].start()
    return copies


def pick_rows(slots, k, cap):
    place = lax.broadcasted_iota(jnp.int32, (cap, slots.shape[1]), 0).astype(F32)
    return jnp.where(place == slots[k : k + 1, :], 1.0, 0.0).astype(BF16)


def fill_chunks(steps, cap, pick, held, copies, tiles, chunks):
    half = held.shape[2]
    data_rows = half // LANES * cap
    step = min(half, 2 * LANES)
    for side in range(2):
        for at, k in enumerate(steps):
            chunks[side * len(steps) + at][data_rows:, :] = tiles[k]
        copies[side].wait()
        for column in range(0, half, step):
            block = jnp.dot(
                pick, held[side, :, column : column + step], preferred_element_type=F32
            ).astype(BF16)
            for at in range(len(steps)):
                chunk = chunks[side * len(steps) + at]
                for part in range(step // LANES):
                    top = (column // LANES + part) * cap
                    chunk[top : top + cap, :] = block[
                        at * cap : (at + 1) * cap, part * LANES : (part + 1) * LANES
                    ]


def route_kernel(
    steps, group, cap, ids_hbm, weight_hbm, grads_hbm, slots_ref, tiles_ref, *rest
):
    chunks = rest[: 2 * len(steps)]
    ids_ref, weight_ref, held, sems = rest[2 * len(steps) :]
    tokens = held.shape[1]
    me = ep_index()
    small = [
        pltpu.make_async_copy(ids_hbm, ids_ref, sems.at[2]),
        pltpu.make_async_copy(weight_hbm, weight_ref, sems.at[3]),
    ]
    for copy in small:
        copy.start()
    copies = start_grads(grads_hbm, held, sems)
    earlier = lax.broadcasted_iota(jnp.int32, (tokens, tokens), 0)
    later = lax.broadcasted_iota(jnp.int32, (tokens, tokens), 1)
    ahead = jnp.where(earlier < later, 1.0, 0.0).astype(BF16)
    for copy in small:
        copy.wait()
    ids = ids_ref[...]
    weights = weight_ref[...].astype(F32)
    members, scales = [], []
    for k in range(group):
        named = ids == (me ^ k)
        members.append(jnp.sum(jnp.where(named, 1.0, 0.0), axis=0, keepdims=True))
        scales.append(jnp.sum(jnp.where(named, weights, 0.0), axis=0, keepdims=True))
    if group % TILE:
        members.append(jnp.zeros((-group % TILE, tokens), F32))
    member = jnp.concatenate(members, axis=0)
    before = jnp.dot(member.astype(BF16), ahead, preferred_element_type=F32)
    slots = jnp.where(member > 0.5, before, -1.0)
    slots_ref[...] = slots
    picks = [pick_rows(slots, k, cap) for k in range(group)]
    base = me * cap
    tile_row = lax.broadcasted_iota(jnp.int32, (TILE, LANES), 0)
    tile_lane = lax.broadcasted_iota(jnp.int32, (TILE, LANES), 1)
    spot = tile_row * LANES + tile_lane
    kept = (spot >= base) & (spot < base + cap)
    tiles = []
    for k in range(group):
        spread = jnp.broadcast_to(scales[k], (TILE, tokens)).astype(BF16)
        doubled = jnp.concatenate([picks[k]] * (LANES // cap), axis=0)
        tile = lax.dot_general(
            spread, doubled, (((1,), (1,)), ((), ())), preferred_element_type=F32
        )
        tiles.append(jnp.where(kept, tile, 0.0).astype(BF16))
        tiles_ref[k] = tiles[k]
    pick = jnp.concatenate([picks[k] for k in steps], axis=0)
    fill_chunks(steps, cap, pick, held, copies, tiles, chunks)


def later_kernel(steps, cap, slots_ref, tiles_ref, grads_hbm, *rest):
    chunks, (held, sems) = rest[-2 - 2 * len(steps) : -2], rest[-2:]
    copies = start_grads(grads_hbm, held, sems)
    slots = slots_ref[...]
    pick = jnp.concatenate([pick_rows(slots, k, cap) for k in steps], axis=0)
    fill_chunks(steps, cap, pick, held, copies, tiles_ref, chunks)


def inner_kernel(own_ref, other_ref, master_ref, inner_ref):
    weights = master_ref[...].astype(BF16)
    slots = own_ref.shape[1]
    for at, ref in ((0, own_ref), (slots, other_ref)):
        inner_ref[at : at + slots, :] = lax.dot_general(
            ref[...], weights, (((0,), (0,)), ((), ())), preferred_element_type=F32
        )


def score_kernel(items, group, cap, inner_ref, *rest):
    chunks, outs = rest[: len(items)], rest[-len(items) :]
    blocks = inner_ref.shape[1] // LANES
    me = ep_index()
    sums = []
    for (side, k), chunk in zip(items, chunks):
        start = pl.multiple_of(side * group * cap + (me ^ k) * cap, cap)
        total = jnp.zeros((cap, LANES), F32)
        for block in range(blocks):
            rows = chunk[block * cap : (block + 1) * cap, :].astype(F32)
            total += rows * inner_ref[pl.ds(start, cap), block * LANES : (block + 1) * LANES]
        sums.append(total)
    fold = LANES // cap
    for at in range(0, len(items), fold):
        some = sums[at : at + fold]
        if len(some) < fold:
            some.append(jnp.zeros(((fold - len(some)) * cap, LANES), F32))
        line = jnp.sum(jnp.concatenate(some, axis=0).T, axis=0, keepdims=True)
        for out in outs[at : at + fold]:
            out[...] = jnp.broadcast_to(line, out.shape)


def update_kernel(
    group, cap, own_ref, other_ref, master_ref, moment_ref, second_ref, *rest
):
    chunks = rest[: 2 * group]
    update_hbm, rows, scaled, total, update, sems = rest[2 * group :]
    slots = group * cap
    hid, half = update.shape
    data_rows = half // LANES * cap
    me = ep_index()
    for side in range(2):
        tile = jnp.zeros((TILE, LANES), F32)
        for k in range(group):
            chunk = chunks[side * group + k]
            tile += chunk[data_rows : data_rows + TILE, :].astype(F32)
            start = pl.multiple_of(side * slots + (me ^ k) * cap, cap)
            for block in range(half // LANES):
                rows[pl.ds(start, cap), block * LANES : (block + 1) * LANES] = chunk[
                    block * cap : (block + 1) * cap, :
                ]
        for part in range(slots // LANES):
            lanes = slice(part * LANES, (part + 1) * LANES)
            line = tile[part : part + 1, :]
            at = side * slots + part * LANES
            for top in range(0, hid, LANES):
                hidden = (own_ref, other_ref)[side][top : top + LANES, lanes]
                scaled[top : top + LANES, at : at + LANES] = (
                    hidden.astype(F32) * line
                ).astype(BF16)
    step = min(half, 2 * LANES)
    piece = 32

    def multiply(turn):
        total[turn % 2] = jnp.dot(
            scaled[...], rows[:, turn * step : (turn + 1) * step], preferred_element_type=F32
        )

    def adam(turn):
        columns = slice(turn * step, (turn + 1) * step)
        for top in range(0, hid, piece):
            lines = slice(top, top + piece)
            grad = total[turn % 2, lines, :]
            first = moment_ref[lines, columns].astype(F32) * (beta_first / first_fix) + grad * (
                (1.0 - beta_first) / first_fix
            )
            square = second_ref[lines, columns].astype(F32) * (beta_second / second_fix) + (
                grad * grad
            ) * ((1.0 - beta_second) / second_fix)
            root = square * lax.rsqrt(square) + adam_eps
            update[lines, columns] = (
                first * pl.reciprocal(root, approx=True) + decay_rate * master_ref[lines, columns]
            )

    copies = []
    multiply(0)
    for turn in range(half // step):
        if turn + 1 < half // step:
            multiply(turn + 1)
        adam(turn)
        columns = slice(turn * step, (turn + 1) * step)
        copies.append(
            pltpu.make_async_copy(update.at[:, columns], update_hbm.at[:, columns], sems.at[turn])
        )
        copies[-1].start()
    for copy in copies:
        copy.wait()


def combine_kernel(places, group, cap, ids_ref, slots_ref, *rest):
    scores, out_ref = rest[:-1], rest[-1]
    tokens = ids_ref.shape[1]
    me = ep_index()
    lines = [ref[0:1, :] for ref in scores]
    lines.append(jnp.zeros((LANES - len(lines), LANES), F32))
    columns = jnp.concatenate(lines, axis=0).T
    place = lax.broadcasted_iota(jnp.int32, (cap, tokens), 0).astype(F32)
    ids = ids_ref[...]
    result = jnp.zeros(ids.shape, F32)
    for k in range(group):
        score = 0.0
        for side in range(2):
            at = places[side * group + k]
            score += columns[at : at + cap, side * group + k : side * group + k + 1]
        chosen = jnp.sum(
            jnp.where(place == slots_ref[k : k + 1, :], score, 0.0), axis=0, keepdims=True
        )
        result = jnp.where(ids == (me ^ k), chosen, result)
    out_ref[...] = result


def moved(array, side, step):
    if (side, step) == (0, 0):
        return array
    sections, group = lax.axis_size("section"), lax.axis_size("ep")
    pairs = []
    for s in range(sections):
        target = (s + side * (sections // 2)) % sections
        for e in range(group):
            pairs.append((s * group + e, target * group + (e ^ step)))
    return lax.ppermute(array, ("section", "ep"), pairs)


def local(grad_out, router_weights, expert_ids, hidden, master, moment, second):
    group = lax.axis_size("ep")
    tokens, width = grad_out.shape[1:]
    top = expert_ids.shape[2]
    hid, slots = hidden.shape[2:]
    half = master.shape[3]
    cap = slots // group
    ids = expert_ids[0].T
    own_hidden = hidden[0, 0]
    param = master[0, 0]
    other_hidden = moved(own_hidden, 1, 0)

    far = group // 2
    steps = [k for k in range(1, group) if k != far]
    later_steps = [0, far]
    chunk = jax.ShapeDtypeStruct((half // LANES * cap + TILE, LANES), BF16)
    slot_rows = group + -group % TILE
    grads = pltpu.with_memory_space_constraint(grad_out[0], pltpu.HBM)
    held = pltpu.VMEM((2, tokens, half), BF16)
    routed = pl.pallas_call(
        functools.partial(route_kernel, steps, group, cap),
        out_shape=[
            jax.ShapeDtypeStruct((slot_rows, tokens), F32),
            jax.ShapeDtypeStruct((group, TILE, LANES), BF16),
        ]
        + [chunk] * (2 * len(steps)),
        in_specs=specs(pltpu.HBM, 3),
        out_specs=specs(pltpu.VMEM, 2 + 2 * len(steps)),
        scratch_shapes=[
            pltpu.VMEM((top, tokens), jnp.int32),
            pltpu.VMEM((top, tokens), BF16),
            held,
            pltpu.SemaphoreType.DMA((4,)),
        ],
        compiler_params=params(),
        cost_estimate=cost(2 * slots * tokens * width, 2 * (tokens + slots) * width),
        name="route",
    )(
        pltpu.with_memory_space_constraint(ids, pltpu.HBM),
        pltpu.with_memory_space_constraint(router_weights[0].T, pltpu.HBM),
        grads,
    )
    slot_of, tiles = routed[:2]
    arrived = {}
    for at in reversed(range(len(steps))):
        for side in range(2):
            sent = routed[2 + side * len(steps) + at]
            arrived[side, steps[at]] = moved(sent, side, steps[at])
    routed = pl.pallas_call(
        functools.partial(later_kernel, later_steps, cap),
        out_shape=[chunk] * (2 * len(later_steps)),
        in_specs=specs(pltpu.VMEM, 2) + specs(pltpu.HBM, 1) + specs(pl.ANY, 2),
        out_specs=specs(pltpu.VMEM, 2 * len(later_steps)),
        scratch_shapes=[held, pltpu.SemaphoreType.DMA((2,))],
        compiler_params=params(),
        cost_estimate=cost(2 * slots * tokens * width, 2 * (tokens + slots) * width),
        name="later",
    )(slot_of, tiles, grads, arrived[0, 1], arrived[1, 1])
    for at, k in ((1, far), (0, 0)):
        for side in range(2):
            arrived[side, k] = moved(routed[side * len(later_steps) + at], side, k)
    chunks = [arrived[side, k] for side in range(2) for k in range(group)]

    inner = pl.pallas_call(
        inner_kernel,
        out_shape=jax.ShapeDtypeStruct((2 * slots, half), F32),
        in_specs=specs(pltpu.VMEM, 3),
        out_specs=specs(pltpu.VMEM, 1)[0],
        compiler_params=params(),
        cost_estimate=cost(4 * slots * hid * half, 4 * hid * half + 8 * slots * half),
        name="inner",
    )(own_hidden, other_hidden, param)

    every = [(side, k) for side in range(2) for k in range(group)]
    last_items = [(0, far), (1, far)]
    waves = [[(0, 0)]]
    for k in steps + [0]:
        for side in range(2):
            if (side, k) != (0, 0):
                if len(waves[-1]) == (4 if len(waves) == 1 else 3):
                    waves.append([])
                waves[-1].append((side, k))
    returned, places = {}, {}
    for items in waves + [last_items]:
        done = list(returned.values())
        lines = pl.pallas_call(
            functools.partial(score_kernel, items, group, cap),
            out_shape=[jax.ShapeDtypeStruct((8, LANES), F32)] * len(items),
            in_specs=specs(pltpu.VMEM, 1 + len(items)) + specs(pl.ANY, len(done)),
            out_specs=specs(pltpu.VMEM, len(items)),
            compiler_params=params(),
            cost_estimate=cost(2 * len(items) * cap * half, 6 * len(items) * cap * half),
            name="score",
        )(inner, *[arrived[item] for item in items], *done)
        for at, (item, line) in enumerate(zip(items, lines)):
            returned[item] = moved(line, *item)
            places[item] = at * cap % LANES

    step = min(half, 2 * LANES)
    update = pl.pallas_call(
        functools.partial(update_kernel, group, cap),
        out_shape=jax.ShapeDtypeStruct((hid, half), F32),
        in_specs=specs(pltpu.VMEM, 5 + 2 * group),
        out_specs=specs(pltpu.HBM, 1)[0],
        scratch_shapes=[
            pltpu.VMEM((2 * slots, half), BF16),
            pltpu.VMEM((hid, 2 * slots), BF16),
            pltpu.VMEM((2, hid, step), F32),
            pltpu.VMEM((hid, half), F32),
            pltpu.SemaphoreType.DMA((half // step,)),
        ],
        compiler_params=params(),
        cost_estimate=cost(4 * slots * hid * half, 12 * hid * half + 4 * slots * half),
        name="update",
    )(own_hidden, other_hidden, param, moment[0, 0], second[0, 0], *chunks)
    router = pl.pallas_call(
        functools.partial(combine_kernel, [places[item] for item in every], group, cap),
        out_shape=jax.ShapeDtypeStruct((top, tokens), F32),
        in_specs=specs(pltpu.VMEM, 2 + 2 * group),
        out_specs=specs(pltpu.VMEM, 1)[0],
        compiler_params=params(),
        cost_estimate=cost(4 * slots * tokens, 8 * top * tokens),
        name="combine",
    )(ids, slot_of, *[returned[item] for item in every])
    return (update[None, None], router.T[None])


def solution(mesh):
    placed = (
        P("section", "ep", None),
        P("section", "ep", None),
        P("section", "ep", None),
        P("section", "ep", None, None),
        P("section", "ep", None, None),
        P("section", "ep", None, None),
        P("section", "ep", None, None),
    )
    return jax.shard_map(
        local,
        mesh=mesh,
        in_specs=placed,
        out_specs=(P("section", "ep", None, None), P("section", "ep", None)),
        check_vma=False,
    )
```

time: 54.4 us -> 53.4 us (0.982)
  starting transfers between devices: 22.7 us -> 33.1 us
  waiting for transfers between devices: 14.9 us -> 7.55 us
  local copies, waits for them, and re-layouts: 4.91 us -> 0.02 us
  Pallas kernels: 10.8 us -> 11.9 us
    ppermute x15, starting transfers between devices: 22.7 us -> 33.1 us  [moved(): return lax.ppermute(array, ('section', 'ep'), pairs)]
    ppermute x15, waiting for transfers between devices: 14.9 us -> 7.55 us  [moved(): return lax.ppermute(array, ('section', 'ep'), pairs)]
    unnamed x16 -> x10, local copies, waits for them, and re-layouts: 4.91 us -> 0.02 us
    pallas_call x3 -> x6, Pallas kernels: 2.77 us -> 5.33 us  [the longest x1 2.09 us: local(): pl.pallas_call(functools.partial(route_kernel, steps, group, cap), out_sh...]
    pallas_call x1, Pallas kernels: 7.02 us -> 5.59 us  [local(): pl.pallas_call(functools.partial(update_kernel, group, cap), out_shape=ja...]
  transfers between devices with their start and end apart: 15 -> 15, of which waited for: 3 -> 4; matrix products, arithmetic and copies ran while one was open for 0% -> 0% of each run, Pallas kernels for 18% -> 20%
where the time goes in v2:
time: 53.4 us; the launch traced here: 53.3 us
  starting transfers between devices  33.1 us (62%)
  Pallas kernels  11.9 us (22%)
  waiting for transfers between devices  7.55 us (14%)
  between operations  0.72 us (1%)
    ppermute x15, starting transfers between devices, moved(): return lax.ppermute(array, ('section', 'ep'), pairs)  33.1 us
    ppermute x15, waiting for transfers between devices, moved(): return lax.ppermute(array, ('section', 'ep'), pairs)  7.55 us
    pallas_call x1, Pallas kernels, local(): pl.pallas_call(functools.partial(update_kernel, group, cap), out_shape=ja...  5.59 us
    pallas_call x1, Pallas kernels, local(): pl.pallas_call(functools.partial(route_kernel, steps, group, cap), out_sh...  2.09 us
    pallas_call x1, Pallas kernels, local(): pl.pallas_call(functools.partial(later_kernel, later_steps, cap), out_sha...  1.88 us
  transfers between devices with their start and end apart: 15, of which 4 were waited for; matrix products, arithmetic and copies ran while one was open for 0% of the time, Pallas kernels for 20%

profile of v2, /device:TPU:0, one launch (start us, length us, event | category | flops | bytes accessed | tf_op | source)
XLA Modules:
  0.0 53.3 jit_solution(8129897225509681490)
XLA Ops:
  0.6 3.0 %collective-permute-start = (bf16[768,256]{1,0:T(8,128)(2,1)}, bf16[768,256]{1,0:T(8,128)(2,1)S(1)}, u32[]{:S(2)}, u32[]{:S(2)}) collective-permute-start(bf16[768,256]{1,0:T(8,128)(2,1)} %bitcast.17), channel_id=1, source_target_pairs={{0,16},{1,17},{2,18},{3,19},{4,20},{5,21},{6,22},{7,23},{8,24},{9,... | collective-permute-start | bytes 1179656 | tf_op jit(solution)/shard_map/ppermute | solution.py:274
  3.7 2.1 %route.1 = (f32[16,512]{1,0:T(8,128)S(1)}, bf16[4,16,128]{2,1,0:T(8,128)(2,1)S(1)}, bf16[528,128]{1,0:T(8,128)(2,1)S(1)}, bf16[528,128]{1,0:T(8,128)(2,1)S(1)}, ...) custom-call(s32[8,512]{1,0:T(8,128)} %bitcast.22, bf16[8,512]{1,0:T(8,128)(2,1)} %bitcast.28, ...), custom_call_target="tpu_custom_call" | custom-call | flops 536870912 | bytes 3145728 | tf_op jit(solution)/shard_map/route/pallas_call | solution.py:296
  5.8 1.6 %collective-permute-start.1 = (bf16[528,128]{1,0:T(8,128)(2,1)S(1)}, bf16[528,128]{1,0:T(8,128)(2,1)S(1)}, u32[]{:S(2)}, u32[]{:S(2)}) collective-permute-start(bf16[528,128]{1,0:T(8,128)(2,1)S(1)} %get-tuple-element.22), channel_id=1, source_target_pairs={{0,1},{1,0},{2,3},{3,2},{4,5},{5,4},{6,7},{7,6},{8,9},{9,8},{10,11... | collective-permute-start | bytes 405512 | tf_op jit(solution)/shard_map/ppermute | solution.py:274
  7.4 4.0 %collective-permute-start.4 = (bf16[528,128]{1,0:T(8,128)(2,1)S(1)}, bf16[528,128]{1,0:T(8,128)(2,1)S(1)}, u32[]{:S(2)}, u32[]{:S(2)}) collective-permute-start(bf16[528,128]{1,0:T(8,128)(2,1)S(1)} %get-tuple-element.26), channel_id=1, source_target_pairs={{0,3},{1,2},{2,1},{3,0},{4,7},{5,6},{6,5},{7,4},{8,11},{9,10},{10,... | collective-permute-start | bytes 405512 | tf_op jit(solution)/shard_map/ppermute | solution.py:274
  11.4 1.2 %collective-permute-start.7 = (bf16[528,128]{1,0:T(8,128)(2,1)S(1)}, bf16[528,128]{1,0:T(8,128)(2,1)S(1)}, u32[]{:S(2)}, u32[]{:S(2)}) collective-permute-start(bf16[528,128]{1,0:T(8,128)(2,1)S(1)} %get-tuple-element.29), channel_id=1, source_target_pairs={{0,19},{1,18},{2,17},{3,16},{4,23},{5,22},{6,21},{7,20},{8,27},{9,... | collective-permute-start | bytes 405512 | tf_op jit(solution)/shard_map/ppermute | solution.py:274
  12.6 1.8 %collective-permute-done.2.rest_1_.rest_5_.rest_2_ = bf16[528,128]{1,0:T(8,128)(2,1)S(1)} collective-permute-done((bf16[528,128]{1,0:T(8,128)(2,1)S(1)}, bf16[528,128]{1,0:T(8,128)(2,1)S(1)}, u32[]{:S(2)}, u32[]{:S(2)}) %collective-permute-start.2) | collective-permute-done | bytes 135200 | tf_op jit(solution)/shard_map/ppermute | solution.py:274
  14.3 1.9 %later.1 = (bf16[528,128]{1,0:T(8,128)(2,1)S(1)}, bf16[528,128]{1,0:T(8,128)(2,1)S(1)}, bf16[528,128]{1,0:T(8,128)(2,1)S(1)}, bf16[528,128]{1,0:T(8,128)(2,1)S(1)}) custom-call(f32[16,512]{1,0:T(8,128)S(1)} %get-tuple-element.20.slots_ref, bf16[4,16,128]{2,1,0:T(8,128)(2,1)S(1)} %get-tuple-element.21.tiles_ref, bf16[512,2048]{1,0:T(8,128)(2,1)} %bitcast.25, ...), custom_call_target="tpu_custom_call" | custom-call | flops 536870912 | bytes 3145728 | tf_op jit(solution)/shard_map/later/pallas_call | solution.py:325
  16.2 1.0 %collective-permute-start.5 = (bf16[528,128]{1,0:T(8,128)(2,1)S(1)}, bf16[528,128]{1,0:T(8,128)(2,1)S(1)}, u32[]{:S(2)}, u32[]{:S(2)}) collective-permute-start(bf16[528,128]{1,0:T(8,128)(2,1)S(1)} %get-tuple-element.27), channel_id=1, source_target_pairs={{0,16},{1,17},{2,18},{3,19},{4,20},{5,21},{6,22},{7,23},{8,24},{9,... | collective-permute-start | bytes 405512 | tf_op jit(solution)/shard_map/ppermute | solution.py:274
  17.2 4.0 %collective-permute-start.3 = (bf16[528,128]{1,0:T(8,128)(2,1)S(1)}, bf16[528,128]{1,0:T(8,128)(2,1)S(1)}, u32[]{:S(2)}, u32[]{:S(2)}) collective-permute-start(bf16[528,128]{1,0:T(8,128)(2,1)S(1)} %get-tuple-element.25), channel_id=1, source_target_pairs={{0,2},{1,3},{2,0},{3,1},{4,6},{5,7},{6,4},{7,5},{8,10},{9,11},{10,... | collective-permute-start | bytes 405512 | tf_op jit(solution)/shard_map/ppermute | solution.py:274
  21.2 0.5 collective-permute-start.6
  21.8 1.0 %inner.1.inner_ref = f32[512,1024]{1,0:T(8,128)S(1)} custom-call(bf16[768,256]{1,0:T(8,128)(2,1)S(1)} %bitcast.18, bf16[768,256]{1,0:T(8,128)(2,1)S(1)} %collective-permute-done.other_ref, f32[768,1024]{1,0:T(8,128)S(1)} %bitcast.16), custom_call_target="tpu_custom_call" | custom-call | flops 805306368 | bytes 5242880 | tf_op jit(solution)/shard_map/inner/pallas_call | solution.py:340
  22.8 0.2 score.3
  23.0 5.5 %collective-permute-start.8 = (f32[8,128]{1,0:T(8,128)S(1)}, f32[8,128]{1,0:T(8,128)S(1)}, u32[]{:S(2)}, u32[]{:S(2)}) collective-permute-start(f32[8,128]{1,0:T(8,128)S(1)} %get-tuple-element.31), channel_id=1, source_target_pairs={{0,1},{1,0},{2,3},{3,2},{4,5},{5,4},{6,7},{7,6},{8,9},{9,8},{10,11... | collective-permute-start | bytes 12296 | tf_op jit(solution)/shard_map/ppermute | solution.py:274
  28.4 2.0 %collective-permute-start.9 = (f32[8,128]{1,0:T(8,128)S(1)}, f32[8,128]{1,0:T(8,128)S(1)}, u32[]{:S(2)}, u32[]{:S(2)}) collective-permute-start(f32[8,128]{1,0:T(8,128)S(1)} %get-tuple-element.32), channel_id=1, source_target_pairs={{0,17},{1,16},{2,19},{3,18},{4,21},{5,20},{6,23},{7,22},{8,25},{9,... | collective-permute-start | bytes 12296 | tf_op jit(solution)/shard_map/ppermute | solution.py:274
  30.5 3.0 %collective-permute-start.10 = (f32[8,128]{1,0:T(8,128)S(1)}, f32[8,128]{1,0:T(8,128)S(1)}, u32[]{:S(2)}, u32[]{:S(2)}) collective-permute-start(f32[8,128]{1,0:T(8,128)S(1)} %get-tuple-element.33), channel_id=1, source_target_pairs={{0,3},{1,2},{2,1},{3,0},{4,7},{5,6},{6,5},{7,4},{8,11},{9,10},{10,... | collective-permute-start | bytes 12296 | tf_op jit(solution)/shard_map/ppermute | solution.py:274
  33.5 2.4 %collective-permute-done.10.rest_5_.rest_3_ = f32[8,128]{1,0:T(8,128)S(1)} collective-permute-done((f32[8,128]{1,0:T(8,128)S(1)}, f32[8,128]{1,0:T(8,128)S(1)}, u32[]{:S(2)}, u32[]{:S(2)}) %collective-permute-start.10) | collective-permute-done | bytes 4128 | tf_op jit(solution)/shard_map/ppermute | solution.py:274
  35.9 0.1 score.4
  36.0 4.3 %collective-permute-start.11 = (f32[8,128]{1,0:T(8,128)S(1)}, f32[8,128]{1,0:T(8,128)S(1)}, u32[]{:S(2)}, u32[]{:S(2)}) collective-permute-start(f32[8,128]{1,0:T(8,128)S(1)} %get-tuple-element.34), channel_id=1, source_target_pairs={{0,19},{1,18},{2,17},{3,16},{4,23},{5,22},{6,21},{7,20},{8,27},{9,... | collective-permute-start | bytes 12296 | tf_op jit(solution)/shard_map/ppermute | solution.py:274
  40.4 0.2 collective-permute-start.12
  40.6 1.8 %collective-permute-done.11.rest_6_.rest_7_ = f32[8,128]{1,0:T(8,128)S(1)} collective-permute-done((f32[8,128]{1,0:T(8,128)S(1)}, f32[8,128]{1,0:T(8,128)S(1)}, u32[]{:S(2)}, u32[]{:S(2)}) %collective-permute-start.11) | collective-permute-done | bytes 4128 | tf_op jit(solution)/shard_map/ppermute | solution.py:274
  42.4 1.6 %collective-permute-done.12.rest_7_.rest_4_ = f32[8,128]{1,0:T(8,128)S(1)} collective-permute-done((f32[8,128]{1,0:T(8,128)S(1)}, f32[8,128]{1,0:T(8,128)S(1)}, u32[]{:S(2)}, u32[]{:S(2)}) %collective-permute-start.12) | collective-permute-done | bytes 4128 | tf_op jit(solution)/shard_map/ppermute | solution.py:274
  44.2 2.6 %collective-permute-start.14 = (f32[8,128]{1,0:T(8,128)S(1)}, f32[8,128]{1,0:T(8,128)S(1)}, u32[]{:S(2)}, u32[]{:S(2)}) collective-permute-start(f32[8,128]{1,0:T(8,128)S(1)} %get-tuple-element.37), channel_id=1, source_target_pairs={{0,18},{1,19},{2,16},{3,17},{4,22},{5,23},{6,20},{7,21},{8,26},{9,... | collective-permute-start | bytes 12296 | tf_op jit(solution)/shard_map/ppermute | solution.py:274
  46.7 5.6 %update.1 = f32[768,1024]{1,0:T(8,128)} custom-call(bf16[768,256]{1,0:T(8,128)(2,1)S(1)} %bitcast.19, bf16[768,256]{1,0:T(8,128)(2,1)S(1)} %collective-permute-done.other_ref, f32[768,1024]{1,0:T(8,128)} %bitcast.15, bf16[768,1024]{1,0:T(8,128)(2,1)S(1)} %bitcast.20, bf16[768,1024]{1,0:T(8,128)(2,1)S(1)} %bitcast.21, ...), custom_call_target="tpu_custom_call" | custom-call | flops 805306368 | bytes 10485760 | tf_op jit(solution)/shard_map/update/pallas_call | solution.py:376
  52.4 0.9 %combine.1 = f32[8,512]{1,0:T(8,128)} custom-call(s32[8,512]{1,0:T(8,128)S(1)} %bitcast.23, f32[16,512]{1,0:T(8,128)S(1)} %get-tuple-element.20.slots_ref, f32[8,128]{1,0:T(8,128)S(1)} %get-tuple-element.30.rest_2_.rest_0_, f32[8,128]{1,0:T(8,128)S(1)} %collective-permute-done.8.rest_3_.rest_1_, f32[8,128]{1,0:T(8,128)S(1)} %collective-permute-done.13.rest_2_, ...), custom_call_target="tpu_custom_call" | custom-call | flops 524288 | bytes 32768 | tf_op jit(solution)/shard_map/combine/pallas_call | solution.py:392
  (24 shorter events, 0.3 us)
Async XLA Ops:
  0.6 20.6 %collective-permute-start = (bf16[768,256]{1,0:T(8,128)(2,1)}, bf16[768,256]{1,0:T(8,128)(2,1)S(1)}, u32[]{:S(2)}, u32[]{:S(2)}) collective-permute-start(bf16[768,256]{1,0:T(8,128)(2,1)} %bitcast.17), channel_id=1, source_target_pairs={{0,16},{1,17},{2,18},{3,19},{4,20},{5,21},{6,22},{7,23},{8,24},{9,... | collective-permute-start | bytes 1179656 | tf_op jit(solution)/shard_map/ppermute | solution.py:274
  3.7 18.1 %copy-start = (f32[1,1,768,1024]{3,2,1,0:T(8,128)S(1)}, f32[1,1,768,1024]{3,2,1,0:T(8,128)}, u32[]{:S(2)}) copy-start(f32[1,1,768,1024]{3,2,1,0:T(8,128)} %param.11) | copy-start | bytes 9437188
  3.7 18.1 %copy-start.1 = (bf16[1,1,768,256]{3,2,1,0:T(8,128)(2,1)S(1)}, bf16[1,1,768,256]{3,2,1,0:T(8,128)(2,1)}, u32[]{:S(2)}) copy-start(bf16[1,1,768,256]{3,2,1,0:T(8,128)(2,1)} %param.10) | copy-start | bytes 1179652
  5.8 6.8 %collective-permute-start.1 = (bf16[528,128]{1,0:T(8,128)(2,1)S(1)}, bf16[528,128]{1,0:T(8,128)(2,1)S(1)}, u32[]{:S(2)}, u32[]{:S(2)}) collective-permute-start(bf16[528,128]{1,0:T(8,128)(2,1)S(1)} %get-tuple-element.22), channel_id=1, source_target_pairs={{0,1},{1,0},{2,3},{3,2},{4,5},{5,4},{6,7},{7,6},{8,9},{9,8},{10,11... | collective-permute-start | bytes 405512 | tf_op jit(solution)/shard_map/ppermute | solution.py:274
  7.4 6.9 %collective-permute-start.2 = (bf16[528,128]{1,0:T(8,128)(2,1)S(1)}, bf16[528,128]{1,0:T(8,128)(2,1)S(1)}, u32[]{:S(2)}, u32[]{:S(2)}) collective-permute-start(bf16[528,128]{1,0:T(8,128)(2,1)S(1)} %get-tuple-element.23), channel_id=1, source_target_pairs={{0,17},{1,16},{2,19},{3,18},{4,21},{5,20},{6,23},{7,22},{8,25},{9,... | collective-permute-start | bytes 405512 | tf_op jit(solution)/shard_map/ppermute | solution.py:274
  7.4 15.4 %collective-permute-start.4 = (bf16[528,128]{1,0:T(8,128)(2,1)S(1)}, bf16[528,128]{1,0:T(8,128)(2,1)S(1)}, u32[]{:S(2)}, u32[]{:S(2)}) collective-permute-start(bf16[528,128]{1,0:T(8,128)(2,1)S(1)} %get-tuple-element.26), channel_id=1, source_target_pairs={{0,3},{1,2},{2,1},{3,0},{4,7},{5,6},{6,5},{7,4},{8,11},{9,10},{10,... | collective-permute-start | bytes 405512 | tf_op jit(solution)/shard_map/ppermute | solution.py:274
  11.4 17.0 %collective-permute-start.7 = (bf16[528,128]{1,0:T(8,128)(2,1)S(1)}, bf16[528,128]{1,0:T(8,128)(2,1)S(1)}, u32[]{:S(2)}, u32[]{:S(2)}) collective-permute-start(bf16[528,128]{1,0:T(8,128)(2,1)S(1)} %get-tuple-element.29), channel_id=1, source_target_pairs={{0,19},{1,18},{2,17},{3,16},{4,23},{5,22},{6,21},{7,20},{8,27},{9,... | collective-permute-start | bytes 405512 | tf_op jit(solution)/shard_map/ppermute | solution.py:274
  16.2 14.3 %collective-permute-start.5 = (bf16[528,128]{1,0:T(8,128)(2,1)S(1)}, bf16[528,128]{1,0:T(8,128)(2,1)S(1)}, u32[]{:S(2)}, u32[]{:S(2)}) collective-permute-start(bf16[528,128]{1,0:T(8,128)(2,1)S(1)} %get-tuple-element.27), channel_id=1, source_target_pairs={{0,16},{1,17},{2,18},{3,19},{4,20},{5,21},{6,22},{7,23},{8,24},{9,... | collective-permute-start | bytes 405512 | tf_op jit(solution)/shard_map/ppermute | solution.py:274
  17.2 23.3 %collective-permute-start.3 = (bf16[528,128]{1,0:T(8,128)(2,1)S(1)}, bf16[528,128]{1,0:T(8,128)(2,1)S(1)}, u32[]{:S(2)}, u32[]{:S(2)}) collective-permute-start(bf16[528,128]{1,0:T(8,128)(2,1)S(1)} %get-tuple-element.25), channel_id=1, source_target_pairs={{0,2},{1,3},{2,0},{3,1},{4,6},{5,7},{6,4},{7,5},{8,10},{9,11},{10,... | collective-permute-start | bytes 405512 | tf_op jit(solution)/shard_map/ppermute | solution.py:274
  21.2 19.3 %collective-permute-start.6 = (bf16[528,128]{1,0:T(8,128)(2,1)S(1)}, bf16[528,128]{1,0:T(8,128)(2,1)S(1)}, u32[]{:S(2)}, u32[]{:S(2)}) collective-permute-start(bf16[528,128]{1,0:T(8,128)(2,1)S(1)} %get-tuple-element.28), channel_id=1, source_target_pairs={{0,18},{1,19},{2,16},{3,17},{4,22},{5,23},{6,20},{7,21},{8,26},{9,... | collective-permute-start | bytes 405512 | tf_op jit(solution)/shard_map/ppermute | solution.py:274
  23.0 10.5 %collective-permute-start.8 = (f32[8,128]{1,0:T(8,128)S(1)}, f32[8,128]{1,0:T(8,128)S(1)}, u32[]{:S(2)}, u32[]{:S(2)}) collective-permute-start(f32[8,128]{1,0:T(8,128)S(1)} %get-tuple-element.31), channel_id=1, source_target_pairs={{0,1},{1,0},{2,3},{3,2},{4,5},{5,4},{6,7},{7,6},{8,9},{9,8},{10,11... | collective-permute-start | bytes 12296 | tf_op jit(solution)/shard_map/ppermute | solution.py:274
  28.4 5.1 %collective-permute-start.9 = (f32[8,128]{1,0:T(8,128)S(1)}, f32[8,128]{1,0:T(8,128)S(1)}, u32[]{:S(2)}, u32[]{:S(2)}) collective-permute-start(f32[8,128]{1,0:T(8,128)S(1)} %get-tuple-element.32), channel_id=1, source_target_pairs={{0,17},{1,16},{2,19},{3,18},{4,21},{5,20},{6,23},{7,22},{8,25},{9,... | collective-permute-start | bytes 12296 | tf_op jit(solution)/shard_map/ppermute | solution.py:274
  30.5 5.4 %collective-permute-start.10 = (f32[8,128]{1,0:T(8,128)S(1)}, f32[8,128]{1,0:T(8,128)S(1)}, u32[]{:S(2)}, u32[]{:S(2)}) collective-permute-start(f32[8,128]{1,0:T(8,128)S(1)} %get-tuple-element.33), channel_id=1, source_target_pairs={{0,3},{1,2},{2,1},{3,0},{4,7},{5,6},{6,5},{7,4},{8,11},{9,10},{10,... | collective-permute-start | bytes 12296 | tf_op jit(solution)/shard_map/ppermute | solution.py:274
  35.9 10.9 %copy-start.2 = (bf16[1,1,768,1024]{3,2,1,0:T(8,128)(2,1)S(1)}, bf16[1,1,768,1024]{3,2,1,0:T(8,128)(2,1)}, u32[]{:S(2)}) copy-start(bf16[1,1,768,1024]{3,2,1,0:T(8,128)(2,1)} %param.12) | copy-start | bytes 4718596
  35.9 10.9 %copy-start.3 = (bf16[1,1,768,1024]{3,2,1,0:T(8,128)(2,1)S(1)}, bf16[1,1,768,1024]{3,2,1,0:T(8,128)(2,1)}, u32[]{:S(2)}) copy-start(bf16[1,1,768,1024]{3,2,1,0:T(8,128)(2,1)} %param.13) | copy-start | bytes 4718596
  36.0 6.4 %collective-permute-start.11 = (f32[8,128]{1,0:T(8,128)S(1)}, f32[8,128]{1,0:T(8,128)S(1)}, u32[]{:S(2)}, u32[]{:S(2)}) collective-permute-start(f32[8,128]{1,0:T(8,128)S(1)} %get-tuple-element.34), channel_id=1, source_target_pairs={{0,19},{1,18},{2,17},{3,16},{4,23},{5,22},{6,21},{7,20},{8,27},{9,... | collective-permute-start | bytes 12296 | tf_op jit(solution)/shard_map/ppermute | solution.py:274
  40.4 3.6 %collective-permute-start.12 = (f32[8,128]{1,0:T(8,128)S(1)}, f32[8,128]{1,0:T(8,128)S(1)}, u32[]{:S(2)}, u32[]{:S(2)}) collective-permute-start(f32[8,128]{1,0:T(8,128)S(1)} %get-tuple-element.35), channel_id=1, source_target_pairs={{0,16},{1,17},{2,18},{3,19},{4,20},{5,21},{6,22},{7,23},{8,24},{9,... | collective-permute-start | bytes 12296 | tf_op jit(solution)/shard_map/ppermute | solution.py:274
  44.1 8.2 %collective-permute-start.13 = (f32[8,128]{1,0:T(8,128)S(1)}, f32[8,128]{1,0:T(8,128)S(1)}, u32[]{:S(2)}, u32[]{:S(2)}) collective-permute-start(f32[8,128]{1,0:T(8,128)S(1)} %get-tuple-element.36), channel_id=1, source_target_pairs={{0,2},{1,3},{2,0},{3,1},{4,6},{5,7},{6,4},{7,5},{8,10},{9,11},{10,... | collective-permute-start | bytes 12296 | tf_op jit(solution)/shard_map/ppermute | solution.py:274
  44.2 8.2 %collective-permute-start.14 = (f32[8,128]{1,0:T(8,128)S(1)}, f32[8,128]{1,0:T(8,128)S(1)}, u32[]{:S(2)}, u32[]{:S(2)}) collective-permute-start(f32[8,128]{1,0:T(8,128)S(1)} %get-tuple-element.37), channel_id=1, source_target_pairs={{0,18},{1,19},{2,16},{3,17},{4,22},{5,23},{6,20},{7,21},{8,26},{9,... | collective-permute-start | bytes 12296 | tf_op jit(solution)/shard_map/ppermute | solution.py:274
  46.7 5.6 %copy-start.4 = (s32[1,512,8]{1,2,0:T(8,128)S(1)}, s32[1,512,8]{1,2,0:T(8,128)}, u32[]{:S(2)}) copy-start(s32[1,512,8]{1,2,0:T(8,128)} %param.9) | copy-start | bytes 49156

commit v3 on v2

--- a/solution.py
+++ b/solution.py
@@ -38,8 +38,7 @@
 
 
 def own_half():
-    sections = lax.axis_size("section")
-    return jnp.where(lax.axis_index("section") < sections // 2, 0, 1).astype(jnp.int32)
+    return lax.axis_index("pair").astype(jnp.int32)
 
 
 def start_grads(grads_hbm, held, sems):
@@ -84,7 +83,7 @@
 
 
 def route_kernel(
-    steps, group, cap, ids_hbm, weight_hbm, grads_hbm, slots_ref, tiles_ref, *rest
+    steps, group, cap, ids_hbm, weight_hbm, grads_hbm, slots_ref, *rest
 ):
     chunks = rest[: 2 * len(steps)]
     ids_ref, weight_ref, held, sems = rest[2 * len(steps) :]
@@ -129,17 +128,8 @@
             spread, doubled, (((1,), (1,)), ((), ())), preferred_element_type=F32
         )
         tiles.append(jnp.where(kept, tile, 0.0).astype(BF16))
-        tiles_ref[k] = tiles[k]
     pick = jnp.concatenate([picks[k] for k in steps], axis=0)
     fill_chunks(steps, cap, pick, held, copies, tiles, chunks)
-
-
-def later_kernel(steps, cap, slots_ref, tiles_ref, grads_hbm, *rest):
-    chunks, (held, sems) = rest[-2 - 2 * len(steps) : -2], rest[-2:]
-    copies = start_grads(grads_hbm, held, sems)
-    slots = slots_ref[...]
-    pick = jnp.concatenate([pick_rows(slots, k, cap) for k in steps], axis=0)
-    fill_chunks(steps, cap, pick, held, copies, tiles_ref, chunks)
 
 
 def inner_kernel(own_ref, other_ref, master_ref, inner_ref):
@@ -151,26 +141,24 @@
         )
 
 
-def score_kernel(items, group, cap, inner_ref, *rest):
-    chunks, outs = rest[: len(items)], rest[-len(items) :]
+def score_kernel(group, cap, inner_ref, *rest):
+    chunks, out_ref = rest[:-1], rest[-1]
     blocks = inner_ref.shape[1] // LANES
     me = ep_index()
-    sums = []
-    for (side, k), chunk in zip(items, chunks):
-        start = pl.multiple_of(side * group * cap + (me ^ k) * cap, cap)
-        total = jnp.zeros((cap, LANES), F32)
-        for block in range(blocks):
-            rows = chunk[block * cap : (block + 1) * cap, :].astype(F32)
-            total += rows * inner_ref[pl.ds(start, cap), block * LANES : (block + 1) * LANES]
-        sums.append(total)
-    fold = LANES // cap
-    for at in range(0, len(items), fold):
-        some = sums[at : at + fold]
-        if len(some) < fold:
-            some.append(jnp.zeros(((fold - len(some)) * cap, LANES), F32))
-        line = jnp.sum(jnp.concatenate(some, axis=0).T, axis=0, keepdims=True)
-        for out in outs[at : at + fold]:
-            out[...] = jnp.broadcast_to(line, out.shape)
+    mine = own_half()
+    for k in range(group):
+        sums = []
+        for side in range(2):
+            start = pl.multiple_of(side * group * cap + (me ^ k) * cap, cap)
+            total = jnp.zeros((cap, LANES), F32)
+            for block in range(blocks):
+                rows = chunks[side * group + k][block * cap : (block + 1) * cap, :].astype(F32)
+                total += rows * inner_ref[pl.ds(start, cap), block * LANES : (block + 1) * LANES]
+            sums.append(total)
+        both = jnp.concatenate(sums, axis=0)
+        line = jnp.sum(both.T, axis=0, keepdims=True)
+        for side in range(2):
+            out_ref[(mine ^ side) * group + (me ^ k)] = jnp.broadcast_to(line, out_ref.shape[1:])
 
 
 def update_kernel(
@@ -240,38 +228,34 @@
         copy.wait()
 
 
-def combine_kernel(places, group, cap, ids_ref, slots_ref, *rest):
-    scores, out_ref = rest[:-1], rest[-1]
+def combine_kernel(group, cap, ids_ref, slots_ref, score_ref, out_ref):
     tokens = ids_ref.shape[1]
     me = ep_index()
-    lines = [ref[0:1, :] for ref in scores]
-    lines.append(jnp.zeros((LANES - len(lines), LANES), F32))
+    mine = own_half()
+    lane = lax.broadcasted_iota(jnp.int32, (1, LANES), 1)
+    lines = []
+    for k in range(group):
+        own = score_ref[mine * group + (me ^ k)][0:1, :]
+        other = score_ref[(1 - mine) * group + (me ^ k)][0:1, :]
+        lines.append(jnp.where(lane < cap, own, other))
+    lines.append(jnp.zeros((LANES - group, LANES), F32))
     columns = jnp.concatenate(lines, axis=0).T
+    columns = columns[:cap] + columns[cap : 2 * cap]
     place = lax.broadcasted_iota(jnp.int32, (cap, tokens), 0).astype(F32)
     ids = ids_ref[...]
     result = jnp.zeros(ids.shape, F32)
     for k in range(group):
-        score = 0.0
-        for side in range(2):
-            at = places[side * group + k]
-            score += columns[at : at + cap, side * group + k : side * group + k + 1]
-        chosen = jnp.sum(
-            jnp.where(place == slots_ref[k : k + 1, :], score, 0.0), axis=0, keepdims=True
-        )
-        result = jnp.where(ids == (me ^ k), chosen, result)
+        at_slot = jnp.where(place == slots_ref[k : k + 1, :], columns[:, k : k + 1], 0.0)
+        result = jnp.where(ids == (me ^ k), jnp.sum(at_slot, axis=0, keepdims=True), result)
     out_ref[...] = result
 
 
 def moved(array, side, step):
-    if (side, step) == (0, 0):
-        return array
-    sections, group = lax.axis_size("section"), lax.axis_size("ep")
-    pairs = []
-    for s in range(sections):
-        target = (s + side * (sections // 2)) % sections
-        for e in range(group):
-            pairs.append((s * group + e, target * group + (e ^ step)))
-    return lax.ppermute(array, ("section", "ep"), pairs)
+    group = lax.axis_size("ep")
+    pairs = [
+        (p * group + e, (p ^ side) * group + (e ^ step)) for p in range(2) for e in range(group)
+    ]
+    return lax.ppermute(array, ("pair", "ep"), pairs)
 
 
 def local(grad_out, router_weights, expert_ids, hidden, master, moment, second):
@@ -286,26 +270,18 @@
     param = master[0, 0]
     other_hidden = moved(own_hidden, 1, 0)
 
-    far = group // 2
-    steps = [k for k in range(1, group) if k != far]
-    later_steps = [0, far]
+    steps = list(range(group))
     chunk = jax.ShapeDtypeStruct((half // LANES * cap + TILE, LANES), BF16)
-    slot_rows = group + -group % TILE
-    grads = pltpu.with_memory_space_constraint(grad_out[0], pltpu.HBM)
-    held = pltpu.VMEM((2, tokens, half), BF16)
     routed = pl.pallas_call(
         functools.partial(route_kernel, steps, group, cap),
-        out_shape=[
-            jax.ShapeDtypeStruct((slot_rows, tokens), F32),
-            jax.ShapeDtypeStruct((group, TILE, LANES), BF16),
-        ]
-        + [chunk] * (2 * len(steps)),
+        out_shape=[jax.ShapeDtypeStruct((group + -group % TILE, tokens), F32)]
+        + [chunk] * (2 * group),
         in_specs=specs(pltpu.HBM, 3),
-        out_specs=specs(pltpu.VMEM, 2 + 2 * len(steps)),
+        out_specs=specs(pltpu.VMEM, 1 + 2 * group),
         scratch_shapes=[
             pltpu.VMEM((top, tokens), jnp.int32),
             pltpu.VMEM((top, tokens), BF16),
-            held,
+            pltpu.VMEM((2, tokens, half), BF16),
             pltpu.SemaphoreType.DMA((4,)),
         ],
         compiler_params=params(),
@@ -314,27 +290,14 @@
     )(
         pltpu.with_memory_space_constraint(ids, pltpu.HBM),
         pltpu.with_memory_space_constraint(router_weights[0].T, pltpu.HBM),
-        grads,
+        pltpu.with_memory_space_constraint(grad_out[0], pltpu.HBM),
     )
-    slot_of, tiles = routed[:2]
-    arrived = {}
-    for at in reversed(range(len(steps))):
-        for side in range(2):
-            sent = routed[2 + side * len(steps) + at]
-            arrived[side, steps[at]] = moved(sent, side, steps[at])
-    routed = pl.pallas_call(
-        functools.partial(later_kernel, later_steps, cap),
-        out_shape=[chunk] * (2 * len(later_steps)),
-        in_specs=specs(pltpu.VMEM, 2) + specs(pltpu.HBM, 1) + specs(pl.ANY, 2),
-        out_specs=specs(pltpu.VMEM, 2 * len(later_steps)),
-        scratch_shapes=[held, pltpu.SemaphoreType.DMA((2,))],
-        compiler_params=params(),
-        cost_estimate=cost(2 * slots * tokens * width, 2 * (tokens + slots) * width),
-        name="later",
-    )(slot_of, tiles, grads, arrived[0, 1], arrived[1, 1])
-    for at, k in ((1, far), (0, 0)):
-        for side in range(2):
-            arrived[side, k] = moved(routed[side * len(later_steps) + at], side, k)
+    slot_of, sent = routed[0], routed[1:]
+    arrived = {(0, 0): sent[0]}
+    by_distance = list(range(group - 1, 1, -1))
+    order = [(0, 1)] + [(side, k) for k in by_distance for side in range(2)] + [(1, 1), (1, 0)]
+    for side, k in order:
+        arrived[side, k] = moved(sent[side * group + k], side, k)
     chunks = [arrived[side, k] for side in range(2) for k in range(group)]
 
     inner = pl.pallas_call(
@@ -347,30 +310,16 @@
         name="inner",
     )(own_hidden, other_hidden, param)
 
-    every = [(side, k) for side in range(2) for k in range(group)]
-    last_items = [(0, far), (1, far)]
-    waves = [[(0, 0)]]
-    for k in steps + [0]:
-        for side in range(2):
-            if (side, k) != (0, 0):
-                if len(waves[-1]) == (4 if len(waves) == 1 else 3):
-                    waves.append([])
-                waves[-1].append((side, k))
-    returned, places = {}, {}
-    for items in waves + [last_items]:
-        done = list(returned.values())
-        lines = pl.pallas_call(
-            functools.partial(score_kernel, items, group, cap),
-            out_shape=[jax.ShapeDtypeStruct((8, LANES), F32)] * len(items),
-            in_specs=specs(pltpu.VMEM, 1 + len(items)) + specs(pl.ANY, len(done)),
-            out_specs=specs(pltpu.VMEM, len(items)),
-            compiler_params=params(),
-            cost_estimate=cost(2 * len(items) * cap * half, 6 * len(items) * cap * half),
-            name="score",
-        )(inner, *[arrived[item] for item in items], *done)
-        for at, (item, line) in enumerate(zip(items, lines)):
-            returned[item] = moved(line, *item)
-            places[item] = at * cap % LANES
+    scores = pl.pallas_call(
+        functools.partial(score_kernel, group, cap),
+        out_shape=jax.ShapeDtypeStruct((2 * group, 8, LANES), F32),
+        in_specs=specs(pltpu.VMEM, 1 + 2 * group),
+        out_specs=specs(pltpu.VMEM, 1)[0],
+        compiler_params=params(),
+        cost_estimate=cost(4 * slots * half, 12 * slots * half),
+        name="score",
+    )(inner, *chunks)
+    returned = lax.all_to_all(scores, ("pair", "ep"), split_axis=0, concat_axis=0, tiled=True)
 
     step = min(half, 2 * LANES)
     update = pl.pallas_call(
@@ -390,31 +339,29 @@
         name="update",
     )(own_hidden, other_hidden, param, moment[0, 0], second[0, 0], *chunks)
     router = pl.pallas_call(
-        functools.partial(combine_kernel, [places[item] for item in every], group, cap),
+        functools.partial(combine_kernel, group, cap),
         out_shape=jax.ShapeDtypeStruct((top, tokens), F32),
-        in_specs=specs(pltpu.VMEM, 2 + 2 * group),
+        in_specs=specs(pltpu.VMEM, 3),
         out_specs=specs(pltpu.VMEM, 1)[0],
         compiler_params=params(),
         cost_estimate=cost(4 * slots * tokens, 8 * top * tokens),
         name="combine",
-    )(ids, slot_of, *[returned[item] for item in every])
+    )(ids, slot_of, returned)
     return (update[None, None], router.T[None])
 
 
 def solution(mesh):
-    placed = (
-        P("section", "ep", None),
-        P("section", "ep", None),
-        P("section", "ep", None),
-        P("section", "ep", None, None),
-        P("section", "ep", None, None),
-        P("section", "ep", None, None),
-        P("section", "ep", None, None),
+    sections, group = mesh.devices.shape
+    split = jax.sharding.Mesh(
+        mesh.devices.reshape(2, sections // 2, group), ("pair", "rest", "ep")
     )
+    section = ("pair", "rest")
+    rows = P(section, "ep", None)
+    blocks = P(section, "ep", None, None)
     return jax.shard_map(
         local,
-        mesh=mesh,
-        in_specs=placed,
-        out_specs=(P("section", "ep", None, None), P("section", "ep", None)),
+        mesh=split,
+        in_specs=(rows, rows, rows, blocks, blocks, blocks, blocks),
+        out_specs=(blocks, rows),
         check_vma=False,
     )

time: 53.4 us -> 46.3 us (0.87)
  starting transfers between devices: 33.1 us -> 16.6 us
  waiting for transfers between devices: 7.55 us -> 14.9 us
  local copies, waits for them, and re-layouts: 0.02 us -> 3.31 us
  Pallas kernels: 11.9 us -> 10.5 us
    ppermute x15 -> x8, starting transfers between devices: 33.1 us -> 11.3 us  [moved(): return lax.ppermute(array, ('pair', 'ep'), pairs)]
    ppermute x15 -> x8, waiting for transfers between devices: 7.55 us -> 14.9 us  [moved(): return lax.ppermute(array, ('pair', 'ep'), pairs)]
    all_to_all x0 -> x1, starting transfers between devices: none -> 5.25 us  [local(): lax.all_to_all(scores, ('pair', 'ep'), split_axis=0, concat_axis=0, tiled...]
    unnamed x10, local copies, waits for them, and re-layouts: 0.02 us -> 3.31 us
    pallas_call x5 -> x2, Pallas kernels: 3.24 us -> 1.78 us  [the longest x1 0.91 us: local(): pl.pallas_call(functools.partial(score_kernel, group, cap), out_shape=jax...]
  transfers between devices with their start and end apart: 15 -> 9, of which waited for: 4 -> 3; matrix products, arithmetic and copies ran while one was open for 0% -> 0% of each run, Pallas kernels for 20% -> 19%
where the time goes in v3:
time: 46.3 us; the launch traced here: 46 us
  starting transfers between devices  16.6 us (36%)
  waiting for transfers between devices  14.9 us (32%)
  Pallas kernels  10.5 us (23%)
  local copies, waits for them, and re-layouts  3.31 us (7%)
  between operations  0.73 us (2%)
    ppermute x8, waiting for transfers between devices, moved(): return lax.ppermute(array, ('pair', 'ep'), pairs)  14.9 us
    ppermute x8, starting transfers between devices, moved(): return lax.ppermute(array, ('pair', 'ep'), pairs)  11.3 us
    pallas_call x1, Pallas kernels, local(): pl.pallas_call(functools.partial(update_kernel, group, cap), out_shape=ja...  5.57 us
    all_to_all x1, starting transfers between devices, local(): lax.all_to_all(scores, ('pair', 'ep'), split_axis=0, concat_axis=0, tiled...  5.25 us
    unnamed x10, local copies, waits for them, and re-layouts  3.31 us
    pallas_call x1, Pallas kernels, local(): pl.pallas_call(functools.partial(route_kernel, steps, group, cap), out_sh...  2.19 us
    pallas_call x1, Pallas kernels, local(): pl.pallas_call(inner_kernel, out_shape=jax.ShapeDtypeStruct((2 * slots, h...  1.01 us
  transfers between devices with their start and end apart: 9, of which 3 were waited for; matrix products, arithmetic and copies ran while one was open for 0% of the time, Pallas kernels for 19%

profile of v3, /device:TPU:0, one launch (start us, length us, event | category | flops | bytes accessed | tf_op | source)
XLA Modules:
  0.0 46.0 jit_solution(6334189421114730155)
XLA Ops:
  0.6 3.0 %collective-permute-start = (bf16[768,256]{1,0:T(8,128)(2,1)}, bf16[768,256]{1,0:T(8,128)(2,1)S(1)}, u32[]{:S(2)}, u32[]{:S(2)}) collective-permute-start(bf16[768,256]{1,0:T(8,128)(2,1)} %bitcast.17), channel_id=1, source_target_pairs={{0,16},{1,17},{2,18},{3,19},{16,0},{17,1},{18,2},{19,3},{4,20},{5,... | collective-permute-start | bytes 1179656 | tf_op jit(solution)/shard_map/ppermute | solution.py:258
  3.7 2.2 %route.1 = (f32[16,512]{1,0:T(8,128)S(1)}, bf16[528,128]{1,0:T(8,128)(2,1)S(1)}, bf16[528,128]{1,0:T(8,128)(2,1)S(1)}, bf16[528,128]{1,0:T(8,128)(2,1)S(1)}, bf1...) custom-call(s32[8,512]{1,0:T(8,128)} %bitcast.22, ...), custom_call_target="tpu_custom_call" | custom-call | flops 536870912 | bytes 3145728 | tf_op jit(solution)/shard_map/route/pallas_call | solution.py:275
  5.9 1.6 %collective-permute-start.1 = (bf16[528,128]{1,0:T(8,128)(2,1)S(1)}, bf16[528,128]{1,0:T(8,128)(2,1)S(1)}, u32[]{:S(2)}, u32[]{:S(2)}) collective-permute-start(bf16[528,128]{1,0:T(8,128)(2,1)S(1)} %get-tuple-element.12), channel_id=1, source_target_pairs={{0,1},{1,0},{2,3},{3,2},{16,17},{17,16},{18,19},{19,18},{4,5},{5,4... | collective-permute-start | bytes 405512 | tf_op jit(solution)/shard_map/ppermute | solution.py:258
  7.5 2.6 %collective-permute-start.2 = (bf16[528,128]{1,0:T(8,128)(2,1)S(1)}, bf16[528,128]{1,0:T(8,128)(2,1)S(1)}, u32[]{:S(2)}, u32[]{:S(2)}) collective-permute-start(bf16[528,128]{1,0:T(8,128)(2,1)S(1)} %get-tuple-element.13), channel_id=1, source_target_pairs={{0,2},{1,3},{2,0},{3,1},{16,18},{17,19},{18,16},{19,17},{4,6},{5,7... | collective-permute-start | bytes 405512 | tf_op jit(solution)/shard_map/ppermute | solution.py:258
  10.1 0.2 collective-permute-start.3
  10.3 0.3 collective-permute-start.4
  10.6 1.9 %collective-permute-done.1.rest_1_ = bf16[528,128]{1,0:T(8,128)(2,1)S(1)} collective-permute-done((bf16[528,128]{1,0:T(8,128)(2,1)S(1)}, bf16[528,128]{1,0:T(8,128)(2,1)S(1)}, u32[]{:S(2)}, u32[]{:S(2)}) %collective-permute-start.1) | collective-permute-done | bytes 135200 | tf_op jit(solution)/shard_map/ppermute | solution.py:258
  12.5 0.6 %collective-permute-start.5 = (bf16[528,128]{1,0:T(8,128)(2,1)S(1)}, bf16[528,128]{1,0:T(8,128)(2,1)S(1)}, u32[]{:S(2)}, u32[]{:S(2)}) collective-permute-start(bf16[528,128]{1,0:T(8,128)(2,1)S(1)} %get-tuple-element.16), channel_id=1, source_target_pairs={{0,17},{1,16},{2,19},{3,18},{16,1},{17,0},{18,3},{19,2},{4,21},{5,... | collective-permute-start | bytes 405512 | tf_op jit(solution)/shard_map/ppermute | solution.py:258
  13.1 7.7 %collective-permute-done.2.rest_2_ = bf16[528,128]{1,0:T(8,128)(2,1)S(1)} collective-permute-done((bf16[528,128]{1,0:T(8,128)(2,1)S(1)}, bf16[528,128]{1,0:T(8,128)(2,1)S(1)}, u32[]{:S(2)}, u32[]{:S(2)}) %collective-permute-start.2) | collective-permute-done | bytes 135200 | tf_op jit(solution)/shard_map/ppermute | solution.py:258
  20.8 0.0 collective-permute-start.6
  20.8 0.0 collective-permute-done.other_ref
  20.8 3.0 %collective-permute-start.7 = (bf16[528,128]{1,0:T(8,128)(2,1)S(1)}, bf16[528,128]{1,0:T(8,128)(2,1)S(1)}, u32[]{:S(2)}, u32[]{:S(2)}) collective-permute-start(bf16[528,128]{1,0:T(8,128)(2,1)S(1)} %get-tuple-element.18), channel_id=1, source_target_pairs={{0,19},{1,18},{2,17},{3,16},{16,3},{17,2},{18,1},{19,0},{4,23},{5,... | collective-permute-start | bytes 405512 | tf_op jit(solution)/shard_map/ppermute | solution.py:258
  23.8 1.9 %copy-done = f32[1,1,768,1024]{3,2,1,0:T(8,128)S(1)} copy-done((f32[1,1,768,1024]{3,2,1,0:T(8,128)S(1)}, f32[1,1,768,1024]{3,2,1,0:T(8,128)}, u32[]{:S(2)}) %copy-start) | copy-done | bytes 3145752
  25.7 1.0 %inner.1.inner_ref = f32[512,1024]{1,0:T(8,128)S(1)} custom-call(bf16[768,256]{1,0:T(8,128)(2,1)S(1)} %bitcast.18, bf16[768,256]{1,0:T(8,128)(2,1)S(1)} %collective-permute-done.other_ref, f32[768,1024]{1,0:T(8,128)S(1)} %bitcast.16), custom_call_target="tpu_custom_call" | custom-call | flops 805306368 | bytes 5242880 | tf_op jit(solution)/shard_map/inner/pallas_call | solution.py:303
  26.7 0.0 copy-start.2
  26.7 0.0 collective-permute-done.3.rest_3_
  26.7 0.0 collective-permute-done.5.rest_5_
  26.7 5.3 %collective-permute-done.6.rest_6_ = bf16[528,128]{1,0:T(8,128)(2,1)S(1)} collective-permute-done((bf16[528,128]{1,0:T(8,128)(2,1)S(1)}, bf16[528,128]{1,0:T(8,128)(2,1)S(1)}, u32[]{:S(2)}, u32[]{:S(2)}) %collective-permute-start.6) | collective-permute-done | bytes 135200 | tf_op jit(solution)/shard_map/ppermute | solution.py:258
  32.0 0.9 %score.1 = f32[8,8,128]{2,1,0:T(8,128)} custom-call(f32[512,1024]{1,0:T(8,128)S(1)} %inner.1.inner_ref, bf16[528,128]{1,0:T(8,128)(2,1)S(1)} %get-tuple-element.11.rest_0_, bf16[528,128]{1,0:T(8,128)(2,1)S(1)} %collective-permute-done.1.rest_1_, bf16[528,128]{1,0:T(8,128)(2,1)S(1)} %collective-permute-done.2.rest_2_, ...), custom_call_target="tpu_custom_call" | custom-call | flops 1048576 | bytes 3145728 | tf_op jit(solution)/shard_map/score/pallas_call | solution.py:313
  32.9 5.2 %all-to-all-start = ((f32[8,8,128]{2,1,0:T(8,128)}), f32[8,8,128]{2,1,0:T(8,128)S(1)}, u32[]{:S(2)}, u32[]{:S(2)}) async-start(f32[8,8,128]{2,1,0:T(8,128)} %score.1), calls=%async_computation | async-start | bytes 65536 | tf_op jit(solution)/shard_map/all_to_all | solution.py:322
  38.2 0.0 copy-start.3
  38.2 1.4 %copy-done.3 = bf16[1,1,768,1024]{3,2,1,0:T(8,128)(2,1)S(1)} copy-done((bf16[1,1,768,1024]{3,2,1,0:T(8,128)(2,1)S(1)}, bf16[1,1,768,1024]{3,2,1,0:T(8,128)(2,1)}, u32[]{:S(2)}) %copy-start.3) | copy-done | bytes 1572888
  39.6 5.6 %update.1 = f32[768,1024]{1,0:T(8,128)} custom-call(bf16[768,256]{1,0:T(8,128)(2,1)S(1)} %bitcast.19, bf16[768,256]{1,0:T(8,128)(2,1)S(1)} %collective-permute-done.other_ref, f32[768,1024]{1,0:T(8,128)} %bitcast.15, bf16[768,1024]{1,0:T(8,128)(2,1)S(1)} %bitcast.20, bf16[768,1024]{1,0:T(8,128)(2,1)S(1)} %bitcast.21, ...), custom_call_target="tpu_custom_call" | custom-call | flops 805306368 | bytes 10485760 | tf_op jit(solution)/shard_map/update/pallas_call | solution.py:325
  45.2 0.9 %combine.1 = f32[8,512]{1,0:T(8,128)} custom-call(s32[8,512]{1,0:T(8,128)S(1)} %bitcast.23, f32[16,512]{1,0:T(8,128)S(1)} %get-tuple-element.19.slots_ref, f32[8,8,128]{2,1,0:T(8,128)S(1)} %all-to-all-done.score_ref), custom_call_target="tpu_custom_call" | custom-call | flops 524288 | bytes 32768 | tf_op jit(solution)/shard_map/combine/pallas_call | solution.py:341
  (9 shorter events, 0.0 us)
Async XLA Ops:
  0.6 23.2 %copy-start.1 = (bf16[1,1,768,256]{3,2,1,0:T(8,128)(2,1)S(1)}, bf16[1,1,768,256]{3,2,1,0:T(8,128)(2,1)}, u32[]{:S(2)}) copy-start(bf16[1,1,768,256]{3,2,1,0:T(8,128)(2,1)} %param.10) | copy-start | bytes 1179652
  0.6 20.1 %collective-permute-start = (bf16[768,256]{1,0:T(8,128)(2,1)}, bf16[768,256]{1,0:T(8,128)(2,1)S(1)}, u32[]{:S(2)}, u32[]{:S(2)}) collective-permute-start(bf16[768,256]{1,0:T(8,128)(2,1)} %bitcast.17), channel_id=1, source_target_pairs={{0,16},{1,17},{2,18},{3,19},{16,0},{17,1},{18,2},{19,3},{4,20},{5,... | collective-permute-start | bytes 1179656 | tf_op jit(solution)/shard_map/ppermute | solution.py:258
  5.9 6.7 %collective-permute-start.1 = (bf16[528,128]{1,0:T(8,128)(2,1)S(1)}, bf16[528,128]{1,0:T(8,128)(2,1)S(1)}, u32[]{:S(2)}, u32[]{:S(2)}) collective-permute-start(bf16[528,128]{1,0:T(8,128)(2,1)S(1)} %get-tuple-element.12), channel_id=1, source_target_pairs={{0,1},{1,0},{2,3},{3,2},{16,17},{17,16},{18,19},{19,18},{4,5},{5,4... | collective-permute-start | bytes 405512 | tf_op jit(solution)/shard_map/ppermute | solution.py:258
  7.5 13.3 %collective-permute-start.2 = (bf16[528,128]{1,0:T(8,128)(2,1)S(1)}, bf16[528,128]{1,0:T(8,128)(2,1)S(1)}, u32[]{:S(2)}, u32[]{:S(2)}) collective-permute-start(bf16[528,128]{1,0:T(8,128)(2,1)S(1)} %get-tuple-element.13), channel_id=1, source_target_pairs={{0,2},{1,3},{2,0},{3,1},{16,18},{17,19},{18,16},{19,17},{4,6},{5,7... | collective-permute-start | bytes 405512 | tf_op jit(solution)/shard_map/ppermute | solution.py:258
  10.1 16.6 %collective-permute-start.3 = (bf16[528,128]{1,0:T(8,128)(2,1)S(1)}, bf16[528,128]{1,0:T(8,128)(2,1)S(1)}, u32[]{:S(2)}, u32[]{:S(2)}) collective-permute-start(bf16[528,128]{1,0:T(8,128)(2,1)S(1)} %get-tuple-element.14), channel_id=1, source_target_pairs={{0,3},{1,2},{2,1},{3,0},{16,19},{17,18},{18,17},{19,16},{4,7},{5,6... | collective-permute-start | bytes 405512 | tf_op jit(solution)/shard_map/ppermute | solution.py:258
  10.3 16.4 %collective-permute-start.4 = (bf16[528,128]{1,0:T(8,128)(2,1)S(1)}, bf16[528,128]{1,0:T(8,128)(2,1)S(1)}, u32[]{:S(2)}, u32[]{:S(2)}) collective-permute-start(bf16[528,128]{1,0:T(8,128)(2,1)S(1)} %get-tuple-element.15), channel_id=1, source_target_pairs={{0,16},{1,17},{2,18},{3,19},{16,0},{17,1},{18,2},{19,3},{4,20},{5,... | collective-permute-start | bytes 405512 | tf_op jit(solution)/shard_map/ppermute | solution.py:258
  12.5 14.2 %collective-permute-start.5 = (bf16[528,128]{1,0:T(8,128)(2,1)S(1)}, bf16[528,128]{1,0:T(8,128)(2,1)S(1)}, u32[]{:S(2)}, u32[]{:S(2)}) collective-permute-start(bf16[528,128]{1,0:T(8,128)(2,1)S(1)} %get-tuple-element.16), channel_id=1, source_target_pairs={{0,17},{1,16},{2,19},{3,18},{16,1},{17,0},{18,3},{19,2},{4,21},{5,... | collective-permute-start | bytes 405512 | tf_op jit(solution)/shard_map/ppermute | solution.py:258
  20.8 11.2 %collective-permute-start.6 = (bf16[528,128]{1,0:T(8,128)(2,1)S(1)}, bf16[528,128]{1,0:T(8,128)(2,1)S(1)}, u32[]{:S(2)}, u32[]{:S(2)}) collective-permute-start(bf16[528,128]{1,0:T(8,128)(2,1)S(1)} %get-tuple-element.17), channel_id=1, source_target_pairs={{0,18},{1,19},{2,16},{3,17},{16,2},{17,3},{18,0},{19,1},{4,22},{5,... | collective-permute-start | bytes 405512 | tf_op jit(solution)/shard_map/ppermute | solution.py:258
  20.8 11.2 %collective-permute-start.7 = (bf16[528,128]{1,0:T(8,128)(2,1)S(1)}, bf16[528,128]{1,0:T(8,128)(2,1)S(1)}, u32[]{:S(2)}, u32[]{:S(2)}) collective-permute-start(bf16[528,128]{1,0:T(8,128)(2,1)S(1)} %get-tuple-element.18), channel_id=1, source_target_pairs={{0,19},{1,18},{2,17},{3,16},{16,3},{17,2},{18,1},{19,0},{4,23},{5,... | collective-permute-start | bytes 405512 | tf_op jit(solution)/shard_map/ppermute | solution.py:258
  23.8 1.9 %copy-start = (f32[1,1,768,1024]{3,2,1,0:T(8,128)S(1)}, f32[1,1,768,1024]{3,2,1,0:T(8,128)}, u32[]{:S(2)}) copy-start(f32[1,1,768,1024]{3,2,1,0:T(8,128)} %param.11) | copy-start | bytes 9437188
  26.7 11.5 %copy-start.2 = (bf16[1,1,768,1024]{3,2,1,0:T(8,128)(2,1)S(1)}, bf16[1,1,768,1024]{3,2,1,0:T(8,128)(2,1)}, u32[]{:S(2)}) copy-start(bf16[1,1,768,1024]{3,2,1,0:T(8,128)(2,1)} %param.12) | copy-start | bytes 4718596
  32.9 12.2 %all-to-all-start = ((f32[8,8,128]{2,1,0:T(8,128)}), f32[8,8,128]{2,1,0:T(8,128)S(1)}, u32[]{:S(2)}, u32[]{:S(2)}) async-start(f32[8,8,128]{2,1,0:T(8,128)} %score.1), calls=%async_computation | async-start | bytes 65536 | tf_op jit(solution)/shard_map/all_to_all | solution.py:322
  38.2 1.4 %copy-start.3 = (bf16[1,1,768,1024]{3,2,1,0:T(8,128)(2,1)S(1)}, bf16[1,1,768,1024]{3,2,1,0:T(8,128)(2,1)}, u32[]{:S(2)}) copy-start(bf16[1,1,768,1024]{3,2,1,0:T(8,128)(2,1)} %param.13) | copy-start | bytes 4718596
  39.6 5.6 %copy-start.4 = (s32[1,512,8]{1,2,0:T(8,128)S(1)}, s32[1,512,8]{1,2,0:T(8,128)}, u32[]{:S(2)}) copy-start(s32[1,512,8]{1,2,0:T(8,128)} %param.9) | copy-start | bytes 49156

commit v4 on v3

--- a/solution.py
+++ b/solution.py
@@ -16,7 +16,7 @@
 
 LANES = 128
 TILE = 16
-VMEM_BYTES = 48 * 1024 * 1024
+VMEM_BYTES = 32 * 1024 * 1024
 F32 = jnp.float32
 BF16 = jnp.bfloat16
 
@@ -61,32 +61,31 @@
     return jnp.where(place == slots[k : k + 1, :], 1.0, 0.0).astype(BF16)
 
 
-def fill_chunks(steps, cap, pick, held, copies, tiles, chunks):
+def fill_chunks(group, cap, pick, held, copies, tiles, chunks):
     half = held.shape[2]
     data_rows = half // LANES * cap
     step = min(half, 2 * LANES)
     for side in range(2):
-        for at, k in enumerate(steps):
-            chunks[side * len(steps) + at][data_rows:, :] = tiles[k]
+        for k in range(group):
+            chunks[side, k][data_rows:, :] = tiles[k]
         copies[side].wait()
         for column in range(0, half, step):
             block = jnp.dot(
                 pick, held[side, :, column : column + step], preferred_element_type=F32
             ).astype(BF16)
-            for at in range(len(steps)):
-                chunk = chunks[side * len(steps) + at]
+            for k in range(group):
                 for part in range(step // LANES):
                     top = (column // LANES + part) * cap
-                    chunk[top : top + cap, :] = block[
-                        at * cap : (at + 1) * cap, part * LANES : (part + 1) * LANES
+                    chunks[side, k][top : top + cap, :] = block[
+                        k * cap : (k + 1) * cap, part * LANES : (part + 1) * LANES
                     ]
 
 
 def route_kernel(
-    steps, group, cap, ids_hbm, weight_hbm, grads_hbm, slots_ref, *rest
+    items, group, cap, ids_hbm, weight_hbm, grads_hbm, slots_ref, *rest
 ):
-    chunks = rest[: 2 * len(steps)]
-    ids_ref, weight_ref, held, sems = rest[2 * len(steps) :]
+    chunks = dict(zip(items, rest))
+    ids_ref, weight_ref, held, sems = rest[len(items) :]
     tokens = held.shape[1]
     me = ep_index()
     small = [
@@ -128,8 +127,8 @@
             spread, doubled, (((1,), (1,)), ((), ())), preferred_element_type=F32
         )
         tiles.append(jnp.where(kept, tile, 0.0).astype(BF16))
-    pick = jnp.concatenate([picks[k] for k in steps], axis=0)
-    fill_chunks(steps, cap, pick, held, copies, tiles, chunks)
+    pick = jnp.concatenate(picks, axis=0)
+    fill_chunks(group, cap, pick, held, copies, tiles, chunks)
 
 
 def inner_kernel(own_ref, other_ref, master_ref, inner_ref):
@@ -145,7 +144,8 @@
     chunks, out_ref = rest[:-1], rest[-1]
     blocks = inner_ref.shape[1] // LANES
     me = ep_index()
-    mine = own_half()
+    row = lax.broadcasted_iota(jnp.int32, out_ref.shape, 0)
+    result = jnp.zeros(out_ref.shape, F32)
     for k in range(group):
         sums = []
         for side in range(2):
@@ -157,15 +157,21 @@
             sums.append(total)
         both = jnp.concatenate(sums, axis=0)
         line = jnp.sum(both.T, axis=0, keepdims=True)
-        for side in range(2):
-            out_ref[(mine ^ side) * group + (me ^ k)] = jnp.broadcast_to(line, out_ref.shape[1:])
+        result = jnp.where(row == (me ^ k), line, result)
+    out_ref[...] = result
 
 
 def update_kernel(
-    group, cap, own_ref, other_ref, master_ref, moment_ref, second_ref, *rest
+    group, cap, own_ref, other_ref, master_ref, moment_hbm, second_hbm, *rest
 ):
     chunks = rest[: 2 * group]
-    update_hbm, rows, scaled, total, update, sems = rest[2 * group :]
+    update_hbm, rows, scaled, total, update, moment_ref, second_ref, sems = rest[2 * group :]
+    loads = [
+        pltpu.make_async_copy(moment_hbm, moment_ref, sems.at[0]),
+        pltpu.make_async_copy(second_hbm, second_ref, sems.at[1]),
+    ]
+    for load in loads:
+        load.start()
     slots = group * cap
     hid, half = update.shape
     data_rows = half // LANES * cap
@@ -215,13 +221,15 @@
 
     copies = []
     multiply(0)
+    for load in loads:
+        load.wait()
     for turn in range(half // step):
         if turn + 1 < half // step:
             multiply(turn + 1)
         adam(turn)
         columns = slice(turn * step, (turn + 1) * step)
         copies.append(
-            pltpu.make_async_copy(update.at[:, columns], update_hbm.at[:, columns], sems.at[turn])
+            pltpu.make_async_copy(update.at[:, columns], update_hbm.at[:, columns], sems.at[2 + turn])
         )
         copies[-1].start()
     for copy in copies:
@@ -232,12 +240,19 @@
     tokens = ids_ref.shape[1]
     me = ep_index()
     mine = own_half()
+    row = lax.broadcasted_iota(jnp.int32, score_ref.shape[1:], 0)
     lane = lax.broadcasted_iota(jnp.int32, (1, LANES), 1)
     lines = []
     for k in range(group):
-        own = score_ref[mine * group + (me ^ k)][0:1, :]
-        other = score_ref[(1 - mine) * group + (me ^ k)][0:1, :]
-        lines.append(jnp.where(lane < cap, own, other))
+        sides = [
+            jnp.sum(
+                jnp.where(row == me, score_ref[(mine ^ side) * group + (me ^ k)], 0.0),
+                axis=0,
+                keepdims=True,
+            )
+            for side in range(2)
+        ]
+        lines.append(jnp.where(lane < cap, sides[0], sides[1]))
     lines.append(jnp.zeros((LANES - group, LANES), F32))
     columns = jnp.concatenate(lines, axis=0).T
     columns = columns[:cap] + columns[cap : 2 * cap]
@@ -251,6 +266,8 @@
 
 
 def moved(array, side, step):
+    if (side, step) == (0, 0):
+        return array
     group = lax.axis_size("ep")
     pairs = [
         (p * group + e, (p ^ side) * group + (e ^ step)) for p in range(2) for e in range(group)
@@ -270,10 +287,11 @@
     param = master[0, 0]
     other_hidden = moved(own_hidden, 1, 0)
 
-    steps = list(range(group))
+    order = [(0, 1)] + [(side, k) for k in range(group - 1, 1, -1) for side in range(2)]
+    order += [(1, 1), (1, 0), (0, 0)]
     chunk = jax.ShapeDtypeStruct((half // LANES * cap + TILE, LANES), BF16)
     routed = pl.pallas_call(
-        functools.partial(route_kernel, steps, group, cap),
+        functools.partial(route_kernel, order, group, cap),
         out_shape=[jax.ShapeDtypeStruct((group + -group % TILE, tokens), F32)]
         + [chunk] * (2 * group),
         in_specs=specs(pltpu.HBM, 3),
@@ -292,12 +310,8 @@
         pltpu.with_memory_space_constraint(router_weights[0].T, pltpu.HBM),
         pltpu.with_memory_space_constraint(grad_out[0], pltpu.HBM),
     )
-    slot_of, sent = routed[0], routed[1:]
-    arrived = {(0, 0): sent[0]}
-    by_distance = list(range(group - 1, 1, -1))
-    order = [(0, 1)] + [(side, k) for k in by_distance for side in range(2)] + [(1, 1), (1, 0)]
-    for side, k in order:
-        arrived[side, k] = moved(sent[side * group + k], side, k)
+    slot_of = routed[0]
+    arrived = {item: moved(sent, *item) for item, sent in zip(order, routed[1:])}
     chunks = [arrived[side, k] for side in range(2) for k in range(group)]
 
     inner = pl.pallas_call(
@@ -312,32 +326,41 @@
 
     scores = pl.pallas_call(
         functools.partial(score_kernel, group, cap),
-        out_shape=jax.ShapeDtypeStruct((2 * group, 8, LANES), F32),
+        out_shape=jax.ShapeDtypeStruct((group + -group % 8, LANES), F32),
         in_specs=specs(pltpu.VMEM, 1 + 2 * group),
         out_specs=specs(pltpu.VMEM, 1)[0],
         compiler_params=params(),
         cost_estimate=cost(4 * slots * half, 12 * slots * half),
         name="score",
     )(inner, *chunks)
-    returned = lax.all_to_all(scores, ("pair", "ep"), split_axis=0, concat_axis=0, tiled=True)
+    returned = lax.all_gather(scores, ("pair", "ep"), axis=0, tiled=False)
 
     step = min(half, 2 * LANES)
     update = pl.pallas_call(
         functools.partial(update_kernel, group, cap),
         out_shape=jax.ShapeDtypeStruct((hid, half), F32),
-        in_specs=specs(pltpu.VMEM, 5 + 2 * group),
+        in_specs=specs(pltpu.VMEM, 3) + specs(pltpu.HBM, 2) + specs(pltpu.VMEM, 2 * group),
         out_specs=specs(pltpu.HBM, 1)[0],
         scratch_shapes=[
             pltpu.VMEM((2 * slots, half), BF16),
             pltpu.VMEM((hid, 2 * slots), BF16),
             pltpu.VMEM((2, hid, step), F32),
             pltpu.VMEM((hid, half), F32),
-            pltpu.SemaphoreType.DMA((half // step,)),
+            pltpu.VMEM((hid, half), BF16),
+            pltpu.VMEM((hid, half), BF16),
+            pltpu.SemaphoreType.DMA((2 + half // step,)),
         ],
         compiler_params=params(),
         cost_estimate=cost(4 * slots * hid * half, 12 * hid * half + 4 * slots * half),
         name="update",
-    )(own_hidden, other_hidden, param, moment[0, 0], second[0, 0], *chunks)
+    )(
+        own_hidden,
+        other_hidden,
+        param,
+        pltpu.with_memory_space_constraint(moment[0, 0], pltpu.HBM),
+        pltpu.with_memory_space_constraint(second[0, 0], pltpu.HBM),
+        *chunks,
+    )
     router = pl.pallas_call(
         functools.partial(combine_kernel, group, cap),
         out_shape=jax.ShapeDtypeStruct((top, tokens), F32),

time: 46.3 us -> 69.9 us (1.51)
  blocking collectives: 0 us -> 31.2 us
  starting transfers between devices: 16.6 us -> 11.3 us
  local copies, waits for them, and re-layouts: 3.31 us -> 1.91 us
  Pallas kernels: 10.5 us -> 9.74 us
    all_gather x0 -> x1, blocking collectives: none -> 31.2 us  [local(): returned = lax.all_gather(scores, ('pair', 'ep'), axis=0, tiled=False)]
    all_to_all x1 -> x0, starting transfers between devices: 5.25 us -> none  [local(): lax.all_to_all(scores, ('pair', 'ep'), split_axis=0, concat_axis=0, tiled...]
    unnamed x10 -> x8, local copies, waits for them, and re-layouts: 3.31 us -> 1.91 us
  transfers between devices with their start and end apart: 9 -> 8, of which waited for: 3 -> 3; matrix products, arithmetic and copies ran while one was open for 0% -> 0% of each run, Pallas kernels for 19% -> 5%
where the time goes in v4:
time: 69.9 us; the launch traced here: 69.7 us
  blocking collectives  31.2 us (45%)
  waiting for transfers between devices  14.9 us (21%)
  starting transfers between devices  11.3 us (16%)
  Pallas kernels  9.74 us (14%)
  local copies, waits for them, and re-layouts  1.91 us (3%)
  between operations  0.71 us (1%)
    all_gather x1, blocking collectives, local(): returned = lax.all_gather(scores, ('pair', 'ep'), axis=0, tiled=False)  31.2 us
    ppermute x8, waiting for transfers between devices, moved(): return lax.ppermute(array, ('pair', 'ep'), pairs)  14.9 us
    ppermute x8, starting transfers between devices, moved(): return lax.ppermute(array, ('pair', 'ep'), pairs)  11.3 us
    pallas_call x1, Pallas kernels, local(): pl.pallas_call(functools.partial(update_kernel, group, cap), out_shape=ja...  5.37 us
    pallas_call x1, Pallas kernels, local(): pl.pallas_call(functools.partial(route_kernel, order, group, cap), out_sh...  2.19 us
    unnamed x8, local copies, waits for them, and re-layouts  1.91 us
  transfers between devices with their start and end apart: 8, of which 3 were waited for; matrix products, arithmetic and copies ran while one was open for 0% of the time, Pallas kernels for 5%

profile of v4, /device:TPU:0, one launch (start us, length us, event | category | flops | bytes accessed | tf_op | source)
XLA Modules:
  0.0 69.7 jit_solution(5305901395521657854)
XLA Ops:
  0.6 3.0 %collective-permute-start = (bf16[768,256]{1,0:T(8,128)(2,1)}, bf16[768,256]{1,0:T(8,128)(2,1)S(1)}, u32[]{:S(2)}, u32[]{:S(2)}) collective-permute-start(bf16[768,256]{1,0:T(8,128)(2,1)} %bitcast.18), channel_id=1, source_target_pairs={{0,16},{1,17},{2,18},{3,19},{16,0},{17,1},{18,2},{19,3},{4,20},{5,... | collective-permute-start | bytes 1179656 | tf_op jit(solution)/shard_map/ppermute | solution.py:275
  3.7 2.2 %route.1 = (f32[16,512]{1,0:T(8,128)S(1)}, bf16[528,128]{1,0:T(8,128)(2,1)S(1)}, bf16[528,128]{1,0:T(8,128)(2,1)S(1)}, bf16[528,128]{1,0:T(8,128)(2,1)S(1)}, bf1...) custom-call(s32[8,512]{1,0:T(8,128)} %bitcast.22, ...), custom_call_target="tpu_custom_call" | custom-call | flops 536870912 | bytes 3145728 | tf_op jit(solution)/shard_map/route/pallas_call | solution.py:293
  5.9 1.6 %collective-permute-start.1 = (bf16[528,128]{1,0:T(8,128)(2,1)S(1)}, bf16[528,128]{1,0:T(8,128)(2,1)S(1)}, u32[]{:S(2)}, u32[]{:S(2)}) collective-permute-start(bf16[528,128]{1,0:T(8,128)(2,1)S(1)} %get-tuple-element.12), channel_id=1, source_target_pairs={{0,1},{1,0},{2,3},{3,2},{16,17},{17,16},{18,19},{19,18},{4,5},{5,4... | collective-permute-start | bytes 405512 | tf_op jit(solution)/shard_map/ppermute | solution.py:275
  7.5 2.6 %collective-permute-start.2 = (bf16[528,128]{1,0:T(8,128)(2,1)S(1)}, bf16[528,128]{1,0:T(8,128)(2,1)S(1)}, u32[]{:S(2)}, u32[]{:S(2)}) collective-permute-start(bf16[528,128]{1,0:T(8,128)(2,1)S(1)} %get-tuple-element.13), channel_id=1, source_target_pairs={{0,2},{1,3},{2,0},{3,1},{16,18},{17,19},{18,16},{19,17},{4,6},{5,7... | collective-permute-start | bytes 405512 | tf_op jit(solution)/shard_map/ppermute | solution.py:275
  10.1 0.2 collective-permute-start.3
  10.3 0.3 collective-permute-start.4
  10.6 1.9 %collective-permute-done.1.rest_1_ = bf16[528,128]{1,0:T(8,128)(2,1)S(1)} collective-permute-done((bf16[528,128]{1,0:T(8,128)(2,1)S(1)}, bf16[528,128]{1,0:T(8,128)(2,1)S(1)}, u32[]{:S(2)}, u32[]{:S(2)}) %collective-permute-start.1) | collective-permute-done | bytes 135200 | tf_op jit(solution)/shard_map/ppermute | solution.py:275
  12.5 0.6 collective-permute-start.5
  13.1 7.7 %collective-permute-done.2.rest_2_ = bf16[528,128]{1,0:T(8,128)(2,1)S(1)} collective-permute-done((bf16[528,128]{1,0:T(8,128)(2,1)S(1)}, bf16[528,128]{1,0:T(8,128)(2,1)S(1)}, u32[]{:S(2)}, u32[]{:S(2)}) %collective-permute-start.2) | collective-permute-done | bytes 135200 | tf_op jit(solution)/shard_map/ppermute | solution.py:275
  20.8 0.0 collective-permute-start.6
  20.8 0.0 collective-permute-done.other_ref
  20.8 3.0 %collective-permute-start.7 = (bf16[528,128]{1,0:T(8,128)(2,1)S(1)}, bf16[528,128]{1,0:T(8,128)(2,1)S(1)}, u32[]{:S(2)}, u32[]{:S(2)}) collective-permute-start(bf16[528,128]{1,0:T(8,128)(2,1)S(1)} %get-tuple-element.18), channel_id=1, source_target_pairs={{0,19},{1,18},{2,17},{3,16},{16,3},{17,2},{18,1},{19,0},{4,23},{5,... | collective-permute-start | bytes 405512 | tf_op jit(solution)/shard_map/ppermute | solution.py:275
  23.8 1.9 %copy-done = f32[1,1,768,1024]{3,2,1,0:T(8,128)S(1)} copy-done((f32[1,1,768,1024]{3,2,1,0:T(8,128)S(1)}, f32[1,1,768,1024]{3,2,1,0:T(8,128)}, u32[]{:S(2)}) %copy-start) | copy-done | bytes 3145752
  25.7 1.0 %inner.1.inner_ref = f32[512,1024]{1,0:T(8,128)S(1)} custom-call(bf16[768,256]{1,0:T(8,128)(2,1)S(1)} %bitcast.19, bf16[768,256]{1,0:T(8,128)(2,1)S(1)} %collective-permute-done.other_ref, f32[768,1024]{1,0:T(8,128)S(1)} %bitcast.16), custom_call_target="tpu_custom_call" | custom-call | flops 805306368 | bytes 5242880 | tf_op jit(solution)/shard_map/inner/pallas_call | solution.py:317
  26.7 0.0 copy-start.3
  26.7 0.0 copy-start.1
  26.7 0.0 collective-permute-done.3.rest_3_
  26.7 0.0 collective-permute-done.4.rest_4_
  26.7 0.0 collective-permute-done.5.rest_5_
  26.8 5.2 %collective-permute-done.6.rest_6_ = bf16[528,128]{1,0:T(8,128)(2,1)S(1)} collective-permute-done((bf16[528,128]{1,0:T(8,128)(2,1)S(1)}, bf16[528,128]{1,0:T(8,128)(2,1)S(1)}, u32[]{:S(2)}, u32[]{:S(2)}) %collective-permute-start.6) | collective-permute-done | bytes 135200 | tf_op jit(solution)/shard_map/ppermute | solution.py:275
  32.0 0.3 score.1
  32.3 31.2 %all-gather = f32[64,128]{1,0:T(8,128)S(1)} all-gather(f32[8,128]{1,0:T(8,128)S(1)} %score.1), channel_id=2, replica_groups=mesh['pair'=2,'rest'=4,'ep'=4] {'pair','ep'}, dimensions={0}, use_global_device_ids=true | all-gather | bytes 36864 | tf_op jit(solution)/shard_map/all_gather | solution.py:336
  63.5 0.9 %combine.1 = f32[8,512]{1,0:T(8,128)} custom-call(s32[8,512]{1,0:T(8,128)S(1)} %bitcast.23, f32[16,512]{1,0:T(8,128)S(1)} %get-tuple-element.19.slots_ref, f32[8,8,128]{2,1,0:T(8,128)S(1)} %bitcast.21), custom_call_target="tpu_custom_call" | custom-call | flops 524288 | bytes 32768 | tf_op jit(solution)/shard_map/combine/pallas_call | solution.py:364
  64.3 5.4 %update.1 = f32[768,1024]{1,0:T(8,128)} custom-call(bf16[768,256]{1,0:T(8,128)(2,1)S(1)} %bitcast.20, bf16[768,256]{1,0:T(8,128)(2,1)S(1)} %collective-permute-done.other_ref, f32[768,1024]{1,0:T(8,128)S(1)} %bitcast.17, bf16[768,1024]{1,0:T(8,128)(2,1)} %bitcast.26, bf16[768,1024]{1,0:T(8,128)(2,1)} %bitcast.27, ...), custom_call_target="tpu_custom_call" | custom-call | flops 805306368 | bytes 10485760 | tf_op jit(solution)/shard_map/update/pallas_call | solution.py:339
  (6 shorter events, 0.0 us)
Async XLA Ops:
  0.6 23.2 %copy-start.2 = (bf16[1,1,768,256]{3,2,1,0:T(8,128)(2,1)S(1)}, bf16[1,1,768,256]{3,2,1,0:T(8,128)(2,1)}, u32[]{:S(2)}) copy-start(bf16[1,1,768,256]{3,2,1,0:T(8,128)(2,1)} %param.10) | copy-start | bytes 1179652
  0.6 20.1 %collective-permute-start = (bf16[768,256]{1,0:T(8,128)(2,1)}, bf16[768,256]{1,0:T(8,128)(2,1)S(1)}, u32[]{:S(2)}, u32[]{:S(2)}) collective-permute-start(bf16[768,256]{1,0:T(8,128)(2,1)} %bitcast.18), channel_id=1, source_target_pairs={{0,16},{1,17},{2,18},{3,19},{16,0},{17,1},{18,2},{19,3},{4,20},{5,... | collective-permute-start | bytes 1179656 | tf_op jit(solution)/shard_map/ppermute | solution.py:275
  5.9 6.7 %collective-permute-start.1 = (bf16[528,128]{1,0:T(8,128)(2,1)S(1)}, bf16[528,128]{1,0:T(8,128)(2,1)S(1)}, u32[]{:S(2)}, u32[]{:S(2)}) collective-permute-start(bf16[528,128]{1,0:T(8,128)(2,1)S(1)} %get-tuple-element.12), channel_id=1, source_target_pairs={{0,1},{1,0},{2,3},{3,2},{16,17},{17,16},{18,19},{19,18},{4,5},{5,4... | collective-permute-start | bytes 405512 | tf_op jit(solution)/shard_map/ppermute | solution.py:275
  7.5 13.3 %collective-permute-start.2 = (bf16[528,128]{1,0:T(8,128)(2,1)S(1)}, bf16[528,128]{1,0:T(8,128)(2,1)S(1)}, u32[]{:S(2)}, u32[]{:S(2)}) collective-permute-start(bf16[528,128]{1,0:T(8,128)(2,1)S(1)} %get-tuple-element.13), channel_id=1, source_target_pairs={{0,2},{1,3},{2,0},{3,1},{16,18},{17,19},{18,16},{19,17},{4,6},{5,7... | collective-permute-start | bytes 405512 | tf_op jit(solution)/shard_map/ppermute | solution.py:275
  10.1 16.6 %collective-permute-start.3 = (bf16[528,128]{1,0:T(8,128)(2,1)S(1)}, bf16[528,128]{1,0:T(8,128)(2,1)S(1)}, u32[]{:S(2)}, u32[]{:S(2)}) collective-permute-start(bf16[528,128]{1,0:T(8,128)(2,1)S(1)} %get-tuple-element.14), channel_id=1, source_target_pairs={{0,3},{1,2},{2,1},{3,0},{16,19},{17,18},{18,17},{19,16},{4,7},{5,6... | collective-permute-start | bytes 405512 | tf_op jit(solution)/shard_map/ppermute | solution.py:275
  10.3 16.4 %collective-permute-start.4 = (bf16[528,128]{1,0:T(8,128)(2,1)S(1)}, bf16[528,128]{1,0:T(8,128)(2,1)S(1)}, u32[]{:S(2)}, u32[]{:S(2)}) collective-permute-start(bf16[528,128]{1,0:T(8,128)(2,1)S(1)} %get-tuple-element.15), channel_id=1, source_target_pairs={{0,16},{1,17},{2,18},{3,19},{16,0},{17,1},{18,2},{19,3},{4,20},{5,... | collective-permute-start | bytes 405512 | tf_op jit(solution)/shard_map/ppermute | solution.py:275
  12.5 14.2 %collective-permute-start.5 = (bf16[528,128]{1,0:T(8,128)(2,1)S(1)}, bf16[528,128]{1,0:T(8,128)(2,1)S(1)}, u32[]{:S(2)}, u32[]{:S(2)}) collective-permute-start(bf16[528,128]{1,0:T(8,128)(2,1)S(1)} %get-tuple-element.16), channel_id=1, source_target_pairs={{0,17},{1,16},{2,19},{3,18},{16,1},{17,0},{18,3},{19,2},{4,21},{5,... | collective-permute-start | bytes 405512 | tf_op jit(solution)/shard_map/ppermute | solution.py:275
  20.8 11.2 %collective-permute-start.6 = (bf16[528,128]{1,0:T(8,128)(2,1)S(1)}, bf16[528,128]{1,0:T(8,128)(2,1)S(1)}, u32[]{:S(2)}, u32[]{:S(2)}) collective-permute-start(bf16[528,128]{1,0:T(8,128)(2,1)S(1)} %get-tuple-element.17), channel_id=1, source_target_pairs={{0,18},{1,19},{2,16},{3,17},{16,2},{17,3},{18,0},{19,1},{4,22},{5,... | collective-permute-start | bytes 405512 | tf_op jit(solution)/shard_map/ppermute | solution.py:275
  20.8 11.2 %collective-permute-start.7 = (bf16[528,128]{1,0:T(8,128)(2,1)S(1)}, bf16[528,128]{1,0:T(8,128)(2,1)S(1)}, u32[]{:S(2)}, u32[]{:S(2)}) collective-permute-start(bf16[528,128]{1,0:T(8,128)(2,1)S(1)} %get-tuple-element.18), channel_id=1, source_target_pairs={{0,19},{1,18},{2,17},{3,16},{16,3},{17,2},{18,1},{19,0},{4,23},{5,... | collective-permute-start | bytes 405512 | tf_op jit(solution)/shard_map/ppermute | solution.py:275
  23.8 1.9 %copy-start = (f32[1,1,768,1024]{3,2,1,0:T(8,128)S(1)}, f32[1,1,768,1024]{3,2,1,0:T(8,128)}, u32[]{:S(2)}) copy-start(f32[1,1,768,1024]{3,2,1,0:T(8,128)} %param.11) | copy-start | bytes 9437188
  26.7 36.8 %copy-start.3 = (s32[1,512,8]{1,2,0:T(8,128)S(1)}, s32[1,512,8]{1,2,0:T(8,128)}, u32[]{:S(2)}) copy-start(s32[1,512,8]{1,2,0:T(8,128)} %param.9) | copy-start | bytes 49156
  26.7 37.6 %copy-start.1 = (f32[1,1,768,1024]{3,2,1,0:T(8,128)S(1)}, f32[1,1,768,1024]{3,2,1,0:T(8,128)}, u32[]{:S(2)}) copy-start(f32[1,1,768,1024]{3,2,1,0:T(8,128)} %param.11) | copy-start | bytes 9437188

commit v5 on v4

--- a/solution.py
+++ b/solution.py
@@ -140,31 +140,30 @@
         )
 
 
-def score_kernel(group, cap, inner_ref, *rest):
-    chunks, out_ref = rest[:-1], rest[-1]
+def score_kernel(items, group, cap, inner_ref, *rest):
+    chunks, out_ref = dict(zip(items, rest)), rest[-1]
     blocks = inner_ref.shape[1] // LANES
     me = ep_index()
-    row = lax.broadcasted_iota(jnp.int32, out_ref.shape, 0)
-    result = jnp.zeros(out_ref.shape, F32)
+    mine = own_half()
     for k in range(group):
         sums = []
         for side in range(2):
             start = pl.multiple_of(side * group * cap + (me ^ k) * cap, cap)
             total = jnp.zeros((cap, LANES), F32)
             for block in range(blocks):
-                rows = chunks[side * group + k][block * cap : (block + 1) * cap, :].astype(F32)
+                rows = chunks[side, k][block * cap : (block + 1) * cap, :].astype(F32)
                 total += rows * inner_ref[pl.ds(start, cap), block * LANES : (block + 1) * LANES]
             sums.append(total)
         both = jnp.concatenate(sums, axis=0)
         line = jnp.sum(both.T, axis=0, keepdims=True)
-        result = jnp.where(row == (me ^ k), line, result)
-    out_ref[...] = result
+        for side in range(2):
+            out_ref[(mine ^ side) * group + (me ^ k)] = jnp.broadcast_to(line, out_ref.shape[1:])
 
 
 def update_kernel(
-    group, cap, own_ref, other_ref, master_ref, moment_hbm, second_hbm, *rest
+    items, group, cap, own_ref, other_ref, master_ref, moment_hbm, second_hbm, *rest
 ):
-    chunks = rest[: 2 * group]
+    chunks = dict(zip(items, rest))
     update_hbm, rows, scaled, total, update, moment_ref, second_ref, sems = rest[2 * group :]
     loads = [
         pltpu.make_async_copy(moment_hbm, moment_ref, sems.at[0]),
@@ -179,7 +178,7 @@
     for side in range(2):
         tile = jnp.zeros((TILE, LANES), F32)
         for k in range(group):
-            chunk = chunks[side * group + k]
+            chunk = chunks[side, k]
             tile += chunk[data_rows : data_rows + TILE, :].astype(F32)
             start = pl.multiple_of(side * slots + (me ^ k) * cap, cap)
             for block in range(half // LANES):
@@ -240,19 +239,12 @@
     tokens = ids_ref.shape[1]
     me = ep_index()
     mine = own_half()
-    row = lax.broadcasted_iota(jnp.int32, score_ref.shape[1:], 0)
     lane = lax.broadcasted_iota(jnp.int32, (1, LANES), 1)
     lines = []
     for k in range(group):
-        sides = [
-            jnp.sum(
-                jnp.where(row == me, score_ref[(mine ^ side) * group + (me ^ k)], 0.0),
-                axis=0,
-                keepdims=True,
-            )
-            for side in range(2)
-        ]
-        lines.append(jnp.where(lane < cap, sides[0], sides[1]))
+        own = score_ref[mine * group + (me ^ k)][0:1, :]
+        other = score_ref[(1 - mine) * group + (me ^ k)][0:1, :]
+        lines.append(jnp.where(lane < cap, own, other))
     lines.append(jnp.zeros((LANES - group, LANES), F32))
     columns = jnp.concatenate(lines, axis=0).T
     columns = columns[:cap] + columns[cap : 2 * cap]
@@ -312,7 +304,7 @@
     )
     slot_of = routed[0]
     arrived = {item: moved(sent, *item) for item, sent in zip(order, routed[1:])}
-    chunks = [arrived[side, k] for side in range(2) for k in range(group)]
+    chunks = [arrived[item] for item in order]
 
     inner = pl.pallas_call(
         inner_kernel,
@@ -325,19 +317,19 @@
     )(own_hidden, other_hidden, param)
 
     scores = pl.pallas_call(
-        functools.partial(score_kernel, group, cap),
-        out_shape=jax.ShapeDtypeStruct((group + -group % 8, LANES), F32),
+        functools.partial(score_kernel, order, group, cap),
+        out_shape=jax.ShapeDtypeStruct((2 * group, 8, LANES), F32),
         in_specs=specs(pltpu.VMEM, 1 + 2 * group),
         out_specs=specs(pltpu.VMEM, 1)[0],
         compiler_params=params(),
         cost_estimate=cost(4 * slots * half, 12 * slots * half),
         name="score",
     )(inner, *chunks)
-    returned = lax.all_gather(scores, ("pair", "ep"), axis=0, tiled=False)
+    returned = lax.all_to_all(scores, ("pair", "ep"), split_axis=0, concat_axis=0, tiled=True)
 
     step = min(half, 2 * LANES)
     update = pl.pallas_call(
-        functools.partial(update_kernel, group, cap),
+        functools.partial(update_kernel, order, group, cap),
         out_shape=jax.ShapeDtypeStruct((hid, half), F32),
         in_specs=specs(pltpu.VMEM, 3) + specs(pltpu.HBM, 2) + specs(pltpu.VMEM, 2 * group),
         out_specs=specs(pltpu.HBM, 1)[0],

time: 69.9 us -> 61.2 us (0.88)
  blocking collectives: 31.2 us -> 0 us
  starting transfers between devices: 11.3 us -> 27.9 us
  local copies, waits for them, and re-layouts: 1.91 us -> 15.3 us
  waiting for transfers between devices: 14.9 us -> 6.07 us
  Pallas kernels: 9.74 us -> 10.5 us
    all_gather x1 -> x0, blocking collectives: 31.2 us -> none  [local(): returned = lax.all_gather(scores, ('pair', 'ep'), axis=0, tiled=False)]
    unnamed x8 -> x50, local copies, waits for them, and re-layouts: 1.91 us -> 15.3 us
    ppermute x8, starting transfers between devices: 11.3 us -> 23.2 us  [moved(): return lax.ppermute(array, ('pair', 'ep'), pairs)]
    ppermute x8, waiting for transfers between devices: 14.9 us -> 6.07 us  [moved(): return lax.ppermute(array, ('pair', 'ep'), pairs)]
    all_to_all x0 -> x1, starting transfers between devices: none -> 4.69 us  [local(): lax.all_to_all(scores, ('pair', 'ep'), split_axis=0, concat_axis=0, tiled...]
    pallas_call x1, Pallas kernels: 0.87 us -> 1.62 us  [local(): pl.pallas_call(functools.partial(combine_kernel, group, cap), out_shape=j...]
  transfers between devices with their start and end apart: 8 -> 9, of which waited for: 3 -> 5; matrix products, arithmetic and copies ran while one was open for 0% -> 0% of each run, Pallas kernels for 5% -> 14%
where the time goes in v5:
time: 61.2 us; the launch traced here: 60.6 us
  starting transfers between devices  27.9 us (46%)
  local copies, waits for them, and re-layouts  15.3 us (25%)
  Pallas kernels  10.5 us (17%)
  waiting for transfers between devices  6.07 us (10%)
  between operations  0.77 us (1%)
    ppermute x8, starting transfers between devices, moved(): return lax.ppermute(array, ('pair', 'ep'), pairs)  23.2 us
    unnamed x50, local copies, waits for them, and re-layouts  15.3 us
    ppermute x8, waiting for transfers between devices, moved(): return lax.ppermute(array, ('pair', 'ep'), pairs)  6.07 us
    pallas_call x1, Pallas kernels, local(): pl.pallas_call(functools.partial(update_kernel, order, group, cap), out_s...  5.37 us
    all_to_all x1, starting transfers between devices, local(): lax.all_to_all(scores, ('pair', 'ep'), split_axis=0, concat_axis=0, tiled...  4.69 us
    pallas_call x1, Pallas kernels, local(): pl.pallas_call(functools.partial(route_kernel, order, group, cap), out_sh...  2.19 us
    pallas_call x1, Pallas kernels, local(): pl.pallas_call(functools.partial(combine_kernel, group, cap), out_shape=j...  1.62 us
  transfers between devices with their start and end apart: 9, of which 5 were waited for; matrix products, arithmetic and copies ran while one was open for 0% of the time, Pallas kernels for 14%

profile of v5, /device:TPU:0, one launch (start us, length us, event | category | flops | bytes accessed | tf_op | source)
XLA Modules:
  0.0 60.6 jit_solution(16266230813366957221)
XLA Ops:
  0.6 3.0 %collective-permute-start = (bf16[768,256]{1,0:T(8,128)(2,1)}, bf16[768,256]{1,0:T(8,128)(2,1)S(1)}, u32[]{:S(2)}, u32[]{:S(2)}) collective-permute-start(bf16[768,256]{1,0:T(8,128)(2,1)} %bitcast.17), channel_id=1, source_target_pairs={{0,16},{1,17},{2,18},{3,19},{16,0},{17,1},{18,2},{19,3},{4,20},{5,... | collective-permute-start | bytes 1179656 | tf_op jit(solution)/shard_map/ppermute | solution.py:267
  3.7 2.2 %route.1 = (f32[16,512]{1,0:T(8,128)S(1)}, bf16[528,128]{1,0:T(8,128)(2,1)S(1)}, bf16[528,128]{1,0:T(8,128)(2,1)S(1)}, bf16[528,128]{1,0:T(8,128)(2,1)S(1)}, bf1...) custom-call(s32[8,512]{1,0:T(8,128)} %bitcast.20, ...), custom_call_target="tpu_custom_call" | custom-call | flops 536870912 | bytes 3145728 | tf_op jit(solution)/shard_map/route/pallas_call | solution.py:285
  6.5 1.6 %collective-permute-start.1 = (bf16[528,128]{1,0:T(8,128)(2,1)S(1)}, bf16[528,128]{1,0:T(8,128)(2,1)S(1)}, u32[]{:S(2)}, u32[]{:S(2)}) collective-permute-start(bf16[528,128]{1,0:T(8,128)(2,1)S(1)} %get-tuple-element.11), channel_id=1, source_target_pairs={{0,1},{1,0},{2,3},{3,2},{16,17},{17,16},{18,19},{19,18},{4,5},{5,4... | collective-permute-start | bytes 405512 | tf_op jit(solution)/shard_map/ppermute | solution.py:267
  8.1 2.5 %collective-permute-start.2 = (bf16[528,128]{1,0:T(8,128)(2,1)S(1)}, bf16[528,128]{1,0:T(8,128)(2,1)S(1)}, u32[]{:S(2)}, u32[]{:S(2)}) collective-permute-start(bf16[528,128]{1,0:T(8,128)(2,1)S(1)} %get-tuple-element.12), channel_id=1, source_target_pairs={{0,3},{1,2},{2,1},{3,0},{16,19},{17,18},{18,17},{19,16},{4,7},{5,6... | collective-permute-start | bytes 405512 | tf_op jit(solution)/shard_map/ppermute | solution.py:267
  10.5 1.3 %collective-permute-start.3 = (bf16[528,128]{1,0:T(8,128)(2,1)S(1)}, bf16[528,128]{1,0:T(8,128)(2,1)S(1)}, u32[]{:S(2)}, u32[]{:S(2)}) collective-permute-start(bf16[528,128]{1,0:T(8,128)(2,1)S(1)} %get-tuple-element.13), channel_id=1, source_target_pairs={{0,19},{1,18},{2,17},{3,16},{16,3},{17,2},{18,1},{19,0},{4,23},{5,... | collective-permute-start | bytes 405512 | tf_op jit(solution)/shard_map/ppermute | solution.py:267
  12.6 3.1 %collective-permute-start.5 = (bf16[528,128]{1,0:T(8,128)(2,1)S(1)}, bf16[528,128]{1,0:T(8,128)(2,1)S(1)}, u32[]{:S(2)}, u32[]{:S(2)}) collective-permute-start(bf16[528,128]{1,0:T(8,128)(2,1)S(1)} %get-tuple-element.15), channel_id=1, source_target_pairs={{0,18},{1,19},{2,16},{3,17},{16,2},{17,3},{18,0},{19,1},{4,22},{5,... | collective-permute-start | bytes 405512 | tf_op jit(solution)/shard_map/ppermute | solution.py:267
  15.7 2.2 %collective-permute-done.2.rest_1_ = bf16[528,128]{1,0:T(8,128)(2,1)S(1)} collective-permute-done((bf16[528,128]{1,0:T(8,128)(2,1)S(1)}, bf16[528,128]{1,0:T(8,128)(2,1)S(1)}, u32[]{:S(2)}, u32[]{:S(2)}) %collective-permute-start.2) | collective-permute-done | bytes 135200 | tf_op jit(solution)/shard_map/ppermute | solution.py:267
  18.0 9.0 %collective-permute-start.6 = (bf16[528,128]{1,0:T(8,128)(2,1)S(1)}, bf16[528,128]{1,0:T(8,128)(2,1)S(1)}, u32[]{:S(2)}, u32[]{:S(2)}) collective-permute-start(bf16[528,128]{1,0:T(8,128)(2,1)S(1)} %get-tuple-element.16), channel_id=1, source_target_pairs={{0,17},{1,16},{2,19},{3,18},{16,1},{17,0},{18,3},{19,2},{4,21},{5,... | collective-permute-start | bytes 405512 | tf_op jit(solution)/shard_map/ppermute | solution.py:267
  27.0 1.9 %collective-permute-start.7 = (bf16[528,128]{1,0:T(8,128)(2,1)S(1)}, bf16[528,128]{1,0:T(8,128)(2,1)S(1)}, u32[]{:S(2)}, u32[]{:S(2)}) collective-permute-start(bf16[528,128]{1,0:T(8,128)(2,1)S(1)} %get-tuple-element.17), channel_id=1, source_target_pairs={{0,16},{1,17},{2,18},{3,19},{16,0},{17,1},{18,2},{19,3},{4,20},{5,... | collective-permute-start | bytes 405512 | tf_op jit(solution)/shard_map/ppermute | solution.py:267
  28.9 1.9 %copy-done = f32[1,1,768,1024]{3,2,1,0:T(8,128)S(1)} copy-done((f32[1,1,768,1024]{3,2,1,0:T(8,128)S(1)}, f32[1,1,768,1024]{3,2,1,0:T(8,128)}, u32[]{:S(2)}) %copy-start) | copy-done | bytes 3145752
  30.8 1.0 %inner.1.inner_ref = f32[512,1024]{1,0:T(8,128)S(1)} custom-call(bf16[768,256]{1,0:T(8,128)(2,1)S(1)} %bitcast.18, bf16[768,256]{1,0:T(8,128)(2,1)S(1)} %collective-permute-done.other_ref, f32[768,1024]{1,0:T(8,128)S(1)} %bitcast.15), custom_call_target="tpu_custom_call" | custom-call | flops 805306368 | bytes 5242880 | tf_op jit(solution)/shard_map/inner/pallas_call | solution.py:309
  31.9 0.9 %collective-permute-done.4.rest_3_ = bf16[528,128]{1,0:T(8,128)(2,1)S(1)} collective-permute-done((bf16[528,128]{1,0:T(8,128)(2,1)S(1)}, bf16[528,128]{1,0:T(8,128)(2,1)S(1)}, u32[]{:S(2)}, u32[]{:S(2)}) %collective-permute-start.4) | collective-permute-done | bytes 135200 | tf_op jit(solution)/shard_map/ppermute | solution.py:267
  32.8 1.8 %collective-permute-done.5.rest_4_ = bf16[528,128]{1,0:T(8,128)(2,1)S(1)} collective-permute-done((bf16[528,128]{1,0:T(8,128)(2,1)S(1)}, bf16[528,128]{1,0:T(8,128)(2,1)S(1)}, u32[]{:S(2)}, u32[]{:S(2)}) %collective-permute-start.5) | collective-permute-done | bytes 135200 | tf_op jit(solution)/shard_map/ppermute | solution.py:267
  39.9 4.7 %all-to-all-start = ((f32[8,8,128]{2,1,0:T(8,128)}), f32[8,8,128]{2,1,0:T(8,128)}, u32[]{:S(2)}, u32[]{:S(2)}) async-start(f32[8,8,128]{2,1,0:T(8,128)} %copy-done.21), calls=%async_computation | async-start | bytes 65536 | tf_op jit(solution)/shard_map/all_to_all | solution.py:328
  44.6 1.0 %copy-done.4 = bf16[768,256]{1,0:T(8,128)(2,1)S(1)} copy-done((bf16[768,256]{1,0:T(8,128)(2,1)S(1)}, bf16[768,256]{1,0:T(8,128)(2,1)}, u32[]{:S(2)}) %copy-start.4) | copy-done | bytes 393240
  45.6 0.9 %copy-done.6 = bf16[528,128]{1,0:T(8,128)(2,1)S(1)} copy-done((bf16[528,128]{1,0:T(8,128)(2,1)S(1)}, bf16[528,128]{1,0:T(8,128)(2,1)}, u32[]{:S(2)}) %copy-start.6) | copy-done | bytes 135192
  46.5 0.9 %copy-done.8 = bf16[528,128]{1,0:T(8,128)(2,1)S(1)} copy-done((bf16[528,128]{1,0:T(8,128)(2,1)S(1)}, bf16[528,128]{1,0:T(8,128)(2,1)}, u32[]{:S(2)}) %copy-start.8) | copy-done | bytes 135192
  47.4 0.9 %copy-done.10 = bf16[528,128]{1,0:T(8,128)(2,1)S(1)} copy-done((bf16[528,128]{1,0:T(8,128)(2,1)S(1)}, bf16[528,128]{1,0:T(8,128)(2,1)}, u32[]{:S(2)}) %copy-start.10) | copy-done | bytes 135192
  48.3 0.9 %copy-done.12 = bf16[528,128]{1,0:T(8,128)(2,1)S(1)} copy-done((bf16[528,128]{1,0:T(8,128)(2,1)S(1)}, bf16[528,128]{1,0:T(8,128)(2,1)}, u32[]{:S(2)}) %copy-start.12) | copy-done | bytes 135192
  49.2 0.9 %copy-done.14 = bf16[528,128]{1,0:T(8,128)(2,1)S(1)} copy-done((bf16[528,128]{1,0:T(8,128)(2,1)S(1)}, bf16[528,128]{1,0:T(8,128)(2,1)}, u32[]{:S(2)}) %copy-start.14) | copy-done | bytes 135192
  50.1 0.9 %copy-done.16 = bf16[528,128]{1,0:T(8,128)(2,1)S(1)} copy-done((bf16[528,128]{1,0:T(8,128)(2,1)S(1)}, bf16[528,128]{1,0:T(8,128)(2,1)}, u32[]{:S(2)}) %copy-start.16) | copy-done | bytes 135192
  51.0 0.9 %copy-done.18 = bf16[528,128]{1,0:T(8,128)(2,1)S(1)} copy-done((bf16[528,128]{1,0:T(8,128)(2,1)S(1)}, bf16[528,128]{1,0:T(8,128)(2,1)}, u32[]{:S(2)}) %copy-start.18) | copy-done | bytes 135192
  52.8 5.4 %update.1 = f32[768,1024]{1,0:T(8,128)} custom-call(bf16[768,256]{1,0:T(8,128)(2,1)S(1)} %bitcast.19, bf16[768,256]{1,0:T(8,128)(2,1)S(1)} %copy-done.4, f32[768,1024]{1,0:T(8,128)S(1)} %bitcast.16, bf16[768,1024]{1,0:T(8,128)(2,1)} %bitcast.24, bf16[768,1024]{1,0:T(8,128)(2,1)} %bitcast.25, bf16[528,128]{1,0:T(8,128)(2,1)S(1)} %copy-done.8, ...), custom_call_target="tpu_custom_call" | custom-call | flops 805306368 | bytes 10485760 | tf_op jit(solution)/shard_map/update/pallas_call | solution.py:331
  59.0 1.6 %combine.1 = f32[8,512]{1,0:T(8,128)} custom-call(s32[8,512]{1,0:T(8,128)S(1)} %bitcast.21, f32[16,512]{1,0:T(8,128)S(1)} %copy-done.24, f32[8,8,128]{2,1,0:T(8,128)} %all-to-all-done.score_ref), custom_call_target="tpu_custom_call" | custom-call | flops 524288 | bytes 32768 | tf_op jit(solution)/shard_map/combine/pallas_call | solution.py:356
  (49 shorter events, 8.4 us)
Async XLA Ops:
  0.6 28.3 %copy-start.2 = (bf16[1,1,768,256]{3,2,1,0:T(8,128)(2,1)S(1)}, bf16[1,1,768,256]{3,2,1,0:T(8,128)(2,1)}, u32[]{:S(2)}) copy-start(bf16[1,1,768,256]{3,2,1,0:T(8,128)(2,1)} %param.10) | copy-start | bytes 1179652
  0.6 26.3 %collective-permute-start = (bf16[768,256]{1,0:T(8,128)(2,1)}, bf16[768,256]{1,0:T(8,128)(2,1)S(1)}, u32[]{:S(2)}, u32[]{:S(2)}) collective-permute-start(bf16[768,256]{1,0:T(8,128)(2,1)} %bitcast.17), channel_id=1, source_target_pairs={{0,16},{1,17},{2,18},{3,19},{16,0},{17,1},{18,2},{19,3},{4,20},{5,... | collective-permute-start | bytes 1179656 | tf_op jit(solution)/shard_map/ppermute | solution.py:267
  6.5 29.2 %copy-start.5 = (bf16[528,128]{1,0:T(8,128)(2,1)}, bf16[528,128]{1,0:T(8,128)(2,1)S(1)}, u32[]{:S(2)}) copy-start(bf16[528,128]{1,0:T(8,128)(2,1)S(1)} %get-tuple-element.18.rest_7_) | copy-start | bytes 405508
  6.5 6.1 %collective-permute-start.1 = (bf16[528,128]{1,0:T(8,128)(2,1)S(1)}, bf16[528,128]{1,0:T(8,128)(2,1)S(1)}, u32[]{:S(2)}, u32[]{:S(2)}) collective-permute-start(bf16[528,128]{1,0:T(8,128)(2,1)S(1)} %get-tuple-element.11), channel_id=1, source_target_pairs={{0,1},{1,0},{2,3},{3,2},{16,17},{17,16},{18,19},{19,18},{4,5},{5,4... | collective-permute-start | bytes 405512 | tf_op jit(solution)/shard_map/ppermute | solution.py:267
  8.1 9.9 %collective-permute-start.2 = (bf16[528,128]{1,0:T(8,128)(2,1)S(1)}, bf16[528,128]{1,0:T(8,128)(2,1)S(1)}, u32[]{:S(2)}, u32[]{:S(2)}) collective-permute-start(bf16[528,128]{1,0:T(8,128)(2,1)S(1)} %get-tuple-element.12), channel_id=1, source_target_pairs={{0,3},{1,2},{2,1},{3,0},{16,19},{17,18},{18,17},{19,16},{4,7},{5,6... | collective-permute-start | bytes 405512 | tf_op jit(solution)/shard_map/ppermute | solution.py:267
  10.5 21.3 %collective-permute-start.3 = (bf16[528,128]{1,0:T(8,128)(2,1)S(1)}, bf16[528,128]{1,0:T(8,128)(2,1)S(1)}, u32[]{:S(2)}, u32[]{:S(2)}) collective-permute-start(bf16[528,128]{1,0:T(8,128)(2,1)S(1)} %get-tuple-element.13), channel_id=1, source_target_pairs={{0,19},{1,18},{2,17},{3,16},{16,3},{17,2},{18,1},{19,0},{4,23},{5,... | collective-permute-start | bytes 405512 | tf_op jit(solution)/shard_map/ppermute | solution.py:267
  11.8 21.0 %collective-permute-start.4 = (bf16[528,128]{1,0:T(8,128)(2,1)S(1)}, bf16[528,128]{1,0:T(8,128)(2,1)S(1)}, u32[]{:S(2)}, u32[]{:S(2)}) collective-permute-start(bf16[528,128]{1,0:T(8,128)(2,1)S(1)} %get-tuple-element.14), channel_id=1, source_target_pairs={{0,2},{1,3},{2,0},{3,1},{16,18},{17,19},{18,16},{19,17},{4,6},{5,7... | collective-permute-start | bytes 405512 | tf_op jit(solution)/shard_map/ppermute | solution.py:267
  12.6 23.1 %copy-start.7 = (bf16[528,128]{1,0:T(8,128)(2,1)}, bf16[528,128]{1,0:T(8,128)(2,1)S(1)}, u32[]{:S(2)}) copy-start(bf16[528,128]{1,0:T(8,128)(2,1)S(1)} %collective-permute-done.1.rest_0_) | copy-start | bytes 405508
  12.6 22.0 %collective-permute-start.5 = (bf16[528,128]{1,0:T(8,128)(2,1)S(1)}, bf16[528,128]{1,0:T(8,128)(2,1)S(1)}, u32[]{:S(2)}, u32[]{:S(2)}) collective-permute-start(bf16[528,128]{1,0:T(8,128)(2,1)S(1)} %get-tuple-element.15), channel_id=1, source_target_pairs={{0,18},{1,19},{2,16},{3,17},{16,2},{17,3},{18,0},{19,1},{4,22},{5,... | collective-permute-start | bytes 405512 | tf_op jit(solution)/shard_map/ppermute | solution.py:267
  18.0 17.7 %copy-start.9 = (bf16[528,128]{1,0:T(8,128)(2,1)}, bf16[528,128]{1,0:T(8,128)(2,1)S(1)}, u32[]{:S(2)}) copy-start(bf16[528,128]{1,0:T(8,128)(2,1)S(1)} %collective-permute-done.2.rest_1_) | copy-start | bytes 405508
  18.0 17.4 %collective-permute-start.6 = (bf16[528,128]{1,0:T(8,128)(2,1)S(1)}, bf16[528,128]{1,0:T(8,128)(2,1)S(1)}, u32[]{:S(2)}, u32[]{:S(2)}) collective-permute-start(bf16[528,128]{1,0:T(8,128)(2,1)S(1)} %get-tuple-element.16), channel_id=1, source_target_pairs={{0,17},{1,16},{2,19},{3,18},{16,1},{17,0},{18,3},{19,2},{4,21},{5,... | collective-permute-start | bytes 405512 | tf_op jit(solution)/shard_map/ppermute | solution.py:267
  27.0 4.9 %copy-start.3 = (bf16[768,256]{1,0:T(8,128)(2,1)}, bf16[768,256]{1,0:T(8,128)(2,1)S(1)}, u32[]{:S(2)}) copy-start(bf16[768,256]{1,0:T(8,128)(2,1)S(1)} %collective-permute-done.other_ref) | copy-start | bytes 1179652
  27.0 8.7 %collective-permute-start.7 = (bf16[528,128]{1,0:T(8,128)(2,1)S(1)}, bf16[528,128]{1,0:T(8,128)(2,1)S(1)}, u32[]{:S(2)}, u32[]{:S(2)}) collective-permute-start(bf16[528,128]{1,0:T(8,128)(2,1)S(1)} %get-tuple-element.17), channel_id=1, source_target_pairs={{0,16},{1,17},{2,18},{3,19},{16,0},{17,1},{18,2},{19,3},{4,20},{5,... | collective-permute-start | bytes 405512 | tf_op jit(solution)/shard_map/ppermute | solution.py:267
  28.9 1.9 %copy-start = (f32[1,1,768,1024]{3,2,1,0:T(8,128)S(1)}, f32[1,1,768,1024]{3,2,1,0:T(8,128)}, u32[]{:S(2)}) copy-start(f32[1,1,768,1024]{3,2,1,0:T(8,128)} %param.11) | copy-start | bytes 9437188
  31.8 12.7 %copy-start.1 = (f32[1,1,768,1024]{3,2,1,0:T(8,128)S(1)}, f32[1,1,768,1024]{3,2,1,0:T(8,128)}, u32[]{:S(2)}) copy-start(f32[1,1,768,1024]{3,2,1,0:T(8,128)} %param.11) | copy-start | bytes 9437188
  39.9 18.3 %all-to-all-start = ((f32[8,8,128]{2,1,0:T(8,128)}), f32[8,8,128]{2,1,0:T(8,128)}, u32[]{:S(2)}, u32[]{:S(2)}) async-start(f32[8,8,128]{2,1,0:T(8,128)} %copy-done.21), calls=%async_computation | async-start | bytes 65536 | tf_op jit(solution)/shard_map/all_to_all | solution.py:328
  44.6 1.0 %copy-start.4 = (bf16[768,256]{1,0:T(8,128)(2,1)S(1)}, bf16[768,256]{1,0:T(8,128)(2,1)}, u32[]{:S(2)}) copy-start(bf16[768,256]{1,0:T(8,128)(2,1)} %copy-done.3) | copy-start | bytes 1179652
  45.6 0.9 %copy-start.6 = (bf16[528,128]{1,0:T(8,128)(2,1)S(1)}, bf16[528,128]{1,0:T(8,128)(2,1)}, u32[]{:S(2)}) copy-start(bf16[528,128]{1,0:T(8,128)(2,1)} %copy-done.5) | copy-start | bytes 405508
  46.5 0.9 %copy-start.8 = (bf16[528,128]{1,0:T(8,128)(2,1)S(1)}, bf16[528,128]{1,0:T(8,128)(2,1)}, u32[]{:S(2)}) copy-start(bf16[528,128]{1,0:T(8,128)(2,1)} %copy-done.7) | copy-start | bytes 405508
  47.4 0.9 %copy-start.10 = (bf16[528,128]{1,0:T(8,128)(2,1)S(1)}, bf16[528,128]{1,0:T(8,128)(2,1)}, u32[]{:S(2)}) copy-start(bf16[528,128]{1,0:T(8,128)(2,1)} %copy-done.9) | copy-start | bytes 405508
  48.3 0.9 %copy-start.12 = (bf16[528,128]{1,0:T(8,128)(2,1)S(1)}, bf16[528,128]{1,0:T(8,128)(2,1)}, u32[]{:S(2)}) copy-start(bf16[528,128]{1,0:T(8,128)(2,1)} %copy-done.11) | copy-start | bytes 405508
  50.1 0.9 %copy-start.16 = (bf16[528,128]{1,0:T(8,128)(2,1)S(1)}, bf16[528,128]{1,0:T(8,128)(2,1)}, u32[]{:S(2)}) copy-start(bf16[528,128]{1,0:T(8,128)(2,1)} %copy-done.15) | copy-start | bytes 405508
  51.0 0.9 %copy-start.18 = (bf16[528,128]{1,0:T(8,128)(2,1)S(1)}, bf16[528,128]{1,0:T(8,128)(2,1)}, u32[]{:S(2)}) copy-start(bf16[528,128]{1,0:T(8,128)(2,1)} %copy-done.17) | copy-start | bytes 405508
  52.8 5.4 %copy-start.22 = (s32[1,512,8]{1,2,0:T(8,128)S(1)}, s32[1,512,8]{1,2,0:T(8,128)}, u32[]{:S(2)}) copy-start(s32[1,512,8]{1,2,0:T(8,128)} %param.9) | copy-start | bytes 49156
  (10 other events, 7.0 us)

commit v6 on v5

--- a/solution.py
+++ b/solution.py
@@ -141,94 +141,115 @@
 
 
 def score_kernel(items, group, cap, inner_ref, *rest):
-    chunks, out_ref = dict(zip(items, rest)), rest[-1]
+    chunks = dict(zip(items, rest))
+    score_ref, rows_ref, scales_ref = rest[len(items) :]
     blocks = inner_ref.shape[1] // LANES
     me = ep_index()
     mine = own_half()
+    scales = [jnp.zeros((TILE, LANES), F32)] * 2
     for k in range(group):
         sums = []
         for side in range(2):
+            chunk = chunks[side, k]
+            scales[side] += chunk[blocks * cap :, :].astype(F32)
             start = pl.multiple_of(side * group * cap + (me ^ k) * cap, cap)
             total = jnp.zeros((cap, LANES), F32)
             for block in range(blocks):
-                rows = chunks[side, k][block * cap : (block + 1) * cap, :].astype(F32)
-                total += rows * inner_ref[pl.ds(start, cap), block * LANES : (block + 1) * LANES]
+                columns = slice(block * LANES, (block + 1) * LANES)
+                rows = chunk[block * cap : (block + 1) * cap, :]
+                rows_ref[pl.ds(start, cap), columns] = rows
+                total += rows.astype(F32) * inner_ref[pl.ds(start, cap), columns]
             sums.append(total)
         both = jnp.concatenate(sums, axis=0)
         line = jnp.sum(both.T, axis=0, keepdims=True)
         for side in range(2):
-            out_ref[(mine ^ side) * group + (me ^ k)] = jnp.broadcast_to(line, out_ref.shape[1:])
+            score_ref[(mine ^ side) * group + (me ^ k)] = jnp.broadcast_to(
+                line, score_ref.shape[1:]
+            )
+    for side in range(2):
+        scales_ref[side] = scales[side]
 
 
 def update_kernel(
-    items, group, cap, own_ref, other_ref, master_ref, moment_hbm, second_hbm, *rest
+    own_ref, other_ref, rows, scales_ref, master_hbm, moment_hbm, second_hbm, update_hbm, *rest
 ):
-    chunks = dict(zip(items, rest))
-    update_hbm, rows, scaled, total, update, moment_ref, second_ref, sems = rest[2 * group :]
-    loads = [
-        pltpu.make_async_copy(moment_hbm, moment_ref, sems.at[0]),
-        pltpu.make_async_copy(second_hbm, second_ref, sems.at[1]),
-    ]
-    for load in loads:
-        load.start()
-    slots = group * cap
+    master_ref, moment_ref, second_ref, scaled, total, update, sems = rest
     hid, half = update.shape
-    data_rows = half // LANES * cap
-    me = ep_index()
-    for side in range(2):
-        tile = jnp.zeros((TILE, LANES), F32)
-        for k in range(group):
-            chunk = chunks[side, k]
-            tile += chunk[data_rows : data_rows + TILE, :].astype(F32)
-            start = pl.multiple_of(side * slots + (me ^ k) * cap, cap)
-            for block in range(half // LANES):
-                rows[pl.ds(start, cap), block * LANES : (block + 1) * LANES] = chunk[
-                    block * cap : (block + 1) * cap, :
-                ]
+    slots = own_ref.shape[1]
+    step = total.shape[2]
+    piece = 2 * TILE
+    turns = half // step
+    loads = []
+    for turn in range(turns):
+        columns = slice(turn * step, (turn + 1) * step)
+        loads.append(
+            [
+                pltpu.make_async_copy(src.at[:, columns], dst.at[:, columns], sems.at[turn, at])
+                for at, (src, dst) in enumerate(
+                    (
+                        (master_hbm, master_ref),
+                        (moment_hbm, moment_ref),
+                        (second_hbm, second_ref),
+                    )
+                )
+            ]
+        )
+        for load in loads[-1]:
+            load.start()
+    for side, ref in enumerate((own_ref, other_ref)):
         for part in range(slots // LANES):
             lanes = slice(part * LANES, (part + 1) * LANES)
-            line = tile[part : part + 1, :]
+            line = scales_ref[side, part : part + 1, :]
             at = side * slots + part * LANES
             for top in range(0, hid, LANES):
-                hidden = (own_ref, other_ref)[side][top : top + LANES, lanes]
                 scaled[top : top + LANES, at : at + LANES] = (
-                    hidden.astype(F32) * line
+                    ref[top : top + LANES, lanes].astype(F32) * line
                 ).astype(BF16)
-    step = min(half, 2 * LANES)
-    piece = 32
 
     def multiply(turn):
         total[turn % 2] = jnp.dot(
             scaled[...], rows[:, turn * step : (turn + 1) * step], preferred_element_type=F32
         )
 
-    def adam(turn):
+    def moments(turn, lines):
         columns = slice(turn * step, (turn + 1) * step)
-        for top in range(0, hid, piece):
-            lines = slice(top, top + piece)
-            grad = total[turn % 2, lines, :]
-            first = moment_ref[lines, columns].astype(F32) * (beta_first / first_fix) + grad * (
-                (1.0 - beta_first) / first_fix
-            )
-            square = second_ref[lines, columns].astype(F32) * (beta_second / second_fix) + (
-                grad * grad
-            ) * ((1.0 - beta_second) / second_fix)
-            root = square * lax.rsqrt(square) + adam_eps
-            update[lines, columns] = (
-                first * pl.reciprocal(root, approx=True) + decay_rate * master_ref[lines, columns]
-            )
+        grad = total[turn % 2, lines, :]
+        first = moment_ref[lines, columns].astype(F32) * (beta_first / first_fix) + grad * (
+            (1.0 - beta_first) / first_fix
+        )
+        square = second_ref[lines, columns].astype(F32) * (beta_second / second_fix) + (
+            grad * grad
+        ) * ((1.0 - beta_second) / second_fix)
+        return first, square, lax.rsqrt(square)
+
+    def inverse(first, square, root):
+        return first, pl.reciprocal(square * root + adam_eps, approx=True)
+
+    def finish(turn, lines, first, scale):
+        columns = slice(turn * step, (turn + 1) * step)
+        update[lines, columns] = first * scale + decay_rate * master_ref[lines, columns]
 
     copies = []
     multiply(0)
-    for load in loads:
-        load.wait()
-    for turn in range(half // step):
-        if turn + 1 < half // step:
+    for turn in range(turns):
+        if turn + 1 < turns:
             multiply(turn + 1)
-        adam(turn)
+        for load in loads[turn]:
+            load.wait()
+        pieces = [slice(top, top + piece) for top in range(0, hid, piece)]
+        held = {}
+        for at in range(len(pieces) + 2):
+            if at < len(pieces):
+                held[at, 0] = moments(turn, pieces[at])
+            if 0 <= at - 1 < len(pieces):
+                held[at - 1, 1] = inverse(*held.pop((at - 1, 0)))
+            if at >= 2:
+                finish(turn, pieces[at - 2], *held.pop((at - 2, 1)))
         columns = slice(turn * step, (turn + 1) * step)
         copies.append(
-            pltpu.make_async_copy(update.at[:, columns], update_hbm.at[:, columns], sems.at[2 + turn])
+            pltpu.make_async_copy(
+                update.at[:, columns], update_hbm.at[:, columns], sems.at[turn, 3]
+            )
         )
         copies[-1].start()
     for copy in copies:
@@ -279,8 +300,7 @@
     param = master[0, 0]
     other_hidden = moved(own_hidden, 1, 0)
 
-    order = [(0, 1)] + [(side, k) for k in range(group - 1, 1, -1) for side in range(2)]
-    order += [(1, 1), (1, 0), (0, 0)]
+    order = [(side, k) for side in range(2) for k in range(group)]
     chunk = jax.ShapeDtypeStruct((half // LANES * cap + TILE, LANES), BF16)
     routed = pl.pallas_call(
         functools.partial(route_kernel, order, group, cap),
@@ -316,11 +336,15 @@
         name="inner",
     )(own_hidden, other_hidden, param)
 
-    scores = pl.pallas_call(
+    scores, placed, scales = pl.pallas_call(
         functools.partial(score_kernel, order, group, cap),
-        out_shape=jax.ShapeDtypeStruct((2 * group, 8, LANES), F32),
+        out_shape=[
+            jax.ShapeDtypeStruct((2 * group, 8, LANES), F32),
+            jax.ShapeDtypeStruct((2 * slots, half), BF16),
+            jax.ShapeDtypeStruct((2, TILE, LANES), F32),
+        ],
         in_specs=specs(pltpu.VMEM, 1 + 2 * group),
-        out_specs=specs(pltpu.VMEM, 1)[0],
+        out_specs=specs(pltpu.VMEM, 3),
         compiler_params=params(),
         cost_estimate=cost(4 * slots * half, 12 * slots * half),
         name="score",
@@ -329,18 +353,18 @@
 
     step = min(half, 2 * LANES)
     update = pl.pallas_call(
-        functools.partial(update_kernel, order, group, cap),
+        update_kernel,
         out_shape=jax.ShapeDtypeStruct((hid, half), F32),
-        in_specs=specs(pltpu.VMEM, 3) + specs(pltpu.HBM, 2) + specs(pltpu.VMEM, 2 * group),
+        in_specs=specs(pltpu.VMEM, 4) + specs(pltpu.HBM, 3),
         out_specs=specs(pltpu.HBM, 1)[0],
         scratch_shapes=[
-            pltpu.VMEM((2 * slots, half), BF16),
+            pltpu.VMEM((hid, half), F32),
+            pltpu.VMEM((hid, half), BF16),
+            pltpu.VMEM((hid, half), BF16),
             pltpu.VMEM((hid, 2 * slots), BF16),
             pltpu.VMEM((2, hid, step), F32),
             pltpu.VMEM((hid, half), F32),
-            pltpu.VMEM((hid, half), BF16),
-            pltpu.VMEM((hid, half), BF16),
-            pltpu.SemaphoreType.DMA((2 + half // step,)),
+            pltpu.SemaphoreType.DMA((half // step, 4)),
         ],
         compiler_params=params(),
         cost_estimate=cost(4 * slots * hid * half, 12 * hid * half + 4 * slots * half),
@@ -348,10 +372,12 @@
     )(
         own_hidden,
         other_hidden,
-        param,
-        pltpu.with_memory_space_constraint(moment[0, 0], pltpu.HBM),
-        pltpu.with_memory_space_constraint(second[0, 0], pltpu.HBM),
-        *chunks,
+        placed,
+        scales,
+        *[
+            pltpu.with_memory_space_constraint(array[0, 0], pltpu.HBM)
+            for array in (master, moment, second)
+        ],
     )
     router = pl.pallas_call(
         functools.partial(combine_kernel, group, cap),

time: 61.2 us -> 46.1 us (0.75)
  local copies, waits for them, and re-layouts: 15.3 us -> 1.9 us
  starting transfers between devices: 27.9 us -> 16.6 us
  waiting for transfers between devices: 6.07 us -> 16.2 us
    unnamed x50 -> x6, local copies, waits for them, and re-layouts: 15.3 us -> 1.9 us
    ppermute x8, starting transfers between devices: 23.2 us -> 11.3 us  [moved(): return lax.ppermute(array, ('pair', 'ep'), pairs)]
    ppermute x8, waiting for transfers between devices: 6.07 us -> 14.9 us  [moved(): return lax.ppermute(array, ('pair', 'ep'), pairs)]
    all_to_all x1, waiting for transfers between devices: 0.01 us -> 1.33 us  [local(): lax.all_to_all(scores, ('pair', 'ep'), split_axis=0, concat_axis=0, tiled...]
    pallas_call x1, Pallas kernels: 1.62 us -> 0.86 us  [local(): pl.pallas_call(functools.partial(combine_kernel, group, cap), out_shape=j...]
    pallas_call x1, Pallas kernels: 0.31 us -> 1.04 us  [local(): pl.pallas_call(functools.partial(score_kernel, order, group, cap), out_sh...]
  transfers between devices with their start and end apart: 9 -> 9, of which waited for: 5 -> 4; matrix products, arithmetic and copies ran while one was open for 0% -> 0% of each run, Pallas kernels for 14% -> 19%
where the time goes in v6:
time: 46.1 us; the launch traced here: 45.9 us
  starting transfers between devices  16.6 us (36%)
  waiting for transfers between devices  16.2 us (35%)
  Pallas kernels  10.5 us (23%)
  local copies, waits for them, and re-layouts  1.9 us (4%)
  between operations  0.7 us (2%)
    ppermute x8, waiting for transfers between devices, moved(): return lax.ppermute(array, ('pair', 'ep'), pairs)  14.9 us
    ppermute x8, starting transfers between devices, moved(): return lax.ppermute(array, ('pair', 'ep'), pairs)  11.3 us
    pallas_call x1, Pallas kernels, local(): pl.pallas_call(update_kernel, out_shape=jax.ShapeDtypeStruct((hid, half),...  5.38 us
    all_to_all x1, starting transfers between devices, local(): lax.all_to_all(scores, ('pair', 'ep'), split_axis=0, concat_axis=0, tiled...  5.25 us
    pallas_call x1, Pallas kernels, local(): pl.pallas_call(functools.partial(route_kernel, order, group, cap), out_sh...  2.19 us
    unnamed x6, local copies, waits for them, and re-layouts  1.9 us
    all_to_all x1, waiting for transfers between devices, local(): lax.all_to_all(scores, ('pair', 'ep'), split_axis=0, concat_axis=0, tiled...  1.33 us
    pallas_call x1, Pallas kernels, local(): pl.pallas_call(functools.partial(score_kernel, order, group, cap), out_sh...  1.04 us
  transfers between devices with their start and end apart: 9, of which 4 were waited for; matrix products, arithmetic and copies ran while one was open for 0% of the time, Pallas kernels for 19%

profile of v6, /device:TPU:0, one launch (start us, length us, event | category | flops | bytes accessed | tf_op | source)
XLA Modules:
  0.0 45.9 jit_solution(10659782524250186610)
XLA Ops:
  0.6 3.0 %collective-permute-start = (bf16[768,256]{1,0:T(8,128)(2,1)}, bf16[768,256]{1,0:T(8,128)(2,1)S(1)}, u32[]{:S(2)}, u32[]{:S(2)}) collective-permute-start(bf16[768,256]{1,0:T(8,128)(2,1)} %bitcast.17), channel_id=1, source_target_pairs={{0,16},{1,17},{2,18},{3,19},{16,0},{17,1},{18,2},{19,3},{4,20},{5,... | collective-permute-start | bytes 1179656 | tf_op jit(solution)/shard_map/ppermute | solution.py:288
  3.7 2.2 %route.1 = (f32[16,512]{1,0:T(8,128)S(1)}, bf16[528,128]{1,0:T(8,128)(2,1)S(1)}, bf16[528,128]{1,0:T(8,128)(2,1)S(1)}, bf16[528,128]{1,0:T(8,128)(2,1)S(1)}, bf1...) custom-call(s32[8,512]{1,0:T(8,128)} %bitcast.20, ...), custom_call_target="tpu_custom_call" | custom-call | flops 536870912 | bytes 3145728 | tf_op jit(solution)/shard_map/route/pallas_call | solution.py:305
  5.9 1.6 %collective-permute-start.1 = (bf16[528,128]{1,0:T(8,128)(2,1)S(1)}, bf16[528,128]{1,0:T(8,128)(2,1)S(1)}, u32[]{:S(2)}, u32[]{:S(2)}) collective-permute-start(bf16[528,128]{1,0:T(8,128)(2,1)S(1)} %get-tuple-element.15), channel_id=1, source_target_pairs={{0,1},{1,0},{2,3},{3,2},{16,17},{17,16},{18,19},{19,18},{4,5},{5,4... | collective-permute-start | bytes 405512 | tf_op jit(solution)/shard_map/ppermute | solution.py:288
  7.5 2.6 %collective-permute-start.2 = (bf16[528,128]{1,0:T(8,128)(2,1)S(1)}, bf16[528,128]{1,0:T(8,128)(2,1)S(1)}, u32[]{:S(2)}, u32[]{:S(2)}) collective-permute-start(bf16[528,128]{1,0:T(8,128)(2,1)S(1)} %get-tuple-element.16), channel_id=1, source_target_pairs={{0,2},{1,3},{2,0},{3,1},{16,18},{17,19},{18,16},{19,17},{4,6},{5,7... | collective-permute-start | bytes 405512 | tf_op jit(solution)/shard_map/ppermute | solution.py:288
  10.1 0.2 collective-permute-start.3
  10.3 0.3 collective-permute-start.4
  10.6 1.9 %collective-permute-done.1.rest_1_ = bf16[528,128]{1,0:T(8,128)(2,1)S(1)} collective-permute-done((bf16[528,128]{1,0:T(8,128)(2,1)S(1)}, bf16[528,128]{1,0:T(8,128)(2,1)S(1)}, u32[]{:S(2)}, u32[]{:S(2)}) %collective-permute-start.1) | collective-permute-done | bytes 135200 | tf_op jit(solution)/shard_map/ppermute | solution.py:288
  12.5 0.6 %collective-permute-start.5 = (bf16[528,128]{1,0:T(8,128)(2,1)S(1)}, bf16[528,128]{1,0:T(8,128)(2,1)S(1)}, u32[]{:S(2)}, u32[]{:S(2)}) collective-permute-start(bf16[528,128]{1,0:T(8,128)(2,1)S(1)} %get-tuple-element.19), channel_id=1, source_target_pairs={{0,17},{1,16},{2,19},{3,18},{16,1},{17,0},{18,3},{19,2},{4,21},{5,... | collective-permute-start | bytes 405512 | tf_op jit(solution)/shard_map/ppermute | solution.py:288
  13.1 7.7 %collective-permute-done.2.rest_2_ = bf16[528,128]{1,0:T(8,128)(2,1)S(1)} collective-permute-done((bf16[528,128]{1,0:T(8,128)(2,1)S(1)}, bf16[528,128]{1,0:T(8,128)(2,1)S(1)}, u32[]{:S(2)}, u32[]{:S(2)}) %collective-permute-start.2) | collective-permute-done | bytes 135200 | tf_op jit(solution)/shard_map/ppermute | solution.py:288
  20.8 0.0 collective-permute-start.6
  20.8 0.0 collective-permute-done.other_ref
  20.8 3.0 %collective-permute-start.7 = (bf16[528,128]{1,0:T(8,128)(2,1)S(1)}, bf16[528,128]{1,0:T(8,128)(2,1)S(1)}, u32[]{:S(2)}, u32[]{:S(2)}) collective-permute-start(bf16[528,128]{1,0:T(8,128)(2,1)S(1)} %get-tuple-element.21), channel_id=1, source_target_pairs={{0,19},{1,18},{2,17},{3,16},{16,3},{17,2},{18,1},{19,0},{4,23},{5,... | collective-permute-start | bytes 405512 | tf_op jit(solution)/shard_map/ppermute | solution.py:288
  23.8 1.9 %copy-done = f32[1,1,768,1024]{3,2,1,0:T(8,128)S(1)} copy-done((f32[1,1,768,1024]{3,2,1,0:T(8,128)S(1)}, f32[1,1,768,1024]{3,2,1,0:T(8,128)}, u32[]{:S(2)}) %copy-start) | copy-done | bytes 3145752
  25.7 1.0 %inner.1.inner_ref = f32[512,1024]{1,0:T(8,128)S(1)} custom-call(bf16[768,256]{1,0:T(8,128)(2,1)S(1)} %bitcast.18, bf16[768,256]{1,0:T(8,128)(2,1)S(1)} %collective-permute-done.other_ref, f32[768,1024]{1,0:T(8,128)S(1)} %bitcast.16), custom_call_target="tpu_custom_call" | custom-call | flops 805306368 | bytes 5242880 | tf_op jit(solution)/shard_map/inner/pallas_call | solution.py:329
  26.7 0.0 collective-permute-done.3.rest_3_
  26.7 0.0 collective-permute-done.4.rest_4_
  26.7 0.0 collective-permute-done.5.rest_5_
  26.7 5.3 %collective-permute-done.6.rest_6_ = bf16[528,128]{1,0:T(8,128)(2,1)S(1)} collective-permute-done((bf16[528,128]{1,0:T(8,128)(2,1)S(1)}, bf16[528,128]{1,0:T(8,128)(2,1)S(1)}, u32[]{:S(2)}, u32[]{:S(2)}) %collective-permute-start.6) | collective-permute-done | bytes 135200 | tf_op jit(solution)/shard_map/ppermute | solution.py:288
  32.0 0.0 collective-permute-done.7.rest_7_
  32.0 1.0 %score.1 = (f32[8,8,128]{2,1,0:T(8,128)}, bf16[512,1024]{1,0:T(8,128)(2,1)S(1)}, f32[2,16,128]{2,1,0:T(8,128)S(1)}) custom-call(f32[512,1024]{1,0:T(8,128)S(1)} %inner.1.inner_ref, bf16[528,128]{1,0:T(8,128)(2,1)S(1)} %get-tuple-element.14.rest_0_, bf16[528,128]{1,0:T(8,128)(2,1)S(1)} %collective-permute-done.1.rest_1_, ...), custom_call_target="tpu_custom_call" | custom-call | flops 1048576 | bytes 3145728 | tf_op jit(solution)/shard_map/score/pallas_call | solution.py:339
  33.0 5.2 %all-to-all-start = ((f32[8,8,128]{2,1,0:T(8,128)}), f32[8,8,128]{2,1,0:T(8,128)S(1)}, u32[]{:S(2)}, u32[]{:S(2)}) async-start(f32[8,8,128]{2,1,0:T(8,128)} %get-tuple-element.25), calls=%async_computation | async-start | bytes 65536 | tf_op jit(solution)/shard_map/all_to_all | solution.py:352
  38.3 5.4 %update.1 = f32[768,1024]{1,0:T(8,128)} custom-call(bf16[768,256]{1,0:T(8,128)(2,1)S(1)} %bitcast.19, bf16[768,256]{1,0:T(8,128)(2,1)S(1)} %collective-permute-done.other_ref, bf16[512,1024]{1,0:T(8,128)(2,1)S(1)} %get-tuple-element.22.rows, f32[2,16,128]{2,1,0:T(8,128)S(1)} %get-tuple-element.23.scales_ref, f32[768,1024]{1,0:T(8,128)} %bitcast.15, ...), custom_call_target="tpu_custom_call" | custom-call | flops 805306368 | bytes 10485760 | tf_op jit(solution)/shard_map/update/pallas_call | solution.py:355
  43.7 1.3 %all-to-all-done.score_ref = f32[8,8,128]{2,1,0:T(8,128)S(1)} async-done(((f32[8,8,128]{2,1,0:T(8,128)}), f32[8,8,128]{2,1,0:T(8,128)S(1)}, u32[]{:S(2)}, u32[]{:S(2)}) %all-to-all-start) | async-done | bytes 32800 | tf_op jit(solution)/shard_map/all_to_all | solution.py:352
  45.0 0.9 %combine.1 = f32[8,512]{1,0:T(8,128)} custom-call(s32[8,512]{1,0:T(8,128)S(1)} %bitcast.21, f32[16,512]{1,0:T(8,128)S(1)} %get-tuple-element.24.slots_ref, f32[8,8,128]{2,1,0:T(8,128)S(1)} %all-to-all-done.score_ref), custom_call_target="tpu_custom_call" | custom-call | flops 524288 | bytes 32768 | tf_op jit(solution)/shard_map/combine/pallas_call | solution.py:382
  (5 shorter events, 0.0 us)
Async XLA Ops:
  0.6 23.2 %copy-start.1 = (bf16[1,1,768,256]{3,2,1,0:T(8,128)(2,1)S(1)}, bf16[1,1,768,256]{3,2,1,0:T(8,128)(2,1)}, u32[]{:S(2)}) copy-start(bf16[1,1,768,256]{3,2,1,0:T(8,128)(2,1)} %param.10) | copy-start | bytes 1179652
  0.6 20.1 %collective-permute-start = (bf16[768,256]{1,0:T(8,128)(2,1)}, bf16[768,256]{1,0:T(8,128)(2,1)S(1)}, u32[]{:S(2)}, u32[]{:S(2)}) collective-permute-start(bf16[768,256]{1,0:T(8,128)(2,1)} %bitcast.17), channel_id=1, source_target_pairs={{0,16},{1,17},{2,18},{3,19},{16,0},{17,1},{18,2},{19,3},{4,20},{5,... | collective-permute-start | bytes 1179656 | tf_op jit(solution)/shard_map/ppermute | solution.py:288
  5.9 6.7 %collective-permute-start.1 = (bf16[528,128]{1,0:T(8,128)(2,1)S(1)}, bf16[528,128]{1,0:T(8,128)(2,1)S(1)}, u32[]{:S(2)}, u32[]{:S(2)}) collective-permute-start(bf16[528,128]{1,0:T(8,128)(2,1)S(1)} %get-tuple-element.15), channel_id=1, source_target_pairs={{0,1},{1,0},{2,3},{3,2},{16,17},{17,16},{18,19},{19,18},{4,5},{5,4... | collective-permute-start | bytes 405512 | tf_op jit(solution)/shard_map/ppermute | solution.py:288
  7.5 13.3 %collective-permute-start.2 = (bf16[528,128]{1,0:T(8,128)(2,1)S(1)}, bf16[528,128]{1,0:T(8,128)(2,1)S(1)}, u32[]{:S(2)}, u32[]{:S(2)}) collective-permute-start(bf16[528,128]{1,0:T(8,128)(2,1)S(1)} %get-tuple-element.16), channel_id=1, source_target_pairs={{0,2},{1,3},{2,0},{3,1},{16,18},{17,19},{18,16},{19,17},{4,6},{5,7... | collective-permute-start | bytes 405512 | tf_op jit(solution)/shard_map/ppermute | solution.py:288
  10.1 16.6 %collective-permute-start.3 = (bf16[528,128]{1,0:T(8,128)(2,1)S(1)}, bf16[528,128]{1,0:T(8,128)(2,1)S(1)}, u32[]{:S(2)}, u32[]{:S(2)}) collective-permute-start(bf16[528,128]{1,0:T(8,128)(2,1)S(1)} %get-tuple-element.17), channel_id=1, source_target_pairs={{0,3},{1,2},{2,1},{3,0},{16,19},{17,18},{18,17},{19,16},{4,7},{5,6... | collective-permute-start | bytes 405512 | tf_op jit(solution)/shard_map/ppermute | solution.py:288
  10.3 16.4 %collective-permute-start.4 = (bf16[528,128]{1,0:T(8,128)(2,1)S(1)}, bf16[528,128]{1,0:T(8,128)(2,1)S(1)}, u32[]{:S(2)}, u32[]{:S(2)}) collective-permute-start(bf16[528,128]{1,0:T(8,128)(2,1)S(1)} %get-tuple-element.18), channel_id=1, source_target_pairs={{0,16},{1,17},{2,18},{3,19},{16,0},{17,1},{18,2},{19,3},{4,20},{5,... | collective-permute-start | bytes 405512 | tf_op jit(solution)/shard_map/ppermute | solution.py:288
  12.5 14.2 %collective-permute-start.5 = (bf16[528,128]{1,0:T(8,128)(2,1)S(1)}, bf16[528,128]{1,0:T(8,128)(2,1)S(1)}, u32[]{:S(2)}, u32[]{:S(2)}) collective-permute-start(bf16[528,128]{1,0:T(8,128)(2,1)S(1)} %get-tuple-element.19), channel_id=1, source_target_pairs={{0,17},{1,16},{2,19},{3,18},{16,1},{17,0},{18,3},{19,2},{4,21},{5,... | collective-permute-start | bytes 405512 | tf_op jit(solution)/shard_map/ppermute | solution.py:288
  20.8 11.2 %collective-permute-start.6 = (bf16[528,128]{1,0:T(8,128)(2,1)S(1)}, bf16[528,128]{1,0:T(8,128)(2,1)S(1)}, u32[]{:S(2)}, u32[]{:S(2)}) collective-permute-start(bf16[528,128]{1,0:T(8,128)(2,1)S(1)} %get-tuple-element.20), channel_id=1, source_target_pairs={{0,18},{1,19},{2,16},{3,17},{16,2},{17,3},{18,0},{19,1},{4,22},{5,... | collective-permute-start | bytes 405512 | tf_op jit(solution)/shard_map/ppermute | solution.py:288
  20.8 11.2 %collective-permute-start.7 = (bf16[528,128]{1,0:T(8,128)(2,1)S(1)}, bf16[528,128]{1,0:T(8,128)(2,1)S(1)}, u32[]{:S(2)}, u32[]{:S(2)}) collective-permute-start(bf16[528,128]{1,0:T(8,128)(2,1)S(1)} %get-tuple-element.21), channel_id=1, source_target_pairs={{0,19},{1,18},{2,17},{3,16},{16,3},{17,2},{18,1},{19,0},{4,23},{5,... | collective-permute-start | bytes 405512 | tf_op jit(solution)/shard_map/ppermute | solution.py:288
  23.8 1.9 %copy-start = (f32[1,1,768,1024]{3,2,1,0:T(8,128)S(1)}, f32[1,1,768,1024]{3,2,1,0:T(8,128)}, u32[]{:S(2)}) copy-start(f32[1,1,768,1024]{3,2,1,0:T(8,128)} %param.11) | copy-start | bytes 9437188
  33.0 12.0 %all-to-all-start = ((f32[8,8,128]{2,1,0:T(8,128)}), f32[8,8,128]{2,1,0:T(8,128)S(1)}, u32[]{:S(2)}, u32[]{:S(2)}) async-start(f32[8,8,128]{2,1,0:T(8,128)} %get-tuple-element.25), calls=%async_computation | async-start | bytes 65536 | tf_op jit(solution)/shard_map/all_to_all | solution.py:352
  38.3 6.7 %copy-start.2 = (s32[1,512,8]{1,2,0:T(8,128)S(1)}, s32[1,512,8]{1,2,0:T(8,128)}, u32[]{:S(2)}) copy-start(s32[1,512,8]{1,2,0:T(8,128)} %param.9) | copy-start | bytes 49156

commit v7 on v6

--- a/solution.py
+++ b/solution.py
@@ -145,7 +145,8 @@
     score_ref, rows_ref, scales_ref = rest[len(items) :]
     blocks = inner_ref.shape[1] // LANES
     me = ep_index()
-    mine = own_half()
+    line_of = lax.broadcasted_iota(jnp.int32, score_ref.shape, 0)
+    scores = jnp.zeros(score_ref.shape, F32)
     scales = [jnp.zeros((TILE, LANES), F32)] * 2
     for k in range(group):
         sums = []
@@ -162,58 +163,36 @@
             sums.append(total)
         both = jnp.concatenate(sums, axis=0)
         line = jnp.sum(both.T, axis=0, keepdims=True)
-        for side in range(2):
-            score_ref[(mine ^ side) * group + (me ^ k)] = jnp.broadcast_to(
-                line, score_ref.shape[1:]
-            )
+        scores = jnp.where(line_of == (me ^ k), line, scores)
+    score_ref[...] = scores
     for side in range(2):
         scales_ref[side] = scales[side]
 
 
-def update_kernel(
-    own_ref, other_ref, rows, scales_ref, master_hbm, moment_hbm, second_hbm, update_hbm, *rest
-):
-    master_ref, moment_ref, second_ref, scaled, total, update, sems = rest
-    hid, half = update.shape
+def merge_kernel(cap, own_ref, other_ref, out_ref):
+    out_ref[...] = own_ref[...] + pltpu.roll(other_ref[...], LANES - cap, axis=1)
+
+
+def update_rows(blocks, operands, scaled, total, update, finished):
+    own_ref, other_ref, rows, scales_ref, master_ref, moment_ref, second_ref = operands
     slots = own_ref.shape[1]
-    step = total.shape[2]
-    piece = 2 * TILE
-    turns = half // step
-    loads = []
-    for turn in range(turns):
-        columns = slice(turn * step, (turn + 1) * step)
-        loads.append(
-            [
-                pltpu.make_async_copy(src.at[:, columns], dst.at[:, columns], sems.at[turn, at])
-                for at, (src, dst) in enumerate(
-                    (
-                        (master_hbm, master_ref),
-                        (moment_hbm, moment_ref),
-                        (second_hbm, second_ref),
-                    )
-                )
-            ]
-        )
-        for load in loads[-1]:
-            load.start()
-    for side, ref in enumerate((own_ref, other_ref)):
-        for part in range(slots // LANES):
-            lanes = slice(part * LANES, (part + 1) * LANES)
-            line = scales_ref[side, part : part + 1, :]
-            at = side * slots + part * LANES
-            for top in range(0, hid, LANES):
-                scaled[top : top + LANES, at : at + LANES] = (
-                    ref[top : top + LANES, lanes].astype(F32) * line
+    half = rows.shape[1]
+    step = min(half, 4 * LANES)
+
+    def multiply(at):
+        block = blocks[at]
+        for side, ref in enumerate((own_ref, other_ref)):
+            for part in range(slots // LANES):
+                lanes = slice(part * LANES, (part + 1) * LANES)
+                column = side * slots + part * LANES
+                scaled[at % 2, :, column : column + LANES] = (
+                    ref[block, lanes].astype(F32) * scales_ref[side, part : part + 1, :]
                 ).astype(BF16)
-
-    def multiply(turn):
-        total[turn % 2] = jnp.dot(
-            scaled[...], rows[:, turn * step : (turn + 1) * step], preferred_element_type=F32
-        )
-
-    def moments(turn, lines):
-        columns = slice(turn * step, (turn + 1) * step)
-        grad = total[turn % 2, lines, :]
+        total[at % 2] = jnp.dot(scaled[at % 2], rows[...], preferred_element_type=F32)
+
+    def moments(at, top, columns):
+        lines = slice(blocks[at].start + top, blocks[at].start + top + TILE)
+        grad = total[at % 2, top : top + TILE, columns]
         first = moment_ref[lines, columns].astype(F32) * (beta_first / first_fix) + grad * (
             (1.0 - beta_first) / first_fix
         )
@@ -225,55 +204,75 @@
     def inverse(first, square, root):
         return first, pl.reciprocal(square * root + adam_eps, approx=True)
 
-    def finish(turn, lines, first, scale):
-        columns = slice(turn * step, (turn + 1) * step)
-        update[lines, columns] = first * scale + decay_rate * master_ref[lines, columns]
-
-    copies = []
+    def finish(at, top, columns, first, scale):
+        lines = slice(blocks[at].start + top, blocks[at].start + top + TILE)
+        place = slice(lines.start - blocks[0].start, lines.stop - blocks[0].start)
+        update[place, columns] = first * scale + decay_rate * master_ref[lines, columns]
+
     multiply(0)
-    for turn in range(turns):
-        if turn + 1 < turns:
-            multiply(turn + 1)
-        for load in loads[turn]:
-            load.wait()
-        pieces = [slice(top, top + piece) for top in range(0, hid, piece)]
+    for at, block in enumerate(blocks):
+        if at + 1 < len(blocks):
+            multiply(at + 1)
+        pieces = [
+            (top, slice(column, column + step))
+            for top in range(0, block.stop - block.start, TILE)
+            for column in range(0, half, step)
+        ]
         held = {}
-        for at in range(len(pieces) + 2):
-            if at < len(pieces):
-                held[at, 0] = moments(turn, pieces[at])
-            if 0 <= at - 1 < len(pieces):
-                held[at - 1, 1] = inverse(*held.pop((at - 1, 0)))
-            if at >= 2:
-                finish(turn, pieces[at - 2], *held.pop((at - 2, 1)))
-        columns = slice(turn * step, (turn + 1) * step)
+        for turn in range(len(pieces) + 2):
+            if turn < len(pieces):
+                held[turn, 0] = moments(at, *pieces[turn])
+            if 0 <= turn - 1 < len(pieces):
+                held[turn - 1, 1] = inverse(*held.pop((turn - 1, 0)))
+            if turn >= 2:
+                finish(at, *pieces[turn - 2], *held.pop((turn - 2, 1)))
+        finished(at)
+
+
+def first_update_kernel(blocks, *refs):
+    scaled, total = refs[-2:]
+    update_rows(blocks, refs[:7], scaled, total, refs[7], lambda at: None)
+
+
+def last_update_kernel(blocks, *refs):
+    earlier, _, update_hbm, scaled, total, update, sems = refs[7:]
+    above = earlier.shape[0]
+    copies = [
+        pltpu.make_async_copy(earlier, update_hbm.at[:above, :], sems.at[len(blocks)])
+    ]
+    copies[0].start()
+
+    def finished(at):
+        block = blocks[at]
         copies.append(
             pltpu.make_async_copy(
-                update.at[:, columns], update_hbm.at[:, columns], sems.at[turn, 3]
+                update.at[block.start - above : block.stop - above, :],
+                update_hbm.at[block, :],
+                sems.at[at],
             )
         )
         copies[-1].start()
+
+    update_rows(blocks, refs[:7], scaled, total, update, finished)
     for copy in copies:
         copy.wait()
 
 
-def combine_kernel(group, cap, ids_ref, slots_ref, score_ref, out_ref):
+def combine_kernel(group, cap, ids_ref, slots_ref, *rest):
+    scores, out_ref = rest[:-1], rest[-1]
     tokens = ids_ref.shape[1]
     me = ep_index()
-    mine = own_half()
-    lane = lax.broadcasted_iota(jnp.int32, (1, LANES), 1)
-    lines = []
-    for k in range(group):
-        own = score_ref[mine * group + (me ^ k)][0:1, :]
-        other = score_ref[(1 - mine) * group + (me ^ k)][0:1, :]
-        lines.append(jnp.where(lane < cap, own, other))
+    row = lax.broadcasted_iota(jnp.int32, scores[0].shape, 0)
+    lines = [
+        jnp.sum(jnp.where(row == me, ref[...], 0.0), axis=0, keepdims=True) for ref in scores
+    ]
     lines.append(jnp.zeros((LANES - group, LANES), F32))
     columns = jnp.concatenate(lines, axis=0).T
-    columns = columns[:cap] + columns[cap : 2 * cap]
     place = lax.broadcasted_iota(jnp.int32, (cap, tokens), 0).astype(F32)
     ids = ids_ref[...]
     result = jnp.zeros(ids.shape, F32)
     for k in range(group):
-        at_slot = jnp.where(place == slots_ref[k : k + 1, :], columns[:, k : k + 1], 0.0)
+        at_slot = jnp.where(place == slots_ref[k : k + 1, :], columns[:cap, k : k + 1], 0.0)
         result = jnp.where(ids == (me ^ k), jnp.sum(at_slot, axis=0, keepdims=True), result)
     out_ref[...] = result
 
@@ -339,7 +338,7 @@
     scores, placed, scales = pl.pallas_call(
         functools.partial(score_kernel, order, group, cap),
         out_shape=[
-            jax.ShapeDtypeStruct((2 * group, 8, LANES), F32),
+            jax.ShapeDtypeStruct((group + -group % 8, LANES), F32),
             jax.ShapeDtypeStruct((2 * slots, half), BF16),
             jax.ShapeDtypeStruct((2, TILE, LANES), F32),
         ],
@@ -349,45 +348,56 @@
         cost_estimate=cost(4 * slots * half, 12 * slots * half),
         name="score",
     )(inner, *chunks)
-    returned = lax.all_to_all(scores, ("pair", "ep"), split_axis=0, concat_axis=0, tiled=True)
-
-    step = min(half, 2 * LANES)
+    other_scores = moved(scores, 1, 0)
+    block = min(hid, 2 * LANES)
+    blocks = [slice(top, top + block) for top in range(0, hid, block)]
+    operands = (own_hidden, other_hidden, placed, scales, param, moment[0, 0], second[0, 0])
+    scratch = [
+        pltpu.VMEM((2, block, 2 * slots), BF16),
+        pltpu.VMEM((2, block, half), F32),
+    ]
+    earlier = pl.pallas_call(
+        functools.partial(first_update_kernel, blocks[:1]),
+        out_shape=jax.ShapeDtypeStruct((block, half), F32),
+        in_specs=specs(pltpu.VMEM, 7),
+        out_specs=specs(pltpu.VMEM, 1)[0],
+        scratch_shapes=scratch,
+        compiler_params=params(),
+        cost_estimate=cost(4 * slots * block * half, 12 * block * half),
+        name="first_update",
+    )(*operands)
+    full_scores = pl.pallas_call(
+        functools.partial(merge_kernel, cap),
+        out_shape=jax.ShapeDtypeStruct(scores.shape, F32),
+        in_specs=specs(pltpu.VMEM, 2),
+        out_specs=specs(pltpu.VMEM, 1)[0],
+        compiler_params=params(),
+        name="merge",
+    )(scores, other_scores)
+    returned = [moved(full_scores, 0, k) for k in range(group)]
     update = pl.pallas_call(
-        update_kernel,
+        functools.partial(last_update_kernel, blocks[1:]),
         out_shape=jax.ShapeDtypeStruct((hid, half), F32),
-        in_specs=specs(pltpu.VMEM, 4) + specs(pltpu.HBM, 3),
+        in_specs=specs(pltpu.VMEM, 8) + specs(pl.ANY, 1),
         out_specs=specs(pltpu.HBM, 1)[0],
-        scratch_shapes=[
-            pltpu.VMEM((hid, half), F32),
-            pltpu.VMEM((hid, half), BF16),
-            pltpu.VMEM((hid, half), BF16),
-            pltpu.VMEM((hid, 2 * slots), BF16),
-            pltpu.VMEM((2, hid, step), F32),
-            pltpu.VMEM((hid, half), F32),
-            pltpu.SemaphoreType.DMA((half // step, 4)),
+        scratch_shapes=scratch
+        + [
+            pltpu.VMEM((hid - block, half), F32),
+            pltpu.SemaphoreType.DMA((len(blocks),)),
         ],
         compiler_params=params(),
-        cost_estimate=cost(4 * slots * hid * half, 12 * hid * half + 4 * slots * half),
-        name="update",
-    )(
-        own_hidden,
-        other_hidden,
-        placed,
-        scales,
-        *[
-            pltpu.with_memory_space_constraint(array[0, 0], pltpu.HBM)
-            for array in (master, moment, second)
-        ],
-    )
+        cost_estimate=cost(4 * slots * (hid - block) * half, 12 * hid * half),
+        name="last_update",
+    )(*operands, earlier, full_scores)
     router = pl.pallas_call(
         functools.partial(combine_kernel, group, cap),
         out_shape=jax.ShapeDtypeStruct((top, tokens), F32),
-        in_specs=specs(pltpu.VMEM, 3),
+        in_specs=specs(pltpu.VMEM, 2 + group),
         out_specs=specs(pltpu.VMEM, 1)[0],
         compiler_params=params(),
         cost_estimate=cost(4 * slots * tokens, 8 * top * tokens),
         name="combine",
-    )(ids, slot_of, returned)
+    )(ids, slot_of, *returned)
     return (update[None, None], router.T[None])
 
 

time: 46.1 us -> 44.3 us (0.961)
  Pallas kernels: 10.5 us -> 7.84 us
  starting transfers between devices: 16.6 us -> 17.3 us
    ppermute x8 -> x12, starting transfers between devices: 11.3 us -> 17.3 us  [moved(): return lax.ppermute(array, ('pair', 'ep'), pairs)]
    all_to_all x1 -> x0, starting transfers between devices: 5.25 us -> none  [local(): lax.all_to_all(scores, ('pair', 'ep'), split_axis=0, concat_axis=0, tiled...]
    pallas_call x1 -> x3, Pallas kernels: 5.38 us -> 3.36 us  [the longest x1 2.51 us: local(): pl.pallas_call(functools.partial(last_update_kernel, blocks[1:]), out_sha...]
    ppermute x8 -> x12, waiting for transfers between devices: 14.9 us -> 16.3 us  [moved(): return lax.ppermute(array, ('pair', 'ep'), pairs)]
    all_to_all x1 -> x0, waiting for transfers between devices: 1.33 us -> none  [local(): lax.all_to_all(scores, ('pair', 'ep'), split_axis=0, concat_axis=0, tiled...]
    pallas_call x1, Pallas kernels: 1.04 us -> 0.44 us  [local(): pl.pallas_call(functools.partial(score_kernel, order, group, cap), out_sh...]
    unnamed x6 -> x12, local copies, waits for them, and re-layouts: 1.9 us -> 1.91 us
  transfers between devices with their start and end apart: 9 -> 12, of which waited for: 4 -> 5; matrix products, arithmetic and copies ran while one was open for 0% -> 0% of each run, Pallas kernels for 19% -> 15%
where the time goes in v7:
time: 44.3 us; the launch traced here: 44.1 us
  starting transfers between devices  17.3 us (39%)
  waiting for transfers between devices  16.3 us (37%)
  Pallas kernels  7.84 us (18%)
  local copies, waits for them, and re-layouts  1.91 us (4%)
  between operations  0.73 us (2%)
    ppermute x12, starting transfers between devices, moved(): return lax.ppermute(array, ('pair', 'ep'), pairs)  17.3 us
    ppermute x12, waiting for transfers between devices, moved(): return lax.ppermute(array, ('pair', 'ep'), pairs)  16.3 us
    pallas_call x1, Pallas kernels, local(): pl.pallas_call(functools.partial(last_update_kernel, blocks[1:]), out_sha...  2.51 us
    pallas_call x1, Pallas kernels, local(): pl.pallas_call(functools.partial(route_kernel, order, group, cap), out_sh...  2.19 us
    unnamed x12, local copies, waits for them, and re-layouts  1.91 us
    pallas_call x1, Pallas kernels, local(): pl.pallas_call(inner_kernel, out_shape=jax.ShapeDtypeStruct((2 * slots, h...  1 us
  transfers between devices with their start and end apart: 12, of which 5 were waited for; matrix products, arithmetic and copies ran while one was open for 0% of the time, Pallas kernels for 15%

profile of v7, /device:TPU:0, one launch (start us, length us, event | category | flops | bytes accessed | tf_op | source)
XLA Modules:
  0.0 44.1 jit_solution(3208419484517198920)
XLA Ops:
  0.6 3.0 %collective-permute-start = (bf16[768,256]{1,0:T(8,128)(2,1)}, bf16[768,256]{1,0:T(8,128)(2,1)S(1)}, u32[]{:S(2)}, u32[]{:S(2)}) collective-permute-start(bf16[768,256]{1,0:T(8,128)(2,1)} %bitcast.22), channel_id=1, source_target_pairs={{0,16},{1,17},{2,18},{3,19},{16,0},{17,1},{18,2},{19,3},{4,20},{5,... | collective-permute-start | bytes 1179656 | tf_op jit(solution)/shard_map/ppermute | solution.py:287
  3.7 2.2 %route.1 = (f32[16,512]{1,0:T(8,128)S(1)}, bf16[528,128]{1,0:T(8,128)(2,1)S(1)}, bf16[528,128]{1,0:T(8,128)(2,1)S(1)}, bf16[528,128]{1,0:T(8,128)(2,1)S(1)}, bf1...) custom-call(s32[8,512]{1,0:T(8,128)} %bitcast.26, ...), custom_call_target="tpu_custom_call" | custom-call | flops 536870912 | bytes 3145728 | tf_op jit(solution)/shard_map/route/pallas_call | solution.py:304
  5.9 1.6 %collective-permute-start.1 = (bf16[528,128]{1,0:T(8,128)(2,1)S(1)}, bf16[528,128]{1,0:T(8,128)(2,1)S(1)}, u32[]{:S(2)}, u32[]{:S(2)}) collective-permute-start(bf16[528,128]{1,0:T(8,128)(2,1)S(1)} %get-tuple-element.15), channel_id=1, source_target_pairs={{0,1},{1,0},{2,3},{3,2},{16,17},{17,16},{18,19},{19,18},{4,5},{5,4... | collective-permute-start | bytes 405512 | tf_op jit(solution)/shard_map/ppermute | solution.py:287
  7.5 2.6 %collective-permute-start.2 = (bf16[528,128]{1,0:T(8,128)(2,1)S(1)}, bf16[528,128]{1,0:T(8,128)(2,1)S(1)}, u32[]{:S(2)}, u32[]{:S(2)}) collective-permute-start(bf16[528,128]{1,0:T(8,128)(2,1)S(1)} %get-tuple-element.16), channel_id=1, source_target_pairs={{0,2},{1,3},{2,0},{3,1},{16,18},{17,19},{18,16},{19,17},{4,6},{5,7... | collective-permute-start | bytes 405512 | tf_op jit(solution)/shard_map/ppermute | solution.py:287
  10.1 0.2 collective-permute-start.3
  10.3 0.3 collective-permute-start.4
  10.6 1.9 %collective-permute-done.1.rest_1_ = bf16[528,128]{1,0:T(8,128)(2,1)S(1)} collective-permute-done((bf16[528,128]{1,0:T(8,128)(2,1)S(1)}, bf16[528,128]{1,0:T(8,128)(2,1)S(1)}, u32[]{:S(2)}, u32[]{:S(2)}) %collective-permute-start.1) | collective-permute-done | bytes 135200 | tf_op jit(solution)/shard_map/ppermute | solution.py:287
  12.5 0.6 %collective-permute-start.5 = (bf16[528,128]{1,0:T(8,128)(2,1)S(1)}, bf16[528,128]{1,0:T(8,128)(2,1)S(1)}, u32[]{:S(2)}, u32[]{:S(2)}) collective-permute-start(bf16[528,128]{1,0:T(8,128)(2,1)S(1)} %get-tuple-element.19), channel_id=1, source_target_pairs={{0,17},{1,16},{2,19},{3,18},{16,1},{17,0},{18,3},{19,2},{4,21},{5,... | collective-permute-start | bytes 405512 | tf_op jit(solution)/shard_map/ppermute | solution.py:287
  13.1 7.7 %collective-permute-done.2.rest_2_ = bf16[528,128]{1,0:T(8,128)(2,1)S(1)} collective-permute-done((bf16[528,128]{1,0:T(8,128)(2,1)S(1)}, bf16[528,128]{1,0:T(8,128)(2,1)S(1)}, u32[]{:S(2)}, u32[]{:S(2)}) %collective-permute-start.2) | collective-permute-done | bytes 135200 | tf_op jit(solution)/shard_map/ppermute | solution.py:287
  20.8 3.0 %collective-permute-start.7 = (bf16[528,128]{1,0:T(8,128)(2,1)S(1)}, bf16[528,128]{1,0:T(8,128)(2,1)S(1)}, u32[]{:S(2)}, u32[]{:S(2)}) collective-permute-start(bf16[528,128]{1,0:T(8,128)(2,1)S(1)} %get-tuple-element.21), channel_id=1, source_target_pairs={{0,19},{1,18},{2,17},{3,16},{16,3},{17,2},{18,1},{19,0},{4,23},{5,... | collective-permute-start | bytes 405512 | tf_op jit(solution)/shard_map/ppermute | solution.py:287
  23.8 1.9 %copy-done = f32[1,1,768,1024]{3,2,1,0:T(8,128)S(1)} copy-done((f32[1,1,768,1024]{3,2,1,0:T(8,128)S(1)}, f32[1,1,768,1024]{3,2,1,0:T(8,128)}, u32[]{:S(2)}) %copy-start) | copy-done | bytes 3145752
  25.7 1.0 %inner.1.inner_ref = f32[512,1024]{1,0:T(8,128)S(1)} custom-call(bf16[768,256]{1,0:T(8,128)(2,1)S(1)} %bitcast.23, bf16[768,256]{1,0:T(8,128)(2,1)S(1)} %collective-permute-done.other_ref.refs_1_, f32[768,1024]{1,0:T(8,128)S(1)} %bitcast.15), custom_call_target="tpu_custom_call" | custom-call | flops 805306368 | bytes 5242880 | tf_op jit(solution)/shard_map/inner/pallas_call | solution.py:328
  26.7 5.3 %collective-permute-done.6.rest_6_ = bf16[528,128]{1,0:T(8,128)(2,1)S(1)} collective-permute-done((bf16[528,128]{1,0:T(8,128)(2,1)S(1)}, bf16[528,128]{1,0:T(8,128)(2,1)S(1)}, u32[]{:S(2)}, u32[]{:S(2)}) %collective-permute-start.6) | collective-permute-done | bytes 135200 | tf_op jit(solution)/shard_map/ppermute | solution.py:287
  32.0 0.4 %score.1 = (f32[8,128]{1,0:T(8,128)S(1)}, bf16[512,1024]{1,0:T(8,128)(2,1)S(1)}, f32[2,16,128]{2,1,0:T(8,128)S(1)}) custom-call(f32[512,1024]{1,0:T(8,128)S(1)} %inner.1.inner_ref, bf16[528,128]{1,0:T(8,128)(2,1)S(1)} %get-tuple-element.14.rest_0_, bf16[528,128]{1,0:T(8,128)(2,1)S(1)} %collective-permute-done.1.rest_1_, ...), custom_call_target="tpu_custom_call" | custom-call | flops 1048576 | bytes 3145728 | tf_op jit(solution)/shard_map/score/pallas_call | solution.py:338
  32.4 1.6 %collective-permute-start.8 = (f32[8,128]{1,0:T(8,128)S(1)}, f32[8,128]{1,0:T(8,128)S(1)}, u32[]{:S(2)}, u32[]{:S(2)}) collective-permute-start(f32[8,128]{1,0:T(8,128)S(1)} %get-tuple-element.24.own_ref), channel_id=1, source_target_pairs={{0,16},{1,17},{2,18},{3,19},{16,0},{17,1},{18,2},{19,3},{4,20},{5,... | collective-permute-start | bytes 12296 | tf_op jit(solution)/shard_map/ppermute | solution.py:287
  34.0 0.8 %first_update.1.refs_7_ = f32[256,1024]{1,0:T(8,128)S(1)} custom-call(bf16[768,256]{1,0:T(8,128)(2,1)S(1)} %bitcast.24, bf16[768,256]{1,0:T(8,128)(2,1)S(1)} %collective-permute-done.other_ref.refs_1_, bf16[512,1024]{1,0:T(8,128)(2,1)S(1)} %get-tuple-element.22.refs_2_, f32[2,16,128]{2,1,0:T(8,128)S(1)} %get-tuple-element.23.refs_3_, ...), custom_call_target="tpu_custom_call" | custom-call | flops 268435456 | bytes 3145728 | tf_op jit(solution)/shard_map/first_update/pallas_call | solution.py:359
  34.8 1.3 %collective-permute-done.8.other_ref = f32[8,128]{1,0:T(8,128)S(1)} collective-permute-done((f32[8,128]{1,0:T(8,128)S(1)}, f32[8,128]{1,0:T(8,128)S(1)}, u32[]{:S(2)}, u32[]{:S(2)}) %collective-permute-start.8) | collective-permute-done | bytes 4128 | tf_op jit(solution)/shard_map/ppermute | solution.py:287
  36.1 0.1 merge.1.refs_8_.rest_0_
  36.2 2.4 %collective-permute-start.11 = (f32[8,128]{1,0:T(8,128)S(1)}, f32[8,128]{1,0:T(8,128)S(1)}, u32[]{:S(2)}, u32[]{:S(2)}) collective-permute-start(f32[8,128]{1,0:T(8,128)S(1)} %merge.1.refs_8_.rest_0_), channel_id=1, source_target_pairs={{0,3},{1,2},{2,1},{3,0},{16,19},{17,18},{18,17},{19,16},{4,7},{5,6... | collective-permute-start | bytes 12296 | tf_op jit(solution)/shard_map/ppermute | solution.py:287
  38.6 1.1 %collective-permute-start.10 = (f32[8,128]{1,0:T(8,128)S(1)}, f32[8,128]{1,0:T(8,128)S(1)}, u32[]{:S(2)}, u32[]{:S(2)}) collective-permute-start(f32[8,128]{1,0:T(8,128)S(1)} %merge.1.refs_8_.rest_0_), channel_id=1, source_target_pairs={{0,2},{1,3},{2,0},{3,1},{16,18},{17,19},{18,16},{19,17},{4,6},{5,7... | collective-permute-start | bytes 12296 | tf_op jit(solution)/shard_map/ppermute | solution.py:287
  39.7 0.9 %collective-permute-start.9 = (f32[8,128]{1,0:T(8,128)S(1)}, f32[8,128]{1,0:T(8,128)S(1)}, u32[]{:S(2)}, u32[]{:S(2)}) collective-permute-start(f32[8,128]{1,0:T(8,128)S(1)} %merge.1.refs_8_.rest_0_), channel_id=1, source_target_pairs={{0,1},{1,0},{2,3},{3,2},{16,17},{17,16},{18,19},{19,18},{4,5},{5,4... | collective-permute-start | bytes 12296 | tf_op jit(solution)/shard_map/ppermute | solution.py:287
  40.6 2.5 %last_update.1 = f32[768,1024]{1,0:T(8,128)} custom-call(bf16[768,256]{1,0:T(8,128)(2,1)S(1)} %bitcast.25, bf16[768,256]{1,0:T(8,128)(2,1)S(1)} %collective-permute-done.other_ref.refs_1_, bf16[512,1024]{1,0:T(8,128)(2,1)S(1)} %get-tuple-element.22.refs_2_, f32[2,16,128]{2,1,0:T(8,128)S(1)} %get-tuple-element.23.refs_3_, f32[768,1024]{1,0:T(8,128)S(1)} %bitcast.17, ...), custom_call_target="tpu_custom_call" | custom-call | flops 536870912 | bytes 9437184 | tf_op jit(solution)/shard_map/last_update/pallas_call | solution.py:378
  43.1 0.1 collective-permute-done.9.rest_1_
  43.3 0.8 %combine.1 = f32[8,512]{1,0:T(8,128)} custom-call(s32[8,512]{1,0:T(8,128)S(1)} %bitcast.27, f32[16,512]{1,0:T(8,128)S(1)} %get-tuple-element.25.slots_ref, f32[8,128]{1,0:T(8,128)S(1)} %merge.1.refs_8_.rest_0_, f32[8,128]{1,0:T(8,128)S(1)} %collective-permute-done.9.rest_1_, f32[8,128]{1,0:T(8,128)S(1)} %collective-permute-done.10.rest_2_, ...), custom_call_target="tpu_custom_call" | custom-call | flops 524288 | bytes 32768 | tf_op jit(solution)/shard_map/combine/pallas_call | solution.py:392
  (19 shorter events, 0.0 us)
Async XLA Ops:
  0.6 23.2 %copy-start.4 = (bf16[1,1,768,256]{3,2,1,0:T(8,128)(2,1)S(1)}, bf16[1,1,768,256]{3,2,1,0:T(8,128)(2,1)}, u32[]{:S(2)}) copy-start(bf16[1,1,768,256]{3,2,1,0:T(8,128)(2,1)} %param.10) | copy-start | bytes 1179652
  0.6 20.1 %collective-permute-start = (bf16[768,256]{1,0:T(8,128)(2,1)}, bf16[768,256]{1,0:T(8,128)(2,1)S(1)}, u32[]{:S(2)}, u32[]{:S(2)}) collective-permute-start(bf16[768,256]{1,0:T(8,128)(2,1)} %bitcast.22), channel_id=1, source_target_pairs={{0,16},{1,17},{2,18},{3,19},{16,0},{17,1},{18,2},{19,3},{4,20},{5,... | collective-permute-start | bytes 1179656 | tf_op jit(solution)/shard_map/ppermute | solution.py:287
  5.9 6.7 %collective-permute-start.1 = (bf16[528,128]{1,0:T(8,128)(2,1)S(1)}, bf16[528,128]{1,0:T(8,128)(2,1)S(1)}, u32[]{:S(2)}, u32[]{:S(2)}) collective-permute-start(bf16[528,128]{1,0:T(8,128)(2,1)S(1)} %get-tuple-element.15), channel_id=1, source_target_pairs={{0,1},{1,0},{2,3},{3,2},{16,17},{17,16},{18,19},{19,18},{4,5},{5,4... | collective-permute-start | bytes 405512 | tf_op jit(solution)/shard_map/ppermute | solution.py:287
  7.5 13.3 %collective-permute-start.2 = (bf16[528,128]{1,0:T(8,128)(2,1)S(1)}, bf16[528,128]{1,0:T(8,128)(2,1)S(1)}, u32[]{:S(2)}, u32[]{:S(2)}) collective-permute-start(bf16[528,128]{1,0:T(8,128)(2,1)S(1)} %get-tuple-element.16), channel_id=1, source_target_pairs={{0,2},{1,3},{2,0},{3,1},{16,18},{17,19},{18,16},{19,17},{4,6},{5,7... | collective-permute-start | bytes 405512 | tf_op jit(solution)/shard_map/ppermute | solution.py:287
  10.1 16.6 %collective-permute-start.3 = (bf16[528,128]{1,0:T(8,128)(2,1)S(1)}, bf16[528,128]{1,0:T(8,128)(2,1)S(1)}, u32[]{:S(2)}, u32[]{:S(2)}) collective-permute-start(bf16[528,128]{1,0:T(8,128)(2,1)S(1)} %get-tuple-element.17), channel_id=1, source_target_pairs={{0,3},{1,2},{2,1},{3,0},{16,19},{17,18},{18,17},{19,16},{4,7},{5,6... | collective-permute-start | bytes 405512 | tf_op jit(solution)/shard_map/ppermute | solution.py:287
  10.3 16.4 %collective-permute-start.4 = (bf16[528,128]{1,0:T(8,128)(2,1)S(1)}, bf16[528,128]{1,0:T(8,128)(2,1)S(1)}, u32[]{:S(2)}, u32[]{:S(2)}) collective-permute-start(bf16[528,128]{1,0:T(8,128)(2,1)S(1)} %get-tuple-element.18), channel_id=1, source_target_pairs={{0,16},{1,17},{2,18},{3,19},{16,0},{17,1},{18,2},{19,3},{4,20},{5,... | collective-permute-start | bytes 405512 | tf_op jit(solution)/shard_map/ppermute | solution.py:287
  12.5 14.2 %collective-permute-start.5 = (bf16[528,128]{1,0:T(8,128)(2,1)S(1)}, bf16[528,128]{1,0:T(8,128)(2,1)S(1)}, u32[]{:S(2)}, u32[]{:S(2)}) collective-permute-start(bf16[528,128]{1,0:T(8,128)(2,1)S(1)} %get-tuple-element.19), channel_id=1, source_target_pairs={{0,17},{1,16},{2,19},{3,18},{16,1},{17,0},{18,3},{19,2},{4,21},{5,... | collective-permute-start | bytes 405512 | tf_op jit(solution)/shard_map/ppermute | solution.py:287
  20.8 11.2 %collective-permute-start.6 = (bf16[528,128]{1,0:T(8,128)(2,1)S(1)}, bf16[528,128]{1,0:T(8,128)(2,1)S(1)}, u32[]{:S(2)}, u32[]{:S(2)}) collective-permute-start(bf16[528,128]{1,0:T(8,128)(2,1)S(1)} %get-tuple-element.20), channel_id=1, source_target_pairs={{0,18},{1,19},{2,16},{3,17},{16,2},{17,3},{18,0},{19,1},{4,22},{5,... | collective-permute-start | bytes 405512 | tf_op jit(solution)/shard_map/ppermute | solution.py:287
  20.8 11.2 %collective-permute-start.7 = (bf16[528,128]{1,0:T(8,128)(2,1)S(1)}, bf16[528,128]{1,0:T(8,128)(2,1)S(1)}, u32[]{:S(2)}, u32[]{:S(2)}) collective-permute-start(bf16[528,128]{1,0:T(8,128)(2,1)S(1)} %get-tuple-element.21), channel_id=1, source_target_pairs={{0,19},{1,18},{2,17},{3,16},{16,3},{17,2},{18,1},{19,0},{4,23},{5,... | collective-permute-start | bytes 405512 | tf_op jit(solution)/shard_map/ppermute | solution.py:287
  23.8 1.9 %copy-start = (f32[1,1,768,1024]{3,2,1,0:T(8,128)S(1)}, f32[1,1,768,1024]{3,2,1,0:T(8,128)}, u32[]{:S(2)}) copy-start(f32[1,1,768,1024]{3,2,1,0:T(8,128)} %param.11) | copy-start | bytes 9437188
  25.7 8.4 %copy-start.2 = (bf16[1,1,768,1024]{3,2,1,0:T(8,128)(2,1)S(1)}, bf16[1,1,768,1024]{3,2,1,0:T(8,128)(2,1)}, u32[]{:S(2)}) copy-start(bf16[1,1,768,1024]{3,2,1,0:T(8,128)(2,1)} %param.12) | copy-start | bytes 4718596
  25.7 8.4 %copy-start.3 = (bf16[1,1,768,1024]{3,2,1,0:T(8,128)(2,1)S(1)}, bf16[1,1,768,1024]{3,2,1,0:T(8,128)(2,1)}, u32[]{:S(2)}) copy-start(bf16[1,1,768,1024]{3,2,1,0:T(8,128)(2,1)} %param.13) | copy-start | bytes 4718596
  26.7 7.3 %copy-start.1 = (f32[1,1,768,1024]{3,2,1,0:T(8,128)S(1)}, f32[1,1,768,1024]{3,2,1,0:T(8,128)}, u32[]{:S(2)}) copy-start(f32[1,1,768,1024]{3,2,1,0:T(8,128)} %param.11) | copy-start | bytes 9437188
  32.4 3.7 %collective-permute-start.8 = (f32[8,128]{1,0:T(8,128)S(1)}, f32[8,128]{1,0:T(8,128)S(1)}, u32[]{:S(2)}, u32[]{:S(2)}) collective-permute-start(f32[8,128]{1,0:T(8,128)S(1)} %get-tuple-element.24.own_ref), channel_id=1, source_target_pairs={{0,16},{1,17},{2,18},{3,19},{16,0},{17,1},{18,2},{19,3},{4,20},{5,... | collective-permute-start | bytes 12296 | tf_op jit(solution)/shard_map/ppermute | solution.py:287
  36.2 7.1 %copy-start.5 = (s32[1,512,8]{1,2,0:T(8,128)S(1)}, s32[1,512,8]{1,2,0:T(8,128)}, u32[]{:S(2)}) copy-start(s32[1,512,8]{1,2,0:T(8,128)} %param.9) | copy-start | bytes 49156
  36.2 6.9 %collective-permute-start.11 = (f32[8,128]{1,0:T(8,128)S(1)}, f32[8,128]{1,0:T(8,128)S(1)}, u32[]{:S(2)}, u32[]{:S(2)}) collective-permute-start(f32[8,128]{1,0:T(8,128)S(1)} %merge.1.refs_8_.rest_0_), channel_id=1, source_target_pairs={{0,3},{1,2},{2,1},{3,0},{16,19},{17,18},{18,17},{19,16},{4,7},{5,6... | collective-permute-start | bytes 12296 | tf_op jit(solution)/shard_map/ppermute | solution.py:287
  38.6 4.5 %collective-permute-start.10 = (f32[8,128]{1,0:T(8,128)S(1)}, f32[8,128]{1,0:T(8,128)S(1)}, u32[]{:S(2)}, u32[]{:S(2)}) collective-permute-start(f32[8,128]{1,0:T(8,128)S(1)} %merge.1.refs_8_.rest_0_), channel_id=1, source_target_pairs={{0,2},{1,3},{2,0},{3,1},{16,18},{17,19},{18,16},{19,17},{4,6},{5,7... | collective-permute-start | bytes 12296 | tf_op jit(solution)/shard_map/ppermute | solution.py:287
  39.7 3.6 %collective-permute-start.9 = (f32[8,128]{1,0:T(8,128)S(1)}, f32[8,128]{1,0:T(8,128)S(1)}, u32[]{:S(2)}, u32[]{:S(2)}) collective-permute-start(f32[8,128]{1,0:T(8,128)S(1)} %merge.1.refs_8_.rest_0_), channel_id=1, source_target_pairs={{0,1},{1,0},{2,3},{3,2},{16,17},{17,16},{18,19},{19,18},{4,5},{5,4... | collective-permute-start | bytes 12296 | tf_op jit(solution)/shard_map/ppermute | solution.py:287

commit v8 on v7

--- a/solution.py
+++ b/solution.py
@@ -131,46 +131,75 @@
     fill_chunks(group, cap, pick, held, copies, tiles, chunks)
 
 
-def inner_kernel(own_ref, other_ref, master_ref, inner_ref):
-    weights = master_ref[...].astype(BF16)
+def inner_kernel(own_ref, other_ref, master_hbm, inner_ref, master_ref, sems):
+    half = master_ref.shape[1]
+    step = min(half, 4 * LANES)
+    parts = [slice(column, column + step) for column in range(0, half, step)]
+    loads = [
+        pltpu.make_async_copy(master_hbm.at[:, part], master_ref.at[:, part], sems.at[at])
+        for at, part in enumerate(parts)
+    ]
+    for load in loads:
+        load.start()
     slots = own_ref.shape[1]
-    for at, ref in ((0, own_ref), (slots, other_ref)):
-        inner_ref[at : at + slots, :] = lax.dot_general(
-            ref[...], weights, (((0,), (0,)), ((), ())), preferred_element_type=F32
-        )
-
-
-def score_kernel(items, group, cap, inner_ref, *rest):
-    chunks = dict(zip(items, rest))
-    score_ref, rows_ref, scales_ref = rest[len(items) :]
+    for load, part in zip(loads, parts):
+        load.wait()
+        weights = master_ref[:, part].astype(BF16)
+        for at, ref in ((0, own_ref), (slots, other_ref)):
+            inner_ref[at : at + slots, part] = lax.dot_general(
+                ref[...], weights, (((0,), (0,)), ((), ())), preferred_element_type=F32
+            )
+
+
+def score_chunks(steps, group, cap, chunks, inner_ref, score_ref):
     blocks = inner_ref.shape[1] // LANES
     me = ep_index()
     line_of = lax.broadcasted_iota(jnp.int32, score_ref.shape, 0)
     scores = jnp.zeros(score_ref.shape, F32)
-    scales = [jnp.zeros((TILE, LANES), F32)] * 2
-    for k in range(group):
+    for k in steps:
         sums = []
         for side in range(2):
-            chunk = chunks[side, k]
-            scales[side] += chunk[blocks * cap :, :].astype(F32)
             start = pl.multiple_of(side * group * cap + (me ^ k) * cap, cap)
             total = jnp.zeros((cap, LANES), F32)
             for block in range(blocks):
-                columns = slice(block * LANES, (block + 1) * LANES)
-                rows = chunk[block * cap : (block + 1) * cap, :]
-                rows_ref[pl.ds(start, cap), columns] = rows
-                total += rows.astype(F32) * inner_ref[pl.ds(start, cap), columns]
+                rows = chunks[side, k][block * cap : (block + 1) * cap, :].astype(F32)
+                total += rows * inner_ref[pl.ds(start, cap), block * LANES : (block + 1) * LANES]
             sums.append(total)
         both = jnp.concatenate(sums, axis=0)
         line = jnp.sum(both.T, axis=0, keepdims=True)
         scores = jnp.where(line_of == (me ^ k), line, scores)
     score_ref[...] = scores
-    for side in range(2):
-        scales_ref[side] = scales[side]
-
-
-def merge_kernel(cap, own_ref, other_ref, out_ref):
-    out_ref[...] = own_ref[...] + pltpu.roll(other_ref[...], LANES - cap, axis=1)
+
+
+def place_chunks(items, group, cap, chunks, rows_ref):
+    blocks = rows_ref.shape[1] // LANES
+    me = ep_index()
+    scales = [jnp.zeros((TILE, LANES), F32)] * 2
+    for side, k in items:
+        chunk = chunks[side, k]
+        start = pl.multiple_of(side * group * cap + (me ^ k) * cap, cap)
+        for block in range(blocks):
+            rows_ref[pl.ds(start, cap), block * LANES : (block + 1) * LANES] = chunk[
+                block * cap : (block + 1) * cap, :
+            ]
+        scales[side] += chunk[blocks * cap :, :].astype(F32)
+    return scales
+
+
+def score_kernel(items, steps, group, cap, inner_ref, *rest):
+    score_ref = rest[-1]
+    score_chunks(steps, group, cap, dict(zip(items, rest)), inner_ref, score_ref)
+
+
+def merge_kernel(group, local_ref, *rest):
+    out_ref = rest[-1]
+    row = lax.broadcasted_iota(jnp.int32, out_ref.shape, 0)
+    me = ep_index()
+    table = jnp.zeros(out_ref.shape, F32)
+    for k, ref in enumerate((local_ref,) + rest[:-1]):
+        line = jnp.sum(jnp.where(row == me, ref[...], 0.0), axis=0, keepdims=True)
+        table = jnp.where(row == k, line, table)
+    out_ref[...] = table
 
 
 def update_rows(blocks, operands, scaled, total, update, finished):
@@ -229,9 +258,14 @@
         finished(at)
 
 
-def first_update_kernel(blocks, *refs):
-    scaled, total = refs[-2:]
-    update_rows(blocks, refs[:7], scaled, total, refs[7], lambda at: None)
+def first_update_kernel(blocks, items, group, cap, *refs):
+    chunks, operands = dict(zip(items, refs)), refs[len(items) : len(items) + 5]
+    update, rows, scales_ref, scaled, total = refs[len(items) + 5 :]
+    scales = place_chunks(items, group, cap, chunks, rows)
+    for side in range(2):
+        scales_ref[side] = scales[side]
+    operands = operands[:2] + (rows, scales_ref) + operands[2:]
+    update_rows(blocks, operands, scaled, total, update, lambda at: None)
 
 
 def last_update_kernel(blocks, *refs):
@@ -258,21 +292,19 @@
         copy.wait()
 
 
-def combine_kernel(group, cap, ids_ref, slots_ref, *rest):
-    scores, out_ref = rest[:-1], rest[-1]
+def combine_kernel(group, cap, ids_ref, slots_ref, own_ref, other_ref, out_ref):
     tokens = ids_ref.shape[1]
     me = ep_index()
-    row = lax.broadcasted_iota(jnp.int32, scores[0].shape, 0)
-    lines = [
-        jnp.sum(jnp.where(row == me, ref[...], 0.0), axis=0, keepdims=True) for ref in scores
-    ]
-    lines.append(jnp.zeros((LANES - group, LANES), F32))
-    columns = jnp.concatenate(lines, axis=0).T
+    lane = lax.broadcasted_iota(jnp.int32, own_ref.shape, 1)
+    lines = jnp.where(lane < cap, own_ref[...], other_ref[...])
+    rest = jnp.zeros((LANES - lines.shape[0], LANES), F32)
+    columns = jnp.concatenate([lines, rest], axis=0).T
+    columns = columns[:cap] + columns[cap : 2 * cap]
     place = lax.broadcasted_iota(jnp.int32, (cap, tokens), 0).astype(F32)
     ids = ids_ref[...]
     result = jnp.zeros(ids.shape, F32)
     for k in range(group):
-        at_slot = jnp.where(place == slots_ref[k : k + 1, :], columns[:cap, k : k + 1], 0.0)
+        at_slot = jnp.where(place == slots_ref[k : k + 1, :], columns[:, k : k + 1], 0.0)
         result = jnp.where(ids == (me ^ k), jnp.sum(at_slot, axis=0, keepdims=True), result)
     out_ref[...] = result
 
@@ -299,7 +331,13 @@
     param = master[0, 0]
     other_hidden = moved(own_hidden, 1, 0)
 
-    order = [(side, k) for side in range(2) for k in range(group)]
+    far = group // 2
+    early = [k for k in range(group) if k != far]
+    wide = [k for k in reversed(early) if k > 1]
+    order = [(0, 1)] + [(0, k) for k in wide] + [(1, 0)] + [(1, k) for k in wide] + [(1, 1)]
+    first_items = [(0, 0)] + order
+    last_items = [(0, far), (1, far)]
+    order = first_items + last_items
     chunk = jax.ShapeDtypeStruct((half // LANES * cap + TILE, LANES), BF16)
     routed = pl.pallas_call(
         functools.partial(route_kernel, order, group, cap),
@@ -323,81 +361,90 @@
     )
     slot_of = routed[0]
     arrived = {item: moved(sent, *item) for item, sent in zip(order, routed[1:])}
-    chunks = [arrived[item] for item in order]
-
     inner = pl.pallas_call(
         inner_kernel,
         out_shape=jax.ShapeDtypeStruct((2 * slots, half), F32),
-        in_specs=specs(pltpu.VMEM, 3),
+        in_specs=specs(pltpu.VMEM, 2) + specs(pltpu.HBM, 1),
         out_specs=specs(pltpu.VMEM, 1)[0],
+        scratch_shapes=[
+            pltpu.VMEM((hid, half), F32),
+            pltpu.SemaphoreType.DMA((half // min(half, 4 * LANES),)),
+        ],
         compiler_params=params(),
         cost_estimate=cost(4 * slots * hid * half, 4 * hid * half + 8 * slots * half),
         name="inner",
-    )(own_hidden, other_hidden, param)
-
-    scores, placed, scales = pl.pallas_call(
-        functools.partial(score_kernel, order, group, cap),
-        out_shape=[
-            jax.ShapeDtypeStruct((group + -group % 8, LANES), F32),
-            jax.ShapeDtypeStruct((2 * slots, half), BF16),
-            jax.ShapeDtypeStruct((2, TILE, LANES), F32),
-        ],
-        in_specs=specs(pltpu.VMEM, 1 + 2 * group),
-        out_specs=specs(pltpu.VMEM, 3),
-        compiler_params=params(),
-        cost_estimate=cost(4 * slots * half, 12 * slots * half),
-        name="score",
-    )(inner, *chunks)
-    other_scores = moved(scores, 1, 0)
+    )(own_hidden, other_hidden, pltpu.with_memory_space_constraint(param, pltpu.HBM))
+
+    tile = jax.ShapeDtypeStruct((group + -group % 8, LANES), F32)
+    returned = {}
+    for items, steps in ((first_items, early), (last_items, [far])):
+        done = list(returned.values())
+        scores = pl.pallas_call(
+            functools.partial(score_kernel, items, steps, group, cap),
+            out_shape=tile,
+            in_specs=specs(pltpu.VMEM, 1 + len(items)) + specs(pl.ANY, len(done)),
+            out_specs=specs(pltpu.VMEM, 1)[0],
+            compiler_params=params(),
+            cost_estimate=cost(2 * len(items) * cap * half, 6 * len(items) * cap * half),
+            name="score",
+        )(inner, *[arrived[item] for item in items], *done)
+        for k in steps:
+            returned[k] = moved(scores, 0, k)
+
     block = min(hid, 2 * LANES)
     blocks = [slice(top, top + block) for top in range(0, hid, block)]
-    operands = (own_hidden, other_hidden, placed, scales, param, moment[0, 0], second[0, 0])
+    above = blocks[-1].start
+    inputs = (param, moment[0, 0], second[0, 0])
     scratch = [
         pltpu.VMEM((2, block, 2 * slots), BF16),
         pltpu.VMEM((2, block, half), F32),
     ]
-    earlier = pl.pallas_call(
-        functools.partial(first_update_kernel, blocks[:1]),
-        out_shape=jax.ShapeDtypeStruct((block, half), F32),
-        in_specs=specs(pltpu.VMEM, 7),
+    earlier, placed, scales = pl.pallas_call(
+        functools.partial(first_update_kernel, blocks[:-1], order, group, cap),
+        out_shape=[
+            jax.ShapeDtypeStruct((above, half), F32),
+            jax.ShapeDtypeStruct((2 * slots, half), BF16),
+            jax.ShapeDtypeStruct((2, TILE, LANES), F32),
+        ],
+        in_specs=specs(pltpu.VMEM, len(order) + 5),
+        out_specs=specs(pltpu.VMEM, 3),
+        scratch_shapes=scratch,
+        compiler_params=params(),
+        cost_estimate=cost(4 * slots * above * half, 12 * above * half),
+        name="first_update",
+    )(*[arrived[item] for item in order], own_hidden, other_hidden, *inputs)
+    own_scores = pl.pallas_call(
+        functools.partial(merge_kernel, group),
+        out_shape=tile,
+        in_specs=specs(pltpu.VMEM, group),
         out_specs=specs(pltpu.VMEM, 1)[0],
-        scratch_shapes=scratch,
-        compiler_params=params(),
-        cost_estimate=cost(4 * slots * block * half, 12 * block * half),
-        name="first_update",
-    )(*operands)
-    full_scores = pl.pallas_call(
-        functools.partial(merge_kernel, cap),
-        out_shape=jax.ShapeDtypeStruct(scores.shape, F32),
-        in_specs=specs(pltpu.VMEM, 2),
-        out_specs=specs(pltpu.VMEM, 1)[0],
         compiler_params=params(),
         name="merge",
-    )(scores, other_scores)
-    returned = [moved(full_scores, 0, k) for k in range(group)]
+    )(*[returned[k] for k in range(group)])
+    other_scores = moved(own_scores, 1, 0)
     update = pl.pallas_call(
-        functools.partial(last_update_kernel, blocks[1:]),
+        functools.partial(last_update_kernel, blocks[-1:]),
         out_shape=jax.ShapeDtypeStruct((hid, half), F32),
         in_specs=specs(pltpu.VMEM, 8) + specs(pl.ANY, 1),
         out_specs=specs(pltpu.HBM, 1)[0],
         scratch_shapes=scratch
         + [
-            pltpu.VMEM((hid - block, half), F32),
-            pltpu.SemaphoreType.DMA((len(blocks),)),
+            pltpu.VMEM((hid - above, half), F32),
+            pltpu.SemaphoreType.DMA((2,)),
         ],
         compiler_params=params(),
-        cost_estimate=cost(4 * slots * (hid - block) * half, 12 * hid * half),
+        cost_estimate=cost(4 * slots * (hid - above) * half, 12 * hid * half),
         name="last_update",
-    )(*operands, earlier, full_scores)
+    )(own_hidden, other_hidden, placed, scales, *inputs, earlier, own_scores)
     router = pl.pallas_call(
         functools.partial(combine_kernel, group, cap),
         out_shape=jax.ShapeDtypeStruct((top, tokens), F32),
-        in_specs=specs(pltpu.VMEM, 2 + group),
+        in_specs=specs(pltpu.VMEM, 4),
         out_specs=specs(pltpu.VMEM, 1)[0],
         compiler_params=params(),
         cost_estimate=cost(4 * slots * tokens, 8 * top * tokens),
         name="combine",
-    )(ids, slot_of, *returned)
+    )(ids, slot_of, own_scores, other_scores)
     return (update[None, None], router.T[None])
 
 

time: 44.3 us -> 43 us (0.971)
  waiting for transfers between devices: 16.3 us -> 7.16 us
  starting transfers between devices: 17.3 us -> 25.2 us
  Pallas kernels: 7.84 us -> 9.72 us
  local copies, waits for them, and re-layouts: 1.91 us -> 0.03 us
    ppermute x12, waiting for transfers between devices: 16.3 us -> 7.16 us  [moved(): return lax.ppermute(array, ('pair', 'ep'), pairs)]
    ppermute x12, starting transfers between devices: 17.3 us -> 25.2 us  [moved(): return lax.ppermute(array, ('pair', 'ep'), pairs)]
    unnamed x12 -> x10, local copies, waits for them, and re-layouts: 1.91 us -> 0.03 us
    pallas_call x1, Pallas kernels: 1 us -> 2.77 us  [local(): pl.pallas_call(inner_kernel, out_shape=jax.ShapeDtypeStruct((2 * slots, h...]
    pallas_call x4 -> x5, Pallas kernels: 3.81 us -> 3.91 us  [the longest x1 1.77 us: local(): pl.pallas_call(functools.partial(last_update_kernel, blocks[-1:]), out_sh...]
  transfers between devices with their start and end apart: 12 -> 12, of which waited for: 5 -> 5; matrix products, arithmetic and copies ran while one was open for 0% -> 0% of each run, Pallas kernels for 15% -> 20%
where the time goes in v8:
time: 43 us; the launch traced here: 42.8 us
  starting transfers between devices  25.2 us (59%)
  Pallas kernels  9.72 us (23%)
  waiting for transfers between devices  7.16 us (17%)
  between operations  0.73 us (2%)
    ppermute x12, starting transfers between devices, moved(): return lax.ppermute(array, ('pair', 'ep'), pairs)  25.2 us
    ppermute x12, waiting for transfers between devices, moved(): return lax.ppermute(array, ('pair', 'ep'), pairs)  7.16 us
    pallas_call x1, Pallas kernels, local(): pl.pallas_call(inner_kernel, out_shape=jax.ShapeDtypeStruct((2 * slots, h...  2.77 us
    pallas_call x1, Pallas kernels, local(): pl.pallas_call(functools.partial(route_kernel, order, group, cap), out_sh...  2.19 us
    pallas_call x1, Pallas kernels, local(): pl.pallas_call(functools.partial(last_update_kernel, blocks[-1:]), out_sh...  1.77 us
    pallas_call x1, Pallas kernels, local(): pl.pallas_call(functools.partial(first_update_kernel, blocks[:-1], order,...  1.73 us
  transfers between devices with their start and end apart: 12, of which 5 were waited for; matrix products, arithmetic and copies ran while one was open for 0% of the time, Pallas kernels for 20%

profile of v8, /device:TPU:0, one launch (start us, length us, event | category | flops | bytes accessed | tf_op | source)
XLA Modules:
  0.0 42.8 jit_solution(12368564568173099691)
XLA Ops:
  0.6 3.0 %collective-permute-start = (bf16[768,256]{1,0:T(8,128)(2,1)}, bf16[768,256]{1,0:T(8,128)(2,1)S(1)}, u32[]{:S(2)}, u32[]{:S(2)}) collective-permute-start(bf16[768,256]{1,0:T(8,128)(2,1)} %bitcast.22), channel_id=1, source_target_pairs={{0,16},{1,17},{2,18},{3,19},{16,0},{17,1},{18,2},{19,3},{4,20},{5,... | collective-permute-start | bytes 1179656 | tf_op jit(solution)/shard_map/ppermute | solution.py:319
  3.7 2.2 %route.1 = (f32[16,512]{1,0:T(8,128)S(1)}, bf16[528,128]{1,0:T(8,128)(2,1)S(1)}, bf16[528,128]{1,0:T(8,128)(2,1)S(1)}, bf16[528,128]{1,0:T(8,128)(2,1)S(1)}, bf1...) custom-call(s32[8,512]{1,0:T(8,128)} %bitcast.26, ...), custom_call_target="tpu_custom_call" | custom-call | flops 536870912 | bytes 3145728 | tf_op jit(solution)/shard_map/route/pallas_call | solution.py:342
  5.9 1.6 %collective-permute-start.1 = (bf16[528,128]{1,0:T(8,128)(2,1)S(1)}, bf16[528,128]{1,0:T(8,128)(2,1)S(1)}, u32[]{:S(2)}, u32[]{:S(2)}) collective-permute-start(bf16[528,128]{1,0:T(8,128)(2,1)S(1)} %get-tuple-element.15), channel_id=1, source_target_pairs={{0,1},{1,0},{2,3},{3,2},{16,17},{17,16},{18,19},{19,18},{4,5},{5,4... | collective-permute-start | bytes 405512 | tf_op jit(solution)/shard_map/ppermute | solution.py:319
  7.5 2.5 %collective-permute-start.2 = (bf16[528,128]{1,0:T(8,128)(2,1)S(1)}, bf16[528,128]{1,0:T(8,128)(2,1)S(1)}, u32[]{:S(2)}, u32[]{:S(2)}) collective-permute-start(bf16[528,128]{1,0:T(8,128)(2,1)S(1)} %get-tuple-element.16), channel_id=1, source_target_pairs={{0,3},{1,2},{2,1},{3,0},{16,19},{17,18},{18,17},{19,16},{4,7},{5,6... | collective-permute-start | bytes 405512 | tf_op jit(solution)/shard_map/ppermute | solution.py:319
  10.0 0.5 %collective-permute-start.3 = (bf16[528,128]{1,0:T(8,128)(2,1)S(1)}, bf16[528,128]{1,0:T(8,128)(2,1)S(1)}, u32[]{:S(2)}, u32[]{:S(2)}) collective-permute-start(bf16[528,128]{1,0:T(8,128)(2,1)S(1)} %get-tuple-element.17), channel_id=1, source_target_pairs={{0,16},{1,17},{2,18},{3,19},{16,0},{17,1},{18,2},{19,3},{4,20},{5,... | collective-permute-start | bytes 405512 | tf_op jit(solution)/shard_map/ppermute | solution.py:319
  10.5 2.3 %collective-permute-start.4 = (bf16[528,128]{1,0:T(8,128)(2,1)S(1)}, bf16[528,128]{1,0:T(8,128)(2,1)S(1)}, u32[]{:S(2)}, u32[]{:S(2)}) collective-permute-start(bf16[528,128]{1,0:T(8,128)(2,1)S(1)} %get-tuple-element.18), channel_id=1, source_target_pairs={{0,19},{1,18},{2,17},{3,16},{16,3},{17,2},{18,1},{19,0},{4,23},{5,... | collective-permute-start | bytes 405512 | tf_op jit(solution)/shard_map/ppermute | solution.py:319
  12.8 0.4 collective-permute-start.5
  13.2 4.1 %collective-permute-done.2.refs_2_.rest_2_ = bf16[528,128]{1,0:T(8,128)(2,1)S(1)} collective-permute-done((bf16[528,128]{1,0:T(8,128)(2,1)S(1)}, bf16[528,128]{1,0:T(8,128)(2,1)S(1)}, u32[]{:S(2)}, u32[]{:S(2)}) %collective-permute-start.2) | collective-permute-done | bytes 135200 | tf_op jit(solution)/shard_map/ppermute | solution.py:319
  17.3 4.7 %collective-permute-start.6 = (bf16[528,128]{1,0:T(8,128)(2,1)S(1)}, bf16[528,128]{1,0:T(8,128)(2,1)S(1)}, u32[]{:S(2)}, u32[]{:S(2)}) collective-permute-start(bf16[528,128]{1,0:T(8,128)(2,1)S(1)} %get-tuple-element.20), channel_id=1, source_target_pairs={{0,2},{1,3},{2,0},{3,1},{16,18},{17,19},{18,16},{19,17},{4,6},{5,7... | collective-permute-start | bytes 405512 | tf_op jit(solution)/shard_map/ppermute | solution.py:319
  22.0 2.8 %inner.1.inner_ref = f32[512,1024]{1,0:T(8,128)S(1)} custom-call(bf16[768,256]{1,0:T(8,128)(2,1)S(1)} %bitcast.23, bf16[768,256]{1,0:T(8,128)(2,1)S(1)} %collective-permute-done.refs_9_.other_ref.refs_1_, f32[768,1024]{1,0:T(8,128)} %bitcast.15), custom_call_target="tpu_custom_call" | custom-call | flops 805306368 | bytes 5242880 | tf_op jit(solution)/shard_map/inner/pallas_call | solution.py:364
  24.8 0.0 copy-start
  24.8 0.3 score.2.rest_2_.local_ref
  25.1 0.8 %collective-permute-start.9 = (f32[8,128]{1,0:T(8,128)S(1)}, f32[8,128]{1,0:T(8,128)S(1)}, u32[]{:S(2)}, u32[]{:S(2)}) collective-permute-start(f32[8,128]{1,0:T(8,128)S(1)} %score.2.rest_2_.local_ref), channel_id=1, source_target_pairs={{0,3},{1,2},{2,1},{3,0},{16,19},{17,18},{18,17},{19,16},{4,7},{5,6... | collective-permute-start | bytes 12296 | tf_op jit(solution)/shard_map/ppermute | solution.py:319
  25.9 5.8 %collective-permute-start.8 = (f32[8,128]{1,0:T(8,128)S(1)}, f32[8,128]{1,0:T(8,128)S(1)}, u32[]{:S(2)}, u32[]{:S(2)}) collective-permute-start(f32[8,128]{1,0:T(8,128)S(1)} %score.2.rest_2_.local_ref), channel_id=1, source_target_pairs={{0,1},{1,0},{2,3},{3,2},{16,17},{17,16},{18,19},{19,18},{4,5},{5,4... | collective-permute-start | bytes 12296 | tf_op jit(solution)/shard_map/ppermute | solution.py:319
  31.7 1.8 %collective-permute-done.7.refs_7_.rest_1_ = bf16[528,128]{1,0:T(8,128)(2,1)S(1)} collective-permute-done((bf16[528,128]{1,0:T(8,128)(2,1)S(1)}, bf16[528,128]{1,0:T(8,128)(2,1)S(1)}, u32[]{:S(2)}, u32[]{:S(2)}) %collective-permute-start.7) | collective-permute-done | bytes 135200 | tf_op jit(solution)/shard_map/ppermute | solution.py:319
  33.5 0.1 collective-permute-done.8.rest_3_.rest_0_
  33.6 0.1 score.3
  33.7 2.0 %collective-permute-start.10 = (f32[8,128]{1,0:T(8,128)S(1)}, f32[8,128]{1,0:T(8,128)S(1)}, u32[]{:S(2)}, u32[]{:S(2)}) collective-permute-start(f32[8,128]{1,0:T(8,128)S(1)} %score.3), channel_id=1, source_target_pairs={{0,2},{1,3},{2,0},{3,1},{16,18},{17,19},{18,16},{19,17},{4,6},{5,7... | collective-permute-start | bytes 12296 | tf_op jit(solution)/shard_map/ppermute | solution.py:319
  35.7 1.7 %first_update.1 = (f32[512,1024]{1,0:T(8,128)S(1)}, bf16[512,1024]{1,0:T(8,128)(2,1)S(1)}, f32[2,16,128]{2,1,0:T(8,128)S(1)}) custom-call(bf16[528,128]{1,0:T(8,128)(2,1)S(1)} %get-tuple-element.14.refs_0_.rest_0_, bf16[528,128]{1,0:T(8,128)(2,1)S(1)} %collective-permute-done.1.refs_1_.rest_1_, bf16[528,128]{1,0:T(8,128)(2,1)S(1)} %collective-permute-done.2.refs_2_.rest_2_, ...), custom_call_target="tpu_custom_call" | custom-call | flops 536870912 | bytes 6291456 | tf_op jit(solution)/shard_map/first_update/pallas_call | solution.py:402
  37.4 0.8 %collective-permute-done.10.rest_1_ = f32[8,128]{1,0:T(8,128)S(1)} collective-permute-done((f32[8,128]{1,0:T(8,128)S(1)}, f32[8,128]{1,0:T(8,128)S(1)}, u32[]{:S(2)}, u32[]{:S(2)}) %collective-permute-start.10) | collective-permute-done | bytes 4128 | tf_op jit(solution)/shard_map/ppermute | solution.py:319
  38.3 1.5 %collective-permute-start.11 = (f32[8,128]{1,0:T(8,128)S(1)}, f32[8,128]{1,0:T(8,128)S(1)}, u32[]{:S(2)}, u32[]{:S(2)}) collective-permute-start(f32[8,128]{1,0:T(8,128)S(1)} %merge.1.refs_8_.own_ref), channel_id=1, source_target_pairs={{0,16},{1,17},{2,18},{3,19},{16,0},{17,1},{18,2},{19,3},{4,20},{5,... | collective-permute-start | bytes 12296 | tf_op jit(solution)/shard_map/ppermute | solution.py:319
  39.8 1.8 %last_update.1 = f32[768,1024]{1,0:T(8,128)} custom-call(bf16[768,256]{1,0:T(8,128)(2,1)S(1)} %bitcast.25, bf16[768,256]{1,0:T(8,128)(2,1)S(1)} %collective-permute-done.refs_9_.other_ref.refs_1_, bf16[512,1024]{1,0:T(8,128)(2,1)S(1)} %get-tuple-element.22.refs_2_, f32[2,16,128]{2,1,0:T(8,128)S(1)} %get-tuple-element.23.refs_3_, f32[768,1024]{1,0:T(8,128)S(1)} %bitcast.17, ...), custom_call_target="tpu_custom_call" | custom-call | flops 268435456 | bytes 9437184 | tf_op jit(solution)/shard_map/last_update/pallas_call | solution.py:425
  41.6 0.4 collective-permute-done.11.other_ref
  42.0 0.8 %combine.1 = f32[8,512]{1,0:T(8,128)} custom-call(s32[8,512]{1,0:T(8,128)S(1)} %bitcast.27, f32[16,512]{1,0:T(8,128)S(1)} %get-tuple-element.25.slots_ref, f32[8,128]{1,0:T(8,128)S(1)} %merge.1.refs_8_.own_ref, f32[8,128]{1,0:T(8,128)S(1)} %collective-permute-done.11.other_ref), custom_call_target="tpu_custom_call" | custom-call | flops 524288 | bytes 32768 | tf_op jit(solution)/shard_map/combine/pallas_call | solution.py:439
  (18 shorter events, 0.1 us)
Async XLA Ops:
  0.6 21.3 %copy-start.3 = (bf16[1,1,768,256]{3,2,1,0:T(8,128)(2,1)S(1)}, bf16[1,1,768,256]{3,2,1,0:T(8,128)(2,1)}, u32[]{:S(2)}) copy-start(bf16[1,1,768,256]{3,2,1,0:T(8,128)(2,1)} %param.10) | copy-start | bytes 1179652
  0.6 21.3 %collective-permute-start = (bf16[768,256]{1,0:T(8,128)(2,1)}, bf16[768,256]{1,0:T(8,128)(2,1)S(1)}, u32[]{:S(2)}, u32[]{:S(2)}) collective-permute-start(bf16[768,256]{1,0:T(8,128)(2,1)} %bitcast.22), channel_id=1, source_target_pairs={{0,16},{1,17},{2,18},{3,19},{16,0},{17,1},{18,2},{19,3},{4,20},{5,... | collective-permute-start | bytes 1179656 | tf_op jit(solution)/shard_map/ppermute | solution.py:319
  5.9 6.9 %collective-permute-start.1 = (bf16[528,128]{1,0:T(8,128)(2,1)S(1)}, bf16[528,128]{1,0:T(8,128)(2,1)S(1)}, u32[]{:S(2)}, u32[]{:S(2)}) collective-permute-start(bf16[528,128]{1,0:T(8,128)(2,1)S(1)} %get-tuple-element.15), channel_id=1, source_target_pairs={{0,1},{1,0},{2,3},{3,2},{16,17},{17,16},{18,19},{19,18},{4,5},{5,4... | collective-permute-start | bytes 405512 | tf_op jit(solution)/shard_map/ppermute | solution.py:319
  7.5 9.8 %collective-permute-start.2 = (bf16[528,128]{1,0:T(8,128)(2,1)S(1)}, bf16[528,128]{1,0:T(8,128)(2,1)S(1)}, u32[]{:S(2)}, u32[]{:S(2)}) collective-permute-start(bf16[528,128]{1,0:T(8,128)(2,1)S(1)} %get-tuple-element.16), channel_id=1, source_target_pairs={{0,3},{1,2},{2,1},{3,0},{16,19},{17,18},{18,17},{19,16},{4,7},{5,6... | collective-permute-start | bytes 405512 | tf_op jit(solution)/shard_map/ppermute | solution.py:319
  10.0 14.8 %collective-permute-start.3 = (bf16[528,128]{1,0:T(8,128)(2,1)S(1)}, bf16[528,128]{1,0:T(8,128)(2,1)S(1)}, u32[]{:S(2)}, u32[]{:S(2)}) collective-permute-start(bf16[528,128]{1,0:T(8,128)(2,1)S(1)} %get-tuple-element.17), channel_id=1, source_target_pairs={{0,16},{1,17},{2,18},{3,19},{16,0},{17,1},{18,2},{19,3},{4,20},{5,... | collective-permute-start | bytes 405512 | tf_op jit(solution)/shard_map/ppermute | solution.py:319
  10.5 14.3 %collective-permute-start.4 = (bf16[528,128]{1,0:T(8,128)(2,1)S(1)}, bf16[528,128]{1,0:T(8,128)(2,1)S(1)}, u32[]{:S(2)}, u32[]{:S(2)}) collective-permute-start(bf16[528,128]{1,0:T(8,128)(2,1)S(1)} %get-tuple-element.18), channel_id=1, source_target_pairs={{0,19},{1,18},{2,17},{3,16},{16,3},{17,2},{18,1},{19,0},{4,23},{5,... | collective-permute-start | bytes 405512 | tf_op jit(solution)/shard_map/ppermute | solution.py:319
  12.8 12.0 %collective-permute-start.5 = (bf16[528,128]{1,0:T(8,128)(2,1)S(1)}, bf16[528,128]{1,0:T(8,128)(2,1)S(1)}, u32[]{:S(2)}, u32[]{:S(2)}) collective-permute-start(bf16[528,128]{1,0:T(8,128)(2,1)S(1)} %get-tuple-element.19), channel_id=1, source_target_pairs={{0,17},{1,16},{2,19},{3,18},{16,1},{17,0},{18,3},{19,2},{4,21},{5,... | collective-permute-start | bytes 405512 | tf_op jit(solution)/shard_map/ppermute | solution.py:319
  17.3 14.4 %collective-permute-start.6 = (bf16[528,128]{1,0:T(8,128)(2,1)S(1)}, bf16[528,128]{1,0:T(8,128)(2,1)S(1)}, u32[]{:S(2)}, u32[]{:S(2)}) collective-permute-start(bf16[528,128]{1,0:T(8,128)(2,1)S(1)} %get-tuple-element.20), channel_id=1, source_target_pairs={{0,2},{1,3},{2,0},{3,1},{16,18},{17,19},{18,16},{19,17},{4,6},{5,7... | collective-permute-start | bytes 405512 | tf_op jit(solution)/shard_map/ppermute | solution.py:319
  22.0 11.5 %collective-permute-start.7 = (bf16[528,128]{1,0:T(8,128)(2,1)S(1)}, bf16[528,128]{1,0:T(8,128)(2,1)S(1)}, u32[]{:S(2)}, u32[]{:S(2)}) collective-permute-start(bf16[528,128]{1,0:T(8,128)(2,1)S(1)} %get-tuple-element.21), channel_id=1, source_target_pairs={{0,18},{1,19},{2,16},{3,17},{16,2},{17,3},{18,0},{19,1},{4,22},{5,... | collective-permute-start | bytes 405512 | tf_op jit(solution)/shard_map/ppermute | solution.py:319
  22.0 13.7 %copy-start.2 = (bf16[1,1,768,1024]{3,2,1,0:T(8,128)(2,1)S(1)}, bf16[1,1,768,1024]{3,2,1,0:T(8,128)(2,1)}, u32[]{:S(2)}) copy-start(bf16[1,1,768,1024]{3,2,1,0:T(8,128)(2,1)} %param.13) | copy-start | bytes 4718596
  24.8 10.9 %copy-start = (f32[1,1,768,1024]{3,2,1,0:T(8,128)S(1)}, f32[1,1,768,1024]{3,2,1,0:T(8,128)}, u32[]{:S(2)}) copy-start(f32[1,1,768,1024]{3,2,1,0:T(8,128)} %param.11) | copy-start | bytes 9437188
  24.8 10.9 %copy-start.1 = (bf16[1,1,768,1024]{3,2,1,0:T(8,128)(2,1)S(1)}, bf16[1,1,768,1024]{3,2,1,0:T(8,128)(2,1)}, u32[]{:S(2)}) copy-start(bf16[1,1,768,1024]{3,2,1,0:T(8,128)(2,1)} %param.12) | copy-start | bytes 4718596
  25.1 8.4 %collective-permute-start.9 = (f32[8,128]{1,0:T(8,128)S(1)}, f32[8,128]{1,0:T(8,128)S(1)}, u32[]{:S(2)}, u32[]{:S(2)}) collective-permute-start(f32[8,128]{1,0:T(8,128)S(1)} %score.2.rest_2_.local_ref), channel_id=1, source_target_pairs={{0,3},{1,2},{2,1},{3,0},{16,19},{17,18},{18,17},{19,16},{4,7},{5,6... | collective-permute-start | bytes 12296 | tf_op jit(solution)/shard_map/ppermute | solution.py:319
  25.9 7.7 %collective-permute-start.8 = (f32[8,128]{1,0:T(8,128)S(1)}, f32[8,128]{1,0:T(8,128)S(1)}, u32[]{:S(2)}, u32[]{:S(2)}) collective-permute-start(f32[8,128]{1,0:T(8,128)S(1)} %score.2.rest_2_.local_ref), channel_id=1, source_target_pairs={{0,1},{1,0},{2,3},{3,2},{16,17},{17,16},{18,19},{19,18},{4,5},{5,4... | collective-permute-start | bytes 12296 | tf_op jit(solution)/shard_map/ppermute | solution.py:319
  33.7 4.6 %collective-permute-start.10 = (f32[8,128]{1,0:T(8,128)S(1)}, f32[8,128]{1,0:T(8,128)S(1)}, u32[]{:S(2)}, u32[]{:S(2)}) collective-permute-start(f32[8,128]{1,0:T(8,128)S(1)} %score.3), channel_id=1, source_target_pairs={{0,2},{1,3},{2,0},{3,1},{16,18},{17,19},{18,16},{19,17},{4,6},{5,7... | collective-permute-start | bytes 12296 | tf_op jit(solution)/shard_map/ppermute | solution.py:319
  38.3 3.7 %collective-permute-start.11 = (f32[8,128]{1,0:T(8,128)S(1)}, f32[8,128]{1,0:T(8,128)S(1)}, u32[]{:S(2)}, u32[]{:S(2)}) collective-permute-start(f32[8,128]{1,0:T(8,128)S(1)} %merge.1.refs_8_.own_ref), channel_id=1, source_target_pairs={{0,16},{1,17},{2,18},{3,19},{16,0},{17,1},{18,2},{19,3},{4,20},{5,... | collective-permute-start | bytes 12296 | tf_op jit(solution)/shard_map/ppermute | solution.py:319
  39.8 2.2 %copy-start.4 = (s32[1,512,8]{1,2,0:T(8,128)S(1)}, s32[1,512,8]{1,2,0:T(8,128)}, u32[]{:S(2)}) copy-start(s32[1,512,8]{1,2,0:T(8,128)} %param.9) | copy-start | bytes 49156

commit v9 on v8

--- a/solution.py
+++ b/solution.py
@@ -61,28 +61,29 @@
     return jnp.where(place == slots[k : k + 1, :], 1.0, 0.0).astype(BF16)
 
 
-def fill_chunks(group, cap, pick, held, copies, tiles, chunks):
+def fill_chunks(steps, cap, picks, held, copies, tiles, chunks):
     half = held.shape[2]
     data_rows = half // LANES * cap
     step = min(half, 2 * LANES)
+    pick = jnp.concatenate([picks[k] for k in steps], axis=0)
     for side in range(2):
-        for k in range(group):
+        for k in steps:
             chunks[side, k][data_rows:, :] = tiles[k]
         copies[side].wait()
         for column in range(0, half, step):
             block = jnp.dot(
                 pick, held[side, :, column : column + step], preferred_element_type=F32
             ).astype(BF16)
-            for k in range(group):
+            for at, k in enumerate(steps):
                 for part in range(step // LANES):
                     top = (column // LANES + part) * cap
                     chunks[side, k][top : top + cap, :] = block[
-                        k * cap : (k + 1) * cap, part * LANES : (part + 1) * LANES
+                        at * cap : (at + 1) * cap, part * LANES : (part + 1) * LANES
                     ]
 
 
 def route_kernel(
-    items, group, cap, ids_hbm, weight_hbm, grads_hbm, slots_ref, *rest
+    items, steps, group, cap, ids_hbm, weight_hbm, grads_hbm, slots_ref, tiles_ref, *rest
 ):
     chunks = dict(zip(items, rest))
     ids_ref, weight_ref, held, sems = rest[len(items) :]
@@ -127,8 +128,17 @@
             spread, doubled, (((1,), (1,)), ((), ())), preferred_element_type=F32
         )
         tiles.append(jnp.where(kept, tile, 0.0).astype(BF16))
-    pick = jnp.concatenate(picks, axis=0)
-    fill_chunks(group, cap, pick, held, copies, tiles, chunks)
+        tiles_ref[k] = tiles[k]
+    fill_chunks(steps, cap, picks, held, copies, tiles, chunks)
+
+
+def later_kernel(items, steps, cap, slots_ref, tiles_ref, grads_hbm, _, *rest):
+    chunks = dict(zip(items, rest))
+    held, sems = rest[len(items) :]
+    copies = start_grads(grads_hbm, held, sems)
+    slots = slots_ref[...]
+    picks = {k: pick_rows(slots, k, cap) for k in steps}
+    fill_chunks(steps, cap, picks, held, copies, tiles_ref, chunks)
 
 
 def inner_kernel(own_ref, other_ref, master_hbm, inner_ref, master_ref, sems):
@@ -332,23 +342,27 @@
     other_hidden = moved(own_hidden, 1, 0)
 
     far = group // 2
-    early = [k for k in range(group) if k != far]
-    wide = [k for k in reversed(early) if k > 1]
-    order = [(0, 1)] + [(0, k) for k in wide] + [(1, 0)] + [(1, k) for k in wide] + [(1, 1)]
-    first_items = [(0, 0)] + order
-    last_items = [(0, far), (1, far)]
+    early = [k for k in range(1, group) if k != far]
+    late = [0, far]
+    first_items = [(side, k) for side in range(2) for k in reversed(early)]
+    last_items = [(0, far), (1, far), (1, 0), (0, 0)]
     order = first_items + last_items
     chunk = jax.ShapeDtypeStruct((half // LANES * cap + TILE, LANES), BF16)
+    grads = pltpu.with_memory_space_constraint(grad_out[0], pltpu.HBM)
+    held = pltpu.VMEM((2, tokens, half), BF16)
     routed = pl.pallas_call(
-        functools.partial(route_kernel, order, group, cap),
-        out_shape=[jax.ShapeDtypeStruct((group + -group % TILE, tokens), F32)]
-        + [chunk] * (2 * group),
+        functools.partial(route_kernel, first_items, early, group, cap),
+        out_shape=[
+            jax.ShapeDtypeStruct((group + -group % TILE, tokens), F32),
+            jax.ShapeDtypeStruct((group, TILE, LANES), BF16),
+        ]
+        + [chunk] * len(first_items),
         in_specs=specs(pltpu.HBM, 3),
-        out_specs=specs(pltpu.VMEM, 1 + 2 * group),
+        out_specs=specs(pltpu.VMEM, 2 + len(first_items)),
         scratch_shapes=[
             pltpu.VMEM((top, tokens), jnp.int32),
             pltpu.VMEM((top, tokens), BF16),
-            pltpu.VMEM((2, tokens, half), BF16),
+            held,
             pltpu.SemaphoreType.DMA((4,)),
         ],
         compiler_params=params(),
@@ -357,10 +371,11 @@
     )(
         pltpu.with_memory_space_constraint(ids, pltpu.HBM),
         pltpu.with_memory_space_constraint(router_weights[0].T, pltpu.HBM),
-        pltpu.with_memory_space_constraint(grad_out[0], pltpu.HBM),
+        grads,
     )
-    slot_of = routed[0]
-    arrived = {item: moved(sent, *item) for item, sent in zip(order, routed[1:])}
+    slot_of, tiles = routed[:2]
+    arrived = {item: moved(sent, *item) for item, sent in zip(first_items, routed[2:])}
+
     inner = pl.pallas_call(
         inner_kernel,
         out_shape=jax.ShapeDtypeStruct((2 * slots, half), F32),
@@ -375,9 +390,21 @@
         name="inner",
     )(own_hidden, other_hidden, pltpu.with_memory_space_constraint(param, pltpu.HBM))
 
+    routed = pl.pallas_call(
+        functools.partial(later_kernel, last_items, late, cap),
+        out_shape=[chunk] * len(last_items),
+        in_specs=specs(pltpu.VMEM, 2) + specs(pltpu.HBM, 1) + specs(pl.ANY, 1),
+        out_specs=specs(pltpu.VMEM, len(last_items)),
+        scratch_shapes=[held, pltpu.SemaphoreType.DMA((2,))],
+        compiler_params=params(),
+        cost_estimate=cost(2 * slots * tokens * width, 2 * (tokens + slots) * width),
+        name="later",
+    )(slot_of, tiles, grads, inner)
+    arrived |= {item: moved(sent, *item) for item, sent in zip(last_items, routed)}
+
     tile = jax.ShapeDtypeStruct((group + -group % 8, LANES), F32)
     returned = {}
-    for items, steps in ((first_items, early), (last_items, [far])):
+    for items, steps in ((first_items, early), (last_items, late)):
         done = list(returned.values())
         scores = pl.pallas_call(
             functools.partial(score_kernel, items, steps, group, cap),

time: 43 us -> 42.8 us (level)
  starting transfers between devices: 25.2 us -> 19.9 us
  waiting for transfers between devices: 7.16 us -> 10.7 us
  Pallas kernels: 9.72 us -> 11.3 us
    ppermute x12, starting transfers between devices: 25.2 us -> 19.9 us  [moved(): return lax.ppermute(array, ('pair', 'ep'), pairs)]
    ppermute x12, waiting for transfers between devices: 7.16 us -> 10.7 us  [moved(): return lax.ppermute(array, ('pair', 'ep'), pairs)]
    pallas_call x1 -> x2, Pallas kernels: 2.19 us -> 3.93 us  [the longest x1 2 us: local(): pl.pallas_call(functools.partial(later_kernel, last_items, late, cap), ou...]
  transfers between devices with their start and end apart: 12 -> 12, of which waited for: 5 -> 6; matrix products, arithmetic and copies ran while one was open for 0% -> 0% of each run, Pallas kernels for 20% -> 24%
where the time goes in v9:
time: 42.8 us; the launch traced here: 42.6 us
  starting transfers between devices  19.9 us (46%)
  Pallas kernels  11.3 us (26%)
  waiting for transfers between devices  10.7 us (25%)
  between operations  0.71 us (2%)
    ppermute x12, starting transfers between devices, moved(): return lax.ppermute(array, ('pair', 'ep'), pairs)  19.9 us
    ppermute x12, waiting for transfers between devices, moved(): return lax.ppermute(array, ('pair', 'ep'), pairs)  10.7 us
    pallas_call x1, Pallas kernels, local(): pl.pallas_call(inner_kernel, out_shape=jax.ShapeDtypeStruct((2 * slots, h...  2.64 us
    pallas_call x1, Pallas kernels, local(): pl.pallas_call(functools.partial(later_kernel, last_items, late, cap), ou...  2 us
    pallas_call x1, Pallas kernels, local(): pl.pallas_call(functools.partial(route_kernel, first_items, early, group,...  1.94 us
    pallas_call x1, Pallas kernels, local(): pl.pallas_call(functools.partial(last_update_kernel, blocks[-1:]), out_sh...  1.77 us
    pallas_call x1, Pallas kernels, local(): pl.pallas_call(functools.partial(first_update_kernel, blocks[:-1], order,...  1.72 us
  transfers between devices with their start and end apart: 12, of which 6 were waited for; matrix products, arithmetic and copies ran while one was open for 0% of the time, Pallas kernels for 24%

profile of v9, /device:TPU:0, one launch (start us, length us, event | category | flops | bytes accessed | tf_op | source)
XLA Modules:
  0.0 42.6 jit_solution(16306810936047367352)
XLA Ops:
  0.6 3.0 %collective-permute-start = (bf16[768,256]{1,0:T(8,128)(2,1)}, bf16[768,256]{1,0:T(8,128)(2,1)S(1)}, u32[]{:S(2)}, u32[]{:S(2)}) collective-permute-start(bf16[768,256]{1,0:T(8,128)(2,1)} %bitcast.22), channel_id=1, source_target_pairs={{0,16},{1,17},{2,18},{3,19},{16,0},{17,1},{18,2},{19,3},{4,20},{5,... | collective-permute-start | bytes 1179656 | tf_op jit(solution)/shard_map/ppermute | solution.py:329
  3.7 1.9 %route.1 = (f32[16,512]{1,0:T(8,128)S(1)}, bf16[4,16,128]{2,1,0:T(8,128)(2,1)S(1)}, bf16[528,128]{1,0:T(8,128)(2,1)S(1)}, bf16[528,128]{1,0:T(8,128)(2,1)S(1)}, ...) custom-call(s32[8,512]{1,0:T(8,128)} %bitcast.26, bf16[8,512]{1,0:T(8,128)(2,1)} %bitcast.32, ...), custom_call_target="tpu_custom_call" | custom-call | flops 536870912 | bytes 3145728 | tf_op jit(solution)/shard_map/route/pallas_call | solution.py:353
  5.6 3.7 %collective-permute-start.1 = (bf16[528,128]{1,0:T(8,128)(2,1)S(1)}, bf16[528,128]{1,0:T(8,128)(2,1)S(1)}, u32[]{:S(2)}, u32[]{:S(2)}) collective-permute-start(bf16[528,128]{1,0:T(8,128)(2,1)S(1)} %get-tuple-element.15), channel_id=1, source_target_pairs={{0,3},{1,2},{2,1},{3,0},{16,19},{17,18},{18,17},{19,16},{4,7},{5,6... | collective-permute-start | bytes 405512 | tf_op jit(solution)/shard_map/ppermute | solution.py:329
  9.3 0.8 %collective-permute-start.3 = (bf16[528,128]{1,0:T(8,128)(2,1)S(1)}, bf16[528,128]{1,0:T(8,128)(2,1)S(1)}, u32[]{:S(2)}, u32[]{:S(2)}) collective-permute-start(bf16[528,128]{1,0:T(8,128)(2,1)S(1)} %get-tuple-element.17), channel_id=1, source_target_pairs={{0,19},{1,18},{2,17},{3,16},{16,3},{17,2},{18,1},{19,0},{4,23},{5,... | collective-permute-start | bytes 405512 | tf_op jit(solution)/shard_map/ppermute | solution.py:329
  10.1 1.4 %collective-permute-start.4 = (bf16[528,128]{1,0:T(8,128)(2,1)S(1)}, bf16[528,128]{1,0:T(8,128)(2,1)S(1)}, u32[]{:S(2)}, u32[]{:S(2)}) collective-permute-start(bf16[528,128]{1,0:T(8,128)(2,1)S(1)} %get-tuple-element.18), channel_id=1, source_target_pairs={{0,17},{1,16},{2,19},{3,18},{16,1},{17,0},{18,3},{19,2},{4,21},{5,... | collective-permute-start | bytes 405512 | tf_op jit(solution)/shard_map/ppermute | solution.py:329
  11.5 1.5 %collective-permute-done.other_ref.refs_9_.refs_1_ = bf16[768,256]{1,0:T(8,128)(2,1)S(1)} collective-permute-done((bf16[768,256]{1,0:T(8,128)(2,1)}, bf16[768,256]{1,0:T(8,128)(2,1)S(1)}, u32[]{:S(2)}, u32[]{:S(2)}) %collective-permute-start) | collective-permute-done | bytes 393248 | tf_op jit(solution)/shard_map/ppermute | solution.py:329
  13.0 2.6 %inner.1._.inner_ref = f32[512,1024]{1,0:T(8,128)S(1)} custom-call(bf16[768,256]{1,0:T(8,128)(2,1)S(1)} %bitcast.23, bf16[768,256]{1,0:T(8,128)(2,1)S(1)} %collective-permute-done.other_ref.refs_9_.refs_1_, f32[768,1024]{1,0:T(8,128)} %bitcast.15), custom_call_target="tpu_custom_call" | custom-call | flops 805306368 | bytes 5242880 | tf_op jit(solution)/shard_map/inner/pallas_call | solution.py:379
  15.7 2.0 %later.1 = (bf16[528,128]{1,0:T(8,128)(2,1)S(1)}, bf16[528,128]{1,0:T(8,128)(2,1)S(1)}, bf16[528,128]{1,0:T(8,128)(2,1)S(1)}, bf16[528,128]{1,0:T(8,128)(2,1)S(1)}) custom-call(f32[16,512]{1,0:T(8,128)S(1)} %get-tuple-element.19.slots_ref, bf16[4,16,128]{2,1,0:T(8,128)(2,1)S(1)} %get-tuple-element.20.tiles_ref, bf16[512,2048]{1,0:T(8,128)(2,1)} %bitcast.29, ...), custom_call_target="tpu_custom_call" | custom-call | flops 536870912 | bytes 3145728 | tf_op jit(solution)/shard_map/later/pallas_call | solution.py:393
  17.7 3.5 %collective-permute-start.5 = (bf16[528,128]{1,0:T(8,128)(2,1)S(1)}, bf16[528,128]{1,0:T(8,128)(2,1)S(1)}, u32[]{:S(2)}, u32[]{:S(2)}) collective-permute-start(bf16[528,128]{1,0:T(8,128)(2,1)S(1)} %get-tuple-element.21), channel_id=1, source_target_pairs={{0,2},{1,3},{2,0},{3,1},{16,18},{17,19},{18,16},{19,17},{4,6},{5,7... | collective-permute-start | bytes 405512 | tf_op jit(solution)/shard_map/ppermute | solution.py:329
  21.2 1.1 %collective-permute-start.6 = (bf16[528,128]{1,0:T(8,128)(2,1)S(1)}, bf16[528,128]{1,0:T(8,128)(2,1)S(1)}, u32[]{:S(2)}, u32[]{:S(2)}) collective-permute-start(bf16[528,128]{1,0:T(8,128)(2,1)S(1)} %get-tuple-element.22), channel_id=1, source_target_pairs={{0,18},{1,19},{2,16},{3,17},{16,2},{17,3},{18,0},{19,1},{4,22},{5,... | collective-permute-start | bytes 405512 | tf_op jit(solution)/shard_map/ppermute | solution.py:329
  22.3 0.6 %collective-permute-start.7 = (bf16[528,128]{1,0:T(8,128)(2,1)S(1)}, bf16[528,128]{1,0:T(8,128)(2,1)S(1)}, u32[]{:S(2)}, u32[]{:S(2)}) collective-permute-start(bf16[528,128]{1,0:T(8,128)(2,1)S(1)} %get-tuple-element.23), channel_id=1, source_target_pairs={{0,16},{1,17},{2,18},{3,19},{16,0},{17,1},{18,2},{19,3},{4,20},{5,... | collective-permute-start | bytes 405512 | tf_op jit(solution)/shard_map/ppermute | solution.py:329
  22.8 0.2 score.2
  23.0 3.6 %collective-permute-start.9 = (f32[8,128]{1,0:T(8,128)S(1)}, f32[8,128]{1,0:T(8,128)S(1)}, u32[]{:S(2)}, u32[]{:S(2)}) collective-permute-start(f32[8,128]{1,0:T(8,128)S(1)} %score.2), channel_id=1, source_target_pairs={{0,3},{1,2},{2,1},{3,0},{16,19},{17,18},{18,17},{19,16},{4,7},{5,6... | collective-permute-start | bytes 12296 | tf_op jit(solution)/shard_map/ppermute | solution.py:329
  26.6 2.2 %collective-permute-done.9.rest_5_.rest_2_ = f32[8,128]{1,0:T(8,128)S(1)} collective-permute-done((f32[8,128]{1,0:T(8,128)S(1)}, f32[8,128]{1,0:T(8,128)S(1)}, u32[]{:S(2)}, u32[]{:S(2)}) %collective-permute-start.9) | collective-permute-done | bytes 4128 | tf_op jit(solution)/shard_map/ppermute | solution.py:329
  28.9 1.8 %collective-permute-done.8.rest_4_.rest_0_ = f32[8,128]{1,0:T(8,128)S(1)} collective-permute-done((f32[8,128]{1,0:T(8,128)S(1)}, f32[8,128]{1,0:T(8,128)S(1)}, u32[]{:S(2)}, u32[]{:S(2)}) %collective-permute-start.8) | collective-permute-done | bytes 4128 | tf_op jit(solution)/shard_map/ppermute | solution.py:329
  30.6 2.7 %collective-permute-done.6.refs_5_.rest_1_ = bf16[528,128]{1,0:T(8,128)(2,1)S(1)} collective-permute-done((bf16[528,128]{1,0:T(8,128)(2,1)S(1)}, bf16[528,128]{1,0:T(8,128)(2,1)S(1)}, u32[]{:S(2)}, u32[]{:S(2)}) %collective-permute-start.6) | collective-permute-done | bytes 135200 | tf_op jit(solution)/shard_map/ppermute | solution.py:329
  33.3 0.2 score.3.local_ref
  33.5 1.6 %collective-permute-start.10 = (f32[8,128]{1,0:T(8,128)S(1)}, f32[8,128]{1,0:T(8,128)S(1)}, u32[]{:S(2)}, u32[]{:S(2)}) collective-permute-start(f32[8,128]{1,0:T(8,128)S(1)} %score.3.local_ref), channel_id=1, source_target_pairs={{0,2},{1,3},{2,0},{3,1},{16,18},{17,19},{18,16},{19,17},{4,6},{5,7... | collective-permute-start | bytes 12296 | tf_op jit(solution)/shard_map/ppermute | solution.py:329
  35.2 1.7 %first_update.1 = (f32[512,1024]{1,0:T(8,128)S(1)}, bf16[512,1024]{1,0:T(8,128)(2,1)S(1)}, f32[2,16,128]{2,1,0:T(8,128)S(1)}) custom-call(bf16[528,128]{1,0:T(8,128)(2,1)S(1)} %collective-permute-done.1.refs_0_.rest_0_, bf16[528,128]{1,0:T(8,128)(2,1)S(1)} %collective-permute-done.2.refs_1_.rest_1_, ...), custom_call_target="tpu_custom_call" | custom-call | flops 536870912 | bytes 6291456 | tf_op jit(solution)/shard_map/first_update/pallas_call | solution.py:429
  36.9 1.2 %collective-permute-done.10.rest_1_ = f32[8,128]{1,0:T(8,128)S(1)} collective-permute-done((f32[8,128]{1,0:T(8,128)S(1)}, f32[8,128]{1,0:T(8,128)S(1)}, u32[]{:S(2)}, u32[]{:S(2)}) %collective-permute-start.10) | collective-permute-done | bytes 4128 | tf_op jit(solution)/shard_map/ppermute | solution.py:329
  38.1 0.6 %collective-permute-start.11 = (f32[8,128]{1,0:T(8,128)S(1)}, f32[8,128]{1,0:T(8,128)S(1)}, u32[]{:S(2)}, u32[]{:S(2)}) collective-permute-start(f32[8,128]{1,0:T(8,128)S(1)} %merge.1.refs_8_.own_ref), channel_id=1, source_target_pairs={{0,16},{1,17},{2,18},{3,19},{16,0},{17,1},{18,2},{19,3},{4,20},{5,... | collective-permute-start | bytes 12296 | tf_op jit(solution)/shard_map/ppermute | solution.py:329
  38.7 1.8 %last_update.1 = f32[768,1024]{1,0:T(8,128)} custom-call(bf16[768,256]{1,0:T(8,128)(2,1)S(1)} %bitcast.25, bf16[768,256]{1,0:T(8,128)(2,1)S(1)} %collective-permute-done.other_ref.refs_9_.refs_1_, bf16[512,1024]{1,0:T(8,128)(2,1)S(1)} %get-tuple-element.25.refs_2_, f32[2,16,128]{2,1,0:T(8,128)S(1)} %get-tuple-element.26.refs_3_, f32[768,1024]{1,0:T(8,128)S(1)} %bitcast.17, ...), custom_call_target="tpu_custom_call" | custom-call | flops 268435456 | bytes 9437184 | tf_op jit(solution)/shard_map/last_update/pallas_call | solution.py:452
  40.4 1.3 %collective-permute-done.11.other_ref = f32[8,128]{1,0:T(8,128)S(1)} collective-permute-done((f32[8,128]{1,0:T(8,128)S(1)}, f32[8,128]{1,0:T(8,128)S(1)}, u32[]{:S(2)}, u32[]{:S(2)}) %collective-permute-start.11) | collective-permute-done | bytes 4128 | tf_op jit(solution)/shard_map/ppermute | solution.py:329
  41.8 0.8 %combine.1 = f32[8,512]{1,0:T(8,128)} custom-call(s32[8,512]{1,0:T(8,128)S(1)} %bitcast.27, f32[16,512]{1,0:T(8,128)S(1)} %get-tuple-element.19.slots_ref, f32[8,128]{1,0:T(8,128)S(1)} %merge.1.refs_8_.own_ref, f32[8,128]{1,0:T(8,128)S(1)} %collective-permute-done.11.other_ref), custom_call_target="tpu_custom_call" | custom-call | flops 524288 | bytes 32768 | tf_op jit(solution)/shard_map/combine/pallas_call | solution.py:466
  (19 shorter events, 0.1 us)
Async XLA Ops:
  0.6 12.4 %copy-start.3 = (bf16[1,1,768,256]{3,2,1,0:T(8,128)(2,1)S(1)}, bf16[1,1,768,256]{3,2,1,0:T(8,128)(2,1)}, u32[]{:S(2)}) copy-start(bf16[1,1,768,256]{3,2,1,0:T(8,128)(2,1)} %param.10) | copy-start | bytes 1179652
  0.6 12.4 %collective-permute-start = (bf16[768,256]{1,0:T(8,128)(2,1)}, bf16[768,256]{1,0:T(8,128)(2,1)S(1)}, u32[]{:S(2)}, u32[]{:S(2)}) collective-permute-start(bf16[768,256]{1,0:T(8,128)(2,1)} %bitcast.22), channel_id=1, source_target_pairs={{0,16},{1,17},{2,18},{3,19},{16,0},{17,1},{18,2},{19,3},{4,20},{5,... | collective-permute-start | bytes 1179656 | tf_op jit(solution)/shard_map/ppermute | solution.py:329
  5.6 15.6 %collective-permute-start.1 = (bf16[528,128]{1,0:T(8,128)(2,1)S(1)}, bf16[528,128]{1,0:T(8,128)(2,1)S(1)}, u32[]{:S(2)}, u32[]{:S(2)}) collective-permute-start(bf16[528,128]{1,0:T(8,128)(2,1)S(1)} %get-tuple-element.15), channel_id=1, source_target_pairs={{0,3},{1,2},{2,1},{3,0},{16,19},{17,18},{18,17},{19,16},{4,7},{5,6... | collective-permute-start | bytes 405512 | tf_op jit(solution)/shard_map/ppermute | solution.py:329
  9.3 13.0 %collective-permute-start.2 = (bf16[528,128]{1,0:T(8,128)(2,1)S(1)}, bf16[528,128]{1,0:T(8,128)(2,1)S(1)}, u32[]{:S(2)}, u32[]{:S(2)}) collective-permute-start(bf16[528,128]{1,0:T(8,128)(2,1)S(1)} %get-tuple-element.16), channel_id=1, source_target_pairs={{0,1},{1,0},{2,3},{3,2},{16,17},{17,16},{18,19},{19,18},{4,5},{5,4... | collective-permute-start | bytes 405512 | tf_op jit(solution)/shard_map/ppermute | solution.py:329
  9.3 13.5 %collective-permute-start.3 = (bf16[528,128]{1,0:T(8,128)(2,1)S(1)}, bf16[528,128]{1,0:T(8,128)(2,1)S(1)}, u32[]{:S(2)}, u32[]{:S(2)}) collective-permute-start(bf16[528,128]{1,0:T(8,128)(2,1)S(1)} %get-tuple-element.17), channel_id=1, source_target_pairs={{0,19},{1,18},{2,17},{3,16},{16,3},{17,2},{18,1},{19,0},{4,23},{5,... | collective-permute-start | bytes 405512 | tf_op jit(solution)/shard_map/ppermute | solution.py:329
  10.1 12.7 %collective-permute-start.4 = (bf16[528,128]{1,0:T(8,128)(2,1)S(1)}, bf16[528,128]{1,0:T(8,128)(2,1)S(1)}, u32[]{:S(2)}, u32[]{:S(2)}) collective-permute-start(bf16[528,128]{1,0:T(8,128)(2,1)S(1)} %get-tuple-element.18), channel_id=1, source_target_pairs={{0,17},{1,16},{2,19},{3,18},{16,1},{17,0},{18,3},{19,2},{4,21},{5,... | collective-permute-start | bytes 405512 | tf_op jit(solution)/shard_map/ppermute | solution.py:329
  15.7 19.5 %copy-start.2 = (bf16[1,1,768,1024]{3,2,1,0:T(8,128)(2,1)S(1)}, bf16[1,1,768,1024]{3,2,1,0:T(8,128)(2,1)}, u32[]{:S(2)}) copy-start(bf16[1,1,768,1024]{3,2,1,0:T(8,128)(2,1)} %param.13) | copy-start | bytes 4718596
  17.7 13.0 %collective-permute-start.5 = (bf16[528,128]{1,0:T(8,128)(2,1)S(1)}, bf16[528,128]{1,0:T(8,128)(2,1)S(1)}, u32[]{:S(2)}, u32[]{:S(2)}) collective-permute-start(bf16[528,128]{1,0:T(8,128)(2,1)S(1)} %get-tuple-element.21), channel_id=1, source_target_pairs={{0,2},{1,3},{2,0},{3,1},{16,18},{17,19},{18,16},{19,17},{4,6},{5,7... | collective-permute-start | bytes 405512 | tf_op jit(solution)/shard_map/ppermute | solution.py:329
  21.2 12.1 %collective-permute-start.6 = (bf16[528,128]{1,0:T(8,128)(2,1)S(1)}, bf16[528,128]{1,0:T(8,128)(2,1)S(1)}, u32[]{:S(2)}, u32[]{:S(2)}) collective-permute-start(bf16[528,128]{1,0:T(8,128)(2,1)S(1)} %get-tuple-element.22), channel_id=1, source_target_pairs={{0,18},{1,19},{2,16},{3,17},{16,2},{17,3},{18,0},{19,1},{4,22},{5,... | collective-permute-start | bytes 405512 | tf_op jit(solution)/shard_map/ppermute | solution.py:329
  22.2 12.9 %copy-start = (f32[1,1,768,1024]{3,2,1,0:T(8,128)S(1)}, f32[1,1,768,1024]{3,2,1,0:T(8,128)}, u32[]{:S(2)}) copy-start(f32[1,1,768,1024]{3,2,1,0:T(8,128)} %param.11) | copy-start | bytes 9437188
  22.2 12.9 %copy-start.1 = (bf16[1,1,768,1024]{3,2,1,0:T(8,128)(2,1)S(1)}, bf16[1,1,768,1024]{3,2,1,0:T(8,128)(2,1)}, u32[]{:S(2)}) copy-start(bf16[1,1,768,1024]{3,2,1,0:T(8,128)(2,1)} %param.12) | copy-start | bytes 4718596
  22.3 11.1 %collective-permute-start.7 = (bf16[528,128]{1,0:T(8,128)(2,1)S(1)}, bf16[528,128]{1,0:T(8,128)(2,1)S(1)}, u32[]{:S(2)}, u32[]{:S(2)}) collective-permute-start(bf16[528,128]{1,0:T(8,128)(2,1)S(1)} %get-tuple-element.23), channel_id=1, source_target_pairs={{0,16},{1,17},{2,18},{3,19},{16,0},{17,1},{18,2},{19,3},{4,20},{5,... | collective-permute-start | bytes 405512 | tf_op jit(solution)/shard_map/ppermute | solution.py:329
  23.0 5.8 %collective-permute-start.9 = (f32[8,128]{1,0:T(8,128)S(1)}, f32[8,128]{1,0:T(8,128)S(1)}, u32[]{:S(2)}, u32[]{:S(2)}) collective-permute-start(f32[8,128]{1,0:T(8,128)S(1)} %score.2), channel_id=1, source_target_pairs={{0,3},{1,2},{2,1},{3,0},{16,19},{17,18},{18,17},{19,16},{4,7},{5,6... | collective-permute-start | bytes 12296 | tf_op jit(solution)/shard_map/ppermute | solution.py:329
  26.6 4.0 %collective-permute-start.8 = (f32[8,128]{1,0:T(8,128)S(1)}, f32[8,128]{1,0:T(8,128)S(1)}, u32[]{:S(2)}, u32[]{:S(2)}) collective-permute-start(f32[8,128]{1,0:T(8,128)S(1)} %score.2), channel_id=1, source_target_pairs={{0,1},{1,0},{2,3},{3,2},{16,17},{17,16},{18,19},{19,18},{4,5},{5,4... | collective-permute-start | bytes 12296 | tf_op jit(solution)/shard_map/ppermute | solution.py:329
  33.5 4.6 %collective-permute-start.10 = (f32[8,128]{1,0:T(8,128)S(1)}, f32[8,128]{1,0:T(8,128)S(1)}, u32[]{:S(2)}, u32[]{:S(2)}) collective-permute-start(f32[8,128]{1,0:T(8,128)S(1)} %score.3.local_ref), channel_id=1, source_target_pairs={{0,2},{1,3},{2,0},{3,1},{16,18},{17,19},{18,16},{19,17},{4,6},{5,7... | collective-permute-start | bytes 12296 | tf_op jit(solution)/shard_map/ppermute | solution.py:329
  38.1 3.7 %collective-permute-start.11 = (f32[8,128]{1,0:T(8,128)S(1)}, f32[8,128]{1,0:T(8,128)S(1)}, u32[]{:S(2)}, u32[]{:S(2)}) collective-permute-start(f32[8,128]{1,0:T(8,128)S(1)} %merge.1.refs_8_.own_ref), channel_id=1, source_target_pairs={{0,16},{1,17},{2,18},{3,19},{16,0},{17,1},{18,2},{19,3},{4,20},{5,... | collective-permute-start | bytes 12296 | tf_op jit(solution)/shard_map/ppermute | solution.py:329
  38.7 3.1 %copy-start.4 = (s32[1,512,8]{1,2,0:T(8,128)S(1)}, s32[1,512,8]{1,2,0:T(8,128)}, u32[]{:S(2)}) copy-start(s32[1,512,8]{1,2,0:T(8,128)} %param.9) | copy-start | bytes 49156

commit v10 on v9

--- a/solution.py
+++ b/solution.py
@@ -132,31 +132,30 @@
     fill_chunks(steps, cap, picks, held, copies, tiles, chunks)
 
 
-def later_kernel(items, steps, cap, slots_ref, tiles_ref, grads_hbm, _, *rest):
+def later_kernel(
+    items, steps, cap, slots_ref, tiles_ref, grads_hbm, own_ref, other_ref, master_hbm, inner_ref, *rest
+):
     chunks = dict(zip(items, rest))
-    held, sems = rest[len(items) :]
+    held, master_ref, sems = rest[len(items) :]
     copies = start_grads(grads_hbm, held, sems)
-    slots = slots_ref[...]
-    picks = {k: pick_rows(slots, k, cap) for k in steps}
-    fill_chunks(steps, cap, picks, held, copies, tiles_ref, chunks)
-
-
-def inner_kernel(own_ref, other_ref, master_hbm, inner_ref, master_ref, sems):
     half = master_ref.shape[1]
     step = min(half, 4 * LANES)
     parts = [slice(column, column + step) for column in range(0, half, step)]
     loads = [
-        pltpu.make_async_copy(master_hbm.at[:, part], master_ref.at[:, part], sems.at[at])
+        pltpu.make_async_copy(master_hbm.at[:, part], master_ref.at[:, part], sems.at[2 + at])
         for at, part in enumerate(parts)
     ]
     for load in loads:
         load.start()
-    slots = own_ref.shape[1]
+    slots = slots_ref[...]
+    picks = {k: pick_rows(slots, k, cap) for k in steps}
+    fill_chunks(steps, cap, picks, held, copies, tiles_ref, chunks)
+    slot_count = own_ref.shape[1]
     for load, part in zip(loads, parts):
         load.wait()
         weights = master_ref[:, part].astype(BF16)
-        for at, ref in ((0, own_ref), (slots, other_ref)):
-            inner_ref[at : at + slots, part] = lax.dot_general(
+        for at, ref in ((0, own_ref), (slot_count, other_ref)):
+            inner_ref[at : at + slot_count, part] = lax.dot_general(
                 ref[...], weights, (((0,), (0,)), ((), ())), preferred_element_type=F32
             )
 
@@ -201,12 +200,12 @@
     score_chunks(steps, group, cap, dict(zip(items, rest)), inner_ref, score_ref)
 
 
-def merge_kernel(group, local_ref, *rest):
-    out_ref = rest[-1]
+def merge_kernel(steps, *rest):
+    refs, out_ref = rest[:-1], rest[-1]
     row = lax.broadcasted_iota(jnp.int32, out_ref.shape, 0)
     me = ep_index()
     table = jnp.zeros(out_ref.shape, F32)
-    for k, ref in enumerate((local_ref,) + rest[:-1]):
+    for k, ref in zip(steps, refs):
         line = jnp.sum(jnp.where(row == me, ref[...], 0.0), axis=0, keepdims=True)
         table = jnp.where(row == k, line, table)
     out_ref[...] = table
@@ -268,45 +267,41 @@
         finished(at)
 
 
-def first_update_kernel(blocks, items, group, cap, *refs):
-    chunks, operands = dict(zip(items, refs)), refs[len(items) : len(items) + 5]
-    update, rows, scales_ref, scaled, total = refs[len(items) + 5 :]
+def update_kernel(items, group, cap, own_ref, other_ref, master_ref, moment_ref, second_ref, *rest):
+    chunks = dict(zip(items, rest))
+    _, update_hbm, rows, scales_ref, scaled, total, update, sems = rest[len(items) :]
+    hid, block = update.shape[0], total.shape[1]
+    blocks = [slice(top, top + block) for top in range(0, hid, block)]
     scales = place_chunks(items, group, cap, chunks, rows)
     for side in range(2):
         scales_ref[side] = scales[side]
-    operands = operands[:2] + (rows, scales_ref) + operands[2:]
-    update_rows(blocks, operands, scaled, total, update, lambda at: None)
-
-
-def last_update_kernel(blocks, *refs):
-    earlier, _, update_hbm, scaled, total, update, sems = refs[7:]
-    above = earlier.shape[0]
-    copies = [
-        pltpu.make_async_copy(earlier, update_hbm.at[:above, :], sems.at[len(blocks)])
-    ]
-    copies[0].start()
+    copies = []
 
     def finished(at):
-        block = blocks[at]
         copies.append(
             pltpu.make_async_copy(
-                update.at[block.start - above : block.stop - above, :],
-                update_hbm.at[block, :],
-                sems.at[at],
+                update.at[blocks[at], :], update_hbm.at[blocks[at], :], sems.at[at]
             )
         )
         copies[-1].start()
 
-    update_rows(blocks, refs[:7], scaled, total, update, finished)
+    operands = (own_ref, other_ref, rows, scales_ref, master_ref, moment_ref, second_ref)
+    update_rows(blocks, operands, scaled, total, update, finished)
     for copy in copies:
         copy.wait()
 
 
-def combine_kernel(group, cap, ids_ref, slots_ref, own_ref, other_ref, out_ref):
+def combine_kernel(
+    far, group, cap, ids_ref, slots_ref, own_ref, other_ref, own_far_ref, other_far_ref, out_ref
+):
     tokens = ids_ref.shape[1]
     me = ep_index()
     lane = lax.broadcasted_iota(jnp.int32, own_ref.shape, 1)
+    row = lax.broadcasted_iota(jnp.int32, own_ref.shape, 0)
     lines = jnp.where(lane < cap, own_ref[...], other_ref[...])
+    last = jnp.where(lane < cap, own_far_ref[...], other_far_ref[...])
+    last = jnp.sum(jnp.where(row == me, last, 0.0), axis=0, keepdims=True)
+    lines = jnp.where(row == far, last, lines)
     rest = jnp.zeros((LANES - lines.shape[0], LANES), F32)
     columns = jnp.concatenate([lines, rest], axis=0).T
     columns = columns[:cap] + columns[cap : 2 * cap]
@@ -342,16 +337,16 @@
     other_hidden = moved(own_hidden, 1, 0)
 
     far = group // 2
-    early = [k for k in range(1, group) if k != far]
+    first = [k for k in range(1, group) if k != far]
     late = [0, far]
-    first_items = [(side, k) for side in range(2) for k in reversed(early)]
-    last_items = [(0, far), (1, far), (1, 0), (0, 0)]
+    first_items = [(side, k) for side in range(2) for k in reversed(first)]
+    last_items = [(0, far), (1, 0), (1, far), (0, 0)]
     order = first_items + last_items
     chunk = jax.ShapeDtypeStruct((half // LANES * cap + TILE, LANES), BF16)
     grads = pltpu.with_memory_space_constraint(grad_out[0], pltpu.HBM)
     held = pltpu.VMEM((2, tokens, half), BF16)
     routed = pl.pallas_call(
-        functools.partial(route_kernel, first_items, early, group, cap),
+        functools.partial(route_kernel, first_items, first, group, cap),
         out_shape=[
             jax.ShapeDtypeStruct((group + -group % TILE, tokens), F32),
             jax.ShapeDtypeStruct((group, TILE, LANES), BF16),
@@ -376,102 +371,98 @@
     slot_of, tiles = routed[:2]
     arrived = {item: moved(sent, *item) for item, sent in zip(first_items, routed[2:])}
 
-    inner = pl.pallas_call(
-        inner_kernel,
-        out_shape=jax.ShapeDtypeStruct((2 * slots, half), F32),
-        in_specs=specs(pltpu.VMEM, 2) + specs(pltpu.HBM, 1),
-        out_specs=specs(pltpu.VMEM, 1)[0],
+    routed = pl.pallas_call(
+        functools.partial(later_kernel, last_items, late, cap),
+        out_shape=[jax.ShapeDtypeStruct((2 * slots, half), F32)] + [chunk] * len(last_items),
+        in_specs=specs(pltpu.VMEM, 2)
+        + specs(pltpu.HBM, 1)
+        + specs(pltpu.VMEM, 2)
+        + specs(pltpu.HBM, 1),
+        out_specs=specs(pltpu.VMEM, 1 + len(last_items)),
         scratch_shapes=[
+            held,
             pltpu.VMEM((hid, half), F32),
-            pltpu.SemaphoreType.DMA((half // min(half, 4 * LANES),)),
+            pltpu.SemaphoreType.DMA((2 + half // min(half, 4 * LANES),)),
         ],
         compiler_params=params(),
-        cost_estimate=cost(4 * slots * hid * half, 4 * hid * half + 8 * slots * half),
-        name="inner",
-    )(own_hidden, other_hidden, pltpu.with_memory_space_constraint(param, pltpu.HBM))
-
-    routed = pl.pallas_call(
-        functools.partial(later_kernel, last_items, late, cap),
-        out_shape=[chunk] * len(last_items),
-        in_specs=specs(pltpu.VMEM, 2) + specs(pltpu.HBM, 1) + specs(pl.ANY, 1),
-        out_specs=specs(pltpu.VMEM, len(last_items)),
-        scratch_shapes=[held, pltpu.SemaphoreType.DMA((2,))],
-        compiler_params=params(),
-        cost_estimate=cost(2 * slots * tokens * width, 2 * (tokens + slots) * width),
+        cost_estimate=cost(
+            2 * slots * tokens * width + 4 * slots * hid * half, 2 * (tokens + slots) * width
+        ),
         name="later",
-    )(slot_of, tiles, grads, inner)
-    arrived |= {item: moved(sent, *item) for item, sent in zip(last_items, routed)}
+    )(
+        slot_of,
+        tiles,
+        grads,
+        own_hidden,
+        other_hidden,
+        pltpu.with_memory_space_constraint(param, pltpu.HBM),
+    )
+    inner = routed[0]
+    arrived |= {item: moved(sent, *item) for item, sent in zip(last_items, routed[1:])}
 
     tile = jax.ShapeDtypeStruct((group + -group % 8, LANES), F32)
-    returned = {}
-    for items, steps in ((first_items, early), (last_items, late)):
-        done = list(returned.values())
-        scores = pl.pallas_call(
+
+    def scored(steps, *after):
+        items = [(side, k) for side in range(2) for k in steps]
+        return pl.pallas_call(
             functools.partial(score_kernel, items, steps, group, cap),
             out_shape=tile,
-            in_specs=specs(pltpu.VMEM, 1 + len(items)) + specs(pl.ANY, len(done)),
+            in_specs=specs(pltpu.VMEM, 1 + len(items)) + specs(pl.ANY, len(after)),
             out_specs=specs(pltpu.VMEM, 1)[0],
             compiler_params=params(),
             cost_estimate=cost(2 * len(items) * cap * half, 6 * len(items) * cap * half),
             name="score",
-        )(inner, *[arrived[item] for item in items], *done)
-        for k in steps:
-            returned[k] = moved(scores, 0, k)
-
-    block = min(hid, 2 * LANES)
-    blocks = [slice(top, top + block) for top in range(0, hid, block)]
-    above = blocks[-1].start
-    inputs = (param, moment[0, 0], second[0, 0])
-    scratch = [
-        pltpu.VMEM((2, block, 2 * slots), BF16),
-        pltpu.VMEM((2, block, half), F32),
-    ]
-    earlier, placed, scales = pl.pallas_call(
-        functools.partial(first_update_kernel, blocks[:-1], order, group, cap),
-        out_shape=[
-            jax.ShapeDtypeStruct((above, half), F32),
-            jax.ShapeDtypeStruct((2 * slots, half), BF16),
-            jax.ShapeDtypeStruct((2, TILE, LANES), F32),
-        ],
-        in_specs=specs(pltpu.VMEM, len(order) + 5),
-        out_specs=specs(pltpu.VMEM, 3),
-        scratch_shapes=scratch,
-        compiler_params=params(),
-        cost_estimate=cost(4 * slots * above * half, 12 * above * half),
-        name="first_update",
-    )(*[arrived[item] for item in order], own_hidden, other_hidden, *inputs)
+        )(inner, *[arrived[item] for item in items], *after)
+
+    early = [0] + first
+    early_scores = scored(early)
     own_scores = pl.pallas_call(
-        functools.partial(merge_kernel, group),
+        functools.partial(merge_kernel, early),
         out_shape=tile,
-        in_specs=specs(pltpu.VMEM, group),
+        in_specs=specs(pltpu.VMEM, len(early)),
         out_specs=specs(pltpu.VMEM, 1)[0],
         compiler_params=params(),
         name="merge",
-    )(*[returned[k] for k in range(group)])
+    )(*[moved(early_scores, 0, k) for k in early])
     other_scores = moved(own_scores, 1, 0)
+    late_scores = scored([far], own_scores)
+    far_scores = [moved(late_scores, side, far) for side in range(2)]
+
+    block = min(hid, 2 * LANES)
     update = pl.pallas_call(
-        functools.partial(last_update_kernel, blocks[-1:]),
+        functools.partial(update_kernel, order, group, cap),
         out_shape=jax.ShapeDtypeStruct((hid, half), F32),
-        in_specs=specs(pltpu.VMEM, 8) + specs(pl.ANY, 1),
+        in_specs=specs(pltpu.VMEM, 5 + len(order)) + specs(pl.ANY, 1),
         out_specs=specs(pltpu.HBM, 1)[0],
-        scratch_shapes=scratch
-        + [
-            pltpu.VMEM((hid - above, half), F32),
-            pltpu.SemaphoreType.DMA((2,)),
+        scratch_shapes=[
+            pltpu.VMEM((2 * slots, half), BF16),
+            pltpu.VMEM((2, TILE, LANES), F32),
+            pltpu.VMEM((2, block, 2 * slots), BF16),
+            pltpu.VMEM((2, block, half), F32),
+            pltpu.VMEM((hid, half), F32),
+            pltpu.SemaphoreType.DMA((hid // block,)),
         ],
         compiler_params=params(),
-        cost_estimate=cost(4 * slots * (hid - above) * half, 12 * hid * half),
-        name="last_update",
-    )(own_hidden, other_hidden, placed, scales, *inputs, earlier, own_scores)
+        cost_estimate=cost(4 * slots * hid * half, 12 * hid * half),
+        name="update",
+    )(
+        own_hidden,
+        other_hidden,
+        param,
+        moment[0, 0],
+        second[0, 0],
+        *[arrived[item] for item in order],
+        late_scores,
+    )
     router = pl.pallas_call(
-        functools.partial(combine_kernel, group, cap),
+        functools.partial(combine_kernel, far, group, cap),
         out_shape=jax.ShapeDtypeStruct((top, tokens), F32),
-        in_specs=specs(pltpu.VMEM, 4),
+        in_specs=specs(pltpu.VMEM, 6),
         out_specs=specs(pltpu.VMEM, 1)[0],
         compiler_params=params(),
         cost_estimate=cost(4 * slots * tokens, 8 * top * tokens),
         name="combine",
-    )(ids, slot_of, own_scores, other_scores)
+    )(ids, slot_of, own_scores, other_scores, *far_scores)
     return (update[None, None], router.T[None])
 
 

time: 42.8 us -> 42.2 us (0.986)
  starting transfers between devices: 19.9 us -> 22.9 us
  waiting for transfers between devices: 10.7 us -> 8.23 us
  Pallas kernels: 11.3 us -> 10.1 us
    ppermute x12 -> x13, starting transfers between devices: 19.9 us -> 22.9 us  [moved(): return lax.ppermute(array, ('pair', 'ep'), pairs)]
    pallas_call x8 -> x6, Pallas kernels: 9.33 us -> 6.7 us  [the longest x1 3.5 us: local(): pl.pallas_call(functools.partial(update_kernel, order, group, cap), out_s...]
    ppermute x12 -> x13, waiting for transfers between devices: 10.7 us -> 8.23 us  [moved(): return lax.ppermute(array, ('pair', 'ep'), pairs)]
    pallas_call x1, Pallas kernels: 2 us -> 3.41 us  [local(): pl.pallas_call(functools.partial(later_kernel, last_items, late, cap), ou...]
  transfers between devices with their start and end apart: 12 -> 13, of which waited for: 6 -> 6; matrix products, arithmetic and copies ran while one was open for 0% -> 0% of each run, Pallas kernels for 24% -> 22%
where the time goes in v10:
time: 42.2 us; the launch traced here: 42 us
  starting transfers between devices  22.9 us (54%)
  Pallas kernels  10.1 us (24%)
  waiting for transfers between devices  8.23 us (20%)
  between operations  0.72 us (2%)
    ppermute x13, starting transfers between devices, moved(): return lax.ppermute(array, ('pair', 'ep'), pairs)  22.9 us
    ppermute x13, waiting for transfers between devices, moved(): return lax.ppermute(array, ('pair', 'ep'), pairs)  8.23 us
    pallas_call x1, Pallas kernels, local(): pl.pallas_call(functools.partial(update_kernel, order, group, cap), out_s...  3.5 us
    pallas_call x1, Pallas kernels, local(): pl.pallas_call(functools.partial(later_kernel, last_items, late, cap), ou...  3.41 us
    pallas_call x1, Pallas kernels, local(): pl.pallas_call(functools.partial(route_kernel, first_items, first, group,...  1.94 us
    pallas_call x1, Pallas kernels, local(): pl.pallas_call(functools.partial(combine_kernel, far, group, cap), out_sh...  0.86 us
  transfers between devices with their start and end apart: 13, of which 6 were waited for; matrix products, arithmetic and copies ran while one was open for 0% of the time, Pallas kernels for 22%

profile of v10, /device:TPU:0, one launch (start us, length us, event | category | flops | bytes accessed | tf_op | source)
XLA Modules:
  0.0 42.0 jit_solution(13835292899317691305)
XLA Ops:
  0.6 3.0 %collective-permute-start = (bf16[768,256]{1,0:T(8,128)(2,1)}, bf16[768,256]{1,0:T(8,128)(2,1)S(1)}, u32[]{:S(2)}, u32[]{:S(2)}) collective-permute-start(bf16[768,256]{1,0:T(8,128)(2,1)} %bitcast.17), channel_id=1, source_target_pairs={{0,16},{1,17},{2,18},{3,19},{16,0},{17,1},{18,2},{19,3},{4,20},{5,... | collective-permute-start | bytes 1179656 | tf_op jit(solution)/shard_map/ppermute | solution.py:324
  3.7 1.9 %route.1 = (f32[16,512]{1,0:T(8,128)S(1)}, bf16[4,16,128]{2,1,0:T(8,128)(2,1)S(1)}, bf16[528,128]{1,0:T(8,128)(2,1)S(1)}, bf16[528,128]{1,0:T(8,128)(2,1)S(1)}, ...) custom-call(s32[8,512]{1,0:T(8,128)} %bitcast.22, bf16[8,512]{1,0:T(8,128)(2,1)} %bitcast.28, ...), custom_call_target="tpu_custom_call" | custom-call | flops 536870912 | bytes 3145728 | tf_op jit(solution)/shard_map/route/pallas_call | solution.py:348
  5.6 3.7 %collective-permute-start.1 = (bf16[528,128]{1,0:T(8,128)(2,1)S(1)}, bf16[528,128]{1,0:T(8,128)(2,1)S(1)}, u32[]{:S(2)}, u32[]{:S(2)}) collective-permute-start(bf16[528,128]{1,0:T(8,128)(2,1)S(1)} %get-tuple-element.13), channel_id=1, source_target_pairs={{0,3},{1,2},{2,1},{3,0},{16,19},{17,18},{18,17},{19,16},{4,7},{5,6... | collective-permute-start | bytes 405512 | tf_op jit(solution)/shard_map/ppermute | solution.py:324
  9.3 0.8 %collective-permute-start.3 = (bf16[528,128]{1,0:T(8,128)(2,1)S(1)}, bf16[528,128]{1,0:T(8,128)(2,1)S(1)}, u32[]{:S(2)}, u32[]{:S(2)}) collective-permute-start(bf16[528,128]{1,0:T(8,128)(2,1)S(1)} %get-tuple-element.15), channel_id=1, source_target_pairs={{0,19},{1,18},{2,17},{3,16},{16,3},{17,2},{18,1},{19,0},{4,23},{5,... | collective-permute-start | bytes 405512 | tf_op jit(solution)/shard_map/ppermute | solution.py:324
  10.1 1.4 %collective-permute-start.4 = (bf16[528,128]{1,0:T(8,128)(2,1)S(1)}, bf16[528,128]{1,0:T(8,128)(2,1)S(1)}, u32[]{:S(2)}, u32[]{:S(2)}) collective-permute-start(bf16[528,128]{1,0:T(8,128)(2,1)S(1)} %get-tuple-element.16), channel_id=1, source_target_pairs={{0,17},{1,16},{2,19},{3,18},{16,1},{17,0},{18,3},{19,2},{4,21},{5,... | collective-permute-start | bytes 405512 | tf_op jit(solution)/shard_map/ppermute | solution.py:324
  11.5 1.5 %collective-permute-done.other_ref = bf16[768,256]{1,0:T(8,128)(2,1)S(1)} collective-permute-done((bf16[768,256]{1,0:T(8,128)(2,1)}, bf16[768,256]{1,0:T(8,128)(2,1)S(1)}, u32[]{:S(2)}, u32[]{:S(2)}) %collective-permute-start) | collective-permute-done | bytes 393248 | tf_op jit(solution)/shard_map/ppermute | solution.py:324
  13.0 3.4 %later.1 = (f32[512,1024]{1,0:T(8,128)S(1)}, bf16[528,128]{1,0:T(8,128)(2,1)S(1)}, bf16[528,128]{1,0:T(8,128)(2,1)S(1)}, bf16[528,128]{1,0:T(8,128)(2,1)S(1)}, bf16[528,128]{1,0:T(8,128)(2,1)S(1)}) custom-call(f32[16,512]{1,0:T(8,128)S(1)} %get-tuple-element.17.slots_ref, bf16[4,16,128]{2,1,0:T(8,128)(2,1)S(1)} %get-tuple-element.18.tiles_ref, ...), custom_call_target="tpu_custom_call" | custom-call | flops 1342177280 | bytes 3145728 | tf_op jit(solution)/shard_map/later/pallas_call | solution.py:374
  16.4 1.8 %collective-permute-start.6 = (bf16[528,128]{1,0:T(8,128)(2,1)S(1)}, bf16[528,128]{1,0:T(8,128)(2,1)S(1)}, u32[]{:S(2)}, u32[]{:S(2)}) collective-permute-start(bf16[528,128]{1,0:T(8,128)(2,1)S(1)} %get-tuple-element.20), channel_id=1, source_target_pairs={{0,16},{1,17},{2,18},{3,19},{16,0},{17,1},{18,2},{19,3},{4,20},{5,... | collective-permute-start | bytes 405512 | tf_op jit(solution)/shard_map/ppermute | solution.py:324
  18.2 0.0 collective-permute-done.1.rest_2_.rest_0_
  18.2 3.2 %collective-permute-start.5 = (bf16[528,128]{1,0:T(8,128)(2,1)S(1)}, bf16[528,128]{1,0:T(8,128)(2,1)S(1)}, u32[]{:S(2)}, u32[]{:S(2)}) collective-permute-start(bf16[528,128]{1,0:T(8,128)(2,1)S(1)} %get-tuple-element.19), channel_id=1, source_target_pairs={{0,2},{1,3},{2,0},{3,1},{16,18},{17,19},{18,16},{19,17},{4,6},{5,7... | collective-permute-start | bytes 405512 | tf_op jit(solution)/shard_map/ppermute | solution.py:324
  21.5 1.0 %collective-permute-done.4.rest_4_.rest_3_ = bf16[528,128]{1,0:T(8,128)(2,1)S(1)} collective-permute-done((bf16[528,128]{1,0:T(8,128)(2,1)S(1)}, bf16[528,128]{1,0:T(8,128)(2,1)S(1)}, u32[]{:S(2)}, u32[]{:S(2)}) %collective-permute-start.4) | collective-permute-done | bytes 135200 | tf_op jit(solution)/shard_map/ppermute | solution.py:324
  22.5 1.8 %collective-permute-done.6.rest_3_.rest_5_ = bf16[528,128]{1,0:T(8,128)(2,1)S(1)} collective-permute-done((bf16[528,128]{1,0:T(8,128)(2,1)S(1)}, bf16[528,128]{1,0:T(8,128)(2,1)S(1)}, u32[]{:S(2)}, u32[]{:S(2)}) %collective-permute-start.6) | collective-permute-done | bytes 135200 | tf_op jit(solution)/shard_map/ppermute | solution.py:324
  24.3 0.3 score.2.rest_0_
  24.6 1.7 %collective-permute-start.9 = (f32[8,128]{1,0:T(8,128)S(1)}, f32[8,128]{1,0:T(8,128)S(1)}, u32[]{:S(2)}, u32[]{:S(2)}) collective-permute-start(f32[8,128]{1,0:T(8,128)S(1)} %score.2.rest_0_), channel_id=1, source_target_pairs={{0,3},{1,2},{2,1},{3,0},{16,19},{17,18},{18,17},{19,16},{4,7},{5,6... | collective-permute-start | bytes 12296 | tf_op jit(solution)/shard_map/ppermute | solution.py:324
  26.3 1.0 %collective-permute-start.8 = (f32[8,128]{1,0:T(8,128)S(1)}, f32[8,128]{1,0:T(8,128)S(1)}, u32[]{:S(2)}, u32[]{:S(2)}) collective-permute-start(f32[8,128]{1,0:T(8,128)S(1)} %score.2.rest_0_), channel_id=1, source_target_pairs={{0,1},{1,0},{2,3},{3,2},{16,17},{17,16},{18,19},{19,18},{4,5},{5,4... | collective-permute-start | bytes 12296 | tf_op jit(solution)/shard_map/ppermute | solution.py:324
  27.3 2.9 %collective-permute-done.9.rest_2_ = f32[8,128]{1,0:T(8,128)S(1)} collective-permute-done((f32[8,128]{1,0:T(8,128)S(1)}, f32[8,128]{1,0:T(8,128)S(1)}, u32[]{:S(2)}, u32[]{:S(2)}) %collective-permute-start.9) | collective-permute-done | bytes 4128 | tf_op jit(solution)/shard_map/ppermute | solution.py:324
  30.2 0.1 collective-permute-done.8.rest_1_
  30.3 2.5 %collective-permute-start.10 = (f32[8,128]{1,0:T(8,128)S(1)}, f32[8,128]{1,0:T(8,128)S(1)}, u32[]{:S(2)}, u32[]{:S(2)}) collective-permute-start(f32[8,128]{1,0:T(8,128)S(1)} %merge.1.rest_2_.own_ref), channel_id=1, source_target_pairs={{0,16},{1,17},{2,18},{3,19},{16,0},{17,1},{18,2},{19,3},{4,20},{5,... | collective-permute-start | bytes 12296 | tf_op jit(solution)/shard_map/ppermute | solution.py:324
  32.8 0.1 score.3.rest_8_
  32.9 3.7 %collective-permute-start.12 = (f32[8,128]{1,0:T(8,128)S(1)}, f32[8,128]{1,0:T(8,128)S(1)}, u32[]{:S(2)}, u32[]{:S(2)}) collective-permute-start(f32[8,128]{1,0:T(8,128)S(1)} %score.3.rest_8_), channel_id=1, source_target_pairs={{0,18},{1,19},{2,16},{3,17},{16,2},{17,3},{18,0},{19,1},{4,22},{5,... | collective-permute-start | bytes 12296 | tf_op jit(solution)/shard_map/ppermute | solution.py:324
  36.7 0.0 copy-start.4
  36.7 3.5 %update.1 = f32[768,1024]{1,0:T(8,128)} custom-call(bf16[768,256]{1,0:T(8,128)(2,1)S(1)} %bitcast.19, bf16[768,256]{1,0:T(8,128)(2,1)S(1)} %collective-permute-done.other_ref, f32[768,1024]{1,0:T(8,128)S(1)} %bitcast.16, bf16[768,1024]{1,0:T(8,128)(2,1)S(1)} %bitcast.20, bf16[768,1024]{1,0:T(8,128)(2,1)S(1)} %bitcast.21, ...), custom_call_target="tpu_custom_call" | custom-call | flops 805306368 | bytes 9437184 | tf_op jit(solution)/shard_map/update/pallas_call | solution.py:432
  40.2 0.9 %collective-permute-done.11.own_far_ref = f32[8,128]{1,0:T(8,128)S(1)} collective-permute-done((f32[8,128]{1,0:T(8,128)S(1)}, f32[8,128]{1,0:T(8,128)S(1)}, u32[]{:S(2)}, u32[]{:S(2)}) %collective-permute-start.11) | collective-permute-done | bytes 4128 | tf_op jit(solution)/shard_map/ppermute | solution.py:324
  41.1 0.9 %combine.1 = f32[8,512]{1,0:T(8,128)} custom-call(s32[8,512]{1,0:T(8,128)S(1)} %bitcast.23, f32[16,512]{1,0:T(8,128)S(1)} %get-tuple-element.17.slots_ref, f32[8,128]{1,0:T(8,128)S(1)} %merge.1.rest_2_.own_ref, f32[8,128]{1,0:T(8,128)S(1)} %collective-permute-done.10.other_ref, f32[8,128]{1,0:T(8,128)S(1)} %collective-permute-done.11.own_far_ref, ...), custom_call_target="tpu_custom_call" | custom-call | flops 524288 | bytes 32768 | tf_op jit(solution)/shard_map/combine/pallas_call | solution.py:457
  (19 shorter events, 0.1 us)
Async XLA Ops:
  0.6 12.4 %copy-start.1 = (bf16[1,1,768,256]{3,2,1,0:T(8,128)(2,1)S(1)}, bf16[1,1,768,256]{3,2,1,0:T(8,128)(2,1)}, u32[]{:S(2)}) copy-start(bf16[1,1,768,256]{3,2,1,0:T(8,128)(2,1)} %param.10) | copy-start | bytes 1179652
  0.6 12.4 %collective-permute-start = (bf16[768,256]{1,0:T(8,128)(2,1)}, bf16[768,256]{1,0:T(8,128)(2,1)S(1)}, u32[]{:S(2)}, u32[]{:S(2)}) collective-permute-start(bf16[768,256]{1,0:T(8,128)(2,1)} %bitcast.17), channel_id=1, source_target_pairs={{0,16},{1,17},{2,18},{3,19},{16,0},{17,1},{18,2},{19,3},{4,20},{5,... | collective-permute-start | bytes 1179656 | tf_op jit(solution)/shard_map/ppermute | solution.py:324
  5.6 12.6 %collective-permute-start.1 = (bf16[528,128]{1,0:T(8,128)(2,1)S(1)}, bf16[528,128]{1,0:T(8,128)(2,1)S(1)}, u32[]{:S(2)}, u32[]{:S(2)}) collective-permute-start(bf16[528,128]{1,0:T(8,128)(2,1)S(1)} %get-tuple-element.13), channel_id=1, source_target_pairs={{0,3},{1,2},{2,1},{3,0},{16,19},{17,18},{18,17},{19,16},{4,7},{5,6... | collective-permute-start | bytes 405512 | tf_op jit(solution)/shard_map/ppermute | solution.py:324
  9.3 12.2 %collective-permute-start.2 = (bf16[528,128]{1,0:T(8,128)(2,1)S(1)}, bf16[528,128]{1,0:T(8,128)(2,1)S(1)}, u32[]{:S(2)}, u32[]{:S(2)}) collective-permute-start(bf16[528,128]{1,0:T(8,128)(2,1)S(1)} %get-tuple-element.14), channel_id=1, source_target_pairs={{0,1},{1,0},{2,3},{3,2},{16,17},{17,16},{18,19},{19,18},{4,5},{5,4... | collective-permute-start | bytes 405512 | tf_op jit(solution)/shard_map/ppermute | solution.py:324
  9.3 12.2 %collective-permute-start.3 = (bf16[528,128]{1,0:T(8,128)(2,1)S(1)}, bf16[528,128]{1,0:T(8,128)(2,1)S(1)}, u32[]{:S(2)}, u32[]{:S(2)}) collective-permute-start(bf16[528,128]{1,0:T(8,128)(2,1)S(1)} %get-tuple-element.15), channel_id=1, source_target_pairs={{0,19},{1,18},{2,17},{3,16},{16,3},{17,2},{18,1},{19,0},{4,23},{5,... | collective-permute-start | bytes 405512 | tf_op jit(solution)/shard_map/ppermute | solution.py:324
  10.1 12.4 %collective-permute-start.4 = (bf16[528,128]{1,0:T(8,128)(2,1)S(1)}, bf16[528,128]{1,0:T(8,128)(2,1)S(1)}, u32[]{:S(2)}, u32[]{:S(2)}) collective-permute-start(bf16[528,128]{1,0:T(8,128)(2,1)S(1)} %get-tuple-element.16), channel_id=1, source_target_pairs={{0,17},{1,16},{2,19},{3,18},{16,1},{17,0},{18,3},{19,2},{4,21},{5,... | collective-permute-start | bytes 405512 | tf_op jit(solution)/shard_map/ppermute | solution.py:324
  13.0 23.6 %copy-start.3 = (bf16[1,1,768,1024]{3,2,1,0:T(8,128)(2,1)S(1)}, bf16[1,1,768,1024]{3,2,1,0:T(8,128)(2,1)}, u32[]{:S(2)}) copy-start(bf16[1,1,768,1024]{3,2,1,0:T(8,128)(2,1)} %param.13) | copy-start | bytes 4718596
  16.4 7.9 %collective-permute-start.6 = (bf16[528,128]{1,0:T(8,128)(2,1)S(1)}, bf16[528,128]{1,0:T(8,128)(2,1)S(1)}, u32[]{:S(2)}, u32[]{:S(2)}) collective-permute-start(bf16[528,128]{1,0:T(8,128)(2,1)S(1)} %get-tuple-element.20), channel_id=1, source_target_pairs={{0,16},{1,17},{2,18},{3,19},{16,0},{17,1},{18,2},{19,3},{4,20},{5,... | collective-permute-start | bytes 405512 | tf_op jit(solution)/shard_map/ppermute | solution.py:324
  18.2 14.5 %collective-permute-start.5 = (bf16[528,128]{1,0:T(8,128)(2,1)S(1)}, bf16[528,128]{1,0:T(8,128)(2,1)S(1)}, u32[]{:S(2)}, u32[]{:S(2)}) collective-permute-start(bf16[528,128]{1,0:T(8,128)(2,1)S(1)} %get-tuple-element.19), channel_id=1, source_target_pairs={{0,2},{1,3},{2,0},{3,1},{16,18},{17,19},{18,16},{19,17},{4,6},{5,7... | collective-permute-start | bytes 405512 | tf_op jit(solution)/shard_map/ppermute | solution.py:324
  21.5 11.3 %collective-permute-start.7 = (bf16[528,128]{1,0:T(8,128)(2,1)S(1)}, bf16[528,128]{1,0:T(8,128)(2,1)S(1)}, u32[]{:S(2)}, u32[]{:S(2)}) collective-permute-start(bf16[528,128]{1,0:T(8,128)(2,1)S(1)} %get-tuple-element.21), channel_id=1, source_target_pairs={{0,18},{1,19},{2,16},{3,17},{16,2},{17,3},{18,0},{19,1},{4,22},{5,... | collective-permute-start | bytes 405512 | tf_op jit(solution)/shard_map/ppermute | solution.py:324
  24.3 12.3 %copy-start = (f32[1,1,768,1024]{3,2,1,0:T(8,128)S(1)}, f32[1,1,768,1024]{3,2,1,0:T(8,128)}, u32[]{:S(2)}) copy-start(f32[1,1,768,1024]{3,2,1,0:T(8,128)} %param.11) | copy-start | bytes 9437188
  24.3 12.3 %copy-start.2 = (bf16[1,1,768,1024]{3,2,1,0:T(8,128)(2,1)S(1)}, bf16[1,1,768,1024]{3,2,1,0:T(8,128)(2,1)}, u32[]{:S(2)}) copy-start(bf16[1,1,768,1024]{3,2,1,0:T(8,128)(2,1)} %param.12) | copy-start | bytes 4718596
  24.6 5.6 %collective-permute-start.9 = (f32[8,128]{1,0:T(8,128)S(1)}, f32[8,128]{1,0:T(8,128)S(1)}, u32[]{:S(2)}, u32[]{:S(2)}) collective-permute-start(f32[8,128]{1,0:T(8,128)S(1)} %score.2.rest_0_), channel_id=1, source_target_pairs={{0,3},{1,2},{2,1},{3,0},{16,19},{17,18},{18,17},{19,16},{4,7},{5,6... | collective-permute-start | bytes 12296 | tf_op jit(solution)/shard_map/ppermute | solution.py:324
  26.3 4.0 %collective-permute-start.8 = (f32[8,128]{1,0:T(8,128)S(1)}, f32[8,128]{1,0:T(8,128)S(1)}, u32[]{:S(2)}, u32[]{:S(2)}) collective-permute-start(f32[8,128]{1,0:T(8,128)S(1)} %score.2.rest_0_), channel_id=1, source_target_pairs={{0,1},{1,0},{2,3},{3,2},{16,17},{17,16},{18,19},{19,18},{4,5},{5,4... | collective-permute-start | bytes 12296 | tf_op jit(solution)/shard_map/ppermute | solution.py:324
  30.3 9.9 %collective-permute-start.10 = (f32[8,128]{1,0:T(8,128)S(1)}, f32[8,128]{1,0:T(8,128)S(1)}, u32[]{:S(2)}, u32[]{:S(2)}) collective-permute-start(f32[8,128]{1,0:T(8,128)S(1)} %merge.1.rest_2_.own_ref), channel_id=1, source_target_pairs={{0,16},{1,17},{2,18},{3,19},{16,0},{17,1},{18,2},{19,3},{4,20},{5,... | collective-permute-start | bytes 12296 | tf_op jit(solution)/shard_map/ppermute | solution.py:324
  32.9 7.3 %collective-permute-start.12 = (f32[8,128]{1,0:T(8,128)S(1)}, f32[8,128]{1,0:T(8,128)S(1)}, u32[]{:S(2)}, u32[]{:S(2)}) collective-permute-start(f32[8,128]{1,0:T(8,128)S(1)} %score.3.rest_8_), channel_id=1, source_target_pairs={{0,18},{1,19},{2,16},{3,17},{16,2},{17,3},{18,0},{19,1},{4,22},{5,... | collective-permute-start | bytes 12296 | tf_op jit(solution)/shard_map/ppermute | solution.py:324
  36.6 4.5 %collective-permute-start.11 = (f32[8,128]{1,0:T(8,128)S(1)}, f32[8,128]{1,0:T(8,128)S(1)}, u32[]{:S(2)}, u32[]{:S(2)}) collective-permute-start(f32[8,128]{1,0:T(8,128)S(1)} %score.3.rest_8_), channel_id=1, source_target_pairs={{0,2},{1,3},{2,0},{3,1},{16,18},{17,19},{18,16},{19,17},{4,6},{5,7... | collective-permute-start | bytes 12296 | tf_op jit(solution)/shard_map/ppermute | solution.py:324
  36.7 4.5 %copy-start.4 = (s32[1,512,8]{1,2,0:T(8,128)S(1)}, s32[1,512,8]{1,2,0:T(8,128)}, u32[]{:S(2)}) copy-start(s32[1,512,8]{1,2,0:T(8,128)} %param.9) | copy-start | bytes 49156

commit v11 on v10

--- a/solution.py
+++ b/solution.py
@@ -414,16 +414,16 @@
             name="score",
         )(inner, *[arrived[item] for item in items], *after)
 
-    early = [0] + first
-    early_scores = scored(early)
+    first_scores = scored(first)
+    returned = [moved(first_scores, 0, k) for k in first]
     own_scores = pl.pallas_call(
-        functools.partial(merge_kernel, early),
+        functools.partial(merge_kernel, first + [0]),
         out_shape=tile,
-        in_specs=specs(pltpu.VMEM, len(early)),
+        in_specs=specs(pltpu.VMEM, group - 1),
         out_specs=specs(pltpu.VMEM, 1)[0],
         compiler_params=params(),
         name="merge",
-    )(*[moved(early_scores, 0, k) for k in early])
+    )(*returned, scored([0]))
     other_scores = moved(own_scores, 1, 0)
     late_scores = scored([far], own_scores)
     far_scores = [moved(late_scores, side, far) for side in range(2)]

time: 42.2 us -> 42.1 us (level)
  starting transfers between devices: 22.9 us -> 22.3 us
  waiting for transfers between devices: 8.23 us -> 8.75 us
    ppermute x13, starting transfers between devices: 22.9 us -> 22.3 us  [moved(): return lax.ppermute(array, ('pair', 'ep'), pairs)]
    ppermute x13, waiting for transfers between devices: 8.23 us -> 8.75 us  [moved(): return lax.ppermute(array, ('pair', 'ep'), pairs)]
where the time goes in v11:
time: 42.1 us; the launch traced here: 41.9 us
  starting transfers between devices  22.3 us (53%)
  Pallas kernels  10.1 us (24%)
  waiting for transfers between devices  8.75 us (21%)
  between operations  0.73 us (2%)
    ppermute x13, starting transfers between devices, moved(): return lax.ppermute(array, ('pair', 'ep'), pairs)  22.3 us
    ppermute x13, waiting for transfers between devices, moved(): return lax.ppermute(array, ('pair', 'ep'), pairs)  8.75 us
    pallas_call x1, Pallas kernels, local(): pl.pallas_call(functools.partial(update_kernel, order, group, cap), out_s...  3.5 us
    pallas_call x1, Pallas kernels, local(): pl.pallas_call(functools.partial(later_kernel, last_items, late, cap), ou...  3.31 us
    pallas_call x1, Pallas kernels, local(): pl.pallas_call(functools.partial(route_kernel, first_items, first, group,...  1.94 us
    pallas_call x1, Pallas kernels, local(): pl.pallas_call(functools.partial(combine_kernel, far, group, cap), out_sh...  0.86 us
  transfers between devices with their start and end apart: 13, of which 6 were waited for; matrix products, arithmetic and copies ran while one was open for 0% of the time, Pallas kernels for 22%

profile of v11, /device:TPU:0, one launch (start us, length us, event | category | flops | bytes accessed | tf_op | source)
XLA Modules:
  0.0 41.9 jit_solution(14844015948869031142)
XLA Ops:
  0.6 3.0 %collective-permute-start = (bf16[768,256]{1,0:T(8,128)(2,1)}, bf16[768,256]{1,0:T(8,128)(2,1)S(1)}, u32[]{:S(2)}, u32[]{:S(2)}) collective-permute-start(bf16[768,256]{1,0:T(8,128)(2,1)} %bitcast.17), channel_id=1, source_target_pairs={{0,16},{1,17},{2,18},{3,19},{16,0},{17,1},{18,2},{19,3},{4,20},{5,... | collective-permute-start | bytes 1179656 | tf_op jit(solution)/shard_map/ppermute | solution.py:324
  3.7 1.9 %route.1 = (f32[16,512]{1,0:T(8,128)S(1)}, bf16[4,16,128]{2,1,0:T(8,128)(2,1)S(1)}, bf16[528,128]{1,0:T(8,128)(2,1)S(1)}, bf16[528,128]{1,0:T(8,128)(2,1)S(1)}, ...) custom-call(s32[8,512]{1,0:T(8,128)} %bitcast.22, bf16[8,512]{1,0:T(8,128)(2,1)} %bitcast.28, ...), custom_call_target="tpu_custom_call" | custom-call | flops 536870912 | bytes 3145728 | tf_op jit(solution)/shard_map/route/pallas_call | solution.py:348
  5.6 3.7 %collective-permute-start.1 = (bf16[528,128]{1,0:T(8,128)(2,1)S(1)}, bf16[528,128]{1,0:T(8,128)(2,1)S(1)}, u32[]{:S(2)}, u32[]{:S(2)}) collective-permute-start(bf16[528,128]{1,0:T(8,128)(2,1)S(1)} %get-tuple-element.13), channel_id=1, source_target_pairs={{0,3},{1,2},{2,1},{3,0},{16,19},{17,18},{18,17},{19,16},{4,7},{5,6... | collective-permute-start | bytes 405512 | tf_op jit(solution)/shard_map/ppermute | solution.py:324
  9.3 0.8 %collective-permute-start.3 = (bf16[528,128]{1,0:T(8,128)(2,1)S(1)}, bf16[528,128]{1,0:T(8,128)(2,1)S(1)}, u32[]{:S(2)}, u32[]{:S(2)}) collective-permute-start(bf16[528,128]{1,0:T(8,128)(2,1)S(1)} %get-tuple-element.15), channel_id=1, source_target_pairs={{0,19},{1,18},{2,17},{3,16},{16,3},{17,2},{18,1},{19,0},{4,23},{5,... | collective-permute-start | bytes 405512 | tf_op jit(solution)/shard_map/ppermute | solution.py:324
  10.1 1.4 %collective-permute-start.4 = (bf16[528,128]{1,0:T(8,128)(2,1)S(1)}, bf16[528,128]{1,0:T(8,128)(2,1)S(1)}, u32[]{:S(2)}, u32[]{:S(2)}) collective-permute-start(bf16[528,128]{1,0:T(8,128)(2,1)S(1)} %get-tuple-element.16), channel_id=1, source_target_pairs={{0,17},{1,16},{2,19},{3,18},{16,1},{17,0},{18,3},{19,2},{4,21},{5,... | collective-permute-start | bytes 405512 | tf_op jit(solution)/shard_map/ppermute | solution.py:324
  11.5 1.5 %collective-permute-done.other_ref = bf16[768,256]{1,0:T(8,128)(2,1)S(1)} collective-permute-done((bf16[768,256]{1,0:T(8,128)(2,1)}, bf16[768,256]{1,0:T(8,128)(2,1)S(1)}, u32[]{:S(2)}, u32[]{:S(2)}) %collective-permute-start) | collective-permute-done | bytes 393248 | tf_op jit(solution)/shard_map/ppermute | solution.py:324
  13.0 3.3 %later.1 = (f32[512,1024]{1,0:T(8,128)S(1)}, bf16[528,128]{1,0:T(8,128)(2,1)S(1)}, bf16[528,128]{1,0:T(8,128)(2,1)S(1)}, bf16[528,128]{1,0:T(8,128)(2,1)S(1)}, bf16[528,128]{1,0:T(8,128)(2,1)S(1)}) custom-call(f32[16,512]{1,0:T(8,128)S(1)} %get-tuple-element.17.slots_ref, bf16[4,16,128]{2,1,0:T(8,128)(2,1)S(1)} %get-tuple-element.18.tiles_ref, ...), custom_call_target="tpu_custom_call" | custom-call | flops 1342177280 | bytes 3145728 | tf_op jit(solution)/shard_map/later/pallas_call | solution.py:374
  16.3 1.8 %collective-permute-start.6 = (bf16[528,128]{1,0:T(8,128)(2,1)S(1)}, bf16[528,128]{1,0:T(8,128)(2,1)S(1)}, u32[]{:S(2)}, u32[]{:S(2)}) collective-permute-start(bf16[528,128]{1,0:T(8,128)(2,1)S(1)} %get-tuple-element.20), channel_id=1, source_target_pairs={{0,16},{1,17},{2,18},{3,19},{16,0},{17,1},{18,2},{19,3},{4,20},{5,... | collective-permute-start | bytes 405512 | tf_op jit(solution)/shard_map/ppermute | solution.py:324
  18.1 3.3 %collective-permute-start.5 = (bf16[528,128]{1,0:T(8,128)(2,1)S(1)}, bf16[528,128]{1,0:T(8,128)(2,1)S(1)}, u32[]{:S(2)}, u32[]{:S(2)}) collective-permute-start(bf16[528,128]{1,0:T(8,128)(2,1)S(1)} %get-tuple-element.19), channel_id=1, source_target_pairs={{0,2},{1,3},{2,0},{3,1},{16,18},{17,19},{18,16},{19,17},{4,6},{5,7... | collective-permute-start | bytes 405512 | tf_op jit(solution)/shard_map/ppermute | solution.py:324
  21.4 1.2 %collective-permute-done.4.rest_2_.rest_3_ = bf16[528,128]{1,0:T(8,128)(2,1)S(1)} collective-permute-done((bf16[528,128]{1,0:T(8,128)(2,1)S(1)}, bf16[528,128]{1,0:T(8,128)(2,1)S(1)}, u32[]{:S(2)}, u32[]{:S(2)}) %collective-permute-start.4) | collective-permute-done | bytes 135200 | tf_op jit(solution)/shard_map/ppermute | solution.py:324
  22.6 0.2 score.3
  22.8 2.5 %collective-permute-start.9 = (f32[8,128]{1,0:T(8,128)S(1)}, f32[8,128]{1,0:T(8,128)S(1)}, u32[]{:S(2)}, u32[]{:S(2)}) collective-permute-start(f32[8,128]{1,0:T(8,128)S(1)} %score.3), channel_id=1, source_target_pairs={{0,3},{1,2},{2,1},{3,0},{16,19},{17,18},{18,17},{19,16},{4,7},{5,6... | collective-permute-start | bytes 12296 | tf_op jit(solution)/shard_map/ppermute | solution.py:324
  25.3 0.0 copy-start.2
  25.3 0.1 score.4.rest_2_
  25.4 2.8 %collective-permute-done.9.rest_1_ = f32[8,128]{1,0:T(8,128)S(1)} collective-permute-done((f32[8,128]{1,0:T(8,128)S(1)}, f32[8,128]{1,0:T(8,128)S(1)}, u32[]{:S(2)}, u32[]{:S(2)}) %collective-permute-start.9) | collective-permute-done | bytes 4128 | tf_op jit(solution)/shard_map/ppermute | solution.py:324
  28.2 1.0 %collective-permute-done.8.rest_0_ = f32[8,128]{1,0:T(8,128)S(1)} collective-permute-done((f32[8,128]{1,0:T(8,128)S(1)}, f32[8,128]{1,0:T(8,128)S(1)}, u32[]{:S(2)}, u32[]{:S(2)}) %collective-permute-start.8) | collective-permute-done | bytes 4128 | tf_op jit(solution)/shard_map/ppermute | solution.py:324
  29.3 1.6 %collective-permute-start.10 = (f32[8,128]{1,0:T(8,128)S(1)}, f32[8,128]{1,0:T(8,128)S(1)}, u32[]{:S(2)}, u32[]{:S(2)}) collective-permute-start(f32[8,128]{1,0:T(8,128)S(1)} %merge.1.rest_2_.own_ref), channel_id=1, source_target_pairs={{0,16},{1,17},{2,18},{3,19},{16,0},{17,1},{18,2},{19,3},{4,20},{5,... | collective-permute-start | bytes 12296 | tf_op jit(solution)/shard_map/ppermute | solution.py:324
  30.9 1.3 %collective-permute-done.7.rest_1_.rest_6_ = bf16[528,128]{1,0:T(8,128)(2,1)S(1)} collective-permute-done((bf16[528,128]{1,0:T(8,128)(2,1)S(1)}, bf16[528,128]{1,0:T(8,128)(2,1)S(1)}, u32[]{:S(2)}, u32[]{:S(2)}) %collective-permute-start.7) | collective-permute-done | bytes 135200 | tf_op jit(solution)/shard_map/ppermute | solution.py:324
  32.2 0.1 score.5.rest_8_
  32.3 4.2 %collective-permute-start.12 = (f32[8,128]{1,0:T(8,128)S(1)}, f32[8,128]{1,0:T(8,128)S(1)}, u32[]{:S(2)}, u32[]{:S(2)}) collective-permute-start(f32[8,128]{1,0:T(8,128)S(1)} %score.5.rest_8_), channel_id=1, source_target_pairs={{0,18},{1,19},{2,16},{3,17},{16,2},{17,3},{18,0},{19,1},{4,22},{5,... | collective-permute-start | bytes 12296 | tf_op jit(solution)/shard_map/ppermute | solution.py:324
  36.5 0.0 copy-start.4
  36.6 3.5 %update.1 = f32[768,1024]{1,0:T(8,128)} custom-call(bf16[768,256]{1,0:T(8,128)(2,1)S(1)} %bitcast.19, bf16[768,256]{1,0:T(8,128)(2,1)S(1)} %collective-permute-done.other_ref, f32[768,1024]{1,0:T(8,128)S(1)} %bitcast.16, bf16[768,1024]{1,0:T(8,128)(2,1)S(1)} %bitcast.20, bf16[768,1024]{1,0:T(8,128)(2,1)S(1)} %bitcast.21, ...), custom_call_target="tpu_custom_call" | custom-call | flops 805306368 | bytes 9437184 | tf_op jit(solution)/shard_map/update/pallas_call | solution.py:432
  40.1 0.9 %collective-permute-done.11.own_far_ref = f32[8,128]{1,0:T(8,128)S(1)} collective-permute-done((f32[8,128]{1,0:T(8,128)S(1)}, f32[8,128]{1,0:T(8,128)S(1)}, u32[]{:S(2)}, u32[]{:S(2)}) %collective-permute-start.11) | collective-permute-done | bytes 4128 | tf_op jit(solution)/shard_map/ppermute | solution.py:324
  41.0 0.9 %combine.1 = f32[8,512]{1,0:T(8,128)} custom-call(s32[8,512]{1,0:T(8,128)S(1)} %bitcast.23, f32[16,512]{1,0:T(8,128)S(1)} %get-tuple-element.17.slots_ref, f32[8,128]{1,0:T(8,128)S(1)} %merge.1.rest_2_.own_ref, f32[8,128]{1,0:T(8,128)S(1)} %collective-permute-done.10.other_ref, f32[8,128]{1,0:T(8,128)S(1)} %collective-permute-done.11.own_far_ref, ...), custom_call_target="tpu_custom_call" | custom-call | flops 524288 | bytes 32768 | tf_op jit(solution)/shard_map/combine/pallas_call | solution.py:457
  (20 shorter events, 0.1 us)
Async XLA Ops:
  0.6 12.4 %copy-start.1 = (bf16[1,1,768,256]{3,2,1,0:T(8,128)(2,1)S(1)}, bf16[1,1,768,256]{3,2,1,0:T(8,128)(2,1)}, u32[]{:S(2)}) copy-start(bf16[1,1,768,256]{3,2,1,0:T(8,128)(2,1)} %param.10) | copy-start | bytes 1179652
  0.6 12.4 %collective-permute-start = (bf16[768,256]{1,0:T(8,128)(2,1)}, bf16[768,256]{1,0:T(8,128)(2,1)S(1)}, u32[]{:S(2)}, u32[]{:S(2)}) collective-permute-start(bf16[768,256]{1,0:T(8,128)(2,1)} %bitcast.17), channel_id=1, source_target_pairs={{0,16},{1,17},{2,18},{3,19},{16,0},{17,1},{18,2},{19,3},{4,20},{5,... | collective-permute-start | bytes 1179656 | tf_op jit(solution)/shard_map/ppermute | solution.py:324
  5.6 12.5 %collective-permute-start.1 = (bf16[528,128]{1,0:T(8,128)(2,1)S(1)}, bf16[528,128]{1,0:T(8,128)(2,1)S(1)}, u32[]{:S(2)}, u32[]{:S(2)}) collective-permute-start(bf16[528,128]{1,0:T(8,128)(2,1)S(1)} %get-tuple-element.13), channel_id=1, source_target_pairs={{0,3},{1,2},{2,1},{3,0},{16,19},{17,18},{18,17},{19,16},{4,7},{5,6... | collective-permute-start | bytes 405512 | tf_op jit(solution)/shard_map/ppermute | solution.py:324
  9.3 12.1 %collective-permute-start.2 = (bf16[528,128]{1,0:T(8,128)(2,1)S(1)}, bf16[528,128]{1,0:T(8,128)(2,1)S(1)}, u32[]{:S(2)}, u32[]{:S(2)}) collective-permute-start(bf16[528,128]{1,0:T(8,128)(2,1)S(1)} %get-tuple-element.14), channel_id=1, source_target_pairs={{0,1},{1,0},{2,3},{3,2},{16,17},{17,16},{18,19},{19,18},{4,5},{5,4... | collective-permute-start | bytes 405512 | tf_op jit(solution)/shard_map/ppermute | solution.py:324
  9.3 12.1 %collective-permute-start.3 = (bf16[528,128]{1,0:T(8,128)(2,1)S(1)}, bf16[528,128]{1,0:T(8,128)(2,1)S(1)}, u32[]{:S(2)}, u32[]{:S(2)}) collective-permute-start(bf16[528,128]{1,0:T(8,128)(2,1)S(1)} %get-tuple-element.15), channel_id=1, source_target_pairs={{0,19},{1,18},{2,17},{3,16},{16,3},{17,2},{18,1},{19,0},{4,23},{5,... | collective-permute-start | bytes 405512 | tf_op jit(solution)/shard_map/ppermute | solution.py:324
  10.1 12.4 %collective-permute-start.4 = (bf16[528,128]{1,0:T(8,128)(2,1)S(1)}, bf16[528,128]{1,0:T(8,128)(2,1)S(1)}, u32[]{:S(2)}, u32[]{:S(2)}) collective-permute-start(bf16[528,128]{1,0:T(8,128)(2,1)S(1)} %get-tuple-element.16), channel_id=1, source_target_pairs={{0,17},{1,16},{2,19},{3,18},{16,1},{17,0},{18,3},{19,2},{4,21},{5,... | collective-permute-start | bytes 405512 | tf_op jit(solution)/shard_map/ppermute | solution.py:324
  16.3 8.9 %collective-permute-start.6 = (bf16[528,128]{1,0:T(8,128)(2,1)S(1)}, bf16[528,128]{1,0:T(8,128)(2,1)S(1)}, u32[]{:S(2)}, u32[]{:S(2)}) collective-permute-start(bf16[528,128]{1,0:T(8,128)(2,1)S(1)} %get-tuple-element.20), channel_id=1, source_target_pairs={{0,16},{1,17},{2,18},{3,19},{16,0},{17,1},{18,2},{19,3},{4,20},{5,... | collective-permute-start | bytes 405512 | tf_op jit(solution)/shard_map/ppermute | solution.py:324
  18.1 12.7 %collective-permute-start.5 = (bf16[528,128]{1,0:T(8,128)(2,1)S(1)}, bf16[528,128]{1,0:T(8,128)(2,1)S(1)}, u32[]{:S(2)}, u32[]{:S(2)}) collective-permute-start(bf16[528,128]{1,0:T(8,128)(2,1)S(1)} %get-tuple-element.19), channel_id=1, source_target_pairs={{0,2},{1,3},{2,0},{3,1},{16,18},{17,19},{18,16},{19,17},{4,6},{5,7... | collective-permute-start | bytes 405512 | tf_op jit(solution)/shard_map/ppermute | solution.py:324
  21.4 10.8 %collective-permute-start.7 = (bf16[528,128]{1,0:T(8,128)(2,1)S(1)}, bf16[528,128]{1,0:T(8,128)(2,1)S(1)}, u32[]{:S(2)}, u32[]{:S(2)}) collective-permute-start(bf16[528,128]{1,0:T(8,128)(2,1)S(1)} %get-tuple-element.21), channel_id=1, source_target_pairs={{0,18},{1,19},{2,16},{3,17},{16,2},{17,3},{18,0},{19,1},{4,22},{5,... | collective-permute-start | bytes 405512 | tf_op jit(solution)/shard_map/ppermute | solution.py:324
  22.6 14.0 %copy-start.3 = (bf16[1,1,768,1024]{3,2,1,0:T(8,128)(2,1)S(1)}, bf16[1,1,768,1024]{3,2,1,0:T(8,128)(2,1)}, u32[]{:S(2)}) copy-start(bf16[1,1,768,1024]{3,2,1,0:T(8,128)(2,1)} %param.13) | copy-start | bytes 4718596
  22.8 5.5 %collective-permute-start.9 = (f32[8,128]{1,0:T(8,128)S(1)}, f32[8,128]{1,0:T(8,128)S(1)}, u32[]{:S(2)}, u32[]{:S(2)}) collective-permute-start(f32[8,128]{1,0:T(8,128)S(1)} %score.3), channel_id=1, source_target_pairs={{0,3},{1,2},{2,1},{3,0},{16,19},{17,18},{18,17},{19,16},{4,7},{5,6... | collective-permute-start | bytes 12296 | tf_op jit(solution)/shard_map/ppermute | solution.py:324
  25.3 4.0 %collective-permute-start.8 = (f32[8,128]{1,0:T(8,128)S(1)}, f32[8,128]{1,0:T(8,128)S(1)}, u32[]{:S(2)}, u32[]{:S(2)}) collective-permute-start(f32[8,128]{1,0:T(8,128)S(1)} %score.3), channel_id=1, source_target_pairs={{0,1},{1,0},{2,3},{3,2},{16,17},{17,16},{18,19},{19,18},{4,5},{5,4... | collective-permute-start | bytes 12296 | tf_op jit(solution)/shard_map/ppermute | solution.py:324
  25.3 11.3 %copy-start = (f32[1,1,768,1024]{3,2,1,0:T(8,128)S(1)}, f32[1,1,768,1024]{3,2,1,0:T(8,128)}, u32[]{:S(2)}) copy-start(f32[1,1,768,1024]{3,2,1,0:T(8,128)} %param.11) | copy-start | bytes 9437188
  25.3 11.3 %copy-start.2 = (bf16[1,1,768,1024]{3,2,1,0:T(8,128)(2,1)S(1)}, bf16[1,1,768,1024]{3,2,1,0:T(8,128)(2,1)}, u32[]{:S(2)}) copy-start(bf16[1,1,768,1024]{3,2,1,0:T(8,128)(2,1)} %param.12) | copy-start | bytes 4718596
  29.3 10.8 %collective-permute-start.10 = (f32[8,128]{1,0:T(8,128)S(1)}, f32[8,128]{1,0:T(8,128)S(1)}, u32[]{:S(2)}, u32[]{:S(2)}) collective-permute-start(f32[8,128]{1,0:T(8,128)S(1)} %merge.1.rest_2_.own_ref), channel_id=1, source_target_pairs={{0,16},{1,17},{2,18},{3,19},{16,0},{17,1},{18,2},{19,3},{4,20},{5,... | collective-permute-start | bytes 12296 | tf_op jit(solution)/shard_map/ppermute | solution.py:324
  32.3 7.8 %collective-permute-start.12 = (f32[8,128]{1,0:T(8,128)S(1)}, f32[8,128]{1,0:T(8,128)S(1)}, u32[]{:S(2)}, u32[]{:S(2)}) collective-permute-start(f32[8,128]{1,0:T(8,128)S(1)} %score.5.rest_8_), channel_id=1, source_target_pairs={{0,18},{1,19},{2,16},{3,17},{16,2},{17,3},{18,0},{19,1},{4,22},{5,... | collective-permute-start | bytes 12296 | tf_op jit(solution)/shard_map/ppermute | solution.py:324
  36.5 4.5 %collective-permute-start.11 = (f32[8,128]{1,0:T(8,128)S(1)}, f32[8,128]{1,0:T(8,128)S(1)}, u32[]{:S(2)}, u32[]{:S(2)}) collective-permute-start(f32[8,128]{1,0:T(8,128)S(1)} %score.5.rest_8_), channel_id=1, source_target_pairs={{0,2},{1,3},{2,0},{3,1},{16,18},{17,19},{18,16},{19,17},{4,6},{5,7... | collective-permute-start | bytes 12296 | tf_op jit(solution)/shard_map/ppermute | solution.py:324
  36.5 4.5 %copy-start.4 = (s32[1,512,8]{1,2,0:T(8,128)S(1)}, s32[1,512,8]{1,2,0:T(8,128)}, u32[]{:S(2)}) copy-start(s32[1,512,8]{1,2,0:T(8,128)} %param.9) | copy-start | bytes 49156

commit v12 on v11

--- a/solution.py
+++ b/solution.py
@@ -120,14 +120,20 @@
     tile_lane = lax.broadcasted_iota(jnp.int32, (TILE, LANES), 1)
     spot = tile_row * LANES + tile_lane
     kept = (spot >= base) & (spot < base + cap)
+    if group % TILE:
+        scales.append(jnp.zeros((-group % TILE, tokens), F32))
+    rows = jnp.concatenate(scales, axis=0)
+    lines = lax.dot_general(
+        rows.astype(BF16),
+        jnp.concatenate(picks, axis=0),
+        (((1,), (1,)), ((), ())),
+        preferred_element_type=F32,
+    )
     tiles = []
     for k in range(group):
-        spread = jnp.broadcast_to(scales[k], (TILE, tokens)).astype(BF16)
-        doubled = jnp.concatenate([picks[k]] * (LANES // cap), axis=0)
-        tile = lax.dot_general(
-            spread, doubled, (((1,), (1,)), ((), ())), preferred_element_type=F32
-        )
-        tiles.append(jnp.where(kept, tile, 0.0).astype(BF16))
+        line = lines[k : k + 1, k * cap : (k + 1) * cap]
+        line = jnp.concatenate([line] * (LANES // cap), axis=1)
+        tiles.append(jnp.where(kept, line, 0.0).astype(BF16))
         tiles_ref[k] = tiles[k]
     fill_chunks(steps, cap, picks, held, copies, tiles, chunks)
 
@@ -160,19 +166,23 @@
             )
 
 
-def score_chunks(steps, group, cap, chunks, inner_ref, score_ref):
+def score_kernel(items, group, cap, inner_ref, *rest):
+    chunks, score_ref = dict(zip(items, rest)), rest[-1]
     blocks = inner_ref.shape[1] // LANES
     me = ep_index()
     line_of = lax.broadcasted_iota(jnp.int32, score_ref.shape, 0)
     scores = jnp.zeros(score_ref.shape, F32)
-    for k in steps:
+    for k in sorted({k for _, k in items}):
         sums = []
         for side in range(2):
-            start = pl.multiple_of(side * group * cap + (me ^ k) * cap, cap)
             total = jnp.zeros((cap, LANES), F32)
-            for block in range(blocks):
-                rows = chunks[side, k][block * cap : (block + 1) * cap, :].astype(F32)
-                total += rows * inner_ref[pl.ds(start, cap), block * LANES : (block + 1) * LANES]
+            if (side, k) in items:
+                start = pl.multiple_of(side * group * cap + (me ^ k) * cap, cap)
+                for block in range(blocks):
+                    rows = chunks[side, k][block * cap : (block + 1) * cap, :].astype(F32)
+                    total += rows * inner_ref[
+                        pl.ds(start, cap), block * LANES : (block + 1) * LANES
+                    ]
             sums.append(total)
         both = jnp.concatenate(sums, axis=0)
         line = jnp.sum(both.T, axis=0, keepdims=True)
@@ -195,13 +205,8 @@
     return scales
 
 
-def score_kernel(items, steps, group, cap, inner_ref, *rest):
-    score_ref = rest[-1]
-    score_chunks(steps, group, cap, dict(zip(items, rest)), inner_ref, score_ref)
-
-
 def merge_kernel(steps, *rest):
-    refs, out_ref = rest[:-1], rest[-1]
+    refs, out_ref = rest[: len(steps)], rest[-1]
     row = lax.broadcasted_iota(jnp.int32, out_ref.shape, 0)
     me = ep_index()
     table = jnp.zeros(out_ref.shape, F32)
@@ -340,7 +345,7 @@
     first = [k for k in range(1, group) if k != far]
     late = [0, far]
     first_items = [(side, k) for side in range(2) for k in reversed(first)]
-    last_items = [(0, far), (1, 0), (1, far), (0, 0)]
+    last_items = [(0, far), (1, far), (1, 0), (0, 0)]
     order = first_items + last_items
     chunk = jax.ShapeDtypeStruct((half // LANES * cap + TILE, LANES), BF16)
     grads = pltpu.with_memory_space_constraint(grad_out[0], pltpu.HBM)
@@ -402,10 +407,9 @@
 
     tile = jax.ShapeDtypeStruct((group + -group % 8, LANES), F32)
 
-    def scored(steps, *after):
-        items = [(side, k) for side in range(2) for k in steps]
+    def scored(items, *after):
         return pl.pallas_call(
-            functools.partial(score_kernel, items, steps, group, cap),
+            functools.partial(score_kernel, items, group, cap),
             out_shape=tile,
             in_specs=specs(pltpu.VMEM, 1 + len(items)) + specs(pl.ANY, len(after)),
             out_specs=specs(pltpu.VMEM, 1)[0],
@@ -414,19 +418,21 @@
             name="score",
         )(inner, *[arrived[item] for item in items], *after)
 
-    first_scores = scored(first)
+    first_scores = scored(first_items)
     returned = [moved(first_scores, 0, k) for k in first]
+    far_scores = [scored([(0, far)], first_scores)]
     own_scores = pl.pallas_call(
         functools.partial(merge_kernel, first + [0]),
         out_shape=tile,
-        in_specs=specs(pltpu.VMEM, group - 1),
+        in_specs=specs(pltpu.VMEM, group - 1) + specs(pl.ANY, 1),
         out_specs=specs(pltpu.VMEM, 1)[0],
         compiler_params=params(),
         name="merge",
-    )(*returned, scored([0]))
+    )(*returned, scored([(0, 0), (1, 0)]), far_scores[0])
     other_scores = moved(own_scores, 1, 0)
-    late_scores = scored([far], own_scores)
-    far_scores = [moved(late_scores, side, far) for side in range(2)]
+    far_scores.append(scored([(1, far)], own_scores))
+    last_scores = far_scores[1]
+    far_scores = [moved(scores, side, far) for side, scores in enumerate(far_scores)]
 
     block = min(hid, 2 * LANES)
     update = pl.pallas_call(
@@ -452,7 +458,7 @@
         moment[0, 0],
         second[0, 0],
         *[arrived[item] for item in order],
-        late_scores,
+        last_scores,
     )
     router = pl.pallas_call(
         functools.partial(combine_kernel, far, group, cap),

time: 42.1 us -> 40.3 us (0.957)
  starting transfers between devices: 22.3 us -> 20.8 us
    ppermute x13, starting transfers between devices: 22.3 us -> 20.8 us  [moved(): return lax.ppermute(array, ('pair', 'ep'), pairs)]
  transfers between devices with their start and end apart: 13 -> 13, of which waited for: 6 -> 4; matrix products, arithmetic and copies ran while one was open for 0% -> 0% of each run, Pallas kernels for 22% -> 23%
where the time goes in v12:
time: 40.3 us; the launch traced here: 40.2 us
  starting transfers between devices  20.8 us (52%)
  Pallas kernels  10.2 us (25%)
  waiting for transfers between devices  8.36 us (21%)
  between operations  0.76 us (2%)
    ppermute x13, starting transfers between devices, moved(): return lax.ppermute(array, ('pair', 'ep'), pairs)  20.8 us
    ppermute x13, waiting for transfers between devices, moved(): return lax.ppermute(array, ('pair', 'ep'), pairs)  8.36 us
    pallas_call x1, Pallas kernels, local(): pl.pallas_call(functools.partial(update_kernel, order, group, cap), out_s...  3.5 us
    pallas_call x1, Pallas kernels, local(): pl.pallas_call(functools.partial(later_kernel, last_items, late, cap), ou...  3.31 us
    pallas_call x1, Pallas kernels, local(): pl.pallas_call(functools.partial(route_kernel, first_items, first, group,...  1.99 us
    pallas_call x1, Pallas kernels, local(): pl.pallas_call(functools.partial(combine_kernel, far, group, cap), out_sh...  0.86 us
  transfers between devices with their start and end apart: 13, of which 4 were waited for; matrix products, arithmetic and copies ran while one was open for 0% of the time, Pallas kernels for 23%

profile of v12, /device:TPU:0, one launch (start us, length us, event | category | flops | bytes accessed | tf_op | source)
XLA Modules:
  0.0 40.2 jit_solution(15013986953057292548)
XLA Ops:
  0.6 3.0 %collective-permute-start = (bf16[768,256]{1,0:T(8,128)(2,1)}, bf16[768,256]{1,0:T(8,128)(2,1)S(1)}, u32[]{:S(2)}, u32[]{:S(2)}) collective-permute-start(bf16[768,256]{1,0:T(8,128)(2,1)} %bitcast.17), channel_id=1, source_target_pairs={{0,16},{1,17},{2,18},{3,19},{16,0},{17,1},{18,2},{19,3},{4,20},{5,... | collective-permute-start | bytes 1179656 | tf_op jit(solution)/shard_map/ppermute | solution.py:329
  3.7 2.0 %route.1 = (f32[16,512]{1,0:T(8,128)S(1)}, bf16[4,16,128]{2,1,0:T(8,128)(2,1)S(1)}, bf16[528,128]{1,0:T(8,128)(2,1)S(1)}, bf16[528,128]{1,0:T(8,128)(2,1)S(1)}, ...) custom-call(s32[8,512]{1,0:T(8,128)} %bitcast.22, bf16[8,512]{1,0:T(8,128)(2,1)} %bitcast.28, ...), custom_call_target="tpu_custom_call" | custom-call | flops 536870912 | bytes 3145728 | tf_op jit(solution)/shard_map/route/pallas_call | solution.py:353
  5.7 3.7 %collective-permute-start.1 = (bf16[528,128]{1,0:T(8,128)(2,1)S(1)}, bf16[528,128]{1,0:T(8,128)(2,1)S(1)}, u32[]{:S(2)}, u32[]{:S(2)}) collective-permute-start(bf16[528,128]{1,0:T(8,128)(2,1)S(1)} %get-tuple-element.13), channel_id=1, source_target_pairs={{0,3},{1,2},{2,1},{3,0},{16,19},{17,18},{18,17},{19,16},{4,7},{5,6... | collective-permute-start | bytes 405512 | tf_op jit(solution)/shard_map/ppermute | solution.py:329
  9.3 0.8 %collective-permute-start.3 = (bf16[528,128]{1,0:T(8,128)(2,1)S(1)}, bf16[528,128]{1,0:T(8,128)(2,1)S(1)}, u32[]{:S(2)}, u32[]{:S(2)}) collective-permute-start(bf16[528,128]{1,0:T(8,128)(2,1)S(1)} %get-tuple-element.15), channel_id=1, source_target_pairs={{0,19},{1,18},{2,17},{3,16},{16,3},{17,2},{18,1},{19,0},{4,23},{5,... | collective-permute-start | bytes 405512 | tf_op jit(solution)/shard_map/ppermute | solution.py:329
  10.2 1.4 %collective-permute-start.4 = (bf16[528,128]{1,0:T(8,128)(2,1)S(1)}, bf16[528,128]{1,0:T(8,128)(2,1)S(1)}, u32[]{:S(2)}, u32[]{:S(2)}) collective-permute-start(bf16[528,128]{1,0:T(8,128)(2,1)S(1)} %get-tuple-element.16), channel_id=1, source_target_pairs={{0,17},{1,16},{2,19},{3,18},{16,1},{17,0},{18,3},{19,2},{4,21},{5,... | collective-permute-start | bytes 405512 | tf_op jit(solution)/shard_map/ppermute | solution.py:329
  11.6 1.4 %collective-permute-done.other_ref = bf16[768,256]{1,0:T(8,128)(2,1)S(1)} collective-permute-done((bf16[768,256]{1,0:T(8,128)(2,1)}, bf16[768,256]{1,0:T(8,128)(2,1)S(1)}, u32[]{:S(2)}, u32[]{:S(2)}) %collective-permute-start) | collective-permute-done | bytes 393248 | tf_op jit(solution)/shard_map/ppermute | solution.py:329
  13.0 3.3 %later.1 = (f32[512,1024]{1,0:T(8,128)S(1)}, bf16[528,128]{1,0:T(8,128)(2,1)S(1)}, bf16[528,128]{1,0:T(8,128)(2,1)S(1)}, bf16[528,128]{1,0:T(8,128)(2,1)S(1)}, bf16[528,128]{1,0:T(8,128)(2,1)S(1)}) custom-call(f32[16,512]{1,0:T(8,128)S(1)} %get-tuple-element.17.slots_ref, bf16[4,16,128]{2,1,0:T(8,128)(2,1)S(1)} %get-tuple-element.18.tiles_ref, ...), custom_call_target="tpu_custom_call" | custom-call | flops 1342177280 | bytes 3145728 | tf_op jit(solution)/shard_map/later/pallas_call | solution.py:379
  16.3 3.5 %collective-permute-start.5 = (bf16[528,128]{1,0:T(8,128)(2,1)S(1)}, bf16[528,128]{1,0:T(8,128)(2,1)S(1)}, u32[]{:S(2)}, u32[]{:S(2)}) collective-permute-start(bf16[528,128]{1,0:T(8,128)(2,1)S(1)} %get-tuple-element.19), channel_id=1, source_target_pairs={{0,2},{1,3},{2,0},{3,1},{16,18},{17,19},{18,16},{19,17},{4,6},{5,7... | collective-permute-start | bytes 405512 | tf_op jit(solution)/shard_map/ppermute | solution.py:329
  19.8 1.5 %collective-permute-start.7 = (bf16[528,128]{1,0:T(8,128)(2,1)S(1)}, bf16[528,128]{1,0:T(8,128)(2,1)S(1)}, u32[]{:S(2)}, u32[]{:S(2)}) collective-permute-start(bf16[528,128]{1,0:T(8,128)(2,1)S(1)} %get-tuple-element.21), channel_id=1, source_target_pairs={{0,16},{1,17},{2,18},{3,19},{16,0},{17,1},{18,2},{19,3},{4,20},{5,... | collective-permute-start | bytes 405512 | tf_op jit(solution)/shard_map/ppermute | solution.py:329
  21.4 0.0 collective-permute-start.6
  21.4 1.2 %collective-permute-done.4.rest_3_ = bf16[528,128]{1,0:T(8,128)(2,1)S(1)} collective-permute-done((bf16[528,128]{1,0:T(8,128)(2,1)S(1)}, bf16[528,128]{1,0:T(8,128)(2,1)S(1)}, u32[]{:S(2)}, u32[]{:S(2)}) %collective-permute-start.4) | collective-permute-done | bytes 135200 | tf_op jit(solution)/shard_map/ppermute | solution.py:329
  22.6 0.2 score.4.rest_1_
  22.8 2.4 %collective-permute-start.9 = (f32[8,128]{1,0:T(8,128)S(1)}, f32[8,128]{1,0:T(8,128)S(1)}, u32[]{:S(2)}, u32[]{:S(2)}) collective-permute-start(f32[8,128]{1,0:T(8,128)S(1)} %score.4.rest_1_), channel_id=1, source_target_pairs={{0,3},{1,2},{2,1},{3,0},{16,19},{17,18},{18,17},{19,16},{4,7},{5,6... | collective-permute-start | bytes 12296 | tf_op jit(solution)/shard_map/ppermute | solution.py:329
  25.2 5.0 %collective-permute-done.5.rest_0_.rest_4_ = bf16[528,128]{1,0:T(8,128)(2,1)S(1)} collective-permute-done((bf16[528,128]{1,0:T(8,128)(2,1)S(1)}, bf16[528,128]{1,0:T(8,128)(2,1)S(1)}, u32[]{:S(2)}, u32[]{:S(2)}) %collective-permute-start.5) | collective-permute-done | bytes 135200 | tf_op jit(solution)/shard_map/ppermute | solution.py:329
  30.2 0.1 score.6.rest_3_
  30.4 0.1 collective-permute-start.11
  30.4 0.0 copy-start
  30.5 0.1 score.5.rest_2_
  30.6 0.9 %collective-permute-start.10 = (f32[8,128]{1,0:T(8,128)S(1)}, f32[8,128]{1,0:T(8,128)S(1)}, u32[]{:S(2)}, u32[]{:S(2)}) collective-permute-start(f32[8,128]{1,0:T(8,128)S(1)} %merge.1.rest_1_.own_ref), channel_id=1, source_target_pairs={{0,16},{1,17},{2,18},{3,19},{16,0},{17,1},{18,2},{19,3},{4,20},{5,... | collective-permute-start | bytes 12296 | tf_op jit(solution)/shard_map/ppermute | solution.py:329
  31.5 0.7 %collective-permute-done.6.rest_0_.rest_5_ = bf16[528,128]{1,0:T(8,128)(2,1)S(1)} collective-permute-done((bf16[528,128]{1,0:T(8,128)(2,1)S(1)}, bf16[528,128]{1,0:T(8,128)(2,1)S(1)}, u32[]{:S(2)}, u32[]{:S(2)}) %collective-permute-start.6) | collective-permute-done | bytes 135200 | tf_op jit(solution)/shard_map/ppermute | solution.py:329
  32.2 0.1 score.7.rest_8_
  32.3 3.4 %collective-permute-start.12 = (f32[8,128]{1,0:T(8,128)S(1)}, f32[8,128]{1,0:T(8,128)S(1)}, u32[]{:S(2)}, u32[]{:S(2)}) collective-permute-start(f32[8,128]{1,0:T(8,128)S(1)} %score.7.rest_8_), channel_id=1, source_target_pairs={{0,18},{1,19},{2,16},{3,17},{16,2},{17,3},{18,0},{19,1},{4,22},{5,... | collective-permute-start | bytes 12296 | tf_op jit(solution)/shard_map/ppermute | solution.py:329
  35.7 3.5 %update.1 = f32[768,1024]{1,0:T(8,128)} custom-call(bf16[768,256]{1,0:T(8,128)(2,1)S(1)} %bitcast.19, bf16[768,256]{1,0:T(8,128)(2,1)S(1)} %collective-permute-done.other_ref, f32[768,1024]{1,0:T(8,128)S(1)} %bitcast.16, bf16[768,1024]{1,0:T(8,128)(2,1)S(1)} %bitcast.20, bf16[768,1024]{1,0:T(8,128)(2,1)S(1)} %bitcast.21, ...), custom_call_target="tpu_custom_call" | custom-call | flops 805306368 | bytes 9437184 | tf_op jit(solution)/shard_map/update/pallas_call | solution.py:438
  39.3 0.9 %combine.1 = f32[8,512]{1,0:T(8,128)} custom-call(s32[8,512]{1,0:T(8,128)S(1)} %bitcast.23, f32[16,512]{1,0:T(8,128)S(1)} %get-tuple-element.17.slots_ref, f32[8,128]{1,0:T(8,128)S(1)} %merge.1.rest_1_.own_ref, f32[8,128]{1,0:T(8,128)S(1)} %collective-permute-done.10.other_ref, f32[8,128]{1,0:T(8,128)S(1)} %collective-permute-done.11.own_far_ref, ...), custom_call_target="tpu_custom_call" | custom-call | flops 524288 | bytes 32768 | tf_op jit(solution)/shard_map/combine/pallas_call | solution.py:463
  (21 shorter events, 0.1 us)
Async XLA Ops:
  0.6 12.4 %copy-start.1 = (bf16[1,1,768,256]{3,2,1,0:T(8,128)(2,1)S(1)}, bf16[1,1,768,256]{3,2,1,0:T(8,128)(2,1)}, u32[]{:S(2)}) copy-start(bf16[1,1,768,256]{3,2,1,0:T(8,128)(2,1)} %param.10) | copy-start | bytes 1179652
  0.6 12.4 %collective-permute-start = (bf16[768,256]{1,0:T(8,128)(2,1)}, bf16[768,256]{1,0:T(8,128)(2,1)S(1)}, u32[]{:S(2)}, u32[]{:S(2)}) collective-permute-start(bf16[768,256]{1,0:T(8,128)(2,1)} %bitcast.17), channel_id=1, source_target_pairs={{0,16},{1,17},{2,18},{3,19},{16,0},{17,1},{18,2},{19,3},{4,20},{5,... | collective-permute-start | bytes 1179656 | tf_op jit(solution)/shard_map/ppermute | solution.py:329
  5.7 14.2 %collective-permute-start.1 = (bf16[528,128]{1,0:T(8,128)(2,1)S(1)}, bf16[528,128]{1,0:T(8,128)(2,1)S(1)}, u32[]{:S(2)}, u32[]{:S(2)}) collective-permute-start(bf16[528,128]{1,0:T(8,128)(2,1)S(1)} %get-tuple-element.13), channel_id=1, source_target_pairs={{0,3},{1,2},{2,1},{3,0},{16,19},{17,18},{18,17},{19,16},{4,7},{5,6... | collective-permute-start | bytes 405512 | tf_op jit(solution)/shard_map/ppermute | solution.py:329
  9.3 12.0 %collective-permute-start.2 = (bf16[528,128]{1,0:T(8,128)(2,1)S(1)}, bf16[528,128]{1,0:T(8,128)(2,1)S(1)}, u32[]{:S(2)}, u32[]{:S(2)}) collective-permute-start(bf16[528,128]{1,0:T(8,128)(2,1)S(1)} %get-tuple-element.14), channel_id=1, source_target_pairs={{0,1},{1,0},{2,3},{3,2},{16,17},{17,16},{18,19},{19,18},{4,5},{5,4... | collective-permute-start | bytes 405512 | tf_op jit(solution)/shard_map/ppermute | solution.py:329
  9.3 12.0 %collective-permute-start.3 = (bf16[528,128]{1,0:T(8,128)(2,1)S(1)}, bf16[528,128]{1,0:T(8,128)(2,1)S(1)}, u32[]{:S(2)}, u32[]{:S(2)}) collective-permute-start(bf16[528,128]{1,0:T(8,128)(2,1)S(1)} %get-tuple-element.15), channel_id=1, source_target_pairs={{0,19},{1,18},{2,17},{3,16},{16,3},{17,2},{18,1},{19,0},{4,23},{5,... | collective-permute-start | bytes 405512 | tf_op jit(solution)/shard_map/ppermute | solution.py:329
  10.2 12.4 %collective-permute-start.4 = (bf16[528,128]{1,0:T(8,128)(2,1)S(1)}, bf16[528,128]{1,0:T(8,128)(2,1)S(1)}, u32[]{:S(2)}, u32[]{:S(2)}) collective-permute-start(bf16[528,128]{1,0:T(8,128)(2,1)S(1)} %get-tuple-element.16), channel_id=1, source_target_pairs={{0,17},{1,16},{2,19},{3,18},{16,1},{17,0},{18,3},{19,2},{4,21},{5,... | collective-permute-start | bytes 405512 | tf_op jit(solution)/shard_map/ppermute | solution.py:329
  16.3 13.9 %collective-permute-start.5 = (bf16[528,128]{1,0:T(8,128)(2,1)S(1)}, bf16[528,128]{1,0:T(8,128)(2,1)S(1)}, u32[]{:S(2)}, u32[]{:S(2)}) collective-permute-start(bf16[528,128]{1,0:T(8,128)(2,1)S(1)} %get-tuple-element.19), channel_id=1, source_target_pairs={{0,2},{1,3},{2,0},{3,1},{16,18},{17,19},{18,16},{19,17},{4,6},{5,7... | collective-permute-start | bytes 405512 | tf_op jit(solution)/shard_map/ppermute | solution.py:329
  19.8 10.6 %collective-permute-start.7 = (bf16[528,128]{1,0:T(8,128)(2,1)S(1)}, bf16[528,128]{1,0:T(8,128)(2,1)S(1)}, u32[]{:S(2)}, u32[]{:S(2)}) collective-permute-start(bf16[528,128]{1,0:T(8,128)(2,1)S(1)} %get-tuple-element.21), channel_id=1, source_target_pairs={{0,16},{1,17},{2,18},{3,19},{16,0},{17,1},{18,2},{19,3},{4,20},{5,... | collective-permute-start | bytes 405512 | tf_op jit(solution)/shard_map/ppermute | solution.py:329
  21.4 10.9 %collective-permute-start.6 = (bf16[528,128]{1,0:T(8,128)(2,1)S(1)}, bf16[528,128]{1,0:T(8,128)(2,1)S(1)}, u32[]{:S(2)}, u32[]{:S(2)}) collective-permute-start(bf16[528,128]{1,0:T(8,128)(2,1)S(1)} %get-tuple-element.20), channel_id=1, source_target_pairs={{0,18},{1,19},{2,16},{3,17},{16,2},{17,3},{18,0},{19,1},{4,22},{5,... | collective-permute-start | bytes 405512 | tf_op jit(solution)/shard_map/ppermute | solution.py:329
  22.8 7.8 %collective-permute-start.9 = (f32[8,128]{1,0:T(8,128)S(1)}, f32[8,128]{1,0:T(8,128)S(1)}, u32[]{:S(2)}, u32[]{:S(2)}) collective-permute-start(f32[8,128]{1,0:T(8,128)S(1)} %score.4.rest_1_), channel_id=1, source_target_pairs={{0,3},{1,2},{2,1},{3,0},{16,19},{17,18},{18,17},{19,16},{4,7},{5,6... | collective-permute-start | bytes 12296 | tf_op jit(solution)/shard_map/ppermute | solution.py:329
  25.2 5.4 %collective-permute-start.8 = (f32[8,128]{1,0:T(8,128)S(1)}, f32[8,128]{1,0:T(8,128)S(1)}, u32[]{:S(2)}, u32[]{:S(2)}) collective-permute-start(f32[8,128]{1,0:T(8,128)S(1)} %score.4.rest_1_), channel_id=1, source_target_pairs={{0,1},{1,0},{2,3},{3,2},{16,17},{17,16},{18,19},{19,18},{4,5},{5,4... | collective-permute-start | bytes 12296 | tf_op jit(solution)/shard_map/ppermute | solution.py:329
  30.2 5.5 %copy-start.2 = (bf16[1,1,768,1024]{3,2,1,0:T(8,128)(2,1)S(1)}, bf16[1,1,768,1024]{3,2,1,0:T(8,128)(2,1)}, u32[]{:S(2)}) copy-start(bf16[1,1,768,1024]{3,2,1,0:T(8,128)(2,1)} %param.12) | copy-start | bytes 4718596
  30.2 5.5 %copy-start.3 = (bf16[1,1,768,1024]{3,2,1,0:T(8,128)(2,1)S(1)}, bf16[1,1,768,1024]{3,2,1,0:T(8,128)(2,1)}, u32[]{:S(2)}) copy-start(bf16[1,1,768,1024]{3,2,1,0:T(8,128)(2,1)} %param.13) | copy-start | bytes 4718596
  30.4 8.9 %collective-permute-start.11 = (f32[8,128]{1,0:T(8,128)S(1)}, f32[8,128]{1,0:T(8,128)S(1)}, u32[]{:S(2)}, u32[]{:S(2)}) collective-permute-start(f32[8,128]{1,0:T(8,128)S(1)} %score.6.rest_3_), channel_id=1, source_target_pairs={{0,2},{1,3},{2,0},{3,1},{16,18},{17,19},{18,16},{19,17},{4,6},{5,7... | collective-permute-start | bytes 12296 | tf_op jit(solution)/shard_map/ppermute | solution.py:329
  30.4 5.3 %copy-start = (f32[1,1,768,1024]{3,2,1,0:T(8,128)S(1)}, f32[1,1,768,1024]{3,2,1,0:T(8,128)}, u32[]{:S(2)}) copy-start(f32[1,1,768,1024]{3,2,1,0:T(8,128)} %param.11) | copy-start | bytes 9437188
  30.6 8.6 %collective-permute-start.10 = (f32[8,128]{1,0:T(8,128)S(1)}, f32[8,128]{1,0:T(8,128)S(1)}, u32[]{:S(2)}, u32[]{:S(2)}) collective-permute-start(f32[8,128]{1,0:T(8,128)S(1)} %merge.1.rest_1_.own_ref), channel_id=1, source_target_pairs={{0,16},{1,17},{2,18},{3,19},{16,0},{17,1},{18,2},{19,3},{4,20},{5,... | collective-permute-start | bytes 12296 | tf_op jit(solution)/shard_map/ppermute | solution.py:329
  32.3 6.9 %collective-permute-start.12 = (f32[8,128]{1,0:T(8,128)S(1)}, f32[8,128]{1,0:T(8,128)S(1)}, u32[]{:S(2)}, u32[]{:S(2)}) collective-permute-start(f32[8,128]{1,0:T(8,128)S(1)} %score.7.rest_8_), channel_id=1, source_target_pairs={{0,18},{1,19},{2,16},{3,17},{16,2},{17,3},{18,0},{19,1},{4,22},{5,... | collective-permute-start | bytes 12296 | tf_op jit(solution)/shard_map/ppermute | solution.py:329
  35.7 3.6 %copy-start.4 = (s32[1,512,8]{1,2,0:T(8,128)S(1)}, s32[1,512,8]{1,2,0:T(8,128)}, u32[]{:S(2)}) copy-start(s32[1,512,8]{1,2,0:T(8,128)} %param.9) | copy-start | bytes 49156

commit v13 on v12

--- a/solution.py
+++ b/solution.py
@@ -13,6 +13,8 @@
 decay_rate = 0.1
 first_fix = 1.0 - 0.9**10
 second_fix = 1.0 - 0.95**10
+first_unit = (1.0 - beta_first) / first_fix
+second_unit = (1.0 - beta_second) / second_fix
 
 LANES = 128
 TILE = 16
@@ -190,19 +192,35 @@
     score_ref[...] = scores
 
 
-def place_chunks(items, group, cap, chunks, rows_ref):
-    blocks = rows_ref.shape[1] // LANES
+def scale_into(scaled, at, hidden, line):
+    for top in range(0, hidden.shape[0], LANES):
+        lines = slice(top, top + LANES)
+        scaled[lines, at : at + LANES] = (hidden[lines, :].astype(F32) * line).astype(BF16)
+
+
+def sum_kernel(items, group, cap, own_ref, other_ref, *rest):
+    chunks = dict(zip(items, rest))
+    grad_ref, rows, scaled = rest[-3:]
+    blocks = rows.shape[1] // LANES
+    slots = group * cap
     me = ep_index()
-    scales = [jnp.zeros((TILE, LANES), F32)] * 2
-    for side, k in items:
-        chunk = chunks[side, k]
-        start = pl.multiple_of(side * group * cap + (me ^ k) * cap, cap)
-        for block in range(blocks):
-            rows_ref[pl.ds(start, cap), block * LANES : (block + 1) * LANES] = chunk[
-                block * cap : (block + 1) * cap, :
-            ]
-        scales[side] += chunk[blocks * cap :, :].astype(F32)
-    return scales
+    for side, hidden in enumerate((own_ref, other_ref)):
+        tile = jnp.zeros((TILE, LANES), F32)
+        for k in range(group):
+            start = pl.multiple_of(side * slots + (me ^ k) * cap, cap)
+            if (side, k) not in items:
+                rows[pl.ds(start, cap), :] = jnp.zeros((cap, rows.shape[1]), BF16)
+                continue
+            chunk = chunks[side, k]
+            tile += chunk[blocks * cap :, :].astype(F32)
+            for block in range(blocks):
+                rows[pl.ds(start, cap), block * LANES : (block + 1) * LANES] = chunk[
+                    block * cap : (block + 1) * cap, :
+                ]
+        for part in range(slots // LANES):
+            lanes = slice(part * LANES, (part + 1) * LANES)
+            scale_into(scaled, side * slots + part * LANES, hidden.at[:, lanes], tile[part : part + 1, :])
+    grad_ref[...] = jnp.dot(scaled[...], rows[...], preferred_element_type=F32)
 
 
 def merge_kernel(steps, *rest):
@@ -216,50 +234,58 @@
     out_ref[...] = table
 
 
-def update_rows(blocks, operands, scaled, total, update, finished):
-    own_ref, other_ref, rows, scales_ref, master_ref, moment_ref, second_ref = operands
-    slots = own_ref.shape[1]
-    half = rows.shape[1]
-    step = min(half, 4 * LANES)
+def update_kernel(items, cap, own_ref, other_ref, grad_ref, master_ref, moment_ref, second_ref, *rest):
+    chunks = dict(zip(items, rest))
+    _, update_hbm, rows, scaled, total, update, sems = rest[len(items) :]
+    hid, half = update.shape
+    block = total.shape[1]
+    width = min(half, 4 * LANES)
+    height = block // 2
+    data_rows = half // LANES * cap
+    rows[...] = jnp.zeros(rows.shape, BF16)
+    for at, ((side, k), chunk) in enumerate(chunks.items()):
+        slot = (ep_index() ^ k) * cap
+        lanes = pl.ds(pl.multiple_of(slot // LANES * LANES, LANES), LANES)
+        start = pl.multiple_of(at * LANES + slot % LANES, cap)
+        for part in range(half // LANES):
+            rows[pl.ds(start, cap), part * LANES : (part + 1) * LANES] = chunk[
+                part * cap : (part + 1) * cap, :
+            ]
+        line = jnp.sum(chunk[data_rows:, :].astype(F32), axis=0, keepdims=True)
+        scale_into(scaled, at * LANES, (own_ref, other_ref)[side].at[:, lanes], line)
 
     def multiply(at):
-        block = blocks[at]
-        for side, ref in enumerate((own_ref, other_ref)):
-            for part in range(slots // LANES):
-                lanes = slice(part * LANES, (part + 1) * LANES)
-                column = side * slots + part * LANES
-                scaled[at % 2, :, column : column + LANES] = (
-                    ref[block, lanes].astype(F32) * scales_ref[side, part : part + 1, :]
-                ).astype(BF16)
-        total[at % 2] = jnp.dot(scaled[at % 2], rows[...], preferred_element_type=F32)
+        total[at % 2] = jnp.dot(
+            scaled[at * block : (at + 1) * block, :], rows[...], preferred_element_type=F32
+        )
 
     def moments(at, top, columns):
-        lines = slice(blocks[at].start + top, blocks[at].start + top + TILE)
-        grad = total[at % 2, top : top + TILE, columns]
-        first = moment_ref[lines, columns].astype(F32) * (beta_first / first_fix) + grad * (
-            (1.0 - beta_first) / first_fix
+        lines = slice(at * block + top, at * block + top + TILE)
+        grad = total[at % 2, top : top + TILE, columns] + grad_ref[lines, columns]
+        first = moment_ref[lines, columns].astype(F32) * (beta_first / (1.0 - beta_first)) + grad
+        square = (
+            second_ref[lines, columns].astype(F32) * (beta_second / (1.0 - beta_second))
+            + grad * grad
         )
-        square = second_ref[lines, columns].astype(F32) * (beta_second / second_fix) + (
-            grad * grad
-        ) * ((1.0 - beta_second) / second_fix)
         return first, square, lax.rsqrt(square)
 
     def inverse(first, square, root):
-        return first, pl.reciprocal(square * root + adam_eps, approx=True)
+        scale = square * root * (second_unit**0.5 / first_unit) + adam_eps / first_unit
+        return first, pl.reciprocal(scale, approx=True)
 
     def finish(at, top, columns, first, scale):
-        lines = slice(blocks[at].start + top, blocks[at].start + top + TILE)
-        place = slice(lines.start - blocks[0].start, lines.stop - blocks[0].start)
-        update[place, columns] = first * scale + decay_rate * master_ref[lines, columns]
-
+        lines = slice(at * block + top, at * block + top + TILE)
+        update[lines, columns] = first * scale + decay_rate * master_ref[lines, columns]
+
+    copies = []
     multiply(0)
-    for at, block in enumerate(blocks):
-        if at + 1 < len(blocks):
+    for at in range(hid // block):
+        if at + 1 < hid // block:
             multiply(at + 1)
         pieces = [
-            (top, slice(column, column + step))
-            for top in range(0, block.stop - block.start, TILE)
-            for column in range(0, half, step)
+            (top, slice(column, column + width))
+            for top in range(0, block, TILE)
+            for column in range(0, half, width)
         ]
         held = {}
         for turn in range(len(pieces) + 2):
@@ -269,29 +295,15 @@
                 held[turn - 1, 1] = inverse(*held.pop((turn - 1, 0)))
             if turn >= 2:
                 finish(at, *pieces[turn - 2], *held.pop((turn - 2, 1)))
-        finished(at)
-
-
-def update_kernel(items, group, cap, own_ref, other_ref, master_ref, moment_ref, second_ref, *rest):
-    chunks = dict(zip(items, rest))
-    _, update_hbm, rows, scales_ref, scaled, total, update, sems = rest[len(items) :]
-    hid, block = update.shape[0], total.shape[1]
-    blocks = [slice(top, top + block) for top in range(0, hid, block)]
-    scales = place_chunks(items, group, cap, chunks, rows)
-    for side in range(2):
-        scales_ref[side] = scales[side]
-    copies = []
-
-    def finished(at):
-        copies.append(
-            pltpu.make_async_copy(
-                update.at[blocks[at], :], update_hbm.at[blocks[at], :], sems.at[at]
-            )
-        )
-        copies[-1].start()
-
-    operands = (own_ref, other_ref, rows, scales_ref, master_ref, moment_ref, second_ref)
-    update_rows(blocks, operands, scaled, total, update, finished)
+                top, columns = pieces[turn - 2]
+                if (top + TILE) % height == 0 and columns.stop == half:
+                    lines = slice(at * block + top + TILE - height, at * block + top + TILE)
+                    copies.append(
+                        pltpu.make_async_copy(
+                            update.at[lines, :], update_hbm.at[lines, :], sems.at[len(copies)]
+                        )
+                    )
+                    copies[-1].start()
     for copy in copies:
         copy.wait()
 
@@ -419,10 +431,25 @@
         )(inner, *[arrived[item] for item in items], *after)
 
     first_scores = scored(first_items)
-    returned = [moved(first_scores, 0, k) for k in first]
-    far_scores = [scored([(0, far)], first_scores)]
+    returned = [moved(first_scores, 0, k) for k in reversed(first)]
+    added = [(0, far), (1, far), (1, 0)]
+    summed = [item for item in order if item not in added]
+    grad = pl.pallas_call(
+        functools.partial(sum_kernel, summed, group, cap),
+        out_shape=jax.ShapeDtypeStruct((hid, half), F32),
+        in_specs=specs(pltpu.VMEM, 2 + len(summed)) + specs(pl.ANY, 1),
+        out_specs=specs(pltpu.VMEM, 1)[0],
+        scratch_shapes=[
+            pltpu.VMEM((2 * slots, half), BF16),
+            pltpu.VMEM((hid, 2 * slots), BF16),
+        ],
+        compiler_params=params(),
+        cost_estimate=cost(4 * slots * hid * half, 4 * hid * half),
+        name="sum",
+    )(own_hidden, other_hidden, *[arrived[item] for item in summed], first_scores)
+    far_scores = [scored([(0, far)], grad)]
     own_scores = pl.pallas_call(
-        functools.partial(merge_kernel, first + [0]),
+        functools.partial(merge_kernel, first[::-1] + [0]),
         out_shape=tile,
         in_specs=specs(pltpu.VMEM, group - 1) + specs(pl.ANY, 1),
         out_specs=specs(pltpu.VMEM, 1)[0],
@@ -436,28 +463,28 @@
 
     block = min(hid, 2 * LANES)
     update = pl.pallas_call(
-        functools.partial(update_kernel, order, group, cap),
+        functools.partial(update_kernel, added, cap),
         out_shape=jax.ShapeDtypeStruct((hid, half), F32),
-        in_specs=specs(pltpu.VMEM, 5 + len(order)) + specs(pl.ANY, 1),
+        in_specs=specs(pltpu.VMEM, 6 + len(added)) + specs(pl.ANY, 1),
         out_specs=specs(pltpu.HBM, 1)[0],
         scratch_shapes=[
-            pltpu.VMEM((2 * slots, half), BF16),
-            pltpu.VMEM((2, TILE, LANES), F32),
-            pltpu.VMEM((2, block, 2 * slots), BF16),
+            pltpu.VMEM((len(added) * LANES, half), BF16),
+            pltpu.VMEM((hid, len(added) * LANES), BF16),
             pltpu.VMEM((2, block, half), F32),
             pltpu.VMEM((hid, half), F32),
-            pltpu.SemaphoreType.DMA((hid // block,)),
+            pltpu.SemaphoreType.DMA((2 * hid // block,)),
         ],
         compiler_params=params(),
-        cost_estimate=cost(4 * slots * hid * half, 12 * hid * half),
+        cost_estimate=cost(6 * LANES * hid * half, 16 * hid * half),
         name="update",
     )(
         own_hidden,
         other_hidden,
+        grad,
         param,
         moment[0, 0],
         second[0, 0],
-        *[arrived[item] for item in order],
+        *[arrived[item] for item in added],
         last_scores,
     )
     router = pl.pallas_call(

time: 40.3 us -> 40 us (level)
  waiting for transfers between devices: 8.36 us -> 7.11 us
  Pallas kernels: 10.2 us -> 11.1 us
    ppermute x13, waiting for transfers between devices: 8.36 us -> 7.11 us  [moved(): return lax.ppermute(array, ('pair', 'ep'), pairs)]
    pallas_call x2 -> x3, Pallas kernels: 3.52 us -> 4.32 us  [the longest x1 3.18 us: local(): pl.pallas_call(functools.partial(update_kernel, added, cap), out_shape=ja...]
  transfers between devices with their start and end apart: 13 -> 13, of which waited for: 4 -> 4; matrix products, arithmetic and copies ran while one was open for 0% -> 0% of each run, Pallas kernels for 23% -> 26%
where the time goes in v13:
time: 40 us; the launch traced here: 39.8 us
  starting transfers between devices  20.9 us (52%)
  Pallas kernels  11.1 us (28%)
  waiting for transfers between devices  7.11 us (18%)
  between operations  0.76 us (2%)
    ppermute x13, starting transfers between devices, moved(): return lax.ppermute(array, ('pair', 'ep'), pairs)  20.9 us
    ppermute x13, waiting for transfers between devices, moved(): return lax.ppermute(array, ('pair', 'ep'), pairs)  7.11 us
    pallas_call x1, Pallas kernels, local(): pl.pallas_call(functools.partial(later_kernel, last_items, late, cap), ou...  3.33 us
    pallas_call x1, Pallas kernels, local(): pl.pallas_call(functools.partial(update_kernel, added, cap), out_shape=ja...  3.18 us
    pallas_call x1, Pallas kernels, local(): pl.pallas_call(functools.partial(route_kernel, first_items, first, group,...  1.99 us
    pallas_call x1, Pallas kernels, local(): pl.pallas_call(functools.partial(sum_kernel, summed, group, cap), out_sha...  1.12 us
    pallas_call x1, Pallas kernels, local(): pl.pallas_call(functools.partial(combine_kernel, far, group, cap), out_sh...  0.86 us
  transfers between devices with their start and end apart: 13, of which 4 were waited for; matrix products, arithmetic and copies ran while one was open for 0% of the time, Pallas kernels for 26%

profile of v13, /device:TPU:0, one launch (start us, length us, event | category | flops | bytes accessed | tf_op | source)
XLA Modules:
  0.0 39.8 jit_solution(10141355141300490125)
XLA Ops:
  0.6 3.0 %collective-permute-start = (bf16[768,256]{1,0:T(8,128)(2,1)}, bf16[768,256]{1,0:T(8,128)(2,1)S(1)}, u32[]{:S(2)}, u32[]{:S(2)}) collective-permute-start(bf16[768,256]{1,0:T(8,128)(2,1)} %bitcast.17), channel_id=1, source_target_pairs={{0,16},{1,17},{2,18},{3,19},{16,0},{17,1},{18,2},{19,3},{4,20},{5,... | collective-permute-start | bytes 1179656 | tf_op jit(solution)/shard_map/ppermute | solution.py:341
  3.7 2.0 %route.1 = (f32[16,512]{1,0:T(8,128)S(1)}, bf16[4,16,128]{2,1,0:T(8,128)(2,1)S(1)}, bf16[528,128]{1,0:T(8,128)(2,1)S(1)}, bf16[528,128]{1,0:T(8,128)(2,1)S(1)}, ...) custom-call(s32[8,512]{1,0:T(8,128)} %bitcast.23, bf16[8,512]{1,0:T(8,128)(2,1)} %bitcast.29, ...), custom_call_target="tpu_custom_call" | custom-call | flops 536870912 | bytes 3145728 | tf_op jit(solution)/shard_map/route/pallas_call | solution.py:365
  5.7 3.7 %collective-permute-start.1 = (bf16[528,128]{1,0:T(8,128)(2,1)S(1)}, bf16[528,128]{1,0:T(8,128)(2,1)S(1)}, u32[]{:S(2)}, u32[]{:S(2)}) collective-permute-start(bf16[528,128]{1,0:T(8,128)(2,1)S(1)} %get-tuple-element.13), channel_id=1, source_target_pairs={{0,3},{1,2},{2,1},{3,0},{16,19},{17,18},{18,17},{19,16},{4,7},{5,6... | collective-permute-start | bytes 405512 | tf_op jit(solution)/shard_map/ppermute | solution.py:341
  9.3 0.8 %collective-permute-start.3 = (bf16[528,128]{1,0:T(8,128)(2,1)S(1)}, bf16[528,128]{1,0:T(8,128)(2,1)S(1)}, u32[]{:S(2)}, u32[]{:S(2)}) collective-permute-start(bf16[528,128]{1,0:T(8,128)(2,1)S(1)} %get-tuple-element.15), channel_id=1, source_target_pairs={{0,19},{1,18},{2,17},{3,16},{16,3},{17,2},{18,1},{19,0},{4,23},{5,... | collective-permute-start | bytes 405512 | tf_op jit(solution)/shard_map/ppermute | solution.py:341
  10.2 1.4 %collective-permute-start.4 = (bf16[528,128]{1,0:T(8,128)(2,1)S(1)}, bf16[528,128]{1,0:T(8,128)(2,1)S(1)}, u32[]{:S(2)}, u32[]{:S(2)}) collective-permute-start(bf16[528,128]{1,0:T(8,128)(2,1)S(1)} %get-tuple-element.16), channel_id=1, source_target_pairs={{0,17},{1,16},{2,19},{3,18},{16,1},{17,0},{18,3},{19,2},{4,21},{5,... | collective-permute-start | bytes 405512 | tf_op jit(solution)/shard_map/ppermute | solution.py:341
  11.6 1.4 %collective-permute-done.other_ref = bf16[768,256]{1,0:T(8,128)(2,1)S(1)} collective-permute-done((bf16[768,256]{1,0:T(8,128)(2,1)}, bf16[768,256]{1,0:T(8,128)(2,1)S(1)}, u32[]{:S(2)}, u32[]{:S(2)}) %collective-permute-start) | collective-permute-done | bytes 393248 | tf_op jit(solution)/shard_map/ppermute | solution.py:341
  13.0 3.3 %later.1 = (f32[512,1024]{1,0:T(8,128)S(1)}, bf16[528,128]{1,0:T(8,128)(2,1)S(1)}, bf16[528,128]{1,0:T(8,128)(2,1)S(1)}, bf16[528,128]{1,0:T(8,128)(2,1)S(1)}, bf16[528,128]{1,0:T(8,128)(2,1)S(1)}) custom-call(f32[16,512]{1,0:T(8,128)S(1)} %get-tuple-element.17.slots_ref, bf16[4,16,128]{2,1,0:T(8,128)(2,1)S(1)} %get-tuple-element.18.tiles_ref, ...), custom_call_target="tpu_custom_call" | custom-call | flops 1342177280 | bytes 3145728 | tf_op jit(solution)/shard_map/later/pallas_call | solution.py:391
  16.3 3.5 %collective-permute-start.5 = (bf16[528,128]{1,0:T(8,128)(2,1)S(1)}, bf16[528,128]{1,0:T(8,128)(2,1)S(1)}, u32[]{:S(2)}, u32[]{:S(2)}) collective-permute-start(bf16[528,128]{1,0:T(8,128)(2,1)S(1)} %get-tuple-element.21), channel_id=1, source_target_pairs={{0,2},{1,3},{2,0},{3,1},{16,18},{17,19},{18,16},{19,17},{4,6},{5,7... | collective-permute-start | bytes 405512 | tf_op jit(solution)/shard_map/ppermute | solution.py:341
  19.8 1.5 %collective-permute-start.7 = (bf16[528,128]{1,0:T(8,128)(2,1)S(1)}, bf16[528,128]{1,0:T(8,128)(2,1)S(1)}, u32[]{:S(2)}, u32[]{:S(2)}) collective-permute-start(bf16[528,128]{1,0:T(8,128)(2,1)S(1)} %get-tuple-element.23), channel_id=1, source_target_pairs={{0,16},{1,17},{2,18},{3,19},{16,0},{17,1},{18,2},{19,3},{4,20},{5,... | collective-permute-start | bytes 405512 | tf_op jit(solution)/shard_map/ppermute | solution.py:341
  21.4 0.0 collective-permute-start.6
  21.4 1.2 %collective-permute-done.4.rest_3_ = bf16[528,128]{1,0:T(8,128)(2,1)S(1)} collective-permute-done((bf16[528,128]{1,0:T(8,128)(2,1)S(1)}, bf16[528,128]{1,0:T(8,128)(2,1)S(1)}, u32[]{:S(2)}, u32[]{:S(2)}) %collective-permute-start.4) | collective-permute-done | bytes 135200 | tf_op jit(solution)/shard_map/ppermute | solution.py:341
  22.6 0.2 score.4.rest_5_
  22.8 2.5 %collective-permute-start.8 = (f32[8,128]{1,0:T(8,128)S(1)}, f32[8,128]{1,0:T(8,128)S(1)}, u32[]{:S(2)}, u32[]{:S(2)}) collective-permute-start(f32[8,128]{1,0:T(8,128)S(1)} %score.4.rest_5_), channel_id=1, source_target_pairs={{0,3},{1,2},{2,1},{3,0},{16,19},{17,18},{18,17},{19,16},{4,7},{5,6... | collective-permute-start | bytes 12296 | tf_op jit(solution)/shard_map/ppermute | solution.py:341
  25.3 1.1 %sum.1.rest_1_.grad_ref = f32[768,1024]{1,0:T(8,128)S(1)} custom-call(bf16[768,256]{1,0:T(8,128)(2,1)S(1)} %bitcast.19, bf16[768,256]{1,0:T(8,128)(2,1)S(1)} %collective-permute-done.other_ref, bf16[528,128]{1,0:T(8,128)(2,1)S(1)} %collective-permute-done.1.rest_0_, bf16[528,128]{1,0:T(8,128)(2,1)S(1)} %collective-permute-done.2.rest_1_, ...), custom_call_target="tpu_custom_call" | custom-call | flops 805306368 | bytes 3145728 | tf_op jit(solution)/shard_map/sum/pallas_call | solution.py:437
  26.4 3.8 %collective-permute-done.5.rest_0_ = bf16[528,128]{1,0:T(8,128)(2,1)S(1)} collective-permute-done((bf16[528,128]{1,0:T(8,128)(2,1)S(1)}, bf16[528,128]{1,0:T(8,128)(2,1)S(1)}, u32[]{:S(2)}, u32[]{:S(2)}) %collective-permute-start.5) | collective-permute-done | bytes 135200 | tf_op jit(solution)/shard_map/ppermute | solution.py:341
  30.2 0.1 score.6.rest_3_
  30.3 0.1 collective-permute-start.11
  30.4 0.1 score.5.rest_2_
  30.6 0.9 %collective-permute-start.10 = (f32[8,128]{1,0:T(8,128)S(1)}, f32[8,128]{1,0:T(8,128)S(1)}, u32[]{:S(2)}, u32[]{:S(2)}) collective-permute-start(f32[8,128]{1,0:T(8,128)S(1)} %merge.1.rest_1_.own_ref), channel_id=1, source_target_pairs={{0,16},{1,17},{2,18},{3,19},{16,0},{17,1},{18,2},{19,3},{4,20},{5,... | collective-permute-start | bytes 12296 | tf_op jit(solution)/shard_map/ppermute | solution.py:341
  31.5 0.7 %collective-permute-done.6.rest_0_.rest_1_ = bf16[528,128]{1,0:T(8,128)(2,1)S(1)} collective-permute-done((bf16[528,128]{1,0:T(8,128)(2,1)S(1)}, bf16[528,128]{1,0:T(8,128)(2,1)S(1)}, u32[]{:S(2)}, u32[]{:S(2)}) %collective-permute-start.6) | collective-permute-done | bytes 135200 | tf_op jit(solution)/shard_map/ppermute | solution.py:341
  32.2 0.1 score.7.rest_3_
  32.3 3.4 %collective-permute-start.12 = (f32[8,128]{1,0:T(8,128)S(1)}, f32[8,128]{1,0:T(8,128)S(1)}, u32[]{:S(2)}, u32[]{:S(2)}) collective-permute-start(f32[8,128]{1,0:T(8,128)S(1)} %score.7.rest_3_), channel_id=1, source_target_pairs={{0,18},{1,19},{2,16},{3,17},{16,2},{17,3},{18,0},{19,1},{4,22},{5,... | collective-permute-start | bytes 12296 | tf_op jit(solution)/shard_map/ppermute | solution.py:341
  35.8 3.2 %update.1 = f32[768,1024]{1,0:T(8,128)} custom-call(bf16[768,256]{1,0:T(8,128)(2,1)S(1)} %bitcast.20, bf16[768,256]{1,0:T(8,128)(2,1)S(1)} %collective-permute-done.other_ref, f32[768,1024]{1,0:T(8,128)S(1)} %sum.1.rest_1_.grad_ref, f32[768,1024]{1,0:T(8,128)S(1)} %bitcast.16, bf16[768,1024]{1,0:T(8,128)(2,1)S(1)} %bitcast.21, ...), custom_call_target="tpu_custom_call" | custom-call | flops 603979776 | bytes 12582912 | tf_op jit(solution)/shard_map/update/pallas_call | solution.py:465
  39.0 0.9 %combine.1 = f32[8,512]{1,0:T(8,128)} custom-call(s32[8,512]{1,0:T(8,128)S(1)} %bitcast.24, f32[16,512]{1,0:T(8,128)S(1)} %get-tuple-element.17.slots_ref, f32[8,128]{1,0:T(8,128)S(1)} %merge.1.rest_1_.own_ref, f32[8,128]{1,0:T(8,128)S(1)} %collective-permute-done.10.other_ref, f32[8,128]{1,0:T(8,128)S(1)} %collective-permute-done.11.own_far_ref, ...), custom_call_target="tpu_custom_call" | custom-call | flops 524288 | bytes 32768 | tf_op jit(solution)/shard_map/combine/pallas_call | solution.py:490
  (22 shorter events, 0.1 us)
Async XLA Ops:
  0.6 12.4 %copy-start.1 = (bf16[1,1,768,256]{3,2,1,0:T(8,128)(2,1)S(1)}, bf16[1,1,768,256]{3,2,1,0:T(8,128)(2,1)}, u32[]{:S(2)}) copy-start(bf16[1,1,768,256]{3,2,1,0:T(8,128)(2,1)} %param.10) | copy-start | bytes 1179652
  0.6 12.4 %collective-permute-start = (bf16[768,256]{1,0:T(8,128)(2,1)}, bf16[768,256]{1,0:T(8,128)(2,1)S(1)}, u32[]{:S(2)}, u32[]{:S(2)}) collective-permute-start(bf16[768,256]{1,0:T(8,128)(2,1)} %bitcast.17), channel_id=1, source_target_pairs={{0,16},{1,17},{2,18},{3,19},{16,0},{17,1},{18,2},{19,3},{4,20},{5,... | collective-permute-start | bytes 1179656 | tf_op jit(solution)/shard_map/ppermute | solution.py:341
  5.7 14.2 %collective-permute-start.1 = (bf16[528,128]{1,0:T(8,128)(2,1)S(1)}, bf16[528,128]{1,0:T(8,128)(2,1)S(1)}, u32[]{:S(2)}, u32[]{:S(2)}) collective-permute-start(bf16[528,128]{1,0:T(8,128)(2,1)S(1)} %get-tuple-element.13), channel_id=1, source_target_pairs={{0,3},{1,2},{2,1},{3,0},{16,19},{17,18},{18,17},{19,16},{4,7},{5,6... | collective-permute-start | bytes 405512 | tf_op jit(solution)/shard_map/ppermute | solution.py:341
  9.3 12.0 %collective-permute-start.2 = (bf16[528,128]{1,0:T(8,128)(2,1)S(1)}, bf16[528,128]{1,0:T(8,128)(2,1)S(1)}, u32[]{:S(2)}, u32[]{:S(2)}) collective-permute-start(bf16[528,128]{1,0:T(8,128)(2,1)S(1)} %get-tuple-element.14), channel_id=1, source_target_pairs={{0,1},{1,0},{2,3},{3,2},{16,17},{17,16},{18,19},{19,18},{4,5},{5,4... | collective-permute-start | bytes 405512 | tf_op jit(solution)/shard_map/ppermute | solution.py:341
  9.3 12.1 %collective-permute-start.3 = (bf16[528,128]{1,0:T(8,128)(2,1)S(1)}, bf16[528,128]{1,0:T(8,128)(2,1)S(1)}, u32[]{:S(2)}, u32[]{:S(2)}) collective-permute-start(bf16[528,128]{1,0:T(8,128)(2,1)S(1)} %get-tuple-element.15), channel_id=1, source_target_pairs={{0,19},{1,18},{2,17},{3,16},{16,3},{17,2},{18,1},{19,0},{4,23},{5,... | collective-permute-start | bytes 405512 | tf_op jit(solution)/shard_map/ppermute | solution.py:341
  10.2 12.4 %collective-permute-start.4 = (bf16[528,128]{1,0:T(8,128)(2,1)S(1)}, bf16[528,128]{1,0:T(8,128)(2,1)S(1)}, u32[]{:S(2)}, u32[]{:S(2)}) collective-permute-start(bf16[528,128]{1,0:T(8,128)(2,1)S(1)} %get-tuple-element.16), channel_id=1, source_target_pairs={{0,17},{1,16},{2,19},{3,18},{16,1},{17,0},{18,3},{19,2},{4,21},{5,... | collective-permute-start | bytes 405512 | tf_op jit(solution)/shard_map/ppermute | solution.py:341
  16.3 13.8 %collective-permute-start.5 = (bf16[528,128]{1,0:T(8,128)(2,1)S(1)}, bf16[528,128]{1,0:T(8,128)(2,1)S(1)}, u32[]{:S(2)}, u32[]{:S(2)}) collective-permute-start(bf16[528,128]{1,0:T(8,128)(2,1)S(1)} %get-tuple-element.21), channel_id=1, source_target_pairs={{0,2},{1,3},{2,0},{3,1},{16,18},{17,19},{18,16},{19,17},{4,6},{5,7... | collective-permute-start | bytes 405512 | tf_op jit(solution)/shard_map/ppermute | solution.py:341
  19.8 10.5 %collective-permute-start.7 = (bf16[528,128]{1,0:T(8,128)(2,1)S(1)}, bf16[528,128]{1,0:T(8,128)(2,1)S(1)}, u32[]{:S(2)}, u32[]{:S(2)}) collective-permute-start(bf16[528,128]{1,0:T(8,128)(2,1)S(1)} %get-tuple-element.23), channel_id=1, source_target_pairs={{0,16},{1,17},{2,18},{3,19},{16,0},{17,1},{18,2},{19,3},{4,20},{5,... | collective-permute-start | bytes 405512 | tf_op jit(solution)/shard_map/ppermute | solution.py:341
  21.4 10.8 %collective-permute-start.6 = (bf16[528,128]{1,0:T(8,128)(2,1)S(1)}, bf16[528,128]{1,0:T(8,128)(2,1)S(1)}, u32[]{:S(2)}, u32[]{:S(2)}) collective-permute-start(bf16[528,128]{1,0:T(8,128)(2,1)S(1)} %get-tuple-element.22), channel_id=1, source_target_pairs={{0,18},{1,19},{2,16},{3,17},{16,2},{17,3},{18,0},{19,1},{4,22},{5,... | collective-permute-start | bytes 405512 | tf_op jit(solution)/shard_map/ppermute | solution.py:341
  22.8 7.7 %collective-permute-start.8 = (f32[8,128]{1,0:T(8,128)S(1)}, f32[8,128]{1,0:T(8,128)S(1)}, u32[]{:S(2)}, u32[]{:S(2)}) collective-permute-start(f32[8,128]{1,0:T(8,128)S(1)} %score.4.rest_5_), channel_id=1, source_target_pairs={{0,3},{1,2},{2,1},{3,0},{16,19},{17,18},{18,17},{19,16},{4,7},{5,6... | collective-permute-start | bytes 12296 | tf_op jit(solution)/shard_map/ppermute | solution.py:341
  25.3 5.3 %collective-permute-start.9 = (f32[8,128]{1,0:T(8,128)S(1)}, f32[8,128]{1,0:T(8,128)S(1)}, u32[]{:S(2)}, u32[]{:S(2)}) collective-permute-start(f32[8,128]{1,0:T(8,128)S(1)} %score.4.rest_5_), channel_id=1, source_target_pairs={{0,1},{1,0},{2,3},{3,2},{16,17},{17,16},{18,19},{19,18},{4,5},{5,4... | collective-permute-start | bytes 12296 | tf_op jit(solution)/shard_map/ppermute | solution.py:341
  30.2 5.6 %copy-start.2 = (bf16[1,1,768,1024]{3,2,1,0:T(8,128)(2,1)S(1)}, bf16[1,1,768,1024]{3,2,1,0:T(8,128)(2,1)}, u32[]{:S(2)}) copy-start(bf16[1,1,768,1024]{3,2,1,0:T(8,128)(2,1)} %param.12) | copy-start | bytes 4718596
  30.2 5.6 %copy-start.3 = (bf16[1,1,768,1024]{3,2,1,0:T(8,128)(2,1)S(1)}, bf16[1,1,768,1024]{3,2,1,0:T(8,128)(2,1)}, u32[]{:S(2)}) copy-start(bf16[1,1,768,1024]{3,2,1,0:T(8,128)(2,1)} %param.13) | copy-start | bytes 4718596
  30.3 5.4 %copy-start = (f32[1,1,768,1024]{3,2,1,0:T(8,128)S(1)}, f32[1,1,768,1024]{3,2,1,0:T(8,128)}, u32[]{:S(2)}) copy-start(f32[1,1,768,1024]{3,2,1,0:T(8,128)} %param.11) | copy-start | bytes 9437188
  30.3 8.7 %collective-permute-start.11 = (f32[8,128]{1,0:T(8,128)S(1)}, f32[8,128]{1,0:T(8,128)S(1)}, u32[]{:S(2)}, u32[]{:S(2)}) collective-permute-start(f32[8,128]{1,0:T(8,128)S(1)} %score.6.rest_3_), channel_id=1, source_target_pairs={{0,2},{1,3},{2,0},{3,1},{16,18},{17,19},{18,16},{19,17},{4,6},{5,7... | collective-permute-start | bytes 12296 | tf_op jit(solution)/shard_map/ppermute | solution.py:341
  30.6 8.4 %collective-permute-start.10 = (f32[8,128]{1,0:T(8,128)S(1)}, f32[8,128]{1,0:T(8,128)S(1)}, u32[]{:S(2)}, u32[]{:S(2)}) collective-permute-start(f32[8,128]{1,0:T(8,128)S(1)} %merge.1.rest_1_.own_ref), channel_id=1, source_target_pairs={{0,16},{1,17},{2,18},{3,19},{16,0},{17,1},{18,2},{19,3},{4,20},{5,... | collective-permute-start | bytes 12296 | tf_op jit(solution)/shard_map/ppermute | solution.py:341
  32.3 6.6 %collective-permute-start.12 = (f32[8,128]{1,0:T(8,128)S(1)}, f32[8,128]{1,0:T(8,128)S(1)}, u32[]{:S(2)}, u32[]{:S(2)}) collective-permute-start(f32[8,128]{1,0:T(8,128)S(1)} %score.7.rest_3_), channel_id=1, source_target_pairs={{0,18},{1,19},{2,16},{3,17},{16,2},{17,3},{18,0},{19,1},{4,22},{5,... | collective-permute-start | bytes 12296 | tf_op jit(solution)/shard_map/ppermute | solution.py:341
  35.7 3.2 %copy-start.4 = (s32[1,512,8]{1,2,0:T(8,128)S(1)}, s32[1,512,8]{1,2,0:T(8,128)}, u32[]{:S(2)}) copy-start(s32[1,512,8]{1,2,0:T(8,128)} %param.9) | copy-start | bytes 49156

commit v14 on v13

--- a/solution.py
+++ b/solution.py
@@ -223,15 +223,10 @@
     grad_ref[...] = jnp.dot(scaled[...], rows[...], preferred_element_type=F32)
 
 
-def merge_kernel(steps, *rest):
-    refs, out_ref = rest[: len(steps)], rest[-1]
-    row = lax.broadcasted_iota(jnp.int32, out_ref.shape, 0)
-    me = ep_index()
-    table = jnp.zeros(out_ref.shape, F32)
-    for k, ref in zip(steps, refs):
-        line = jnp.sum(jnp.where(row == me, ref[...], 0.0), axis=0, keepdims=True)
-        table = jnp.where(row == k, line, table)
-    out_ref[...] = table
+def merge_kernel(cap, own_ref, other_ref, _, out_ref):
+    lane = lax.broadcasted_iota(jnp.int32, own_ref.shape, 1)
+    scores = own_ref[...] + pltpu.roll(other_ref[...], LANES - cap, axis=1)
+    out_ref[...] = jnp.where(lane < cap, scores, 0.0)
 
 
 def update_kernel(items, cap, own_ref, other_ref, grad_ref, master_ref, moment_ref, second_ref, *rest):
@@ -308,17 +303,20 @@
         copy.wait()
 
 
-def combine_kernel(
-    far, group, cap, ids_ref, slots_ref, own_ref, other_ref, own_far_ref, other_far_ref, out_ref
-):
+def combine_kernel(steps, group, cap, ids_ref, slots_ref, *rest):
+    refs, out_ref = iter(rest[:-1]), rest[-1]
     tokens = ids_ref.shape[1]
     me = ep_index()
-    lane = lax.broadcasted_iota(jnp.int32, own_ref.shape, 1)
-    row = lax.broadcasted_iota(jnp.int32, own_ref.shape, 0)
-    lines = jnp.where(lane < cap, own_ref[...], other_ref[...])
-    last = jnp.where(lane < cap, own_far_ref[...], other_far_ref[...])
-    last = jnp.sum(jnp.where(row == me, last, 0.0), axis=0, keepdims=True)
-    lines = jnp.where(row == far, last, lines)
+    shape = rest[0].shape
+    lane = lax.broadcasted_iota(jnp.int32, shape, 1)
+    row = lax.broadcasted_iota(jnp.int32, shape, 0)
+    lines = jnp.zeros(shape, F32)
+    for k, tiles in steps:
+        scores = next(refs)[...]
+        if tiles == 2:
+            scores = jnp.where(lane < cap, scores, next(refs)[...])
+        line = jnp.sum(jnp.where(row == me, scores, 0.0), axis=0, keepdims=True)
+        lines = jnp.where(row == k, line, lines)
     rest = jnp.zeros((LANES - lines.shape[0], LANES), F32)
     columns = jnp.concatenate([lines, rest], axis=0).T
     columns = columns[:cap] + columns[cap : 2 * cap]
@@ -426,12 +424,12 @@
             in_specs=specs(pltpu.VMEM, 1 + len(items)) + specs(pl.ANY, len(after)),
             out_specs=specs(pltpu.VMEM, 1)[0],
             compiler_params=params(),
-            cost_estimate=cost(2 * len(items) * cap * half, 6 * len(items) * cap * half),
+            cost_estimate=cost(2 * cap * half, 6 * cap * half),
             name="score",
         )(inner, *[arrived[item] for item in items], *after)
 
     first_scores = scored(first_items)
-    returned = [moved(first_scores, 0, k) for k in reversed(first)]
+    other_scores = moved(first_scores, 1, 0)
     added = [(0, far), (1, far), (1, 0)]
     summed = [item for item in order if item not in added]
     grad = pl.pallas_call(
@@ -447,19 +445,20 @@
         cost_estimate=cost(4 * slots * hid * half, 4 * hid * half),
         name="sum",
     )(own_hidden, other_hidden, *[arrived[item] for item in summed], first_scores)
-    far_scores = [scored([(0, far)], grad)]
-    own_scores = pl.pallas_call(
-        functools.partial(merge_kernel, first[::-1] + [0]),
+    merged = pl.pallas_call(
+        functools.partial(merge_kernel, cap),
         out_shape=tile,
-        in_specs=specs(pltpu.VMEM, group - 1) + specs(pl.ANY, 1),
+        in_specs=specs(pltpu.VMEM, 2) + specs(pl.ANY, 1),
         out_specs=specs(pltpu.VMEM, 1)[0],
         compiler_params=params(),
         name="merge",
-    )(*returned, scored([(0, 0), (1, 0)]), far_scores[0])
-    other_scores = moved(own_scores, 1, 0)
-    far_scores.append(scored([(1, far)], own_scores))
-    last_scores = far_scores[1]
-    far_scores = [moved(scores, side, far) for side, scores in enumerate(far_scores)]
+    )(first_scores, other_scores, grad)
+    returned = {k: [moved(merged, 0, k)] for k in first}
+    zero_scores = scored([(0, 0), (1, 0)], merged)
+    returned[0] = [zero_scores, moved(zero_scores, 1, 0)]
+    own_far = scored([(0, far)], merged)
+    last_scores = scored([(1, far)], zero_scores, own_far)
+    returned[far] = [moved(own_far, 0, far), moved(last_scores, 1, far)]
 
     block = min(hid, 2 * LANES)
     update = pl.pallas_call(
@@ -487,15 +486,18 @@
         *[arrived[item] for item in added],
         last_scores,
     )
+    shares = [array for arrays in returned.values() for array in arrays]
     router = pl.pallas_call(
-        functools.partial(combine_kernel, far, group, cap),
+        functools.partial(
+            combine_kernel, [(k, len(arrays)) for k, arrays in returned.items()], group, cap
+        ),
         out_shape=jax.ShapeDtypeStruct((top, tokens), F32),
-        in_specs=specs(pltpu.VMEM, 6),
+        in_specs=specs(pltpu.VMEM, 2 + len(shares)),
         out_specs=specs(pltpu.VMEM, 1)[0],
         compiler_params=params(),
         cost_estimate=cost(4 * slots * tokens, 8 * top * tokens),
         name="combine",
-    )(ids, slot_of, own_scores, other_scores, *far_scores)
+    )(ids, slot_of, *shares)
     return (update[None, None], router.T[None])
 
 

time: 40 us -> 39.5 us (0.988)
  waiting for transfers between devices: 7.11 us -> 5.41 us
  starting transfers between devices: 20.9 us -> 22.1 us
    ppermute x13 -> x14, waiting for transfers between devices: 7.11 us -> 5.41 us  [moved(): return lax.ppermute(array, ('pair', 'ep'), pairs)]
    ppermute x13 -> x14, starting transfers between devices: 20.9 us -> 22.1 us  [moved(): return lax.ppermute(array, ('pair', 'ep'), pairs)]
  transfers between devices with their start and end apart: 13 -> 14, of which waited for: 4 -> 5; matrix products, arithmetic and copies ran while one was open for 0% -> 0% of each run, Pallas kernels for 26% -> 26%
where the time goes in v14:
time: 39.5 us; the launch traced here: 39.3 us
  starting transfers between devices  22.1 us (56%)
  Pallas kernels  11.1 us (28%)
  waiting for transfers between devices  5.41 us (14%)
  between operations  0.72 us (2%)
    ppermute x14, starting transfers between devices, moved(): return lax.ppermute(array, ('pair', 'ep'), pairs)  22.1 us
    ppermute x14, waiting for transfers between devices, moved(): return lax.ppermute(array, ('pair', 'ep'), pairs)  5.41 us
    pallas_call x1, Pallas kernels, local(): pl.pallas_call(functools.partial(later_kernel, last_items, late, cap), ou...  3.33 us
    pallas_call x1, Pallas kernels, local(): pl.pallas_call(functools.partial(update_kernel, added, cap), out_shape=ja...  3.18 us
    pallas_call x1, Pallas kernels, local(): pl.pallas_call(functools.partial(route_kernel, first_items, first, group,...  1.99 us
    pallas_call x1, Pallas kernels, local(): pl.pallas_call(functools.partial(sum_kernel, summed, group, cap), out_sha...  1.12 us
    pallas_call x1, Pallas kernels, local(): pl.pallas_call(functools.partial(combine_kernel, [(k, len(arrays)) for k,...  0.87 us
  transfers between devices with their start and end apart: 14, of which 5 were waited for; matrix products, arithmetic and copies ran while one was open for 0% of the time, Pallas kernels for 26%

profile of v14, /device:TPU:0, one launch (start us, length us, event | category | flops | bytes accessed | tf_op | source)
XLA Modules:
  0.0 39.3 jit_solution(2745771710260963705)
XLA Ops:
  0.6 3.0 %collective-permute-start = (bf16[768,256]{1,0:T(8,128)(2,1)}, bf16[768,256]{1,0:T(8,128)(2,1)S(1)}, u32[]{:S(2)}, u32[]{:S(2)}) collective-permute-start(bf16[768,256]{1,0:T(8,128)(2,1)} %bitcast.17), channel_id=1, source_target_pairs={{0,16},{1,17},{2,18},{3,19},{16,0},{17,1},{18,2},{19,3},{4,20},{5,... | collective-permute-start | bytes 1179656 | tf_op jit(solution)/shard_map/ppermute | solution.py:339
  3.7 2.0 %route.1 = (f32[16,512]{1,0:T(8,128)S(1)}, bf16[4,16,128]{2,1,0:T(8,128)(2,1)S(1)}, bf16[528,128]{1,0:T(8,128)(2,1)S(1)}, bf16[528,128]{1,0:T(8,128)(2,1)S(1)}, ...) custom-call(s32[8,512]{1,0:T(8,128)} %bitcast.23, bf16[8,512]{1,0:T(8,128)(2,1)} %bitcast.29, ...), custom_call_target="tpu_custom_call" | custom-call | flops 536870912 | bytes 3145728 | tf_op jit(solution)/shard_map/route/pallas_call | solution.py:363
  5.7 3.7 %collective-permute-start.1 = (bf16[528,128]{1,0:T(8,128)(2,1)S(1)}, bf16[528,128]{1,0:T(8,128)(2,1)S(1)}, u32[]{:S(2)}, u32[]{:S(2)}) collective-permute-start(bf16[528,128]{1,0:T(8,128)(2,1)S(1)} %get-tuple-element.13), channel_id=1, source_target_pairs={{0,3},{1,2},{2,1},{3,0},{16,19},{17,18},{18,17},{19,16},{4,7},{5,6... | collective-permute-start | bytes 405512 | tf_op jit(solution)/shard_map/ppermute | solution.py:339
  9.3 0.8 %collective-permute-start.3 = (bf16[528,128]{1,0:T(8,128)(2,1)S(1)}, bf16[528,128]{1,0:T(8,128)(2,1)S(1)}, u32[]{:S(2)}, u32[]{:S(2)}) collective-permute-start(bf16[528,128]{1,0:T(8,128)(2,1)S(1)} %get-tuple-element.15), channel_id=1, source_target_pairs={{0,19},{1,18},{2,17},{3,16},{16,3},{17,2},{18,1},{19,0},{4,23},{5,... | collective-permute-start | bytes 405512 | tf_op jit(solution)/shard_map/ppermute | solution.py:339
  10.2 1.4 %collective-permute-start.4 = (bf16[528,128]{1,0:T(8,128)(2,1)S(1)}, bf16[528,128]{1,0:T(8,128)(2,1)S(1)}, u32[]{:S(2)}, u32[]{:S(2)}) collective-permute-start(bf16[528,128]{1,0:T(8,128)(2,1)S(1)} %get-tuple-element.16), channel_id=1, source_target_pairs={{0,17},{1,16},{2,19},{3,18},{16,1},{17,0},{18,3},{19,2},{4,21},{5,... | collective-permute-start | bytes 405512 | tf_op jit(solution)/shard_map/ppermute | solution.py:339
  11.6 1.4 %collective-permute-done.other_ref = bf16[768,256]{1,0:T(8,128)(2,1)S(1)} collective-permute-done((bf16[768,256]{1,0:T(8,128)(2,1)}, bf16[768,256]{1,0:T(8,128)(2,1)S(1)}, u32[]{:S(2)}, u32[]{:S(2)}) %collective-permute-start) | collective-permute-done | bytes 393248 | tf_op jit(solution)/shard_map/ppermute | solution.py:339
  13.0 3.3 %later.1 = (f32[512,1024]{1,0:T(8,128)S(1)}, bf16[528,128]{1,0:T(8,128)(2,1)S(1)}, bf16[528,128]{1,0:T(8,128)(2,1)S(1)}, bf16[528,128]{1,0:T(8,128)(2,1)S(1)}, bf16[528,128]{1,0:T(8,128)(2,1)S(1)}) custom-call(f32[16,512]{1,0:T(8,128)S(1)} %get-tuple-element.17.slots_ref, bf16[4,16,128]{2,1,0:T(8,128)(2,1)S(1)} %get-tuple-element.18.tiles_ref, ...), custom_call_target="tpu_custom_call" | custom-call | flops 1342177280 | bytes 3145728 | tf_op jit(solution)/shard_map/later/pallas_call | solution.py:389
  16.3 3.5 %collective-permute-start.5 = (bf16[528,128]{1,0:T(8,128)(2,1)S(1)}, bf16[528,128]{1,0:T(8,128)(2,1)S(1)}, u32[]{:S(2)}, u32[]{:S(2)}) collective-permute-start(bf16[528,128]{1,0:T(8,128)(2,1)S(1)} %get-tuple-element.21), channel_id=1, source_target_pairs={{0,2},{1,3},{2,0},{3,1},{16,18},{17,19},{18,16},{19,17},{4,6},{5,7... | collective-permute-start | bytes 405512 | tf_op jit(solution)/shard_map/ppermute | solution.py:339
  19.8 1.5 %collective-permute-start.7 = (bf16[528,128]{1,0:T(8,128)(2,1)S(1)}, bf16[528,128]{1,0:T(8,128)(2,1)S(1)}, u32[]{:S(2)}, u32[]{:S(2)}) collective-permute-start(bf16[528,128]{1,0:T(8,128)(2,1)S(1)} %get-tuple-element.23), channel_id=1, source_target_pairs={{0,16},{1,17},{2,18},{3,19},{16,0},{17,1},{18,2},{19,3},{4,20},{5,... | collective-permute-start | bytes 405512 | tf_op jit(solution)/shard_map/ppermute | solution.py:339
  21.4 1.2 %collective-permute-done.4.rest_3_ = bf16[528,128]{1,0:T(8,128)(2,1)S(1)} collective-permute-done((bf16[528,128]{1,0:T(8,128)(2,1)S(1)}, bf16[528,128]{1,0:T(8,128)(2,1)S(1)}, u32[]{:S(2)}, u32[]{:S(2)}) %collective-permute-start.4) | collective-permute-done | bytes 135200 | tf_op jit(solution)/shard_map/ppermute | solution.py:339
  22.6 0.2 score.4.rest_5_.own_ref
  22.8 1.1 %collective-permute-start.8 = (f32[8,128]{1,0:T(8,128)S(1)}, f32[8,128]{1,0:T(8,128)S(1)}, u32[]{:S(2)}, u32[]{:S(2)}) collective-permute-start(f32[8,128]{1,0:T(8,128)S(1)} %score.4.rest_5_.own_ref), channel_id=1, source_target_pairs={{0,16},{1,17},{2,18},{3,19},{16,0},{17,1},{18,2},{19,3},{4,20},{5,... | collective-permute-start | bytes 12296 | tf_op jit(solution)/shard_map/ppermute | solution.py:339
  23.9 1.1 %sum.1._.grad_ref = f32[768,1024]{1,0:T(8,128)S(1)} custom-call(bf16[768,256]{1,0:T(8,128)(2,1)S(1)} %bitcast.19, bf16[768,256]{1,0:T(8,128)(2,1)S(1)} %collective-permute-done.other_ref, bf16[528,128]{1,0:T(8,128)(2,1)S(1)} %collective-permute-done.1.rest_0_, bf16[528,128]{1,0:T(8,128)(2,1)S(1)} %collective-permute-done.2.rest_1_, ...), custom_call_target="tpu_custom_call" | custom-call | flops 805306368 | bytes 3145728 | tf_op jit(solution)/shard_map/sum/pallas_call | solution.py:435
  25.1 1.4 %collective-permute-done.8.other_ref = f32[8,128]{1,0:T(8,128)S(1)} collective-permute-done((f32[8,128]{1,0:T(8,128)S(1)}, f32[8,128]{1,0:T(8,128)S(1)}, u32[]{:S(2)}, u32[]{:S(2)}) %collective-permute-start.8) | collective-permute-done | bytes 4128 | tf_op jit(solution)/shard_map/ppermute | solution.py:339
  26.6 2.4 %collective-permute-start.10 = (f32[8,128]{1,0:T(8,128)S(1)}, f32[8,128]{1,0:T(8,128)S(1)}, u32[]{:S(2)}, u32[]{:S(2)}) collective-permute-start(f32[8,128]{1,0:T(8,128)S(1)} %merge.1.rest_2_.rest_1_), channel_id=1, source_target_pairs={{0,3},{1,2},{2,1},{3,0},{16,19},{17,18},{18,17},{19,16},{4,7},{5,6... | collective-permute-start | bytes 12296 | tf_op jit(solution)/shard_map/ppermute | solution.py:339
  28.9 1.2 %collective-permute-done.5.rest_0_ = bf16[528,128]{1,0:T(8,128)(2,1)S(1)} collective-permute-done((bf16[528,128]{1,0:T(8,128)(2,1)S(1)}, bf16[528,128]{1,0:T(8,128)(2,1)S(1)}, u32[]{:S(2)}, u32[]{:S(2)}) %collective-permute-start.5) | collective-permute-done | bytes 135200 | tf_op jit(solution)/shard_map/ppermute | solution.py:339
  30.1 0.1 score.6.rest_2_
  30.3 0.9 %collective-permute-start.12 = (f32[8,128]{1,0:T(8,128)S(1)}, f32[8,128]{1,0:T(8,128)S(1)}, u32[]{:S(2)}, u32[]{:S(2)}) collective-permute-start(f32[8,128]{1,0:T(8,128)S(1)} %score.6.rest_2_), channel_id=1, source_target_pairs={{0,2},{1,3},{2,0},{3,1},{16,18},{17,19},{18,16},{19,17},{4,6},{5,7... | collective-permute-start | bytes 12296 | tf_op jit(solution)/shard_map/ppermute | solution.py:339
  31.2 0.1 score.5.rest_1_.rest_2_
  31.3 1.6 %collective-permute-start.11 = (f32[8,128]{1,0:T(8,128)S(1)}, f32[8,128]{1,0:T(8,128)S(1)}, u32[]{:S(2)}, u32[]{:S(2)}) collective-permute-start(f32[8,128]{1,0:T(8,128)S(1)} %score.5.rest_1_.rest_2_), channel_id=1, source_target_pairs={{0,16},{1,17},{2,18},{3,19},{16,0},{17,1},{18,2},{19,3},{4,20},{5,... | collective-permute-start | bytes 12296 | tf_op jit(solution)/shard_map/ppermute | solution.py:339
  33.0 2.1 %collective-permute-start.13 = (f32[8,128]{1,0:T(8,128)S(1)}, f32[8,128]{1,0:T(8,128)S(1)}, u32[]{:S(2)}, u32[]{:S(2)}) collective-permute-start(f32[8,128]{1,0:T(8,128)S(1)} %score.7.rest_3_), channel_id=1, source_target_pairs={{0,18},{1,19},{2,16},{3,17},{16,2},{17,3},{18,0},{19,1},{4,22},{5,... | collective-permute-start | bytes 12296 | tf_op jit(solution)/shard_map/ppermute | solution.py:339
  35.1 3.2 %update.1 = f32[768,1024]{1,0:T(8,128)} custom-call(bf16[768,256]{1,0:T(8,128)(2,1)S(1)} %bitcast.20, bf16[768,256]{1,0:T(8,128)(2,1)S(1)} %collective-permute-done.other_ref, f32[768,1024]{1,0:T(8,128)S(1)} %sum.1._.grad_ref, f32[768,1024]{1,0:T(8,128)S(1)} %bitcast.16, bf16[768,1024]{1,0:T(8,128)(2,1)S(1)} %bitcast.21, bf16[768,1024]{1,0:T(8,128)(2,1)S(1)} %bitcast.22, ...), custom_call_target="tpu_custom_call" | custom-call | flops 603979776 | bytes 12582912 | tf_op jit(solution)/shard_map/update/pallas_call | solution.py:464
  38.3 0.2 collective-permute-done.13.rest_5_
  38.5 0.9 %combine.1 = f32[8,512]{1,0:T(8,128)} custom-call(s32[8,512]{1,0:T(8,128)S(1)} %bitcast.24, f32[16,512]{1,0:T(8,128)S(1)} %get-tuple-element.17.slots_ref, f32[8,128]{1,0:T(8,128)S(1)} %collective-permute-done.9.rest_0_, f32[8,128]{1,0:T(8,128)S(1)} %collective-permute-done.10.rest_1_, f32[8,128]{1,0:T(8,128)S(1)} %score.5.rest_1_.rest_2_, ...), custom_call_target="tpu_custom_call" | custom-call | flops 524288 | bytes 32768 | tf_op jit(solution)/shard_map/combine/pallas_call | solution.py:490
  (24 shorter events, 0.2 us)
Async XLA Ops:
  0.6 12.4 %copy-start.1 = (bf16[1,1,768,256]{3,2,1,0:T(8,128)(2,1)S(1)}, bf16[1,1,768,256]{3,2,1,0:T(8,128)(2,1)}, u32[]{:S(2)}) copy-start(bf16[1,1,768,256]{3,2,1,0:T(8,128)(2,1)} %param.10) | copy-start | bytes 1179652
  0.6 12.4 %collective-permute-start = (bf16[768,256]{1,0:T(8,128)(2,1)}, bf16[768,256]{1,0:T(8,128)(2,1)S(1)}, u32[]{:S(2)}, u32[]{:S(2)}) collective-permute-start(bf16[768,256]{1,0:T(8,128)(2,1)} %bitcast.17), channel_id=1, source_target_pairs={{0,16},{1,17},{2,18},{3,19},{16,0},{17,1},{18,2},{19,3},{4,20},{5,... | collective-permute-start | bytes 1179656 | tf_op jit(solution)/shard_map/ppermute | solution.py:339
  5.7 14.2 %collective-permute-start.1 = (bf16[528,128]{1,0:T(8,128)(2,1)S(1)}, bf16[528,128]{1,0:T(8,128)(2,1)S(1)}, u32[]{:S(2)}, u32[]{:S(2)}) collective-permute-start(bf16[528,128]{1,0:T(8,128)(2,1)S(1)} %get-tuple-element.13), channel_id=1, source_target_pairs={{0,3},{1,2},{2,1},{3,0},{16,19},{17,18},{18,17},{19,16},{4,7},{5,6... | collective-permute-start | bytes 405512 | tf_op jit(solution)/shard_map/ppermute | solution.py:339
  9.3 12.0 %collective-permute-start.2 = (bf16[528,128]{1,0:T(8,128)(2,1)S(1)}, bf16[528,128]{1,0:T(8,128)(2,1)S(1)}, u32[]{:S(2)}, u32[]{:S(2)}) collective-permute-start(bf16[528,128]{1,0:T(8,128)(2,1)S(1)} %get-tuple-element.14), channel_id=1, source_target_pairs={{0,1},{1,0},{2,3},{3,2},{16,17},{17,16},{18,19},{19,18},{4,5},{5,4... | collective-permute-start | bytes 405512 | tf_op jit(solution)/shard_map/ppermute | solution.py:339
  9.3 12.1 %collective-permute-start.3 = (bf16[528,128]{1,0:T(8,128)(2,1)S(1)}, bf16[528,128]{1,0:T(8,128)(2,1)S(1)}, u32[]{:S(2)}, u32[]{:S(2)}) collective-permute-start(bf16[528,128]{1,0:T(8,128)(2,1)S(1)} %get-tuple-element.15), channel_id=1, source_target_pairs={{0,19},{1,18},{2,17},{3,16},{16,3},{17,2},{18,1},{19,0},{4,23},{5,... | collective-permute-start | bytes 405512 | tf_op jit(solution)/shard_map/ppermute | solution.py:339
  10.2 12.4 %collective-permute-start.4 = (bf16[528,128]{1,0:T(8,128)(2,1)S(1)}, bf16[528,128]{1,0:T(8,128)(2,1)S(1)}, u32[]{:S(2)}, u32[]{:S(2)}) collective-permute-start(bf16[528,128]{1,0:T(8,128)(2,1)S(1)} %get-tuple-element.16), channel_id=1, source_target_pairs={{0,17},{1,16},{2,19},{3,18},{16,1},{17,0},{18,3},{19,2},{4,21},{5,... | collective-permute-start | bytes 405512 | tf_op jit(solution)/shard_map/ppermute | solution.py:339
  16.3 13.8 %collective-permute-start.5 = (bf16[528,128]{1,0:T(8,128)(2,1)S(1)}, bf16[528,128]{1,0:T(8,128)(2,1)S(1)}, u32[]{:S(2)}, u32[]{:S(2)}) collective-permute-start(bf16[528,128]{1,0:T(8,128)(2,1)S(1)} %get-tuple-element.21), channel_id=1, source_target_pairs={{0,2},{1,3},{2,0},{3,1},{16,18},{17,19},{18,16},{19,17},{4,6},{5,7... | collective-permute-start | bytes 405512 | tf_op jit(solution)/shard_map/ppermute | solution.py:339
  19.8 11.3 %collective-permute-start.7 = (bf16[528,128]{1,0:T(8,128)(2,1)S(1)}, bf16[528,128]{1,0:T(8,128)(2,1)S(1)}, u32[]{:S(2)}, u32[]{:S(2)}) collective-permute-start(bf16[528,128]{1,0:T(8,128)(2,1)S(1)} %get-tuple-element.23), channel_id=1, source_target_pairs={{0,16},{1,17},{2,18},{3,19},{16,0},{17,1},{18,2},{19,3},{4,20},{5,... | collective-permute-start | bytes 405512 | tf_op jit(solution)/shard_map/ppermute | solution.py:339
  21.4 11.5 %collective-permute-start.6 = (bf16[528,128]{1,0:T(8,128)(2,1)S(1)}, bf16[528,128]{1,0:T(8,128)(2,1)S(1)}, u32[]{:S(2)}, u32[]{:S(2)}) collective-permute-start(bf16[528,128]{1,0:T(8,128)(2,1)S(1)} %get-tuple-element.22), channel_id=1, source_target_pairs={{0,18},{1,19},{2,16},{3,17},{16,2},{17,3},{18,0},{19,1},{4,22},{5,... | collective-permute-start | bytes 405512 | tf_op jit(solution)/shard_map/ppermute | solution.py:339
  22.8 3.7 %collective-permute-start.8 = (f32[8,128]{1,0:T(8,128)S(1)}, f32[8,128]{1,0:T(8,128)S(1)}, u32[]{:S(2)}, u32[]{:S(2)}) collective-permute-start(f32[8,128]{1,0:T(8,128)S(1)} %score.4.rest_5_.own_ref), channel_id=1, source_target_pairs={{0,16},{1,17},{2,18},{3,19},{16,0},{17,1},{18,2},{19,3},{4,20},{5,... | collective-permute-start | bytes 12296 | tf_op jit(solution)/shard_map/ppermute | solution.py:339
  26.6 11.7 %collective-permute-start.10 = (f32[8,128]{1,0:T(8,128)S(1)}, f32[8,128]{1,0:T(8,128)S(1)}, u32[]{:S(2)}, u32[]{:S(2)}) collective-permute-start(f32[8,128]{1,0:T(8,128)S(1)} %merge.1.rest_2_.rest_1_), channel_id=1, source_target_pairs={{0,3},{1,2},{2,1},{3,0},{16,19},{17,18},{18,17},{19,16},{4,7},{5,6... | collective-permute-start | bytes 12296 | tf_op jit(solution)/shard_map/ppermute | solution.py:339
  28.9 9.4 %collective-permute-start.9 = (f32[8,128]{1,0:T(8,128)S(1)}, f32[8,128]{1,0:T(8,128)S(1)}, u32[]{:S(2)}, u32[]{:S(2)}) collective-permute-start(f32[8,128]{1,0:T(8,128)S(1)} %merge.1.rest_2_.rest_1_), channel_id=1, source_target_pairs={{0,1},{1,0},{2,3},{3,2},{16,17},{17,16},{18,19},{19,18},{4,5},{5,4... | collective-permute-start | bytes 12296 | tf_op jit(solution)/shard_map/ppermute | solution.py:339
  30.1 5.0 %copy-start.2 = (bf16[1,1,768,1024]{3,2,1,0:T(8,128)(2,1)S(1)}, bf16[1,1,768,1024]{3,2,1,0:T(8,128)(2,1)}, u32[]{:S(2)}) copy-start(bf16[1,1,768,1024]{3,2,1,0:T(8,128)(2,1)} %param.12) | copy-start | bytes 4718596
  30.1 5.0 %copy-start.3 = (bf16[1,1,768,1024]{3,2,1,0:T(8,128)(2,1)S(1)}, bf16[1,1,768,1024]{3,2,1,0:T(8,128)(2,1)}, u32[]{:S(2)}) copy-start(bf16[1,1,768,1024]{3,2,1,0:T(8,128)(2,1)} %param.13) | copy-start | bytes 4718596
  30.2 4.9 %copy-start = (f32[1,1,768,1024]{3,2,1,0:T(8,128)S(1)}, f32[1,1,768,1024]{3,2,1,0:T(8,128)}, u32[]{:S(2)}) copy-start(f32[1,1,768,1024]{3,2,1,0:T(8,128)} %param.11) | copy-start | bytes 9437188
  30.3 8.2 %collective-permute-start.12 = (f32[8,128]{1,0:T(8,128)S(1)}, f32[8,128]{1,0:T(8,128)S(1)}, u32[]{:S(2)}, u32[]{:S(2)}) collective-permute-start(f32[8,128]{1,0:T(8,128)S(1)} %score.6.rest_2_), channel_id=1, source_target_pairs={{0,2},{1,3},{2,0},{3,1},{16,18},{17,19},{18,16},{19,17},{4,6},{5,7... | collective-permute-start | bytes 12296 | tf_op jit(solution)/shard_map/ppermute | solution.py:339
  31.3 7.1 %collective-permute-start.11 = (f32[8,128]{1,0:T(8,128)S(1)}, f32[8,128]{1,0:T(8,128)S(1)}, u32[]{:S(2)}, u32[]{:S(2)}) collective-permute-start(f32[8,128]{1,0:T(8,128)S(1)} %score.5.rest_1_.rest_2_), channel_id=1, source_target_pairs={{0,16},{1,17},{2,18},{3,19},{16,0},{17,1},{18,2},{19,3},{4,20},{5,... | collective-permute-start | bytes 12296 | tf_op jit(solution)/shard_map/ppermute | solution.py:339
  33.0 5.5 %collective-permute-start.13 = (f32[8,128]{1,0:T(8,128)S(1)}, f32[8,128]{1,0:T(8,128)S(1)}, u32[]{:S(2)}, u32[]{:S(2)}) collective-permute-start(f32[8,128]{1,0:T(8,128)S(1)} %score.7.rest_3_), channel_id=1, source_target_pairs={{0,18},{1,19},{2,16},{3,17},{16,2},{17,3},{18,0},{19,1},{4,22},{5,... | collective-permute-start | bytes 12296 | tf_op jit(solution)/shard_map/ppermute | solution.py:339
  35.1 3.4 %copy-start.4 = (s32[1,512,8]{1,2,0:T(8,128)S(1)}, s32[1,512,8]{1,2,0:T(8,128)}, u32[]{:S(2)}) copy-start(s32[1,512,8]{1,2,0:T(8,128)} %param.9) | copy-start | bytes 49156

commit v15 on v14

--- a/solution.py
+++ b/solution.py
@@ -456,8 +456,8 @@
     returned = {k: [moved(merged, 0, k)] for k in first}
     zero_scores = scored([(0, 0), (1, 0)], merged)
     returned[0] = [zero_scores, moved(zero_scores, 1, 0)]
-    own_far = scored([(0, far)], merged)
-    last_scores = scored([(1, far)], zero_scores, own_far)
+    own_far = scored([(0, far)], zero_scores)
+    last_scores = scored([(1, far)], own_far)
     returned[far] = [moved(own_far, 0, far), moved(last_scores, 1, far)]
 
     block = min(hid, 2 * LANES)

time: 39.5 us -> 39.4 us (level)
  waiting for transfers between devices: 5.41 us -> 4.98 us
    ppermute x14, waiting for transfers between devices: 5.41 us -> 4.98 us  [moved(): return lax.ppermute(array, ('pair', 'ep'), pairs)]
  transfers between devices with their start and end apart: 14 -> 14, of which waited for: 5 -> 4; matrix products, arithmetic and copies ran while one was open for 0% -> 0% of each run, Pallas kernels for 26% -> 26%
where the time goes in v15:
time: 39.4 us; the launch traced here: 39.3 us
  starting transfers between devices  22.4 us (57%)
  Pallas kernels  11.1 us (28%)
  waiting for transfers between devices  4.98 us (13%)
  between operations  0.73 us (2%)
    ppermute x14, starting transfers between devices, moved(): return lax.ppermute(array, ('pair', 'ep'), pairs)  22.4 us
    ppermute x14, waiting for transfers between devices, moved(): return lax.ppermute(array, ('pair', 'ep'), pairs)  4.98 us
    pallas_call x1, Pallas kernels, local(): pl.pallas_call(functools.partial(later_kernel, last_items, late, cap), ou...  3.33 us
    pallas_call x1, Pallas kernels, local(): pl.pallas_call(functools.partial(update_kernel, added, cap), out_shape=ja...  3.18 us
    pallas_call x1, Pallas kernels, local(): pl.pallas_call(functools.partial(route_kernel, first_items, first, group,...  1.99 us
    pallas_call x1, Pallas kernels, local(): pl.pallas_call(functools.partial(sum_kernel, summed, group, cap), out_sha...  1.13 us
    pallas_call x1, Pallas kernels, local(): pl.pallas_call(functools.partial(combine_kernel, [(k, len(arrays)) for k,...  0.87 us
  transfers between devices with their start and end apart: 14, of which 4 were waited for; matrix products, arithmetic and copies ran while one was open for 0% of the time, Pallas kernels for 26%

profile of v15, /device:TPU:0, one launch (start us, length us, event | category | flops | bytes accessed | tf_op | source)
XLA Modules:
  0.0 39.3 jit_solution(4351508070086397658)
XLA Ops:
  0.6 3.0 %collective-permute-start = (bf16[768,256]{1,0:T(8,128)(2,1)}, bf16[768,256]{1,0:T(8,128)(2,1)S(1)}, u32[]{:S(2)}, u32[]{:S(2)}) collective-permute-start(bf16[768,256]{1,0:T(8,128)(2,1)} %bitcast.17), channel_id=1, source_target_pairs={{0,16},{1,17},{2,18},{3,19},{16,0},{17,1},{18,2},{19,3},{4,20},{5,... | collective-permute-start | bytes 1179656 | tf_op jit(solution)/shard_map/ppermute | solution.py:339
  3.7 2.0 %route.1 = (f32[16,512]{1,0:T(8,128)S(1)}, bf16[4,16,128]{2,1,0:T(8,128)(2,1)S(1)}, bf16[528,128]{1,0:T(8,128)(2,1)S(1)}, bf16[528,128]{1,0:T(8,128)(2,1)S(1)}, ...) custom-call(s32[8,512]{1,0:T(8,128)} %bitcast.23, bf16[8,512]{1,0:T(8,128)(2,1)} %bitcast.29, ...), custom_call_target="tpu_custom_call" | custom-call | flops 536870912 | bytes 3145728 | tf_op jit(solution)/shard_map/route/pallas_call | solution.py:363
  5.7 3.7 %collective-permute-start.1 = (bf16[528,128]{1,0:T(8,128)(2,1)S(1)}, bf16[528,128]{1,0:T(8,128)(2,1)S(1)}, u32[]{:S(2)}, u32[]{:S(2)}) collective-permute-start(bf16[528,128]{1,0:T(8,128)(2,1)S(1)} %get-tuple-element.13), channel_id=1, source_target_pairs={{0,3},{1,2},{2,1},{3,0},{16,19},{17,18},{18,17},{19,16},{4,7},{5,6... | collective-permute-start | bytes 405512 | tf_op jit(solution)/shard_map/ppermute | solution.py:339
  9.3 0.8 %collective-permute-start.3 = (bf16[528,128]{1,0:T(8,128)(2,1)S(1)}, bf16[528,128]{1,0:T(8,128)(2,1)S(1)}, u32[]{:S(2)}, u32[]{:S(2)}) collective-permute-start(bf16[528,128]{1,0:T(8,128)(2,1)S(1)} %get-tuple-element.15), channel_id=1, source_target_pairs={{0,19},{1,18},{2,17},{3,16},{16,3},{17,2},{18,1},{19,0},{4,23},{5,... | collective-permute-start | bytes 405512 | tf_op jit(solution)/shard_map/ppermute | solution.py:339
  10.2 1.4 %collective-permute-start.4 = (bf16[528,128]{1,0:T(8,128)(2,1)S(1)}, bf16[528,128]{1,0:T(8,128)(2,1)S(1)}, u32[]{:S(2)}, u32[]{:S(2)}) collective-permute-start(bf16[528,128]{1,0:T(8,128)(2,1)S(1)} %get-tuple-element.16), channel_id=1, source_target_pairs={{0,17},{1,16},{2,19},{3,18},{16,1},{17,0},{18,3},{19,2},{4,21},{5,... | collective-permute-start | bytes 405512 | tf_op jit(solution)/shard_map/ppermute | solution.py:339
  11.6 1.4 %collective-permute-done.other_ref = bf16[768,256]{1,0:T(8,128)(2,1)S(1)} collective-permute-done((bf16[768,256]{1,0:T(8,128)(2,1)}, bf16[768,256]{1,0:T(8,128)(2,1)S(1)}, u32[]{:S(2)}, u32[]{:S(2)}) %collective-permute-start) | collective-permute-done | bytes 393248 | tf_op jit(solution)/shard_map/ppermute | solution.py:339
  13.0 3.3 %later.1 = (f32[512,1024]{1,0:T(8,128)S(1)}, bf16[528,128]{1,0:T(8,128)(2,1)S(1)}, bf16[528,128]{1,0:T(8,128)(2,1)S(1)}, bf16[528,128]{1,0:T(8,128)(2,1)S(1)}, bf16[528,128]{1,0:T(8,128)(2,1)S(1)}) custom-call(f32[16,512]{1,0:T(8,128)S(1)} %get-tuple-element.17.slots_ref, bf16[4,16,128]{2,1,0:T(8,128)(2,1)S(1)} %get-tuple-element.18.tiles_ref, ...), custom_call_target="tpu_custom_call" | custom-call | flops 1342177280 | bytes 3145728 | tf_op jit(solution)/shard_map/later/pallas_call | solution.py:389
  16.3 1.8 %collective-permute-start.7 = (bf16[528,128]{1,0:T(8,128)(2,1)S(1)}, bf16[528,128]{1,0:T(8,128)(2,1)S(1)}, u32[]{:S(2)}, u32[]{:S(2)}) collective-permute-start(bf16[528,128]{1,0:T(8,128)(2,1)S(1)} %get-tuple-element.23), channel_id=1, source_target_pairs={{0,16},{1,17},{2,18},{3,19},{16,0},{17,1},{18,2},{19,3},{4,20},{5,... | collective-permute-start | bytes 405512 | tf_op jit(solution)/shard_map/ppermute | solution.py:339
  18.1 3.2 %collective-permute-start.5 = (bf16[528,128]{1,0:T(8,128)(2,1)S(1)}, bf16[528,128]{1,0:T(8,128)(2,1)S(1)}, u32[]{:S(2)}, u32[]{:S(2)}) collective-permute-start(bf16[528,128]{1,0:T(8,128)(2,1)S(1)} %get-tuple-element.21), channel_id=1, source_target_pairs={{0,2},{1,3},{2,0},{3,1},{16,18},{17,19},{18,16},{19,17},{4,6},{5,7... | collective-permute-start | bytes 405512 | tf_op jit(solution)/shard_map/ppermute | solution.py:339
  21.4 1.3 %collective-permute-done.4.rest_3_ = bf16[528,128]{1,0:T(8,128)(2,1)S(1)} collective-permute-done((bf16[528,128]{1,0:T(8,128)(2,1)S(1)}, bf16[528,128]{1,0:T(8,128)(2,1)S(1)}, u32[]{:S(2)}, u32[]{:S(2)}) %collective-permute-start.4) | collective-permute-done | bytes 135200 | tf_op jit(solution)/shard_map/ppermute | solution.py:339
  22.6 0.2 score.4.rest_5_.own_ref
  22.8 1.5 %collective-permute-start.8 = (f32[8,128]{1,0:T(8,128)S(1)}, f32[8,128]{1,0:T(8,128)S(1)}, u32[]{:S(2)}, u32[]{:S(2)}) collective-permute-start(f32[8,128]{1,0:T(8,128)S(1)} %score.4.rest_5_.own_ref), channel_id=1, source_target_pairs={{0,16},{1,17},{2,18},{3,19},{16,0},{17,1},{18,2},{19,3},{4,20},{5,... | collective-permute-start | bytes 12296 | tf_op jit(solution)/shard_map/ppermute | solution.py:339
  24.3 1.1 %sum.1._.grad_ref = f32[768,1024]{1,0:T(8,128)S(1)} custom-call(bf16[768,256]{1,0:T(8,128)(2,1)S(1)} %bitcast.19, bf16[768,256]{1,0:T(8,128)(2,1)S(1)} %collective-permute-done.other_ref, bf16[528,128]{1,0:T(8,128)(2,1)S(1)} %collective-permute-done.1.rest_0_, bf16[528,128]{1,0:T(8,128)(2,1)S(1)} %collective-permute-done.2.rest_1_, ...), custom_call_target="tpu_custom_call" | custom-call | flops 805306368 | bytes 3145728 | tf_op jit(solution)/shard_map/sum/pallas_call | solution.py:435
  25.5 1.0 %collective-permute-done.8.other_ref = f32[8,128]{1,0:T(8,128)S(1)} collective-permute-done((f32[8,128]{1,0:T(8,128)S(1)}, f32[8,128]{1,0:T(8,128)S(1)}, u32[]{:S(2)}, u32[]{:S(2)}) %collective-permute-start.8) | collective-permute-done | bytes 4128 | tf_op jit(solution)/shard_map/ppermute | solution.py:339
  26.6 2.4 %collective-permute-start.10 = (f32[8,128]{1,0:T(8,128)S(1)}, f32[8,128]{1,0:T(8,128)S(1)}, u32[]{:S(2)}, u32[]{:S(2)}) collective-permute-start(f32[8,128]{1,0:T(8,128)S(1)} %merge.1.rest_2_), channel_id=1, source_target_pairs={{0,3},{1,2},{2,1},{3,0},{16,19},{17,18},{18,17},{19,16},{4,7},{5,6... | collective-permute-start | bytes 12296 | tf_op jit(solution)/shard_map/ppermute | solution.py:339
  29.0 0.1 score.5.rest_1_.rest_2_
  29.1 1.7 %collective-permute-start.11 = (f32[8,128]{1,0:T(8,128)S(1)}, f32[8,128]{1,0:T(8,128)S(1)}, u32[]{:S(2)}, u32[]{:S(2)}) collective-permute-start(f32[8,128]{1,0:T(8,128)S(1)} %score.5.rest_1_.rest_2_), channel_id=1, source_target_pairs={{0,16},{1,17},{2,18},{3,19},{16,0},{17,1},{18,2},{19,3},{4,20},{5,... | collective-permute-start | bytes 12296 | tf_op jit(solution)/shard_map/ppermute | solution.py:339
  30.8 0.1 score.6.rest_1_
  30.9 1.9 %collective-permute-start.12 = (f32[8,128]{1,0:T(8,128)S(1)}, f32[8,128]{1,0:T(8,128)S(1)}, u32[]{:S(2)}, u32[]{:S(2)}) collective-permute-start(f32[8,128]{1,0:T(8,128)S(1)} %score.6.rest_1_), channel_id=1, source_target_pairs={{0,2},{1,3},{2,0},{3,1},{16,18},{17,19},{18,16},{19,17},{4,6},{5,7... | collective-permute-start | bytes 12296 | tf_op jit(solution)/shard_map/ppermute | solution.py:339
  32.8 0.1 score.7.rest_3_
  32.9 1.0 %collective-permute-start.13 = (f32[8,128]{1,0:T(8,128)S(1)}, f32[8,128]{1,0:T(8,128)S(1)}, u32[]{:S(2)}, u32[]{:S(2)}) collective-permute-start(f32[8,128]{1,0:T(8,128)S(1)} %score.7.rest_3_), channel_id=1, source_target_pairs={{0,18},{1,19},{2,16},{3,17},{16,2},{17,3},{18,0},{19,1},{4,22},{5,... | collective-permute-start | bytes 12296 | tf_op jit(solution)/shard_map/ppermute | solution.py:339
  34.0 3.2 %update.1 = f32[768,1024]{1,0:T(8,128)} custom-call(bf16[768,256]{1,0:T(8,128)(2,1)S(1)} %bitcast.20, bf16[768,256]{1,0:T(8,128)(2,1)S(1)} %collective-permute-done.other_ref, f32[768,1024]{1,0:T(8,128)S(1)} %sum.1._.grad_ref, f32[768,1024]{1,0:T(8,128)S(1)} %bitcast.16, bf16[768,1024]{1,0:T(8,128)(2,1)S(1)} %bitcast.21, bf16[768,1024]{1,0:T(8,128)(2,1)S(1)} %bitcast.22, ...), custom_call_target="tpu_custom_call" | custom-call | flops 603979776 | bytes 12582912 | tf_op jit(solution)/shard_map/update/pallas_call | solution.py:464
  37.2 1.2 %collective-permute-done.13.rest_5_ = f32[8,128]{1,0:T(8,128)S(1)} collective-permute-done((f32[8,128]{1,0:T(8,128)S(1)}, f32[8,128]{1,0:T(8,128)S(1)}, u32[]{:S(2)}, u32[]{:S(2)}) %collective-permute-start.13) | collective-permute-done | bytes 4128 | tf_op jit(solution)/shard_map/ppermute | solution.py:339
  38.4 0.9 %combine.1 = f32[8,512]{1,0:T(8,128)} custom-call(s32[8,512]{1,0:T(8,128)S(1)} %bitcast.24, f32[16,512]{1,0:T(8,128)S(1)} %get-tuple-element.17.slots_ref, f32[8,128]{1,0:T(8,128)S(1)} %collective-permute-done.9.rest_0_, f32[8,128]{1,0:T(8,128)S(1)} %collective-permute-done.10.rest_1_, f32[8,128]{1,0:T(8,128)S(1)} %score.5.rest_1_.rest_2_, ...), custom_call_target="tpu_custom_call" | custom-call | flops 524288 | bytes 32768 | tf_op jit(solution)/shard_map/combine/pallas_call | solution.py:490
  (24 shorter events, 0.1 us)
Async XLA Ops:
  0.6 12.4 %copy-start.1 = (bf16[1,1,768,256]{3,2,1,0:T(8,128)(2,1)S(1)}, bf16[1,1,768,256]{3,2,1,0:T(8,128)(2,1)}, u32[]{:S(2)}) copy-start(bf16[1,1,768,256]{3,2,1,0:T(8,128)(2,1)} %param.10) | copy-start | bytes 1179652
  0.6 12.4 %collective-permute-start = (bf16[768,256]{1,0:T(8,128)(2,1)}, bf16[768,256]{1,0:T(8,128)(2,1)S(1)}, u32[]{:S(2)}, u32[]{:S(2)}) collective-permute-start(bf16[768,256]{1,0:T(8,128)(2,1)} %bitcast.17), channel_id=1, source_target_pairs={{0,16},{1,17},{2,18},{3,19},{16,0},{17,1},{18,2},{19,3},{4,20},{5,... | collective-permute-start | bytes 1179656 | tf_op jit(solution)/shard_map/ppermute | solution.py:339
  5.7 12.5 %collective-permute-start.1 = (bf16[528,128]{1,0:T(8,128)(2,1)S(1)}, bf16[528,128]{1,0:T(8,128)(2,1)S(1)}, u32[]{:S(2)}, u32[]{:S(2)}) collective-permute-start(bf16[528,128]{1,0:T(8,128)(2,1)S(1)} %get-tuple-element.13), channel_id=1, source_target_pairs={{0,3},{1,2},{2,1},{3,0},{16,19},{17,18},{18,17},{19,16},{4,7},{5,6... | collective-permute-start | bytes 405512 | tf_op jit(solution)/shard_map/ppermute | solution.py:339
  9.3 12.0 %collective-permute-start.2 = (bf16[528,128]{1,0:T(8,128)(2,1)S(1)}, bf16[528,128]{1,0:T(8,128)(2,1)S(1)}, u32[]{:S(2)}, u32[]{:S(2)}) collective-permute-start(bf16[528,128]{1,0:T(8,128)(2,1)S(1)} %get-tuple-element.14), channel_id=1, source_target_pairs={{0,1},{1,0},{2,3},{3,2},{16,17},{17,16},{18,19},{19,18},{4,5},{5,4... | collective-permute-start | bytes 405512 | tf_op jit(solution)/shard_map/ppermute | solution.py:339
  9.3 12.0 %collective-permute-start.3 = (bf16[528,128]{1,0:T(8,128)(2,1)S(1)}, bf16[528,128]{1,0:T(8,128)(2,1)S(1)}, u32[]{:S(2)}, u32[]{:S(2)}) collective-permute-start(bf16[528,128]{1,0:T(8,128)(2,1)S(1)} %get-tuple-element.15), channel_id=1, source_target_pairs={{0,19},{1,18},{2,17},{3,16},{16,3},{17,2},{18,1},{19,0},{4,23},{5,... | collective-permute-start | bytes 405512 | tf_op jit(solution)/shard_map/ppermute | solution.py:339
  10.2 12.5 %collective-permute-start.4 = (bf16[528,128]{1,0:T(8,128)(2,1)S(1)}, bf16[528,128]{1,0:T(8,128)(2,1)S(1)}, u32[]{:S(2)}, u32[]{:S(2)}) collective-permute-start(bf16[528,128]{1,0:T(8,128)(2,1)S(1)} %get-tuple-element.16), channel_id=1, source_target_pairs={{0,17},{1,16},{2,19},{3,18},{16,1},{17,0},{18,3},{19,2},{4,21},{5,... | collective-permute-start | bytes 405512 | tf_op jit(solution)/shard_map/ppermute | solution.py:339
  16.3 12.6 %collective-permute-start.7 = (bf16[528,128]{1,0:T(8,128)(2,1)S(1)}, bf16[528,128]{1,0:T(8,128)(2,1)S(1)}, u32[]{:S(2)}, u32[]{:S(2)}) collective-permute-start(bf16[528,128]{1,0:T(8,128)(2,1)S(1)} %get-tuple-element.23), channel_id=1, source_target_pairs={{0,16},{1,17},{2,18},{3,19},{16,0},{17,1},{18,2},{19,3},{4,20},{5,... | collective-permute-start | bytes 405512 | tf_op jit(solution)/shard_map/ppermute | solution.py:339
  18.1 12.6 %collective-permute-start.5 = (bf16[528,128]{1,0:T(8,128)(2,1)S(1)}, bf16[528,128]{1,0:T(8,128)(2,1)S(1)}, u32[]{:S(2)}, u32[]{:S(2)}) collective-permute-start(bf16[528,128]{1,0:T(8,128)(2,1)S(1)} %get-tuple-element.21), channel_id=1, source_target_pairs={{0,2},{1,3},{2,0},{3,1},{16,18},{17,19},{18,16},{19,17},{4,6},{5,7... | collective-permute-start | bytes 405512 | tf_op jit(solution)/shard_map/ppermute | solution.py:339
  21.4 11.4 %collective-permute-start.6 = (bf16[528,128]{1,0:T(8,128)(2,1)S(1)}, bf16[528,128]{1,0:T(8,128)(2,1)S(1)}, u32[]{:S(2)}, u32[]{:S(2)}) collective-permute-start(bf16[528,128]{1,0:T(8,128)(2,1)S(1)} %get-tuple-element.22), channel_id=1, source_target_pairs={{0,18},{1,19},{2,16},{3,17},{16,2},{17,3},{18,0},{19,1},{4,22},{5,... | collective-permute-start | bytes 405512 | tf_op jit(solution)/shard_map/ppermute | solution.py:339
  22.8 3.7 %collective-permute-start.8 = (f32[8,128]{1,0:T(8,128)S(1)}, f32[8,128]{1,0:T(8,128)S(1)}, u32[]{:S(2)}, u32[]{:S(2)}) collective-permute-start(f32[8,128]{1,0:T(8,128)S(1)} %score.4.rest_5_.own_ref), channel_id=1, source_target_pairs={{0,16},{1,17},{2,18},{3,19},{16,0},{17,1},{18,2},{19,3},{4,20},{5,... | collective-permute-start | bytes 12296 | tf_op jit(solution)/shard_map/ppermute | solution.py:339
  26.6 10.6 %collective-permute-start.10 = (f32[8,128]{1,0:T(8,128)S(1)}, f32[8,128]{1,0:T(8,128)S(1)}, u32[]{:S(2)}, u32[]{:S(2)}) collective-permute-start(f32[8,128]{1,0:T(8,128)S(1)} %merge.1.rest_2_), channel_id=1, source_target_pairs={{0,3},{1,2},{2,1},{3,0},{16,19},{17,18},{18,17},{19,16},{4,7},{5,6... | collective-permute-start | bytes 12296 | tf_op jit(solution)/shard_map/ppermute | solution.py:339
  28.9 8.2 %collective-permute-start.9 = (f32[8,128]{1,0:T(8,128)S(1)}, f32[8,128]{1,0:T(8,128)S(1)}, u32[]{:S(2)}, u32[]{:S(2)}) collective-permute-start(f32[8,128]{1,0:T(8,128)S(1)} %merge.1.rest_2_), channel_id=1, source_target_pairs={{0,1},{1,0},{2,3},{3,2},{16,17},{17,16},{18,19},{19,18},{4,5},{5,4... | collective-permute-start | bytes 12296 | tf_op jit(solution)/shard_map/ppermute | solution.py:339
  29.0 5.0 %copy-start.2 = (bf16[1,1,768,1024]{3,2,1,0:T(8,128)(2,1)S(1)}, bf16[1,1,768,1024]{3,2,1,0:T(8,128)(2,1)}, u32[]{:S(2)}) copy-start(bf16[1,1,768,1024]{3,2,1,0:T(8,128)(2,1)} %param.12) | copy-start | bytes 4718596
  29.0 5.0 %copy-start.3 = (bf16[1,1,768,1024]{3,2,1,0:T(8,128)(2,1)S(1)}, bf16[1,1,768,1024]{3,2,1,0:T(8,128)(2,1)}, u32[]{:S(2)}) copy-start(bf16[1,1,768,1024]{3,2,1,0:T(8,128)(2,1)} %param.13) | copy-start | bytes 4718596
  29.1 4.8 %copy-start = (f32[1,1,768,1024]{3,2,1,0:T(8,128)S(1)}, f32[1,1,768,1024]{3,2,1,0:T(8,128)}, u32[]{:S(2)}) copy-start(f32[1,1,768,1024]{3,2,1,0:T(8,128)} %param.11) | copy-start | bytes 9437188
  29.1 9.3 %collective-permute-start.11 = (f32[8,128]{1,0:T(8,128)S(1)}, f32[8,128]{1,0:T(8,128)S(1)}, u32[]{:S(2)}, u32[]{:S(2)}) collective-permute-start(f32[8,128]{1,0:T(8,128)S(1)} %score.5.rest_1_.rest_2_), channel_id=1, source_target_pairs={{0,16},{1,17},{2,18},{3,19},{16,0},{17,1},{18,2},{19,3},{4,20},{5,... | collective-permute-start | bytes 12296 | tf_op jit(solution)/shard_map/ppermute | solution.py:339
  30.9 7.5 %collective-permute-start.12 = (f32[8,128]{1,0:T(8,128)S(1)}, f32[8,128]{1,0:T(8,128)S(1)}, u32[]{:S(2)}, u32[]{:S(2)}) collective-permute-start(f32[8,128]{1,0:T(8,128)S(1)} %score.6.rest_1_), channel_id=1, source_target_pairs={{0,2},{1,3},{2,0},{3,1},{16,18},{17,19},{18,16},{19,17},{4,6},{5,7... | collective-permute-start | bytes 12296 | tf_op jit(solution)/shard_map/ppermute | solution.py:339
  32.9 5.5 %collective-permute-start.13 = (f32[8,128]{1,0:T(8,128)S(1)}, f32[8,128]{1,0:T(8,128)S(1)}, u32[]{:S(2)}, u32[]{:S(2)}) collective-permute-start(f32[8,128]{1,0:T(8,128)S(1)} %score.7.rest_3_), channel_id=1, source_target_pairs={{0,18},{1,19},{2,16},{3,17},{16,2},{17,3},{18,0},{19,1},{4,22},{5,... | collective-permute-start | bytes 12296 | tf_op jit(solution)/shard_map/ppermute | solution.py:339
  33.9 4.5 %copy-start.4 = (s32[1,512,8]{1,2,0:T(8,128)S(1)}, s32[1,512,8]{1,2,0:T(8,128)}, u32[]{:S(2)}) copy-start(s32[1,512,8]{1,2,0:T(8,128)} %param.9) | copy-start | bytes 49156

commit v16 on v15

--- a/solution.py
+++ b/solution.py
@@ -354,8 +354,8 @@
     far = group // 2
     first = [k for k in range(1, group) if k != far]
     late = [0, far]
-    first_items = [(side, k) for side in range(2) for k in reversed(first)]
-    last_items = [(0, far), (1, far), (1, 0), (0, 0)]
+    first_items = [(0, k) for k in reversed(first)] + [(1, k) for k in first]
+    last_items = [(1, far), (0, far), (1, 0), (0, 0)]
     order = first_items + last_items
     chunk = jax.ShapeDtypeStruct((half // LANES * cap + TILE, LANES), BF16)
     grads = pltpu.with_memory_space_constraint(grad_out[0], pltpu.HBM)
@@ -430,7 +430,7 @@
 
     first_scores = scored(first_items)
     other_scores = moved(first_scores, 1, 0)
-    added = [(0, far), (1, far), (1, 0)]
+    added = [(1, far), (0, far), (1, 0)]
     summed = [item for item in order if item not in added]
     grad = pl.pallas_call(
         functools.partial(sum_kernel, summed, group, cap),
@@ -456,9 +456,9 @@
     returned = {k: [moved(merged, 0, k)] for k in first}
     zero_scores = scored([(0, 0), (1, 0)], merged)
     returned[0] = [zero_scores, moved(zero_scores, 1, 0)]
-    own_far = scored([(0, far)], zero_scores)
-    last_scores = scored([(1, far)], own_far)
-    returned[far] = [moved(own_far, 0, far), moved(last_scores, 1, far)]
+    other_far = scored([(1, far)], zero_scores)
+    last_scores = scored([(0, far)], other_far)
+    returned[far] = [moved(last_scores, 0, far), moved(other_far, 1, far)]
 
     block = min(hid, 2 * LANES)
     update = pl.pallas_call(

time: 39.4 us -> 44 us (1.12)
  starting transfers between devices: 22.4 us -> 30 us
  waiting for transfers between devices: 4.98 us -> 1.89 us
    ppermute x14, starting transfers between devices: 22.4 us -> 30 us  [moved(): return lax.ppermute(array, ('pair', 'ep'), pairs)]
    ppermute x14, waiting for transfers between devices: 4.98 us -> 1.89 us  [moved(): return lax.ppermute(array, ('pair', 'ep'), pairs)]
  transfers between devices with their start and end apart: 14 -> 14, of which waited for: 4 -> 2; matrix products, arithmetic and copies ran while one was open for 0% -> 0% of each run, Pallas kernels for 26% -> 23%
where the time goes in v16:
time: 44 us; the launch traced here: 43.8 us
  starting transfers between devices  30 us (68%)
  Pallas kernels  11.1 us (25%)
  waiting for transfers between devices  1.89 us (4%)
  between operations  0.75 us (2%)
    ppermute x14, starting transfers between devices, moved(): return lax.ppermute(array, ('pair', 'ep'), pairs)  30 us
    pallas_call x1, Pallas kernels, local(): pl.pallas_call(functools.partial(later_kernel, last_items, late, cap), ou...  3.33 us
    pallas_call x1, Pallas kernels, local(): pl.pallas_call(functools.partial(update_kernel, added, cap), out_shape=ja...  3.18 us
    pallas_call x1, Pallas kernels, local(): pl.pallas_call(functools.partial(route_kernel, first_items, first, group,...  1.99 us
    ppermute x14, waiting for transfers between devices, moved(): return lax.ppermute(array, ('pair', 'ep'), pairs)  1.89 us
    pallas_call x1, Pallas kernels, local(): pl.pallas_call(functools.partial(sum_kernel, summed, group, cap), out_sha...  1.12 us
  transfers between devices with their start and end apart: 14, of which 2 were waited for; matrix products, arithmetic and copies ran while one was open for 0% of the time, Pallas kernels for 23%

profile of v16, /device:TPU:0, one launch (start us, length us, event | category | flops | bytes accessed | tf_op | source)
XLA Modules:
  0.0 43.8 jit_solution(8665382500271963428)
XLA Ops:
  0.6 3.0 %collective-permute-start = (bf16[768,256]{1,0:T(8,128)(2,1)}, bf16[768,256]{1,0:T(8,128)(2,1)S(1)}, u32[]{:S(2)}, u32[]{:S(2)}) collective-permute-start(bf16[768,256]{1,0:T(8,128)(2,1)} %bitcast.17), channel_id=1, source_target_pairs={{0,16},{1,17},{2,18},{3,19},{16,0},{17,1},{18,2},{19,3},{4,20},{5,... | collective-permute-start | bytes 1179656 | tf_op jit(solution)/shard_map/ppermute | solution.py:339
  3.7 2.0 %route.1 = (f32[16,512]{1,0:T(8,128)S(1)}, bf16[4,16,128]{2,1,0:T(8,128)(2,1)S(1)}, bf16[528,128]{1,0:T(8,128)(2,1)S(1)}, bf16[528,128]{1,0:T(8,128)(2,1)S(1)}, ...) custom-call(s32[8,512]{1,0:T(8,128)} %bitcast.23, bf16[8,512]{1,0:T(8,128)(2,1)} %bitcast.29, ...), custom_call_target="tpu_custom_call" | custom-call | flops 536870912 | bytes 3145728 | tf_op jit(solution)/shard_map/route/pallas_call | solution.py:363
  5.7 3.7 %collective-permute-start.1 = (bf16[528,128]{1,0:T(8,128)(2,1)S(1)}, bf16[528,128]{1,0:T(8,128)(2,1)S(1)}, u32[]{:S(2)}, u32[]{:S(2)}) collective-permute-start(bf16[528,128]{1,0:T(8,128)(2,1)S(1)} %get-tuple-element.13), channel_id=1, source_target_pairs={{0,3},{1,2},{2,1},{3,0},{16,19},{17,18},{18,17},{19,16},{4,7},{5,6... | collective-permute-start | bytes 405512 | tf_op jit(solution)/shard_map/ppermute | solution.py:339
  9.3 2.0 %collective-permute-start.3 = (bf16[528,128]{1,0:T(8,128)(2,1)S(1)}, bf16[528,128]{1,0:T(8,128)(2,1)S(1)}, u32[]{:S(2)}, u32[]{:S(2)}) collective-permute-start(bf16[528,128]{1,0:T(8,128)(2,1)S(1)} %get-tuple-element.15), channel_id=1, source_target_pairs={{0,17},{1,16},{2,19},{3,18},{16,1},{17,0},{18,3},{19,2},{4,21},{5,... | collective-permute-start | bytes 405512 | tf_op jit(solution)/shard_map/ppermute | solution.py:339
  11.3 1.2 %collective-permute-start.4 = (bf16[528,128]{1,0:T(8,128)(2,1)S(1)}, bf16[528,128]{1,0:T(8,128)(2,1)S(1)}, u32[]{:S(2)}, u32[]{:S(2)}) collective-permute-start(bf16[528,128]{1,0:T(8,128)(2,1)S(1)} %get-tuple-element.16), channel_id=1, source_target_pairs={{0,19},{1,18},{2,17},{3,16},{16,3},{17,2},{18,1},{19,0},{4,23},{5,... | collective-permute-start | bytes 405512 | tf_op jit(solution)/shard_map/ppermute | solution.py:339
  12.5 0.5 %collective-permute-done.other_ref = bf16[768,256]{1,0:T(8,128)(2,1)S(1)} collective-permute-done((bf16[768,256]{1,0:T(8,128)(2,1)}, bf16[768,256]{1,0:T(8,128)(2,1)S(1)}, u32[]{:S(2)}, u32[]{:S(2)}) %collective-permute-start) | collective-permute-done | bytes 393248 | tf_op jit(solution)/shard_map/ppermute | solution.py:339
  13.0 3.3 %later.1 = (f32[512,1024]{1,0:T(8,128)S(1)}, bf16[528,128]{1,0:T(8,128)(2,1)S(1)}, bf16[528,128]{1,0:T(8,128)(2,1)S(1)}, bf16[528,128]{1,0:T(8,128)(2,1)S(1)}, bf16[528,128]{1,0:T(8,128)(2,1)S(1)}) custom-call(f32[16,512]{1,0:T(8,128)S(1)} %get-tuple-element.17.slots_ref, bf16[4,16,128]{2,1,0:T(8,128)(2,1)S(1)} %get-tuple-element.18.tiles_ref, ...), custom_call_target="tpu_custom_call" | custom-call | flops 1342177280 | bytes 3145728 | tf_op jit(solution)/shard_map/later/pallas_call | solution.py:389
  16.3 1.8 %collective-permute-start.7 = (bf16[528,128]{1,0:T(8,128)(2,1)S(1)}, bf16[528,128]{1,0:T(8,128)(2,1)S(1)}, u32[]{:S(2)}, u32[]{:S(2)}) collective-permute-start(bf16[528,128]{1,0:T(8,128)(2,1)S(1)} %get-tuple-element.23), channel_id=1, source_target_pairs={{0,16},{1,17},{2,18},{3,19},{16,0},{17,1},{18,2},{19,3},{4,20},{5,... | collective-permute-start | bytes 405512 | tf_op jit(solution)/shard_map/ppermute | solution.py:339
  18.1 8.9 %collective-permute-start.5 = (bf16[528,128]{1,0:T(8,128)(2,1)S(1)}, bf16[528,128]{1,0:T(8,128)(2,1)S(1)}, u32[]{:S(2)}, u32[]{:S(2)}) collective-permute-start(bf16[528,128]{1,0:T(8,128)(2,1)S(1)} %get-tuple-element.21), channel_id=1, source_target_pairs={{0,18},{1,19},{2,16},{3,17},{16,2},{17,3},{18,0},{19,1},{4,22},{5,... | collective-permute-start | bytes 405512 | tf_op jit(solution)/shard_map/ppermute | solution.py:339
  27.0 0.1 collective-permute-start.6
  27.2 0.2 score.4.rest_5_.own_ref
  27.4 1.5 %collective-permute-start.8 = (f32[8,128]{1,0:T(8,128)S(1)}, f32[8,128]{1,0:T(8,128)S(1)}, u32[]{:S(2)}, u32[]{:S(2)}) collective-permute-start(f32[8,128]{1,0:T(8,128)S(1)} %score.4.rest_5_.own_ref), channel_id=1, source_target_pairs={{0,16},{1,17},{2,18},{3,19},{16,0},{17,1},{18,2},{19,3},{4,20},{5,... | collective-permute-start | bytes 12296 | tf_op jit(solution)/shard_map/ppermute | solution.py:339
  28.8 1.1 %sum.1._.grad_ref = f32[768,1024]{1,0:T(8,128)S(1)} custom-call(bf16[768,256]{1,0:T(8,128)(2,1)S(1)} %bitcast.19, bf16[768,256]{1,0:T(8,128)(2,1)S(1)} %collective-permute-done.other_ref, bf16[528,128]{1,0:T(8,128)(2,1)S(1)} %collective-permute-done.1.rest_0_, bf16[528,128]{1,0:T(8,128)(2,1)S(1)} %collective-permute-done.2.rest_1_, ...), custom_call_target="tpu_custom_call" | custom-call | flops 805306368 | bytes 3145728 | tf_op jit(solution)/shard_map/sum/pallas_call | solution.py:435
  30.0 1.3 %collective-permute-done.8.other_ref = f32[8,128]{1,0:T(8,128)S(1)} collective-permute-done((f32[8,128]{1,0:T(8,128)S(1)}, f32[8,128]{1,0:T(8,128)S(1)}, u32[]{:S(2)}, u32[]{:S(2)}) %collective-permute-start.8) | collective-permute-done | bytes 4128 | tf_op jit(solution)/shard_map/ppermute | solution.py:339
  31.3 0.1 merge.1.rest_2_
  31.4 3.3 %collective-permute-start.9 = (f32[8,128]{1,0:T(8,128)S(1)}, f32[8,128]{1,0:T(8,128)S(1)}, u32[]{:S(2)}, u32[]{:S(2)}) collective-permute-start(f32[8,128]{1,0:T(8,128)S(1)} %merge.1.rest_2_), channel_id=1, source_target_pairs={{0,1},{1,0},{2,3},{3,2},{16,17},{17,16},{18,19},{19,18},{4,5},{5,4... | collective-permute-start | bytes 12296 | tf_op jit(solution)/shard_map/ppermute | solution.py:339
  34.7 0.1 score.5.rest_1_.rest_2_
  34.8 1.4 %collective-permute-start.11 = (f32[8,128]{1,0:T(8,128)S(1)}, f32[8,128]{1,0:T(8,128)S(1)}, u32[]{:S(2)}, u32[]{:S(2)}) collective-permute-start(f32[8,128]{1,0:T(8,128)S(1)} %score.5.rest_1_.rest_2_), channel_id=1, source_target_pairs={{0,16},{1,17},{2,18},{3,19},{16,0},{17,1},{18,2},{19,3},{4,20},{5,... | collective-permute-start | bytes 12296 | tf_op jit(solution)/shard_map/ppermute | solution.py:339
  36.2 0.1 score.6.rest_1_
  36.3 1.3 %collective-permute-start.13 = (f32[8,128]{1,0:T(8,128)S(1)}, f32[8,128]{1,0:T(8,128)S(1)}, u32[]{:S(2)}, u32[]{:S(2)}) collective-permute-start(f32[8,128]{1,0:T(8,128)S(1)} %score.6.rest_1_), channel_id=1, source_target_pairs={{0,18},{1,19},{2,16},{3,17},{16,2},{17,3},{18,0},{19,1},{4,22},{5,... | collective-permute-start | bytes 12296 | tf_op jit(solution)/shard_map/ppermute | solution.py:339
  37.6 0.1 score.7.rest_3_
  37.8 1.9 %collective-permute-start.12 = (f32[8,128]{1,0:T(8,128)S(1)}, f32[8,128]{1,0:T(8,128)S(1)}, u32[]{:S(2)}, u32[]{:S(2)}) collective-permute-start(f32[8,128]{1,0:T(8,128)S(1)} %score.7.rest_3_), channel_id=1, source_target_pairs={{0,2},{1,3},{2,0},{3,1},{16,18},{17,19},{18,16},{19,17},{4,6},{5,7... | collective-permute-start | bytes 12296 | tf_op jit(solution)/shard_map/ppermute | solution.py:339
  39.7 3.2 %update.1 = f32[768,1024]{1,0:T(8,128)} custom-call(bf16[768,256]{1,0:T(8,128)(2,1)S(1)} %bitcast.20, bf16[768,256]{1,0:T(8,128)(2,1)S(1)} %collective-permute-done.other_ref, f32[768,1024]{1,0:T(8,128)S(1)} %sum.1._.grad_ref, f32[768,1024]{1,0:T(8,128)S(1)} %bitcast.16, bf16[768,1024]{1,0:T(8,128)(2,1)S(1)} %bitcast.21, bf16[768,1024]{1,0:T(8,128)(2,1)S(1)} %bitcast.22, ...), custom_call_target="tpu_custom_call" | custom-call | flops 603979776 | bytes 12582912 | tf_op jit(solution)/shard_map/update/pallas_call | solution.py:464
  42.9 0.9 %combine.1 = f32[8,512]{1,0:T(8,128)} custom-call(s32[8,512]{1,0:T(8,128)S(1)} %bitcast.24, f32[16,512]{1,0:T(8,128)S(1)} %get-tuple-element.17.slots_ref, f32[8,128]{1,0:T(8,128)S(1)} %collective-permute-done.9.rest_0_, f32[8,128]{1,0:T(8,128)S(1)} %collective-permute-done.10.rest_1_, f32[8,128]{1,0:T(8,128)S(1)} %score.5.rest_1_.rest_2_, ...), custom_call_target="tpu_custom_call" | custom-call | flops 524288 | bytes 32768 | tf_op jit(solution)/shard_map/combine/pallas_call | solution.py:490
  (24 shorter events, 0.1 us)
Async XLA Ops:
  0.6 12.4 %copy-start.1 = (bf16[1,1,768,256]{3,2,1,0:T(8,128)(2,1)S(1)}, bf16[1,1,768,256]{3,2,1,0:T(8,128)(2,1)}, u32[]{:S(2)}) copy-start(bf16[1,1,768,256]{3,2,1,0:T(8,128)(2,1)} %param.10) | copy-start | bytes 1179652
  0.6 12.4 %collective-permute-start = (bf16[768,256]{1,0:T(8,128)(2,1)}, bf16[768,256]{1,0:T(8,128)(2,1)S(1)}, u32[]{:S(2)}, u32[]{:S(2)}) collective-permute-start(bf16[768,256]{1,0:T(8,128)(2,1)} %bitcast.17), channel_id=1, source_target_pairs={{0,16},{1,17},{2,18},{3,19},{16,0},{17,1},{18,2},{19,3},{4,20},{5,... | collective-permute-start | bytes 1179656 | tf_op jit(solution)/shard_map/ppermute | solution.py:339
  5.7 12.5 %collective-permute-start.1 = (bf16[528,128]{1,0:T(8,128)(2,1)S(1)}, bf16[528,128]{1,0:T(8,128)(2,1)S(1)}, u32[]{:S(2)}, u32[]{:S(2)}) collective-permute-start(bf16[528,128]{1,0:T(8,128)(2,1)S(1)} %get-tuple-element.13), channel_id=1, source_target_pairs={{0,3},{1,2},{2,1},{3,0},{16,19},{17,18},{18,17},{19,16},{4,7},{5,6... | collective-permute-start | bytes 405512 | tf_op jit(solution)/shard_map/ppermute | solution.py:339
  9.3 17.7 %collective-permute-start.2 = (bf16[528,128]{1,0:T(8,128)(2,1)S(1)}, bf16[528,128]{1,0:T(8,128)(2,1)S(1)}, u32[]{:S(2)}, u32[]{:S(2)}) collective-permute-start(bf16[528,128]{1,0:T(8,128)(2,1)S(1)} %get-tuple-element.14), channel_id=1, source_target_pairs={{0,1},{1,0},{2,3},{3,2},{16,17},{17,16},{18,19},{19,18},{4,5},{5,4... | collective-permute-start | bytes 405512 | tf_op jit(solution)/shard_map/ppermute | solution.py:339
  9.3 17.8 %collective-permute-start.3 = (bf16[528,128]{1,0:T(8,128)(2,1)S(1)}, bf16[528,128]{1,0:T(8,128)(2,1)S(1)}, u32[]{:S(2)}, u32[]{:S(2)}) collective-permute-start(bf16[528,128]{1,0:T(8,128)(2,1)S(1)} %get-tuple-element.15), channel_id=1, source_target_pairs={{0,17},{1,16},{2,19},{3,18},{16,1},{17,0},{18,3},{19,2},{4,21},{5,... | collective-permute-start | bytes 405512 | tf_op jit(solution)/shard_map/ppermute | solution.py:339
  11.3 15.9 %collective-permute-start.4 = (bf16[528,128]{1,0:T(8,128)(2,1)S(1)}, bf16[528,128]{1,0:T(8,128)(2,1)S(1)}, u32[]{:S(2)}, u32[]{:S(2)}) collective-permute-start(bf16[528,128]{1,0:T(8,128)(2,1)S(1)} %get-tuple-element.16), channel_id=1, source_target_pairs={{0,19},{1,18},{2,17},{3,16},{16,3},{17,2},{18,1},{19,0},{4,23},{5,... | collective-permute-start | bytes 405512 | tf_op jit(solution)/shard_map/ppermute | solution.py:339
  16.3 18.4 %collective-permute-start.7 = (bf16[528,128]{1,0:T(8,128)(2,1)S(1)}, bf16[528,128]{1,0:T(8,128)(2,1)S(1)}, u32[]{:S(2)}, u32[]{:S(2)}) collective-permute-start(bf16[528,128]{1,0:T(8,128)(2,1)S(1)} %get-tuple-element.23), channel_id=1, source_target_pairs={{0,16},{1,17},{2,18},{3,19},{16,0},{17,1},{18,2},{19,3},{4,20},{5,... | collective-permute-start | bytes 405512 | tf_op jit(solution)/shard_map/ppermute | solution.py:339
  18.1 18.1 %collective-permute-start.5 = (bf16[528,128]{1,0:T(8,128)(2,1)S(1)}, bf16[528,128]{1,0:T(8,128)(2,1)S(1)}, u32[]{:S(2)}, u32[]{:S(2)}) collective-permute-start(bf16[528,128]{1,0:T(8,128)(2,1)S(1)} %get-tuple-element.21), channel_id=1, source_target_pairs={{0,18},{1,19},{2,16},{3,17},{16,2},{17,3},{18,0},{19,1},{4,22},{5,... | collective-permute-start | bytes 405512 | tf_op jit(solution)/shard_map/ppermute | solution.py:339
  27.0 10.6 %collective-permute-start.6 = (bf16[528,128]{1,0:T(8,128)(2,1)S(1)}, bf16[528,128]{1,0:T(8,128)(2,1)S(1)}, u32[]{:S(2)}, u32[]{:S(2)}) collective-permute-start(bf16[528,128]{1,0:T(8,128)(2,1)S(1)} %get-tuple-element.22), channel_id=1, source_target_pairs={{0,2},{1,3},{2,0},{3,1},{16,18},{17,19},{18,16},{19,17},{4,6},{5,7... | collective-permute-start | bytes 405512 | tf_op jit(solution)/shard_map/ppermute | solution.py:339
  27.4 3.9 %collective-permute-start.8 = (f32[8,128]{1,0:T(8,128)S(1)}, f32[8,128]{1,0:T(8,128)S(1)}, u32[]{:S(2)}, u32[]{:S(2)}) collective-permute-start(f32[8,128]{1,0:T(8,128)S(1)} %score.4.rest_5_.own_ref), channel_id=1, source_target_pairs={{0,16},{1,17},{2,18},{3,19},{16,0},{17,1},{18,2},{19,3},{4,20},{5,... | collective-permute-start | bytes 12296 | tf_op jit(solution)/shard_map/ppermute | solution.py:339
  31.4 11.5 %collective-permute-start.10 = (f32[8,128]{1,0:T(8,128)S(1)}, f32[8,128]{1,0:T(8,128)S(1)}, u32[]{:S(2)}, u32[]{:S(2)}) collective-permute-start(f32[8,128]{1,0:T(8,128)S(1)} %merge.1.rest_2_), channel_id=1, source_target_pairs={{0,3},{1,2},{2,1},{3,0},{16,19},{17,18},{18,17},{19,16},{4,7},{5,6... | collective-permute-start | bytes 12296 | tf_op jit(solution)/shard_map/ppermute | solution.py:339
  31.4 11.5 %collective-permute-start.9 = (f32[8,128]{1,0:T(8,128)S(1)}, f32[8,128]{1,0:T(8,128)S(1)}, u32[]{:S(2)}, u32[]{:S(2)}) collective-permute-start(f32[8,128]{1,0:T(8,128)S(1)} %merge.1.rest_2_), channel_id=1, source_target_pairs={{0,1},{1,0},{2,3},{3,2},{16,17},{17,16},{18,19},{19,18},{4,5},{5,4... | collective-permute-start | bytes 12296 | tf_op jit(solution)/shard_map/ppermute | solution.py:339
  34.7 5.0 %copy-start.2 = (bf16[1,1,768,1024]{3,2,1,0:T(8,128)(2,1)S(1)}, bf16[1,1,768,1024]{3,2,1,0:T(8,128)(2,1)}, u32[]{:S(2)}) copy-start(bf16[1,1,768,1024]{3,2,1,0:T(8,128)(2,1)} %param.12) | copy-start | bytes 4718596
  34.7 5.0 %copy-start.3 = (bf16[1,1,768,1024]{3,2,1,0:T(8,128)(2,1)S(1)}, bf16[1,1,768,1024]{3,2,1,0:T(8,128)(2,1)}, u32[]{:S(2)}) copy-start(bf16[1,1,768,1024]{3,2,1,0:T(8,128)(2,1)} %param.13) | copy-start | bytes 4718596
  34.8 4.8 %copy-start = (f32[1,1,768,1024]{3,2,1,0:T(8,128)S(1)}, f32[1,1,768,1024]{3,2,1,0:T(8,128)}, u32[]{:S(2)}) copy-start(f32[1,1,768,1024]{3,2,1,0:T(8,128)} %param.11) | copy-start | bytes 9437188
  34.8 8.1 %collective-permute-start.11 = (f32[8,128]{1,0:T(8,128)S(1)}, f32[8,128]{1,0:T(8,128)S(1)}, u32[]{:S(2)}, u32[]{:S(2)}) collective-permute-start(f32[8,128]{1,0:T(8,128)S(1)} %score.5.rest_1_.rest_2_), channel_id=1, source_target_pairs={{0,16},{1,17},{2,18},{3,19},{16,0},{17,1},{18,2},{19,3},{4,20},{5,... | collective-permute-start | bytes 12296 | tf_op jit(solution)/shard_map/ppermute | solution.py:339
  36.3 6.6 %collective-permute-start.13 = (f32[8,128]{1,0:T(8,128)S(1)}, f32[8,128]{1,0:T(8,128)S(1)}, u32[]{:S(2)}, u32[]{:S(2)}) collective-permute-start(f32[8,128]{1,0:T(8,128)S(1)} %score.6.rest_1_), channel_id=1, source_target_pairs={{0,18},{1,19},{2,16},{3,17},{16,2},{17,3},{18,0},{19,1},{4,22},{5,... | collective-permute-start | bytes 12296 | tf_op jit(solution)/shard_map/ppermute | solution.py:339
  37.8 5.1 %collective-permute-start.12 = (f32[8,128]{1,0:T(8,128)S(1)}, f32[8,128]{1,0:T(8,128)S(1)}, u32[]{:S(2)}, u32[]{:S(2)}) collective-permute-start(f32[8,128]{1,0:T(8,128)S(1)} %score.7.rest_3_), channel_id=1, source_target_pairs={{0,2},{1,3},{2,0},{3,1},{16,18},{17,19},{18,16},{19,17},{4,6},{5,7... | collective-permute-start | bytes 12296 | tf_op jit(solution)/shard_map/ppermute | solution.py:339
  39.7 3.2 %copy-start.4 = (s32[1,512,8]{1,2,0:T(8,128)S(1)}, s32[1,512,8]{1,2,0:T(8,128)}, u32[]{:S(2)}) copy-start(s32[1,512,8]{1,2,0:T(8,128)} %param.9) | copy-start | bytes 49156

commit v17 on v16

--- a/solution.py
+++ b/solution.py
@@ -354,7 +354,7 @@
     far = group // 2
     first = [k for k in range(1, group) if k != far]
     late = [0, far]
-    first_items = [(0, k) for k in reversed(first)] + [(1, k) for k in first]
+    first_items = [(side, k) for side in range(2) for k in reversed(first)]
     last_items = [(1, far), (0, far), (1, 0), (0, 0)]
     order = first_items + last_items
     chunk = jax.ShapeDtypeStruct((half // LANES * cap + TILE, LANES), BF16)

time: 44 us -> 39.1 us (0.89)
  starting transfers between devices: 30 us -> 23.3 us
  waiting for transfers between devices: 1.89 us -> 3.81 us
    ppermute x14, starting transfers between devices: 30 us -> 23.3 us  [moved(): return lax.ppermute(array, ('pair', 'ep'), pairs)]
    ppermute x14, waiting for transfers between devices: 1.89 us -> 3.81 us  [moved(): return lax.ppermute(array, ('pair', 'ep'), pairs)]
  transfers between devices with their start and end apart: 14 -> 14, of which waited for: 2 -> 4; matrix products, arithmetic and copies ran while one was open for 0% -> 0% of each run, Pallas kernels for 23% -> 26%
where the time goes in v17:
time: 39.1 us; the launch traced here: 39 us
  starting transfers between devices  23.3 us (60%)
  Pallas kernels  11.1 us (28%)
  waiting for transfers between devices  3.81 us (10%)
  between operations  0.75 us (2%)
    ppermute x14, starting transfers between devices, moved(): return lax.ppermute(array, ('pair', 'ep'), pairs)  23.3 us
    ppermute x14, waiting for transfers between devices, moved(): return lax.ppermute(array, ('pair', 'ep'), pairs)  3.81 us
    pallas_call x1, Pallas kernels, local(): pl.pallas_call(functools.partial(later_kernel, last_items, late, cap), ou...  3.33 us
    pallas_call x1, Pallas kernels, local(): pl.pallas_call(functools.partial(update_kernel, added, cap), out_shape=ja...  3.18 us
    pallas_call x1, Pallas kernels, local(): pl.pallas_call(functools.partial(route_kernel, first_items, first, group,...  1.99 us
    pallas_call x1, Pallas kernels, local(): pl.pallas_call(functools.partial(sum_kernel, summed, group, cap), out_sha...  1.12 us
    pallas_call x1, Pallas kernels, local(): pl.pallas_call(functools.partial(combine_kernel, [(k, len(arrays)) for k,...  0.87 us
  transfers between devices with their start and end apart: 14, of which 4 were waited for; matrix products, arithmetic and copies ran while one was open for 0% of the time, Pallas kernels for 26%

profile of v17, /device:TPU:0, one launch (start us, length us, event | category | flops | bytes accessed | tf_op | source)
XLA Modules:
  0.0 39.0 jit_solution(2483891064118472871)
XLA Ops:
  0.6 3.0 %collective-permute-start = (bf16[768,256]{1,0:T(8,128)(2,1)}, bf16[768,256]{1,0:T(8,128)(2,1)S(1)}, u32[]{:S(2)}, u32[]{:S(2)}) collective-permute-start(bf16[768,256]{1,0:T(8,128)(2,1)} %bitcast.17), channel_id=1, source_target_pairs={{0,16},{1,17},{2,18},{3,19},{16,0},{17,1},{18,2},{19,3},{4,20},{5,... | collective-permute-start | bytes 1179656 | tf_op jit(solution)/shard_map/ppermute | solution.py:339
  3.7 2.0 %route.1 = (f32[16,512]{1,0:T(8,128)S(1)}, bf16[4,16,128]{2,1,0:T(8,128)(2,1)S(1)}, bf16[528,128]{1,0:T(8,128)(2,1)S(1)}, bf16[528,128]{1,0:T(8,128)(2,1)S(1)}, ...) custom-call(s32[8,512]{1,0:T(8,128)} %bitcast.23, bf16[8,512]{1,0:T(8,128)(2,1)} %bitcast.29, ...), custom_call_target="tpu_custom_call" | custom-call | flops 536870912 | bytes 3145728 | tf_op jit(solution)/shard_map/route/pallas_call | solution.py:363
  5.7 3.7 %collective-permute-start.1 = (bf16[528,128]{1,0:T(8,128)(2,1)S(1)}, bf16[528,128]{1,0:T(8,128)(2,1)S(1)}, u32[]{:S(2)}, u32[]{:S(2)}) collective-permute-start(bf16[528,128]{1,0:T(8,128)(2,1)S(1)} %get-tuple-element.13), channel_id=1, source_target_pairs={{0,3},{1,2},{2,1},{3,0},{16,19},{17,18},{18,17},{19,16},{4,7},{5,6... | collective-permute-start | bytes 405512 | tf_op jit(solution)/shard_map/ppermute | solution.py:339
  9.3 0.8 %collective-permute-start.3 = (bf16[528,128]{1,0:T(8,128)(2,1)S(1)}, bf16[528,128]{1,0:T(8,128)(2,1)S(1)}, u32[]{:S(2)}, u32[]{:S(2)}) collective-permute-start(bf16[528,128]{1,0:T(8,128)(2,1)S(1)} %get-tuple-element.15), channel_id=1, source_target_pairs={{0,19},{1,18},{2,17},{3,16},{16,3},{17,2},{18,1},{19,0},{4,23},{5,... | collective-permute-start | bytes 405512 | tf_op jit(solution)/shard_map/ppermute | solution.py:339
  10.2 1.4 %collective-permute-start.4 = (bf16[528,128]{1,0:T(8,128)(2,1)S(1)}, bf16[528,128]{1,0:T(8,128)(2,1)S(1)}, u32[]{:S(2)}, u32[]{:S(2)}) collective-permute-start(bf16[528,128]{1,0:T(8,128)(2,1)S(1)} %get-tuple-element.16), channel_id=1, source_target_pairs={{0,17},{1,16},{2,19},{3,18},{16,1},{17,0},{18,3},{19,2},{4,21},{5,... | collective-permute-start | bytes 405512 | tf_op jit(solution)/shard_map/ppermute | solution.py:339
  11.6 1.4 %collective-permute-done.other_ref = bf16[768,256]{1,0:T(8,128)(2,1)S(1)} collective-permute-done((bf16[768,256]{1,0:T(8,128)(2,1)}, bf16[768,256]{1,0:T(8,128)(2,1)S(1)}, u32[]{:S(2)}, u32[]{:S(2)}) %collective-permute-start) | collective-permute-done | bytes 393248 | tf_op jit(solution)/shard_map/ppermute | solution.py:339
  13.0 3.3 %later.1 = (f32[512,1024]{1,0:T(8,128)S(1)}, bf16[528,128]{1,0:T(8,128)(2,1)S(1)}, bf16[528,128]{1,0:T(8,128)(2,1)S(1)}, bf16[528,128]{1,0:T(8,128)(2,1)S(1)}, bf16[528,128]{1,0:T(8,128)(2,1)S(1)}) custom-call(f32[16,512]{1,0:T(8,128)S(1)} %get-tuple-element.17.slots_ref, bf16[4,16,128]{2,1,0:T(8,128)(2,1)S(1)} %get-tuple-element.18.tiles_ref, ...), custom_call_target="tpu_custom_call" | custom-call | flops 1342177280 | bytes 3145728 | tf_op jit(solution)/shard_map/later/pallas_call | solution.py:389
  16.3 1.8 %collective-permute-start.7 = (bf16[528,128]{1,0:T(8,128)(2,1)S(1)}, bf16[528,128]{1,0:T(8,128)(2,1)S(1)}, u32[]{:S(2)}, u32[]{:S(2)}) collective-permute-start(bf16[528,128]{1,0:T(8,128)(2,1)S(1)} %get-tuple-element.23), channel_id=1, source_target_pairs={{0,16},{1,17},{2,18},{3,19},{16,0},{17,1},{18,2},{19,3},{4,20},{5,... | collective-permute-start | bytes 405512 | tf_op jit(solution)/shard_map/ppermute | solution.py:339
  18.1 3.2 %collective-permute-start.5 = (bf16[528,128]{1,0:T(8,128)(2,1)S(1)}, bf16[528,128]{1,0:T(8,128)(2,1)S(1)}, u32[]{:S(2)}, u32[]{:S(2)}) collective-permute-start(bf16[528,128]{1,0:T(8,128)(2,1)S(1)} %get-tuple-element.21), channel_id=1, source_target_pairs={{0,18},{1,19},{2,16},{3,17},{16,2},{17,3},{18,0},{19,1},{4,22},{5,... | collective-permute-start | bytes 405512 | tf_op jit(solution)/shard_map/ppermute | solution.py:339
  21.3 0.1 collective-permute-start.6
  21.5 1.0 %collective-permute-done.4.rest_3_ = bf16[528,128]{1,0:T(8,128)(2,1)S(1)} collective-permute-done((bf16[528,128]{1,0:T(8,128)(2,1)S(1)}, bf16[528,128]{1,0:T(8,128)(2,1)S(1)}, u32[]{:S(2)}, u32[]{:S(2)}) %collective-permute-start.4) | collective-permute-done | bytes 135200 | tf_op jit(solution)/shard_map/ppermute | solution.py:339
  22.5 0.2 score.4.rest_5_.own_ref
  22.7 1.6 %collective-permute-start.8 = (f32[8,128]{1,0:T(8,128)S(1)}, f32[8,128]{1,0:T(8,128)S(1)}, u32[]{:S(2)}, u32[]{:S(2)}) collective-permute-start(f32[8,128]{1,0:T(8,128)S(1)} %score.4.rest_5_.own_ref), channel_id=1, source_target_pairs={{0,16},{1,17},{2,18},{3,19},{16,0},{17,1},{18,2},{19,3},{4,20},{5,... | collective-permute-start | bytes 12296 | tf_op jit(solution)/shard_map/ppermute | solution.py:339
  24.3 1.1 %sum.1._.grad_ref = f32[768,1024]{1,0:T(8,128)S(1)} custom-call(bf16[768,256]{1,0:T(8,128)(2,1)S(1)} %bitcast.19, bf16[768,256]{1,0:T(8,128)(2,1)S(1)} %collective-permute-done.other_ref, bf16[528,128]{1,0:T(8,128)(2,1)S(1)} %collective-permute-done.1.rest_0_, bf16[528,128]{1,0:T(8,128)(2,1)S(1)} %collective-permute-done.2.rest_1_, ...), custom_call_target="tpu_custom_call" | custom-call | flops 805306368 | bytes 3145728 | tf_op jit(solution)/shard_map/sum/pallas_call | solution.py:435
  25.5 0.9 %collective-permute-done.8.other_ref = f32[8,128]{1,0:T(8,128)S(1)} collective-permute-done((f32[8,128]{1,0:T(8,128)S(1)}, f32[8,128]{1,0:T(8,128)S(1)}, u32[]{:S(2)}, u32[]{:S(2)}) %collective-permute-start.8) | collective-permute-done | bytes 4128 | tf_op jit(solution)/shard_map/ppermute | solution.py:339
  26.4 2.5 %collective-permute-start.10 = (f32[8,128]{1,0:T(8,128)S(1)}, f32[8,128]{1,0:T(8,128)S(1)}, u32[]{:S(2)}, u32[]{:S(2)}) collective-permute-start(f32[8,128]{1,0:T(8,128)S(1)} %merge.1.rest_2_), channel_id=1, source_target_pairs={{0,3},{1,2},{2,1},{3,0},{16,19},{17,18},{18,17},{19,16},{4,7},{5,6... | collective-permute-start | bytes 12296 | tf_op jit(solution)/shard_map/ppermute | solution.py:339
  28.9 0.2 collective-permute-start.9
  29.2 0.1 score.5.rest_1_.rest_2_
  29.3 1.5 %collective-permute-start.11 = (f32[8,128]{1,0:T(8,128)S(1)}, f32[8,128]{1,0:T(8,128)S(1)}, u32[]{:S(2)}, u32[]{:S(2)}) collective-permute-start(f32[8,128]{1,0:T(8,128)S(1)} %score.5.rest_1_.rest_2_), channel_id=1, source_target_pairs={{0,16},{1,17},{2,18},{3,19},{16,0},{17,1},{18,2},{19,3},{4,20},{5,... | collective-permute-start | bytes 12296 | tf_op jit(solution)/shard_map/ppermute | solution.py:339
  30.8 0.4 %collective-permute-done.5.rest_0_ = bf16[528,128]{1,0:T(8,128)(2,1)S(1)} collective-permute-done((bf16[528,128]{1,0:T(8,128)(2,1)S(1)}, bf16[528,128]{1,0:T(8,128)(2,1)S(1)}, u32[]{:S(2)}, u32[]{:S(2)}) %collective-permute-start.5) | collective-permute-done | bytes 135200 | tf_op jit(solution)/shard_map/ppermute | solution.py:339
  31.3 1.4 %collective-permute-start.13 = (f32[8,128]{1,0:T(8,128)S(1)}, f32[8,128]{1,0:T(8,128)S(1)}, u32[]{:S(2)}, u32[]{:S(2)}) collective-permute-start(f32[8,128]{1,0:T(8,128)S(1)} %score.6.rest_1_), channel_id=1, source_target_pairs={{0,18},{1,19},{2,16},{3,17},{16,2},{17,3},{18,0},{19,1},{4,22},{5,... | collective-permute-start | bytes 12296 | tf_op jit(solution)/shard_map/ppermute | solution.py:339
  32.8 2.0 %collective-permute-start.12 = (f32[8,128]{1,0:T(8,128)S(1)}, f32[8,128]{1,0:T(8,128)S(1)}, u32[]{:S(2)}, u32[]{:S(2)}) collective-permute-start(f32[8,128]{1,0:T(8,128)S(1)} %score.7.rest_3_), channel_id=1, source_target_pairs={{0,2},{1,3},{2,0},{3,1},{16,18},{17,19},{18,16},{19,17},{4,6},{5,7... | collective-permute-start | bytes 12296 | tf_op jit(solution)/shard_map/ppermute | solution.py:339
  34.8 3.2 %update.1 = f32[768,1024]{1,0:T(8,128)} custom-call(bf16[768,256]{1,0:T(8,128)(2,1)S(1)} %bitcast.20, bf16[768,256]{1,0:T(8,128)(2,1)S(1)} %collective-permute-done.other_ref, f32[768,1024]{1,0:T(8,128)S(1)} %sum.1._.grad_ref, f32[768,1024]{1,0:T(8,128)S(1)} %bitcast.16, bf16[768,1024]{1,0:T(8,128)(2,1)S(1)} %bitcast.21, bf16[768,1024]{1,0:T(8,128)(2,1)S(1)} %bitcast.22, ...), custom_call_target="tpu_custom_call" | custom-call | flops 603979776 | bytes 12582912 | tf_op jit(solution)/shard_map/update/pallas_call | solution.py:464
  38.1 0.9 %combine.1 = f32[8,512]{1,0:T(8,128)} custom-call(s32[8,512]{1,0:T(8,128)S(1)} %bitcast.24, f32[16,512]{1,0:T(8,128)S(1)} %get-tuple-element.17.slots_ref, f32[8,128]{1,0:T(8,128)S(1)} %collective-permute-done.9.rest_0_, f32[8,128]{1,0:T(8,128)S(1)} %collective-permute-done.10.rest_1_, f32[8,128]{1,0:T(8,128)S(1)} %score.5.rest_1_.rest_2_, ...), custom_call_target="tpu_custom_call" | custom-call | flops 524288 | bytes 32768 | tf_op jit(solution)/shard_map/combine/pallas_call | solution.py:490
  (24 shorter events, 0.4 us)
Async XLA Ops:
  0.6 12.4 %copy-start.1 = (bf16[1,1,768,256]{3,2,1,0:T(8,128)(2,1)S(1)}, bf16[1,1,768,256]{3,2,1,0:T(8,128)(2,1)}, u32[]{:S(2)}) copy-start(bf16[1,1,768,256]{3,2,1,0:T(8,128)(2,1)} %param.10) | copy-start | bytes 1179652
  0.6 12.4 %collective-permute-start = (bf16[768,256]{1,0:T(8,128)(2,1)}, bf16[768,256]{1,0:T(8,128)(2,1)S(1)}, u32[]{:S(2)}, u32[]{:S(2)}) collective-permute-start(bf16[768,256]{1,0:T(8,128)(2,1)} %bitcast.17), channel_id=1, source_target_pairs={{0,16},{1,17},{2,18},{3,19},{16,0},{17,1},{18,2},{19,3},{4,20},{5,... | collective-permute-start | bytes 1179656 | tf_op jit(solution)/shard_map/ppermute | solution.py:339
  5.7 12.5 %collective-permute-start.1 = (bf16[528,128]{1,0:T(8,128)(2,1)S(1)}, bf16[528,128]{1,0:T(8,128)(2,1)S(1)}, u32[]{:S(2)}, u32[]{:S(2)}) collective-permute-start(bf16[528,128]{1,0:T(8,128)(2,1)S(1)} %get-tuple-element.13), channel_id=1, source_target_pairs={{0,3},{1,2},{2,1},{3,0},{16,19},{17,18},{18,17},{19,16},{4,7},{5,6... | collective-permute-start | bytes 405512 | tf_op jit(solution)/shard_map/ppermute | solution.py:339
  9.3 12.0 %collective-permute-start.2 = (bf16[528,128]{1,0:T(8,128)(2,1)S(1)}, bf16[528,128]{1,0:T(8,128)(2,1)S(1)}, u32[]{:S(2)}, u32[]{:S(2)}) collective-permute-start(bf16[528,128]{1,0:T(8,128)(2,1)S(1)} %get-tuple-element.14), channel_id=1, source_target_pairs={{0,1},{1,0},{2,3},{3,2},{16,17},{17,16},{18,19},{19,18},{4,5},{5,4... | collective-permute-start | bytes 405512 | tf_op jit(solution)/shard_map/ppermute | solution.py:339
  9.3 12.1 %collective-permute-start.3 = (bf16[528,128]{1,0:T(8,128)(2,1)S(1)}, bf16[528,128]{1,0:T(8,128)(2,1)S(1)}, u32[]{:S(2)}, u32[]{:S(2)}) collective-permute-start(bf16[528,128]{1,0:T(8,128)(2,1)S(1)} %get-tuple-element.15), channel_id=1, source_target_pairs={{0,19},{1,18},{2,17},{3,16},{16,3},{17,2},{18,1},{19,0},{4,23},{5,... | collective-permute-start | bytes 405512 | tf_op jit(solution)/shard_map/ppermute | solution.py:339
  10.2 12.3 %collective-permute-start.4 = (bf16[528,128]{1,0:T(8,128)(2,1)S(1)}, bf16[528,128]{1,0:T(8,128)(2,1)S(1)}, u32[]{:S(2)}, u32[]{:S(2)}) collective-permute-start(bf16[528,128]{1,0:T(8,128)(2,1)S(1)} %get-tuple-element.16), channel_id=1, source_target_pairs={{0,17},{1,16},{2,19},{3,18},{16,1},{17,0},{18,3},{19,2},{4,21},{5,... | collective-permute-start | bytes 405512 | tf_op jit(solution)/shard_map/ppermute | solution.py:339
  16.3 12.8 %collective-permute-start.7 = (bf16[528,128]{1,0:T(8,128)(2,1)S(1)}, bf16[528,128]{1,0:T(8,128)(2,1)S(1)}, u32[]{:S(2)}, u32[]{:S(2)}) collective-permute-start(bf16[528,128]{1,0:T(8,128)(2,1)S(1)} %get-tuple-element.23), channel_id=1, source_target_pairs={{0,16},{1,17},{2,18},{3,19},{16,0},{17,1},{18,2},{19,3},{4,20},{5,... | collective-permute-start | bytes 405512 | tf_op jit(solution)/shard_map/ppermute | solution.py:339
  18.1 13.1 %collective-permute-start.5 = (bf16[528,128]{1,0:T(8,128)(2,1)S(1)}, bf16[528,128]{1,0:T(8,128)(2,1)S(1)}, u32[]{:S(2)}, u32[]{:S(2)}) collective-permute-start(bf16[528,128]{1,0:T(8,128)(2,1)S(1)} %get-tuple-element.21), channel_id=1, source_target_pairs={{0,18},{1,19},{2,16},{3,17},{16,2},{17,3},{18,0},{19,1},{4,22},{5,... | collective-permute-start | bytes 405512 | tf_op jit(solution)/shard_map/ppermute | solution.py:339
  21.3 11.4 %collective-permute-start.6 = (bf16[528,128]{1,0:T(8,128)(2,1)S(1)}, bf16[528,128]{1,0:T(8,128)(2,1)S(1)}, u32[]{:S(2)}, u32[]{:S(2)}) collective-permute-start(bf16[528,128]{1,0:T(8,128)(2,1)S(1)} %get-tuple-element.22), channel_id=1, source_target_pairs={{0,2},{1,3},{2,0},{3,1},{16,18},{17,19},{18,16},{19,17},{4,6},{5,7... | collective-permute-start | bytes 405512 | tf_op jit(solution)/shard_map/ppermute | solution.py:339
  22.7 3.7 %collective-permute-start.8 = (f32[8,128]{1,0:T(8,128)S(1)}, f32[8,128]{1,0:T(8,128)S(1)}, u32[]{:S(2)}, u32[]{:S(2)}) collective-permute-start(f32[8,128]{1,0:T(8,128)S(1)} %score.4.rest_5_.own_ref), channel_id=1, source_target_pairs={{0,16},{1,17},{2,18},{3,19},{16,0},{17,1},{18,2},{19,3},{4,20},{5,... | collective-permute-start | bytes 12296 | tf_op jit(solution)/shard_map/ppermute | solution.py:339
  26.4 11.6 %collective-permute-start.10 = (f32[8,128]{1,0:T(8,128)S(1)}, f32[8,128]{1,0:T(8,128)S(1)}, u32[]{:S(2)}, u32[]{:S(2)}) collective-permute-start(f32[8,128]{1,0:T(8,128)S(1)} %merge.1.rest_2_), channel_id=1, source_target_pairs={{0,3},{1,2},{2,1},{3,0},{16,19},{17,18},{18,17},{19,16},{4,7},{5,6... | collective-permute-start | bytes 12296 | tf_op jit(solution)/shard_map/ppermute | solution.py:339
  28.9 9.1 %collective-permute-start.9 = (f32[8,128]{1,0:T(8,128)S(1)}, f32[8,128]{1,0:T(8,128)S(1)}, u32[]{:S(2)}, u32[]{:S(2)}) collective-permute-start(f32[8,128]{1,0:T(8,128)S(1)} %merge.1.rest_2_), channel_id=1, source_target_pairs={{0,1},{1,0},{2,3},{3,2},{16,17},{17,16},{18,19},{19,18},{4,5},{5,4... | collective-permute-start | bytes 12296 | tf_op jit(solution)/shard_map/ppermute | solution.py:339
  29.2 5.7 %copy-start.2 = (bf16[1,1,768,1024]{3,2,1,0:T(8,128)(2,1)S(1)}, bf16[1,1,768,1024]{3,2,1,0:T(8,128)(2,1)}, u32[]{:S(2)}) copy-start(bf16[1,1,768,1024]{3,2,1,0:T(8,128)(2,1)} %param.12) | copy-start | bytes 4718596
  29.2 5.7 %copy-start.3 = (bf16[1,1,768,1024]{3,2,1,0:T(8,128)(2,1)S(1)}, bf16[1,1,768,1024]{3,2,1,0:T(8,128)(2,1)}, u32[]{:S(2)}) copy-start(bf16[1,1,768,1024]{3,2,1,0:T(8,128)(2,1)} %param.13) | copy-start | bytes 4718596
  29.3 5.5 %copy-start = (f32[1,1,768,1024]{3,2,1,0:T(8,128)S(1)}, f32[1,1,768,1024]{3,2,1,0:T(8,128)}, u32[]{:S(2)}) copy-start(f32[1,1,768,1024]{3,2,1,0:T(8,128)} %param.11) | copy-start | bytes 9437188
  29.3 8.8 %collective-permute-start.11 = (f32[8,128]{1,0:T(8,128)S(1)}, f32[8,128]{1,0:T(8,128)S(1)}, u32[]{:S(2)}, u32[]{:S(2)}) collective-permute-start(f32[8,128]{1,0:T(8,128)S(1)} %score.5.rest_1_.rest_2_), channel_id=1, source_target_pairs={{0,16},{1,17},{2,18},{3,19},{16,0},{17,1},{18,2},{19,3},{4,20},{5,... | collective-permute-start | bytes 12296 | tf_op jit(solution)/shard_map/ppermute | solution.py:339
  31.3 6.7 %collective-permute-start.13 = (f32[8,128]{1,0:T(8,128)S(1)}, f32[8,128]{1,0:T(8,128)S(1)}, u32[]{:S(2)}, u32[]{:S(2)}) collective-permute-start(f32[8,128]{1,0:T(8,128)S(1)} %score.6.rest_1_), channel_id=1, source_target_pairs={{0,18},{1,19},{2,16},{3,17},{16,2},{17,3},{18,0},{19,1},{4,22},{5,... | collective-permute-start | bytes 12296 | tf_op jit(solution)/shard_map/ppermute | solution.py:339
  32.8 5.2 %collective-permute-start.12 = (f32[8,128]{1,0:T(8,128)S(1)}, f32[8,128]{1,0:T(8,128)S(1)}, u32[]{:S(2)}, u32[]{:S(2)}) collective-permute-start(f32[8,128]{1,0:T(8,128)S(1)} %score.7.rest_3_), channel_id=1, source_target_pairs={{0,2},{1,3},{2,0},{3,1},{16,18},{17,19},{18,16},{19,17},{4,6},{5,7... | collective-permute-start | bytes 12296 | tf_op jit(solution)/shard_map/ppermute | solution.py:339
  34.8 3.3 %copy-start.4 = (s32[1,512,8]{1,2,0:T(8,128)S(1)}, s32[1,512,8]{1,2,0:T(8,128)}, u32[]{:S(2)}) copy-start(s32[1,512,8]{1,2,0:T(8,128)} %param.9) | copy-start | bytes 49156

commit v18 on v17

--- a/solution.py
+++ b/solution.py
@@ -230,33 +230,43 @@
 
 
 def update_kernel(items, cap, own_ref, other_ref, grad_ref, master_ref, moment_ref, second_ref, *rest):
-    chunks = dict(zip(items, rest))
+    chunks = rest[: len(items)]
     _, update_hbm, rows, scaled, total, update, sems = rest[len(items) :]
     hid, half = update.shape
-    block = total.shape[1]
     width = min(half, 4 * LANES)
-    height = block // 2
+    height = LANES
     data_rows = half // LANES * cap
-    rows[...] = jnp.zeros(rows.shape, BF16)
-    for at, ((side, k), chunk) in enumerate(chunks.items()):
-        slot = (ep_index() ^ k) * cap
-        lanes = pl.ds(pl.multiple_of(slot // LANES * LANES, LANES), LANES)
-        start = pl.multiple_of(at * LANES + slot % LANES, cap)
-        for part in range(half // LANES):
-            rows[pl.ds(start, cap), part * LANES : (part + 1) * LANES] = chunk[
-                part * cap : (part + 1) * cap, :
+    me = ep_index()
+    for at in range(0, len(items), 2):
+        parts = []
+        for turn, ((side, k), chunk) in enumerate(zip(items[at : at + 2], chunks[at : at + 2])):
+            slot = (me ^ k) * cap
+            lanes = pl.ds(pl.multiple_of(slot // LANES * LANES, LANES), LANES)
+            place = slot % LANES if turn == 0 else (LANES - cap) - slot % LANES
+            start = pl.multiple_of(at // 2 * LANES + place, cap)
+            for part in range(half // LANES):
+                rows[pl.ds(start, cap), part * LANES : (part + 1) * LANES] = chunk[
+                    part * cap : (part + 1) * cap, :
+                ]
+            line = jnp.sum(chunk[data_rows:, :].astype(F32), axis=0, keepdims=True)
+            parts.append(((own_ref, other_ref)[side], lanes, line))
+        if len(parts) == 1:
+            start = pl.multiple_of(at // 2 * LANES + (LANES - cap) - place, cap)
+            rows[pl.ds(start, cap), :] = jnp.zeros((cap, half), BF16)
+        for top in range(0, hid, LANES):
+            values = [
+                hidden[top : top + LANES, lanes].astype(F32) * line for hidden, lanes, line in parts
             ]
-        line = jnp.sum(chunk[data_rows:, :].astype(F32), axis=0, keepdims=True)
-        scale_into(scaled, at * LANES, (own_ref, other_ref)[side].at[:, lanes], line)
-
-    def multiply(at):
-        total[at % 2] = jnp.dot(
-            scaled[at * block : (at + 1) * block, :], rows[...], preferred_element_type=F32
-        )
-
-    def moments(at, top, columns):
-        lines = slice(at * block + top, at * block + top + TILE)
-        grad = total[at % 2, top : top + TILE, columns] + grad_ref[lines, columns]
+            if len(values) == 2:
+                values[0] += pltpu.roll(values[1], LANES - cap, axis=1)
+            scaled[top : top + LANES, at // 2 * LANES : (at // 2 + 1) * LANES] = values[0].astype(
+                BF16
+            )
+    total[...] = jnp.dot(scaled[...], rows[...], preferred_element_type=F32)
+
+    def moments(top, columns):
+        lines = slice(top, top + TILE)
+        grad = total[lines, columns] + grad_ref[lines, columns]
         first = moment_ref[lines, columns].astype(F32) * (beta_first / (1.0 - beta_first)) + grad
         square = (
             second_ref[lines, columns].astype(F32) * (beta_second / (1.0 - beta_second))
@@ -268,37 +278,33 @@
         scale = square * root * (second_unit**0.5 / first_unit) + adam_eps / first_unit
         return first, pl.reciprocal(scale, approx=True)
 
-    def finish(at, top, columns, first, scale):
-        lines = slice(at * block + top, at * block + top + TILE)
+    def finish(top, columns, first, scale):
+        lines = slice(top, top + TILE)
         update[lines, columns] = first * scale + decay_rate * master_ref[lines, columns]
 
     copies = []
-    multiply(0)
-    for at in range(hid // block):
-        if at + 1 < hid // block:
-            multiply(at + 1)
-        pieces = [
-            (top, slice(column, column + width))
-            for top in range(0, block, TILE)
-            for column in range(0, half, width)
-        ]
-        held = {}
-        for turn in range(len(pieces) + 2):
-            if turn < len(pieces):
-                held[turn, 0] = moments(at, *pieces[turn])
-            if 0 <= turn - 1 < len(pieces):
-                held[turn - 1, 1] = inverse(*held.pop((turn - 1, 0)))
-            if turn >= 2:
-                finish(at, *pieces[turn - 2], *held.pop((turn - 2, 1)))
-                top, columns = pieces[turn - 2]
-                if (top + TILE) % height == 0 and columns.stop == half:
-                    lines = slice(at * block + top + TILE - height, at * block + top + TILE)
-                    copies.append(
-                        pltpu.make_async_copy(
-                            update.at[lines, :], update_hbm.at[lines, :], sems.at[len(copies)]
-                        )
+    pieces = [
+        (top, slice(column, column + width))
+        for top in range(0, hid, TILE)
+        for column in range(0, half, width)
+    ]
+    held = {}
+    for turn in range(len(pieces) + 2):
+        if turn < len(pieces):
+            held[turn, 0] = moments(*pieces[turn])
+        if 0 <= turn - 1 < len(pieces):
+            held[turn - 1, 1] = inverse(*held.pop((turn - 1, 0)))
+        if turn >= 2:
+            finish(*pieces[turn - 2], *held.pop((turn - 2, 1)))
+            top, columns = pieces[turn - 2]
+            if (top + TILE) % height == 0 and columns.stop == half:
+                lines = slice(top + TILE - height, top + TILE)
+                copies.append(
+                    pltpu.make_async_copy(
+                        update.at[lines, :], update_hbm.at[lines, :], sems.at[len(copies)]
                     )
-                    copies[-1].start()
+                )
+                copies[-1].start()
     for copy in copies:
         copy.wait()
 
@@ -460,21 +466,21 @@
     last_scores = scored([(0, far)], other_far)
     returned[far] = [moved(last_scores, 0, far), moved(other_far, 1, far)]
 
-    block = min(hid, 2 * LANES)
+    depth = -(-len(added) // 2) * LANES
     update = pl.pallas_call(
         functools.partial(update_kernel, added, cap),
         out_shape=jax.ShapeDtypeStruct((hid, half), F32),
         in_specs=specs(pltpu.VMEM, 6 + len(added)) + specs(pl.ANY, 1),
         out_specs=specs(pltpu.HBM, 1)[0],
         scratch_shapes=[
-            pltpu.VMEM((len(added) * LANES, half), BF16),
-            pltpu.VMEM((hid, len(added) * LANES), BF16),
-            pltpu.VMEM((2, block, half), F32),
+            pltpu.VMEM((depth, half), BF16),
+            pltpu.VMEM((hid, depth), BF16),
             pltpu.VMEM((hid, half), F32),
-            pltpu.SemaphoreType.DMA((2 * hid // block,)),
+            pltpu.VMEM((hid, half), F32),
+            pltpu.SemaphoreType.DMA((hid // LANES,)),
         ],
         compiler_params=params(),
-        cost_estimate=cost(6 * LANES * hid * half, 16 * hid * half),
+        cost_estimate=cost(2 * depth * hid * half, 16 * hid * half),
         name="update",
     )(
         own_hidden,

time: 39.1 us -> 39 us (level)
  no operation moved by 1% of the time
where the time goes in v18:
time: 39 us; the launch traced here: 38.8 us
  starting transfers between devices  23.3 us (60%)
  Pallas kernels  11 us (28%)
  waiting for transfers between devices  3.81 us (10%)
  between operations  0.75 us (2%)
    ppermute x14, starting transfers between devices, moved(): return lax.ppermute(array, ('pair', 'ep'), pairs)  23.3 us
    ppermute x14, waiting for transfers between devices, moved(): return lax.ppermute(array, ('pair', 'ep'), pairs)  3.81 us
    pallas_call x1, Pallas kernels, local(): pl.pallas_call(functools.partial(later_kernel, last_items, late, cap), ou...  3.33 us
    pallas_call x1, Pallas kernels, local(): pl.pallas_call(functools.partial(update_kernel, added, cap), out_shape=ja...  3.03 us
    pallas_call x1, Pallas kernels, local(): pl.pallas_call(functools.partial(route_kernel, first_items, first, group,...  1.99 us
    pallas_call x1, Pallas kernels, local(): pl.pallas_call(functools.partial(sum_kernel, summed, group, cap), out_sha...  1.12 us
    pallas_call x1, Pallas kernels, local(): pl.pallas_call(functools.partial(combine_kernel, [(k, len(arrays)) for k,...  0.87 us
  transfers between devices with their start and end apart: 14, of which 4 were waited for; matrix products, arithmetic and copies ran while one was open for 0% of the time, Pallas kernels for 26%

profile of v18, /device:TPU:0, one launch (start us, length us, event | category | flops | bytes accessed | tf_op | source)
XLA Modules:
  0.0 38.8 jit_solution(17278966108857082948)
XLA Ops:
  0.6 3.0 %collective-permute-start = (bf16[768,256]{1,0:T(8,128)(2,1)}, bf16[768,256]{1,0:T(8,128)(2,1)S(1)}, u32[]{:S(2)}, u32[]{:S(2)}) collective-permute-start(bf16[768,256]{1,0:T(8,128)(2,1)} %bitcast.17), channel_id=1, source_target_pairs={{0,16},{1,17},{2,18},{3,19},{16,0},{17,1},{18,2},{19,3},{4,20},{5,... | collective-permute-start | bytes 1179656 | tf_op jit(solution)/shard_map/ppermute | solution.py:345
  3.7 2.0 %route.1 = (f32[16,512]{1,0:T(8,128)S(1)}, bf16[4,16,128]{2,1,0:T(8,128)(2,1)S(1)}, bf16[528,128]{1,0:T(8,128)(2,1)S(1)}, bf16[528,128]{1,0:T(8,128)(2,1)S(1)}, ...) custom-call(s32[8,512]{1,0:T(8,128)} %bitcast.23, bf16[8,512]{1,0:T(8,128)(2,1)} %bitcast.29, ...), custom_call_target="tpu_custom_call" | custom-call | flops 536870912 | bytes 3145728 | tf_op jit(solution)/shard_map/route/pallas_call | solution.py:369
  5.7 3.7 %collective-permute-start.1 = (bf16[528,128]{1,0:T(8,128)(2,1)S(1)}, bf16[528,128]{1,0:T(8,128)(2,1)S(1)}, u32[]{:S(2)}, u32[]{:S(2)}) collective-permute-start(bf16[528,128]{1,0:T(8,128)(2,1)S(1)} %get-tuple-element.13), channel_id=1, source_target_pairs={{0,3},{1,2},{2,1},{3,0},{16,19},{17,18},{18,17},{19,16},{4,7},{5,6... | collective-permute-start | bytes 405512 | tf_op jit(solution)/shard_map/ppermute | solution.py:345
  9.3 0.8 %collective-permute-start.3 = (bf16[528,128]{1,0:T(8,128)(2,1)S(1)}, bf16[528,128]{1,0:T(8,128)(2,1)S(1)}, u32[]{:S(2)}, u32[]{:S(2)}) collective-permute-start(bf16[528,128]{1,0:T(8,128)(2,1)S(1)} %get-tuple-element.15), channel_id=1, source_target_pairs={{0,19},{1,18},{2,17},{3,16},{16,3},{17,2},{18,1},{19,0},{4,23},{5,... | collective-permute-start | bytes 405512 | tf_op jit(solution)/shard_map/ppermute | solution.py:345
  10.2 1.4 %collective-permute-start.4 = (bf16[528,128]{1,0:T(8,128)(2,1)S(1)}, bf16[528,128]{1,0:T(8,128)(2,1)S(1)}, u32[]{:S(2)}, u32[]{:S(2)}) collective-permute-start(bf16[528,128]{1,0:T(8,128)(2,1)S(1)} %get-tuple-element.16), channel_id=1, source_target_pairs={{0,17},{1,16},{2,19},{3,18},{16,1},{17,0},{18,3},{19,2},{4,21},{5,... | collective-permute-start | bytes 405512 | tf_op jit(solution)/shard_map/ppermute | solution.py:345
  11.6 1.4 %collective-permute-done.other_ref = bf16[768,256]{1,0:T(8,128)(2,1)S(1)} collective-permute-done((bf16[768,256]{1,0:T(8,128)(2,1)}, bf16[768,256]{1,0:T(8,128)(2,1)S(1)}, u32[]{:S(2)}, u32[]{:S(2)}) %collective-permute-start) | collective-permute-done | bytes 393248 | tf_op jit(solution)/shard_map/ppermute | solution.py:345
  13.0 3.3 %later.1 = (f32[512,1024]{1,0:T(8,128)S(1)}, bf16[528,128]{1,0:T(8,128)(2,1)S(1)}, bf16[528,128]{1,0:T(8,128)(2,1)S(1)}, bf16[528,128]{1,0:T(8,128)(2,1)S(1)}, bf16[528,128]{1,0:T(8,128)(2,1)S(1)}) custom-call(f32[16,512]{1,0:T(8,128)S(1)} %get-tuple-element.17.slots_ref, bf16[4,16,128]{2,1,0:T(8,128)(2,1)S(1)} %get-tuple-element.18.tiles_ref, ...), custom_call_target="tpu_custom_call" | custom-call | flops 1342177280 | bytes 3145728 | tf_op jit(solution)/shard_map/later/pallas_call | solution.py:395
  16.3 1.8 %collective-permute-start.7 = (bf16[528,128]{1,0:T(8,128)(2,1)S(1)}, bf16[528,128]{1,0:T(8,128)(2,1)S(1)}, u32[]{:S(2)}, u32[]{:S(2)}) collective-permute-start(bf16[528,128]{1,0:T(8,128)(2,1)S(1)} %get-tuple-element.23), channel_id=1, source_target_pairs={{0,16},{1,17},{2,18},{3,19},{16,0},{17,1},{18,2},{19,3},{4,20},{5,... | collective-permute-start | bytes 405512 | tf_op jit(solution)/shard_map/ppermute | solution.py:345
  18.1 3.2 %collective-permute-start.5 = (bf16[528,128]{1,0:T(8,128)(2,1)S(1)}, bf16[528,128]{1,0:T(8,128)(2,1)S(1)}, u32[]{:S(2)}, u32[]{:S(2)}) collective-permute-start(bf16[528,128]{1,0:T(8,128)(2,1)S(1)} %get-tuple-element.21), channel_id=1, source_target_pairs={{0,18},{1,19},{2,16},{3,17},{16,2},{17,3},{18,0},{19,1},{4,22},{5,... | collective-permute-start | bytes 405512 | tf_op jit(solution)/shard_map/ppermute | solution.py:345
  21.3 0.1 collective-permute-start.6
  21.5 1.0 %collective-permute-done.4.rest_3_ = bf16[528,128]{1,0:T(8,128)(2,1)S(1)} collective-permute-done((bf16[528,128]{1,0:T(8,128)(2,1)S(1)}, bf16[528,128]{1,0:T(8,128)(2,1)S(1)}, u32[]{:S(2)}, u32[]{:S(2)}) %collective-permute-start.4) | collective-permute-done | bytes 135200 | tf_op jit(solution)/shard_map/ppermute | solution.py:345
  22.5 0.2 score.4.rest_5_.own_ref
  22.7 1.6 %collective-permute-start.8 = (f32[8,128]{1,0:T(8,128)S(1)}, f32[8,128]{1,0:T(8,128)S(1)}, u32[]{:S(2)}, u32[]{:S(2)}) collective-permute-start(f32[8,128]{1,0:T(8,128)S(1)} %score.4.rest_5_.own_ref), channel_id=1, source_target_pairs={{0,16},{1,17},{2,18},{3,19},{16,0},{17,1},{18,2},{19,3},{4,20},{5,... | collective-permute-start | bytes 12296 | tf_op jit(solution)/shard_map/ppermute | solution.py:345
  24.3 1.1 %sum.1._.grad_ref = f32[768,1024]{1,0:T(8,128)S(1)} custom-call(bf16[768,256]{1,0:T(8,128)(2,1)S(1)} %bitcast.19, bf16[768,256]{1,0:T(8,128)(2,1)S(1)} %collective-permute-done.other_ref, bf16[528,128]{1,0:T(8,128)(2,1)S(1)} %collective-permute-done.1.rest_0_, bf16[528,128]{1,0:T(8,128)(2,1)S(1)} %collective-permute-done.2.rest_1_, ...), custom_call_target="tpu_custom_call" | custom-call | flops 805306368 | bytes 3145728 | tf_op jit(solution)/shard_map/sum/pallas_call | solution.py:441
  25.5 0.9 %collective-permute-done.8.other_ref = f32[8,128]{1,0:T(8,128)S(1)} collective-permute-done((f32[8,128]{1,0:T(8,128)S(1)}, f32[8,128]{1,0:T(8,128)S(1)}, u32[]{:S(2)}, u32[]{:S(2)}) %collective-permute-start.8) | collective-permute-done | bytes 4128 | tf_op jit(solution)/shard_map/ppermute | solution.py:345
  26.4 2.5 %collective-permute-start.10 = (f32[8,128]{1,0:T(8,128)S(1)}, f32[8,128]{1,0:T(8,128)S(1)}, u32[]{:S(2)}, u32[]{:S(2)}) collective-permute-start(f32[8,128]{1,0:T(8,128)S(1)} %merge.1.rest_2_), channel_id=1, source_target_pairs={{0,3},{1,2},{2,1},{3,0},{16,19},{17,18},{18,17},{19,16},{4,7},{5,6... | collective-permute-start | bytes 12296 | tf_op jit(solution)/shard_map/ppermute | solution.py:345
  28.9 0.2 collective-permute-start.9
  29.2 0.1 score.5.rest_1_.rest_2_
  29.3 1.5 %collective-permute-start.11 = (f32[8,128]{1,0:T(8,128)S(1)}, f32[8,128]{1,0:T(8,128)S(1)}, u32[]{:S(2)}, u32[]{:S(2)}) collective-permute-start(f32[8,128]{1,0:T(8,128)S(1)} %score.5.rest_1_.rest_2_), channel_id=1, source_target_pairs={{0,16},{1,17},{2,18},{3,19},{16,0},{17,1},{18,2},{19,3},{4,20},{5,... | collective-permute-start | bytes 12296 | tf_op jit(solution)/shard_map/ppermute | solution.py:345
  30.8 0.4 %collective-permute-done.5.rest_0_ = bf16[528,128]{1,0:T(8,128)(2,1)S(1)} collective-permute-done((bf16[528,128]{1,0:T(8,128)(2,1)S(1)}, bf16[528,128]{1,0:T(8,128)(2,1)S(1)}, u32[]{:S(2)}, u32[]{:S(2)}) %collective-permute-start.5) | collective-permute-done | bytes 135200 | tf_op jit(solution)/shard_map/ppermute | solution.py:345
  31.3 1.4 %collective-permute-start.13 = (f32[8,128]{1,0:T(8,128)S(1)}, f32[8,128]{1,0:T(8,128)S(1)}, u32[]{:S(2)}, u32[]{:S(2)}) collective-permute-start(f32[8,128]{1,0:T(8,128)S(1)} %score.6.rest_1_), channel_id=1, source_target_pairs={{0,18},{1,19},{2,16},{3,17},{16,2},{17,3},{18,0},{19,1},{4,22},{5,... | collective-permute-start | bytes 12296 | tf_op jit(solution)/shard_map/ppermute | solution.py:345
  32.8 2.0 %collective-permute-start.12 = (f32[8,128]{1,0:T(8,128)S(1)}, f32[8,128]{1,0:T(8,128)S(1)}, u32[]{:S(2)}, u32[]{:S(2)}) collective-permute-start(f32[8,128]{1,0:T(8,128)S(1)} %score.7.rest_3_), channel_id=1, source_target_pairs={{0,2},{1,3},{2,0},{3,1},{16,18},{17,19},{18,16},{19,17},{4,6},{5,7... | collective-permute-start | bytes 12296 | tf_op jit(solution)/shard_map/ppermute | solution.py:345
  34.8 3.0 %update.1 = f32[768,1024]{1,0:T(8,128)} custom-call(bf16[768,256]{1,0:T(8,128)(2,1)S(1)} %bitcast.20, bf16[768,256]{1,0:T(8,128)(2,1)S(1)} %collective-permute-done.other_ref, f32[768,1024]{1,0:T(8,128)S(1)} %sum.1._.grad_ref, f32[768,1024]{1,0:T(8,128)S(1)} %bitcast.16, bf16[768,1024]{1,0:T(8,128)(2,1)S(1)} %bitcast.21, bf16[768,1024]{1,0:T(8,128)(2,1)S(1)} %bitcast.22, ...), custom_call_target="tpu_custom_call" | custom-call | flops 402653184 | bytes 12582912 | tf_op jit(solution)/shard_map/update/pallas_call | solution.py:470
  37.9 0.9 %combine.1 = f32[8,512]{1,0:T(8,128)} custom-call(s32[8,512]{1,0:T(8,128)S(1)} %bitcast.24, f32[16,512]{1,0:T(8,128)S(1)} %get-tuple-element.17.slots_ref, f32[8,128]{1,0:T(8,128)S(1)} %collective-permute-done.9.rest_0_, f32[8,128]{1,0:T(8,128)S(1)} %collective-permute-done.10.rest_1_, f32[8,128]{1,0:T(8,128)S(1)} %score.5.rest_1_.rest_2_, ...), custom_call_target="tpu_custom_call" | custom-call | flops 524288 | bytes 32768 | tf_op jit(solution)/shard_map/combine/pallas_call | solution.py:496
  (24 shorter events, 0.4 us)
Async XLA Ops:
  0.6 12.4 %copy-start.1 = (bf16[1,1,768,256]{3,2,1,0:T(8,128)(2,1)S(1)}, bf16[1,1,768,256]{3,2,1,0:T(8,128)(2,1)}, u32[]{:S(2)}) copy-start(bf16[1,1,768,256]{3,2,1,0:T(8,128)(2,1)} %param.10) | copy-start | bytes 1179652
  0.6 12.4 %collective-permute-start = (bf16[768,256]{1,0:T(8,128)(2,1)}, bf16[768,256]{1,0:T(8,128)(2,1)S(1)}, u32[]{:S(2)}, u32[]{:S(2)}) collective-permute-start(bf16[768,256]{1,0:T(8,128)(2,1)} %bitcast.17), channel_id=1, source_target_pairs={{0,16},{1,17},{2,18},{3,19},{16,0},{17,1},{18,2},{19,3},{4,20},{5,... | collective-permute-start | bytes 1179656 | tf_op jit(solution)/shard_map/ppermute | solution.py:345
  5.7 12.5 %collective-permute-start.1 = (bf16[528,128]{1,0:T(8,128)(2,1)S(1)}, bf16[528,128]{1,0:T(8,128)(2,1)S(1)}, u32[]{:S(2)}, u32[]{:S(2)}) collective-permute-start(bf16[528,128]{1,0:T(8,128)(2,1)S(1)} %get-tuple-element.13), channel_id=1, source_target_pairs={{0,3},{1,2},{2,1},{3,0},{16,19},{17,18},{18,17},{19,16},{4,7},{5,6... | collective-permute-start | bytes 405512 | tf_op jit(solution)/shard_map/ppermute | solution.py:345
  9.3 12.0 %collective-permute-start.2 = (bf16[528,128]{1,0:T(8,128)(2,1)S(1)}, bf16[528,128]{1,0:T(8,128)(2,1)S(1)}, u32[]{:S(2)}, u32[]{:S(2)}) collective-permute-start(bf16[528,128]{1,0:T(8,128)(2,1)S(1)} %get-tuple-element.14), channel_id=1, source_target_pairs={{0,1},{1,0},{2,3},{3,2},{16,17},{17,16},{18,19},{19,18},{4,5},{5,4... | collective-permute-start | bytes 405512 | tf_op jit(solution)/shard_map/ppermute | solution.py:345
  9.3 12.1 %collective-permute-start.3 = (bf16[528,128]{1,0:T(8,128)(2,1)S(1)}, bf16[528,128]{1,0:T(8,128)(2,1)S(1)}, u32[]{:S(2)}, u32[]{:S(2)}) collective-permute-start(bf16[528,128]{1,0:T(8,128)(2,1)S(1)} %get-tuple-element.15), channel_id=1, source_target_pairs={{0,19},{1,18},{2,17},{3,16},{16,3},{17,2},{18,1},{19,0},{4,23},{5,... | collective-permute-start | bytes 405512 | tf_op jit(solution)/shard_map/ppermute | solution.py:345
  10.2 12.3 %collective-permute-start.4 = (bf16[528,128]{1,0:T(8,128)(2,1)S(1)}, bf16[528,128]{1,0:T(8,128)(2,1)S(1)}, u32[]{:S(2)}, u32[]{:S(2)}) collective-permute-start(bf16[528,128]{1,0:T(8,128)(2,1)S(1)} %get-tuple-element.16), channel_id=1, source_target_pairs={{0,17},{1,16},{2,19},{3,18},{16,1},{17,0},{18,3},{19,2},{4,21},{5,... | collective-permute-start | bytes 405512 | tf_op jit(solution)/shard_map/ppermute | solution.py:345
  16.3 12.8 %collective-permute-start.7 = (bf16[528,128]{1,0:T(8,128)(2,1)S(1)}, bf16[528,128]{1,0:T(8,128)(2,1)S(1)}, u32[]{:S(2)}, u32[]{:S(2)}) collective-permute-start(bf16[528,128]{1,0:T(8,128)(2,1)S(1)} %get-tuple-element.23), channel_id=1, source_target_pairs={{0,16},{1,17},{2,18},{3,19},{16,0},{17,1},{18,2},{19,3},{4,20},{5,... | collective-permute-start | bytes 405512 | tf_op jit(solution)/shard_map/ppermute | solution.py:345
  18.1 13.1 %collective-permute-start.5 = (bf16[528,128]{1,0:T(8,128)(2,1)S(1)}, bf16[528,128]{1,0:T(8,128)(2,1)S(1)}, u32[]{:S(2)}, u32[]{:S(2)}) collective-permute-start(bf16[528,128]{1,0:T(8,128)(2,1)S(1)} %get-tuple-element.21), channel_id=1, source_target_pairs={{0,18},{1,19},{2,16},{3,17},{16,2},{17,3},{18,0},{19,1},{4,22},{5,... | collective-permute-start | bytes 405512 | tf_op jit(solution)/shard_map/ppermute | solution.py:345
  21.3 11.4 %collective-permute-start.6 = (bf16[528,128]{1,0:T(8,128)(2,1)S(1)}, bf16[528,128]{1,0:T(8,128)(2,1)S(1)}, u32[]{:S(2)}, u32[]{:S(2)}) collective-permute-start(bf16[528,128]{1,0:T(8,128)(2,1)S(1)} %get-tuple-element.22), channel_id=1, source_target_pairs={{0,2},{1,3},{2,0},{3,1},{16,18},{17,19},{18,16},{19,17},{4,6},{5,7... | collective-permute-start | bytes 405512 | tf_op jit(solution)/shard_map/ppermute | solution.py:345
  22.7 3.7 %collective-permute-start.8 = (f32[8,128]{1,0:T(8,128)S(1)}, f32[8,128]{1,0:T(8,128)S(1)}, u32[]{:S(2)}, u32[]{:S(2)}) collective-permute-start(f32[8,128]{1,0:T(8,128)S(1)} %score.4.rest_5_.own_ref), channel_id=1, source_target_pairs={{0,16},{1,17},{2,18},{3,19},{16,0},{17,1},{18,2},{19,3},{4,20},{5,... | collective-permute-start | bytes 12296 | tf_op jit(solution)/shard_map/ppermute | solution.py:345
  26.4 11.4 %collective-permute-start.10 = (f32[8,128]{1,0:T(8,128)S(1)}, f32[8,128]{1,0:T(8,128)S(1)}, u32[]{:S(2)}, u32[]{:S(2)}) collective-permute-start(f32[8,128]{1,0:T(8,128)S(1)} %merge.1.rest_2_), channel_id=1, source_target_pairs={{0,3},{1,2},{2,1},{3,0},{16,19},{17,18},{18,17},{19,16},{4,7},{5,6... | collective-permute-start | bytes 12296 | tf_op jit(solution)/shard_map/ppermute | solution.py:345
  28.9 8.9 %collective-permute-start.9 = (f32[8,128]{1,0:T(8,128)S(1)}, f32[8,128]{1,0:T(8,128)S(1)}, u32[]{:S(2)}, u32[]{:S(2)}) collective-permute-start(f32[8,128]{1,0:T(8,128)S(1)} %merge.1.rest_2_), channel_id=1, source_target_pairs={{0,1},{1,0},{2,3},{3,2},{16,17},{17,16},{18,19},{19,18},{4,5},{5,4... | collective-permute-start | bytes 12296 | tf_op jit(solution)/shard_map/ppermute | solution.py:345
  29.2 5.7 %copy-start.2 = (bf16[1,1,768,1024]{3,2,1,0:T(8,128)(2,1)S(1)}, bf16[1,1,768,1024]{3,2,1,0:T(8,128)(2,1)}, u32[]{:S(2)}) copy-start(bf16[1,1,768,1024]{3,2,1,0:T(8,128)(2,1)} %param.12) | copy-start | bytes 4718596
  29.2 5.7 %copy-start.3 = (bf16[1,1,768,1024]{3,2,1,0:T(8,128)(2,1)S(1)}, bf16[1,1,768,1024]{3,2,1,0:T(8,128)(2,1)}, u32[]{:S(2)}) copy-start(bf16[1,1,768,1024]{3,2,1,0:T(8,128)(2,1)} %param.13) | copy-start | bytes 4718596
  29.3 5.5 %copy-start = (f32[1,1,768,1024]{3,2,1,0:T(8,128)S(1)}, f32[1,1,768,1024]{3,2,1,0:T(8,128)}, u32[]{:S(2)}) copy-start(f32[1,1,768,1024]{3,2,1,0:T(8,128)} %param.11) | copy-start | bytes 9437188
  29.3 8.6 %collective-permute-start.11 = (f32[8,128]{1,0:T(8,128)S(1)}, f32[8,128]{1,0:T(8,128)S(1)}, u32[]{:S(2)}, u32[]{:S(2)}) collective-permute-start(f32[8,128]{1,0:T(8,128)S(1)} %score.5.rest_1_.rest_2_), channel_id=1, source_target_pairs={{0,16},{1,17},{2,18},{3,19},{16,0},{17,1},{18,2},{19,3},{4,20},{5,... | collective-permute-start | bytes 12296 | tf_op jit(solution)/shard_map/ppermute | solution.py:345
  31.3 6.6 %collective-permute-start.13 = (f32[8,128]{1,0:T(8,128)S(1)}, f32[8,128]{1,0:T(8,128)S(1)}, u32[]{:S(2)}, u32[]{:S(2)}) collective-permute-start(f32[8,128]{1,0:T(8,128)S(1)} %score.6.rest_1_), channel_id=1, source_target_pairs={{0,18},{1,19},{2,16},{3,17},{16,2},{17,3},{18,0},{19,1},{4,22},{5,... | collective-permute-start | bytes 12296 | tf_op jit(solution)/shard_map/ppermute | solution.py:345
  32.8 5.1 %collective-permute-start.12 = (f32[8,128]{1,0:T(8,128)S(1)}, f32[8,128]{1,0:T(8,128)S(1)}, u32[]{:S(2)}, u32[]{:S(2)}) collective-permute-start(f32[8,128]{1,0:T(8,128)S(1)} %score.7.rest_3_), channel_id=1, source_target_pairs={{0,2},{1,3},{2,0},{3,1},{16,18},{17,19},{18,16},{19,17},{4,6},{5,7... | collective-permute-start | bytes 12296 | tf_op jit(solution)/shard_map/ppermute | solution.py:345
  34.8 3.1 %copy-start.4 = (s32[1,512,8]{1,2,0:T(8,128)S(1)}, s32[1,512,8]{1,2,0:T(8,128)}, u32[]{:S(2)}) copy-start(s32[1,512,8]{1,2,0:T(8,128)} %param.9) | copy-start | bytes 49156

commit v19 on v18

--- a/solution.py
+++ b/solution.py
@@ -66,22 +66,17 @@
 def fill_chunks(steps, cap, picks, held, copies, tiles, chunks):
     half = held.shape[2]
     data_rows = half // LANES * cap
-    step = min(half, 2 * LANES)
     pick = jnp.concatenate([picks[k] for k in steps], axis=0)
     for side in range(2):
         for k in steps:
             chunks[side, k][data_rows:, :] = tiles[k]
         copies[side].wait()
-        for column in range(0, half, step):
-            block = jnp.dot(
-                pick, held[side, :, column : column + step], preferred_element_type=F32
-            ).astype(BF16)
-            for at, k in enumerate(steps):
-                for part in range(step // LANES):
-                    top = (column // LANES + part) * cap
-                    chunks[side, k][top : top + cap, :] = block[
-                        at * cap : (at + 1) * cap, part * LANES : (part + 1) * LANES
-                    ]
+        block = jnp.dot(pick, held[side], preferred_element_type=F32).astype(BF16)
+        for at, k in enumerate(steps):
+            for part in range(half // LANES):
+                chunks[side, k][part * cap : (part + 1) * cap, :] = block[
+                    at * cap : (at + 1) * cap, part * LANES : (part + 1) * LANES
+                ]
 
 
 def route_kernel(
@@ -146,26 +141,18 @@
     chunks = dict(zip(items, rest))
     held, master_ref, sems = rest[len(items) :]
     copies = start_grads(grads_hbm, held, sems)
-    half = master_ref.shape[1]
-    step = min(half, 4 * LANES)
-    parts = [slice(column, column + step) for column in range(0, half, step)]
-    loads = [
-        pltpu.make_async_copy(master_hbm.at[:, part], master_ref.at[:, part], sems.at[2 + at])
-        for at, part in enumerate(parts)
-    ]
-    for load in loads:
-        load.start()
+    load = pltpu.make_async_copy(master_hbm, master_ref, sems.at[2])
+    load.start()
     slots = slots_ref[...]
     picks = {k: pick_rows(slots, k, cap) for k in steps}
     fill_chunks(steps, cap, picks, held, copies, tiles_ref, chunks)
     slot_count = own_ref.shape[1]
-    for load, part in zip(loads, parts):
-        load.wait()
-        weights = master_ref[:, part].astype(BF16)
-        for at, ref in ((0, own_ref), (slot_count, other_ref)):
-            inner_ref[at : at + slot_count, part] = lax.dot_general(
-                ref[...], weights, (((0,), (0,)), ((), ())), preferred_element_type=F32
-            )
+    load.wait()
+    weights = master_ref[...].astype(BF16)
+    for at, ref in ((0, own_ref), (slot_count, other_ref)):
+        inner_ref[at : at + slot_count, :] = lax.dot_general(
+            ref[...], weights, (((0,), (0,)), ((), ())), preferred_element_type=F32
+        )
 
 
 def score_kernel(items, group, cap, inner_ref, *rest):
@@ -403,7 +390,7 @@
         scratch_shapes=[
             held,
             pltpu.VMEM((hid, half), F32),
-            pltpu.SemaphoreType.DMA((2 + half // min(half, 4 * LANES),)),
+            pltpu.SemaphoreType.DMA((3,)),
         ],
         compiler_params=params(),
         cost_estimate=cost(

time: 39 us -> 39.1 us (level)
  waiting for transfers between devices: 3.81 us -> 2.87 us
  starting transfers between devices: 23.3 us -> 24.1 us
    ppermute x14, waiting for transfers between devices: 3.81 us -> 2.87 us  [moved(): return lax.ppermute(array, ('pair', 'ep'), pairs)]
    ppermute x14, starting transfers between devices: 23.3 us -> 24.1 us  [moved(): return lax.ppermute(array, ('pair', 'ep'), pairs)]
  transfers between devices with their start and end apart: 14 -> 14, of which waited for: 4 -> 3; matrix products, arithmetic and copies ran while one was open for 0% -> 0% of each run, Pallas kernels for 26% -> 27%
where the time goes in v19:
time: 39.1 us; the launch traced here: 39 us
  starting transfers between devices  24.1 us (62%)
  Pallas kernels  11.2 us (29%)
  waiting for transfers between devices  2.87 us (7%)
  between operations  0.75 us (2%)
    ppermute x14, starting transfers between devices, moved(): return lax.ppermute(array, ('pair', 'ep'), pairs)  24.1 us
    pallas_call x1, Pallas kernels, local(): pl.pallas_call(functools.partial(later_kernel, last_items, late, cap), ou...  3.6 us
    pallas_call x1, Pallas kernels, local(): pl.pallas_call(functools.partial(update_kernel, added, cap), out_shape=ja...  3.03 us
    ppermute x14, waiting for transfers between devices, moved(): return lax.ppermute(array, ('pair', 'ep'), pairs)  2.87 us
    pallas_call x1, Pallas kernels, local(): pl.pallas_call(functools.partial(route_kernel, first_items, first, group,...  1.99 us
    pallas_call x1, Pallas kernels, local(): pl.pallas_call(functools.partial(sum_kernel, summed, group, cap), out_sha...  1.12 us
    pallas_call x1, Pallas kernels, local(): pl.pallas_call(functools.partial(combine_kernel, [(k, len(arrays)) for k,...  0.87 us
  transfers between devices with their start and end apart: 14, of which 3 were waited for; matrix products, arithmetic and copies ran while one was open for 0% of the time, Pallas kernels for 27%

profile of v19, /device:TPU:0, one launch (start us, length us, event | category | flops | bytes accessed | tf_op | source)
XLA Modules:
  0.0 39.0 jit_solution(4330625566853087355)
XLA Ops:
  0.6 3.0 %collective-permute-start = (bf16[768,256]{1,0:T(8,128)(2,1)}, bf16[768,256]{1,0:T(8,128)(2,1)S(1)}, u32[]{:S(2)}, u32[]{:S(2)}) collective-permute-start(bf16[768,256]{1,0:T(8,128)(2,1)} %bitcast.17), channel_id=1, source_target_pairs={{0,16},{1,17},{2,18},{3,19},{16,0},{17,1},{18,2},{19,3},{4,20},{5,... | collective-permute-start | bytes 1179656 | tf_op jit(solution)/shard_map/ppermute | solution.py:332
  3.7 2.0 %route.1 = (f32[16,512]{1,0:T(8,128)S(1)}, bf16[4,16,128]{2,1,0:T(8,128)(2,1)S(1)}, bf16[528,128]{1,0:T(8,128)(2,1)S(1)}, bf16[528,128]{1,0:T(8,128)(2,1)S(1)}, ...) custom-call(s32[8,512]{1,0:T(8,128)} %bitcast.23, bf16[8,512]{1,0:T(8,128)(2,1)} %bitcast.29, ...), custom_call_target="tpu_custom_call" | custom-call | flops 536870912 | bytes 3145728 | tf_op jit(solution)/shard_map/route/pallas_call | solution.py:356
  5.7 3.7 %collective-permute-start.1 = (bf16[528,128]{1,0:T(8,128)(2,1)S(1)}, bf16[528,128]{1,0:T(8,128)(2,1)S(1)}, u32[]{:S(2)}, u32[]{:S(2)}) collective-permute-start(bf16[528,128]{1,0:T(8,128)(2,1)S(1)} %get-tuple-element.13), channel_id=1, source_target_pairs={{0,3},{1,2},{2,1},{3,0},{16,19},{17,18},{18,17},{19,16},{4,7},{5,6... | collective-permute-start | bytes 405512 | tf_op jit(solution)/shard_map/ppermute | solution.py:332
  9.3 0.8 %collective-permute-start.3 = (bf16[528,128]{1,0:T(8,128)(2,1)S(1)}, bf16[528,128]{1,0:T(8,128)(2,1)S(1)}, u32[]{:S(2)}, u32[]{:S(2)}) collective-permute-start(bf16[528,128]{1,0:T(8,128)(2,1)S(1)} %get-tuple-element.15), channel_id=1, source_target_pairs={{0,19},{1,18},{2,17},{3,16},{16,3},{17,2},{18,1},{19,0},{4,23},{5,... | collective-permute-start | bytes 405512 | tf_op jit(solution)/shard_map/ppermute | solution.py:332
  10.2 1.4 %collective-permute-start.4 = (bf16[528,128]{1,0:T(8,128)(2,1)S(1)}, bf16[528,128]{1,0:T(8,128)(2,1)S(1)}, u32[]{:S(2)}, u32[]{:S(2)}) collective-permute-start(bf16[528,128]{1,0:T(8,128)(2,1)S(1)} %get-tuple-element.16), channel_id=1, source_target_pairs={{0,17},{1,16},{2,19},{3,18},{16,1},{17,0},{18,3},{19,2},{4,21},{5,... | collective-permute-start | bytes 405512 | tf_op jit(solution)/shard_map/ppermute | solution.py:332
  11.6 1.4 %collective-permute-done.other_ref = bf16[768,256]{1,0:T(8,128)(2,1)S(1)} collective-permute-done((bf16[768,256]{1,0:T(8,128)(2,1)}, bf16[768,256]{1,0:T(8,128)(2,1)S(1)}, u32[]{:S(2)}, u32[]{:S(2)}) %collective-permute-start) | collective-permute-done | bytes 393248 | tf_op jit(solution)/shard_map/ppermute | solution.py:332
  13.0 3.6 %later.1 = (f32[512,1024]{1,0:T(8,128)S(1)}, bf16[528,128]{1,0:T(8,128)(2,1)S(1)}, bf16[528,128]{1,0:T(8,128)(2,1)S(1)}, bf16[528,128]{1,0:T(8,128)(2,1)S(1)}, bf16[528,128]{1,0:T(8,128)(2,1)S(1)}) custom-call(f32[16,512]{1,0:T(8,128)S(1)} %get-tuple-element.17.slots_ref, bf16[4,16,128]{2,1,0:T(8,128)(2,1)S(1)} %get-tuple-element.18.tiles_ref, ...), custom_call_target="tpu_custom_call" | custom-call | flops 1342177280 | bytes 3145728 | tf_op jit(solution)/shard_map/later/pallas_call | solution.py:382
  16.6 1.8 %collective-permute-start.7 = (bf16[528,128]{1,0:T(8,128)(2,1)S(1)}, bf16[528,128]{1,0:T(8,128)(2,1)S(1)}, u32[]{:S(2)}, u32[]{:S(2)}) collective-permute-start(bf16[528,128]{1,0:T(8,128)(2,1)S(1)} %get-tuple-element.23), channel_id=1, source_target_pairs={{0,16},{1,17},{2,18},{3,19},{16,0},{17,1},{18,2},{19,3},{4,20},{5,... | collective-permute-start | bytes 405512 | tf_op jit(solution)/shard_map/ppermute | solution.py:332
  18.4 3.2 %collective-permute-start.5 = (bf16[528,128]{1,0:T(8,128)(2,1)S(1)}, bf16[528,128]{1,0:T(8,128)(2,1)S(1)}, u32[]{:S(2)}, u32[]{:S(2)}) collective-permute-start(bf16[528,128]{1,0:T(8,128)(2,1)S(1)} %get-tuple-element.21), channel_id=1, source_target_pairs={{0,18},{1,19},{2,16},{3,17},{16,2},{17,3},{18,0},{19,1},{4,22},{5,... | collective-permute-start | bytes 405512 | tf_op jit(solution)/shard_map/ppermute | solution.py:332
  21.6 0.1 collective-permute-start.6
  21.7 0.2 score.4.rest_5_.own_ref
  21.9 2.2 %collective-permute-start.8 = (f32[8,128]{1,0:T(8,128)S(1)}, f32[8,128]{1,0:T(8,128)S(1)}, u32[]{:S(2)}, u32[]{:S(2)}) collective-permute-start(f32[8,128]{1,0:T(8,128)S(1)} %score.4.rest_5_.own_ref), channel_id=1, source_target_pairs={{0,16},{1,17},{2,18},{3,19},{16,0},{17,1},{18,2},{19,3},{4,20},{5,... | collective-permute-start | bytes 12296 | tf_op jit(solution)/shard_map/ppermute | solution.py:332
  24.1 1.1 %sum.1._.grad_ref = f32[768,1024]{1,0:T(8,128)S(1)} custom-call(bf16[768,256]{1,0:T(8,128)(2,1)S(1)} %bitcast.19, bf16[768,256]{1,0:T(8,128)(2,1)S(1)} %collective-permute-done.other_ref, bf16[528,128]{1,0:T(8,128)(2,1)S(1)} %collective-permute-done.1.rest_0_, bf16[528,128]{1,0:T(8,128)(2,1)S(1)} %collective-permute-done.2.rest_1_, ...), custom_call_target="tpu_custom_call" | custom-call | flops 805306368 | bytes 3145728 | tf_op jit(solution)/shard_map/sum/pallas_call | solution.py:428
  25.3 0.9 %collective-permute-done.8.other_ref = f32[8,128]{1,0:T(8,128)S(1)} collective-permute-done((f32[8,128]{1,0:T(8,128)S(1)}, f32[8,128]{1,0:T(8,128)S(1)}, u32[]{:S(2)}, u32[]{:S(2)}) %collective-permute-start.8) | collective-permute-done | bytes 4128 | tf_op jit(solution)/shard_map/ppermute | solution.py:332
  26.2 3.0 %collective-permute-start.10 = (f32[8,128]{1,0:T(8,128)S(1)}, f32[8,128]{1,0:T(8,128)S(1)}, u32[]{:S(2)}, u32[]{:S(2)}) collective-permute-start(f32[8,128]{1,0:T(8,128)S(1)} %merge.1.rest_2_), channel_id=1, source_target_pairs={{0,3},{1,2},{2,1},{3,0},{16,19},{17,18},{18,17},{19,16},{4,7},{5,6... | collective-permute-start | bytes 12296 | tf_op jit(solution)/shard_map/ppermute | solution.py:332
  29.2 0.2 collective-permute-start.9
  29.4 0.1 score.5.rest_1_.rest_2_
  29.6 1.4 %collective-permute-start.11 = (f32[8,128]{1,0:T(8,128)S(1)}, f32[8,128]{1,0:T(8,128)S(1)}, u32[]{:S(2)}, u32[]{:S(2)}) collective-permute-start(f32[8,128]{1,0:T(8,128)S(1)} %score.5.rest_1_.rest_2_), channel_id=1, source_target_pairs={{0,16},{1,17},{2,18},{3,19},{16,0},{17,1},{18,2},{19,3},{4,20},{5,... | collective-permute-start | bytes 12296 | tf_op jit(solution)/shard_map/ppermute | solution.py:332
  31.0 0.6 %collective-permute-done.5.rest_0_ = bf16[528,128]{1,0:T(8,128)(2,1)S(1)} collective-permute-done((bf16[528,128]{1,0:T(8,128)(2,1)S(1)}, bf16[528,128]{1,0:T(8,128)(2,1)S(1)}, u32[]{:S(2)}, u32[]{:S(2)}) %collective-permute-start.5) | collective-permute-done | bytes 135200 | tf_op jit(solution)/shard_map/ppermute | solution.py:332
  31.6 0.9 %collective-permute-start.13 = (f32[8,128]{1,0:T(8,128)S(1)}, f32[8,128]{1,0:T(8,128)S(1)}, u32[]{:S(2)}, u32[]{:S(2)}) collective-permute-start(f32[8,128]{1,0:T(8,128)S(1)} %score.6.rest_1_), channel_id=1, source_target_pairs={{0,18},{1,19},{2,16},{3,17},{16,2},{17,3},{18,0},{19,1},{4,22},{5,... | collective-permute-start | bytes 12296 | tf_op jit(solution)/shard_map/ppermute | solution.py:332
  32.5 0.1 score.7.rest_3_
  32.6 2.3 %collective-permute-start.12 = (f32[8,128]{1,0:T(8,128)S(1)}, f32[8,128]{1,0:T(8,128)S(1)}, u32[]{:S(2)}, u32[]{:S(2)}) collective-permute-start(f32[8,128]{1,0:T(8,128)S(1)} %score.7.rest_3_), channel_id=1, source_target_pairs={{0,2},{1,3},{2,0},{3,1},{16,18},{17,19},{18,16},{19,17},{4,6},{5,7... | collective-permute-start | bytes 12296 | tf_op jit(solution)/shard_map/ppermute | solution.py:332
  35.0 3.0 %update.1 = f32[768,1024]{1,0:T(8,128)} custom-call(bf16[768,256]{1,0:T(8,128)(2,1)S(1)} %bitcast.20, bf16[768,256]{1,0:T(8,128)(2,1)S(1)} %collective-permute-done.other_ref, f32[768,1024]{1,0:T(8,128)S(1)} %sum.1._.grad_ref, f32[768,1024]{1,0:T(8,128)S(1)} %bitcast.16, bf16[768,1024]{1,0:T(8,128)(2,1)S(1)} %bitcast.21, bf16[768,1024]{1,0:T(8,128)(2,1)S(1)} %bitcast.22, ...), custom_call_target="tpu_custom_call" | custom-call | flops 402653184 | bytes 12582912 | tf_op jit(solution)/shard_map/update/pallas_call | solution.py:457
  38.1 0.9 %combine.1 = f32[8,512]{1,0:T(8,128)} custom-call(s32[8,512]{1,0:T(8,128)S(1)} %bitcast.24, f32[16,512]{1,0:T(8,128)S(1)} %get-tuple-element.17.slots_ref, f32[8,128]{1,0:T(8,128)S(1)} %collective-permute-done.9.rest_0_, f32[8,128]{1,0:T(8,128)S(1)} %collective-permute-done.10.rest_1_, f32[8,128]{1,0:T(8,128)S(1)} %score.5.rest_1_.rest_2_, ...), custom_call_target="tpu_custom_call" | custom-call | flops 524288 | bytes 32768 | tf_op jit(solution)/shard_map/combine/pallas_call | solution.py:483
  (24 shorter events, 0.3 us)
Async XLA Ops:
  0.6 12.4 %copy-start.1 = (bf16[1,1,768,256]{3,2,1,0:T(8,128)(2,1)S(1)}, bf16[1,1,768,256]{3,2,1,0:T(8,128)(2,1)}, u32[]{:S(2)}) copy-start(bf16[1,1,768,256]{3,2,1,0:T(8,128)(2,1)} %param.10) | copy-start | bytes 1179652
  0.6 12.4 %collective-permute-start = (bf16[768,256]{1,0:T(8,128)(2,1)}, bf16[768,256]{1,0:T(8,128)(2,1)S(1)}, u32[]{:S(2)}, u32[]{:S(2)}) collective-permute-start(bf16[768,256]{1,0:T(8,128)(2,1)} %bitcast.17), channel_id=1, source_target_pairs={{0,16},{1,17},{2,18},{3,19},{16,0},{17,1},{18,2},{19,3},{4,20},{5,... | collective-permute-start | bytes 1179656 | tf_op jit(solution)/shard_map/ppermute | solution.py:332
  5.7 12.8 %collective-permute-start.1 = (bf16[528,128]{1,0:T(8,128)(2,1)S(1)}, bf16[528,128]{1,0:T(8,128)(2,1)S(1)}, u32[]{:S(2)}, u32[]{:S(2)}) collective-permute-start(bf16[528,128]{1,0:T(8,128)(2,1)S(1)} %get-tuple-element.13), channel_id=1, source_target_pairs={{0,3},{1,2},{2,1},{3,0},{16,19},{17,18},{18,17},{19,16},{4,7},{5,6... | collective-permute-start | bytes 405512 | tf_op jit(solution)/shard_map/ppermute | solution.py:332
  9.3 12.2 %collective-permute-start.2 = (bf16[528,128]{1,0:T(8,128)(2,1)S(1)}, bf16[528,128]{1,0:T(8,128)(2,1)S(1)}, u32[]{:S(2)}, u32[]{:S(2)}) collective-permute-start(bf16[528,128]{1,0:T(8,128)(2,1)S(1)} %get-tuple-element.14), channel_id=1, source_target_pairs={{0,1},{1,0},{2,3},{3,2},{16,17},{17,16},{18,19},{19,18},{4,5},{5,4... | collective-permute-start | bytes 405512 | tf_op jit(solution)/shard_map/ppermute | solution.py:332
  9.3 12.4 %collective-permute-start.3 = (bf16[528,128]{1,0:T(8,128)(2,1)S(1)}, bf16[528,128]{1,0:T(8,128)(2,1)S(1)}, u32[]{:S(2)}, u32[]{:S(2)}) collective-permute-start(bf16[528,128]{1,0:T(8,128)(2,1)S(1)} %get-tuple-element.15), channel_id=1, source_target_pairs={{0,19},{1,18},{2,17},{3,16},{16,3},{17,2},{18,1},{19,0},{4,23},{5,... | collective-permute-start | bytes 405512 | tf_op jit(solution)/shard_map/ppermute | solution.py:332
  10.2 11.6 %collective-permute-start.4 = (bf16[528,128]{1,0:T(8,128)(2,1)S(1)}, bf16[528,128]{1,0:T(8,128)(2,1)S(1)}, u32[]{:S(2)}, u32[]{:S(2)}) collective-permute-start(bf16[528,128]{1,0:T(8,128)(2,1)S(1)} %get-tuple-element.16), channel_id=1, source_target_pairs={{0,17},{1,16},{2,19},{3,18},{16,1},{17,0},{18,3},{19,2},{4,21},{5,... | collective-permute-start | bytes 405512 | tf_op jit(solution)/shard_map/ppermute | solution.py:332
  16.6 12.8 %collective-permute-start.7 = (bf16[528,128]{1,0:T(8,128)(2,1)S(1)}, bf16[528,128]{1,0:T(8,128)(2,1)S(1)}, u32[]{:S(2)}, u32[]{:S(2)}) collective-permute-start(bf16[528,128]{1,0:T(8,128)(2,1)S(1)} %get-tuple-element.23), channel_id=1, source_target_pairs={{0,16},{1,17},{2,18},{3,19},{16,0},{17,1},{18,2},{19,3},{4,20},{5,... | collective-permute-start | bytes 405512 | tf_op jit(solution)/shard_map/ppermute | solution.py:332
  18.4 13.1 %collective-permute-start.5 = (bf16[528,128]{1,0:T(8,128)(2,1)S(1)}, bf16[528,128]{1,0:T(8,128)(2,1)S(1)}, u32[]{:S(2)}, u32[]{:S(2)}) collective-permute-start(bf16[528,128]{1,0:T(8,128)(2,1)S(1)} %get-tuple-element.21), channel_id=1, source_target_pairs={{0,18},{1,19},{2,16},{3,17},{16,2},{17,3},{18,0},{19,1},{4,22},{5,... | collective-permute-start | bytes 405512 | tf_op jit(solution)/shard_map/ppermute | solution.py:332
  21.6 10.9 %collective-permute-start.6 = (bf16[528,128]{1,0:T(8,128)(2,1)S(1)}, bf16[528,128]{1,0:T(8,128)(2,1)S(1)}, u32[]{:S(2)}, u32[]{:S(2)}) collective-permute-start(bf16[528,128]{1,0:T(8,128)(2,1)S(1)} %get-tuple-element.22), channel_id=1, source_target_pairs={{0,2},{1,3},{2,0},{3,1},{16,18},{17,19},{18,16},{19,17},{4,6},{5,7... | collective-permute-start | bytes 405512 | tf_op jit(solution)/shard_map/ppermute | solution.py:332
  21.9 4.2 %collective-permute-start.8 = (f32[8,128]{1,0:T(8,128)S(1)}, f32[8,128]{1,0:T(8,128)S(1)}, u32[]{:S(2)}, u32[]{:S(2)}) collective-permute-start(f32[8,128]{1,0:T(8,128)S(1)} %score.4.rest_5_.own_ref), channel_id=1, source_target_pairs={{0,16},{1,17},{2,18},{3,19},{16,0},{17,1},{18,2},{19,3},{4,20},{5,... | collective-permute-start | bytes 12296 | tf_op jit(solution)/shard_map/ppermute | solution.py:332
  26.2 11.9 %collective-permute-start.10 = (f32[8,128]{1,0:T(8,128)S(1)}, f32[8,128]{1,0:T(8,128)S(1)}, u32[]{:S(2)}, u32[]{:S(2)}) collective-permute-start(f32[8,128]{1,0:T(8,128)S(1)} %merge.1.rest_2_), channel_id=1, source_target_pairs={{0,3},{1,2},{2,1},{3,0},{16,19},{17,18},{18,17},{19,16},{4,7},{5,6... | collective-permute-start | bytes 12296 | tf_op jit(solution)/shard_map/ppermute | solution.py:332
  29.2 8.8 %collective-permute-start.9 = (f32[8,128]{1,0:T(8,128)S(1)}, f32[8,128]{1,0:T(8,128)S(1)}, u32[]{:S(2)}, u32[]{:S(2)}) collective-permute-start(f32[8,128]{1,0:T(8,128)S(1)} %merge.1.rest_2_), channel_id=1, source_target_pairs={{0,1},{1,0},{2,3},{3,2},{16,17},{17,16},{18,19},{19,18},{4,5},{5,4... | collective-permute-start | bytes 12296 | tf_op jit(solution)/shard_map/ppermute | solution.py:332
  29.4 5.6 %copy-start.2 = (bf16[1,1,768,1024]{3,2,1,0:T(8,128)(2,1)S(1)}, bf16[1,1,768,1024]{3,2,1,0:T(8,128)(2,1)}, u32[]{:S(2)}) copy-start(bf16[1,1,768,1024]{3,2,1,0:T(8,128)(2,1)} %param.12) | copy-start | bytes 4718596
  29.4 5.6 %copy-start.3 = (bf16[1,1,768,1024]{3,2,1,0:T(8,128)(2,1)S(1)}, bf16[1,1,768,1024]{3,2,1,0:T(8,128)(2,1)}, u32[]{:S(2)}) copy-start(bf16[1,1,768,1024]{3,2,1,0:T(8,128)(2,1)} %param.13) | copy-start | bytes 4718596
  29.6 5.4 %copy-start = (f32[1,1,768,1024]{3,2,1,0:T(8,128)S(1)}, f32[1,1,768,1024]{3,2,1,0:T(8,128)}, u32[]{:S(2)}) copy-start(f32[1,1,768,1024]{3,2,1,0:T(8,128)} %param.11) | copy-start | bytes 9437188
  29.6 8.5 %collective-permute-start.11 = (f32[8,128]{1,0:T(8,128)S(1)}, f32[8,128]{1,0:T(8,128)S(1)}, u32[]{:S(2)}, u32[]{:S(2)}) collective-permute-start(f32[8,128]{1,0:T(8,128)S(1)} %score.5.rest_1_.rest_2_), channel_id=1, source_target_pairs={{0,16},{1,17},{2,18},{3,19},{16,0},{17,1},{18,2},{19,3},{4,20},{5,... | collective-permute-start | bytes 12296 | tf_op jit(solution)/shard_map/ppermute | solution.py:332
  31.6 6.4 %collective-permute-start.13 = (f32[8,128]{1,0:T(8,128)S(1)}, f32[8,128]{1,0:T(8,128)S(1)}, u32[]{:S(2)}, u32[]{:S(2)}) collective-permute-start(f32[8,128]{1,0:T(8,128)S(1)} %score.6.rest_1_), channel_id=1, source_target_pairs={{0,18},{1,19},{2,16},{3,17},{16,2},{17,3},{18,0},{19,1},{4,22},{5,... | collective-permute-start | bytes 12296 | tf_op jit(solution)/shard_map/ppermute | solution.py:332
  32.6 5.4 %collective-permute-start.12 = (f32[8,128]{1,0:T(8,128)S(1)}, f32[8,128]{1,0:T(8,128)S(1)}, u32[]{:S(2)}, u32[]{:S(2)}) collective-permute-start(f32[8,128]{1,0:T(8,128)S(1)} %score.7.rest_3_), channel_id=1, source_target_pairs={{0,2},{1,3},{2,0},{3,1},{16,18},{17,19},{18,16},{19,17},{4,6},{5,7... | collective-permute-start | bytes 12296 | tf_op jit(solution)/shard_map/ppermute | solution.py:332
  35.0 3.1 %copy-start.4 = (s32[1,512,8]{1,2,0:T(8,128)S(1)}, s32[1,512,8]{1,2,0:T(8,128)}, u32[]{:S(2)}) copy-start(s32[1,512,8]{1,2,0:T(8,128)} %param.9) | copy-start | bytes 49156

commit v20 on v18

--- a/solution.py
+++ b/solution.py
@@ -66,22 +66,17 @@
 def fill_chunks(steps, cap, picks, held, copies, tiles, chunks):
     half = held.shape[2]
     data_rows = half // LANES * cap
-    step = min(half, 2 * LANES)
     pick = jnp.concatenate([picks[k] for k in steps], axis=0)
     for side in range(2):
         for k in steps:
             chunks[side, k][data_rows:, :] = tiles[k]
         copies[side].wait()
-        for column in range(0, half, step):
-            block = jnp.dot(
-                pick, held[side, :, column : column + step], preferred_element_type=F32
-            ).astype(BF16)
-            for at, k in enumerate(steps):
-                for part in range(step // LANES):
-                    top = (column // LANES + part) * cap
-                    chunks[side, k][top : top + cap, :] = block[
-                        at * cap : (at + 1) * cap, part * LANES : (part + 1) * LANES
-                    ]
+        block = jnp.dot(pick, held[side], preferred_element_type=F32).astype(BF16)
+        for at, k in enumerate(steps):
+            for part in range(half // LANES):
+                chunks[side, k][part * cap : (part + 1) * cap, :] = block[
+                    at * cap : (at + 1) * cap, part * LANES : (part + 1) * LANES
+                ]
 
 
 def route_kernel(
@@ -234,7 +229,7 @@
     _, update_hbm, rows, scaled, total, update, sems = rest[len(items) :]
     hid, half = update.shape
     width = min(half, 4 * LANES)
-    height = LANES
+    height = 2 * TILE
     data_rows = half // LANES * cap
     me = ep_index()
     for at in range(0, len(items), 2):
@@ -477,7 +472,7 @@
             pltpu.VMEM((hid, depth), BF16),
             pltpu.VMEM((hid, half), F32),
             pltpu.VMEM((hid, half), F32),
-            pltpu.SemaphoreType.DMA((hid // LANES,)),
+            pltpu.SemaphoreType.DMA((hid // (2 * TILE),)),
         ],
         compiler_params=params(),
         cost_estimate=cost(2 * depth * hid * half, 16 * hid * half),

time: 39 us -> 39 us (level)
  no operation moved by 1% of the time
where the time goes in v20:
time: 39 us; the launch traced here: 38.8 us
  starting transfers between devices  23.3 us (60%)
  Pallas kernels  11 us (28%)
  waiting for transfers between devices  3.81 us (10%)
  between operations  0.75 us (2%)
    ppermute x14, starting transfers between devices, moved(): return lax.ppermute(array, ('pair', 'ep'), pairs)  23.3 us
    ppermute x14, waiting for transfers between devices, moved(): return lax.ppermute(array, ('pair', 'ep'), pairs)  3.81 us
    pallas_call x1, Pallas kernels, local(): pl.pallas_call(functools.partial(later_kernel, last_items, late, cap), ou...  3.33 us
    pallas_call x1, Pallas kernels, local(): pl.pallas_call(functools.partial(update_kernel, added, cap), out_shape=ja...  3.07 us
    pallas_call x1, Pallas kernels, local(): pl.pallas_call(functools.partial(route_kernel, first_items, first, group,...  1.99 us
    pallas_call x1, Pallas kernels, local(): pl.pallas_call(functools.partial(sum_kernel, summed, group, cap), out_sha...  1.12 us
    pallas_call x1, Pallas kernels, local(): pl.pallas_call(functools.partial(combine_kernel, [(k, len(arrays)) for k,...  0.87 us
  transfers between devices with their start and end apart: 14, of which 4 were waited for; matrix products, arithmetic and copies ran while one was open for 0% of the time, Pallas kernels for 26%

profile of v20, /device:TPU:0, one launch (start us, length us, event | category | flops | bytes accessed | tf_op | source)
XLA Modules:
  0.0 38.8 jit_solution(9382760501370288029)
XLA Ops:
  0.6 3.0 %collective-permute-start = (bf16[768,256]{1,0:T(8,128)(2,1)}, bf16[768,256]{1,0:T(8,128)(2,1)S(1)}, u32[]{:S(2)}, u32[]{:S(2)}) collective-permute-start(bf16[768,256]{1,0:T(8,128)(2,1)} %bitcast.17), channel_id=1, source_target_pairs={{0,16},{1,17},{2,18},{3,19},{16,0},{17,1},{18,2},{19,3},{4,20},{5,... | collective-permute-start | bytes 1179656 | tf_op jit(solution)/shard_map/ppermute | solution.py:340
  3.7 2.0 %route.1 = (f32[16,512]{1,0:T(8,128)S(1)}, bf16[4,16,128]{2,1,0:T(8,128)(2,1)S(1)}, bf16[528,128]{1,0:T(8,128)(2,1)S(1)}, bf16[528,128]{1,0:T(8,128)(2,1)S(1)}, ...) custom-call(s32[8,512]{1,0:T(8,128)} %bitcast.23, bf16[8,512]{1,0:T(8,128)(2,1)} %bitcast.29, ...), custom_call_target="tpu_custom_call" | custom-call | flops 536870912 | bytes 3145728 | tf_op jit(solution)/shard_map/route/pallas_call | solution.py:364
  5.7 3.7 %collective-permute-start.1 = (bf16[528,128]{1,0:T(8,128)(2,1)S(1)}, bf16[528,128]{1,0:T(8,128)(2,1)S(1)}, u32[]{:S(2)}, u32[]{:S(2)}) collective-permute-start(bf16[528,128]{1,0:T(8,128)(2,1)S(1)} %get-tuple-element.13), channel_id=1, source_target_pairs={{0,3},{1,2},{2,1},{3,0},{16,19},{17,18},{18,17},{19,16},{4,7},{5,6... | collective-permute-start | bytes 405512 | tf_op jit(solution)/shard_map/ppermute | solution.py:340
  9.3 0.8 %collective-permute-start.3 = (bf16[528,128]{1,0:T(8,128)(2,1)S(1)}, bf16[528,128]{1,0:T(8,128)(2,1)S(1)}, u32[]{:S(2)}, u32[]{:S(2)}) collective-permute-start(bf16[528,128]{1,0:T(8,128)(2,1)S(1)} %get-tuple-element.15), channel_id=1, source_target_pairs={{0,19},{1,18},{2,17},{3,16},{16,3},{17,2},{18,1},{19,0},{4,23},{5,... | collective-permute-start | bytes 405512 | tf_op jit(solution)/shard_map/ppermute | solution.py:340
  10.2 1.4 %collective-permute-start.4 = (bf16[528,128]{1,0:T(8,128)(2,1)S(1)}, bf16[528,128]{1,0:T(8,128)(2,1)S(1)}, u32[]{:S(2)}, u32[]{:S(2)}) collective-permute-start(bf16[528,128]{1,0:T(8,128)(2,1)S(1)} %get-tuple-element.16), channel_id=1, source_target_pairs={{0,17},{1,16},{2,19},{3,18},{16,1},{17,0},{18,3},{19,2},{4,21},{5,... | collective-permute-start | bytes 405512 | tf_op jit(solution)/shard_map/ppermute | solution.py:340
  11.6 1.4 %collective-permute-done.other_ref = bf16[768,256]{1,0:T(8,128)(2,1)S(1)} collective-permute-done((bf16[768,256]{1,0:T(8,128)(2,1)}, bf16[768,256]{1,0:T(8,128)(2,1)S(1)}, u32[]{:S(2)}, u32[]{:S(2)}) %collective-permute-start) | collective-permute-done | bytes 393248 | tf_op jit(solution)/shard_map/ppermute | solution.py:340
  13.0 3.3 %later.1 = (f32[512,1024]{1,0:T(8,128)S(1)}, bf16[528,128]{1,0:T(8,128)(2,1)S(1)}, bf16[528,128]{1,0:T(8,128)(2,1)S(1)}, bf16[528,128]{1,0:T(8,128)(2,1)S(1)}, bf16[528,128]{1,0:T(8,128)(2,1)S(1)}) custom-call(f32[16,512]{1,0:T(8,128)S(1)} %get-tuple-element.17.slots_ref, bf16[4,16,128]{2,1,0:T(8,128)(2,1)S(1)} %get-tuple-element.18.tiles_ref, ...), custom_call_target="tpu_custom_call" | custom-call | flops 1342177280 | bytes 3145728 | tf_op jit(solution)/shard_map/later/pallas_call | solution.py:390
  16.3 1.8 %collective-permute-start.7 = (bf16[528,128]{1,0:T(8,128)(2,1)S(1)}, bf16[528,128]{1,0:T(8,128)(2,1)S(1)}, u32[]{:S(2)}, u32[]{:S(2)}) collective-permute-start(bf16[528,128]{1,0:T(8,128)(2,1)S(1)} %get-tuple-element.23), channel_id=1, source_target_pairs={{0,16},{1,17},{2,18},{3,19},{16,0},{17,1},{18,2},{19,3},{4,20},{5,... | collective-permute-start | bytes 405512 | tf_op jit(solution)/shard_map/ppermute | solution.py:340
  18.1 3.2 %collective-permute-start.5 = (bf16[528,128]{1,0:T(8,128)(2,1)S(1)}, bf16[528,128]{1,0:T(8,128)(2,1)S(1)}, u32[]{:S(2)}, u32[]{:S(2)}) collective-permute-start(bf16[528,128]{1,0:T(8,128)(2,1)S(1)} %get-tuple-element.21), channel_id=1, source_target_pairs={{0,18},{1,19},{2,16},{3,17},{16,2},{17,3},{18,0},{19,1},{4,22},{5,... | collective-permute-start | bytes 405512 | tf_op jit(solution)/shard_map/ppermute | solution.py:340
  21.3 0.1 collective-permute-start.6
  21.5 1.0 %collective-permute-done.4.rest_3_ = bf16[528,128]{1,0:T(8,128)(2,1)S(1)} collective-permute-done((bf16[528,128]{1,0:T(8,128)(2,1)S(1)}, bf16[528,128]{1,0:T(8,128)(2,1)S(1)}, u32[]{:S(2)}, u32[]{:S(2)}) %collective-permute-start.4) | collective-permute-done | bytes 135200 | tf_op jit(solution)/shard_map/ppermute | solution.py:340
  22.5 0.2 score.4.rest_5_.own_ref
  22.7 1.6 %collective-permute-start.8 = (f32[8,128]{1,0:T(8,128)S(1)}, f32[8,128]{1,0:T(8,128)S(1)}, u32[]{:S(2)}, u32[]{:S(2)}) collective-permute-start(f32[8,128]{1,0:T(8,128)S(1)} %score.4.rest_5_.own_ref), channel_id=1, source_target_pairs={{0,16},{1,17},{2,18},{3,19},{16,0},{17,1},{18,2},{19,3},{4,20},{5,... | collective-permute-start | bytes 12296 | tf_op jit(solution)/shard_map/ppermute | solution.py:340
  24.3 1.1 %sum.1._.grad_ref = f32[768,1024]{1,0:T(8,128)S(1)} custom-call(bf16[768,256]{1,0:T(8,128)(2,1)S(1)} %bitcast.19, bf16[768,256]{1,0:T(8,128)(2,1)S(1)} %collective-permute-done.other_ref, bf16[528,128]{1,0:T(8,128)(2,1)S(1)} %collective-permute-done.1.rest_0_, bf16[528,128]{1,0:T(8,128)(2,1)S(1)} %collective-permute-done.2.rest_1_, ...), custom_call_target="tpu_custom_call" | custom-call | flops 805306368 | bytes 3145728 | tf_op jit(solution)/shard_map/sum/pallas_call | solution.py:436
  25.5 0.9 %collective-permute-done.8.other_ref = f32[8,128]{1,0:T(8,128)S(1)} collective-permute-done((f32[8,128]{1,0:T(8,128)S(1)}, f32[8,128]{1,0:T(8,128)S(1)}, u32[]{:S(2)}, u32[]{:S(2)}) %collective-permute-start.8) | collective-permute-done | bytes 4128 | tf_op jit(solution)/shard_map/ppermute | solution.py:340
  26.4 2.5 %collective-permute-start.10 = (f32[8,128]{1,0:T(8,128)S(1)}, f32[8,128]{1,0:T(8,128)S(1)}, u32[]{:S(2)}, u32[]{:S(2)}) collective-permute-start(f32[8,128]{1,0:T(8,128)S(1)} %merge.1.rest_2_), channel_id=1, source_target_pairs={{0,3},{1,2},{2,1},{3,0},{16,19},{17,18},{18,17},{19,16},{4,7},{5,6... | collective-permute-start | bytes 12296 | tf_op jit(solution)/shard_map/ppermute | solution.py:340
  28.9 0.2 collective-permute-start.9
  29.2 0.1 score.5.rest_1_.rest_2_
  29.3 1.5 %collective-permute-start.11 = (f32[8,128]{1,0:T(8,128)S(1)}, f32[8,128]{1,0:T(8,128)S(1)}, u32[]{:S(2)}, u32[]{:S(2)}) collective-permute-start(f32[8,128]{1,0:T(8,128)S(1)} %score.5.rest_1_.rest_2_), channel_id=1, source_target_pairs={{0,16},{1,17},{2,18},{3,19},{16,0},{17,1},{18,2},{19,3},{4,20},{5,... | collective-permute-start | bytes 12296 | tf_op jit(solution)/shard_map/ppermute | solution.py:340
  30.8 0.4 %collective-permute-done.5.rest_0_ = bf16[528,128]{1,0:T(8,128)(2,1)S(1)} collective-permute-done((bf16[528,128]{1,0:T(8,128)(2,1)S(1)}, bf16[528,128]{1,0:T(8,128)(2,1)S(1)}, u32[]{:S(2)}, u32[]{:S(2)}) %collective-permute-start.5) | collective-permute-done | bytes 135200 | tf_op jit(solution)/shard_map/ppermute | solution.py:340
  31.3 1.4 %collective-permute-start.13 = (f32[8,128]{1,0:T(8,128)S(1)}, f32[8,128]{1,0:T(8,128)S(1)}, u32[]{:S(2)}, u32[]{:S(2)}) collective-permute-start(f32[8,128]{1,0:T(8,128)S(1)} %score.6.rest_1_), channel_id=1, source_target_pairs={{0,18},{1,19},{2,16},{3,17},{16,2},{17,3},{18,0},{19,1},{4,22},{5,... | collective-permute-start | bytes 12296 | tf_op jit(solution)/shard_map/ppermute | solution.py:340
  32.8 2.0 %collective-permute-start.12 = (f32[8,128]{1,0:T(8,128)S(1)}, f32[8,128]{1,0:T(8,128)S(1)}, u32[]{:S(2)}, u32[]{:S(2)}) collective-permute-start(f32[8,128]{1,0:T(8,128)S(1)} %score.7.rest_3_), channel_id=1, source_target_pairs={{0,2},{1,3},{2,0},{3,1},{16,18},{17,19},{18,16},{19,17},{4,6},{5,7... | collective-permute-start | bytes 12296 | tf_op jit(solution)/shard_map/ppermute | solution.py:340
  34.8 3.1 %update.1 = f32[768,1024]{1,0:T(8,128)} custom-call(bf16[768,256]{1,0:T(8,128)(2,1)S(1)} %bitcast.20, bf16[768,256]{1,0:T(8,128)(2,1)S(1)} %collective-permute-done.other_ref, f32[768,1024]{1,0:T(8,128)S(1)} %sum.1._.grad_ref, f32[768,1024]{1,0:T(8,128)S(1)} %bitcast.16, bf16[768,1024]{1,0:T(8,128)(2,1)S(1)} %bitcast.21, bf16[768,1024]{1,0:T(8,128)(2,1)S(1)} %bitcast.22, ...), custom_call_target="tpu_custom_call" | custom-call | flops 402653184 | bytes 12582912 | tf_op jit(solution)/shard_map/update/pallas_call | solution.py:465
  38.0 0.9 %combine.1 = f32[8,512]{1,0:T(8,128)} custom-call(s32[8,512]{1,0:T(8,128)S(1)} %bitcast.24, f32[16,512]{1,0:T(8,128)S(1)} %get-tuple-element.17.slots_ref, f32[8,128]{1,0:T(8,128)S(1)} %collective-permute-done.9.rest_0_, f32[8,128]{1,0:T(8,128)S(1)} %collective-permute-done.10.rest_1_, f32[8,128]{1,0:T(8,128)S(1)} %score.5.rest_1_.rest_2_, ...), custom_call_target="tpu_custom_call" | custom-call | flops 524288 | bytes 32768 | tf_op jit(solution)/shard_map/combine/pallas_call | solution.py:491
  (24 shorter events, 0.4 us)
Async XLA Ops:
  0.6 12.4 %copy-start.1 = (bf16[1,1,768,256]{3,2,1,0:T(8,128)(2,1)S(1)}, bf16[1,1,768,256]{3,2,1,0:T(8,128)(2,1)}, u32[]{:S(2)}) copy-start(bf16[1,1,768,256]{3,2,1,0:T(8,128)(2,1)} %param.10) | copy-start | bytes 1179652
  0.6 12.4 %collective-permute-start = (bf16[768,256]{1,0:T(8,128)(2,1)}, bf16[768,256]{1,0:T(8,128)(2,1)S(1)}, u32[]{:S(2)}, u32[]{:S(2)}) collective-permute-start(bf16[768,256]{1,0:T(8,128)(2,1)} %bitcast.17), channel_id=1, source_target_pairs={{0,16},{1,17},{2,18},{3,19},{16,0},{17,1},{18,2},{19,3},{4,20},{5,... | collective-permute-start | bytes 1179656 | tf_op jit(solution)/shard_map/ppermute | solution.py:340
  5.7 12.5 %collective-permute-start.1 = (bf16[528,128]{1,0:T(8,128)(2,1)S(1)}, bf16[528,128]{1,0:T(8,128)(2,1)S(1)}, u32[]{:S(2)}, u32[]{:S(2)}) collective-permute-start(bf16[528,128]{1,0:T(8,128)(2,1)S(1)} %get-tuple-element.13), channel_id=1, source_target_pairs={{0,3},{1,2},{2,1},{3,0},{16,19},{17,18},{18,17},{19,16},{4,7},{5,6... | collective-permute-start | bytes 405512 | tf_op jit(solution)/shard_map/ppermute | solution.py:340
  9.3 12.0 %collective-permute-start.2 = (bf16[528,128]{1,0:T(8,128)(2,1)S(1)}, bf16[528,128]{1,0:T(8,128)(2,1)S(1)}, u32[]{:S(2)}, u32[]{:S(2)}) collective-permute-start(bf16[528,128]{1,0:T(8,128)(2,1)S(1)} %get-tuple-element.14), channel_id=1, source_target_pairs={{0,1},{1,0},{2,3},{3,2},{16,17},{17,16},{18,19},{19,18},{4,5},{5,4... | collective-permute-start | bytes 405512 | tf_op jit(solution)/shard_map/ppermute | solution.py:340
  9.3 12.1 %collective-permute-start.3 = (bf16[528,128]{1,0:T(8,128)(2,1)S(1)}, bf16[528,128]{1,0:T(8,128)(2,1)S(1)}, u32[]{:S(2)}, u32[]{:S(2)}) collective-permute-start(bf16[528,128]{1,0:T(8,128)(2,1)S(1)} %get-tuple-element.15), channel_id=1, source_target_pairs={{0,19},{1,18},{2,17},{3,16},{16,3},{17,2},{18,1},{19,0},{4,23},{5,... | collective-permute-start | bytes 405512 | tf_op jit(solution)/shard_map/ppermute | solution.py:340
  10.2 12.3 %collective-permute-start.4 = (bf16[528,128]{1,0:T(8,128)(2,1)S(1)}, bf16[528,128]{1,0:T(8,128)(2,1)S(1)}, u32[]{:S(2)}, u32[]{:S(2)}) collective-permute-start(bf16[528,128]{1,0:T(8,128)(2,1)S(1)} %get-tuple-element.16), channel_id=1, source_target_pairs={{0,17},{1,16},{2,19},{3,18},{16,1},{17,0},{18,3},{19,2},{4,21},{5,... | collective-permute-start | bytes 405512 | tf_op jit(solution)/shard_map/ppermute | solution.py:340
  16.3 12.8 %collective-permute-start.7 = (bf16[528,128]{1,0:T(8,128)(2,1)S(1)}, bf16[528,128]{1,0:T(8,128)(2,1)S(1)}, u32[]{:S(2)}, u32[]{:S(2)}) collective-permute-start(bf16[528,128]{1,0:T(8,128)(2,1)S(1)} %get-tuple-element.23), channel_id=1, source_target_pairs={{0,16},{1,17},{2,18},{3,19},{16,0},{17,1},{18,2},{19,3},{4,20},{5,... | collective-permute-start | bytes 405512 | tf_op jit(solution)/shard_map/ppermute | solution.py:340
  18.1 13.1 %collective-permute-start.5 = (bf16[528,128]{1,0:T(8,128)(2,1)S(1)}, bf16[528,128]{1,0:T(8,128)(2,1)S(1)}, u32[]{:S(2)}, u32[]{:S(2)}) collective-permute-start(bf16[528,128]{1,0:T(8,128)(2,1)S(1)} %get-tuple-element.21), channel_id=1, source_target_pairs={{0,18},{1,19},{2,16},{3,17},{16,2},{17,3},{18,0},{19,1},{4,22},{5,... | collective-permute-start | bytes 405512 | tf_op jit(solution)/shard_map/ppermute | solution.py:340
  21.3 11.4 %collective-permute-start.6 = (bf16[528,128]{1,0:T(8,128)(2,1)S(1)}, bf16[528,128]{1,0:T(8,128)(2,1)S(1)}, u32[]{:S(2)}, u32[]{:S(2)}) collective-permute-start(bf16[528,128]{1,0:T(8,128)(2,1)S(1)} %get-tuple-element.22), channel_id=1, source_target_pairs={{0,2},{1,3},{2,0},{3,1},{16,18},{17,19},{18,16},{19,17},{4,6},{5,7... | collective-permute-start | bytes 405512 | tf_op jit(solution)/shard_map/ppermute | solution.py:340
  22.7 3.7 %collective-permute-start.8 = (f32[8,128]{1,0:T(8,128)S(1)}, f32[8,128]{1,0:T(8,128)S(1)}, u32[]{:S(2)}, u32[]{:S(2)}) collective-permute-start(f32[8,128]{1,0:T(8,128)S(1)} %score.4.rest_5_.own_ref), channel_id=1, source_target_pairs={{0,16},{1,17},{2,18},{3,19},{16,0},{17,1},{18,2},{19,3},{4,20},{5,... | collective-permute-start | bytes 12296 | tf_op jit(solution)/shard_map/ppermute | solution.py:340
  26.4 11.5 %collective-permute-start.10 = (f32[8,128]{1,0:T(8,128)S(1)}, f32[8,128]{1,0:T(8,128)S(1)}, u32[]{:S(2)}, u32[]{:S(2)}) collective-permute-start(f32[8,128]{1,0:T(8,128)S(1)} %merge.1.rest_2_), channel_id=1, source_target_pairs={{0,3},{1,2},{2,1},{3,0},{16,19},{17,18},{18,17},{19,16},{4,7},{5,6... | collective-permute-start | bytes 12296 | tf_op jit(solution)/shard_map/ppermute | solution.py:340
  28.9 9.0 %collective-permute-start.9 = (f32[8,128]{1,0:T(8,128)S(1)}, f32[8,128]{1,0:T(8,128)S(1)}, u32[]{:S(2)}, u32[]{:S(2)}) collective-permute-start(f32[8,128]{1,0:T(8,128)S(1)} %merge.1.rest_2_), channel_id=1, source_target_pairs={{0,1},{1,0},{2,3},{3,2},{16,17},{17,16},{18,19},{19,18},{4,5},{5,4... | collective-permute-start | bytes 12296 | tf_op jit(solution)/shard_map/ppermute | solution.py:340
  29.2 5.7 %copy-start.2 = (bf16[1,1,768,1024]{3,2,1,0:T(8,128)(2,1)S(1)}, bf16[1,1,768,1024]{3,2,1,0:T(8,128)(2,1)}, u32[]{:S(2)}) copy-start(bf16[1,1,768,1024]{3,2,1,0:T(8,128)(2,1)} %param.12) | copy-start | bytes 4718596
  29.2 5.7 %copy-start.3 = (bf16[1,1,768,1024]{3,2,1,0:T(8,128)(2,1)S(1)}, bf16[1,1,768,1024]{3,2,1,0:T(8,128)(2,1)}, u32[]{:S(2)}) copy-start(bf16[1,1,768,1024]{3,2,1,0:T(8,128)(2,1)} %param.13) | copy-start | bytes 4718596
  29.3 5.5 %copy-start = (f32[1,1,768,1024]{3,2,1,0:T(8,128)S(1)}, f32[1,1,768,1024]{3,2,1,0:T(8,128)}, u32[]{:S(2)}) copy-start(f32[1,1,768,1024]{3,2,1,0:T(8,128)} %param.11) | copy-start | bytes 9437188
  29.3 8.6 %collective-permute-start.11 = (f32[8,128]{1,0:T(8,128)S(1)}, f32[8,128]{1,0:T(8,128)S(1)}, u32[]{:S(2)}, u32[]{:S(2)}) collective-permute-start(f32[8,128]{1,0:T(8,128)S(1)} %score.5.rest_1_.rest_2_), channel_id=1, source_target_pairs={{0,16},{1,17},{2,18},{3,19},{16,0},{17,1},{18,2},{19,3},{4,20},{5,... | collective-permute-start | bytes 12296 | tf_op jit(solution)/shard_map/ppermute | solution.py:340
  31.3 6.6 %collective-permute-start.13 = (f32[8,128]{1,0:T(8,128)S(1)}, f32[8,128]{1,0:T(8,128)S(1)}, u32[]{:S(2)}, u32[]{:S(2)}) collective-permute-start(f32[8,128]{1,0:T(8,128)S(1)} %score.6.rest_1_), channel_id=1, source_target_pairs={{0,18},{1,19},{2,16},{3,17},{16,2},{17,3},{18,0},{19,1},{4,22},{5,... | collective-permute-start | bytes 12296 | tf_op jit(solution)/shard_map/ppermute | solution.py:340
  32.8 5.1 %collective-permute-start.12 = (f32[8,128]{1,0:T(8,128)S(1)}, f32[8,128]{1,0:T(8,128)S(1)}, u32[]{:S(2)}, u32[]{:S(2)}) collective-permute-start(f32[8,128]{1,0:T(8,128)S(1)} %score.7.rest_3_), channel_id=1, source_target_pairs={{0,2},{1,3},{2,0},{3,1},{16,18},{17,19},{18,16},{19,17},{4,6},{5,7... | collective-permute-start | bytes 12296 | tf_op jit(solution)/shard_map/ppermute | solution.py:340
  34.8 3.1 %copy-start.4 = (s32[1,512,8]{1,2,0:T(8,128)S(1)}, s32[1,512,8]{1,2,0:T(8,128)}, u32[]{:S(2)}) copy-start(s32[1,512,8]{1,2,0:T(8,128)} %param.9) | copy-start | bytes 49156

commit v21 on v20

--- a/solution.py
+++ b/solution.py
@@ -229,7 +229,7 @@
     _, update_hbm, rows, scaled, total, update, sems = rest[len(items) :]
     hid, half = update.shape
     width = min(half, 4 * LANES)
-    height = 2 * TILE
+    height = hid // sems.shape[0]
     data_rows = half // LANES * cap
     me = ep_index()
     for at in range(0, len(items), 2):
@@ -259,8 +259,7 @@
             )
     total[...] = jnp.dot(scaled[...], rows[...], preferred_element_type=F32)
 
-    def moments(top, columns):
-        lines = slice(top, top + TILE)
+    def moments(lines, columns):
         grad = total[lines, columns] + grad_ref[lines, columns]
         first = moment_ref[lines, columns].astype(F32) * (beta_first / (1.0 - beta_first)) + grad
         square = (
@@ -273,35 +272,36 @@
         scale = square * root * (second_unit**0.5 / first_unit) + adam_eps / first_unit
         return first, pl.reciprocal(scale, approx=True)
 
-    def finish(top, columns, first, scale):
-        lines = slice(top, top + TILE)
+    def finish(lines, columns, first, scale):
         update[lines, columns] = first * scale + decay_rate * master_ref[lines, columns]
 
-    copies = []
-    pieces = [
-        (top, slice(column, column + width))
-        for top in range(0, hid, TILE)
-        for column in range(0, half, width)
-    ]
-    held = {}
-    for turn in range(len(pieces) + 2):
-        if turn < len(pieces):
-            held[turn, 0] = moments(*pieces[turn])
-        if 0 <= turn - 1 < len(pieces):
-            held[turn - 1, 1] = inverse(*held.pop((turn - 1, 0)))
-        if turn >= 2:
-            finish(*pieces[turn - 2], *held.pop((turn - 2, 1)))
-            top, columns = pieces[turn - 2]
-            if (top + TILE) % height == 0 and columns.stop == half:
-                lines = slice(top + TILE - height, top + TILE)
-                copies.append(
-                    pltpu.make_async_copy(
-                        update.at[lines, :], update_hbm.at[lines, :], sems.at[len(copies)]
-                    )
-                )
-                copies[-1].start()
-    for copy in copies:
-        copy.wait()
+    def copy_out(turn):
+        lines = pl.ds(pl.multiple_of(turn * height, height), height)
+        return pltpu.make_async_copy(update.at[lines, :], update_hbm.at[lines, :], sems.at[turn])
+
+    def adam(turn, carry):
+        pieces = [
+            (pl.ds(pl.multiple_of(turn * height + top, TILE), TILE), slice(column, column + width))
+            for top in range(0, height, TILE)
+            for column in range(0, half, width)
+        ]
+        held = {}
+        for at in range(len(pieces) + 2):
+            if at < len(pieces):
+                held[at, 0] = moments(*pieces[at])
+            if 0 <= at - 1 < len(pieces):
+                held[at - 1, 1] = inverse(*held.pop((at - 1, 0)))
+            if at >= 2:
+                finish(*pieces[at - 2], *held.pop((at - 2, 1)))
+        copy_out(turn).start()
+        return carry
+
+    def settle(turn, carry):
+        copy_out(turn).wait()
+        return carry
+
+    lax.fori_loop(0, hid // height, adam, 0)
+    lax.fori_loop(0, hid // height, settle, 0)
 
 
 def combine_kernel(steps, group, cap, ids_ref, slots_ref, *rest):
@@ -472,7 +472,7 @@
             pltpu.VMEM((hid, depth), BF16),
             pltpu.VMEM((hid, half), F32),
             pltpu.VMEM((hid, half), F32),
-            pltpu.SemaphoreType.DMA((hid // (2 * TILE),)),
+            pltpu.SemaphoreType.DMA((hid // (6 * TILE),)),
         ],
         compiler_params=params(),
         cost_estimate=cost(2 * depth * hid * half, 16 * hid * half),

time: 39 us -> 39.3 us (level)
  transfers between devices with their start and end apart: 14 -> 14, of which waited for: 4 -> 4; matrix products, arithmetic and copies ran while one was open for 0% -> 0% of each run, Pallas kernels for 26% -> 27%
where the time goes in v21:
time: 39.3 us; the launch traced here: 39.2 us
  starting transfers between devices  23.3 us (59%)
  Pallas kernels  11.3 us (29%)
  waiting for transfers between devices  3.81 us (10%)
  between operations  0.75 us (2%)
    ppermute x14, starting transfers between devices, moved(): return lax.ppermute(array, ('pair', 'ep'), pairs)  23.3 us
    ppermute x14, waiting for transfers between devices, moved(): return lax.ppermute(array, ('pair', 'ep'), pairs)  3.81 us
    pallas_call x1, Pallas kernels, local(): pl.pallas_call(functools.partial(update_kernel, added, cap), out_shape=ja...  3.39 us
    pallas_call x1, Pallas kernels, local(): pl.pallas_call(functools.partial(later_kernel, last_items, late, cap), ou...  3.33 us
    pallas_call x1, Pallas kernels, local(): pl.pallas_call(functools.partial(route_kernel, first_items, first, group,...  1.99 us
    pallas_call x1, Pallas kernels, local(): pl.pallas_call(functools.partial(sum_kernel, summed, group, cap), out_sha...  1.12 us
    pallas_call x1, Pallas kernels, local(): pl.pallas_call(functools.partial(combine_kernel, [(k, len(arrays)) for k,...  0.87 us
  transfers between devices with their start and end apart: 14, of which 4 were waited for; matrix products, arithmetic and copies ran while one was open for 0% of the time, Pallas kernels for 27%

profile of v21, /device:TPU:0, one launch (start us, length us, event | category | flops | bytes accessed | tf_op | source)
XLA Modules:
  0.0 39.2 jit_solution(12135350507477255034)
XLA Ops:
  0.6 3.0 %collective-permute-start = (bf16[768,256]{1,0:T(8,128)(2,1)}, bf16[768,256]{1,0:T(8,128)(2,1)S(1)}, u32[]{:S(2)}, u32[]{:S(2)}) collective-permute-start(bf16[768,256]{1,0:T(8,128)(2,1)} %bitcast.17), channel_id=1, source_target_pairs={{0,16},{1,17},{2,18},{3,19},{16,0},{17,1},{18,2},{19,3},{4,20},{5,... | collective-permute-start | bytes 1179656 | tf_op jit(solution)/shard_map/ppermute | solution.py:340
  3.7 2.0 %route.1 = (f32[16,512]{1,0:T(8,128)S(1)}, bf16[4,16,128]{2,1,0:T(8,128)(2,1)S(1)}, bf16[528,128]{1,0:T(8,128)(2,1)S(1)}, bf16[528,128]{1,0:T(8,128)(2,1)S(1)}, ...) custom-call(s32[8,512]{1,0:T(8,128)} %bitcast.23, bf16[8,512]{1,0:T(8,128)(2,1)} %bitcast.29, ...), custom_call_target="tpu_custom_call" | custom-call | flops 536870912 | bytes 3145728 | tf_op jit(solution)/shard_map/route/pallas_call | solution.py:364
  5.7 3.7 %collective-permute-start.1 = (bf16[528,128]{1,0:T(8,128)(2,1)S(1)}, bf16[528,128]{1,0:T(8,128)(2,1)S(1)}, u32[]{:S(2)}, u32[]{:S(2)}) collective-permute-start(bf16[528,128]{1,0:T(8,128)(2,1)S(1)} %get-tuple-element.13), channel_id=1, source_target_pairs={{0,3},{1,2},{2,1},{3,0},{16,19},{17,18},{18,17},{19,16},{4,7},{5,6... | collective-permute-start | bytes 405512 | tf_op jit(solution)/shard_map/ppermute | solution.py:340
  9.3 0.8 %collective-permute-start.3 = (bf16[528,128]{1,0:T(8,128)(2,1)S(1)}, bf16[528,128]{1,0:T(8,128)(2,1)S(1)}, u32[]{:S(2)}, u32[]{:S(2)}) collective-permute-start(bf16[528,128]{1,0:T(8,128)(2,1)S(1)} %get-tuple-element.15), channel_id=1, source_target_pairs={{0,19},{1,18},{2,17},{3,16},{16,3},{17,2},{18,1},{19,0},{4,23},{5,... | collective-permute-start | bytes 405512 | tf_op jit(solution)/shard_map/ppermute | solution.py:340
  10.2 1.4 %collective-permute-start.4 = (bf16[528,128]{1,0:T(8,128)(2,1)S(1)}, bf16[528,128]{1,0:T(8,128)(2,1)S(1)}, u32[]{:S(2)}, u32[]{:S(2)}) collective-permute-start(bf16[528,128]{1,0:T(8,128)(2,1)S(1)} %get-tuple-element.16), channel_id=1, source_target_pairs={{0,17},{1,16},{2,19},{3,18},{16,1},{17,0},{18,3},{19,2},{4,21},{5,... | collective-permute-start | bytes 405512 | tf_op jit(solution)/shard_map/ppermute | solution.py:340
  11.6 1.4 %collective-permute-done.other_ref = bf16[768,256]{1,0:T(8,128)(2,1)S(1)} collective-permute-done((bf16[768,256]{1,0:T(8,128)(2,1)}, bf16[768,256]{1,0:T(8,128)(2,1)S(1)}, u32[]{:S(2)}, u32[]{:S(2)}) %collective-permute-start) | collective-permute-done | bytes 393248 | tf_op jit(solution)/shard_map/ppermute | solution.py:340
  13.0 3.3 %later.1 = (f32[512,1024]{1,0:T(8,128)S(1)}, bf16[528,128]{1,0:T(8,128)(2,1)S(1)}, bf16[528,128]{1,0:T(8,128)(2,1)S(1)}, bf16[528,128]{1,0:T(8,128)(2,1)S(1)}, bf16[528,128]{1,0:T(8,128)(2,1)S(1)}) custom-call(f32[16,512]{1,0:T(8,128)S(1)} %get-tuple-element.17.slots_ref, bf16[4,16,128]{2,1,0:T(8,128)(2,1)S(1)} %get-tuple-element.18.tiles_ref, ...), custom_call_target="tpu_custom_call" | custom-call | flops 1342177280 | bytes 3145728 | tf_op jit(solution)/shard_map/later/pallas_call | solution.py:390
  16.3 1.8 %collective-permute-start.7 = (bf16[528,128]{1,0:T(8,128)(2,1)S(1)}, bf16[528,128]{1,0:T(8,128)(2,1)S(1)}, u32[]{:S(2)}, u32[]{:S(2)}) collective-permute-start(bf16[528,128]{1,0:T(8,128)(2,1)S(1)} %get-tuple-element.23), channel_id=1, source_target_pairs={{0,16},{1,17},{2,18},{3,19},{16,0},{17,1},{18,2},{19,3},{4,20},{5,... | collective-permute-start | bytes 405512 | tf_op jit(solution)/shard_map/ppermute | solution.py:340
  18.1 3.2 %collective-permute-start.5 = (bf16[528,128]{1,0:T(8,128)(2,1)S(1)}, bf16[528,128]{1,0:T(8,128)(2,1)S(1)}, u32[]{:S(2)}, u32[]{:S(2)}) collective-permute-start(bf16[528,128]{1,0:T(8,128)(2,1)S(1)} %get-tuple-element.21), channel_id=1, source_target_pairs={{0,18},{1,19},{2,16},{3,17},{16,2},{17,3},{18,0},{19,1},{4,22},{5,... | collective-permute-start | bytes 405512 | tf_op jit(solution)/shard_map/ppermute | solution.py:340
  21.3 0.1 collective-permute-start.6
  21.5 1.0 %collective-permute-done.4.rest_3_ = bf16[528,128]{1,0:T(8,128)(2,1)S(1)} collective-permute-done((bf16[528,128]{1,0:T(8,128)(2,1)S(1)}, bf16[528,128]{1,0:T(8,128)(2,1)S(1)}, u32[]{:S(2)}, u32[]{:S(2)}) %collective-permute-start.4) | collective-permute-done | bytes 135200 | tf_op jit(solution)/shard_map/ppermute | solution.py:340
  22.5 0.2 score.4.rest_5_.own_ref
  22.7 1.6 %collective-permute-start.8 = (f32[8,128]{1,0:T(8,128)S(1)}, f32[8,128]{1,0:T(8,128)S(1)}, u32[]{:S(2)}, u32[]{:S(2)}) collective-permute-start(f32[8,128]{1,0:T(8,128)S(1)} %score.4.rest_5_.own_ref), channel_id=1, source_target_pairs={{0,16},{1,17},{2,18},{3,19},{16,0},{17,1},{18,2},{19,3},{4,20},{5,... | collective-permute-start | bytes 12296 | tf_op jit(solution)/shard_map/ppermute | solution.py:340
  24.3 1.1 %sum.1._.grad_ref = f32[768,1024]{1,0:T(8,128)S(1)} custom-call(bf16[768,256]{1,0:T(8,128)(2,1)S(1)} %bitcast.19, bf16[768,256]{1,0:T(8,128)(2,1)S(1)} %collective-permute-done.other_ref, bf16[528,128]{1,0:T(8,128)(2,1)S(1)} %collective-permute-done.1.rest_0_, bf16[528,128]{1,0:T(8,128)(2,1)S(1)} %collective-permute-done.2.rest_1_, ...), custom_call_target="tpu_custom_call" | custom-call | flops 805306368 | bytes 3145728 | tf_op jit(solution)/shard_map/sum/pallas_call | solution.py:436
  25.5 0.9 %collective-permute-done.8.other_ref = f32[8,128]{1,0:T(8,128)S(1)} collective-permute-done((f32[8,128]{1,0:T(8,128)S(1)}, f32[8,128]{1,0:T(8,128)S(1)}, u32[]{:S(2)}, u32[]{:S(2)}) %collective-permute-start.8) | collective-permute-done | bytes 4128 | tf_op jit(solution)/shard_map/ppermute | solution.py:340
  26.4 2.5 %collective-permute-start.10 = (f32[8,128]{1,0:T(8,128)S(1)}, f32[8,128]{1,0:T(8,128)S(1)}, u32[]{:S(2)}, u32[]{:S(2)}) collective-permute-start(f32[8,128]{1,0:T(8,128)S(1)} %merge.1.rest_2_), channel_id=1, source_target_pairs={{0,3},{1,2},{2,1},{3,0},{16,19},{17,18},{18,17},{19,16},{4,7},{5,6... | collective-permute-start | bytes 12296 | tf_op jit(solution)/shard_map/ppermute | solution.py:340
  28.9 0.2 collective-permute-start.9
  29.2 0.1 score.5.rest_1_.rest_2_
  29.3 1.5 %collective-permute-start.11 = (f32[8,128]{1,0:T(8,128)S(1)}, f32[8,128]{1,0:T(8,128)S(1)}, u32[]{:S(2)}, u32[]{:S(2)}) collective-permute-start(f32[8,128]{1,0:T(8,128)S(1)} %score.5.rest_1_.rest_2_), channel_id=1, source_target_pairs={{0,16},{1,17},{2,18},{3,19},{16,0},{17,1},{18,2},{19,3},{4,20},{5,... | collective-permute-start | bytes 12296 | tf_op jit(solution)/shard_map/ppermute | solution.py:340
  30.8 0.4 %collective-permute-done.5.rest_0_ = bf16[528,128]{1,0:T(8,128)(2,1)S(1)} collective-permute-done((bf16[528,128]{1,0:T(8,128)(2,1)S(1)}, bf16[528,128]{1,0:T(8,128)(2,1)S(1)}, u32[]{:S(2)}, u32[]{:S(2)}) %collective-permute-start.5) | collective-permute-done | bytes 135200 | tf_op jit(solution)/shard_map/ppermute | solution.py:340
  31.3 1.4 %collective-permute-start.13 = (f32[8,128]{1,0:T(8,128)S(1)}, f32[8,128]{1,0:T(8,128)S(1)}, u32[]{:S(2)}, u32[]{:S(2)}) collective-permute-start(f32[8,128]{1,0:T(8,128)S(1)} %score.6.rest_1_), channel_id=1, source_target_pairs={{0,18},{1,19},{2,16},{3,17},{16,2},{17,3},{18,0},{19,1},{4,22},{5,... | collective-permute-start | bytes 12296 | tf_op jit(solution)/shard_map/ppermute | solution.py:340
  32.8 2.0 %collective-permute-start.12 = (f32[8,128]{1,0:T(8,128)S(1)}, f32[8,128]{1,0:T(8,128)S(1)}, u32[]{:S(2)}, u32[]{:S(2)}) collective-permute-start(f32[8,128]{1,0:T(8,128)S(1)} %score.7.rest_3_), channel_id=1, source_target_pairs={{0,2},{1,3},{2,0},{3,1},{16,18},{17,19},{18,16},{19,17},{4,6},{5,7... | collective-permute-start | bytes 12296 | tf_op jit(solution)/shard_map/ppermute | solution.py:340
  34.8 3.4 %update.1 = f32[768,1024]{1,0:T(8,128)} custom-call(bf16[768,256]{1,0:T(8,128)(2,1)S(1)} %bitcast.20, bf16[768,256]{1,0:T(8,128)(2,1)S(1)} %collective-permute-done.other_ref, f32[768,1024]{1,0:T(8,128)S(1)} %sum.1._.grad_ref, f32[768,1024]{1,0:T(8,128)S(1)} %bitcast.16, bf16[768,1024]{1,0:T(8,128)(2,1)S(1)} %bitcast.21, bf16[768,1024]{1,0:T(8,128)(2,1)S(1)} %bitcast.22, ...), custom_call_target="tpu_custom_call" | custom-call | flops 402653184 | bytes 12582912 | tf_op jit(solution)/shard_map/update/pallas_call | solution.py:465
  38.3 0.9 %combine.1 = f32[8,512]{1,0:T(8,128)} custom-call(s32[8,512]{1,0:T(8,128)S(1)} %bitcast.24, f32[16,512]{1,0:T(8,128)S(1)} %get-tuple-element.17.slots_ref, f32[8,128]{1,0:T(8,128)S(1)} %collective-permute-done.9.rest_0_, f32[8,128]{1,0:T(8,128)S(1)} %collective-permute-done.10.rest_1_, f32[8,128]{1,0:T(8,128)S(1)} %score.5.rest_1_.rest_2_, ...), custom_call_target="tpu_custom_call" | custom-call | flops 524288 | bytes 32768 | tf_op jit(solution)/shard_map/combine/pallas_call | solution.py:491
  (24 shorter events, 0.4 us)
Async XLA Ops:
  0.6 12.4 %copy-start.1 = (bf16[1,1,768,256]{3,2,1,0:T(8,128)(2,1)S(1)}, bf16[1,1,768,256]{3,2,1,0:T(8,128)(2,1)}, u32[]{:S(2)}) copy-start(bf16[1,1,768,256]{3,2,1,0:T(8,128)(2,1)} %param.10) | copy-start | bytes 1179652
  0.6 12.4 %collective-permute-start = (bf16[768,256]{1,0:T(8,128)(2,1)}, bf16[768,256]{1,0:T(8,128)(2,1)S(1)}, u32[]{:S(2)}, u32[]{:S(2)}) collective-permute-start(bf16[768,256]{1,0:T(8,128)(2,1)} %bitcast.17), channel_id=1, source_target_pairs={{0,16},{1,17},{2,18},{3,19},{16,0},{17,1},{18,2},{19,3},{4,20},{5,... | collective-permute-start | bytes 1179656 | tf_op jit(solution)/shard_map/ppermute | solution.py:340
  5.7 12.5 %collective-permute-start.1 = (bf16[528,128]{1,0:T(8,128)(2,1)S(1)}, bf16[528,128]{1,0:T(8,128)(2,1)S(1)}, u32[]{:S(2)}, u32[]{:S(2)}) collective-permute-start(bf16[528,128]{1,0:T(8,128)(2,1)S(1)} %get-tuple-element.13), channel_id=1, source_target_pairs={{0,3},{1,2},{2,1},{3,0},{16,19},{17,18},{18,17},{19,16},{4,7},{5,6... | collective-permute-start | bytes 405512 | tf_op jit(solution)/shard_map/ppermute | solution.py:340
  9.3 12.0 %collective-permute-start.2 = (bf16[528,128]{1,0:T(8,128)(2,1)S(1)}, bf16[528,128]{1,0:T(8,128)(2,1)S(1)}, u32[]{:S(2)}, u32[]{:S(2)}) collective-permute-start(bf16[528,128]{1,0:T(8,128)(2,1)S(1)} %get-tuple-element.14), channel_id=1, source_target_pairs={{0,1},{1,0},{2,3},{3,2},{16,17},{17,16},{18,19},{19,18},{4,5},{5,4... | collective-permute-start | bytes 405512 | tf_op jit(solution)/shard_map/ppermute | solution.py:340
  9.3 12.1 %collective-permute-start.3 = (bf16[528,128]{1,0:T(8,128)(2,1)S(1)}, bf16[528,128]{1,0:T(8,128)(2,1)S(1)}, u32[]{:S(2)}, u32[]{:S(2)}) collective-permute-start(bf16[528,128]{1,0:T(8,128)(2,1)S(1)} %get-tuple-element.15), channel_id=1, source_target_pairs={{0,19},{1,18},{2,17},{3,16},{16,3},{17,2},{18,1},{19,0},{4,23},{5,... | collective-permute-start | bytes 405512 | tf_op jit(solution)/shard_map/ppermute | solution.py:340
  10.2 12.3 %collective-permute-start.4 = (bf16[528,128]{1,0:T(8,128)(2,1)S(1)}, bf16[528,128]{1,0:T(8,128)(2,1)S(1)}, u32[]{:S(2)}, u32[]{:S(2)}) collective-permute-start(bf16[528,128]{1,0:T(8,128)(2,1)S(1)} %get-tuple-element.16), channel_id=1, source_target_pairs={{0,17},{1,16},{2,19},{3,18},{16,1},{17,0},{18,3},{19,2},{4,21},{5,... | collective-permute-start | bytes 405512 | tf_op jit(solution)/shard_map/ppermute | solution.py:340
  16.3 12.8 %collective-permute-start.7 = (bf16[528,128]{1,0:T(8,128)(2,1)S(1)}, bf16[528,128]{1,0:T(8,128)(2,1)S(1)}, u32[]{:S(2)}, u32[]{:S(2)}) collective-permute-start(bf16[528,128]{1,0:T(8,128)(2,1)S(1)} %get-tuple-element.23), channel_id=1, source_target_pairs={{0,16},{1,17},{2,18},{3,19},{16,0},{17,1},{18,2},{19,3},{4,20},{5,... | collective-permute-start | bytes 405512 | tf_op jit(solution)/shard_map/ppermute | solution.py:340
  18.1 13.1 %collective-permute-start.5 = (bf16[528,128]{1,0:T(8,128)(2,1)S(1)}, bf16[528,128]{1,0:T(8,128)(2,1)S(1)}, u32[]{:S(2)}, u32[]{:S(2)}) collective-permute-start(bf16[528,128]{1,0:T(8,128)(2,1)S(1)} %get-tuple-element.21), channel_id=1, source_target_pairs={{0,18},{1,19},{2,16},{3,17},{16,2},{17,3},{18,0},{19,1},{4,22},{5,... | collective-permute-start | bytes 405512 | tf_op jit(solution)/shard_map/ppermute | solution.py:340
  21.3 11.4 %collective-permute-start.6 = (bf16[528,128]{1,0:T(8,128)(2,1)S(1)}, bf16[528,128]{1,0:T(8,128)(2,1)S(1)}, u32[]{:S(2)}, u32[]{:S(2)}) collective-permute-start(bf16[528,128]{1,0:T(8,128)(2,1)S(1)} %get-tuple-element.22), channel_id=1, source_target_pairs={{0,2},{1,3},{2,0},{3,1},{16,18},{17,19},{18,16},{19,17},{4,6},{5,7... | collective-permute-start | bytes 405512 | tf_op jit(solution)/shard_map/ppermute | solution.py:340
  22.7 3.7 %collective-permute-start.8 = (f32[8,128]{1,0:T(8,128)S(1)}, f32[8,128]{1,0:T(8,128)S(1)}, u32[]{:S(2)}, u32[]{:S(2)}) collective-permute-start(f32[8,128]{1,0:T(8,128)S(1)} %score.4.rest_5_.own_ref), channel_id=1, source_target_pairs={{0,16},{1,17},{2,18},{3,19},{16,0},{17,1},{18,2},{19,3},{4,20},{5,... | collective-permute-start | bytes 12296 | tf_op jit(solution)/shard_map/ppermute | solution.py:340
  26.4 11.8 %collective-permute-start.10 = (f32[8,128]{1,0:T(8,128)S(1)}, f32[8,128]{1,0:T(8,128)S(1)}, u32[]{:S(2)}, u32[]{:S(2)}) collective-permute-start(f32[8,128]{1,0:T(8,128)S(1)} %merge.1.rest_2_), channel_id=1, source_target_pairs={{0,3},{1,2},{2,1},{3,0},{16,19},{17,18},{18,17},{19,16},{4,7},{5,6... | collective-permute-start | bytes 12296 | tf_op jit(solution)/shard_map/ppermute | solution.py:340
  28.9 9.3 %collective-permute-start.9 = (f32[8,128]{1,0:T(8,128)S(1)}, f32[8,128]{1,0:T(8,128)S(1)}, u32[]{:S(2)}, u32[]{:S(2)}) collective-permute-start(f32[8,128]{1,0:T(8,128)S(1)} %merge.1.rest_2_), channel_id=1, source_target_pairs={{0,1},{1,0},{2,3},{3,2},{16,17},{17,16},{18,19},{19,18},{4,5},{5,4... | collective-permute-start | bytes 12296 | tf_op jit(solution)/shard_map/ppermute | solution.py:340
  29.2 5.7 %copy-start.2 = (bf16[1,1,768,1024]{3,2,1,0:T(8,128)(2,1)S(1)}, bf16[1,1,768,1024]{3,2,1,0:T(8,128)(2,1)}, u32[]{:S(2)}) copy-start(bf16[1,1,768,1024]{3,2,1,0:T(8,128)(2,1)} %param.12) | copy-start | bytes 4718596
  29.2 5.7 %copy-start.3 = (bf16[1,1,768,1024]{3,2,1,0:T(8,128)(2,1)S(1)}, bf16[1,1,768,1024]{3,2,1,0:T(8,128)(2,1)}, u32[]{:S(2)}) copy-start(bf16[1,1,768,1024]{3,2,1,0:T(8,128)(2,1)} %param.13) | copy-start | bytes 4718596
  29.3 5.5 %copy-start = (f32[1,1,768,1024]{3,2,1,0:T(8,128)S(1)}, f32[1,1,768,1024]{3,2,1,0:T(8,128)}, u32[]{:S(2)}) copy-start(f32[1,1,768,1024]{3,2,1,0:T(8,128)} %param.11) | copy-start | bytes 9437188
  29.3 9.0 %collective-permute-start.11 = (f32[8,128]{1,0:T(8,128)S(1)}, f32[8,128]{1,0:T(8,128)S(1)}, u32[]{:S(2)}, u32[]{:S(2)}) collective-permute-start(f32[8,128]{1,0:T(8,128)S(1)} %score.5.rest_1_.rest_2_), channel_id=1, source_target_pairs={{0,16},{1,17},{2,18},{3,19},{16,0},{17,1},{18,2},{19,3},{4,20},{5,... | collective-permute-start | bytes 12296 | tf_op jit(solution)/shard_map/ppermute | solution.py:340
  31.3 6.9 %collective-permute-start.13 = (f32[8,128]{1,0:T(8,128)S(1)}, f32[8,128]{1,0:T(8,128)S(1)}, u32[]{:S(2)}, u32[]{:S(2)}) collective-permute-start(f32[8,128]{1,0:T(8,128)S(1)} %score.6.rest_1_), channel_id=1, source_target_pairs={{0,18},{1,19},{2,16},{3,17},{16,2},{17,3},{18,0},{19,1},{4,22},{5,... | collective-permute-start | bytes 12296 | tf_op jit(solution)/shard_map/ppermute | solution.py:340
  32.8 5.4 %collective-permute-start.12 = (f32[8,128]{1,0:T(8,128)S(1)}, f32[8,128]{1,0:T(8,128)S(1)}, u32[]{:S(2)}, u32[]{:S(2)}) collective-permute-start(f32[8,128]{1,0:T(8,128)S(1)} %score.7.rest_3_), channel_id=1, source_target_pairs={{0,2},{1,3},{2,0},{3,1},{16,18},{17,19},{18,16},{19,17},{4,6},{5,7... | collective-permute-start | bytes 12296 | tf_op jit(solution)/shard_map/ppermute | solution.py:340
  34.8 3.5 %copy-start.4 = (s32[1,512,8]{1,2,0:T(8,128)S(1)}, s32[1,512,8]{1,2,0:T(8,128)}, u32[]{:S(2)}) copy-start(s32[1,512,8]{1,2,0:T(8,128)} %param.9) | copy-start | bytes 49156

commit v22 on v20

--- a/solution.py
+++ b/solution.py
@@ -193,9 +193,9 @@
         scaled[lines, at : at + LANES] = (hidden[lines, :].astype(F32) * line).astype(BF16)
 
 
-def sum_kernel(items, group, cap, own_ref, other_ref, *rest):
+def sum_kernel(items, group, cap, own_ref, other_ref, moment_ref, second_ref, *rest):
     chunks = dict(zip(items, rest))
-    grad_ref, rows, scaled = rest[-3:]
+    grad_ref, first_ref, square_ref, rows, scaled = rest[-5:]
     blocks = rows.shape[1] // LANES
     slots = group * cap
     me = ep_index()
@@ -216,6 +216,12 @@
             lanes = slice(part * LANES, (part + 1) * LANES)
             scale_into(scaled, side * slots + part * LANES, hidden.at[:, lanes], tile[part : part + 1, :])
     grad_ref[...] = jnp.dot(scaled[...], rows[...], preferred_element_type=F32)
+    for top in range(0, grad_ref.shape[0], TILE):
+        lines = slice(top, top + TILE)
+        first_ref[lines, :] = (
+            moment_ref[lines, :].astype(F32) * (beta_first / (1.0 - beta_first)) + grad_ref[lines, :]
+        )
+        square_ref[lines, :] = second_ref[lines, :].astype(F32) * (beta_second / (1.0 - beta_second))
 
 
 def merge_kernel(cap, own_ref, other_ref, _, out_ref):
@@ -224,7 +230,7 @@
     out_ref[...] = jnp.where(lane < cap, scores, 0.0)
 
 
-def update_kernel(items, cap, own_ref, other_ref, grad_ref, master_ref, moment_ref, second_ref, *rest):
+def update_kernel(items, cap, own_ref, other_ref, grad_ref, first_ref, square_ref, master_ref, *rest):
     chunks = rest[: len(items)]
     _, update_hbm, rows, scaled, total, update, sems = rest[len(items) :]
     hid, half = update.shape
@@ -261,12 +267,10 @@
 
     def moments(top, columns):
         lines = slice(top, top + TILE)
-        grad = total[lines, columns] + grad_ref[lines, columns]
-        first = moment_ref[lines, columns].astype(F32) * (beta_first / (1.0 - beta_first)) + grad
-        square = (
-            second_ref[lines, columns].astype(F32) * (beta_second / (1.0 - beta_second))
-            + grad * grad
-        )
+        added = total[lines, columns]
+        grad = added + grad_ref[lines, columns]
+        first = added + first_ref[lines, columns]
+        square = square_ref[lines, columns] + grad * grad
         return first, square, lax.rsqrt(square)
 
     def inverse(first, square, root):
@@ -433,11 +437,11 @@
     other_scores = moved(first_scores, 1, 0)
     added = [(1, far), (0, far), (1, 0)]
     summed = [item for item in order if item not in added]
-    grad = pl.pallas_call(
+    grad, *prepared = pl.pallas_call(
         functools.partial(sum_kernel, summed, group, cap),
-        out_shape=jax.ShapeDtypeStruct((hid, half), F32),
-        in_specs=specs(pltpu.VMEM, 2 + len(summed)) + specs(pl.ANY, 1),
-        out_specs=specs(pltpu.VMEM, 1)[0],
+        out_shape=[jax.ShapeDtypeStruct((hid, half), F32)] * 3,
+        in_specs=specs(pltpu.VMEM, 4 + len(summed)) + specs(pl.ANY, 1),
+        out_specs=specs(pltpu.VMEM, 3),
         scratch_shapes=[
             pltpu.VMEM((2 * slots, half), BF16),
             pltpu.VMEM((hid, 2 * slots), BF16),
@@ -445,7 +449,14 @@
         compiler_params=params(),
         cost_estimate=cost(4 * slots * hid * half, 4 * hid * half),
         name="sum",
-    )(own_hidden, other_hidden, *[arrived[item] for item in summed], first_scores)
+    )(
+        own_hidden,
+        other_hidden,
+        moment[0, 0],
+        second[0, 0],
+        *[arrived[item] for item in summed],
+        first_scores,
+    )
     merged = pl.pallas_call(
         functools.partial(merge_kernel, cap),
         out_shape=tile,
@@ -481,9 +492,8 @@
         own_hidden,
         other_hidden,
         grad,
+        *prepared,
         param,
-        moment[0, 0],
-        second[0, 0],
         *[arrived[item] for item in added],
         last_scores,
     )

time: 39 us -> 39.8 us (1.021)
  local copies, waits for them, and re-layouts: 0.02 us -> 1.01 us
  waiting for transfers between devices: 3.81 us -> 3.36 us
    unnamed x10 -> x12, local copies, waits for them, and re-layouts: 0.02 us -> 1.01 us
    ppermute x14, waiting for transfers between devices: 3.81 us -> 3.36 us  [moved(): return lax.ppermute(array, ('pair', 'ep'), pairs)]
where the time goes in v22:
time: 39.8 us; the launch traced here: 39.6 us
  starting transfers between devices  23.1 us (58%)
  Pallas kernels  11.3 us (28%)
  waiting for transfers between devices  3.36 us (8%)
  local copies, waits for them, and re-layouts  1.01 us (3%)
  between operations  0.73 us (2%)
    ppermute x14, starting transfers between devices, moved(): return lax.ppermute(array, ('pair', 'ep'), pairs)  23.1 us
    pallas_call x1, Pallas kernels, local(): pl.pallas_call(functools.partial(later_kernel, last_items, late, cap), ou...  3.45 us
    ppermute x14, waiting for transfers between devices, moved(): return lax.ppermute(array, ('pair', 'ep'), pairs)  3.36 us
    pallas_call x1, Pallas kernels, local(): pl.pallas_call(functools.partial(update_kernel, added, cap), out_shape=ja...  2.99 us
    pallas_call x1, Pallas kernels, local(): pl.pallas_call(functools.partial(route_kernel, first_items, first, group,...  1.99 us
    pallas_call x1, Pallas kernels, local(): pl.pallas_call(functools.partial(sum_kernel, summed, group, cap), out_sha...  1.37 us
    unnamed x12, local copies, waits for them, and re-layouts  1.01 us
    pallas_call x1, Pallas kernels, local(): pl.pallas_call(functools.partial(combine_kernel, [(k, len(arrays)) for k,...  0.87 us
  transfers between devices with their start and end apart: 14, of which 4 were waited for; matrix products, arithmetic and copies ran while one was open for 0% of the time, Pallas kernels for 26%

profile of v22, /device:TPU:0, one launch (start us, length us, event | category | flops | bytes accessed | tf_op | source)
XLA Modules:
  0.0 39.6 jit_solution(6903554693318296717)
XLA Ops:
  0.6 3.0 %collective-permute-start = (bf16[768,256]{1,0:T(8,128)(2,1)}, bf16[768,256]{1,0:T(8,128)(2,1)S(1)}, u32[]{:S(2)}, u32[]{:S(2)}) collective-permute-start(bf16[768,256]{1,0:T(8,128)(2,1)} %bitcast.17), channel_id=1, source_target_pairs={{0,16},{1,17},{2,18},{3,19},{16,0},{17,1},{18,2},{19,3},{4,20},{5,... | collective-permute-start | bytes 1179656 | tf_op jit(solution)/shard_map/ppermute | solution.py:344
  3.7 2.0 %route.1 = (f32[16,512]{1,0:T(8,128)S(1)}, bf16[4,16,128]{2,1,0:T(8,128)(2,1)S(1)}, bf16[528,128]{1,0:T(8,128)(2,1)S(1)}, bf16[528,128]{1,0:T(8,128)(2,1)S(1)}, ...) custom-call(s32[8,512]{1,0:T(8,128)} %bitcast.23, bf16[8,512]{1,0:T(8,128)(2,1)} %bitcast.29, ...), custom_call_target="tpu_custom_call" | custom-call | flops 536870912 | bytes 3145728 | tf_op jit(solution)/shard_map/route/pallas_call | solution.py:368
  5.7 3.7 %collective-permute-start.1 = (bf16[528,128]{1,0:T(8,128)(2,1)S(1)}, bf16[528,128]{1,0:T(8,128)(2,1)S(1)}, u32[]{:S(2)}, u32[]{:S(2)}) collective-permute-start(bf16[528,128]{1,0:T(8,128)(2,1)S(1)} %get-tuple-element.16), channel_id=1, source_target_pairs={{0,3},{1,2},{2,1},{3,0},{16,19},{17,18},{18,17},{19,16},{4,7},{5,6... | collective-permute-start | bytes 405512 | tf_op jit(solution)/shard_map/ppermute | solution.py:344
  9.3 0.8 %collective-permute-start.3 = (bf16[528,128]{1,0:T(8,128)(2,1)S(1)}, bf16[528,128]{1,0:T(8,128)(2,1)S(1)}, u32[]{:S(2)}, u32[]{:S(2)}) collective-permute-start(bf16[528,128]{1,0:T(8,128)(2,1)S(1)} %get-tuple-element.18), channel_id=1, source_target_pairs={{0,19},{1,18},{2,17},{3,16},{16,3},{17,2},{18,1},{19,0},{4,23},{5,... | collective-permute-start | bytes 405512 | tf_op jit(solution)/shard_map/ppermute | solution.py:344
  10.2 1.4 %collective-permute-start.4 = (bf16[528,128]{1,0:T(8,128)(2,1)S(1)}, bf16[528,128]{1,0:T(8,128)(2,1)S(1)}, u32[]{:S(2)}, u32[]{:S(2)}) collective-permute-start(bf16[528,128]{1,0:T(8,128)(2,1)S(1)} %get-tuple-element.19), channel_id=1, source_target_pairs={{0,17},{1,16},{2,19},{3,18},{16,1},{17,0},{18,3},{19,2},{4,21},{5,... | collective-permute-start | bytes 405512 | tf_op jit(solution)/shard_map/ppermute | solution.py:344
  11.6 1.4 %collective-permute-done.other_ref = bf16[768,256]{1,0:T(8,128)(2,1)S(1)} collective-permute-done((bf16[768,256]{1,0:T(8,128)(2,1)}, bf16[768,256]{1,0:T(8,128)(2,1)S(1)}, u32[]{:S(2)}, u32[]{:S(2)}) %collective-permute-start) | collective-permute-done | bytes 393248 | tf_op jit(solution)/shard_map/ppermute | solution.py:344
  13.0 1.0 %copy-done.1 = bf16[1,1,768,256]{3,2,1,0:T(8,128)(2,1)S(1)} copy-done((bf16[1,1,768,256]{3,2,1,0:T(8,128)(2,1)S(1)}, bf16[1,1,768,256]{3,2,1,0:T(8,128)(2,1)}, u32[]{:S(2)}) %copy-start.1) | copy-done | bytes 393240
  14.0 3.5 %later.1 = (f32[512,1024]{1,0:T(8,128)S(1)}, bf16[528,128]{1,0:T(8,128)(2,1)S(1)}, bf16[528,128]{1,0:T(8,128)(2,1)S(1)}, bf16[528,128]{1,0:T(8,128)(2,1)S(1)}, bf16[528,128]{1,0:T(8,128)(2,1)S(1)}) custom-call(f32[16,512]{1,0:T(8,128)S(1)} %get-tuple-element.20.slots_ref, bf16[4,16,128]{2,1,0:T(8,128)(2,1)S(1)} %get-tuple-element.21.tiles_ref, ...), custom_call_target="tpu_custom_call" | custom-call | flops 1342177280 | bytes 3145728 | tf_op jit(solution)/shard_map/later/pallas_call | solution.py:394
  17.5 1.8 %collective-permute-start.7 = (bf16[528,128]{1,0:T(8,128)(2,1)S(1)}, bf16[528,128]{1,0:T(8,128)(2,1)S(1)}, u32[]{:S(2)}, u32[]{:S(2)}) collective-permute-start(bf16[528,128]{1,0:T(8,128)(2,1)S(1)} %get-tuple-element.29), channel_id=1, source_target_pairs={{0,16},{1,17},{2,18},{3,19},{16,0},{17,1},{18,2},{19,3},{4,20},{5,... | collective-permute-start | bytes 405512 | tf_op jit(solution)/shard_map/ppermute | solution.py:344
  19.3 3.2 %collective-permute-start.5 = (bf16[528,128]{1,0:T(8,128)(2,1)S(1)}, bf16[528,128]{1,0:T(8,128)(2,1)S(1)}, u32[]{:S(2)}, u32[]{:S(2)}) collective-permute-start(bf16[528,128]{1,0:T(8,128)(2,1)S(1)} %get-tuple-element.27), channel_id=1, source_target_pairs={{0,18},{1,19},{2,16},{3,17},{16,2},{17,3},{18,0},{19,1},{4,22},{5,... | collective-permute-start | bytes 405512 | tf_op jit(solution)/shard_map/ppermute | solution.py:344
  22.4 0.1 collective-permute-start.6
  22.6 0.2 score.4.rest_5_.own_ref
  22.8 1.5 %collective-permute-start.8 = (f32[8,128]{1,0:T(8,128)S(1)}, f32[8,128]{1,0:T(8,128)S(1)}, u32[]{:S(2)}, u32[]{:S(2)}) collective-permute-start(f32[8,128]{1,0:T(8,128)S(1)} %score.4.rest_5_.own_ref), channel_id=1, source_target_pairs={{0,16},{1,17},{2,18},{3,19},{16,0},{17,1},{18,2},{19,3},{4,20},{5,... | collective-permute-start | bytes 12296 | tf_op jit(solution)/shard_map/ppermute | solution.py:344
  24.3 1.4 %sum.1 = (f32[768,1024]{1,0:T(8,128)S(1)}, f32[768,1024]{1,0:T(8,128)S(1)}, f32[768,1024]{1,0:T(8,128)S(1)}) custom-call(bf16[768,256]{1,0:T(8,128)(2,1)S(1)} %bitcast.19, bf16[768,256]{1,0:T(8,128)(2,1)S(1)} %collective-permute-done.other_ref, bf16[768,1024]{1,0:T(8,128)(2,1)S(1)} %bitcast.21, bf16[768,1024]{1,0:T(8,128)(2,1)S(1)} %bitcast.22, ...), custom_call_target="tpu_custom_call" | custom-call | flops 805306368 | bytes 3145728 | tf_op jit(solution)/shard_map/sum/pallas_call | solution.py:440
  25.6 0.8 %collective-permute-done.8.other_ref = f32[8,128]{1,0:T(8,128)S(1)} collective-permute-done((f32[8,128]{1,0:T(8,128)S(1)}, f32[8,128]{1,0:T(8,128)S(1)}, u32[]{:S(2)}, u32[]{:S(2)}) %collective-permute-start.8) | collective-permute-done | bytes 4128 | tf_op jit(solution)/shard_map/ppermute | solution.py:344
  26.5 3.5 %collective-permute-start.10 = (f32[8,128]{1,0:T(8,128)S(1)}, f32[8,128]{1,0:T(8,128)S(1)}, u32[]{:S(2)}, u32[]{:S(2)}) collective-permute-start(f32[8,128]{1,0:T(8,128)S(1)} %merge.1.rest_2_), channel_id=1, source_target_pairs={{0,3},{1,2},{2,1},{3,0},{16,19},{17,18},{18,17},{19,16},{4,7},{5,6... | collective-permute-start | bytes 12296 | tf_op jit(solution)/shard_map/ppermute | solution.py:344
  30.1 0.2 collective-permute-start.9
  30.4 1.4 %collective-permute-start.11 = (f32[8,128]{1,0:T(8,128)S(1)}, f32[8,128]{1,0:T(8,128)S(1)}, u32[]{:S(2)}, u32[]{:S(2)}) collective-permute-start(f32[8,128]{1,0:T(8,128)S(1)} %score.5.rest_1_.rest_2_), channel_id=1, source_target_pairs={{0,16},{1,17},{2,18},{3,19},{16,0},{17,1},{18,2},{19,3},{4,20},{5,... | collective-permute-start | bytes 12296 | tf_op jit(solution)/shard_map/ppermute | solution.py:344
  31.8 0.5 %collective-permute-done.5.rest_0_ = bf16[528,128]{1,0:T(8,128)(2,1)S(1)} collective-permute-done((bf16[528,128]{1,0:T(8,128)(2,1)S(1)}, bf16[528,128]{1,0:T(8,128)(2,1)S(1)}, u32[]{:S(2)}, u32[]{:S(2)}) %collective-permute-start.5) | collective-permute-done | bytes 135200 | tf_op jit(solution)/shard_map/ppermute | solution.py:344
  32.4 0.4 collective-permute-start.13
  32.8 0.6 %collective-permute-done.6.rest_0_.rest_1_ = bf16[528,128]{1,0:T(8,128)(2,1)S(1)} collective-permute-done((bf16[528,128]{1,0:T(8,128)(2,1)S(1)}, bf16[528,128]{1,0:T(8,128)(2,1)S(1)}, u32[]{:S(2)}, u32[]{:S(2)}) %collective-permute-start.6) | collective-permute-done | bytes 135200 | tf_op jit(solution)/shard_map/ppermute | solution.py:344
  33.5 2.1 %collective-permute-start.12 = (f32[8,128]{1,0:T(8,128)S(1)}, f32[8,128]{1,0:T(8,128)S(1)}, u32[]{:S(2)}, u32[]{:S(2)}) collective-permute-start(f32[8,128]{1,0:T(8,128)S(1)} %score.7.rest_3_), channel_id=1, source_target_pairs={{0,2},{1,3},{2,0},{3,1},{16,18},{17,19},{18,16},{19,17},{4,6},{5,7... | collective-permute-start | bytes 12296 | tf_op jit(solution)/shard_map/ppermute | solution.py:344
  35.6 3.0 %update.1 = f32[768,1024]{1,0:T(8,128)} custom-call(bf16[768,256]{1,0:T(8,128)(2,1)S(1)} %bitcast.20, bf16[768,256]{1,0:T(8,128)(2,1)S(1)} %collective-permute-done.other_ref, f32[768,1024]{1,0:T(8,128)S(1)} %get-tuple-element.24._.grad_ref, f32[768,1024]{1,0:T(8,128)S(1)} %get-tuple-element.25.first_ref, f32[768,1024]{1,0:T(8,128)S(1)} %get-tuple-element.26.square_ref, ...), custom_call_target="tpu_custom_call" | custom-call | flops 402653184 | bytes 12582912 | tf_op jit(solution)/shard_map/update/pallas_call | solution.py:476
  38.7 0.9 %combine.1 = f32[8,512]{1,0:T(8,128)} custom-call(s32[8,512]{1,0:T(8,128)S(1)} %bitcast.24, f32[16,512]{1,0:T(8,128)S(1)} %get-tuple-element.20.slots_ref, f32[8,128]{1,0:T(8,128)S(1)} %collective-permute-done.9.rest_0_, f32[8,128]{1,0:T(8,128)S(1)} %collective-permute-done.10.rest_1_, f32[8,128]{1,0:T(8,128)S(1)} %score.5.rest_1_.rest_2_, ...), custom_call_target="tpu_custom_call" | custom-call | flops 524288 | bytes 32768 | tf_op jit(solution)/shard_map/combine/pallas_call | solution.py:501
  (26 shorter events, 0.5 us)
Async XLA Ops:
  0.6 12.4 %collective-permute-start = (bf16[768,256]{1,0:T(8,128)(2,1)}, bf16[768,256]{1,0:T(8,128)(2,1)S(1)}, u32[]{:S(2)}, u32[]{:S(2)}) collective-permute-start(bf16[768,256]{1,0:T(8,128)(2,1)} %bitcast.17), channel_id=1, source_target_pairs={{0,16},{1,17},{2,18},{3,19},{16,0},{17,1},{18,2},{19,3},{4,20},{5,... | collective-permute-start | bytes 1179656 | tf_op jit(solution)/shard_map/ppermute | solution.py:344
  5.7 13.6 %collective-permute-start.1 = (bf16[528,128]{1,0:T(8,128)(2,1)S(1)}, bf16[528,128]{1,0:T(8,128)(2,1)S(1)}, u32[]{:S(2)}, u32[]{:S(2)}) collective-permute-start(bf16[528,128]{1,0:T(8,128)(2,1)S(1)} %get-tuple-element.16), channel_id=1, source_target_pairs={{0,3},{1,2},{2,1},{3,0},{16,19},{17,18},{18,17},{19,16},{4,7},{5,6... | collective-permute-start | bytes 405512 | tf_op jit(solution)/shard_map/ppermute | solution.py:344
  9.3 13.1 %collective-permute-start.2 = (bf16[528,128]{1,0:T(8,128)(2,1)S(1)}, bf16[528,128]{1,0:T(8,128)(2,1)S(1)}, u32[]{:S(2)}, u32[]{:S(2)}) collective-permute-start(bf16[528,128]{1,0:T(8,128)(2,1)S(1)} %get-tuple-element.17), channel_id=1, source_target_pairs={{0,1},{1,0},{2,3},{3,2},{16,17},{17,16},{18,19},{19,18},{4,5},{5,4... | collective-permute-start | bytes 405512 | tf_op jit(solution)/shard_map/ppermute | solution.py:344
  9.3 13.2 %collective-permute-start.3 = (bf16[528,128]{1,0:T(8,128)(2,1)S(1)}, bf16[528,128]{1,0:T(8,128)(2,1)S(1)}, u32[]{:S(2)}, u32[]{:S(2)}) collective-permute-start(bf16[528,128]{1,0:T(8,128)(2,1)S(1)} %get-tuple-element.18), channel_id=1, source_target_pairs={{0,19},{1,18},{2,17},{3,16},{16,3},{17,2},{18,1},{19,0},{4,23},{5,... | collective-permute-start | bytes 405512 | tf_op jit(solution)/shard_map/ppermute | solution.py:344
  10.2 12.4 %collective-permute-start.4 = (bf16[528,128]{1,0:T(8,128)(2,1)S(1)}, bf16[528,128]{1,0:T(8,128)(2,1)S(1)}, u32[]{:S(2)}, u32[]{:S(2)}) collective-permute-start(bf16[528,128]{1,0:T(8,128)(2,1)S(1)} %get-tuple-element.19), channel_id=1, source_target_pairs={{0,17},{1,16},{2,19},{3,18},{16,1},{17,0},{18,3},{19,2},{4,21},{5,... | collective-permute-start | bytes 405512 | tf_op jit(solution)/shard_map/ppermute | solution.py:344
  13.0 1.0 %copy-start.1 = (bf16[1,1,768,256]{3,2,1,0:T(8,128)(2,1)S(1)}, bf16[1,1,768,256]{3,2,1,0:T(8,128)(2,1)}, u32[]{:S(2)}) copy-start(bf16[1,1,768,256]{3,2,1,0:T(8,128)(2,1)} %param.10) | copy-start | bytes 1179652
  14.0 10.3 %copy-start.2 = (bf16[1,1,768,256]{3,2,1,0:T(8,128)(2,1)S(1)}, bf16[1,1,768,256]{3,2,1,0:T(8,128)(2,1)}, u32[]{:S(2)}) copy-start(bf16[1,1,768,256]{3,2,1,0:T(8,128)(2,1)} %param.10) | copy-start | bytes 1179652
  14.0 10.3 %copy-start.3 = (bf16[1,1,768,1024]{3,2,1,0:T(8,128)(2,1)S(1)}, bf16[1,1,768,1024]{3,2,1,0:T(8,128)(2,1)}, u32[]{:S(2)}) copy-start(bf16[1,1,768,1024]{3,2,1,0:T(8,128)(2,1)} %param.12) | copy-start | bytes 4718596
  14.0 10.3 %copy-start.4 = (bf16[1,1,768,1024]{3,2,1,0:T(8,128)(2,1)S(1)}, bf16[1,1,768,1024]{3,2,1,0:T(8,128)(2,1)}, u32[]{:S(2)}) copy-start(bf16[1,1,768,1024]{3,2,1,0:T(8,128)(2,1)} %param.13) | copy-start | bytes 4718596
  17.5 12.8 %collective-permute-start.7 = (bf16[528,128]{1,0:T(8,128)(2,1)S(1)}, bf16[528,128]{1,0:T(8,128)(2,1)S(1)}, u32[]{:S(2)}, u32[]{:S(2)}) collective-permute-start(bf16[528,128]{1,0:T(8,128)(2,1)S(1)} %get-tuple-element.29), channel_id=1, source_target_pairs={{0,16},{1,17},{2,18},{3,19},{16,0},{17,1},{18,2},{19,3},{4,20},{5,... | collective-permute-start | bytes 405512 | tf_op jit(solution)/shard_map/ppermute | solution.py:344
  19.3 13.0 %collective-permute-start.5 = (bf16[528,128]{1,0:T(8,128)(2,1)S(1)}, bf16[528,128]{1,0:T(8,128)(2,1)S(1)}, u32[]{:S(2)}, u32[]{:S(2)}) collective-permute-start(bf16[528,128]{1,0:T(8,128)(2,1)S(1)} %get-tuple-element.27), channel_id=1, source_target_pairs={{0,18},{1,19},{2,16},{3,17},{16,2},{17,3},{18,0},{19,1},{4,22},{5,... | collective-permute-start | bytes 405512 | tf_op jit(solution)/shard_map/ppermute | solution.py:344
  22.4 10.9 %collective-permute-start.6 = (bf16[528,128]{1,0:T(8,128)(2,1)S(1)}, bf16[528,128]{1,0:T(8,128)(2,1)S(1)}, u32[]{:S(2)}, u32[]{:S(2)}) collective-permute-start(bf16[528,128]{1,0:T(8,128)(2,1)S(1)} %get-tuple-element.28), channel_id=1, source_target_pairs={{0,2},{1,3},{2,0},{3,1},{16,18},{17,19},{18,16},{19,17},{4,6},{5,7... | collective-permute-start | bytes 405512 | tf_op jit(solution)/shard_map/ppermute | solution.py:344
  22.8 3.7 %collective-permute-start.8 = (f32[8,128]{1,0:T(8,128)S(1)}, f32[8,128]{1,0:T(8,128)S(1)}, u32[]{:S(2)}, u32[]{:S(2)}) collective-permute-start(f32[8,128]{1,0:T(8,128)S(1)} %score.4.rest_5_.own_ref), channel_id=1, source_target_pairs={{0,16},{1,17},{2,18},{3,19},{16,0},{17,1},{18,2},{19,3},{4,20},{5,... | collective-permute-start | bytes 12296 | tf_op jit(solution)/shard_map/ppermute | solution.py:344
  26.5 9.1 %copy-start = (f32[1,1,768,1024]{3,2,1,0:T(8,128)S(1)}, f32[1,1,768,1024]{3,2,1,0:T(8,128)}, u32[]{:S(2)}) copy-start(f32[1,1,768,1024]{3,2,1,0:T(8,128)} %param.11) | copy-start | bytes 9437188
  26.5 12.1 %collective-permute-start.10 = (f32[8,128]{1,0:T(8,128)S(1)}, f32[8,128]{1,0:T(8,128)S(1)}, u32[]{:S(2)}, u32[]{:S(2)}) collective-permute-start(f32[8,128]{1,0:T(8,128)S(1)} %merge.1.rest_2_), channel_id=1, source_target_pairs={{0,3},{1,2},{2,1},{3,0},{16,19},{17,18},{18,17},{19,16},{4,7},{5,6... | collective-permute-start | bytes 12296 | tf_op jit(solution)/shard_map/ppermute | solution.py:344
  30.1 8.6 %collective-permute-start.9 = (f32[8,128]{1,0:T(8,128)S(1)}, f32[8,128]{1,0:T(8,128)S(1)}, u32[]{:S(2)}, u32[]{:S(2)}) collective-permute-start(f32[8,128]{1,0:T(8,128)S(1)} %merge.1.rest_2_), channel_id=1, source_target_pairs={{0,1},{1,0},{2,3},{3,2},{16,17},{17,16},{18,19},{19,18},{4,5},{5,4... | collective-permute-start | bytes 12296 | tf_op jit(solution)/shard_map/ppermute | solution.py:344
  30.4 8.3 %collective-permute-start.11 = (f32[8,128]{1,0:T(8,128)S(1)}, f32[8,128]{1,0:T(8,128)S(1)}, u32[]{:S(2)}, u32[]{:S(2)}) collective-permute-start(f32[8,128]{1,0:T(8,128)S(1)} %score.5.rest_1_.rest_2_), channel_id=1, source_target_pairs={{0,16},{1,17},{2,18},{3,19},{16,0},{17,1},{18,2},{19,3},{4,20},{5,... | collective-permute-start | bytes 12296 | tf_op jit(solution)/shard_map/ppermute | solution.py:344
  32.4 6.3 %collective-permute-start.13 = (f32[8,128]{1,0:T(8,128)S(1)}, f32[8,128]{1,0:T(8,128)S(1)}, u32[]{:S(2)}, u32[]{:S(2)}) collective-permute-start(f32[8,128]{1,0:T(8,128)S(1)} %score.6.rest_1_), channel_id=1, source_target_pairs={{0,18},{1,19},{2,16},{3,17},{16,2},{17,3},{18,0},{19,1},{4,22},{5,... | collective-permute-start | bytes 12296 | tf_op jit(solution)/shard_map/ppermute | solution.py:344
  33.5 5.2 %collective-permute-start.12 = (f32[8,128]{1,0:T(8,128)S(1)}, f32[8,128]{1,0:T(8,128)S(1)}, u32[]{:S(2)}, u32[]{:S(2)}) collective-permute-start(f32[8,128]{1,0:T(8,128)S(1)} %score.7.rest_3_), channel_id=1, source_target_pairs={{0,2},{1,3},{2,0},{3,1},{16,18},{17,19},{18,16},{19,17},{4,6},{5,7... | collective-permute-start | bytes 12296 | tf_op jit(solution)/shard_map/ppermute | solution.py:344
  35.6 3.1 %copy-start.5 = (s32[1,512,8]{1,2,0:T(8,128)S(1)}, s32[1,512,8]{1,2,0:T(8,128)}, u32[]{:S(2)}) copy-start(s32[1,512,8]{1,2,0:T(8,128)} %param.9) | copy-start | bytes 49156

commit v23 on v20

--- a/solution.py
+++ b/solution.py
@@ -18,6 +18,7 @@
 
 LANES = 128
 TILE = 16
+PARTS = 4
 VMEM_BYTES = 32 * 1024 * 1024
 F32 = jnp.float32
 BF16 = jnp.bfloat16
@@ -44,17 +45,22 @@
 
 
 def start_grads(grads_hbm, held, sems):
-    half = held.shape[2]
+    tokens, half = held.shape[1:]
+    step = tokens // PARTS
     mine = own_half()
     copies = []
     for side in range(2):
         column = pl.multiple_of((1 - mine if side else mine) * half, half)
-        copies.append(
-            pltpu.make_async_copy(
-                grads_hbm.at[:, pl.ds(column, half)], held.at[side], sems.at[side]
+        copies.append([])
+        for part in range(PARTS):
+            lines = slice(part * step, (part + 1) * step)
+            copy = pltpu.make_async_copy(
+                grads_hbm.at[lines, pl.ds(column, half)],
+                held.at[side, lines],
+                sems.at[side * PARTS + part],
             )
-        )
-        copies[-1].start()
+            copy.start()
+            copies[side].append(copy)
     return copies
 
 
@@ -70,7 +76,8 @@
     for side in range(2):
         for k in steps:
             chunks[side, k][data_rows:, :] = tiles[k]
-        copies[side].wait()
+        for copy in copies[side]:
+            copy.wait()
         block = jnp.dot(pick, held[side], preferred_element_type=F32).astype(BF16)
         for at, k in enumerate(steps):
             for part in range(half // LANES):
@@ -87,8 +94,8 @@
     tokens = held.shape[1]
     me = ep_index()
     small = [
-        pltpu.make_async_copy(ids_hbm, ids_ref, sems.at[2]),
-        pltpu.make_async_copy(weight_hbm, weight_ref, sems.at[3]),
+        pltpu.make_async_copy(ids_hbm, ids_ref, sems.at[2 * PARTS]),
+        pltpu.make_async_copy(weight_hbm, weight_ref, sems.at[2 * PARTS + 1]),
     ]
     for copy in small:
         copy.start()
@@ -145,7 +152,7 @@
     step = min(half, 4 * LANES)
     parts = [slice(column, column + step) for column in range(0, half, step)]
     loads = [
-        pltpu.make_async_copy(master_hbm.at[:, part], master_ref.at[:, part], sems.at[2 + at])
+        pltpu.make_async_copy(master_hbm.at[:, part], master_ref.at[:, part], sems.at[2 * PARTS + at])
         for at, part in enumerate(parts)
     ]
     for load in loads:
@@ -374,7 +381,7 @@
             pltpu.VMEM((top, tokens), jnp.int32),
             pltpu.VMEM((top, tokens), BF16),
             held,
-            pltpu.SemaphoreType.DMA((4,)),
+            pltpu.SemaphoreType.DMA((2 * PARTS + 2,)),
         ],
         compiler_params=params(),
         cost_estimate=cost(2 * slots * tokens * width, 2 * (tokens + slots) * width),
@@ -398,7 +405,7 @@
         scratch_shapes=[
             held,
             pltpu.VMEM((hid, half), F32),
-            pltpu.SemaphoreType.DMA((2 + half // min(half, 4 * LANES),)),
+            pltpu.SemaphoreType.DMA((2 * PARTS + half // min(half, 4 * LANES),)),
         ],
         compiler_params=params(),
         cost_estimate=cost(

time: 39 us -> 39 us (level)
  no operation moved by 1% of the time
where the time goes in v23:
time: 39 us; the launch traced here: 38.8 us
  starting transfers between devices  23.2 us (59%)
  Pallas kernels  11.1 us (28%)
  waiting for transfers between devices  3.79 us (10%)
  between operations  0.75 us (2%)
    ppermute x14, starting transfers between devices, moved(): return lax.ppermute(array, ('pair', 'ep'), pairs)  23.2 us
    ppermute x14, waiting for transfers between devices, moved(): return lax.ppermute(array, ('pair', 'ep'), pairs)  3.79 us
    pallas_call x1, Pallas kernels, local(): pl.pallas_call(functools.partial(later_kernel, last_items, late, cap), ou...  3.39 us
    pallas_call x1, Pallas kernels, local(): pl.pallas_call(functools.partial(update_kernel, added, cap), out_shape=ja...  3.07 us
    pallas_call x1, Pallas kernels, local(): pl.pallas_call(functools.partial(route_kernel, first_items, first, group,...  2 us
    pallas_call x1, Pallas kernels, local(): pl.pallas_call(functools.partial(sum_kernel, summed, group, cap), out_sha...  1.12 us
    pallas_call x1, Pallas kernels, local(): pl.pallas_call(functools.partial(combine_kernel, [(k, len(arrays)) for k,...  0.87 us
  transfers between devices with their start and end apart: 14, of which 4 were waited for; matrix products, arithmetic and copies ran while one was open for 0% of the time, Pallas kernels for 26%

profile of v23, /device:TPU:0, one launch (start us, length us, event | category | flops | bytes accessed | tf_op | source)
XLA Modules:
  0.0 38.8 jit_solution(17612709164443011618)
XLA Ops:
  0.6 3.0 %collective-permute-start = (bf16[768,256]{1,0:T(8,128)(2,1)}, bf16[768,256]{1,0:T(8,128)(2,1)S(1)}, u32[]{:S(2)}, u32[]{:S(2)}) collective-permute-start(bf16[768,256]{1,0:T(8,128)(2,1)} %bitcast.17), channel_id=1, source_target_pairs={{0,16},{1,17},{2,18},{3,19},{16,0},{17,1},{18,2},{19,3},{4,20},{5,... | collective-permute-start | bytes 1179656 | tf_op jit(solution)/shard_map/ppermute | solution.py:347
  3.7 2.0 %route.1 = (f32[16,512]{1,0:T(8,128)S(1)}, bf16[4,16,128]{2,1,0:T(8,128)(2,1)S(1)}, bf16[528,128]{1,0:T(8,128)(2,1)S(1)}, bf16[528,128]{1,0:T(8,128)(2,1)S(1)}, ...) custom-call(s32[8,512]{1,0:T(8,128)} %bitcast.23, bf16[8,512]{1,0:T(8,128)(2,1)} %bitcast.29, ...), custom_call_target="tpu_custom_call" | custom-call | flops 536870912 | bytes 3145728 | tf_op jit(solution)/shard_map/route/pallas_call | solution.py:371
  5.7 3.7 %collective-permute-start.1 = (bf16[528,128]{1,0:T(8,128)(2,1)S(1)}, bf16[528,128]{1,0:T(8,128)(2,1)S(1)}, u32[]{:S(2)}, u32[]{:S(2)}) collective-permute-start(bf16[528,128]{1,0:T(8,128)(2,1)S(1)} %get-tuple-element.13), channel_id=1, source_target_pairs={{0,3},{1,2},{2,1},{3,0},{16,19},{17,18},{18,17},{19,16},{4,7},{5,6... | collective-permute-start | bytes 405512 | tf_op jit(solution)/shard_map/ppermute | solution.py:347
  9.4 0.8 %collective-permute-start.3 = (bf16[528,128]{1,0:T(8,128)(2,1)S(1)}, bf16[528,128]{1,0:T(8,128)(2,1)S(1)}, u32[]{:S(2)}, u32[]{:S(2)}) collective-permute-start(bf16[528,128]{1,0:T(8,128)(2,1)S(1)} %get-tuple-element.15), channel_id=1, source_target_pairs={{0,19},{1,18},{2,17},{3,16},{16,3},{17,2},{18,1},{19,0},{4,23},{5,... | collective-permute-start | bytes 405512 | tf_op jit(solution)/shard_map/ppermute | solution.py:347
  10.2 1.4 %collective-permute-start.4 = (bf16[528,128]{1,0:T(8,128)(2,1)S(1)}, bf16[528,128]{1,0:T(8,128)(2,1)S(1)}, u32[]{:S(2)}, u32[]{:S(2)}) collective-permute-start(bf16[528,128]{1,0:T(8,128)(2,1)S(1)} %get-tuple-element.16), channel_id=1, source_target_pairs={{0,17},{1,16},{2,19},{3,18},{16,1},{17,0},{18,3},{19,2},{4,21},{5,... | collective-permute-start | bytes 405512 | tf_op jit(solution)/shard_map/ppermute | solution.py:347
  11.6 1.4 %collective-permute-done.other_ref = bf16[768,256]{1,0:T(8,128)(2,1)S(1)} collective-permute-done((bf16[768,256]{1,0:T(8,128)(2,1)}, bf16[768,256]{1,0:T(8,128)(2,1)S(1)}, u32[]{:S(2)}, u32[]{:S(2)}) %collective-permute-start) | collective-permute-done | bytes 393248 | tf_op jit(solution)/shard_map/ppermute | solution.py:347
  13.0 3.4 %later.1 = (f32[512,1024]{1,0:T(8,128)S(1)}, bf16[528,128]{1,0:T(8,128)(2,1)S(1)}, bf16[528,128]{1,0:T(8,128)(2,1)S(1)}, bf16[528,128]{1,0:T(8,128)(2,1)S(1)}, bf16[528,128]{1,0:T(8,128)(2,1)S(1)}) custom-call(f32[16,512]{1,0:T(8,128)S(1)} %get-tuple-element.17.slots_ref, bf16[4,16,128]{2,1,0:T(8,128)(2,1)S(1)} %get-tuple-element.18.tiles_ref, ...), custom_call_target="tpu_custom_call" | custom-call | flops 1342177280 | bytes 3145728 | tf_op jit(solution)/shard_map/later/pallas_call | solution.py:397
  16.4 1.8 %collective-permute-start.7 = (bf16[528,128]{1,0:T(8,128)(2,1)S(1)}, bf16[528,128]{1,0:T(8,128)(2,1)S(1)}, u32[]{:S(2)}, u32[]{:S(2)}) collective-permute-start(bf16[528,128]{1,0:T(8,128)(2,1)S(1)} %get-tuple-element.23), channel_id=1, source_target_pairs={{0,16},{1,17},{2,18},{3,19},{16,0},{17,1},{18,2},{19,3},{4,20},{5,... | collective-permute-start | bytes 405512 | tf_op jit(solution)/shard_map/ppermute | solution.py:347
  18.2 3.2 %collective-permute-start.5 = (bf16[528,128]{1,0:T(8,128)(2,1)S(1)}, bf16[528,128]{1,0:T(8,128)(2,1)S(1)}, u32[]{:S(2)}, u32[]{:S(2)}) collective-permute-start(bf16[528,128]{1,0:T(8,128)(2,1)S(1)} %get-tuple-element.21), channel_id=1, source_target_pairs={{0,18},{1,19},{2,16},{3,17},{16,2},{17,3},{18,0},{19,1},{4,22},{5,... | collective-permute-start | bytes 405512 | tf_op jit(solution)/shard_map/ppermute | solution.py:347
  21.4 0.1 collective-permute-start.6
  21.5 1.0 %collective-permute-done.4.rest_3_ = bf16[528,128]{1,0:T(8,128)(2,1)S(1)} collective-permute-done((bf16[528,128]{1,0:T(8,128)(2,1)S(1)}, bf16[528,128]{1,0:T(8,128)(2,1)S(1)}, u32[]{:S(2)}, u32[]{:S(2)}) %collective-permute-start.4) | collective-permute-done | bytes 135200 | tf_op jit(solution)/shard_map/ppermute | solution.py:347
  22.5 0.2 score.4.rest_5_.own_ref
  22.7 1.6 %collective-permute-start.8 = (f32[8,128]{1,0:T(8,128)S(1)}, f32[8,128]{1,0:T(8,128)S(1)}, u32[]{:S(2)}, u32[]{:S(2)}) collective-permute-start(f32[8,128]{1,0:T(8,128)S(1)} %score.4.rest_5_.own_ref), channel_id=1, source_target_pairs={{0,16},{1,17},{2,18},{3,19},{16,0},{17,1},{18,2},{19,3},{4,20},{5,... | collective-permute-start | bytes 12296 | tf_op jit(solution)/shard_map/ppermute | solution.py:347
  24.3 1.1 %sum.1._.grad_ref = f32[768,1024]{1,0:T(8,128)S(1)} custom-call(bf16[768,256]{1,0:T(8,128)(2,1)S(1)} %bitcast.19, bf16[768,256]{1,0:T(8,128)(2,1)S(1)} %collective-permute-done.other_ref, bf16[528,128]{1,0:T(8,128)(2,1)S(1)} %collective-permute-done.1.rest_0_, bf16[528,128]{1,0:T(8,128)(2,1)S(1)} %collective-permute-done.2.rest_1_, ...), custom_call_target="tpu_custom_call" | custom-call | flops 805306368 | bytes 3145728 | tf_op jit(solution)/shard_map/sum/pallas_call | solution.py:443
  25.5 0.9 %collective-permute-done.8.other_ref = f32[8,128]{1,0:T(8,128)S(1)} collective-permute-done((f32[8,128]{1,0:T(8,128)S(1)}, f32[8,128]{1,0:T(8,128)S(1)}, u32[]{:S(2)}, u32[]{:S(2)}) %collective-permute-start.8) | collective-permute-done | bytes 4128 | tf_op jit(solution)/shard_map/ppermute | solution.py:347
  26.5 2.5 %collective-permute-start.10 = (f32[8,128]{1,0:T(8,128)S(1)}, f32[8,128]{1,0:T(8,128)S(1)}, u32[]{:S(2)}, u32[]{:S(2)}) collective-permute-start(f32[8,128]{1,0:T(8,128)S(1)} %merge.1.rest_2_), channel_id=1, source_target_pairs={{0,3},{1,2},{2,1},{3,0},{16,19},{17,18},{18,17},{19,16},{4,7},{5,6... | collective-permute-start | bytes 12296 | tf_op jit(solution)/shard_map/ppermute | solution.py:347
  29.0 0.2 collective-permute-start.9
  29.2 0.1 score.5.rest_1_.rest_2_
  29.4 1.5 %collective-permute-start.11 = (f32[8,128]{1,0:T(8,128)S(1)}, f32[8,128]{1,0:T(8,128)S(1)}, u32[]{:S(2)}, u32[]{:S(2)}) collective-permute-start(f32[8,128]{1,0:T(8,128)S(1)} %score.5.rest_1_.rest_2_), channel_id=1, source_target_pairs={{0,16},{1,17},{2,18},{3,19},{16,0},{17,1},{18,2},{19,3},{4,20},{5,... | collective-permute-start | bytes 12296 | tf_op jit(solution)/shard_map/ppermute | solution.py:347
  30.9 0.4 %collective-permute-done.5.rest_0_ = bf16[528,128]{1,0:T(8,128)(2,1)S(1)} collective-permute-done((bf16[528,128]{1,0:T(8,128)(2,1)S(1)}, bf16[528,128]{1,0:T(8,128)(2,1)S(1)}, u32[]{:S(2)}, u32[]{:S(2)}) %collective-permute-start.5) | collective-permute-done | bytes 135200 | tf_op jit(solution)/shard_map/ppermute | solution.py:347
  31.4 1.3 %collective-permute-start.13 = (f32[8,128]{1,0:T(8,128)S(1)}, f32[8,128]{1,0:T(8,128)S(1)}, u32[]{:S(2)}, u32[]{:S(2)}) collective-permute-start(f32[8,128]{1,0:T(8,128)S(1)} %score.6.rest_1_), channel_id=1, source_target_pairs={{0,18},{1,19},{2,16},{3,17},{16,2},{17,3},{18,0},{19,1},{4,22},{5,... | collective-permute-start | bytes 12296 | tf_op jit(solution)/shard_map/ppermute | solution.py:347
  32.8 2.0 %collective-permute-start.12 = (f32[8,128]{1,0:T(8,128)S(1)}, f32[8,128]{1,0:T(8,128)S(1)}, u32[]{:S(2)}, u32[]{:S(2)}) collective-permute-start(f32[8,128]{1,0:T(8,128)S(1)} %score.7.rest_3_), channel_id=1, source_target_pairs={{0,2},{1,3},{2,0},{3,1},{16,18},{17,19},{18,16},{19,17},{4,6},{5,7... | collective-permute-start | bytes 12296 | tf_op jit(solution)/shard_map/ppermute | solution.py:347
  34.8 3.1 %update.1 = f32[768,1024]{1,0:T(8,128)} custom-call(bf16[768,256]{1,0:T(8,128)(2,1)S(1)} %bitcast.20, bf16[768,256]{1,0:T(8,128)(2,1)S(1)} %collective-permute-done.other_ref, f32[768,1024]{1,0:T(8,128)S(1)} %sum.1._.grad_ref, f32[768,1024]{1,0:T(8,128)S(1)} %bitcast.16, bf16[768,1024]{1,0:T(8,128)(2,1)S(1)} %bitcast.21, bf16[768,1024]{1,0:T(8,128)(2,1)S(1)} %bitcast.22, ...), custom_call_target="tpu_custom_call" | custom-call | flops 402653184 | bytes 12582912 | tf_op jit(solution)/shard_map/update/pallas_call | solution.py:472
  38.0 0.9 %combine.1 = f32[8,512]{1,0:T(8,128)} custom-call(s32[8,512]{1,0:T(8,128)S(1)} %bitcast.24, f32[16,512]{1,0:T(8,128)S(1)} %get-tuple-element.17.slots_ref, f32[8,128]{1,0:T(8,128)S(1)} %collective-permute-done.9.rest_0_, f32[8,128]{1,0:T(8,128)S(1)} %collective-permute-done.10.rest_1_, f32[8,128]{1,0:T(8,128)S(1)} %score.5.rest_1_.rest_2_, ...), custom_call_target="tpu_custom_call" | custom-call | flops 524288 | bytes 32768 | tf_op jit(solution)/shard_map/combine/pallas_call | solution.py:498
  (24 shorter events, 0.4 us)
Async XLA Ops:
  0.6 12.4 %copy-start.1 = (bf16[1,1,768,256]{3,2,1,0:T(8,128)(2,1)S(1)}, bf16[1,1,768,256]{3,2,1,0:T(8,128)(2,1)}, u32[]{:S(2)}) copy-start(bf16[1,1,768,256]{3,2,1,0:T(8,128)(2,1)} %param.10) | copy-start | bytes 1179652
  0.6 12.4 %collective-permute-start = (bf16[768,256]{1,0:T(8,128)(2,1)}, bf16[768,256]{1,0:T(8,128)(2,1)S(1)}, u32[]{:S(2)}, u32[]{:S(2)}) collective-permute-start(bf16[768,256]{1,0:T(8,128)(2,1)} %bitcast.17), channel_id=1, source_target_pairs={{0,16},{1,17},{2,18},{3,19},{16,0},{17,1},{18,2},{19,3},{4,20},{5,... | collective-permute-start | bytes 1179656 | tf_op jit(solution)/shard_map/ppermute | solution.py:347
  5.7 12.5 %collective-permute-start.1 = (bf16[528,128]{1,0:T(8,128)(2,1)S(1)}, bf16[528,128]{1,0:T(8,128)(2,1)S(1)}, u32[]{:S(2)}, u32[]{:S(2)}) collective-permute-start(bf16[528,128]{1,0:T(8,128)(2,1)S(1)} %get-tuple-element.13), channel_id=1, source_target_pairs={{0,3},{1,2},{2,1},{3,0},{16,19},{17,18},{18,17},{19,16},{4,7},{5,6... | collective-permute-start | bytes 405512 | tf_op jit(solution)/shard_map/ppermute | solution.py:347
  9.4 12.0 %collective-permute-start.2 = (bf16[528,128]{1,0:T(8,128)(2,1)S(1)}, bf16[528,128]{1,0:T(8,128)(2,1)S(1)}, u32[]{:S(2)}, u32[]{:S(2)}) collective-permute-start(bf16[528,128]{1,0:T(8,128)(2,1)S(1)} %get-tuple-element.14), channel_id=1, source_target_pairs={{0,1},{1,0},{2,3},{3,2},{16,17},{17,16},{18,19},{19,18},{4,5},{5,4... | collective-permute-start | bytes 405512 | tf_op jit(solution)/shard_map/ppermute | solution.py:347
  9.4 12.2 %collective-permute-start.3 = (bf16[528,128]{1,0:T(8,128)(2,1)S(1)}, bf16[528,128]{1,0:T(8,128)(2,1)S(1)}, u32[]{:S(2)}, u32[]{:S(2)}) collective-permute-start(bf16[528,128]{1,0:T(8,128)(2,1)S(1)} %get-tuple-element.15), channel_id=1, source_target_pairs={{0,19},{1,18},{2,17},{3,16},{16,3},{17,2},{18,1},{19,0},{4,23},{5,... | collective-permute-start | bytes 405512 | tf_op jit(solution)/shard_map/ppermute | solution.py:347
  10.2 12.3 %collective-permute-start.4 = (bf16[528,128]{1,0:T(8,128)(2,1)S(1)}, bf16[528,128]{1,0:T(8,128)(2,1)S(1)}, u32[]{:S(2)}, u32[]{:S(2)}) collective-permute-start(bf16[528,128]{1,0:T(8,128)(2,1)S(1)} %get-tuple-element.16), channel_id=1, source_target_pairs={{0,17},{1,16},{2,19},{3,18},{16,1},{17,0},{18,3},{19,2},{4,21},{5,... | collective-permute-start | bytes 405512 | tf_op jit(solution)/shard_map/ppermute | solution.py:347
  16.4 12.8 %collective-permute-start.7 = (bf16[528,128]{1,0:T(8,128)(2,1)S(1)}, bf16[528,128]{1,0:T(8,128)(2,1)S(1)}, u32[]{:S(2)}, u32[]{:S(2)}) collective-permute-start(bf16[528,128]{1,0:T(8,128)(2,1)S(1)} %get-tuple-element.23), channel_id=1, source_target_pairs={{0,16},{1,17},{2,18},{3,19},{16,0},{17,1},{18,2},{19,3},{4,20},{5,... | collective-permute-start | bytes 405512 | tf_op jit(solution)/shard_map/ppermute | solution.py:347
  18.2 13.1 %collective-permute-start.5 = (bf16[528,128]{1,0:T(8,128)(2,1)S(1)}, bf16[528,128]{1,0:T(8,128)(2,1)S(1)}, u32[]{:S(2)}, u32[]{:S(2)}) collective-permute-start(bf16[528,128]{1,0:T(8,128)(2,1)S(1)} %get-tuple-element.21), channel_id=1, source_target_pairs={{0,18},{1,19},{2,16},{3,17},{16,2},{17,3},{18,0},{19,1},{4,22},{5,... | collective-permute-start | bytes 405512 | tf_op jit(solution)/shard_map/ppermute | solution.py:347
  21.4 11.3 %collective-permute-start.6 = (bf16[528,128]{1,0:T(8,128)(2,1)S(1)}, bf16[528,128]{1,0:T(8,128)(2,1)S(1)}, u32[]{:S(2)}, u32[]{:S(2)}) collective-permute-start(bf16[528,128]{1,0:T(8,128)(2,1)S(1)} %get-tuple-element.22), channel_id=1, source_target_pairs={{0,2},{1,3},{2,0},{3,1},{16,18},{17,19},{18,16},{19,17},{4,6},{5,7... | collective-permute-start | bytes 405512 | tf_op jit(solution)/shard_map/ppermute | solution.py:347
  22.7 3.7 %collective-permute-start.8 = (f32[8,128]{1,0:T(8,128)S(1)}, f32[8,128]{1,0:T(8,128)S(1)}, u32[]{:S(2)}, u32[]{:S(2)}) collective-permute-start(f32[8,128]{1,0:T(8,128)S(1)} %score.4.rest_5_.own_ref), channel_id=1, source_target_pairs={{0,16},{1,17},{2,18},{3,19},{16,0},{17,1},{18,2},{19,3},{4,20},{5,... | collective-permute-start | bytes 12296 | tf_op jit(solution)/shard_map/ppermute | solution.py:347
  26.5 11.5 %collective-permute-start.10 = (f32[8,128]{1,0:T(8,128)S(1)}, f32[8,128]{1,0:T(8,128)S(1)}, u32[]{:S(2)}, u32[]{:S(2)}) collective-permute-start(f32[8,128]{1,0:T(8,128)S(1)} %merge.1.rest_2_), channel_id=1, source_target_pairs={{0,3},{1,2},{2,1},{3,0},{16,19},{17,18},{18,17},{19,16},{4,7},{5,6... | collective-permute-start | bytes 12296 | tf_op jit(solution)/shard_map/ppermute | solution.py:347
  29.0 8.9 %collective-permute-start.9 = (f32[8,128]{1,0:T(8,128)S(1)}, f32[8,128]{1,0:T(8,128)S(1)}, u32[]{:S(2)}, u32[]{:S(2)}) collective-permute-start(f32[8,128]{1,0:T(8,128)S(1)} %merge.1.rest_2_), channel_id=1, source_target_pairs={{0,1},{1,0},{2,3},{3,2},{16,17},{17,16},{18,19},{19,18},{4,5},{5,4... | collective-permute-start | bytes 12296 | tf_op jit(solution)/shard_map/ppermute | solution.py:347
  29.2 5.6 %copy-start.2 = (bf16[1,1,768,1024]{3,2,1,0:T(8,128)(2,1)S(1)}, bf16[1,1,768,1024]{3,2,1,0:T(8,128)(2,1)}, u32[]{:S(2)}) copy-start(bf16[1,1,768,1024]{3,2,1,0:T(8,128)(2,1)} %param.12) | copy-start | bytes 4718596
  29.2 5.6 %copy-start.3 = (bf16[1,1,768,1024]{3,2,1,0:T(8,128)(2,1)S(1)}, bf16[1,1,768,1024]{3,2,1,0:T(8,128)(2,1)}, u32[]{:S(2)}) copy-start(bf16[1,1,768,1024]{3,2,1,0:T(8,128)(2,1)} %param.13) | copy-start | bytes 4718596
  29.4 5.5 %copy-start = (f32[1,1,768,1024]{3,2,1,0:T(8,128)S(1)}, f32[1,1,768,1024]{3,2,1,0:T(8,128)}, u32[]{:S(2)}) copy-start(f32[1,1,768,1024]{3,2,1,0:T(8,128)} %param.11) | copy-start | bytes 9437188
  29.4 8.6 %collective-permute-start.11 = (f32[8,128]{1,0:T(8,128)S(1)}, f32[8,128]{1,0:T(8,128)S(1)}, u32[]{:S(2)}, u32[]{:S(2)}) collective-permute-start(f32[8,128]{1,0:T(8,128)S(1)} %score.5.rest_1_.rest_2_), channel_id=1, source_target_pairs={{0,16},{1,17},{2,18},{3,19},{16,0},{17,1},{18,2},{19,3},{4,20},{5,... | collective-permute-start | bytes 12296 | tf_op jit(solution)/shard_map/ppermute | solution.py:347
  31.4 6.6 %collective-permute-start.13 = (f32[8,128]{1,0:T(8,128)S(1)}, f32[8,128]{1,0:T(8,128)S(1)}, u32[]{:S(2)}, u32[]{:S(2)}) collective-permute-start(f32[8,128]{1,0:T(8,128)S(1)} %score.6.rest_1_), channel_id=1, source_target_pairs={{0,18},{1,19},{2,16},{3,17},{16,2},{17,3},{18,0},{19,1},{4,22},{5,... | collective-permute-start | bytes 12296 | tf_op jit(solution)/shard_map/ppermute | solution.py:347
  32.8 5.1 %collective-permute-start.12 = (f32[8,128]{1,0:T(8,128)S(1)}, f32[8,128]{1,0:T(8,128)S(1)}, u32[]{:S(2)}, u32[]{:S(2)}) collective-permute-start(f32[8,128]{1,0:T(8,128)S(1)} %score.7.rest_3_), channel_id=1, source_target_pairs={{0,2},{1,3},{2,0},{3,1},{16,18},{17,19},{18,16},{19,17},{4,6},{5,7... | collective-permute-start | bytes 12296 | tf_op jit(solution)/shard_map/ppermute | solution.py:347
  34.8 3.1 %copy-start.4 = (s32[1,512,8]{1,2,0:T(8,128)S(1)}, s32[1,512,8]{1,2,0:T(8,128)}, u32[]{:S(2)}) copy-start(s32[1,512,8]{1,2,0:T(8,128)} %param.9) | copy-start | bytes 49156

commit v24 on v20

--- a/solution.py
+++ b/solution.py
@@ -63,14 +63,15 @@
     return jnp.where(place == slots[k : k + 1, :], 1.0, 0.0).astype(BF16)
 
 
-def fill_chunks(steps, cap, picks, held, copies, tiles, chunks):
+def fill_chunks(steps, cap, picks, held, copies, tiles, chunks, ready=False):
     half = held.shape[2]
     data_rows = half // LANES * cap
     pick = jnp.concatenate([picks[k] for k in steps], axis=0)
     for side in range(2):
+        if side > 0 or not ready:
+            copies[side].wait()
         for k in steps:
             chunks[side, k][data_rows:, :] = tiles[k]
-        copies[side].wait()
         block = jnp.dot(pick, held[side], preferred_element_type=F32).astype(BF16)
         for at, k in enumerate(steps):
             for part in range(half // LANES):
@@ -111,6 +112,7 @@
     before = jnp.dot(member.astype(BF16), ahead, preferred_element_type=F32)
     slots = jnp.where(member > 0.5, before, -1.0)
     slots_ref[...] = slots
+    copies[0].wait()
     picks = [pick_rows(slots, k, cap) for k in range(group)]
     base = me * cap
     tile_row = lax.broadcasted_iota(jnp.int32, (TILE, LANES), 0)
@@ -132,7 +134,7 @@
         line = jnp.concatenate([line] * (LANES // cap), axis=1)
         tiles.append(jnp.where(kept, line, 0.0).astype(BF16))
         tiles_ref[k] = tiles[k]
-    fill_chunks(steps, cap, picks, held, copies, tiles, chunks)
+    fill_chunks(steps, cap, picks, held, copies, tiles, chunks, ready=True)
 
 
 def later_kernel(

time: 39 us -> 39 us (level)
  no operation moved by 1% of the time
where the time goes in v24:
time: 39 us; the launch traced here: 38.8 us
  starting transfers between devices  23.2 us (59%)
  Pallas kernels  11 us (28%)
  waiting for transfers between devices  3.82 us (10%)
  between operations  0.75 us (2%)
    ppermute x14, starting transfers between devices, moved(): return lax.ppermute(array, ('pair', 'ep'), pairs)  23.2 us
    ppermute x14, waiting for transfers between devices, moved(): return lax.ppermute(array, ('pair', 'ep'), pairs)  3.82 us
    pallas_call x1, Pallas kernels, local(): pl.pallas_call(functools.partial(later_kernel, last_items, late, cap), ou...  3.33 us
    pallas_call x1, Pallas kernels, local(): pl.pallas_call(functools.partial(update_kernel, added, cap), out_shape=ja...  3.08 us
    pallas_call x1, Pallas kernels, local(): pl.pallas_call(functools.partial(route_kernel, first_items, first, group,...  1.98 us
    pallas_call x1, Pallas kernels, local(): pl.pallas_call(functools.partial(sum_kernel, summed, group, cap), out_sha...  1.12 us
    pallas_call x1, Pallas kernels, local(): pl.pallas_call(functools.partial(combine_kernel, [(k, len(arrays)) for k,...  0.87 us
  transfers between devices with their start and end apart: 14, of which 4 were waited for; matrix products, arithmetic and copies ran while one was open for 0% of the time, Pallas kernels for 26%

profile of v24, /device:TPU:0, one launch (start us, length us, event | category | flops | bytes accessed | tf_op | source)
XLA Modules:
  0.0 38.8 jit_solution(2523937711899180415)
XLA Ops:
  0.6 3.0 %collective-permute-start = (bf16[768,256]{1,0:T(8,128)(2,1)}, bf16[768,256]{1,0:T(8,128)(2,1)S(1)}, u32[]{:S(2)}, u32[]{:S(2)}) collective-permute-start(bf16[768,256]{1,0:T(8,128)(2,1)} %bitcast.17), channel_id=1, source_target_pairs={{0,16},{1,17},{2,18},{3,19},{16,0},{17,1},{18,2},{19,3},{4,20},{5,... | collective-permute-start | bytes 1179656 | tf_op jit(solution)/shard_map/ppermute | solution.py:342
  3.7 2.0 %route.1 = (f32[16,512]{1,0:T(8,128)S(1)}, bf16[4,16,128]{2,1,0:T(8,128)(2,1)S(1)}, bf16[528,128]{1,0:T(8,128)(2,1)S(1)}, bf16[528,128]{1,0:T(8,128)(2,1)S(1)}, ...) custom-call(s32[8,512]{1,0:T(8,128)} %bitcast.23, bf16[8,512]{1,0:T(8,128)(2,1)} %bitcast.29, ...), custom_call_target="tpu_custom_call" | custom-call | flops 536870912 | bytes 3145728 | tf_op jit(solution)/shard_map/route/pallas_call | solution.py:366
  5.7 3.7 %collective-permute-start.1 = (bf16[528,128]{1,0:T(8,128)(2,1)S(1)}, bf16[528,128]{1,0:T(8,128)(2,1)S(1)}, u32[]{:S(2)}, u32[]{:S(2)}) collective-permute-start(bf16[528,128]{1,0:T(8,128)(2,1)S(1)} %get-tuple-element.13), channel_id=1, source_target_pairs={{0,3},{1,2},{2,1},{3,0},{16,19},{17,18},{18,17},{19,16},{4,7},{5,6... | collective-permute-start | bytes 405512 | tf_op jit(solution)/shard_map/ppermute | solution.py:342
  9.3 0.8 %collective-permute-start.3 = (bf16[528,128]{1,0:T(8,128)(2,1)S(1)}, bf16[528,128]{1,0:T(8,128)(2,1)S(1)}, u32[]{:S(2)}, u32[]{:S(2)}) collective-permute-start(bf16[528,128]{1,0:T(8,128)(2,1)S(1)} %get-tuple-element.15), channel_id=1, source_target_pairs={{0,19},{1,18},{2,17},{3,16},{16,3},{17,2},{18,1},{19,0},{4,23},{5,... | collective-permute-start | bytes 405512 | tf_op jit(solution)/shard_map/ppermute | solution.py:342
  10.2 1.4 %collective-permute-start.4 = (bf16[528,128]{1,0:T(8,128)(2,1)S(1)}, bf16[528,128]{1,0:T(8,128)(2,1)S(1)}, u32[]{:S(2)}, u32[]{:S(2)}) collective-permute-start(bf16[528,128]{1,0:T(8,128)(2,1)S(1)} %get-tuple-element.16), channel_id=1, source_target_pairs={{0,17},{1,16},{2,19},{3,18},{16,1},{17,0},{18,3},{19,2},{4,21},{5,... | collective-permute-start | bytes 405512 | tf_op jit(solution)/shard_map/ppermute | solution.py:342
  11.6 1.4 %collective-permute-done.other_ref = bf16[768,256]{1,0:T(8,128)(2,1)S(1)} collective-permute-done((bf16[768,256]{1,0:T(8,128)(2,1)}, bf16[768,256]{1,0:T(8,128)(2,1)S(1)}, u32[]{:S(2)}, u32[]{:S(2)}) %collective-permute-start) | collective-permute-done | bytes 393248 | tf_op jit(solution)/shard_map/ppermute | solution.py:342
  13.0 3.3 %later.1 = (f32[512,1024]{1,0:T(8,128)S(1)}, bf16[528,128]{1,0:T(8,128)(2,1)S(1)}, bf16[528,128]{1,0:T(8,128)(2,1)S(1)}, bf16[528,128]{1,0:T(8,128)(2,1)S(1)}, bf16[528,128]{1,0:T(8,128)(2,1)S(1)}) custom-call(f32[16,512]{1,0:T(8,128)S(1)} %get-tuple-element.17.slots_ref, bf16[4,16,128]{2,1,0:T(8,128)(2,1)S(1)} %get-tuple-element.18.tiles_ref, ...), custom_call_target="tpu_custom_call" | custom-call | flops 1342177280 | bytes 3145728 | tf_op jit(solution)/shard_map/later/pallas_call | solution.py:392
  16.3 1.8 %collective-permute-start.7 = (bf16[528,128]{1,0:T(8,128)(2,1)S(1)}, bf16[528,128]{1,0:T(8,128)(2,1)S(1)}, u32[]{:S(2)}, u32[]{:S(2)}) collective-permute-start(bf16[528,128]{1,0:T(8,128)(2,1)S(1)} %get-tuple-element.23), channel_id=1, source_target_pairs={{0,16},{1,17},{2,18},{3,19},{16,0},{17,1},{18,2},{19,3},{4,20},{5,... | collective-permute-start | bytes 405512 | tf_op jit(solution)/shard_map/ppermute | solution.py:342
  18.1 3.2 %collective-permute-start.5 = (bf16[528,128]{1,0:T(8,128)(2,1)S(1)}, bf16[528,128]{1,0:T(8,128)(2,1)S(1)}, u32[]{:S(2)}, u32[]{:S(2)}) collective-permute-start(bf16[528,128]{1,0:T(8,128)(2,1)S(1)} %get-tuple-element.21), channel_id=1, source_target_pairs={{0,18},{1,19},{2,16},{3,17},{16,2},{17,3},{18,0},{19,1},{4,22},{5,... | collective-permute-start | bytes 405512 | tf_op jit(solution)/shard_map/ppermute | solution.py:342
  21.3 0.1 collective-permute-start.6
  21.5 1.0 %collective-permute-done.4.rest_3_ = bf16[528,128]{1,0:T(8,128)(2,1)S(1)} collective-permute-done((bf16[528,128]{1,0:T(8,128)(2,1)S(1)}, bf16[528,128]{1,0:T(8,128)(2,1)S(1)}, u32[]{:S(2)}, u32[]{:S(2)}) %collective-permute-start.4) | collective-permute-done | bytes 135200 | tf_op jit(solution)/shard_map/ppermute | solution.py:342
  22.5 0.2 score.4.rest_5_.own_ref
  22.7 1.6 %collective-permute-start.8 = (f32[8,128]{1,0:T(8,128)S(1)}, f32[8,128]{1,0:T(8,128)S(1)}, u32[]{:S(2)}, u32[]{:S(2)}) collective-permute-start(f32[8,128]{1,0:T(8,128)S(1)} %score.4.rest_5_.own_ref), channel_id=1, source_target_pairs={{0,16},{1,17},{2,18},{3,19},{16,0},{17,1},{18,2},{19,3},{4,20},{5,... | collective-permute-start | bytes 12296 | tf_op jit(solution)/shard_map/ppermute | solution.py:342
  24.3 1.1 %sum.1._.grad_ref = f32[768,1024]{1,0:T(8,128)S(1)} custom-call(bf16[768,256]{1,0:T(8,128)(2,1)S(1)} %bitcast.19, bf16[768,256]{1,0:T(8,128)(2,1)S(1)} %collective-permute-done.other_ref, bf16[528,128]{1,0:T(8,128)(2,1)S(1)} %collective-permute-done.1.rest_0_, bf16[528,128]{1,0:T(8,128)(2,1)S(1)} %collective-permute-done.2.rest_1_, ...), custom_call_target="tpu_custom_call" | custom-call | flops 805306368 | bytes 3145728 | tf_op jit(solution)/shard_map/sum/pallas_call | solution.py:438
  25.4 0.9 %collective-permute-done.8.other_ref = f32[8,128]{1,0:T(8,128)S(1)} collective-permute-done((f32[8,128]{1,0:T(8,128)S(1)}, f32[8,128]{1,0:T(8,128)S(1)}, u32[]{:S(2)}, u32[]{:S(2)}) %collective-permute-start.8) | collective-permute-done | bytes 4128 | tf_op jit(solution)/shard_map/ppermute | solution.py:342
  26.4 2.5 %collective-permute-start.10 = (f32[8,128]{1,0:T(8,128)S(1)}, f32[8,128]{1,0:T(8,128)S(1)}, u32[]{:S(2)}, u32[]{:S(2)}) collective-permute-start(f32[8,128]{1,0:T(8,128)S(1)} %merge.1.rest_2_), channel_id=1, source_target_pairs={{0,3},{1,2},{2,1},{3,0},{16,19},{17,18},{18,17},{19,16},{4,7},{5,6... | collective-permute-start | bytes 12296 | tf_op jit(solution)/shard_map/ppermute | solution.py:342
  28.9 0.2 collective-permute-start.9
  29.2 0.1 score.5.rest_1_.rest_2_
  29.3 1.5 %collective-permute-start.11 = (f32[8,128]{1,0:T(8,128)S(1)}, f32[8,128]{1,0:T(8,128)S(1)}, u32[]{:S(2)}, u32[]{:S(2)}) collective-permute-start(f32[8,128]{1,0:T(8,128)S(1)} %score.5.rest_1_.rest_2_), channel_id=1, source_target_pairs={{0,16},{1,17},{2,18},{3,19},{16,0},{17,1},{18,2},{19,3},{4,20},{5,... | collective-permute-start | bytes 12296 | tf_op jit(solution)/shard_map/ppermute | solution.py:342
  30.8 0.4 %collective-permute-done.5.rest_0_ = bf16[528,128]{1,0:T(8,128)(2,1)S(1)} collective-permute-done((bf16[528,128]{1,0:T(8,128)(2,1)S(1)}, bf16[528,128]{1,0:T(8,128)(2,1)S(1)}, u32[]{:S(2)}, u32[]{:S(2)}) %collective-permute-start.5) | collective-permute-done | bytes 135200 | tf_op jit(solution)/shard_map/ppermute | solution.py:342
  31.3 1.4 %collective-permute-start.13 = (f32[8,128]{1,0:T(8,128)S(1)}, f32[8,128]{1,0:T(8,128)S(1)}, u32[]{:S(2)}, u32[]{:S(2)}) collective-permute-start(f32[8,128]{1,0:T(8,128)S(1)} %score.6.rest_1_), channel_id=1, source_target_pairs={{0,18},{1,19},{2,16},{3,17},{16,2},{17,3},{18,0},{19,1},{4,22},{5,... | collective-permute-start | bytes 12296 | tf_op jit(solution)/shard_map/ppermute | solution.py:342
  32.8 2.0 %collective-permute-start.12 = (f32[8,128]{1,0:T(8,128)S(1)}, f32[8,128]{1,0:T(8,128)S(1)}, u32[]{:S(2)}, u32[]{:S(2)}) collective-permute-start(f32[8,128]{1,0:T(8,128)S(1)} %score.7.rest_3_), channel_id=1, source_target_pairs={{0,2},{1,3},{2,0},{3,1},{16,18},{17,19},{18,16},{19,17},{4,6},{5,7... | collective-permute-start | bytes 12296 | tf_op jit(solution)/shard_map/ppermute | solution.py:342
  34.8 3.1 %update.1 = f32[768,1024]{1,0:T(8,128)} custom-call(bf16[768,256]{1,0:T(8,128)(2,1)S(1)} %bitcast.20, bf16[768,256]{1,0:T(8,128)(2,1)S(1)} %collective-permute-done.other_ref, f32[768,1024]{1,0:T(8,128)S(1)} %sum.1._.grad_ref, f32[768,1024]{1,0:T(8,128)S(1)} %bitcast.16, bf16[768,1024]{1,0:T(8,128)(2,1)S(1)} %bitcast.21, bf16[768,1024]{1,0:T(8,128)(2,1)S(1)} %bitcast.22, ...), custom_call_target="tpu_custom_call" | custom-call | flops 402653184 | bytes 12582912 | tf_op jit(solution)/shard_map/update/pallas_call | solution.py:467
  38.0 0.9 %combine.1 = f32[8,512]{1,0:T(8,128)} custom-call(s32[8,512]{1,0:T(8,128)S(1)} %bitcast.24, f32[16,512]{1,0:T(8,128)S(1)} %get-tuple-element.17.slots_ref, f32[8,128]{1,0:T(8,128)S(1)} %collective-permute-done.9.rest_0_, f32[8,128]{1,0:T(8,128)S(1)} %collective-permute-done.10.rest_1_, f32[8,128]{1,0:T(8,128)S(1)} %score.5.rest_1_.rest_2_, ...), custom_call_target="tpu_custom_call" | custom-call | flops 524288 | bytes 32768 | tf_op jit(solution)/shard_map/combine/pallas_call | solution.py:493
  (24 shorter events, 0.4 us)
Async XLA Ops:
  0.6 12.4 %copy-start.1 = (bf16[1,1,768,256]{3,2,1,0:T(8,128)(2,1)S(1)}, bf16[1,1,768,256]{3,2,1,0:T(8,128)(2,1)}, u32[]{:S(2)}) copy-start(bf16[1,1,768,256]{3,2,1,0:T(8,128)(2,1)} %param.10) | copy-start | bytes 1179652
  0.6 12.4 %collective-permute-start = (bf16[768,256]{1,0:T(8,128)(2,1)}, bf16[768,256]{1,0:T(8,128)(2,1)S(1)}, u32[]{:S(2)}, u32[]{:S(2)}) collective-permute-start(bf16[768,256]{1,0:T(8,128)(2,1)} %bitcast.17), channel_id=1, source_target_pairs={{0,16},{1,17},{2,18},{3,19},{16,0},{17,1},{18,2},{19,3},{4,20},{5,... | collective-permute-start | bytes 1179656 | tf_op jit(solution)/shard_map/ppermute | solution.py:342
  5.7 12.5 %collective-permute-start.1 = (bf16[528,128]{1,0:T(8,128)(2,1)S(1)}, bf16[528,128]{1,0:T(8,128)(2,1)S(1)}, u32[]{:S(2)}, u32[]{:S(2)}) collective-permute-start(bf16[528,128]{1,0:T(8,128)(2,1)S(1)} %get-tuple-element.13), channel_id=1, source_target_pairs={{0,3},{1,2},{2,1},{3,0},{16,19},{17,18},{18,17},{19,16},{4,7},{5,6... | collective-permute-start | bytes 405512 | tf_op jit(solution)/shard_map/ppermute | solution.py:342
  9.3 12.0 %collective-permute-start.2 = (bf16[528,128]{1,0:T(8,128)(2,1)S(1)}, bf16[528,128]{1,0:T(8,128)(2,1)S(1)}, u32[]{:S(2)}, u32[]{:S(2)}) collective-permute-start(bf16[528,128]{1,0:T(8,128)(2,1)S(1)} %get-tuple-element.14), channel_id=1, source_target_pairs={{0,1},{1,0},{2,3},{3,2},{16,17},{17,16},{18,19},{19,18},{4,5},{5,4... | collective-permute-start | bytes 405512 | tf_op jit(solution)/shard_map/ppermute | solution.py:342
  9.3 12.1 %collective-permute-start.3 = (bf16[528,128]{1,0:T(8,128)(2,1)S(1)}, bf16[528,128]{1,0:T(8,128)(2,1)S(1)}, u32[]{:S(2)}, u32[]{:S(2)}) collective-permute-start(bf16[528,128]{1,0:T(8,128)(2,1)S(1)} %get-tuple-element.15), channel_id=1, source_target_pairs={{0,19},{1,18},{2,17},{3,16},{16,3},{17,2},{18,1},{19,0},{4,23},{5,... | collective-permute-start | bytes 405512 | tf_op jit(solution)/shard_map/ppermute | solution.py:342
  10.2 12.3 %collective-permute-start.4 = (bf16[528,128]{1,0:T(8,128)(2,1)S(1)}, bf16[528,128]{1,0:T(8,128)(2,1)S(1)}, u32[]{:S(2)}, u32[]{:S(2)}) collective-permute-start(bf16[528,128]{1,0:T(8,128)(2,1)S(1)} %get-tuple-element.16), channel_id=1, source_target_pairs={{0,17},{1,16},{2,19},{3,18},{16,1},{17,0},{18,3},{19,2},{4,21},{5,... | collective-permute-start | bytes 405512 | tf_op jit(solution)/shard_map/ppermute | solution.py:342
  16.3 12.8 %collective-permute-start.7 = (bf16[528,128]{1,0:T(8,128)(2,1)S(1)}, bf16[528,128]{1,0:T(8,128)(2,1)S(1)}, u32[]{:S(2)}, u32[]{:S(2)}) collective-permute-start(bf16[528,128]{1,0:T(8,128)(2,1)S(1)} %get-tuple-element.23), channel_id=1, source_target_pairs={{0,16},{1,17},{2,18},{3,19},{16,0},{17,1},{18,2},{19,3},{4,20},{5,... | collective-permute-start | bytes 405512 | tf_op jit(solution)/shard_map/ppermute | solution.py:342
  18.1 13.1 %collective-permute-start.5 = (bf16[528,128]{1,0:T(8,128)(2,1)S(1)}, bf16[528,128]{1,0:T(8,128)(2,1)S(1)}, u32[]{:S(2)}, u32[]{:S(2)}) collective-permute-start(bf16[528,128]{1,0:T(8,128)(2,1)S(1)} %get-tuple-element.21), channel_id=1, source_target_pairs={{0,18},{1,19},{2,16},{3,17},{16,2},{17,3},{18,0},{19,1},{4,22},{5,... | collective-permute-start | bytes 405512 | tf_op jit(solution)/shard_map/ppermute | solution.py:342
  21.3 11.4 %collective-permute-start.6 = (bf16[528,128]{1,0:T(8,128)(2,1)S(1)}, bf16[528,128]{1,0:T(8,128)(2,1)S(1)}, u32[]{:S(2)}, u32[]{:S(2)}) collective-permute-start(bf16[528,128]{1,0:T(8,128)(2,1)S(1)} %get-tuple-element.22), channel_id=1, source_target_pairs={{0,2},{1,3},{2,0},{3,1},{16,18},{17,19},{18,16},{19,17},{4,6},{5,7... | collective-permute-start | bytes 405512 | tf_op jit(solution)/shard_map/ppermute | solution.py:342
  22.7 3.7 %collective-permute-start.8 = (f32[8,128]{1,0:T(8,128)S(1)}, f32[8,128]{1,0:T(8,128)S(1)}, u32[]{:S(2)}, u32[]{:S(2)}) collective-permute-start(f32[8,128]{1,0:T(8,128)S(1)} %score.4.rest_5_.own_ref), channel_id=1, source_target_pairs={{0,16},{1,17},{2,18},{3,19},{16,0},{17,1},{18,2},{19,3},{4,20},{5,... | collective-permute-start | bytes 12296 | tf_op jit(solution)/shard_map/ppermute | solution.py:342
  26.4 11.5 %collective-permute-start.10 = (f32[8,128]{1,0:T(8,128)S(1)}, f32[8,128]{1,0:T(8,128)S(1)}, u32[]{:S(2)}, u32[]{:S(2)}) collective-permute-start(f32[8,128]{1,0:T(8,128)S(1)} %merge.1.rest_2_), channel_id=1, source_target_pairs={{0,3},{1,2},{2,1},{3,0},{16,19},{17,18},{18,17},{19,16},{4,7},{5,6... | collective-permute-start | bytes 12296 | tf_op jit(solution)/shard_map/ppermute | solution.py:342
  28.9 9.0 %collective-permute-start.9 = (f32[8,128]{1,0:T(8,128)S(1)}, f32[8,128]{1,0:T(8,128)S(1)}, u32[]{:S(2)}, u32[]{:S(2)}) collective-permute-start(f32[8,128]{1,0:T(8,128)S(1)} %merge.1.rest_2_), channel_id=1, source_target_pairs={{0,1},{1,0},{2,3},{3,2},{16,17},{17,16},{18,19},{19,18},{4,5},{5,4... | collective-permute-start | bytes 12296 | tf_op jit(solution)/shard_map/ppermute | solution.py:342
  29.2 5.7 %copy-start.2 = (bf16[1,1,768,1024]{3,2,1,0:T(8,128)(2,1)S(1)}, bf16[1,1,768,1024]{3,2,1,0:T(8,128)(2,1)}, u32[]{:S(2)}) copy-start(bf16[1,1,768,1024]{3,2,1,0:T(8,128)(2,1)} %param.12) | copy-start | bytes 4718596
  29.2 5.7 %copy-start.3 = (bf16[1,1,768,1024]{3,2,1,0:T(8,128)(2,1)S(1)}, bf16[1,1,768,1024]{3,2,1,0:T(8,128)(2,1)}, u32[]{:S(2)}) copy-start(bf16[1,1,768,1024]{3,2,1,0:T(8,128)(2,1)} %param.13) | copy-start | bytes 4718596
  29.3 5.5 %copy-start = (f32[1,1,768,1024]{3,2,1,0:T(8,128)S(1)}, f32[1,1,768,1024]{3,2,1,0:T(8,128)}, u32[]{:S(2)}) copy-start(f32[1,1,768,1024]{3,2,1,0:T(8,128)} %param.11) | copy-start | bytes 9437188
  29.3 8.7 %collective-permute-start.11 = (f32[8,128]{1,0:T(8,128)S(1)}, f32[8,128]{1,0:T(8,128)S(1)}, u32[]{:S(2)}, u32[]{:S(2)}) collective-permute-start(f32[8,128]{1,0:T(8,128)S(1)} %score.5.rest_1_.rest_2_), channel_id=1, source_target_pairs={{0,16},{1,17},{2,18},{3,19},{16,0},{17,1},{18,2},{19,3},{4,20},{5,... | collective-permute-start | bytes 12296 | tf_op jit(solution)/shard_map/ppermute | solution.py:342
  31.3 6.6 %collective-permute-start.13 = (f32[8,128]{1,0:T(8,128)S(1)}, f32[8,128]{1,0:T(8,128)S(1)}, u32[]{:S(2)}, u32[]{:S(2)}) collective-permute-start(f32[8,128]{1,0:T(8,128)S(1)} %score.6.rest_1_), channel_id=1, source_target_pairs={{0,18},{1,19},{2,16},{3,17},{16,2},{17,3},{18,0},{19,1},{4,22},{5,... | collective-permute-start | bytes 12296 | tf_op jit(solution)/shard_map/ppermute | solution.py:342
  32.8 5.1 %collective-permute-start.12 = (f32[8,128]{1,0:T(8,128)S(1)}, f32[8,128]{1,0:T(8,128)S(1)}, u32[]{:S(2)}, u32[]{:S(2)}) collective-permute-start(f32[8,128]{1,0:T(8,128)S(1)} %score.7.rest_3_), channel_id=1, source_target_pairs={{0,2},{1,3},{2,0},{3,1},{16,18},{17,19},{18,16},{19,17},{4,6},{5,7... | collective-permute-start | bytes 12296 | tf_op jit(solution)/shard_map/ppermute | solution.py:342
  34.8 3.1 %copy-start.4 = (s32[1,512,8]{1,2,0:T(8,128)S(1)}, s32[1,512,8]{1,2,0:T(8,128)}, u32[]{:S(2)}) copy-start(s32[1,512,8]{1,2,0:T(8,128)} %param.9) | copy-start | bytes 49156

commit v25 on v20

--- a/solution.py
+++ b/solution.py
@@ -226,8 +226,9 @@
 
 def update_kernel(items, cap, own_ref, other_ref, grad_ref, master_ref, moment_ref, second_ref, *rest):
     chunks = rest[: len(items)]
-    _, update_hbm, rows, scaled, total, update, sems = rest[len(items) :]
-    hid, half = update.shape
+    _, update_hbm, tail_ref, rows, scaled, total, update, sems = rest[len(items) :]
+    hid, half = total.shape
+    cut = update.shape[0]
     width = min(half, 4 * LANES)
     height = 2 * TILE
     data_rows = half // LANES * cap
@@ -274,8 +275,10 @@
         return first, pl.reciprocal(scale, approx=True)
 
     def finish(top, columns, first, scale):
-        lines = slice(top, top + TILE)
-        update[lines, columns] = first * scale + decay_rate * master_ref[lines, columns]
+        out, place = (update, top) if top < cut else (tail_ref, top - cut)
+        out[place : place + TILE, columns] = (
+            first * scale + decay_rate * master_ref[top : top + TILE, columns]
+        )
 
     copies = []
     pieces = [
@@ -292,7 +295,7 @@
         if turn >= 2:
             finish(*pieces[turn - 2], *held.pop((turn - 2, 1)))
             top, columns = pieces[turn - 2]
-            if (top + TILE) % height == 0 and columns.stop == half:
+            if top < cut and (top + TILE) % height == 0 and columns.stop == half:
                 lines = slice(top + TILE - height, top + TILE)
                 copies.append(
                     pltpu.make_async_copy(
@@ -304,8 +307,11 @@
         copy.wait()
 
 
-def combine_kernel(steps, group, cap, ids_ref, slots_ref, *rest):
-    refs, out_ref = iter(rest[:-1]), rest[-1]
+def combine_kernel(steps, group, cap, _, tail_ref, ids_ref, slots_ref, *rest):
+    refs, (out_ref, update_hbm, sem) = iter(rest[:-3]), rest[-3:]
+    cut = update_hbm.shape[0] - tail_ref.shape[0]
+    copy = pltpu.make_async_copy(tail_ref, update_hbm.at[cut:, :], sem)
+    copy.start()
     tokens = ids_ref.shape[1]
     me = ep_index()
     shape = rest[0].shape
@@ -328,6 +334,7 @@
         at_slot = jnp.where(place == slots_ref[k : k + 1, :], columns[:, k : k + 1], 0.0)
         result = jnp.where(ids == (me ^ k), jnp.sum(at_slot, axis=0, keepdims=True), result)
     out_ref[...] = result
+    copy.wait()
 
 
 def moved(array, side, step):
@@ -462,16 +469,20 @@
     returned[far] = [moved(last_scores, 0, far), moved(other_far, 1, far)]
 
     depth = -(-len(added) // 2) * LANES
-    update = pl.pallas_call(
+    kept = 2 * LANES if hid > 2 * LANES else hid // 2
+    update, tail = pl.pallas_call(
         functools.partial(update_kernel, added, cap),
-        out_shape=jax.ShapeDtypeStruct((hid, half), F32),
+        out_shape=[
+            jax.ShapeDtypeStruct((hid, half), F32),
+            jax.ShapeDtypeStruct((kept, half), F32),
+        ],
         in_specs=specs(pltpu.VMEM, 6 + len(added)) + specs(pl.ANY, 1),
-        out_specs=specs(pltpu.HBM, 1)[0],
+        out_specs=specs(pltpu.HBM, 1) + specs(pltpu.VMEM, 1),
         scratch_shapes=[
             pltpu.VMEM((depth, half), BF16),
             pltpu.VMEM((hid, depth), BF16),
             pltpu.VMEM((hid, half), F32),
-            pltpu.VMEM((hid, half), F32),
+            pltpu.VMEM((hid - kept, half), F32),
             pltpu.SemaphoreType.DMA((hid // (2 * TILE),)),
         ],
         compiler_params=params(),
@@ -488,17 +499,22 @@
         last_scores,
     )
     shares = [array for arrays in returned.values() for array in arrays]
-    router = pl.pallas_call(
+    router, update = pl.pallas_call(
         functools.partial(
             combine_kernel, [(k, len(arrays)) for k, arrays in returned.items()], group, cap
         ),
-        out_shape=jax.ShapeDtypeStruct((top, tokens), F32),
-        in_specs=specs(pltpu.VMEM, 2 + len(shares)),
-        out_specs=specs(pltpu.VMEM, 1)[0],
+        out_shape=[
+            jax.ShapeDtypeStruct((top, tokens), F32),
+            jax.ShapeDtypeStruct((hid, half), F32),
+        ],
+        in_specs=specs(pltpu.HBM, 1) + specs(pltpu.VMEM, 3 + len(shares)),
+        out_specs=specs(pltpu.VMEM, 1) + specs(pltpu.HBM, 1),
+        input_output_aliases={0: 1},
+        scratch_shapes=[pltpu.SemaphoreType.DMA],
         compiler_params=params(),
         cost_estimate=cost(4 * slots * tokens, 8 * top * tokens),
         name="combine",
-    )(ids, slot_of, *shares)
+    )(update, tail, ids, slot_of, *shares)
     return (update[None, None], router.T[None])
 
 

time: 39 us -> 40.3 us (1.033)
  local copies, waits for them, and re-layouts: 0.02 us -> 1.01 us
    unnamed x10 -> x12, local copies, waits for them, and re-layouts: 0.02 us -> 1.01 us
    pallas_call x1, Pallas kernels: 0.87 us -> 1.59 us  [local(): pl.pallas_call(functools.partial(combine_kernel, [(k, len(arrays)) for k,...]
  transfers between devices with their start and end apart: 14 -> 14, of which waited for: 4 -> 4; matrix products, arithmetic and copies ran while one was open for 0% -> 0% of each run, Pallas kernels for 26% -> 25%
where the time goes in v25:
time: 40.3 us; the launch traced here: 40 us
  starting transfers between devices  23.3 us (58%)
  Pallas kernels  11.4 us (28%)
  waiting for transfers between devices  3.54 us (9%)
  local copies, waits for them, and re-layouts  1.01 us (3%)
  between operations  0.73 us (2%)
    ppermute x14, starting transfers between devices, moved(): return lax.ppermute(array, ('pair', 'ep'), pairs)  23.3 us
    ppermute x14, waiting for transfers between devices, moved(): return lax.ppermute(array, ('pair', 'ep'), pairs)  3.54 us
    pallas_call x1, Pallas kernels, local(): pl.pallas_call(functools.partial(later_kernel, last_items, late, cap), ou...  3.35 us
    pallas_call x1, Pallas kernels, local(): pl.pallas_call(functools.partial(update_kernel, added, cap), out_shape=[j...  2.73 us
    pallas_call x1, Pallas kernels, local(): pl.pallas_call(functools.partial(route_kernel, first_items, first, group,...  1.99 us
    pallas_call x1, Pallas kernels, local(): pl.pallas_call(functools.partial(combine_kernel, [(k, len(arrays)) for k,...  1.59 us
    pallas_call x1, Pallas kernels, local(): pl.pallas_call(functools.partial(sum_kernel, summed, group, cap), out_sha...  1.12 us
    unnamed x12, local copies, waits for them, and re-layouts  1.01 us
  transfers between devices with their start and end apart: 14, of which 4 were waited for; matrix products, arithmetic and copies ran while one was open for 0% of the time, Pallas kernels for 25%

profile of v25, /device:TPU:0, one launch (start us, length us, event | category | flops | bytes accessed | tf_op | source)
XLA Modules:
  0.0 40.0 jit_solution(16407472713676109890)
XLA Ops:
  0.6 3.0 %collective-permute-start = (bf16[768,256]{1,0:T(8,128)(2,1)}, bf16[768,256]{1,0:T(8,128)(2,1)S(1)}, u32[]{:S(2)}, u32[]{:S(2)}) collective-permute-start(bf16[768,256]{1,0:T(8,128)(2,1)} %bitcast.17), channel_id=1, source_target_pairs={{0,16},{1,17},{2,18},{3,19},{16,0},{17,1},{18,2},{19,3},{4,20},{5,... | collective-permute-start | bytes 1179656 | tf_op jit(solution)/shard_map/ppermute | solution.py:347
  3.7 2.0 %route.1 = (f32[16,512]{1,0:T(8,128)S(1)}, bf16[4,16,128]{2,1,0:T(8,128)(2,1)S(1)}, bf16[528,128]{1,0:T(8,128)(2,1)S(1)}, bf16[528,128]{1,0:T(8,128)(2,1)S(1)}, ...) custom-call(s32[8,512]{1,0:T(8,128)} %bitcast.23, bf16[8,512]{1,0:T(8,128)(2,1)} %bitcast.28, ...), custom_call_target="tpu_custom_call" | custom-call | flops 536870912 | bytes 3145728 | tf_op jit(solution)/shard_map/route/pallas_call | solution.py:371
  5.7 3.7 %collective-permute-start.1 = (bf16[528,128]{1,0:T(8,128)(2,1)S(1)}, bf16[528,128]{1,0:T(8,128)(2,1)S(1)}, u32[]{:S(2)}, u32[]{:S(2)}) collective-permute-start(bf16[528,128]{1,0:T(8,128)(2,1)S(1)} %get-tuple-element.17), channel_id=1, source_target_pairs={{0,3},{1,2},{2,1},{3,0},{16,19},{17,18},{18,17},{19,16},{4,7},{5,6... | collective-permute-start | bytes 405512 | tf_op jit(solution)/shard_map/ppermute | solution.py:347
  9.3 0.8 %collective-permute-start.3 = (bf16[528,128]{1,0:T(8,128)(2,1)S(1)}, bf16[528,128]{1,0:T(8,128)(2,1)S(1)}, u32[]{:S(2)}, u32[]{:S(2)}) collective-permute-start(bf16[528,128]{1,0:T(8,128)(2,1)S(1)} %get-tuple-element.19), channel_id=1, source_target_pairs={{0,19},{1,18},{2,17},{3,16},{16,3},{17,2},{18,1},{19,0},{4,23},{5,... | collective-permute-start | bytes 405512 | tf_op jit(solution)/shard_map/ppermute | solution.py:347
  10.2 1.4 %collective-permute-start.4 = (bf16[528,128]{1,0:T(8,128)(2,1)S(1)}, bf16[528,128]{1,0:T(8,128)(2,1)S(1)}, u32[]{:S(2)}, u32[]{:S(2)}) collective-permute-start(bf16[528,128]{1,0:T(8,128)(2,1)S(1)} %get-tuple-element.20), channel_id=1, source_target_pairs={{0,17},{1,16},{2,19},{3,18},{16,1},{17,0},{18,3},{19,2},{4,21},{5,... | collective-permute-start | bytes 405512 | tf_op jit(solution)/shard_map/ppermute | solution.py:347
  11.6 1.4 %collective-permute-done.other_ref = bf16[768,256]{1,0:T(8,128)(2,1)S(1)} collective-permute-done((bf16[768,256]{1,0:T(8,128)(2,1)}, bf16[768,256]{1,0:T(8,128)(2,1)S(1)}, u32[]{:S(2)}, u32[]{:S(2)}) %collective-permute-start) | collective-permute-done | bytes 393248 | tf_op jit(solution)/shard_map/ppermute | solution.py:347
  13.0 1.0 %copy-done.1 = bf16[1,1,768,256]{3,2,1,0:T(8,128)(2,1)S(1)} copy-done((bf16[1,1,768,256]{3,2,1,0:T(8,128)(2,1)S(1)}, bf16[1,1,768,256]{3,2,1,0:T(8,128)(2,1)}, u32[]{:S(2)}) %copy-start.1) | copy-done | bytes 393240
  14.0 3.3 %later.1 = (f32[512,1024]{1,0:T(8,128)S(1)}, bf16[528,128]{1,0:T(8,128)(2,1)S(1)}, bf16[528,128]{1,0:T(8,128)(2,1)S(1)}, bf16[528,128]{1,0:T(8,128)(2,1)S(1)}, bf16[528,128]{1,0:T(8,128)(2,1)S(1)}) custom-call(f32[16,512]{1,0:T(8,128)S(1)} %get-tuple-element.21.slots_ref, bf16[4,16,128]{2,1,0:T(8,128)(2,1)S(1)} %get-tuple-element.22.tiles_ref, ...), custom_call_target="tpu_custom_call" | custom-call | flops 1342177280 | bytes 3145728 | tf_op jit(solution)/shard_map/later/pallas_call | solution.py:397
  17.3 1.8 %collective-permute-start.7 = (bf16[528,128]{1,0:T(8,128)(2,1)S(1)}, bf16[528,128]{1,0:T(8,128)(2,1)S(1)}, u32[]{:S(2)}, u32[]{:S(2)}) collective-permute-start(bf16[528,128]{1,0:T(8,128)(2,1)S(1)} %get-tuple-element.27), channel_id=1, source_target_pairs={{0,16},{1,17},{2,18},{3,19},{16,0},{17,1},{18,2},{19,3},{4,20},{5,... | collective-permute-start | bytes 405512 | tf_op jit(solution)/shard_map/ppermute | solution.py:347
  19.2 3.2 %collective-permute-start.5 = (bf16[528,128]{1,0:T(8,128)(2,1)S(1)}, bf16[528,128]{1,0:T(8,128)(2,1)S(1)}, u32[]{:S(2)}, u32[]{:S(2)}) collective-permute-start(bf16[528,128]{1,0:T(8,128)(2,1)S(1)} %get-tuple-element.25), channel_id=1, source_target_pairs={{0,18},{1,19},{2,16},{3,17},{16,2},{17,3},{18,0},{19,1},{4,22},{5,... | collective-permute-start | bytes 405512 | tf_op jit(solution)/shard_map/ppermute | solution.py:347
  22.3 0.1 collective-permute-start.6
  22.5 0.2 score.4.rest_5_.own_ref
  22.7 1.5 %collective-permute-start.8 = (f32[8,128]{1,0:T(8,128)S(1)}, f32[8,128]{1,0:T(8,128)S(1)}, u32[]{:S(2)}, u32[]{:S(2)}) collective-permute-start(f32[8,128]{1,0:T(8,128)S(1)} %score.4.rest_5_.own_ref), channel_id=1, source_target_pairs={{0,16},{1,17},{2,18},{3,19},{16,0},{17,1},{18,2},{19,3},{4,20},{5,... | collective-permute-start | bytes 12296 | tf_op jit(solution)/shard_map/ppermute | solution.py:347
  24.1 1.1 %sum.1._.grad_ref = f32[768,1024]{1,0:T(8,128)S(1)} custom-call(bf16[768,256]{1,0:T(8,128)(2,1)S(1)} %bitcast.19, bf16[768,256]{1,0:T(8,128)(2,1)S(1)} %collective-permute-done.other_ref, bf16[528,128]{1,0:T(8,128)(2,1)S(1)} %collective-permute-done.1.rest_0_, bf16[528,128]{1,0:T(8,128)(2,1)S(1)} %collective-permute-done.2.rest_1_, ...), custom_call_target="tpu_custom_call" | custom-call | flops 805306368 | bytes 3145728 | tf_op jit(solution)/shard_map/sum/pallas_call | solution.py:443
  25.3 1.1 %collective-permute-done.8.other_ref = f32[8,128]{1,0:T(8,128)S(1)} collective-permute-done((f32[8,128]{1,0:T(8,128)S(1)}, f32[8,128]{1,0:T(8,128)S(1)}, u32[]{:S(2)}, u32[]{:S(2)}) %collective-permute-start.8) | collective-permute-done | bytes 4128 | tf_op jit(solution)/shard_map/ppermute | solution.py:347
  26.4 3.6 %collective-permute-start.10 = (f32[8,128]{1,0:T(8,128)S(1)}, f32[8,128]{1,0:T(8,128)S(1)}, u32[]{:S(2)}, u32[]{:S(2)}) collective-permute-start(f32[8,128]{1,0:T(8,128)S(1)} %merge.1.rest_2_), channel_id=1, source_target_pairs={{0,3},{1,2},{2,1},{3,0},{16,19},{17,18},{18,17},{19,16},{4,7},{5,6... | collective-permute-start | bytes 12296 | tf_op jit(solution)/shard_map/ppermute | solution.py:347
  30.0 0.2 collective-permute-start.9
  30.3 1.4 %collective-permute-start.11 = (f32[8,128]{1,0:T(8,128)S(1)}, f32[8,128]{1,0:T(8,128)S(1)}, u32[]{:S(2)}, u32[]{:S(2)}) collective-permute-start(f32[8,128]{1,0:T(8,128)S(1)} %score.5.rest_1_.rest_2_), channel_id=1, source_target_pairs={{0,16},{1,17},{2,18},{3,19},{16,0},{17,1},{18,2},{19,3},{4,20},{5,... | collective-permute-start | bytes 12296 | tf_op jit(solution)/shard_map/ppermute | solution.py:347
  31.7 0.5 %collective-permute-done.5.rest_0_ = bf16[528,128]{1,0:T(8,128)(2,1)S(1)} collective-permute-done((bf16[528,128]{1,0:T(8,128)(2,1)S(1)}, bf16[528,128]{1,0:T(8,128)(2,1)S(1)}, u32[]{:S(2)}, u32[]{:S(2)}) %collective-permute-start.5) | collective-permute-done | bytes 135200 | tf_op jit(solution)/shard_map/ppermute | solution.py:347
  32.3 0.4 collective-permute-start.13
  32.7 0.6 %collective-permute-done.6.rest_0_.rest_1_ = bf16[528,128]{1,0:T(8,128)(2,1)S(1)} collective-permute-done((bf16[528,128]{1,0:T(8,128)(2,1)S(1)}, bf16[528,128]{1,0:T(8,128)(2,1)S(1)}, u32[]{:S(2)}, u32[]{:S(2)}) %collective-permute-start.6) | collective-permute-done | bytes 135200 | tf_op jit(solution)/shard_map/ppermute | solution.py:347
  33.4 2.3 %collective-permute-start.12 = (f32[8,128]{1,0:T(8,128)S(1)}, f32[8,128]{1,0:T(8,128)S(1)}, u32[]{:S(2)}, u32[]{:S(2)}) collective-permute-start(f32[8,128]{1,0:T(8,128)S(1)} %score.7.rest_3_), channel_id=1, source_target_pairs={{0,2},{1,3},{2,0},{3,1},{16,18},{17,19},{18,16},{19,17},{4,6},{5,7... | collective-permute-start | bytes 12296 | tf_op jit(solution)/shard_map/ppermute | solution.py:347
  35.6 2.7 %update.1 = (f32[768,1024]{1,0:T(8,128)}, f32[256,1024]{1,0:T(8,128)S(1)}) custom-call(bf16[768,256]{1,0:T(8,128)(2,1)S(1)} %bitcast.20, bf16[768,256]{1,0:T(8,128)(2,1)S(1)} %collective-permute-done.other_ref, f32[768,1024]{1,0:T(8,128)S(1)} %sum.1._.grad_ref, f32[768,1024]{1,0:T(8,128)S(1)} %bitcast.16, bf16[768,1024]{1,0:T(8,128)(2,1)S(1)} %bitcast.21, ...), custom_call_target="tpu_custom_call" | custom-call | flops 402653184 | bytes 12582912 | tf_op jit(solution)/shard_map/update/pallas_call | solution.py:473
  38.5 1.6 %combine.1 = (f32[8,512]{1,0:T(8,128)}, f32[768,1024]{1,0:T(8,128)}) custom-call(f32[768,1024]{1,0:T(8,128)} %get-tuple-element.28._, f32[256,1024]{1,0:T(8,128)S(1)} %get-tuple-element.29.tail_ref, s32[8,512]{1,0:T(8,128)S(1)} %bitcast.24, f32[16,512]{1,0:T(8,128)S(1)} %get-tuple-element.21.slots_ref, ...), custom_call_target="tpu_custom_call", output_to_operand_aliasing={{1}: (0, {})} | custom-call | flops 524288 | bytes 32768 | tf_op jit(solution)/shard_map/combine/pallas_call | solution.py:502
  (26 shorter events, 0.5 us)
Async XLA Ops:
  0.6 12.4 %collective-permute-start = (bf16[768,256]{1,0:T(8,128)(2,1)}, bf16[768,256]{1,0:T(8,128)(2,1)S(1)}, u32[]{:S(2)}, u32[]{:S(2)}) collective-permute-start(bf16[768,256]{1,0:T(8,128)(2,1)} %bitcast.17), channel_id=1, source_target_pairs={{0,16},{1,17},{2,18},{3,19},{16,0},{17,1},{18,2},{19,3},{4,20},{5,... | collective-permute-start | bytes 1179656 | tf_op jit(solution)/shard_map/ppermute | solution.py:347
  5.7 13.5 %collective-permute-start.1 = (bf16[528,128]{1,0:T(8,128)(2,1)S(1)}, bf16[528,128]{1,0:T(8,128)(2,1)S(1)}, u32[]{:S(2)}, u32[]{:S(2)}) collective-permute-start(bf16[528,128]{1,0:T(8,128)(2,1)S(1)} %get-tuple-element.17), channel_id=1, source_target_pairs={{0,3},{1,2},{2,1},{3,0},{16,19},{17,18},{18,17},{19,16},{4,7},{5,6... | collective-permute-start | bytes 405512 | tf_op jit(solution)/shard_map/ppermute | solution.py:347
  9.3 13.0 %collective-permute-start.2 = (bf16[528,128]{1,0:T(8,128)(2,1)S(1)}, bf16[528,128]{1,0:T(8,128)(2,1)S(1)}, u32[]{:S(2)}, u32[]{:S(2)}) collective-permute-start(bf16[528,128]{1,0:T(8,128)(2,1)S(1)} %get-tuple-element.18), channel_id=1, source_target_pairs={{0,1},{1,0},{2,3},{3,2},{16,17},{17,16},{18,19},{19,18},{4,5},{5,4... | collective-permute-start | bytes 405512 | tf_op jit(solution)/shard_map/ppermute | solution.py:347
  9.3 13.1 %collective-permute-start.3 = (bf16[528,128]{1,0:T(8,128)(2,1)S(1)}, bf16[528,128]{1,0:T(8,128)(2,1)S(1)}, u32[]{:S(2)}, u32[]{:S(2)}) collective-permute-start(bf16[528,128]{1,0:T(8,128)(2,1)S(1)} %get-tuple-element.19), channel_id=1, source_target_pairs={{0,19},{1,18},{2,17},{3,16},{16,3},{17,2},{18,1},{19,0},{4,23},{5,... | collective-permute-start | bytes 405512 | tf_op jit(solution)/shard_map/ppermute | solution.py:347
  10.2 12.3 %collective-permute-start.4 = (bf16[528,128]{1,0:T(8,128)(2,1)S(1)}, bf16[528,128]{1,0:T(8,128)(2,1)S(1)}, u32[]{:S(2)}, u32[]{:S(2)}) collective-permute-start(bf16[528,128]{1,0:T(8,128)(2,1)S(1)} %get-tuple-element.20), channel_id=1, source_target_pairs={{0,17},{1,16},{2,19},{3,18},{16,1},{17,0},{18,3},{19,2},{4,21},{5,... | collective-permute-start | bytes 405512 | tf_op jit(solution)/shard_map/ppermute | solution.py:347
  13.0 1.0 %copy-start.1 = (bf16[1,1,768,256]{3,2,1,0:T(8,128)(2,1)S(1)}, bf16[1,1,768,256]{3,2,1,0:T(8,128)(2,1)}, u32[]{:S(2)}) copy-start(bf16[1,1,768,256]{3,2,1,0:T(8,128)(2,1)} %param.10) | copy-start | bytes 1179652
  14.0 10.2 %copy-start.2 = (bf16[1,1,768,256]{3,2,1,0:T(8,128)(2,1)S(1)}, bf16[1,1,768,256]{3,2,1,0:T(8,128)(2,1)}, u32[]{:S(2)}) copy-start(bf16[1,1,768,256]{3,2,1,0:T(8,128)(2,1)} %param.10) | copy-start | bytes 1179652
  17.3 12.9 %collective-permute-start.7 = (bf16[528,128]{1,0:T(8,128)(2,1)S(1)}, bf16[528,128]{1,0:T(8,128)(2,1)S(1)}, u32[]{:S(2)}, u32[]{:S(2)}) collective-permute-start(bf16[528,128]{1,0:T(8,128)(2,1)S(1)} %get-tuple-element.27), channel_id=1, source_target_pairs={{0,16},{1,17},{2,18},{3,19},{16,0},{17,1},{18,2},{19,3},{4,20},{5,... | collective-permute-start | bytes 405512 | tf_op jit(solution)/shard_map/ppermute | solution.py:347
  19.2 13.0 %collective-permute-start.5 = (bf16[528,128]{1,0:T(8,128)(2,1)S(1)}, bf16[528,128]{1,0:T(8,128)(2,1)S(1)}, u32[]{:S(2)}, u32[]{:S(2)}) collective-permute-start(bf16[528,128]{1,0:T(8,128)(2,1)S(1)} %get-tuple-element.25), channel_id=1, source_target_pairs={{0,18},{1,19},{2,16},{3,17},{16,2},{17,3},{18,0},{19,1},{4,22},{5,... | collective-permute-start | bytes 405512 | tf_op jit(solution)/shard_map/ppermute | solution.py:347
  22.3 10.9 %collective-permute-start.6 = (bf16[528,128]{1,0:T(8,128)(2,1)S(1)}, bf16[528,128]{1,0:T(8,128)(2,1)S(1)}, u32[]{:S(2)}, u32[]{:S(2)}) collective-permute-start(bf16[528,128]{1,0:T(8,128)(2,1)S(1)} %get-tuple-element.26), channel_id=1, source_target_pairs={{0,2},{1,3},{2,0},{3,1},{16,18},{17,19},{18,16},{19,17},{4,6},{5,7... | collective-permute-start | bytes 405512 | tf_op jit(solution)/shard_map/ppermute | solution.py:347
  22.7 3.7 %collective-permute-start.8 = (f32[8,128]{1,0:T(8,128)S(1)}, f32[8,128]{1,0:T(8,128)S(1)}, u32[]{:S(2)}, u32[]{:S(2)}) collective-permute-start(f32[8,128]{1,0:T(8,128)S(1)} %score.4.rest_5_.own_ref), channel_id=1, source_target_pairs={{0,16},{1,17},{2,18},{3,19},{16,0},{17,1},{18,2},{19,3},{4,20},{5,... | collective-permute-start | bytes 12296 | tf_op jit(solution)/shard_map/ppermute | solution.py:347
  26.4 9.2 %copy-start = (f32[1,1,768,1024]{3,2,1,0:T(8,128)S(1)}, f32[1,1,768,1024]{3,2,1,0:T(8,128)}, u32[]{:S(2)}) copy-start(f32[1,1,768,1024]{3,2,1,0:T(8,128)} %param.11) | copy-start | bytes 9437188
  26.4 9.2 %copy-start.3 = (bf16[1,1,768,1024]{3,2,1,0:T(8,128)(2,1)S(1)}, bf16[1,1,768,1024]{3,2,1,0:T(8,128)(2,1)}, u32[]{:S(2)}) copy-start(bf16[1,1,768,1024]{3,2,1,0:T(8,128)(2,1)} %param.12) | copy-start | bytes 4718596
  26.4 9.2 %copy-start.4 = (bf16[1,1,768,1024]{3,2,1,0:T(8,128)(2,1)S(1)}, bf16[1,1,768,1024]{3,2,1,0:T(8,128)(2,1)}, u32[]{:S(2)}) copy-start(bf16[1,1,768,1024]{3,2,1,0:T(8,128)(2,1)} %param.13) | copy-start | bytes 4718596
  26.4 12.0 %collective-permute-start.10 = (f32[8,128]{1,0:T(8,128)S(1)}, f32[8,128]{1,0:T(8,128)S(1)}, u32[]{:S(2)}, u32[]{:S(2)}) collective-permute-start(f32[8,128]{1,0:T(8,128)S(1)} %merge.1.rest_2_), channel_id=1, source_target_pairs={{0,3},{1,2},{2,1},{3,0},{16,19},{17,18},{18,17},{19,16},{4,7},{5,6... | collective-permute-start | bytes 12296 | tf_op jit(solution)/shard_map/ppermute | solution.py:347
  30.0 8.4 %collective-permute-start.9 = (f32[8,128]{1,0:T(8,128)S(1)}, f32[8,128]{1,0:T(8,128)S(1)}, u32[]{:S(2)}, u32[]{:S(2)}) collective-permute-start(f32[8,128]{1,0:T(8,128)S(1)} %merge.1.rest_2_), channel_id=1, source_target_pairs={{0,1},{1,0},{2,3},{3,2},{16,17},{17,16},{18,19},{19,18},{4,5},{5,4... | collective-permute-start | bytes 12296 | tf_op jit(solution)/shard_map/ppermute | solution.py:347
  30.3 8.1 %collective-permute-start.11 = (f32[8,128]{1,0:T(8,128)S(1)}, f32[8,128]{1,0:T(8,128)S(1)}, u32[]{:S(2)}, u32[]{:S(2)}) collective-permute-start(f32[8,128]{1,0:T(8,128)S(1)} %score.5.rest_1_.rest_2_), channel_id=1, source_target_pairs={{0,16},{1,17},{2,18},{3,19},{16,0},{17,1},{18,2},{19,3},{4,20},{5,... | collective-permute-start | bytes 12296 | tf_op jit(solution)/shard_map/ppermute | solution.py:347
  32.3 6.1 %collective-permute-start.13 = (f32[8,128]{1,0:T(8,128)S(1)}, f32[8,128]{1,0:T(8,128)S(1)}, u32[]{:S(2)}, u32[]{:S(2)}) collective-permute-start(f32[8,128]{1,0:T(8,128)S(1)} %score.6.rest_1_), channel_id=1, source_target_pairs={{0,18},{1,19},{2,16},{3,17},{16,2},{17,3},{18,0},{19,1},{4,22},{5,... | collective-permute-start | bytes 12296 | tf_op jit(solution)/shard_map/ppermute | solution.py:347
  33.4 5.0 %collective-permute-start.12 = (f32[8,128]{1,0:T(8,128)S(1)}, f32[8,128]{1,0:T(8,128)S(1)}, u32[]{:S(2)}, u32[]{:S(2)}) collective-permute-start(f32[8,128]{1,0:T(8,128)S(1)} %score.7.rest_3_), channel_id=1, source_target_pairs={{0,2},{1,3},{2,0},{3,1},{16,18},{17,19},{18,16},{19,17},{4,6},{5,7... | collective-permute-start | bytes 12296 | tf_op jit(solution)/shard_map/ppermute | solution.py:347
  35.6 2.8 %copy-start.5 = (s32[1,512,8]{1,2,0:T(8,128)S(1)}, s32[1,512,8]{1,2,0:T(8,128)}, u32[]{:S(2)}) copy-start(s32[1,512,8]{1,2,0:T(8,128)} %param.9) | copy-start | bytes 49156

commit v26 on v20

--- a/solution.py
+++ b/solution.py
@@ -262,7 +262,10 @@
     def moments(top, columns):
         lines = slice(top, top + TILE)
         grad = total[lines, columns] + grad_ref[lines, columns]
-        first = moment_ref[lines, columns].astype(F32) * (beta_first / (1.0 - beta_first)) + grad
+        unit = first_unit / second_unit**0.5
+        first = moment_ref[lines, columns].astype(F32) * (
+            unit * beta_first / (1.0 - beta_first)
+        ) + grad * unit
         square = (
             second_ref[lines, columns].astype(F32) * (beta_second / (1.0 - beta_second))
             + grad * grad
@@ -270,8 +273,8 @@
         return first, square, lax.rsqrt(square)
 
     def inverse(first, square, root):
-        scale = square * root * (second_unit**0.5 / first_unit) + adam_eps / first_unit
-        return first, pl.reciprocal(scale, approx=True)
+        below = square * root + adam_eps / second_unit**0.5
+        return first, root * (2.0 - below * root)
 
     def finish(top, columns, first, scale):
         lines = slice(top, top + TILE)

time: 39 us -> 39.1 us (level)
  no operation moved by 1% of the time
where the time goes in v26:
time: 39.1 us; the launch traced here: 39 us
  starting transfers between devices  23.3 us (60%)
  Pallas kernels  11.1 us (28%)
  waiting for transfers between devices  3.81 us (10%)
  between operations  0.75 us (2%)
    ppermute x14, starting transfers between devices, moved(): return lax.ppermute(array, ('pair', 'ep'), pairs)  23.3 us
    ppermute x14, waiting for transfers between devices, moved(): return lax.ppermute(array, ('pair', 'ep'), pairs)  3.81 us
    pallas_call x1, Pallas kernels, local(): pl.pallas_call(functools.partial(later_kernel, last_items, late, cap), ou...  3.33 us
    pallas_call x1, Pallas kernels, local(): pl.pallas_call(functools.partial(update_kernel, added, cap), out_shape=ja...  3.18 us
    pallas_call x1, Pallas kernels, local(): pl.pallas_call(functools.partial(route_kernel, first_items, first, group,...  1.99 us
    pallas_call x1, Pallas kernels, local(): pl.pallas_call(functools.partial(sum_kernel, summed, group, cap), out_sha...  1.12 us
    pallas_call x1, Pallas kernels, local(): pl.pallas_call(functools.partial(combine_kernel, [(k, len(arrays)) for k,...  0.87 us
  transfers between devices with their start and end apart: 14, of which 4 were waited for; matrix products, arithmetic and copies ran while one was open for 0% of the time, Pallas kernels for 26%

profile of v26, /device:TPU:0, one launch (start us, length us, event | category | flops | bytes accessed | tf_op | source)
XLA Modules:
  0.0 39.0 jit_solution(15007980268327265562)
XLA Ops:
  0.6 3.0 %collective-permute-start = (bf16[768,256]{1,0:T(8,128)(2,1)}, bf16[768,256]{1,0:T(8,128)(2,1)S(1)}, u32[]{:S(2)}, u32[]{:S(2)}) collective-permute-start(bf16[768,256]{1,0:T(8,128)(2,1)} %bitcast.17), channel_id=1, source_target_pairs={{0,16},{1,17},{2,18},{3,19},{16,0},{17,1},{18,2},{19,3},{4,20},{5,... | collective-permute-start | bytes 1179656 | tf_op jit(solution)/shard_map/ppermute | solution.py:343
  3.7 2.0 %route.1 = (f32[16,512]{1,0:T(8,128)S(1)}, bf16[4,16,128]{2,1,0:T(8,128)(2,1)S(1)}, bf16[528,128]{1,0:T(8,128)(2,1)S(1)}, bf16[528,128]{1,0:T(8,128)(2,1)S(1)}, ...) custom-call(s32[8,512]{1,0:T(8,128)} %bitcast.23, bf16[8,512]{1,0:T(8,128)(2,1)} %bitcast.29, ...), custom_call_target="tpu_custom_call" | custom-call | flops 536870912 | bytes 3145728 | tf_op jit(solution)/shard_map/route/pallas_call | solution.py:367
  5.7 3.7 %collective-permute-start.1 = (bf16[528,128]{1,0:T(8,128)(2,1)S(1)}, bf16[528,128]{1,0:T(8,128)(2,1)S(1)}, u32[]{:S(2)}, u32[]{:S(2)}) collective-permute-start(bf16[528,128]{1,0:T(8,128)(2,1)S(1)} %get-tuple-element.13), channel_id=1, source_target_pairs={{0,3},{1,2},{2,1},{3,0},{16,19},{17,18},{18,17},{19,16},{4,7},{5,6... | collective-permute-start | bytes 405512 | tf_op jit(solution)/shard_map/ppermute | solution.py:343
  9.3 0.8 %collective-permute-start.3 = (bf16[528,128]{1,0:T(8,128)(2,1)S(1)}, bf16[528,128]{1,0:T(8,128)(2,1)S(1)}, u32[]{:S(2)}, u32[]{:S(2)}) collective-permute-start(bf16[528,128]{1,0:T(8,128)(2,1)S(1)} %get-tuple-element.15), channel_id=1, source_target_pairs={{0,19},{1,18},{2,17},{3,16},{16,3},{17,2},{18,1},{19,0},{4,23},{5,... | collective-permute-start | bytes 405512 | tf_op jit(solution)/shard_map/ppermute | solution.py:343
  10.2 1.4 %collective-permute-start.4 = (bf16[528,128]{1,0:T(8,128)(2,1)S(1)}, bf16[528,128]{1,0:T(8,128)(2,1)S(1)}, u32[]{:S(2)}, u32[]{:S(2)}) collective-permute-start(bf16[528,128]{1,0:T(8,128)(2,1)S(1)} %get-tuple-element.16), channel_id=1, source_target_pairs={{0,17},{1,16},{2,19},{3,18},{16,1},{17,0},{18,3},{19,2},{4,21},{5,... | collective-permute-start | bytes 405512 | tf_op jit(solution)/shard_map/ppermute | solution.py:343
  11.6 1.4 %collective-permute-done.other_ref = bf16[768,256]{1,0:T(8,128)(2,1)S(1)} collective-permute-done((bf16[768,256]{1,0:T(8,128)(2,1)}, bf16[768,256]{1,0:T(8,128)(2,1)S(1)}, u32[]{:S(2)}, u32[]{:S(2)}) %collective-permute-start) | collective-permute-done | bytes 393248 | tf_op jit(solution)/shard_map/ppermute | solution.py:343
  13.0 3.3 %later.1 = (f32[512,1024]{1,0:T(8,128)S(1)}, bf16[528,128]{1,0:T(8,128)(2,1)S(1)}, bf16[528,128]{1,0:T(8,128)(2,1)S(1)}, bf16[528,128]{1,0:T(8,128)(2,1)S(1)}, bf16[528,128]{1,0:T(8,128)(2,1)S(1)}) custom-call(f32[16,512]{1,0:T(8,128)S(1)} %get-tuple-element.17.slots_ref, bf16[4,16,128]{2,1,0:T(8,128)(2,1)S(1)} %get-tuple-element.18.tiles_ref, ...), custom_call_target="tpu_custom_call" | custom-call | flops 1342177280 | bytes 3145728 | tf_op jit(solution)/shard_map/later/pallas_call | solution.py:393
  16.3 1.8 %collective-permute-start.7 = (bf16[528,128]{1,0:T(8,128)(2,1)S(1)}, bf16[528,128]{1,0:T(8,128)(2,1)S(1)}, u32[]{:S(2)}, u32[]{:S(2)}) collective-permute-start(bf16[528,128]{1,0:T(8,128)(2,1)S(1)} %get-tuple-element.23), channel_id=1, source_target_pairs={{0,16},{1,17},{2,18},{3,19},{16,0},{17,1},{18,2},{19,3},{4,20},{5,... | collective-permute-start | bytes 405512 | tf_op jit(solution)/shard_map/ppermute | solution.py:343
  18.1 3.2 %collective-permute-start.5 = (bf16[528,128]{1,0:T(8,128)(2,1)S(1)}, bf16[528,128]{1,0:T(8,128)(2,1)S(1)}, u32[]{:S(2)}, u32[]{:S(2)}) collective-permute-start(bf16[528,128]{1,0:T(8,128)(2,1)S(1)} %get-tuple-element.21), channel_id=1, source_target_pairs={{0,18},{1,19},{2,16},{3,17},{16,2},{17,3},{18,0},{19,1},{4,22},{5,... | collective-permute-start | bytes 405512 | tf_op jit(solution)/shard_map/ppermute | solution.py:343
  21.3 0.1 collective-permute-start.6
  21.5 1.0 %collective-permute-done.4.rest_3_ = bf16[528,128]{1,0:T(8,128)(2,1)S(1)} collective-permute-done((bf16[528,128]{1,0:T(8,128)(2,1)S(1)}, bf16[528,128]{1,0:T(8,128)(2,1)S(1)}, u32[]{:S(2)}, u32[]{:S(2)}) %collective-permute-start.4) | collective-permute-done | bytes 135200 | tf_op jit(solution)/shard_map/ppermute | solution.py:343
  22.5 0.2 score.4.rest_5_.own_ref
  22.7 1.6 %collective-permute-start.8 = (f32[8,128]{1,0:T(8,128)S(1)}, f32[8,128]{1,0:T(8,128)S(1)}, u32[]{:S(2)}, u32[]{:S(2)}) collective-permute-start(f32[8,128]{1,0:T(8,128)S(1)} %score.4.rest_5_.own_ref), channel_id=1, source_target_pairs={{0,16},{1,17},{2,18},{3,19},{16,0},{17,1},{18,2},{19,3},{4,20},{5,... | collective-permute-start | bytes 12296 | tf_op jit(solution)/shard_map/ppermute | solution.py:343
  24.3 1.1 %sum.1._.grad_ref = f32[768,1024]{1,0:T(8,128)S(1)} custom-call(bf16[768,256]{1,0:T(8,128)(2,1)S(1)} %bitcast.19, bf16[768,256]{1,0:T(8,128)(2,1)S(1)} %collective-permute-done.other_ref, bf16[528,128]{1,0:T(8,128)(2,1)S(1)} %collective-permute-done.1.rest_0_, bf16[528,128]{1,0:T(8,128)(2,1)S(1)} %collective-permute-done.2.rest_1_, ...), custom_call_target="tpu_custom_call" | custom-call | flops 805306368 | bytes 3145728 | tf_op jit(solution)/shard_map/sum/pallas_call | solution.py:439
  25.5 0.9 %collective-permute-done.8.other_ref = f32[8,128]{1,0:T(8,128)S(1)} collective-permute-done((f32[8,128]{1,0:T(8,128)S(1)}, f32[8,128]{1,0:T(8,128)S(1)}, u32[]{:S(2)}, u32[]{:S(2)}) %collective-permute-start.8) | collective-permute-done | bytes 4128 | tf_op jit(solution)/shard_map/ppermute | solution.py:343
  26.4 2.5 %collective-permute-start.10 = (f32[8,128]{1,0:T(8,128)S(1)}, f32[8,128]{1,0:T(8,128)S(1)}, u32[]{:S(2)}, u32[]{:S(2)}) collective-permute-start(f32[8,128]{1,0:T(8,128)S(1)} %merge.1.rest_2_), channel_id=1, source_target_pairs={{0,3},{1,2},{2,1},{3,0},{16,19},{17,18},{18,17},{19,16},{4,7},{5,6... | collective-permute-start | bytes 12296 | tf_op jit(solution)/shard_map/ppermute | solution.py:343
  28.9 0.2 collective-permute-start.9
  29.2 0.1 score.5.rest_1_.rest_2_
  29.3 1.5 %collective-permute-start.11 = (f32[8,128]{1,0:T(8,128)S(1)}, f32[8,128]{1,0:T(8,128)S(1)}, u32[]{:S(2)}, u32[]{:S(2)}) collective-permute-start(f32[8,128]{1,0:T(8,128)S(1)} %score.5.rest_1_.rest_2_), channel_id=1, source_target_pairs={{0,16},{1,17},{2,18},{3,19},{16,0},{17,1},{18,2},{19,3},{4,20},{5,... | collective-permute-start | bytes 12296 | tf_op jit(solution)/shard_map/ppermute | solution.py:343
  30.8 0.4 %collective-permute-done.5.rest_0_ = bf16[528,128]{1,0:T(8,128)(2,1)S(1)} collective-permute-done((bf16[528,128]{1,0:T(8,128)(2,1)S(1)}, bf16[528,128]{1,0:T(8,128)(2,1)S(1)}, u32[]{:S(2)}, u32[]{:S(2)}) %collective-permute-start.5) | collective-permute-done | bytes 135200 | tf_op jit(solution)/shard_map/ppermute | solution.py:343
  31.3 1.4 %collective-permute-start.13 = (f32[8,128]{1,0:T(8,128)S(1)}, f32[8,128]{1,0:T(8,128)S(1)}, u32[]{:S(2)}, u32[]{:S(2)}) collective-permute-start(f32[8,128]{1,0:T(8,128)S(1)} %score.6.rest_1_), channel_id=1, source_target_pairs={{0,18},{1,19},{2,16},{3,17},{16,2},{17,3},{18,0},{19,1},{4,22},{5,... | collective-permute-start | bytes 12296 | tf_op jit(solution)/shard_map/ppermute | solution.py:343
  32.8 2.0 %collective-permute-start.12 = (f32[8,128]{1,0:T(8,128)S(1)}, f32[8,128]{1,0:T(8,128)S(1)}, u32[]{:S(2)}, u32[]{:S(2)}) collective-permute-start(f32[8,128]{1,0:T(8,128)S(1)} %score.7.rest_3_), channel_id=1, source_target_pairs={{0,2},{1,3},{2,0},{3,1},{16,18},{17,19},{18,16},{19,17},{4,6},{5,7... | collective-permute-start | bytes 12296 | tf_op jit(solution)/shard_map/ppermute | solution.py:343
  34.8 3.2 %update.1 = f32[768,1024]{1,0:T(8,128)} custom-call(bf16[768,256]{1,0:T(8,128)(2,1)S(1)} %bitcast.20, bf16[768,256]{1,0:T(8,128)(2,1)S(1)} %collective-permute-done.other_ref, f32[768,1024]{1,0:T(8,128)S(1)} %sum.1._.grad_ref, f32[768,1024]{1,0:T(8,128)S(1)} %bitcast.16, bf16[768,1024]{1,0:T(8,128)(2,1)S(1)} %bitcast.21, bf16[768,1024]{1,0:T(8,128)(2,1)S(1)} %bitcast.22, ...), custom_call_target="tpu_custom_call" | custom-call | flops 402653184 | bytes 12582912 | tf_op jit(solution)/shard_map/update/pallas_call | solution.py:468
  38.1 0.9 %combine.1 = f32[8,512]{1,0:T(8,128)} custom-call(s32[8,512]{1,0:T(8,128)S(1)} %bitcast.24, f32[16,512]{1,0:T(8,128)S(1)} %get-tuple-element.17.slots_ref, f32[8,128]{1,0:T(8,128)S(1)} %collective-permute-done.9.rest_0_, f32[8,128]{1,0:T(8,128)S(1)} %collective-permute-done.10.rest_1_, f32[8,128]{1,0:T(8,128)S(1)} %score.5.rest_1_.rest_2_, ...), custom_call_target="tpu_custom_call" | custom-call | flops 524288 | bytes 32768 | tf_op jit(solution)/shard_map/combine/pallas_call | solution.py:494
  (24 shorter events, 0.4 us)
Async XLA Ops:
  0.6 12.4 %copy-start.1 = (bf16[1,1,768,256]{3,2,1,0:T(8,128)(2,1)S(1)}, bf16[1,1,768,256]{3,2,1,0:T(8,128)(2,1)}, u32[]{:S(2)}) copy-start(bf16[1,1,768,256]{3,2,1,0:T(8,128)(2,1)} %param.10) | copy-start | bytes 1179652
  0.6 12.4 %collective-permute-start = (bf16[768,256]{1,0:T(8,128)(2,1)}, bf16[768,256]{1,0:T(8,128)(2,1)S(1)}, u32[]{:S(2)}, u32[]{:S(2)}) collective-permute-start(bf16[768,256]{1,0:T(8,128)(2,1)} %bitcast.17), channel_id=1, source_target_pairs={{0,16},{1,17},{2,18},{3,19},{16,0},{17,1},{18,2},{19,3},{4,20},{5,... | collective-permute-start | bytes 1179656 | tf_op jit(solution)/shard_map/ppermute | solution.py:343
  5.7 12.5 %collective-permute-start.1 = (bf16[528,128]{1,0:T(8,128)(2,1)S(1)}, bf16[528,128]{1,0:T(8,128)(2,1)S(1)}, u32[]{:S(2)}, u32[]{:S(2)}) collective-permute-start(bf16[528,128]{1,0:T(8,128)(2,1)S(1)} %get-tuple-element.13), channel_id=1, source_target_pairs={{0,3},{1,2},{2,1},{3,0},{16,19},{17,18},{18,17},{19,16},{4,7},{5,6... | collective-permute-start | bytes 405512 | tf_op jit(solution)/shard_map/ppermute | solution.py:343
  9.3 12.0 %collective-permute-start.2 = (bf16[528,128]{1,0:T(8,128)(2,1)S(1)}, bf16[528,128]{1,0:T(8,128)(2,1)S(1)}, u32[]{:S(2)}, u32[]{:S(2)}) collective-permute-start(bf16[528,128]{1,0:T(8,128)(2,1)S(1)} %get-tuple-element.14), channel_id=1, source_target_pairs={{0,1},{1,0},{2,3},{3,2},{16,17},{17,16},{18,19},{19,18},{4,5},{5,4... | collective-permute-start | bytes 405512 | tf_op jit(solution)/shard_map/ppermute | solution.py:343
  9.3 12.1 %collective-permute-start.3 = (bf16[528,128]{1,0:T(8,128)(2,1)S(1)}, bf16[528,128]{1,0:T(8,128)(2,1)S(1)}, u32[]{:S(2)}, u32[]{:S(2)}) collective-permute-start(bf16[528,128]{1,0:T(8,128)(2,1)S(1)} %get-tuple-element.15), channel_id=1, source_target_pairs={{0,19},{1,18},{2,17},{3,16},{16,3},{17,2},{18,1},{19,0},{4,23},{5,... | collective-permute-start | bytes 405512 | tf_op jit(solution)/shard_map/ppermute | solution.py:343
  10.2 12.3 %collective-permute-start.4 = (bf16[528,128]{1,0:T(8,128)(2,1)S(1)}, bf16[528,128]{1,0:T(8,128)(2,1)S(1)}, u32[]{:S(2)}, u32[]{:S(2)}) collective-permute-start(bf16[528,128]{1,0:T(8,128)(2,1)S(1)} %get-tuple-element.16), channel_id=1, source_target_pairs={{0,17},{1,16},{2,19},{3,18},{16,1},{17,0},{18,3},{19,2},{4,21},{5,... | collective-permute-start | bytes 405512 | tf_op jit(solution)/shard_map/ppermute | solution.py:343
  16.3 12.8 %collective-permute-start.7 = (bf16[528,128]{1,0:T(8,128)(2,1)S(1)}, bf16[528,128]{1,0:T(8,128)(2,1)S(1)}, u32[]{:S(2)}, u32[]{:S(2)}) collective-permute-start(bf16[528,128]{1,0:T(8,128)(2,1)S(1)} %get-tuple-element.23), channel_id=1, source_target_pairs={{0,16},{1,17},{2,18},{3,19},{16,0},{17,1},{18,2},{19,3},{4,20},{5,... | collective-permute-start | bytes 405512 | tf_op jit(solution)/shard_map/ppermute | solution.py:343
  18.1 13.1 %collective-permute-start.5 = (bf16[528,128]{1,0:T(8,128)(2,1)S(1)}, bf16[528,128]{1,0:T(8,128)(2,1)S(1)}, u32[]{:S(2)}, u32[]{:S(2)}) collective-permute-start(bf16[528,128]{1,0:T(8,128)(2,1)S(1)} %get-tuple-element.21), channel_id=1, source_target_pairs={{0,18},{1,19},{2,16},{3,17},{16,2},{17,3},{18,0},{19,1},{4,22},{5,... | collective-permute-start | bytes 405512 | tf_op jit(solution)/shard_map/ppermute | solution.py:343
  21.3 11.4 %collective-permute-start.6 = (bf16[528,128]{1,0:T(8,128)(2,1)S(1)}, bf16[528,128]{1,0:T(8,128)(2,1)S(1)}, u32[]{:S(2)}, u32[]{:S(2)}) collective-permute-start(bf16[528,128]{1,0:T(8,128)(2,1)S(1)} %get-tuple-element.22), channel_id=1, source_target_pairs={{0,2},{1,3},{2,0},{3,1},{16,18},{17,19},{18,16},{19,17},{4,6},{5,7... | collective-permute-start | bytes 405512 | tf_op jit(solution)/shard_map/ppermute | solution.py:343
  22.7 3.7 %collective-permute-start.8 = (f32[8,128]{1,0:T(8,128)S(1)}, f32[8,128]{1,0:T(8,128)S(1)}, u32[]{:S(2)}, u32[]{:S(2)}) collective-permute-start(f32[8,128]{1,0:T(8,128)S(1)} %score.4.rest_5_.own_ref), channel_id=1, source_target_pairs={{0,16},{1,17},{2,18},{3,19},{16,0},{17,1},{18,2},{19,3},{4,20},{5,... | collective-permute-start | bytes 12296 | tf_op jit(solution)/shard_map/ppermute | solution.py:343
  26.4 11.6 %collective-permute-start.10 = (f32[8,128]{1,0:T(8,128)S(1)}, f32[8,128]{1,0:T(8,128)S(1)}, u32[]{:S(2)}, u32[]{:S(2)}) collective-permute-start(f32[8,128]{1,0:T(8,128)S(1)} %merge.1.rest_2_), channel_id=1, source_target_pairs={{0,3},{1,2},{2,1},{3,0},{16,19},{17,18},{18,17},{19,16},{4,7},{5,6... | collective-permute-start | bytes 12296 | tf_op jit(solution)/shard_map/ppermute | solution.py:343
  28.9 9.1 %collective-permute-start.9 = (f32[8,128]{1,0:T(8,128)S(1)}, f32[8,128]{1,0:T(8,128)S(1)}, u32[]{:S(2)}, u32[]{:S(2)}) collective-permute-start(f32[8,128]{1,0:T(8,128)S(1)} %merge.1.rest_2_), channel_id=1, source_target_pairs={{0,1},{1,0},{2,3},{3,2},{16,17},{17,16},{18,19},{19,18},{4,5},{5,4... | collective-permute-start | bytes 12296 | tf_op jit(solution)/shard_map/ppermute | solution.py:343
  29.2 5.7 %copy-start.2 = (bf16[1,1,768,1024]{3,2,1,0:T(8,128)(2,1)S(1)}, bf16[1,1,768,1024]{3,2,1,0:T(8,128)(2,1)}, u32[]{:S(2)}) copy-start(bf16[1,1,768,1024]{3,2,1,0:T(8,128)(2,1)} %param.12) | copy-start | bytes 4718596
  29.2 5.7 %copy-start.3 = (bf16[1,1,768,1024]{3,2,1,0:T(8,128)(2,1)S(1)}, bf16[1,1,768,1024]{3,2,1,0:T(8,128)(2,1)}, u32[]{:S(2)}) copy-start(bf16[1,1,768,1024]{3,2,1,0:T(8,128)(2,1)} %param.13) | copy-start | bytes 4718596
  29.3 5.5 %copy-start = (f32[1,1,768,1024]{3,2,1,0:T(8,128)S(1)}, f32[1,1,768,1024]{3,2,1,0:T(8,128)}, u32[]{:S(2)}) copy-start(f32[1,1,768,1024]{3,2,1,0:T(8,128)} %param.11) | copy-start | bytes 9437188
  29.3 8.8 %collective-permute-start.11 = (f32[8,128]{1,0:T(8,128)S(1)}, f32[8,128]{1,0:T(8,128)S(1)}, u32[]{:S(2)}, u32[]{:S(2)}) collective-permute-start(f32[8,128]{1,0:T(8,128)S(1)} %score.5.rest_1_.rest_2_), channel_id=1, source_target_pairs={{0,16},{1,17},{2,18},{3,19},{16,0},{17,1},{18,2},{19,3},{4,20},{5,... | collective-permute-start | bytes 12296 | tf_op jit(solution)/shard_map/ppermute | solution.py:343
  31.3 6.7 %collective-permute-start.13 = (f32[8,128]{1,0:T(8,128)S(1)}, f32[8,128]{1,0:T(8,128)S(1)}, u32[]{:S(2)}, u32[]{:S(2)}) collective-permute-start(f32[8,128]{1,0:T(8,128)S(1)} %score.6.rest_1_), channel_id=1, source_target_pairs={{0,18},{1,19},{2,16},{3,17},{16,2},{17,3},{18,0},{19,1},{4,22},{5,... | collective-permute-start | bytes 12296 | tf_op jit(solution)/shard_map/ppermute | solution.py:343
  32.8 5.2 %collective-permute-start.12 = (f32[8,128]{1,0:T(8,128)S(1)}, f32[8,128]{1,0:T(8,128)S(1)}, u32[]{:S(2)}, u32[]{:S(2)}) collective-permute-start(f32[8,128]{1,0:T(8,128)S(1)} %score.7.rest_3_), channel_id=1, source_target_pairs={{0,2},{1,3},{2,0},{3,1},{16,18},{17,19},{18,16},{19,17},{4,6},{5,7... | collective-permute-start | bytes 12296 | tf_op jit(solution)/shard_map/ppermute | solution.py:343
  34.8 3.2 %copy-start.4 = (s32[1,512,8]{1,2,0:T(8,128)S(1)}, s32[1,512,8]{1,2,0:T(8,128)}, u32[]{:S(2)}) copy-start(s32[1,512,8]{1,2,0:T(8,128)} %param.9) | copy-start | bytes 49156

commit v27 on v20

--- a/solution.py
+++ b/solution.py
@@ -80,24 +80,19 @@
 
 
 def route_kernel(
-    items, steps, group, cap, ids_hbm, weight_hbm, grads_hbm, slots_ref, tiles_ref, *rest
+    items, steps, group, cap, ids_hbm, weight_ref, grads_hbm, slots_ref, tiles_ref, *rest
 ):
     chunks = dict(zip(items, rest))
-    ids_ref, weight_ref, held, sems = rest[len(items) :]
+    ids_ref, held, sems = rest[len(items) :]
     tokens = held.shape[1]
     me = ep_index()
-    small = [
-        pltpu.make_async_copy(ids_hbm, ids_ref, sems.at[2]),
-        pltpu.make_async_copy(weight_hbm, weight_ref, sems.at[3]),
-    ]
-    for copy in small:
-        copy.start()
+    small = pltpu.make_async_copy(ids_hbm, ids_ref, sems.at[2])
+    small.start()
     copies = start_grads(grads_hbm, held, sems)
     earlier = lax.broadcasted_iota(jnp.int32, (tokens, tokens), 0)
     later = lax.broadcasted_iota(jnp.int32, (tokens, tokens), 1)
     ahead = jnp.where(earlier < later, 1.0, 0.0).astype(BF16)
-    for copy in small:
-        copy.wait()
+    small.wait()
     ids = ids_ref[...]
     weights = weight_ref[...].astype(F32)
     members, scales = [], []
@@ -368,20 +363,19 @@
             jax.ShapeDtypeStruct((group, TILE, LANES), BF16),
         ]
         + [chunk] * len(first_items),
-        in_specs=specs(pltpu.HBM, 3),
+        in_specs=specs(pltpu.HBM, 1) + specs(pltpu.VMEM, 1) + specs(pltpu.HBM, 1),
         out_specs=specs(pltpu.VMEM, 2 + len(first_items)),
         scratch_shapes=[
             pltpu.VMEM((top, tokens), jnp.int32),
-            pltpu.VMEM((top, tokens), BF16),
             held,
-            pltpu.SemaphoreType.DMA((4,)),
+            pltpu.SemaphoreType.DMA((3,)),
         ],
         compiler_params=params(),
         cost_estimate=cost(2 * slots * tokens * width, 2 * (tokens + slots) * width),
         name="route",
     )(
         pltpu.with_memory_space_constraint(ids, pltpu.HBM),
-        pltpu.with_memory_space_constraint(router_weights[0].T, pltpu.HBM),
+        router_weights[0].T,
         grads,
     )
     slot_of, tiles = routed[:2]

time: 39 us -> 39.4 us (1.010)
  starting transfers between devices: 23.3 us -> 22.5 us
  local copies, waits for them, and re-layouts: 0.02 us -> 0.72 us
  waiting for transfers between devices: 3.81 us -> 4.23 us
    ppermute x14, starting transfers between devices: 23.3 us -> 22.5 us  [moved(): return lax.ppermute(array, ('pair', 'ep'), pairs)]
    unnamed x10 -> x12, local copies, waits for them, and re-layouts: 0.02 us -> 0.72 us
    ppermute x14, waiting for transfers between devices: 3.81 us -> 4.23 us  [moved(): return lax.ppermute(array, ('pair', 'ep'), pairs)]
where the time goes in v27:
time: 39.4 us; the launch traced here: 39.1 us
  starting transfers between devices  22.5 us (57%)
  Pallas kernels  11 us (28%)
  waiting for transfers between devices  4.23 us (11%)
  local copies, waits for them, and re-layouts  0.72 us (2%)
  between operations  0.72 us (2%)
    ppermute x14, starting transfers between devices, moved(): return lax.ppermute(array, ('pair', 'ep'), pairs)  22.5 us
    ppermute x14, waiting for transfers between devices, moved(): return lax.ppermute(array, ('pair', 'ep'), pairs)  4.23 us
    pallas_call x1, Pallas kernels, local(): pl.pallas_call(functools.partial(later_kernel, last_items, late, cap), ou...  3.33 us
    pallas_call x1, Pallas kernels, local(): pl.pallas_call(functools.partial(update_kernel, added, cap), out_shape=ja...  3.08 us
    pallas_call x1, Pallas kernels, local(): pl.pallas_call(functools.partial(route_kernel, first_items, first, group,...  1.96 us
    pallas_call x1, Pallas kernels, local(): pl.pallas_call(functools.partial(sum_kernel, summed, group, cap), out_sha...  1.12 us
    pallas_call x1, Pallas kernels, local(): pl.pallas_call(functools.partial(combine_kernel, [(k, len(arrays)) for k,...  0.87 us
  transfers between devices with their start and end apart: 14, of which 4 were waited for; matrix products, arithmetic and copies ran while one was open for 0% of the time, Pallas kernels for 26%

profile of v27, /device:TPU:0, one launch (start us, length us, event | category | flops | bytes accessed | tf_op | source)
XLA Modules:
  0.0 39.1 jit_solution(9977770510375416455)
XLA Ops:
  0.6 3.0 %collective-permute-start = (bf16[768,256]{1,0:T(8,128)(2,1)}, bf16[768,256]{1,0:T(8,128)(2,1)S(1)}, u32[]{:S(2)}, u32[]{:S(2)}) collective-permute-start(bf16[768,256]{1,0:T(8,128)(2,1)} %bitcast.17), channel_id=1, source_target_pairs={{0,16},{1,17},{2,18},{3,19},{16,0},{17,1},{18,2},{19,3},{4,20},{5,... | collective-permute-start | bytes 1179656 | tf_op jit(solution)/shard_map/ppermute | solution.py:335
  3.7 0.7 %copy-done.5 = bf16[1,512,8]{1,2,0:T(8,128)(2,1)S(1)} copy-done((bf16[1,512,8]{1,2,0:T(8,128)(2,1)S(1)}, bf16[1,512,8]{1,2,0:T(8,128)(2,1)}, u32[]{:S(2)}) %copy-start.5) | copy-done | bytes 8216
  4.4 2.0 %route.1 = (f32[16,512]{1,0:T(8,128)S(1)}, bf16[4,16,128]{2,1,0:T(8,128)(2,1)S(1)}, bf16[528,128]{1,0:T(8,128)(2,1)S(1)}, bf16[528,128]{1,0:T(8,128)(2,1)S(1)}, ...) custom-call(s32[8,512]{1,0:T(8,128)} %bitcast.23, bf16[8,512]{1,0:T(8,128)(2,1)S(1)} %bitcast.25, ...), custom_call_target="tpu_custom_call" | custom-call | flops 536870912 | bytes 3145728 | tf_op jit(solution)/shard_map/route/pallas_call | solution.py:359
  6.3 3.7 %collective-permute-start.1 = (bf16[528,128]{1,0:T(8,128)(2,1)S(1)}, bf16[528,128]{1,0:T(8,128)(2,1)S(1)}, u32[]{:S(2)}, u32[]{:S(2)}) collective-permute-start(bf16[528,128]{1,0:T(8,128)(2,1)S(1)} %get-tuple-element.13), channel_id=1, source_target_pairs={{0,3},{1,2},{2,1},{3,0},{16,19},{17,18},{18,17},{19,16},{4,7},{5,6... | collective-permute-start | bytes 405512 | tf_op jit(solution)/shard_map/ppermute | solution.py:335
  10.0 0.8 %collective-permute-start.3 = (bf16[528,128]{1,0:T(8,128)(2,1)S(1)}, bf16[528,128]{1,0:T(8,128)(2,1)S(1)}, u32[]{:S(2)}, u32[]{:S(2)}) collective-permute-start(bf16[528,128]{1,0:T(8,128)(2,1)S(1)} %get-tuple-element.15), channel_id=1, source_target_pairs={{0,19},{1,18},{2,17},{3,16},{16,3},{17,2},{18,1},{19,0},{4,23},{5,... | collective-permute-start | bytes 405512 | tf_op jit(solution)/shard_map/ppermute | solution.py:335
  10.9 1.4 %collective-permute-start.4 = (bf16[528,128]{1,0:T(8,128)(2,1)S(1)}, bf16[528,128]{1,0:T(8,128)(2,1)S(1)}, u32[]{:S(2)}, u32[]{:S(2)}) collective-permute-start(bf16[528,128]{1,0:T(8,128)(2,1)S(1)} %get-tuple-element.16), channel_id=1, source_target_pairs={{0,17},{1,16},{2,19},{3,18},{16,1},{17,0},{18,3},{19,2},{4,21},{5,... | collective-permute-start | bytes 405512 | tf_op jit(solution)/shard_map/ppermute | solution.py:335
  12.3 0.7 %collective-permute-done.other_ref = bf16[768,256]{1,0:T(8,128)(2,1)S(1)} collective-permute-done((bf16[768,256]{1,0:T(8,128)(2,1)}, bf16[768,256]{1,0:T(8,128)(2,1)S(1)}, u32[]{:S(2)}, u32[]{:S(2)}) %collective-permute-start) | collective-permute-done | bytes 393248 | tf_op jit(solution)/shard_map/ppermute | solution.py:335
  13.0 3.3 %later.1 = (f32[512,1024]{1,0:T(8,128)S(1)}, bf16[528,128]{1,0:T(8,128)(2,1)S(1)}, bf16[528,128]{1,0:T(8,128)(2,1)S(1)}, bf16[528,128]{1,0:T(8,128)(2,1)S(1)}, bf16[528,128]{1,0:T(8,128)(2,1)S(1)}) custom-call(f32[16,512]{1,0:T(8,128)S(1)} %get-tuple-element.17.slots_ref, bf16[4,16,128]{2,1,0:T(8,128)(2,1)S(1)} %get-tuple-element.18.tiles_ref, ...), custom_call_target="tpu_custom_call" | custom-call | flops 1342177280 | bytes 3145728 | tf_op jit(solution)/shard_map/later/pallas_call | solution.py:384
  16.3 1.8 %collective-permute-start.7 = (bf16[528,128]{1,0:T(8,128)(2,1)S(1)}, bf16[528,128]{1,0:T(8,128)(2,1)S(1)}, u32[]{:S(2)}, u32[]{:S(2)}) collective-permute-start(bf16[528,128]{1,0:T(8,128)(2,1)S(1)} %get-tuple-element.23), channel_id=1, source_target_pairs={{0,16},{1,17},{2,18},{3,19},{16,0},{17,1},{18,2},{19,3},{4,20},{5,... | collective-permute-start | bytes 405512 | tf_op jit(solution)/shard_map/ppermute | solution.py:335
  18.1 2.9 %collective-permute-start.5 = (bf16[528,128]{1,0:T(8,128)(2,1)S(1)}, bf16[528,128]{1,0:T(8,128)(2,1)S(1)}, u32[]{:S(2)}, u32[]{:S(2)}) collective-permute-start(bf16[528,128]{1,0:T(8,128)(2,1)S(1)} %get-tuple-element.21), channel_id=1, source_target_pairs={{0,18},{1,19},{2,16},{3,17},{16,2},{17,3},{18,0},{19,1},{4,22},{5,... | collective-permute-start | bytes 405512 | tf_op jit(solution)/shard_map/ppermute | solution.py:335
  21.1 0.1 collective-permute-start.6
  21.2 2.1 %collective-permute-done.4.rest_3_ = bf16[528,128]{1,0:T(8,128)(2,1)S(1)} collective-permute-done((bf16[528,128]{1,0:T(8,128)(2,1)S(1)}, bf16[528,128]{1,0:T(8,128)(2,1)S(1)}, u32[]{:S(2)}, u32[]{:S(2)}) %collective-permute-start.4) | collective-permute-done | bytes 135200 | tf_op jit(solution)/shard_map/ppermute | solution.py:335
  23.4 0.2 score.4.rest_5_.own_ref
  23.6 1.3 %collective-permute-start.8 = (f32[8,128]{1,0:T(8,128)S(1)}, f32[8,128]{1,0:T(8,128)S(1)}, u32[]{:S(2)}, u32[]{:S(2)}) collective-permute-start(f32[8,128]{1,0:T(8,128)S(1)} %score.4.rest_5_.own_ref), channel_id=1, source_target_pairs={{0,16},{1,17},{2,18},{3,19},{16,0},{17,1},{18,2},{19,3},{4,20},{5,... | collective-permute-start | bytes 12296 | tf_op jit(solution)/shard_map/ppermute | solution.py:335
  24.9 1.1 %sum.1._.grad_ref = f32[768,1024]{1,0:T(8,128)S(1)} custom-call(bf16[768,256]{1,0:T(8,128)(2,1)S(1)} %bitcast.19, bf16[768,256]{1,0:T(8,128)(2,1)S(1)} %collective-permute-done.other_ref, bf16[528,128]{1,0:T(8,128)(2,1)S(1)} %collective-permute-done.1.rest_0_, bf16[528,128]{1,0:T(8,128)(2,1)S(1)} %collective-permute-done.2.rest_1_, ...), custom_call_target="tpu_custom_call" | custom-call | flops 805306368 | bytes 3145728 | tf_op jit(solution)/shard_map/sum/pallas_call | solution.py:430
  26.0 1.2 %collective-permute-done.8.other_ref = f32[8,128]{1,0:T(8,128)S(1)} collective-permute-done((f32[8,128]{1,0:T(8,128)S(1)}, f32[8,128]{1,0:T(8,128)S(1)}, u32[]{:S(2)}, u32[]{:S(2)}) %collective-permute-start.8) | collective-permute-done | bytes 4128 | tf_op jit(solution)/shard_map/ppermute | solution.py:335
  27.3 1.4 %collective-permute-start.10 = (f32[8,128]{1,0:T(8,128)S(1)}, f32[8,128]{1,0:T(8,128)S(1)}, u32[]{:S(2)}, u32[]{:S(2)}) collective-permute-start(f32[8,128]{1,0:T(8,128)S(1)} %merge.1.rest_2_), channel_id=1, source_target_pairs={{0,3},{1,2},{2,1},{3,0},{16,19},{17,18},{18,17},{19,16},{4,7},{5,6... | collective-permute-start | bytes 12296 | tf_op jit(solution)/shard_map/ppermute | solution.py:335
  28.7 1.1 %collective-permute-start.9 = (f32[8,128]{1,0:T(8,128)S(1)}, f32[8,128]{1,0:T(8,128)S(1)}, u32[]{:S(2)}, u32[]{:S(2)}) collective-permute-start(f32[8,128]{1,0:T(8,128)S(1)} %merge.1.rest_2_), channel_id=1, source_target_pairs={{0,1},{1,0},{2,3},{3,2},{16,17},{17,16},{18,19},{19,18},{4,5},{5,4... | collective-permute-start | bytes 12296 | tf_op jit(solution)/shard_map/ppermute | solution.py:335
  30.0 1.5 %collective-permute-start.11 = (f32[8,128]{1,0:T(8,128)S(1)}, f32[8,128]{1,0:T(8,128)S(1)}, u32[]{:S(2)}, u32[]{:S(2)}) collective-permute-start(f32[8,128]{1,0:T(8,128)S(1)} %score.5.rest_1_.rest_2_), channel_id=1, source_target_pairs={{0,16},{1,17},{2,18},{3,19},{16,0},{17,1},{18,2},{19,3},{4,20},{5,... | collective-permute-start | bytes 12296 | tf_op jit(solution)/shard_map/ppermute | solution.py:335
  31.6 1.9 %collective-permute-start.13 = (f32[8,128]{1,0:T(8,128)S(1)}, f32[8,128]{1,0:T(8,128)S(1)}, u32[]{:S(2)}, u32[]{:S(2)}) collective-permute-start(f32[8,128]{1,0:T(8,128)S(1)} %score.6.rest_1_), channel_id=1, source_target_pairs={{0,18},{1,19},{2,16},{3,17},{16,2},{17,3},{18,0},{19,1},{4,22},{5,... | collective-permute-start | bytes 12296 | tf_op jit(solution)/shard_map/ppermute | solution.py:335
  33.7 1.3 %collective-permute-start.12 = (f32[8,128]{1,0:T(8,128)S(1)}, f32[8,128]{1,0:T(8,128)S(1)}, u32[]{:S(2)}, u32[]{:S(2)}) collective-permute-start(f32[8,128]{1,0:T(8,128)S(1)} %score.7.rest_3_), channel_id=1, source_target_pairs={{0,2},{1,3},{2,0},{3,1},{16,18},{17,19},{18,16},{19,17},{4,6},{5,7... | collective-permute-start | bytes 12296 | tf_op jit(solution)/shard_map/ppermute | solution.py:335
  35.0 3.1 %update.1 = f32[768,1024]{1,0:T(8,128)} custom-call(bf16[768,256]{1,0:T(8,128)(2,1)S(1)} %bitcast.20, bf16[768,256]{1,0:T(8,128)(2,1)S(1)} %collective-permute-done.other_ref, f32[768,1024]{1,0:T(8,128)S(1)} %sum.1._.grad_ref, f32[768,1024]{1,0:T(8,128)S(1)} %bitcast.16, bf16[768,1024]{1,0:T(8,128)(2,1)S(1)} %bitcast.21, bf16[768,1024]{1,0:T(8,128)(2,1)S(1)} %bitcast.22, ...), custom_call_target="tpu_custom_call" | custom-call | flops 402653184 | bytes 12582912 | tf_op jit(solution)/shard_map/update/pallas_call | solution.py:459
  38.1 0.1 collective-permute-done.12.rest_4_
  38.3 0.9 %combine.1 = f32[8,512]{1,0:T(8,128)} custom-call(s32[8,512]{1,0:T(8,128)S(1)} %bitcast.24, f32[16,512]{1,0:T(8,128)S(1)} %get-tuple-element.17.slots_ref, f32[8,128]{1,0:T(8,128)S(1)} %collective-permute-done.9.rest_0_, f32[8,128]{1,0:T(8,128)S(1)} %collective-permute-done.10.rest_1_, f32[8,128]{1,0:T(8,128)S(1)} %score.5.rest_1_.rest_2_, ...), custom_call_target="tpu_custom_call" | custom-call | flops 524288 | bytes 32768 | tf_op jit(solution)/shard_map/combine/pallas_call | solution.py:485
  (26 shorter events, 0.5 us)
Async XLA Ops:
  0.6 12.4 %copy-start.1 = (bf16[1,1,768,256]{3,2,1,0:T(8,128)(2,1)S(1)}, bf16[1,1,768,256]{3,2,1,0:T(8,128)(2,1)}, u32[]{:S(2)}) copy-start(bf16[1,1,768,256]{3,2,1,0:T(8,128)(2,1)} %param.10) | copy-start | bytes 1179652
  0.6 12.4 %collective-permute-start = (bf16[768,256]{1,0:T(8,128)(2,1)}, bf16[768,256]{1,0:T(8,128)(2,1)S(1)}, u32[]{:S(2)}, u32[]{:S(2)}) collective-permute-start(bf16[768,256]{1,0:T(8,128)(2,1)} %bitcast.17), channel_id=1, source_target_pairs={{0,16},{1,17},{2,18},{3,19},{16,0},{17,1},{18,2},{19,3},{4,20},{5,... | collective-permute-start | bytes 1179656 | tf_op jit(solution)/shard_map/ppermute | solution.py:335
  3.7 0.7 %copy-start.5 = (bf16[1,512,8]{1,2,0:T(8,128)(2,1)S(1)}, bf16[1,512,8]{1,2,0:T(8,128)(2,1)}, u32[]{:S(2)}) copy-start(bf16[1,512,8]{1,2,0:T(8,128)(2,1)} %param.8) | copy-start | bytes 24580
  6.3 11.8 %collective-permute-start.1 = (bf16[528,128]{1,0:T(8,128)(2,1)S(1)}, bf16[528,128]{1,0:T(8,128)(2,1)S(1)}, u32[]{:S(2)}, u32[]{:S(2)}) collective-permute-start(bf16[528,128]{1,0:T(8,128)(2,1)S(1)} %get-tuple-element.13), channel_id=1, source_target_pairs={{0,3},{1,2},{2,1},{3,0},{16,19},{17,18},{18,17},{19,16},{4,7},{5,6... | collective-permute-start | bytes 405512 | tf_op jit(solution)/shard_map/ppermute | solution.py:335
  10.0 11.1 %collective-permute-start.2 = (bf16[528,128]{1,0:T(8,128)(2,1)S(1)}, bf16[528,128]{1,0:T(8,128)(2,1)S(1)}, u32[]{:S(2)}, u32[]{:S(2)}) collective-permute-start(bf16[528,128]{1,0:T(8,128)(2,1)S(1)} %get-tuple-element.14), channel_id=1, source_target_pairs={{0,1},{1,0},{2,3},{3,2},{16,17},{17,16},{18,19},{19,18},{4,5},{5,4... | collective-permute-start | bytes 405512 | tf_op jit(solution)/shard_map/ppermute | solution.py:335
  10.0 11.2 %collective-permute-start.3 = (bf16[528,128]{1,0:T(8,128)(2,1)S(1)}, bf16[528,128]{1,0:T(8,128)(2,1)S(1)}, u32[]{:S(2)}, u32[]{:S(2)}) collective-permute-start(bf16[528,128]{1,0:T(8,128)(2,1)S(1)} %get-tuple-element.15), channel_id=1, source_target_pairs={{0,19},{1,18},{2,17},{3,16},{16,3},{17,2},{18,1},{19,0},{4,23},{5,... | collective-permute-start | bytes 405512 | tf_op jit(solution)/shard_map/ppermute | solution.py:335
  10.9 12.5 %collective-permute-start.4 = (bf16[528,128]{1,0:T(8,128)(2,1)S(1)}, bf16[528,128]{1,0:T(8,128)(2,1)S(1)}, u32[]{:S(2)}, u32[]{:S(2)}) collective-permute-start(bf16[528,128]{1,0:T(8,128)(2,1)S(1)} %get-tuple-element.16), channel_id=1, source_target_pairs={{0,17},{1,16},{2,19},{3,18},{16,1},{17,0},{18,3},{19,2},{4,21},{5,... | collective-permute-start | bytes 405512 | tf_op jit(solution)/shard_map/ppermute | solution.py:335
  16.3 13.5 %collective-permute-start.7 = (bf16[528,128]{1,0:T(8,128)(2,1)S(1)}, bf16[528,128]{1,0:T(8,128)(2,1)S(1)}, u32[]{:S(2)}, u32[]{:S(2)}) collective-permute-start(bf16[528,128]{1,0:T(8,128)(2,1)S(1)} %get-tuple-element.23), channel_id=1, source_target_pairs={{0,16},{1,17},{2,18},{3,19},{16,0},{17,1},{18,2},{19,3},{4,20},{5,... | collective-permute-start | bytes 405512 | tf_op jit(solution)/shard_map/ppermute | solution.py:335
  18.1 13.4 %collective-permute-start.5 = (bf16[528,128]{1,0:T(8,128)(2,1)S(1)}, bf16[528,128]{1,0:T(8,128)(2,1)S(1)}, u32[]{:S(2)}, u32[]{:S(2)}) collective-permute-start(bf16[528,128]{1,0:T(8,128)(2,1)S(1)} %get-tuple-element.21), channel_id=1, source_target_pairs={{0,18},{1,19},{2,16},{3,17},{16,2},{17,3},{18,0},{19,1},{4,22},{5,... | collective-permute-start | bytes 405512 | tf_op jit(solution)/shard_map/ppermute | solution.py:335
  21.1 12.5 %collective-permute-start.6 = (bf16[528,128]{1,0:T(8,128)(2,1)S(1)}, bf16[528,128]{1,0:T(8,128)(2,1)S(1)}, u32[]{:S(2)}, u32[]{:S(2)}) collective-permute-start(bf16[528,128]{1,0:T(8,128)(2,1)S(1)} %get-tuple-element.22), channel_id=1, source_target_pairs={{0,2},{1,3},{2,0},{3,1},{16,18},{17,19},{18,16},{19,17},{4,6},{5,7... | collective-permute-start | bytes 405512 | tf_op jit(solution)/shard_map/ppermute | solution.py:335
  23.6 3.7 %collective-permute-start.8 = (f32[8,128]{1,0:T(8,128)S(1)}, f32[8,128]{1,0:T(8,128)S(1)}, u32[]{:S(2)}, u32[]{:S(2)}) collective-permute-start(f32[8,128]{1,0:T(8,128)S(1)} %score.4.rest_5_.own_ref), channel_id=1, source_target_pairs={{0,16},{1,17},{2,18},{3,19},{16,0},{17,1},{18,2},{19,3},{4,20},{5,... | collective-permute-start | bytes 12296 | tf_op jit(solution)/shard_map/ppermute | solution.py:335
  27.3 10.8 %collective-permute-start.10 = (f32[8,128]{1,0:T(8,128)S(1)}, f32[8,128]{1,0:T(8,128)S(1)}, u32[]{:S(2)}, u32[]{:S(2)}) collective-permute-start(f32[8,128]{1,0:T(8,128)S(1)} %merge.1.rest_2_), channel_id=1, source_target_pairs={{0,3},{1,2},{2,1},{3,0},{16,19},{17,18},{18,17},{19,16},{4,7},{5,6... | collective-permute-start | bytes 12296 | tf_op jit(solution)/shard_map/ppermute | solution.py:335
  28.7 9.4 %collective-permute-start.9 = (f32[8,128]{1,0:T(8,128)S(1)}, f32[8,128]{1,0:T(8,128)S(1)}, u32[]{:S(2)}, u32[]{:S(2)}) collective-permute-start(f32[8,128]{1,0:T(8,128)S(1)} %merge.1.rest_2_), channel_id=1, source_target_pairs={{0,1},{1,0},{2,3},{3,2},{16,17},{17,16},{18,19},{19,18},{4,5},{5,4... | collective-permute-start | bytes 12296 | tf_op jit(solution)/shard_map/ppermute | solution.py:335
  29.8 5.1 %copy-start.2 = (bf16[1,1,768,1024]{3,2,1,0:T(8,128)(2,1)S(1)}, bf16[1,1,768,1024]{3,2,1,0:T(8,128)(2,1)}, u32[]{:S(2)}) copy-start(bf16[1,1,768,1024]{3,2,1,0:T(8,128)(2,1)} %param.12) | copy-start | bytes 4718596
  29.8 5.1 %copy-start.3 = (bf16[1,1,768,1024]{3,2,1,0:T(8,128)(2,1)S(1)}, bf16[1,1,768,1024]{3,2,1,0:T(8,128)(2,1)}, u32[]{:S(2)}) copy-start(bf16[1,1,768,1024]{3,2,1,0:T(8,128)(2,1)} %param.13) | copy-start | bytes 4718596
  30.0 5.0 %copy-start = (f32[1,1,768,1024]{3,2,1,0:T(8,128)S(1)}, f32[1,1,768,1024]{3,2,1,0:T(8,128)}, u32[]{:S(2)}) copy-start(f32[1,1,768,1024]{3,2,1,0:T(8,128)} %param.11) | copy-start | bytes 9437188
  30.0 8.3 %collective-permute-start.11 = (f32[8,128]{1,0:T(8,128)S(1)}, f32[8,128]{1,0:T(8,128)S(1)}, u32[]{:S(2)}, u32[]{:S(2)}) collective-permute-start(f32[8,128]{1,0:T(8,128)S(1)} %score.5.rest_1_.rest_2_), channel_id=1, source_target_pairs={{0,16},{1,17},{2,18},{3,19},{16,0},{17,1},{18,2},{19,3},{4,20},{5,... | collective-permute-start | bytes 12296 | tf_op jit(solution)/shard_map/ppermute | solution.py:335
  31.6 6.6 %collective-permute-start.13 = (f32[8,128]{1,0:T(8,128)S(1)}, f32[8,128]{1,0:T(8,128)S(1)}, u32[]{:S(2)}, u32[]{:S(2)}) collective-permute-start(f32[8,128]{1,0:T(8,128)S(1)} %score.6.rest_1_), channel_id=1, source_target_pairs={{0,18},{1,19},{2,16},{3,17},{16,2},{17,3},{18,0},{19,1},{4,22},{5,... | collective-permute-start | bytes 12296 | tf_op jit(solution)/shard_map/ppermute | solution.py:335
  33.7 4.6 %collective-permute-start.12 = (f32[8,128]{1,0:T(8,128)S(1)}, f32[8,128]{1,0:T(8,128)S(1)}, u32[]{:S(2)}, u32[]{:S(2)}) collective-permute-start(f32[8,128]{1,0:T(8,128)S(1)} %score.7.rest_3_), channel_id=1, source_target_pairs={{0,2},{1,3},{2,0},{3,1},{16,18},{17,19},{18,16},{19,17},{4,6},{5,7... | collective-permute-start | bytes 12296 | tf_op jit(solution)/shard_map/ppermute | solution.py:335
  35.0 3.3 %copy-start.4 = (s32[1,512,8]{1,2,0:T(8,128)S(1)}, s32[1,512,8]{1,2,0:T(8,128)}, u32[]{:S(2)}) copy-start(s32[1,512,8]{1,2,0:T(8,128)} %param.9) | copy-start | bytes 49156

commit v28 on v20

--- a/solution.py
+++ b/solution.py
@@ -228,7 +228,7 @@
     chunks = rest[: len(items)]
     _, update_hbm, rows, scaled, total, update, sems = rest[len(items) :]
     hid, half = update.shape
-    width = min(half, 4 * LANES)
+    width = min(half, 2 * LANES)
     height = 2 * TILE
     data_rows = half // LANES * cap
     me = ep_index()

time: 39 us -> 39 us (level)
  no operation moved by 1% of the time
where the time goes in v28:
time: 39 us; the launch traced here: 38.8 us
  starting transfers between devices  23.3 us (60%)
  Pallas kernels  11 us (28%)
  waiting for transfers between devices  3.81 us (10%)
  between operations  0.75 us (2%)
    ppermute x14, starting transfers between devices, moved(): return lax.ppermute(array, ('pair', 'ep'), pairs)  23.3 us
    ppermute x14, waiting for transfers between devices, moved(): return lax.ppermute(array, ('pair', 'ep'), pairs)  3.81 us
    pallas_call x1, Pallas kernels, local(): pl.pallas_call(functools.partial(later_kernel, last_items, late, cap), ou...  3.33 us
    pallas_call x1, Pallas kernels, local(): pl.pallas_call(functools.partial(update_kernel, added, cap), out_shape=ja...  3.07 us
    pallas_call x1, Pallas kernels, local(): pl.pallas_call(functools.partial(route_kernel, first_items, first, group,...  1.99 us
    pallas_call x1, Pallas kernels, local(): pl.pallas_call(functools.partial(sum_kernel, summed, group, cap), out_sha...  1.12 us
    pallas_call x1, Pallas kernels, local(): pl.pallas_call(functools.partial(combine_kernel, [(k, len(arrays)) for k,...  0.87 us
  transfers between devices with their start and end apart: 14, of which 4 were waited for; matrix products, arithmetic and copies ran while one was open for 0% of the time, Pallas kernels for 26%

profile of v28, /device:TPU:0, one launch (start us, length us, event | category | flops | bytes accessed | tf_op | source)
XLA Modules:
  0.0 38.8 jit_solution(17229964916904607512)
XLA Ops:
  0.6 3.0 %collective-permute-start = (bf16[768,256]{1,0:T(8,128)(2,1)}, bf16[768,256]{1,0:T(8,128)(2,1)S(1)}, u32[]{:S(2)}, u32[]{:S(2)}) collective-permute-start(bf16[768,256]{1,0:T(8,128)(2,1)} %bitcast.17), channel_id=1, source_target_pairs={{0,16},{1,17},{2,18},{3,19},{16,0},{17,1},{18,2},{19,3},{4,20},{5,... | collective-permute-start | bytes 1179656 | tf_op jit(solution)/shard_map/ppermute | solution.py:340
  3.7 2.0 %route.1 = (f32[16,512]{1,0:T(8,128)S(1)}, bf16[4,16,128]{2,1,0:T(8,128)(2,1)S(1)}, bf16[528,128]{1,0:T(8,128)(2,1)S(1)}, bf16[528,128]{1,0:T(8,128)(2,1)S(1)}, ...) custom-call(s32[8,512]{1,0:T(8,128)} %bitcast.23, bf16[8,512]{1,0:T(8,128)(2,1)} %bitcast.29, ...), custom_call_target="tpu_custom_call" | custom-call | flops 536870912 | bytes 3145728 | tf_op jit(solution)/shard_map/route/pallas_call | solution.py:364
  5.7 3.7 %collective-permute-start.1 = (bf16[528,128]{1,0:T(8,128)(2,1)S(1)}, bf16[528,128]{1,0:T(8,128)(2,1)S(1)}, u32[]{:S(2)}, u32[]{:S(2)}) collective-permute-start(bf16[528,128]{1,0:T(8,128)(2,1)S(1)} %get-tuple-element.13), channel_id=1, source_target_pairs={{0,3},{1,2},{2,1},{3,0},{16,19},{17,18},{18,17},{19,16},{4,7},{5,6... | collective-permute-start | bytes 405512 | tf_op jit(solution)/shard_map/ppermute | solution.py:340
  9.3 0.8 %collective-permute-start.3 = (bf16[528,128]{1,0:T(8,128)(2,1)S(1)}, bf16[528,128]{1,0:T(8,128)(2,1)S(1)}, u32[]{:S(2)}, u32[]{:S(2)}) collective-permute-start(bf16[528,128]{1,0:T(8,128)(2,1)S(1)} %get-tuple-element.15), channel_id=1, source_target_pairs={{0,19},{1,18},{2,17},{3,16},{16,3},{17,2},{18,1},{19,0},{4,23},{5,... | collective-permute-start | bytes 405512 | tf_op jit(solution)/shard_map/ppermute | solution.py:340
  10.2 1.4 %collective-permute-start.4 = (bf16[528,128]{1,0:T(8,128)(2,1)S(1)}, bf16[528,128]{1,0:T(8,128)(2,1)S(1)}, u32[]{:S(2)}, u32[]{:S(2)}) collective-permute-start(bf16[528,128]{1,0:T(8,128)(2,1)S(1)} %get-tuple-element.16), channel_id=1, source_target_pairs={{0,17},{1,16},{2,19},{3,18},{16,1},{17,0},{18,3},{19,2},{4,21},{5,... | collective-permute-start | bytes 405512 | tf_op jit(solution)/shard_map/ppermute | solution.py:340
  11.6 1.4 %collective-permute-done.other_ref = bf16[768,256]{1,0:T(8,128)(2,1)S(1)} collective-permute-done((bf16[768,256]{1,0:T(8,128)(2,1)}, bf16[768,256]{1,0:T(8,128)(2,1)S(1)}, u32[]{:S(2)}, u32[]{:S(2)}) %collective-permute-start) | collective-permute-done | bytes 393248 | tf_op jit(solution)/shard_map/ppermute | solution.py:340
  13.0 3.3 %later.1 = (f32[512,1024]{1,0:T(8,128)S(1)}, bf16[528,128]{1,0:T(8,128)(2,1)S(1)}, bf16[528,128]{1,0:T(8,128)(2,1)S(1)}, bf16[528,128]{1,0:T(8,128)(2,1)S(1)}, bf16[528,128]{1,0:T(8,128)(2,1)S(1)}) custom-call(f32[16,512]{1,0:T(8,128)S(1)} %get-tuple-element.17.slots_ref, bf16[4,16,128]{2,1,0:T(8,128)(2,1)S(1)} %get-tuple-element.18.tiles_ref, ...), custom_call_target="tpu_custom_call" | custom-call | flops 1342177280 | bytes 3145728 | tf_op jit(solution)/shard_map/later/pallas_call | solution.py:390
  16.3 1.8 %collective-permute-start.7 = (bf16[528,128]{1,0:T(8,128)(2,1)S(1)}, bf16[528,128]{1,0:T(8,128)(2,1)S(1)}, u32[]{:S(2)}, u32[]{:S(2)}) collective-permute-start(bf16[528,128]{1,0:T(8,128)(2,1)S(1)} %get-tuple-element.23), channel_id=1, source_target_pairs={{0,16},{1,17},{2,18},{3,19},{16,0},{17,1},{18,2},{19,3},{4,20},{5,... | collective-permute-start | bytes 405512 | tf_op jit(solution)/shard_map/ppermute | solution.py:340
  18.1 3.2 %collective-permute-start.5 = (bf16[528,128]{1,0:T(8,128)(2,1)S(1)}, bf16[528,128]{1,0:T(8,128)(2,1)S(1)}, u32[]{:S(2)}, u32[]{:S(2)}) collective-permute-start(bf16[528,128]{1,0:T(8,128)(2,1)S(1)} %get-tuple-element.21), channel_id=1, source_target_pairs={{0,18},{1,19},{2,16},{3,17},{16,2},{17,3},{18,0},{19,1},{4,22},{5,... | collective-permute-start | bytes 405512 | tf_op jit(solution)/shard_map/ppermute | solution.py:340
  21.3 0.1 collective-permute-start.6
  21.5 1.0 %collective-permute-done.4.rest_3_ = bf16[528,128]{1,0:T(8,128)(2,1)S(1)} collective-permute-done((bf16[528,128]{1,0:T(8,128)(2,1)S(1)}, bf16[528,128]{1,0:T(8,128)(2,1)S(1)}, u32[]{:S(2)}, u32[]{:S(2)}) %collective-permute-start.4) | collective-permute-done | bytes 135200 | tf_op jit(solution)/shard_map/ppermute | solution.py:340
  22.5 0.2 score.4.rest_5_.own_ref
  22.7 1.6 %collective-permute-start.8 = (f32[8,128]{1,0:T(8,128)S(1)}, f32[8,128]{1,0:T(8,128)S(1)}, u32[]{:S(2)}, u32[]{:S(2)}) collective-permute-start(f32[8,128]{1,0:T(8,128)S(1)} %score.4.rest_5_.own_ref), channel_id=1, source_target_pairs={{0,16},{1,17},{2,18},{3,19},{16,0},{17,1},{18,2},{19,3},{4,20},{5,... | collective-permute-start | bytes 12296 | tf_op jit(solution)/shard_map/ppermute | solution.py:340
  24.3 1.1 %sum.1._.grad_ref = f32[768,1024]{1,0:T(8,128)S(1)} custom-call(bf16[768,256]{1,0:T(8,128)(2,1)S(1)} %bitcast.19, bf16[768,256]{1,0:T(8,128)(2,1)S(1)} %collective-permute-done.other_ref, bf16[528,128]{1,0:T(8,128)(2,1)S(1)} %collective-permute-done.1.rest_0_, bf16[528,128]{1,0:T(8,128)(2,1)S(1)} %collective-permute-done.2.rest_1_, ...), custom_call_target="tpu_custom_call" | custom-call | flops 805306368 | bytes 3145728 | tf_op jit(solution)/shard_map/sum/pallas_call | solution.py:436
  25.5 0.9 %collective-permute-done.8.other_ref = f32[8,128]{1,0:T(8,128)S(1)} collective-permute-done((f32[8,128]{1,0:T(8,128)S(1)}, f32[8,128]{1,0:T(8,128)S(1)}, u32[]{:S(2)}, u32[]{:S(2)}) %collective-permute-start.8) | collective-permute-done | bytes 4128 | tf_op jit(solution)/shard_map/ppermute | solution.py:340
  26.4 2.5 %collective-permute-start.10 = (f32[8,128]{1,0:T(8,128)S(1)}, f32[8,128]{1,0:T(8,128)S(1)}, u32[]{:S(2)}, u32[]{:S(2)}) collective-permute-start(f32[8,128]{1,0:T(8,128)S(1)} %merge.1.rest_2_), channel_id=1, source_target_pairs={{0,3},{1,2},{2,1},{3,0},{16,19},{17,18},{18,17},{19,16},{4,7},{5,6... | collective-permute-start | bytes 12296 | tf_op jit(solution)/shard_map/ppermute | solution.py:340
  28.9 0.2 collective-permute-start.9
  29.2 0.1 score.5.rest_1_.rest_2_
  29.3 1.5 %collective-permute-start.11 = (f32[8,128]{1,0:T(8,128)S(1)}, f32[8,128]{1,0:T(8,128)S(1)}, u32[]{:S(2)}, u32[]{:S(2)}) collective-permute-start(f32[8,128]{1,0:T(8,128)S(1)} %score.5.rest_1_.rest_2_), channel_id=1, source_target_pairs={{0,16},{1,17},{2,18},{3,19},{16,0},{17,1},{18,2},{19,3},{4,20},{5,... | collective-permute-start | bytes 12296 | tf_op jit(solution)/shard_map/ppermute | solution.py:340
  30.8 0.4 %collective-permute-done.5.rest_0_ = bf16[528,128]{1,0:T(8,128)(2,1)S(1)} collective-permute-done((bf16[528,128]{1,0:T(8,128)(2,1)S(1)}, bf16[528,128]{1,0:T(8,128)(2,1)S(1)}, u32[]{:S(2)}, u32[]{:S(2)}) %collective-permute-start.5) | collective-permute-done | bytes 135200 | tf_op jit(solution)/shard_map/ppermute | solution.py:340
  31.3 1.4 %collective-permute-start.13 = (f32[8,128]{1,0:T(8,128)S(1)}, f32[8,128]{1,0:T(8,128)S(1)}, u32[]{:S(2)}, u32[]{:S(2)}) collective-permute-start(f32[8,128]{1,0:T(8,128)S(1)} %score.6.rest_1_), channel_id=1, source_target_pairs={{0,18},{1,19},{2,16},{3,17},{16,2},{17,3},{18,0},{19,1},{4,22},{5,... | collective-permute-start | bytes 12296 | tf_op jit(solution)/shard_map/ppermute | solution.py:340
  32.8 2.0 %collective-permute-start.12 = (f32[8,128]{1,0:T(8,128)S(1)}, f32[8,128]{1,0:T(8,128)S(1)}, u32[]{:S(2)}, u32[]{:S(2)}) collective-permute-start(f32[8,128]{1,0:T(8,128)S(1)} %score.7.rest_3_), channel_id=1, source_target_pairs={{0,2},{1,3},{2,0},{3,1},{16,18},{17,19},{18,16},{19,17},{4,6},{5,7... | collective-permute-start | bytes 12296 | tf_op jit(solution)/shard_map/ppermute | solution.py:340
  34.8 3.1 %update.1 = f32[768,1024]{1,0:T(8,128)} custom-call(bf16[768,256]{1,0:T(8,128)(2,1)S(1)} %bitcast.20, bf16[768,256]{1,0:T(8,128)(2,1)S(1)} %collective-permute-done.other_ref, f32[768,1024]{1,0:T(8,128)S(1)} %sum.1._.grad_ref, f32[768,1024]{1,0:T(8,128)S(1)} %bitcast.16, bf16[768,1024]{1,0:T(8,128)(2,1)S(1)} %bitcast.21, bf16[768,1024]{1,0:T(8,128)(2,1)S(1)} %bitcast.22, ...), custom_call_target="tpu_custom_call" | custom-call | flops 402653184 | bytes 12582912 | tf_op jit(solution)/shard_map/update/pallas_call | solution.py:465
  38.0 0.9 %combine.1 = f32[8,512]{1,0:T(8,128)} custom-call(s32[8,512]{1,0:T(8,128)S(1)} %bitcast.24, f32[16,512]{1,0:T(8,128)S(1)} %get-tuple-element.17.slots_ref, f32[8,128]{1,0:T(8,128)S(1)} %collective-permute-done.9.rest_0_, f32[8,128]{1,0:T(8,128)S(1)} %collective-permute-done.10.rest_1_, f32[8,128]{1,0:T(8,128)S(1)} %score.5.rest_1_.rest_2_, ...), custom_call_target="tpu_custom_call" | custom-call | flops 524288 | bytes 32768 | tf_op jit(solution)/shard_map/combine/pallas_call | solution.py:491
  (24 shorter events, 0.4 us)
Async XLA Ops:
  0.6 12.4 %copy-start.1 = (bf16[1,1,768,256]{3,2,1,0:T(8,128)(2,1)S(1)}, bf16[1,1,768,256]{3,2,1,0:T(8,128)(2,1)}, u32[]{:S(2)}) copy-start(bf16[1,1,768,256]{3,2,1,0:T(8,128)(2,1)} %param.10) | copy-start | bytes 1179652
  0.6 12.4 %collective-permute-start = (bf16[768,256]{1,0:T(8,128)(2,1)}, bf16[768,256]{1,0:T(8,128)(2,1)S(1)}, u32[]{:S(2)}, u32[]{:S(2)}) collective-permute-start(bf16[768,256]{1,0:T(8,128)(2,1)} %bitcast.17), channel_id=1, source_target_pairs={{0,16},{1,17},{2,18},{3,19},{16,0},{17,1},{18,2},{19,3},{4,20},{5,... | collective-permute-start | bytes 1179656 | tf_op jit(solution)/shard_map/ppermute | solution.py:340
  5.7 12.5 %collective-permute-start.1 = (bf16[528,128]{1,0:T(8,128)(2,1)S(1)}, bf16[528,128]{1,0:T(8,128)(2,1)S(1)}, u32[]{:S(2)}, u32[]{:S(2)}) collective-permute-start(bf16[528,128]{1,0:T(8,128)(2,1)S(1)} %get-tuple-element.13), channel_id=1, source_target_pairs={{0,3},{1,2},{2,1},{3,0},{16,19},{17,18},{18,17},{19,16},{4,7},{5,6... | collective-permute-start | bytes 405512 | tf_op jit(solution)/shard_map/ppermute | solution.py:340
  9.3 12.0 %collective-permute-start.2 = (bf16[528,128]{1,0:T(8,128)(2,1)S(1)}, bf16[528,128]{1,0:T(8,128)(2,1)S(1)}, u32[]{:S(2)}, u32[]{:S(2)}) collective-permute-start(bf16[528,128]{1,0:T(8,128)(2,1)S(1)} %get-tuple-element.14), channel_id=1, source_target_pairs={{0,1},{1,0},{2,3},{3,2},{16,17},{17,16},{18,19},{19,18},{4,5},{5,4... | collective-permute-start | bytes 405512 | tf_op jit(solution)/shard_map/ppermute | solution.py:340
  9.3 12.1 %collective-permute-start.3 = (bf16[528,128]{1,0:T(8,128)(2,1)S(1)}, bf16[528,128]{1,0:T(8,128)(2,1)S(1)}, u32[]{:S(2)}, u32[]{:S(2)}) collective-permute-start(bf16[528,128]{1,0:T(8,128)(2,1)S(1)} %get-tuple-element.15), channel_id=1, source_target_pairs={{0,19},{1,18},{2,17},{3,16},{16,3},{17,2},{18,1},{19,0},{4,23},{5,... | collective-permute-start | bytes 405512 | tf_op jit(solution)/shard_map/ppermute | solution.py:340
  10.2 12.3 %collective-permute-start.4 = (bf16[528,128]{1,0:T(8,128)(2,1)S(1)}, bf16[528,128]{1,0:T(8,128)(2,1)S(1)}, u32[]{:S(2)}, u32[]{:S(2)}) collective-permute-start(bf16[528,128]{1,0:T(8,128)(2,1)S(1)} %get-tuple-element.16), channel_id=1, source_target_pairs={{0,17},{1,16},{2,19},{3,18},{16,1},{17,0},{18,3},{19,2},{4,21},{5,... | collective-permute-start | bytes 405512 | tf_op jit(solution)/shard_map/ppermute | solution.py:340
  16.3 12.8 %collective-permute-start.7 = (bf16[528,128]{1,0:T(8,128)(2,1)S(1)}, bf16[528,128]{1,0:T(8,128)(2,1)S(1)}, u32[]{:S(2)}, u32[]{:S(2)}) collective-permute-start(bf16[528,128]{1,0:T(8,128)(2,1)S(1)} %get-tuple-element.23), channel_id=1, source_target_pairs={{0,16},{1,17},{2,18},{3,19},{16,0},{17,1},{18,2},{19,3},{4,20},{5,... | collective-permute-start | bytes 405512 | tf_op jit(solution)/shard_map/ppermute | solution.py:340
  18.1 13.1 %collective-permute-start.5 = (bf16[528,128]{1,0:T(8,128)(2,1)S(1)}, bf16[528,128]{1,0:T(8,128)(2,1)S(1)}, u32[]{:S(2)}, u32[]{:S(2)}) collective-permute-start(bf16[528,128]{1,0:T(8,128)(2,1)S(1)} %get-tuple-element.21), channel_id=1, source_target_pairs={{0,18},{1,19},{2,16},{3,17},{16,2},{17,3},{18,0},{19,1},{4,22},{5,... | collective-permute-start | bytes 405512 | tf_op jit(solution)/shard_map/ppermute | solution.py:340
  21.3 11.4 %collective-permute-start.6 = (bf16[528,128]{1,0:T(8,128)(2,1)S(1)}, bf16[528,128]{1,0:T(8,128)(2,1)S(1)}, u32[]{:S(2)}, u32[]{:S(2)}) collective-permute-start(bf16[528,128]{1,0:T(8,128)(2,1)S(1)} %get-tuple-element.22), channel_id=1, source_target_pairs={{0,2},{1,3},{2,0},{3,1},{16,18},{17,19},{18,16},{19,17},{4,6},{5,7... | collective-permute-start | bytes 405512 | tf_op jit(solution)/shard_map/ppermute | solution.py:340
  22.7 3.7 %collective-permute-start.8 = (f32[8,128]{1,0:T(8,128)S(1)}, f32[8,128]{1,0:T(8,128)S(1)}, u32[]{:S(2)}, u32[]{:S(2)}) collective-permute-start(f32[8,128]{1,0:T(8,128)S(1)} %score.4.rest_5_.own_ref), channel_id=1, source_target_pairs={{0,16},{1,17},{2,18},{3,19},{16,0},{17,1},{18,2},{19,3},{4,20},{5,... | collective-permute-start | bytes 12296 | tf_op jit(solution)/shard_map/ppermute | solution.py:340
  26.4 11.5 %collective-permute-start.10 = (f32[8,128]{1,0:T(8,128)S(1)}, f32[8,128]{1,0:T(8,128)S(1)}, u32[]{:S(2)}, u32[]{:S(2)}) collective-permute-start(f32[8,128]{1,0:T(8,128)S(1)} %merge.1.rest_2_), channel_id=1, source_target_pairs={{0,3},{1,2},{2,1},{3,0},{16,19},{17,18},{18,17},{19,16},{4,7},{5,6... | collective-permute-start | bytes 12296 | tf_op jit(solution)/shard_map/ppermute | solution.py:340
  28.9 9.0 %collective-permute-start.9 = (f32[8,128]{1,0:T(8,128)S(1)}, f32[8,128]{1,0:T(8,128)S(1)}, u32[]{:S(2)}, u32[]{:S(2)}) collective-permute-start(f32[8,128]{1,0:T(8,128)S(1)} %merge.1.rest_2_), channel_id=1, source_target_pairs={{0,1},{1,0},{2,3},{3,2},{16,17},{17,16},{18,19},{19,18},{4,5},{5,4... | collective-permute-start | bytes 12296 | tf_op jit(solution)/shard_map/ppermute | solution.py:340
  29.2 5.7 %copy-start.2 = (bf16[1,1,768,1024]{3,2,1,0:T(8,128)(2,1)S(1)}, bf16[1,1,768,1024]{3,2,1,0:T(8,128)(2,1)}, u32[]{:S(2)}) copy-start(bf16[1,1,768,1024]{3,2,1,0:T(8,128)(2,1)} %param.12) | copy-start | bytes 4718596
  29.2 5.7 %copy-start.3 = (bf16[1,1,768,1024]{3,2,1,0:T(8,128)(2,1)S(1)}, bf16[1,1,768,1024]{3,2,1,0:T(8,128)(2,1)}, u32[]{:S(2)}) copy-start(bf16[1,1,768,1024]{3,2,1,0:T(8,128)(2,1)} %param.13) | copy-start | bytes 4718596
  29.3 5.5 %copy-start = (f32[1,1,768,1024]{3,2,1,0:T(8,128)S(1)}, f32[1,1,768,1024]{3,2,1,0:T(8,128)}, u32[]{:S(2)}) copy-start(f32[1,1,768,1024]{3,2,1,0:T(8,128)} %param.11) | copy-start | bytes 9437188
  29.3 8.6 %collective-permute-start.11 = (f32[8,128]{1,0:T(8,128)S(1)}, f32[8,128]{1,0:T(8,128)S(1)}, u32[]{:S(2)}, u32[]{:S(2)}) collective-permute-start(f32[8,128]{1,0:T(8,128)S(1)} %score.5.rest_1_.rest_2_), channel_id=1, source_target_pairs={{0,16},{1,17},{2,18},{3,19},{16,0},{17,1},{18,2},{19,3},{4,20},{5,... | collective-permute-start | bytes 12296 | tf_op jit(solution)/shard_map/ppermute | solution.py:340
  31.3 6.6 %collective-permute-start.13 = (f32[8,128]{1,0:T(8,128)S(1)}, f32[8,128]{1,0:T(8,128)S(1)}, u32[]{:S(2)}, u32[]{:S(2)}) collective-permute-start(f32[8,128]{1,0:T(8,128)S(1)} %score.6.rest_1_), channel_id=1, source_target_pairs={{0,18},{1,19},{2,16},{3,17},{16,2},{17,3},{18,0},{19,1},{4,22},{5,... | collective-permute-start | bytes 12296 | tf_op jit(solution)/shard_map/ppermute | solution.py:340
  32.8 5.1 %collective-permute-start.12 = (f32[8,128]{1,0:T(8,128)S(1)}, f32[8,128]{1,0:T(8,128)S(1)}, u32[]{:S(2)}, u32[]{:S(2)}) collective-permute-start(f32[8,128]{1,0:T(8,128)S(1)} %score.7.rest_3_), channel_id=1, source_target_pairs={{0,2},{1,3},{2,0},{3,1},{16,18},{17,19},{18,16},{19,17},{4,6},{5,7... | collective-permute-start | bytes 12296 | tf_op jit(solution)/shard_map/ppermute | solution.py:340
  34.8 3.1 %copy-start.4 = (s32[1,512,8]{1,2,0:T(8,128)S(1)}, s32[1,512,8]{1,2,0:T(8,128)}, u32[]{:S(2)}) copy-start(s32[1,512,8]{1,2,0:T(8,128)} %param.9) | copy-start | bytes 49156
